TPU v7x, 32 devices: a whole 2x2x4 slice. The times are simulated.
32 devices in a mesh: dp: 16 (over z, y, core), own: 2 (over x).
Axes of the slice: x: 2, y: 2, z: 4, core: 2. Of those that a mesh axis runs over, the one named last changes fastest.
Arguments:
- wide_rows: bfloat16 [8, 24576, 256], P(None, ('dp', 'own'))
- narrow_rows: bfloat16 [8, 24576, 128], P(None, ('dp', 'own'))
- owner_map: int32 [8], replicated, may hold values from 0 to 1, as said below
Outputs:
- kept_inverse: float32 [10, 256, 256], P('own', None, 'dp')
- update: float32 [8, 128, 256], P(None, 'own', 'dp')
Inputs may be any that keep to these rules, and one draw needn't show every extreme that they name: owner_map[l] names the owner of layer l; no owner has more than 5 layers, and one owner has exactly 5.
All inputs are finite; a program needn't handle non-finite values.
Results may differ from a plain program's by a relative error of at most 0.0003.
Values sent between devices are 32-bit elements; how exact they have to be, the bound alone decides.
No kernel may reach another device: no remote copies, remote signals or barrier semaphores. Data moves between devices by JAX's collectives and lax.ppermute only.
A program may use at most 64 MiB of HBM per device.

v0:
```python
import jax
import jax.numpy as jnp
from jax import lax
from jax.sharding import PartitionSpec as P

DAMP = 0.5


def split_stats(flat, wide, narrow):
    count = flat.shape[0]
    wpart = flat[:, : wide * wide].reshape(count, wide, wide)
    npart = flat[:, wide * wide : wide * wide + narrow * narrow].reshape(count, narrow, narrow)
    mpart = flat[:, wide * wide + narrow * narrow :].reshape(count, narrow, wide)
    return (wpart, npart, mpart)


def damped_factor(cov):
    size = cov.shape[-1]
    return jax.vmap(jnp.linalg.cholesky)(cov + DAMP * jnp.eye(size, dtype=jnp.float32))


def solve_many(factors, rhs):
    return jax.vmap(lambda c, b: jax.scipy.linalg.cho_solve((c, True), b))(factors, rhs)


def on_device(wide_rows, narrow_rows, owner_map):
    layers, rows, wide = wide_rows.shape
    narrow = narrow_rows.shape[2]
    n_dp = lax.axis_size("dp")
    n_own = lax.axis_size("own")
    per_owner = layers // n_own + 1
    total = rows * n_dp * n_own
    wcov = (
        jnp.einsum("lrw,lrv->lwv", wide_rows, wide_rows, preferred_element_type=jnp.float32) / total
    )
    ncov = (
        jnp.einsum("lrn,lrm->lnm", narrow_rows, narrow_rows, preferred_element_type=jnp.float32)
        / total
    )
    mixed = (
        jnp.einsum("lrn,lrw->lnw", narrow_rows, wide_rows, preferred_element_type=jnp.float32)
        / total
    )
    flat = jnp.concatenate(
        [wcov.reshape(layers, -1), ncov.reshape(layers, -1), mixed.reshape(layers, -1)], axis=1
    )
    same = owner_map[:, None] == owner_map[None, :]
    order = jnp.arange(layers, dtype=jnp.int32)
    earlier = order[None, :] < order[:, None]
    rank = jnp.sum((same & earlier).astype(jnp.int32), axis=1)
    slot = owner_map * per_owner + rank
    slot_count = n_own * per_owner
    slot_table = (slot[:, None] == jnp.arange(slot_count, dtype=jnp.int32)[None, :]).astype(
        jnp.float32
    )
    col_width = wide // n_dp
    row_width = narrow // n_own
    dp_index = lax.axis_index("dp")
    own_index = lax.axis_index("own")
    pick_cols = lax.dynamic_slice_in_dim(
        jnp.eye(wide, dtype=jnp.float32), dp_index * col_width, col_width, 1
    )
    summed = lax.psum(flat, ("dp", "own"))
    wpart, npart, mpart = split_stats(summed, wide, narrow)
    inverse_cols = solve_many(
        damped_factor(wpart), jnp.broadcast_to(pick_cols, (layers, wide, col_width))
    )
    own_table = lax.dynamic_slice_in_dim(slot_table, own_index * per_owner, per_owner, 1)
    filled = jnp.sum(own_table, axis=0)
    kept = jnp.einsum("lc,lwk->cwk", own_table, inverse_cols, precision=lax.Precision.HIGHEST)
    kept = kept + (1.0 - filled)[:, None, None] * pick_cols[None, :, :] / DAMP
    pick_rows = lax.dynamic_slice_in_dim(
        jnp.eye(narrow, dtype=jnp.float32), own_index * row_width, row_width, 1
    )
    narrow_inv = solve_many(
        damped_factor(npart), jnp.broadcast_to(pick_rows, (layers, narrow, row_width))
    )
    inner = jnp.einsum("lnw,lwk->lnk", mpart, inverse_cols, precision=lax.Precision.HIGHEST)
    update = jnp.einsum("lnr,lnk->lrk", narrow_inv, inner, precision=lax.Precision.HIGHEST)
    return (kept, update)


def solution(mesh):
    in_specs = (P(None, ("dp", "own"), None), P(None, ("dp", "own"), None), P())
    out_specs = (P("own", None, "dp"), P(None, "own", "dp"))
    return jax.shard_map(
        on_device, mesh=mesh, in_specs=in_specs, out_specs=out_specs, check_vma=False
    )
```

profile of v0, /device:TPU:0, one launch (start us, length us, event | category | flops | bytes accessed | tf_op | source)
XLA Modules:
  0.0 834.5 jit_solution(16258324259214081875)
XLA Ops:
  7.2 2.7 fusion.2
  14.5 2.1 pad_maximum_fusion
  19.8 139.0 %all-reduce.3.cloned.1.call-done = f32[8,114688]{1,0:T(8,128)} async-done(((f32[8,114688]{1,0:T(8,128)}), f32[8,114688]{1,0:T(8,128)}) %all-reduce.3.cloned.1.call-update) | async-done | bytes 3670032 | tf_op jit(solution)/shard_map/psum | solution.py:63
  160.8 2.0 copy.51
  164.7 2.0 copy.52
  166.7 2.1 fusion.12
  168.8 95.2 %custom-call.35 = f32[8,128,128]{2,1,0:T(8,128)} custom-call(f32[8,128,128]{2,1,0:T(8,128)} %fusion.12), custom_call_target="Cholesky" | custom-call | tf_op jit(solution)/shard_map/vmap(jit(cholesky))/cholesky | solution.py:19
  267.6 2.9 copy.40
  270.5 3.2 broadcast_add_fusion
  273.7 2.9 copy.41
  276.6 2.5 fusion
  281.3 95.3 %custom-call.31 = f32[8,128,128]{2,1,0:T(8,128)} custom-call(f32[8,128,128]{2,1,0:T(8,128)} %cholesky.185), custom_call_target="Cholesky" | custom-call | tf_op jit(solution)/shard_map/vmap(jit(cholesky))/cholesky | solution.py:19
  378.4 80.0 %custom-call.32 = f32[8,1,128,128]{2,3,1,0:T(8,128)} custom-call(f32[8,1,128,128]{3,2,1,0:T(8,128)} %select_bitcast_fusion.1), custom_call_target="InvertDiagBlocksLowerTriangular" | custom-call | tf_op jit(solution)/shard_map/vmap(jit(cholesky))/cholesky | solution.py:19
  458.5 2.7 cholesky.173
  462.7 2.0 convolution_subtract_fusion
  464.7 95.3 %custom-call.33 = f32[8,128,128]{2,1,0:T(8,128)} custom-call(f32[8,128,128]{2,1,0:T(8,128)} %convolution_subtract_fusion), custom_call_target="Cholesky" | custom-call | tf_op jit(solution)/shard_map/vmap(jit(cholesky))/cholesky | solution.py:19
  560.0 2.4 select_reduce_fusion
  563.4 80.0 %custom-call.36 = f32[8,1,128,128]{2,3,1,0:T(8,128)} custom-call(f32[8,1,128,128]{3,2,1,0:T(8,128)} %select_bitcast_fusion), custom_call_target="InvertDiagBlocksLowerTriangular" | custom-call | tf_op jit(solution)/shard_map/vmap(jit(_cho_solve))/triangular_solve | solution.py:23
  643.6 3.2 select_select_fusion
  646.9 8.2 while.1
  647.5 3.6 bitcast_dynamic-update-slice_fusion.2
  651.7 3.4 bitcast_dynamic-update-slice_fusion.2
  655.1 158.6 %custom-call.34 = f32[8,2,128,128]{2,3,1,0:T(8,128)} custom-call(f32[8,2,128,128]{3,2,1,0:T(8,128)} %bitcast.95), custom_call_target="InvertDiagBlocksLowerTriangular" | custom-call | tf_op jit(solution)/shard_map/vmap(jit(_cho_solve))/triangular_solve | solution.py:23
  815.4 2.0 convolution_subtract_fusion.2
  (97 shorter events, 35.0 us)
Async XLA Ops:
  7.2 2.8 copy-start
  7.2 151.6 %all-reduce.3.cloned.1.call-start = ((), (), s32[]{:S(2)}) async-start(), calls=%async_computation | async-start | bytes 7340032 | tf_op jit(solution)/shard_map/psum | solution.py:63
  7.2 3.3 copy-start.1
  16.6 1.0 copy-start.18
  16.6 1.9 copy-start.8
  17.8 0.8 copy-start.15
  18.6 0.6 copy-start.10
  264.0 1.6 slice-start
  279.1 1.3 copy-start.2
  458.5 2.7 copy-start.3
  458.5 2.7 copy-start.7
  461.2 98.8 %copy-start.9 = (pred[128,128]{1,0:T(8,128)(4,1)S(1)}, pred[128,128]{1,0:T(8,128)(4,1)}, u32[]{:S(2)}) copy-start(pred[128,128]{1,0:T(8,128)(4,1)} %copy-done.8) | copy-start | bytes 49156
  559.9 2.5 copy-start.6
  643.6 3.3 copy-start.19
  646.9 166.8 %copy-start.13 = (f32[128,16]{0,1:T(8,128)S(1)}, f32[128,16]{0,1:T(8,128)}, u32[]{:S(2)}) copy-start(f32[128,16]{0,1:T(8,128)} %get-tuple-element.31) | copy-start | bytes 24580
  646.9 168.5 %copy-start.14 = (f32[128,16]{0,1:T(8,128)S(1)}, f32[128,16]{0,1:T(8,128)}, u32[]{:S(2)}) copy-start(f32[128,16]{0,1:T(8,128)} %get-tuple-element.30) | copy-start | bytes 24580
  813.7 5.3 copy-start.4
  819.0 3.5 slice-start.1
  821.6 2.2 copy-start.11
  821.6 2.2 copy-start.16
  821.6 2.2 copy-start.17
  822.5 2.3 copy-start.5
  822.5 2.3 copy-start.12
Sparse Core Ops, SparseCore 0:
  16.7 142.0 all-reduce.2
where the time goes:
time: 836 us; the launch traced here: 834 us
  other arithmetic  627 us (75%)
  waiting for transfers between devices  139 us (17%)
  local copies, waits for them, and re-layouts  33.4 us (4%)
  matrix products  21.1 us (3%)
  between operations  14.3 us (2%)
    another operation x11, other arithmetic, damped_factor(): jax.vmap(jnp.linalg.cholesky)(cov + DAMP * jnp.eye(size, dtype=jnp.float32))  370 us
    another operation x7, other arithmetic, solve_many(): jax.scipy.linalg.cho_solve((c, True), b)  244 us
    psum x1, waiting for transfers between devices, on_device(): summed = lax.psum(flat, ('dp', 'own'))  139 us
  transfers between devices with their start and end apart: 1, of which 1 were waited for; matrix products, arithmetic and copies ran while one was open for 0% of the time, Pallas kernels for 0%

commit v1 on v0

v1 whole, which is shorter than its diff:
```python
import functools

import jax
import jax.numpy as jnp
import numpy as np
from jax import lax
from jax.experimental import pallas as pl
from jax.experimental.pallas import tpu as pltpu
from jax.sharding import PartitionSpec as P

DAMP = 0.5
LANES = 128
PANEL = 8
VMEM_LIMIT = 48 * 1024 * 1024
HIGHEST = lax.Precision.HIGHEST


def transposed_dot(a, b, precision=None):
    return lax.dot_general(
        a, b, (((0,), (0,)), ((), ())), precision=precision, preferred_element_type=jnp.float32
    )


def gram_kernel(place, wide_ref, narrow_ref, *refs):
    outs, blocks, mixed_blocks = refs[:8], refs[8], refs[9]
    a_keep, a_send, b_keep, b_send, ma_keep, ma_send, mb_keep, mb_send = outs
    wide = wide_ref[0]
    narrow = narrow_ref[0]
    wcov = transposed_dot(wide, wide)
    mixed = transposed_dot(narrow, wide)
    half = wcov.shape[0] // 2
    low = mixed.shape[0] // 2
    blocks[0] = wcov[:half, :half]
    blocks[1] = wcov[:half, half:]
    blocks[2] = wcov[half:, half:]
    blocks[3] = transposed_dot(narrow, narrow)
    mixed_blocks[0] = mixed[:low, :half]
    mixed_blocks[1] = mixed[low:, :half]
    mixed_blocks[2] = mixed[:low, half:]
    mixed_blocks[3] = mixed[low:, half:]
    core, near = place[1], place[2]
    for q in range(2):
        kept = core * 2 + (q ^ near)
        sent = (1 - core) * 2 + (q ^ near)
        rows = half // 2
        a_keep[0, 0, 0, q] = blocks[kept, :rows]
        b_keep[0, 0, 0, q] = blocks[kept, rows:]
        a_send[0, 0, 0, q] = blocks[sent, :rows]
        b_send[0, 0, 0, q] = blocks[sent, rows:]
        rows = low // 2
        ma_keep[0, 0, 0, q] = mixed_blocks[kept, :rows]
        mb_keep[0, 0, 0, q] = mixed_blocks[kept, rows:]
        ma_send[0, 0, 0, q] = mixed_blocks[sent, :rows]
        mb_send[0, 0, 0, q] = mixed_blocks[sent, rows:]


def gram(place, wide_rows, narrow_rows):
    layers, rows, wide = wide_rows.shape
    narrow = narrow_rows.shape[2]

    def layer_block(i, place):
        return (jnp.bitwise_xor(i, place[0]), 0, 0)

    def order_a(i, place):
        return (i % 2, (i // 2) % 2, i // 4, 0, 0, 0)

    def order_b(i, place):
        return ((i // 2) % 2, i % 2, i // 4, 0, 0, 0)

    specs, shapes = [], []
    for height in (wide // 4, narrow // 4):
        for order in (order_a, order_a, order_b, order_b):
            specs.append(pl.BlockSpec((1, 1, 1, 2, height, LANES), order))
            shapes.append(jax.ShapeDtypeStruct((2, 2, 2, 2, height, LANES), jnp.float32))
    return pl.pallas_call(
        gram_kernel,
        grid_spec=pltpu.PrefetchScalarGridSpec(
            num_scalar_prefetch=1,
            grid=(layers,),
            in_specs=[
                pl.BlockSpec((1, rows, wide), layer_block),
                pl.BlockSpec((1, rows, narrow), layer_block),
            ],
            out_specs=specs,
            scratch_shapes=[
                pltpu.VMEM((4, wide // 2, LANES), jnp.float32),
                pltpu.VMEM((4, narrow // 2, LANES), jnp.float32),
            ],
        ),
        out_shape=shapes,
        compiler_params=pltpu.CompilerParams(vmem_limit_bytes=VMEM_LIMIT),
        name="gram",
    )(place, wide_rows, narrow_rows)


def lane_gather(x, index):
    return jnp.take_along_axis(x, index, axis=1, mode="promise_in_bounds")


def trailing_update(a_ref, left_ref, right_ref, base):
    size = a_ref.shape[1]
    a_ref[pl.ds(pl.multiple_of(base, PANEL), PANEL), :] = jnp.zeros((PANEL, size), jnp.float32)
    lane = lax.broadcasted_iota(jnp.int32, (1, size), 1)
    swept = (lane >= base - PANEL) & (lane < base)
    update = transposed_dot(left_ref[...], right_ref[...])
    a_ref[PANEL : PANEL + size, :] = (
        jnp.where(swept, 0.0, a_ref[PANEL : PANEL + size, :]) - update
    )


def sweep_panel(a_ref, left_ref, right_ref, tile, step, panel):
    size = a_ref.shape[1]
    tiles = size // LANES
    first = step * PANEL
    base = tile * LANES + first
    trailing_update(a_ref, left_ref, right_ref, base)

    shape = (PANEL, LANES)
    sub = lax.broadcasted_iota(jnp.int32, shape, 0)
    lane = lax.broadcasted_iota(jnp.int32, shape, 1)
    parts = [panel[:, LANES * t : LANES * (t + 1)] for t in range(tiles)]
    rows = [
        [jnp.broadcast_to(part[k : k + 1, :], shape) for part in parts] for k in range(PANEL)
    ]
    index = [jnp.full(shape, 0, jnp.int32) + (first + i) for i in range(PANEL)]
    d = [[None] * PANEL for _ in range(PANEL)]
    for j in range(PANEL):
        for i in range(j, PANEL):
            d[i][j] = lane_gather(rows[j][tile], index[i])
    own = (lane >= first) & (lane < first + PANEL)
    q = [[None] * tiles for _ in range(PANEL)]
    factor = [[None] * PANEL for _ in range(PANEL)]
    for k in range(PANEL):
        scale = lax.rsqrt(d[k][k])
        for i in range(k + 1, PANEL):
            factor[i][k] = d[i][k] * scale
        for i in range(k + 1, PANEL):
            for j in range(k + 1, i + 1):
                d[i][j] = d[i][j] - factor[i][k] * factor[j][k]
        for t in range(tiles):
            value = rows[k][t]
            if t == tile:
                value = jnp.where(own, jnp.where(lane == first + k, -1.0, 0.0), value)
            for j in range(k):
                value = value - factor[k][j] * q[j][t]
            q[k][t] = value * scale

    packed = []
    for t in range(tiles):
        value = q[0][t]
        for k in range(1, PANEL):
            value = jnp.where(sub == k, q[k][t], value)
        packed.append(value)
    whole = jnp.concatenate(packed, axis=1) if tiles > 1 else packed[0]
    high = whole.astype(jnp.bfloat16).astype(jnp.float32)
    rest = whole - high
    middle = rest.astype(jnp.bfloat16).astype(jnp.float32)
    low = rest - middle
    left = jnp.concatenate([high, high, middle, middle, high, low], axis=0)
    right = jnp.concatenate([high, middle, high, middle, low, high], axis=0)
    left_ref[...] = left.astype(jnp.bfloat16)
    right_ref[...] = right.astype(jnp.bfloat16)

    after = pl.multiple_of(base + 2 * PANEL, PANEL)
    following = a_ref[pl.ds(after, PANEL), :]
    last = first == LANES - PANEL
    next_lane = jnp.where(last, 0, first + PANEL) + sub
    weights = []
    for k in range(PANEL):
        source = q[k][tile]
        if tile + 1 < tiles:
            source = jnp.where(last, q[k][tile + 1], source)
        weights.append(lane_gather(source, next_lane))
    result = []
    for t in range(tiles):
        value = following[:, LANES * t : LANES * (t + 1)]
        if t == tile:
            value = jnp.where(own, 0.0, value)
        terms = [weights[k] * q[k][t] for k in range(PANEL)]
        while len(terms) > 1:
            terms = [terms[i] + terms[i + 1] for i in range(0, len(terms), 2)]
        result.append(value - terms[0])
    return jnp.concatenate(result, axis=1) if tiles > 1 else result[0]


def inverse_kernel(total, place, *refs):
    pieces, refs = refs[:4], refs[4:]
    winv_ref, ninv_ref, blocks, wa, na, wl, wr, nl, nr = refs
    mine = place[1] * 2 + place[2]
    for r in range(4):
        blocks[jnp.bitwise_xor(mine, r)] = pieces[r][...]
    half = blocks.shape[1]

    def eye(size):
        return jnp.where(
            lax.broadcasted_iota(jnp.int32, (size, size), 0)
            == lax.broadcasted_iota(jnp.int32, (size, size), 1),
            DAMP,
            0.0,
        )

    wide, narrow = wa.shape[1], na.shape[1]
    wa[...] = jnp.zeros(wa.shape, jnp.float32)
    na[...] = jnp.zeros(na.shape, jnp.float32)
    corner = blocks[1] / total
    damp = eye(half)
    wa[PANEL : PANEL + half, :half] = blocks[0] / total + damp
    wa[PANEL : PANEL + half, half:] = corner
    wa[PANEL + half : PANEL + wide, :half] = corner.T
    wa[PANEL + half : PANEL + wide, half:] = blocks[2] / total + damp
    na[PANEL : PANEL + narrow, :] = blocks[3] / total + damp
    for ref in (wl, wr, nl, nr):
        ref[...] = jnp.zeros(ref.shape, ref.dtype)

    def both(step, carry):
        wp, np_ = carry
        wp = sweep_panel(wa, wl, wr, 0, step, wp)
        np_ = sweep_panel(na, nl, nr, 0, step, np_)
        return (wp, np_)

    steps = LANES // PANEL
    start = (wa[PANEL : 2 * PANEL, :], na[PANEL : 2 * PANEL, :])
    panel, _ = lax.fori_loop(0, steps, both, start)
    trailing_update(na, nl, nr, narrow)
    ninv_ref[...] = -na[PANEL : PANEL + narrow, :]

    def only(step, panel):
        return sweep_panel(wa, wl, wr, 1, step, panel)

    lax.fori_loop(0, steps, only, panel)
    trailing_update(wa, wl, wr, wide)
    winv_ref[...] = -wa[PANEL : PANEL + wide, :]


def inverses(place, pieces, wide, narrow, total):
    vmem = pl.BlockSpec(memory_space=pltpu.VMEM)
    splits = 6 * PANEL
    return pl.pallas_call(
        functools.partial(inverse_kernel, total),
        in_specs=[pl.BlockSpec(memory_space=pltpu.SMEM)] + [vmem] * 4,
        out_specs=[vmem] * 2,
        out_shape=[
            jax.ShapeDtypeStruct((wide, wide), jnp.float32),
            jax.ShapeDtypeStruct((narrow, narrow), jnp.float32),
        ],
        scratch_shapes=[
            pltpu.VMEM((4, wide // 2, LANES), jnp.float32),
            pltpu.VMEM((wide + 2 * PANEL, wide), jnp.float32),
            pltpu.VMEM((narrow + 2 * PANEL, narrow), jnp.float32),
            pltpu.VMEM((splits, wide), jnp.bfloat16),
            pltpu.VMEM((splits, wide), jnp.bfloat16),
            pltpu.VMEM((splits, narrow), jnp.bfloat16),
            pltpu.VMEM((splits, narrow), jnp.bfloat16),
        ],
        compiler_params=pltpu.CompilerParams(vmem_limit_bytes=VMEM_LIMIT),
        name="inverses",
    )(place, *pieces)


def aligned_rows(ref, index, count):
    if count % PANEL == 0:
        return ref[pl.ds(pl.multiple_of(index * count, count), count), :]
    per_slab = PANEL // count
    slab = ref[pl.ds(pl.multiple_of(index // per_slab * PANEL, PANEL), PANEL), :]
    value = slab[:count]
    for i in range(1, per_slab):
        value = jnp.where(index % per_slab == i, slab[i * count : (i + 1) * count], value)
    return value


def product_kernel(total, far_stride, place, winv_ref, ninv_ref, *refs):
    pieces, (out_ref, blocks) = refs[:4], refs[4:]
    mine = place[1] * 2 + place[2]
    for r in range(4):
        blocks[jnp.bitwise_xor(mine, r)] = pieces[r][...]
    low = blocks.shape[1]
    ninv = ninv_ref[...]
    parts = []
    for h in range(2):
        mixed = blocks[2 * h : 2 * h + 2].reshape(2 * low, LANES) / total
        parts.append(transposed_dot(mixed, ninv, HIGHEST))
    inner = jnp.concatenate(parts, axis=0)
    cols = out_ref.shape[1]
    wide = winv_ref.shape[1]
    for j in range(4):
        index = place[3] + (j // 2) * far_stride + (j % 2) * 2
        picked = aligned_rows(winv_ref, index, cols)
        update = lax.dot_general(
            picked,
            inner,
            (((1,), (0,)), ((), ())),
            precision=HIGHEST,
            preferred_element_type=jnp.float32,
        )
        for x in range(2):
            out_ref[2 * j + x, :, :wide] = picked
            out_ref[2 * j + x, :, wide:] = update


def products(place, winv, ninv, pieces, cols, far_stride, total):
    vmem = pl.BlockSpec(memory_space=pltpu.VMEM)
    wide, narrow = winv.shape[0], ninv.shape[0]
    return pl.pallas_call(
        functools.partial(product_kernel, total, far_stride),
        in_specs=[pl.BlockSpec(memory_space=pltpu.SMEM)] + [vmem] * 6,
        out_specs=vmem,
        out_shape=jax.ShapeDtypeStruct((8, cols, wide + narrow), jnp.float32),
        scratch_shapes=[pltpu.VMEM((4, narrow // 2, LANES), jnp.float32)],
        compiler_params=pltpu.CompilerParams(vmem_limit_bytes=VMEM_LIMIT),
        name="products",
    )(place, winv, ninv, *pieces)


def placing_kernel(place, owner_map, got_ref, kept_ref, update_ref, turned):
    layers, cols, _ = got_ref.shape
    wide = kept_ref.shape[1]
    rows = update_ref.shape[1]
    own, dp = place[4], place[5]
    sub = lax.broadcasted_iota(jnp.int32, (cols, wide), 0)
    lane = lax.broadcasted_iota(jnp.int32, (cols, wide), 1)
    empty = jnp.where(lane == sub + dp * cols, 1.0 / DAMP, 0.0)
    owners = [owner_map[l] for l in range(layers)]
    ranks = []
    for l in range(layers):
        rank = jnp.int32(0)
        for j in range(l):
            rank = rank + (owners[j] == owners[l]).astype(jnp.int32)
        ranks.append(rank)
    for c in range(kept_ref.shape[0]):
        value = empty
        for l in range(layers):
            taken = (owners[l] == own) & (ranks[l] == c)
            value = jnp.where(taken, got_ref[l, :, :wide], value)
        kept_ref[c] = value.T
    for l in range(layers):
        turned[...] = got_ref[l, :, wide:].T
        update_ref[l] = turned[pl.ds(pl.multiple_of(own * rows, rows), rows), :]


def placing(place, owner_map, got, wide, narrow, slots, rows):
    vmem = pl.BlockSpec(memory_space=pltpu.VMEM)
    smem = pl.BlockSpec(memory_space=pltpu.SMEM)
    layers, cols, _ = got.shape
    return pl.pallas_call(
        placing_kernel,
        in_specs=[smem, smem, vmem],
        out_specs=[vmem, vmem],
        out_shape=[
            jax.ShapeDtypeStruct((slots, wide, cols), jnp.float32),
            jax.ShapeDtypeStruct((layers, rows, cols), jnp.float32),
        ],
        scratch_shapes=[pltpu.VMEM((narrow, cols), jnp.float32)],
        compiler_params=pltpu.CompilerParams(vmem_limit_bytes=VMEM_LIMIT),
        name="placing",
    )(place, owner_map, got)


def swap(value, axis):
    return lax.ppermute(value, axis, [(0, 1), (1, 0)])


def swap_both(value, axes):
    return lax.ppermute(value, axes, [(0, 3), (1, 2), (2, 1), (3, 0)])


def fold(value, axis):
    return value[0] + swap(value[1], axis)


def reduce_pieces(a_keep, a_send, b_keep, b_send, names):
    core, near, far, first, second, extra = names
    a = a_keep + swap(a_send, core)
    b = b_keep + swap(b_send, core)
    a = fold(a, first)
    b = fold(b, second)
    a = fold(a, second)
    b = fold(b, first)
    both = jnp.concatenate([a, b], axis=2)
    both = jnp.moveaxis(both, 1, 0)
    both = fold(both, near)
    both = fold(both, far)
    if extra:
        both = lax.psum(both, extra)
    return [both, swap(both, near), swap(both, core), swap_both(both, (near, core))]


def on_device(dp_names, own_names, wide_rows, narrow_rows, owner_map):
    layers, rows, wide = wide_rows.shape
    narrow = narrow_rows.shape[2]
    n_dp, n_own = 2 ** len(dp_names), 2 ** len(own_names)
    total = float(rows * n_dp * n_own)
    core, second, near, far = dp_names[-1], dp_names[-2], dp_names[1], dp_names[0]
    first = own_names[-1]
    extra = tuple(
        n for n in dp_names + own_names if n not in (core, near, far, first, second)
    )
    names = (core, near, far, first, second, extra)
    index = {name: lax.axis_index(name) for name in dp_names + own_names}

    def combine(axes):
        value = jnp.int32(0)
        for name in axes:
            value = value * 2 + index[name]
        return value

    dp_index = combine(dp_names)
    far_stride = n_dp // 2
    place = jnp.stack(
        [
            index[far] * 4 + index[second] * 2 + index[first],
            index[core],
            index[near],
            dp_index - index[far] * far_stride - index[second] * 2,
            combine(own_names),
            dp_index,
        ]
    ).astype(jnp.int32)

    outs = gram(place, wide_rows, narrow_rows)
    squares = reduce_pieces(*outs[:4], names)
    mixed = reduce_pieces(*outs[4:], names)
    winv, ninv = inverses(place, squares, wide, narrow, total)
    cols = wide // n_dp
    sent = products(place, winv, ninv, mixed, cols, far_stride, total)
    got = lax.all_to_all(sent, (far, second, first), 0, 0)
    kept, update = placing(
        place, owner_map, got, wide, narrow, layers // n_own + 1, narrow // n_own
    )
    return (kept, update)


def solution(mesh):
    n_dp, n_own = mesh.shape["dp"], mesh.shape["own"]
    dp_names = tuple(f"dp{i}" for i in range(int(np.log2(n_dp))))
    own_names = tuple(f"own{i}" for i in range(int(np.log2(n_own))))
    names = dp_names + own_names
    bits = jax.sharding.Mesh(mesh.devices.reshape((2,) * len(names)), names)
    in_specs = (P(None, names, None), P(None, names, None), P())
    out_specs = (P(own_names, None, dp_names), P(None, own_names, dp_names))
    return jax.shard_map(
        functools.partial(on_device, dp_names, own_names),
        mesh=bits,
        in_specs=in_specs,
        out_specs=out_specs,
        check_vma=False,
    )
```

time: 836 us -> 84.7 us (0.10)
  other arithmetic: 627 us -> 0.41 us
  waiting for transfers between devices: 139 us -> 24.9 us
  local copies, waits for them, and re-layouts: 33.4 us -> 3.33 us
  starting transfers between devices: 0.04 us -> 21.9 us
  matrix products: 21.1 us -> 0 us
  Pallas kernels: 0 us -> 20.1 us
  between operations: 14.3 us -> 0.94 us
  blocking collectives: 0 us -> 12.9 us
    another operation x18 -> x0, other arithmetic: 614 us -> none  [the longest x11 370 us: damped_factor(): jax.vmap(jnp.linalg.cholesky)(cov + DAMP * jnp.eye(size, dtype=jnp.float32))]
    psum x1 -> x0, waiting for transfers between devices: 139 us -> none  [on_device(): summed = lax.psum(flat, ('dp', 'own'))]
    ppermute x0 -> x22, waiting for transfers between devices: none -> 24.9 us  [the longest x20 24 us: swap(): return lax.ppermute(value, axis, [(0, 1), (1, 0)])]
    ppermute x0 -> x22, starting transfers between devices: none -> 21.9 us  [the longest x20 21.8 us: swap(): return lax.ppermute(value, axis, [(0, 1), (1, 0)])]
    pallas_call x0 -> x4, Pallas kernels: none -> 20.1 us  [the longest x1 11.1 us: inverses(): pl.pallas_call(functools.partial(inverse_kernel, total), in_specs=[pl.Blo...]
    another operation x10 -> x0, matrix products: 13.9 us -> none  [the longest x8 10.4 us: solve_many(): jax.scipy.linalg.cho_solve((c, True), b)]
    all_to_all x0 -> x1, blocking collectives: none -> 12.9 us  [on_device(): got = lax.all_to_all(sent, (far, second, first), 0, 0)]
    another operation x10 -> x1, local copies, waits for them, and re-layouts: 12.4 us -> 0.08 us  [on_device(): jnp.stack([index[far] * 4 + index[second] * 2 + index[first], index[core]...]
  transfers between devices with their start and end apart: 1 -> 22, of which waited for: 1 -> 12; matrix products, arithmetic and copies ran while one was open for 0% -> 1% of each run, Pallas kernels for 0% -> 13%
where the time goes in v1:
time: 84.7 us; the launch traced here: 84.4 us
  waiting for transfers between devices  24.9 us (29%)
  starting transfers between devices  21.9 us (26%)
  Pallas kernels  20.1 us (24%)
  blocking collectives  12.9 us (15%)
  local copies, waits for them, and re-layouts  3.33 us (4%)
  between operations  0.94 us (1%)
    ppermute x20, waiting for transfers between devices, swap(): return lax.ppermute(value, axis, [(0, 1), (1, 0)])  24 us
    ppermute x20, starting transfers between devices, swap(): return lax.ppermute(value, axis, [(0, 1), (1, 0)])  21.8 us
    all_to_all x1, blocking collectives, on_device(): got = lax.all_to_all(sent, (far, second, first), 0, 0)  12.9 us
    pallas_call x1, Pallas kernels, inverses(): pl.pallas_call(functools.partial(inverse_kernel, total), in_specs=[pl.Blo...  11.1 us
    pallas_call x1, Pallas kernels, gram(): pl.pallas_call(gram_kernel, grid_spec=pltpu.PrefetchScalarGridSpec(num_sc...  6.83 us
  transfers between devices with their start and end apart: 22, of which 12 were waited for; matrix products, arithmetic and copies ran while one was open for 1% of the time, Pallas kernels for 13%

profile of v1, /device:TPU:0, one launch (start us, length us, event | category | flops | bytes accessed | tf_op | source)
XLA Modules:
  0.0 84.4 jit_solution(6739438096922946218)
XLA Ops:
  0.7 1.4 %copy-done = bf16[8,768,128]{2,1,0:T(8,128)(2,1)S(1)} copy-done((bf16[8,768,128]{2,1,0:T(8,128)(2,1)S(1)}, bf16[8,768,128]{2,1,0:T(8,128)(2,1)}, u32[]{:S(2)}) %copy-start) | copy-done | bytes 1572888
  2.1 6.8 %gram.1 = (f32[2,2,2,2,64,128]{5,4,3,2,1,0:T(8,128)S(1)}, f32[2,2,2,2,64,128]{5,4,3,2,1,0:T(8,128)S(1)}, f32[2,2,2,2,64,128]{5,4,3,2,1,0:T(8,128)S(1)}, f32[2,2,...) custom-call(s32[6]{0:T(128)S(1)} %stack.27.place, ...), custom_call_target="tpu_custom_call" | custom-call | tf_op jit(solution)/shard_map/gram/pallas_call | solution.py:75
  10.8 2.9 %collective-permute-start.15 = (f32[2,2,2,32,128]{4,3,1,2,0:T(8,128)S(1)}, f32[2,2,2,32,128]{4,3,1,2,0:T(8,128)S(1)}, u32[]{:S(2)}, u32[]{:S(2)}) collective-permute-start(f32[2,2,2,32,128]{4,3,1,2,0:T(8,128)S(1)} %slice_bitcast_fusion.4), channel_id=1, source_target_pairs={{0,4},{4,0},{1,5},{5,1},{2,6},{6,2},{3,7},{7,3},{8,12},{12,8},{9,1... | collective-permute-start | bytes 393224 | tf_op jit(solution)/shard_map/ppermute | solution.py:359
  13.8 1.6 %collective-permute-start.12 = (f32[2,2,2,32,128]{4,3,1,2,0:T(8,128)S(1)}, f32[2,2,2,32,128]{4,3,1,2,0:T(8,128)S(1)}, u32[]{:S(2)}, u32[]{:S(2)}) collective-permute-start(f32[2,2,2,32,128]{4,3,1,2,0:T(8,128)S(1)} %slice_bitcast_fusion.6), channel_id=1, source_target_pairs={{0,1},{1,0},{2,3},{3,2},{4,5},{5,4},{6,7},{7,6},{8,9},{9,8},{10,11... | collective-permute-start | bytes 393224 | tf_op jit(solution)/shard_map/ppermute | solution.py:359
  15.3 2.2 %collective-permute-done.15 = f32[2,2,2,32,128]{4,3,1,2,0:T(8,128)S(1)} collective-permute-done((f32[2,2,2,32,128]{4,3,1,2,0:T(8,128)S(1)}, f32[2,2,2,32,128]{4,3,1,2,0:T(8,128)S(1)}, u32[]{:S(2)}, u32[]{:S(2)}) %collective-permute-start.15) | collective-permute-done | bytes 131104 | tf_op jit(solution)/shard_map/ppermute | solution.py:359
  17.5 1.8 %collective-permute-start.16 = (f32[2,2,32,128]{3,2,0,1:T(8,128)S(1)}, f32[2,2,32,128]{3,2,0,1:T(8,128)S(1)}, u32[]{:S(2)}, u32[]{:S(2)}) collective-permute-start(f32[2,2,32,128]{3,2,0,1:T(8,128)S(1)} %slice_bitcast_fusion.16), channel_id=1, source_target_pairs={{0,1},{1,0},{2,3},{3,2},{4,5},{5,4},{6,7},{7,6},{8,9},{9,8},{10,11... | collective-permute-start | bytes 196616 | tf_op jit(solution)/shard_map/ppermute | solution.py:359
  19.4 1.6 %collective-permute-start.13 = (f32[2,2,32,128]{3,2,0,1:T(8,128)S(1)}, f32[2,2,32,128]{3,2,0,1:T(8,128)S(1)}, u32[]{:S(2)}, u32[]{:S(2)}) collective-permute-start(f32[2,2,32,128]{3,2,0,1:T(8,128)S(1)} %slice_bitcast_fusion.18), channel_id=1, source_target_pairs={{0,4},{4,0},{1,5},{5,1},{2,6},{6,2},{3,7},{7,3},{8,12},{12,8},{9,1... | collective-permute-start | bytes 196616 | tf_op jit(solution)/shard_map/ppermute | solution.py:359
  21.9 1.8 %collective-permute-done.13 = f32[2,2,32,128]{3,2,0,1:T(8,128)S(1)} collective-permute-done((f32[2,2,32,128]{3,2,0,1:T(8,128)S(1)}, f32[2,2,32,128]{3,2,0,1:T(8,128)S(1)}, u32[]{:S(2)}, u32[]{:S(2)}) %collective-permute-start.13) | collective-permute-done | bytes 65568 | tf_op jit(solution)/shard_map/ppermute | solution.py:359
  23.7 1.6 %collective-permute-start.17 = (f32[2,64,128]{2,1,0:T(8,128)S(1)}, f32[2,64,128]{2,1,0:T(8,128)S(1)}, u32[]{:S(2)}, u32[]{:S(2)}) collective-permute-start(f32[2,64,128]{2,1,0:T(8,128)S(1)} %slice_bitcast_fusion.14), channel_id=1, source_target_pairs={{0,8},{8,0},{1,9},{9,1},{2,10},{10,2},{3,11},{11,3},{4,12},{12,4},... | collective-permute-start | bytes 196616 | tf_op jit(solution)/shard_map/ppermute | solution.py:359
  25.5 1.6 %collective-permute-start.4 = (f32[2,2,2,64,128]{4,3,1,2,0:T(8,128)S(1)}, f32[2,2,2,64,128]{4,3,1,2,0:T(8,128)S(1)}, u32[]{:S(2)}, u32[]{:S(2)}) collective-permute-start(f32[2,2,2,64,128]{4,3,1,2,0:T(8,128)S(1)} %slice_bitcast_fusion), channel_id=1, source_target_pairs={{0,4},{4,0},{1,5},{5,1},{2,6},{6,2},{3,7},{7,3},{8,12},{12,8},{9,1... | collective-permute-start | bytes 786440 | tf_op jit(solution)/shard_map/ppermute | solution.py:359
  27.8 4.1 %collective-permute-done.4 = f32[2,2,2,64,128]{4,3,1,2,0:T(8,128)S(1)} collective-permute-done((f32[2,2,2,64,128]{4,3,1,2,0:T(8,128)S(1)}, f32[2,2,2,64,128]{4,3,1,2,0:T(8,128)S(1)}, u32[]{:S(2)}, u32[]{:S(2)}) %collective-permute-start.4) | collective-permute-done | bytes 262176 | tf_op jit(solution)/shard_map/ppermute | solution.py:359
  32.0 1.3 %collective-permute-start.5 = (f32[2,2,64,128]{3,2,0,1:T(8,128)S(1)}, f32[2,2,64,128]{3,2,0,1:T(8,128)S(1)}, u32[]{:S(2)}, u32[]{:S(2)}) collective-permute-start(f32[2,2,64,128]{3,2,0,1:T(8,128)S(1)} %slice_bitcast_fusion.10), channel_id=1, source_target_pairs={{0,1},{1,0},{2,3},{3,2},{4,5},{5,4},{6,7},{7,6},{8,9},{9,8},{10,11... | collective-permute-start | bytes 393224 | tf_op jit(solution)/shard_map/ppermute | solution.py:359
  33.3 1.7 %collective-permute-done.1 = f32[2,2,2,64,128]{4,3,1,2,0:T(8,128)S(1)} collective-permute-done((f32[2,2,2,64,128]{4,3,1,2,0:T(8,128)S(1)}, f32[2,2,2,64,128]{4,3,1,2,0:T(8,128)S(1)}, u32[]{:S(2)}, u32[]{:S(2)}) %collective-permute-start.1) | collective-permute-done | bytes 262176 | tf_op jit(solution)/shard_map/ppermute | solution.py:359
  35.4 1.6 %collective-permute-done.5 = f32[2,2,64,128]{3,2,0,1:T(8,128)S(1)} collective-permute-done((f32[2,2,64,128]{3,2,0,1:T(8,128)S(1)}, f32[2,2,64,128]{3,2,0,1:T(8,128)S(1)}, u32[]{:S(2)}, u32[]{:S(2)}) %collective-permute-start.5) | collective-permute-done | bytes 131104 | tf_op jit(solution)/shard_map/ppermute | solution.py:359
  37.0 3.1 %collective-permute-done.2 = f32[2,2,64,128]{3,2,0,1:T(8,128)S(1)} collective-permute-done((f32[2,2,64,128]{3,2,0,1:T(8,128)S(1)}, f32[2,2,64,128]{3,2,0,1:T(8,128)S(1)}, u32[]{:S(2)}, u32[]{:S(2)}) %collective-permute-start.2) | collective-permute-done | bytes 131104 | tf_op jit(solution)/shard_map/ppermute | solution.py:359
  40.7 4.9 %collective-permute-done.6 = f32[2,128,128]{2,1,0:T(8,128)S(1)} collective-permute-done((f32[2,128,128]{2,1,0:T(8,128)S(1)}, f32[2,128,128]{2,1,0:T(8,128)S(1)}, u32[]{:S(2)}, u32[]{:S(2)}) %collective-permute-start.6) | collective-permute-done | bytes 131104 | tf_op jit(solution)/shard_map/ppermute | solution.py:359
  45.6 2.3 %collective-permute-start.7 = (f32[128,128]{1,0:T(8,128)S(1)}, f32[128,128]{1,0:T(8,128)S(1)}, u32[]{:S(2)}, u32[]{:S(2)}) collective-permute-start(f32[128,128]{1,0:T(8,128)S(1)} %slice_bitcast_fusion.20), channel_id=1, source_target_pairs={{0,16},{16,0},{1,17},{17,1},{2,18},{18,2},{3,19},{19,3},{4,20},{20... | collective-permute-start | bytes 196616 | tf_op jit(solution)/shard_map/ppermute | solution.py:359
  48.6 2.9 %collective-permute-done.7 = f32[128,128]{1,0:T(8,128)S(1)} collective-permute-done((f32[128,128]{1,0:T(8,128)S(1)}, f32[128,128]{1,0:T(8,128)S(1)}, u32[]{:S(2)}, u32[]{:S(2)}) %collective-permute-start.7) | collective-permute-done | bytes 65568 | tf_op jit(solution)/shard_map/ppermute | solution.py:359
  52.1 1.6 %collective-permute-start.8 = (f32[128,128]{1,0:T(8,128)S(1)}, f32[128,128]{1,0:T(8,128)S(1)}, u32[]{:S(2)}, u32[]{:S(2)}) collective-permute-start(f32[128,128]{1,0:T(8,128)S(1)} %fusion.10.refs_0_), channel_id=1, source_target_pairs={{0,8},{8,0},{1,9},{9,1},{2,10},{10,2},{3,11},{11,3},{4,12},{12,4},... | collective-permute-start | bytes 196616 | tf_op jit(solution)/shard_map/ppermute | solution.py:359
  55.3 1.0 %collective-permute-start.19 = (f32[64,128]{1,0:T(8,128)S(1)}, f32[64,128]{1,0:T(8,128)S(1)}, u32[]{:S(2)}, u32[]{:S(2)}) collective-permute-start(f32[64,128]{1,0:T(8,128)S(1)} %fusion.11.refs_0_), channel_id=1, source_target_pairs={{0,8},{8,0},{1,9},{9,1},{2,10},{10,2},{3,11},{11,3},{4,12},{12,4},... | collective-permute-start | bytes 98312 | tf_op jit(solution)/shard_map/ppermute | solution.py:359
  56.7 11.1 %inverses.1 = (f32[256,256]{1,0:T(8,128)S(1)}, f32[128,128]{1,0:T(8,128)S(1)}) custom-call(s32[6]{0:T(128)S(1)} %stack.27.place, f32[128,128]{1,0:T(8,128)S(1)} %fusion.10.refs_0_, f32[128,128]{1,0:T(8,128)S(1)} %collective-permute-done.8.refs_1_, f32[128,128]{1,0:T(8,128)S(1)} %collective-permute-done.9.refs_2_, f32[128,128]{1,0:T(8,128)S(1)} %collective-permute-done.10.refs_3_), custom_call_target="tpu_custom_call" | custom-call | tf_op jit(solution)/shard_map/inverses/pallas_call | solution.py:238
  67.8 1.2 %products.1 = f32[8,16,384]{2,1,0:T(8,128)S(1)} custom-call(s32[6]{0:T(128)S(1)} %stack.27.place, f32[256,256]{1,0:T(8,128)S(1)} %get-tuple-element.16.winv_ref, f32[128,128]{1,0:T(8,128)S(1)} %get-tuple-element.17.ninv_ref, f32[64,128]{1,0:T(8,128)S(1)} %fusion.11.refs_0_, f32[64,128]{1,0:T(8,128)S(1)} %collective-permute-done.19.refs_1_, ...), custom_call_target="tpu_custom_call" | custom-call | tf_op jit(solution)/shard_map/products/pallas_call | solution.py:303
  69.0 12.9 %all_to_all.5.got_ref = f32[8,16,384]{2,1,0:T(8,128)S(1)} all-to-all(f32[8,16,384]{2,1,0:T(8,128)S(1)} %products.1), channel_id=1, replica_groups=mesh['dp0'=2,'dp1'=2,'dp2'=2,'dp3'=2,'own0'=2] {'dp0','dp2','own0'}, dimensions={0} | all-to-all | bytes 393216 | tf_op jit(solution)/shard_map/all_to_all | solution.py:425
  81.8 1.0 %placing.1 = (f32[5,256,16]{2,1,0:T(8,128)S(1)}, f32[8,64,16]{2,1,0:T(8,128)S(1)}) custom-call(s32[6]{0:T(128)S(1)} %stack.27.place, s32[8]{0:T(128)S(1)} %copy-done.1, f32[8,16,384]{2,1,0:T(8,128)S(1)} %all_to_all.5.got_ref), custom_call_target="tpu_custom_call" | custom-call | tf_op jit(solution)/shard_map/placing/pallas_call | solution.py:344
  (66 shorter events, 9.5 us)
Async XLA Ops:
  0.7 1.4 %copy-start = (bf16[8,768,128]{2,1,0:T(8,128)(2,1)S(1)}, bf16[8,768,128]{2,1,0:T(8,128)(2,1)}, u32[]{:S(2)}) copy-start(bf16[8,768,128]{2,1,0:T(8,128)(2,1)} %narrow_ref.1) | copy-start | bytes 4718596
  9.0 1.7 %collective-permute-start.14 = (f32[2,2,2,2,32,128]{5,4,2,3,1,0:T(8,128)S(1)}, f32[2,2,2,2,32,128]{5,4,2,3,1,0:T(8,128)S(1)}, u32[]{:S(2)}, u32[]{:S(2)}) collective-permute-start(f32[2,2,2,2,32,128]{5,4,2,3,1,0:T(8,128)S(1)} %copy.11), channel_id=1, source_target_pairs={{0,2},{2,0},{1,3},{3,1},{4,6},{6,4},{5,7},{7,5},{8,10},{10,8},{9,1... | collective-permute-start | bytes 786440 | tf_op jit(solution)/shard_map/ppermute | solution.py:359
  9.6 4.2 %collective-permute-start.11 = (f32[2,2,2,2,32,128]{5,4,2,3,1,0:T(8,128)S(1)}, f32[2,2,2,2,32,128]{5,4,2,3,1,0:T(8,128)S(1)}, u32[]{:S(2)}, u32[]{:S(2)}) collective-permute-start(f32[2,2,2,2,32,128]{5,4,2,3,1,0:T(8,128)S(1)} %copy.9), channel_id=1, source_target_pairs={{0,2},{2,0},{1,3},{3,1},{4,6},{6,4},{5,7},{7,5},{8,10},{10,8},{9,1... | collective-permute-start | bytes 786440 | tf_op jit(solution)/shard_map/ppermute | solution.py:359
  9.7 15.7 %collective-permute-start.3 = (f32[2,2,2,2,64,128]{5,4,2,3,1,0:T(8,128)S(1)}, f32[2,2,2,2,64,128]{5,4,2,3,1,0:T(8,128)S(1)}, u32[]{:S(2)}, u32[]{:S(2)}) collective-permute-start(f32[2,2,2,2,64,128]{5,4,2,3,1,0:T(8,128)S(1)} %copy.7), channel_id=1, source_target_pairs={{0,2},{2,0},{1,3},{3,1},{4,6},{6,4},{5,7},{7,5},{8,10},{10,8},{9,1... | collective-permute-start | bytes 1572872 | tf_op jit(solution)/shard_map/ppermute | solution.py:359
  10.3 16.8 %collective-permute-start = (f32[2,2,2,2,64,128]{5,4,2,3,1,0:T(8,128)S(1)}, f32[2,2,2,2,64,128]{5,4,2,3,1,0:T(8,128)S(1)}, u32[]{:S(2)}, u32[]{:S(2)}) collective-permute-start(f32[2,2,2,2,64,128]{5,4,2,3,1,0:T(8,128)S(1)} %copy.5), channel_id=1, source_target_pairs={{0,2},{2,0},{1,3},{3,1},{4,6},{6,4},{5,7},{7,5},{8,10},{10,8},{9,1... | collective-permute-start | bytes 1572872 | tf_op jit(solution)/shard_map/ppermute | solution.py:359
  10.8 6.7 %collective-permute-start.15 = (f32[2,2,2,32,128]{4,3,1,2,0:T(8,128)S(1)}, f32[2,2,2,32,128]{4,3,1,2,0:T(8,128)S(1)}, u32[]{:S(2)}, u32[]{:S(2)}) collective-permute-start(f32[2,2,2,32,128]{4,3,1,2,0:T(8,128)S(1)} %slice_bitcast_fusion.4), channel_id=1, source_target_pairs={{0,4},{4,0},{1,5},{5,1},{2,6},{6,2},{3,7},{7,3},{8,12},{12,8},{9,1... | collective-permute-start | bytes 393224 | tf_op jit(solution)/shard_map/ppermute | solution.py:359
  13.8 5.6 %collective-permute-start.12 = (f32[2,2,2,32,128]{4,3,1,2,0:T(8,128)S(1)}, f32[2,2,2,32,128]{4,3,1,2,0:T(8,128)S(1)}, u32[]{:S(2)}, u32[]{:S(2)}) collective-permute-start(f32[2,2,2,32,128]{4,3,1,2,0:T(8,128)S(1)} %slice_bitcast_fusion.6), channel_id=1, source_target_pairs={{0,1},{1,0},{2,3},{3,2},{4,5},{5,4},{6,7},{7,6},{8,9},{9,8},{10,11... | collective-permute-start | bytes 393224 | tf_op jit(solution)/shard_map/ppermute | solution.py:359
  17.5 4.3 %collective-permute-start.16 = (f32[2,2,32,128]{3,2,0,1:T(8,128)S(1)}, f32[2,2,32,128]{3,2,0,1:T(8,128)S(1)}, u32[]{:S(2)}, u32[]{:S(2)}) collective-permute-start(f32[2,2,32,128]{3,2,0,1:T(8,128)S(1)} %slice_bitcast_fusion.16), channel_id=1, source_target_pairs={{0,1},{1,0},{2,3},{3,2},{4,5},{5,4},{6,7},{7,6},{8,9},{9,8},{10,11... | collective-permute-start | bytes 196616 | tf_op jit(solution)/shard_map/ppermute | solution.py:359
  19.4 4.3 %collective-permute-start.13 = (f32[2,2,32,128]{3,2,0,1:T(8,128)S(1)}, f32[2,2,32,128]{3,2,0,1:T(8,128)S(1)}, u32[]{:S(2)}, u32[]{:S(2)}) collective-permute-start(f32[2,2,32,128]{3,2,0,1:T(8,128)S(1)} %slice_bitcast_fusion.18), channel_id=1, source_target_pairs={{0,4},{4,0},{1,5},{5,1},{2,6},{6,2},{3,7},{7,3},{8,12},{12,8},{9,1... | collective-permute-start | bytes 196616 | tf_op jit(solution)/shard_map/ppermute | solution.py:359
  23.7 16.9 %collective-permute-start.17 = (f32[2,64,128]{2,1,0:T(8,128)S(1)}, f32[2,64,128]{2,1,0:T(8,128)S(1)}, u32[]{:S(2)}, u32[]{:S(2)}) collective-permute-start(f32[2,64,128]{2,1,0:T(8,128)S(1)} %slice_bitcast_fusion.14), channel_id=1, source_target_pairs={{0,8},{8,0},{1,9},{9,1},{2,10},{10,2},{3,11},{11,3},{4,12},{12,4},... | collective-permute-start | bytes 196616 | tf_op jit(solution)/shard_map/ppermute | solution.py:359
  25.5 6.4 %collective-permute-start.4 = (f32[2,2,2,64,128]{4,3,1,2,0:T(8,128)S(1)}, f32[2,2,2,64,128]{4,3,1,2,0:T(8,128)S(1)}, u32[]{:S(2)}, u32[]{:S(2)}) collective-permute-start(f32[2,2,2,64,128]{4,3,1,2,0:T(8,128)S(1)} %slice_bitcast_fusion), channel_id=1, source_target_pairs={{0,4},{4,0},{1,5},{5,1},{2,6},{6,2},{3,7},{7,3},{8,12},{12,8},{9,1... | collective-permute-start | bytes 786440 | tf_op jit(solution)/shard_map/ppermute | solution.py:359
  27.2 54.7 %copy-start.1 = (s32[8]{0:T(128)S(1)}, s32[8]{0:T(128)}, u32[]{:S(2)}) copy-start(s32[8]{0:T(128)} %owner_map.1) | copy-start | bytes 100
  27.2 7.8 %collective-permute-start.1 = (f32[2,2,2,64,128]{4,3,1,2,0:T(8,128)S(1)}, f32[2,2,2,64,128]{4,3,1,2,0:T(8,128)S(1)}, u32[]{:S(2)}, u32[]{:S(2)}) collective-permute-start(f32[2,2,2,64,128]{4,3,1,2,0:T(8,128)S(1)} %slice_bitcast_fusion.2), channel_id=1, source_target_pairs={{0,1},{1,0},{2,3},{3,2},{4,5},{5,4},{6,7},{7,6},{8,9},{9,8},{10,11... | collective-permute-start | bytes 786440 | tf_op jit(solution)/shard_map/ppermute | solution.py:359
  32.0 5.0 %collective-permute-start.5 = (f32[2,2,64,128]{3,2,0,1:T(8,128)S(1)}, f32[2,2,64,128]{3,2,0,1:T(8,128)S(1)}, u32[]{:S(2)}, u32[]{:S(2)}) collective-permute-start(f32[2,2,64,128]{3,2,0,1:T(8,128)S(1)} %slice_bitcast_fusion.10), channel_id=1, source_target_pairs={{0,1},{1,0},{2,3},{3,2},{4,5},{5,4},{6,7},{7,6},{8,9},{9,8},{10,11... | collective-permute-start | bytes 393224 | tf_op jit(solution)/shard_map/ppermute | solution.py:359
  35.1 5.0 %collective-permute-start.2 = (f32[2,2,64,128]{3,2,0,1:T(8,128)S(1)}, f32[2,2,64,128]{3,2,0,1:T(8,128)S(1)}, u32[]{:S(2)}, u32[]{:S(2)}) collective-permute-start(f32[2,2,64,128]{3,2,0,1:T(8,128)S(1)} %slice_bitcast_fusion.12), channel_id=1, source_target_pairs={{0,4},{4,0},{1,5},{5,1},{2,6},{6,2},{3,7},{7,3},{8,12},{12,8},{9,1... | collective-permute-start | bytes 393224 | tf_op jit(solution)/shard_map/ppermute | solution.py:359
  40.2 5.4 %collective-permute-start.6 = (f32[2,128,128]{2,1,0:T(8,128)S(1)}, f32[2,128,128]{2,1,0:T(8,128)S(1)}, u32[]{:S(2)}, u32[]{:S(2)}) collective-permute-start(f32[2,128,128]{2,1,0:T(8,128)S(1)} %slice_bitcast_fusion.8), channel_id=1, source_target_pairs={{0,8},{8,0},{1,9},{9,1},{2,10},{10,2},{3,11},{11,3},{4,12},{12,4},... | collective-permute-start | bytes 393224 | tf_op jit(solution)/shard_map/ppermute | solution.py:359
  45.6 5.9 %collective-permute-start.7 = (f32[128,128]{1,0:T(8,128)S(1)}, f32[128,128]{1,0:T(8,128)S(1)}, u32[]{:S(2)}, u32[]{:S(2)}) collective-permute-start(f32[128,128]{1,0:T(8,128)S(1)} %slice_bitcast_fusion.20), channel_id=1, source_target_pairs={{0,16},{16,0},{1,17},{17,1},{2,18},{18,2},{3,19},{19,3},{4,20},{20... | collective-permute-start | bytes 196616 | tf_op jit(solution)/shard_map/ppermute | solution.py:359
  47.9 5.8 %collective-permute-start.18 = (f32[64,128]{1,0:T(8,128)S(1)}, f32[64,128]{1,0:T(8,128)S(1)}, u32[]{:S(2)}, u32[]{:S(2)}) collective-permute-start(f32[64,128]{1,0:T(8,128)S(1)} %slice_bitcast_fusion.22), channel_id=1, source_target_pairs={{0,16},{16,0},{1,17},{17,1},{2,18},{18,2},{3,19},{19,3},{4,20},{20... | collective-permute-start | bytes 98312 | tf_op jit(solution)/shard_map/ppermute | solution.py:359
  51.5 3.8 %collective-permute-start.10 = (f32[128,128]{1,0:T(8,128)S(1)}, f32[128,128]{1,0:T(8,128)S(1)}, u32[]{:S(2)}, u32[]{:S(2)}) collective-permute-start(f32[128,128]{1,0:T(8,128)S(1)} %fusion.10.refs_0_), channel_id=1, source_target_pairs={{0,10},{2,8},{8,2},{10,0},{1,11},{3,9},{9,3},{11,1},{4,14},{6,12},... | collective-permute-start | bytes 196616 | tf_op jit(solution)/shard_map/ppermute | solution.py:363
  51.6 4.7 %collective-permute-start.9 = (f32[128,128]{1,0:T(8,128)S(1)}, f32[128,128]{1,0:T(8,128)S(1)}, u32[]{:S(2)}, u32[]{:S(2)}) collective-permute-start(f32[128,128]{1,0:T(8,128)S(1)} %fusion.10.refs_0_), channel_id=1, source_target_pairs={{0,2},{2,0},{1,3},{3,1},{4,6},{6,4},{5,7},{7,5},{8,10},{10,8},{9,1... | collective-permute-start | bytes 196616 | tf_op jit(solution)/shard_map/ppermute | solution.py:359
  52.1 4.5 %collective-permute-start.8 = (f32[128,128]{1,0:T(8,128)S(1)}, f32[128,128]{1,0:T(8,128)S(1)}, u32[]{:S(2)}, u32[]{:S(2)}) collective-permute-start(f32[128,128]{1,0:T(8,128)S(1)} %fusion.10.refs_0_), channel_id=1, source_target_pairs={{0,8},{8,0},{1,9},{9,1},{2,10},{10,2},{3,11},{11,3},{4,12},{12,4},... | collective-permute-start | bytes 196616 | tf_op jit(solution)/shard_map/ppermute | solution.py:359
  53.7 14.0 %collective-permute-start.21 = (f32[64,128]{1,0:T(8,128)S(1)}, f32[64,128]{1,0:T(8,128)S(1)}, u32[]{:S(2)}, u32[]{:S(2)}) collective-permute-start(f32[64,128]{1,0:T(8,128)S(1)} %fusion.11.refs_0_), channel_id=1, source_target_pairs={{0,10},{2,8},{8,2},{10,0},{1,11},{3,9},{9,3},{11,1},{4,14},{6,12},... | collective-permute-start | bytes 98312 | tf_op jit(solution)/shard_map/ppermute | solution.py:363
  53.8 14.0 %collective-permute-start.20 = (f32[64,128]{1,0:T(8,128)S(1)}, f32[64,128]{1,0:T(8,128)S(1)}, u32[]{:S(2)}, u32[]{:S(2)}) collective-permute-start(f32[64,128]{1,0:T(8,128)S(1)} %fusion.11.refs_0_), channel_id=1, source_target_pairs={{0,2},{2,0},{1,3},{3,1},{4,6},{6,4},{5,7},{7,5},{8,10},{10,8},{9,1... | collective-permute-start | bytes 98312 | tf_op jit(solution)/shard_map/ppermute | solution.py:359
  55.3 12.5 %collective-permute-start.19 = (f32[64,128]{1,0:T(8,128)S(1)}, f32[64,128]{1,0:T(8,128)S(1)}, u32[]{:S(2)}, u32[]{:S(2)}) collective-permute-start(f32[64,128]{1,0:T(8,128)S(1)} %fusion.11.refs_0_), channel_id=1, source_target_pairs={{0,8},{8,0},{1,9},{9,1},{2,10},{10,2},{3,11},{11,3},{4,12},{12,4},... | collective-permute-start | bytes 98312 | tf_op jit(solution)/shard_map/ppermute | solution.py:359

commit v2 on v1

v2 whole, which is shorter than its diff:
```python
import functools

import jax
import jax.numpy as jnp
import numpy as np
from jax import lax
from jax.experimental import pallas as pl
from jax.experimental.pallas import tpu as pltpu
from jax.sharding import PartitionSpec as P

DAMP = 0.5
LANES = 128
PANEL = 8
VMEM_LIMIT = 48 * 1024 * 1024
HIGHEST = lax.Precision.HIGHEST
VMEM = pl.BlockSpec(memory_space=pltpu.VMEM)
SMEM = pl.BlockSpec(memory_space=pltpu.SMEM)
HBM = pl.BlockSpec(memory_space=pltpu.HBM)
PARAMS = pltpu.CompilerParams(vmem_limit_bytes=VMEM_LIMIT)


class Place:
    def __init__(self, dp_names, own_names):
        self.dp, self.own = dp_names, own_names
        self.core, self.second, self.near, self.far = (
            dp_names[-1],
            dp_names[-2],
            dp_names[1],
            dp_names[0],
        )
        self.first = own_names[-1]
        used = (self.core, self.second, self.near, self.far, self.first)
        self.extra = tuple(n for n in dp_names + own_names if n not in used)

    def index(self, names):
        value = jnp.int32(0)
        for name in names:
            value = value * 2 + lax.axis_index(name)
        return value

    def layer(self):
        return self.index((self.far, self.second, self.first))

    def quarter(self):
        return self.index((self.core, self.near))


def transposed_dot(a, b, precision=None):
    return lax.dot_general(
        a, b, (((0,), (0,)), ((), ())), precision=precision, preferred_element_type=jnp.float32
    )


def read_layers(place, sources, buffers, sems):
    layer = place.layer()
    copies = []
    for i in range(buffers[0].shape[0]):
        group = [
            pltpu.make_async_copy(
                source.at[jnp.bitwise_xor(layer, i)], buffer.at[i], sems.at[i, s]
            )
            for s, (source, buffer) in enumerate(zip(sources, buffers))
        ]
        for copy in group:
            copy.start()
        copies.append(group)
    return copies


def write_quarters(place, i, flat, keep_ref, send_ref):
    rows = keep_ref.shape[3]
    quarter = place.quarter()
    for q in range(2):
        kept = pl.multiple_of(jnp.bitwise_xor(quarter, q) * rows, PANEL)
        sent = pl.multiple_of(jnp.bitwise_xor(quarter, 2 + q) * rows, PANEL)
        keep_ref[i % 4, i // 4, q] = flat[i, pl.ds(kept, rows), :]
        send_ref[i % 4, i // 4, q] = flat[i, pl.ds(sent, rows), :]


def iotas(shape):
    return (
        lax.broadcasted_iota(jnp.int32, shape, 0),
        lax.broadcasted_iota(jnp.int32, shape, 1),
    )


def pack_squares(flat, i, first, corner, second, narrow):
    n = LANES
    row, col = iotas((n, n))
    flat[i, :n] = jnp.where(row >= col, first, second)
    flat[i, n : 2 * n] = corner
    h = n // 2
    row_h, col_h = iotas((h, n))
    lower = pltpu.roll(narrow[h:], h, 1)
    flat[i, 2 * n : 2 * n + h] = jnp.where(
        (col_h >= h) | (row_h >= col_h), narrow[:h], lower
    )
    diagonal = row == col
    pair = [
        jnp.sum(jnp.where(diagonal, block, 0.0), axis=0, keepdims=True)
        for block in (second, narrow)
    ]
    row_p, _ = iotas((PANEL, n))
    shape = (PANEL, n)
    base = 2 * n + h
    flat[i, base : base + PANEL] = jnp.where(
        row_p == 0,
        jnp.broadcast_to(pair[0], shape),
        jnp.where(row_p == 1, jnp.broadcast_to(pair[1], shape), 0.0),
    )
    pad = flat.shape[1] - base - PANEL
    flat[i, base + PANEL :] = jnp.zeros((pad, n), jnp.float32)


def unpack_squares(flat):
    n = LANES
    h = n // 2
    row, col = iotas((n, n))
    packed = flat[:n]
    turned = packed.T
    corner = flat[n : 2 * n]
    folded = jnp.concatenate([flat[2 * n : 2 * n + h], jnp.zeros((h, n), jnp.float32)], axis=0)
    slab = flat[2 * n + h : 2 * n + h + PANEL]
    second_diagonal = jnp.broadcast_to(slab[0:1], (n, n))
    narrow_diagonal = jnp.broadcast_to(slab[1:2], (n, n))
    first = jnp.where(row >= col, packed, turned)
    second = jnp.where(col > row, packed, turned)
    second = jnp.where(row == col, second_diagonal, second)
    folded_t = folded.T
    top = jnp.where((col >= h) | (col <= row), folded, folded_t)
    moved = pltpu.roll(pltpu.roll(folded, h, 0), h, 1)
    moved_t = pltpu.roll(pltpu.roll(folded_t, h, 0), h, 1)
    corner_n = jnp.where(col > row, moved, moved_t)
    corner_n = jnp.where(row == col, narrow_diagonal, corner_n)
    bottom = jnp.where(col < h, folded_t, corner_n)
    return (first, corner, second, jnp.where(row < h, top, bottom))


def squares_kernel(place, wide_hbm, narrow_hbm, keep_ref, send_ref, wides, narrows, flat, sems):
    copies = read_layers(place, (wide_hbm, narrow_hbm), (wides, narrows), sems)
    for i, group in enumerate(copies):
        for copy in group:
            copy.wait()
        wide = wides[i]
        narrow = narrows[i]
        wcov = transposed_dot(wide, wide)
        ncov = transposed_dot(narrow, narrow)
        n = LANES
        pack_squares(flat, i, wcov[:n, :n], wcov[:n, n:], wcov[n:, n:], ncov)
        write_quarters(place, i, flat, keep_ref, send_ref)


def mixed_kernel(place, wide_hbm, narrow_hbm, keep_ref, send_ref, wides, narrows, flat, sems):
    copies = read_layers(place, (wide_hbm, narrow_hbm), (wides, narrows), sems)
    for i, group in enumerate(copies):
        for copy in group:
            copy.wait()
        mixed = transposed_dot(narrows[i], wides[i])
        flat[i, :LANES] = mixed[:, :LANES]
        flat[i, LANES:] = mixed[:, LANES:]
        write_quarters(place, i, flat, keep_ref, send_ref)


def gram(kernel, name, place, quarter_rows, wide_rows, narrow_rows):
    layers = wide_rows.shape[0]
    shape = jax.ShapeDtypeStruct((4, 2, 2, quarter_rows, LANES), jnp.float32)
    macs = wide_rows.shape[1] * wide_rows.shape[2] * 256
    return pl.pallas_call(
        functools.partial(kernel, place),
        in_specs=[HBM, HBM],
        out_specs=[VMEM, VMEM],
        out_shape=[shape, shape],
        scratch_shapes=[
            pltpu.VMEM(wide_rows.shape, wide_rows.dtype),
            pltpu.VMEM(narrow_rows.shape, narrow_rows.dtype),
            pltpu.VMEM((layers, 4 * quarter_rows, LANES), jnp.float32),
            pltpu.SemaphoreType.DMA((layers, 2)),
        ],
        cost_estimate=pl.CostEstimate(
            flops=2 * layers * macs, bytes_accessed=2 * wide_rows.size * 2, transcendentals=0
        ),
        compiler_params=PARAMS,
        name=name,
    )(wide_rows, narrow_rows)


def lane_gather(x, index):
    return jnp.take_along_axis(x, index, axis=1, mode="promise_in_bounds")


def trailing_update(a_ref, left_ref, right_ref, base):
    size = a_ref.shape[1]
    a_ref[pl.ds(pl.multiple_of(base, PANEL), PANEL), :] = jnp.zeros((PANEL, size), jnp.float32)
    lane = lax.broadcasted_iota(jnp.int32, (1, size), 1)
    swept = (lane >= base - PANEL) & (lane < base)
    update = transposed_dot(left_ref[...], right_ref[...])
    a_ref[PANEL : PANEL + size, :] = (
        jnp.where(swept, 0.0, a_ref[PANEL : PANEL + size, :]) - update
    )


def sweep_panel(a_ref, left_ref, right_ref, tile, step, panel):
    size = a_ref.shape[1]
    tiles = size // LANES
    first = step * PANEL
    base = tile * LANES + first
    trailing_update(a_ref, left_ref, right_ref, base)

    shape = (PANEL, LANES)
    sub = lax.broadcasted_iota(jnp.int32, shape, 0)
    lane = lax.broadcasted_iota(jnp.int32, shape, 1)
    parts = [panel[:, LANES * t : LANES * (t + 1)] for t in range(tiles)]
    rows = [
        [jnp.broadcast_to(part[k : k + 1, :], shape) for part in parts] for k in range(PANEL)
    ]
    index = [jnp.full(shape, 0, jnp.int32) + (first + i) for i in range(PANEL)]
    d = [[None] * PANEL for _ in range(PANEL)]
    for j in range(PANEL):
        for i in range(j, PANEL):
            d[i][j] = lane_gather(rows[j][tile], index[i])
    own = (lane >= first) & (lane < first + PANEL)
    q = [[None] * tiles for _ in range(PANEL)]
    factor = [[None] * PANEL for _ in range(PANEL)]
    for k in range(PANEL):
        scale = lax.rsqrt(d[k][k])
        for i in range(k + 1, PANEL):
            factor[i][k] = d[i][k] * scale
        for i in range(k + 1, PANEL):
            for j in range(k + 1, i + 1):
                d[i][j] = d[i][j] - factor[i][k] * factor[j][k]
        for t in range(tiles):
            value = rows[k][t]
            if t == tile:
                value = jnp.where(own, jnp.where(lane == first + k, -1.0, 0.0), value)
            for j in range(k):
                value = value - factor[k][j] * q[j][t]
            q[k][t] = value * scale

    packed = []
    for t in range(tiles):
        value = q[0][t]
        for k in range(1, PANEL):
            value = jnp.where(sub == k, q[k][t], value)
        packed.append(value)
    whole = jnp.concatenate(packed, axis=1) if tiles > 1 else packed[0]
    high = whole.astype(jnp.bfloat16).astype(jnp.float32)
    rest = whole - high
    middle = rest.astype(jnp.bfloat16).astype(jnp.float32)
    low = rest - middle
    left = jnp.concatenate([high, high, middle, middle, high, low], axis=0)
    right = jnp.concatenate([high, middle, high, middle, low, high], axis=0)
    left_ref[...] = left.astype(jnp.bfloat16)
    right_ref[...] = right.astype(jnp.bfloat16)

    after = pl.multiple_of(base + 2 * PANEL, PANEL)
    following = a_ref[pl.ds(after, PANEL), :]
    last = first == LANES - PANEL
    next_lane = jnp.where(last, 0, first + PANEL) + sub
    weights = []
    for k in range(PANEL):
        source = q[k][tile]
        if tile + 1 < tiles:
            source = jnp.where(last, q[k][tile + 1], source)
        weights.append(lane_gather(source, next_lane))
    result = []
    for t in range(tiles):
        value = following[:, LANES * t : LANES * (t + 1)]
        if t == tile:
            value = jnp.where(own, 0.0, value)
        terms = [weights[k] * q[k][t] for k in range(PANEL)]
        while len(terms) > 1:
            terms = [terms[i] + terms[i + 1] for i in range(0, len(terms), 2)]
        result.append(value - terms[0])
    return jnp.concatenate(result, axis=1) if tiles > 1 else result[0]


def place_pieces(place, flat, pieces):
    quarter = place.quarter()
    rows = pieces[0].shape[0]
    for r, piece in enumerate(pieces):
        start = pl.multiple_of(jnp.bitwise_xor(quarter, r) * rows, PANEL)
        flat[pl.ds(start, rows), :] = piece[...]


def first_half_kernel(place, total, *refs):
    pieces, refs = refs[:4], refs[4:]
    ninv_ref, wa, wl, wr, panel_ref, flat, na, nl, nr = refs
    place_pieces(place, flat, pieces)
    wide, narrow = wa.shape[1], na.shape[1]
    half = LANES
    first, corner, second, square = unpack_squares(flat)
    row, col = iotas((half, half))
    damp = jnp.where(row == col, DAMP, 0.0)
    wa[:PANEL] = jnp.zeros((PANEL, wide), jnp.float32)
    wa[PANEL + wide :] = jnp.zeros((PANEL, wide), jnp.float32)
    na[:PANEL] = jnp.zeros((PANEL, narrow), jnp.float32)
    na[PANEL + narrow :] = jnp.zeros((PANEL, narrow), jnp.float32)
    corner = corner / total
    wa[PANEL : PANEL + half, :half] = first / total + damp
    wa[PANEL : PANEL + half, half:] = corner
    wa[PANEL + half : PANEL + wide, :half] = corner.T
    wa[PANEL + half : PANEL + wide, half:] = second / total + damp
    na[PANEL : PANEL + narrow, :] = square / total + damp
    for ref in (wl, wr, nl, nr):
        ref[...] = jnp.zeros(ref.shape, ref.dtype)

    def both(step, carry):
        wide_panel, narrow_panel = carry
        wide_panel = sweep_panel(wa, wl, wr, 0, step, wide_panel)
        narrow_panel = sweep_panel(na, nl, nr, 0, step, narrow_panel)
        return (wide_panel, narrow_panel)

    start = (wa[PANEL : 2 * PANEL, :], na[PANEL : 2 * PANEL, :])
    panel, _ = lax.fori_loop(0, LANES // PANEL, both, start)
    panel_ref[...] = panel
    trailing_update(na, nl, nr, narrow)
    ninv_ref[...] = -na[PANEL : PANEL + narrow, :]


def second_half_kernel(wa_in, wl_in, wr_in, panel_ref, winv_ref, wa, wl, wr):
    wide = wa.shape[1]
    wa[...] = wa_in[...]
    wl[...] = wl_in[...]
    wr[...] = wr_in[...]

    def only(step, panel):
        return sweep_panel(wa, wl, wr, 1, step, panel)

    lax.fori_loop(0, LANES // PANEL, only, panel_ref[...])
    trailing_update(wa, wl, wr, wide)
    winv_ref[...] = -wa[PANEL : PANEL + wide, :]


def sweep_cost(wide):
    return pl.CostEstimate(
        flops=64 * wide * wide * wide, bytes_accessed=16 * wide * wide, transcendentals=0
    )


def first_half(place, pieces, wide, narrow, total):
    splits = 6 * PANEL
    rows = pieces[0].shape[0]
    matrix = (wide + 2 * PANEL, wide)
    return pl.pallas_call(
        functools.partial(first_half_kernel, place, total),
        in_specs=[VMEM] * 4,
        out_specs=[VMEM] * 5,
        out_shape=[
            jax.ShapeDtypeStruct((narrow, narrow), jnp.float32),
            jax.ShapeDtypeStruct(matrix, jnp.float32),
            jax.ShapeDtypeStruct((splits, wide), jnp.bfloat16),
            jax.ShapeDtypeStruct((splits, wide), jnp.bfloat16),
            jax.ShapeDtypeStruct((PANEL, wide), jnp.float32),
        ],
        scratch_shapes=[
            pltpu.VMEM((4 * rows, LANES), jnp.float32),
            pltpu.VMEM((narrow + 2 * PANEL, narrow), jnp.float32),
            pltpu.VMEM((splits, narrow), jnp.bfloat16),
            pltpu.VMEM((splits, narrow), jnp.bfloat16),
        ],
        cost_estimate=sweep_cost(wide),
        compiler_params=PARAMS,
        name="first_half",
    )(*pieces)


def second_half(wa, wl, wr, panel):
    wide = wa.shape[1]
    return pl.pallas_call(
        second_half_kernel,
        in_specs=[VMEM] * 4,
        out_specs=VMEM,
        out_shape=jax.ShapeDtypeStruct((wide, wide), jnp.float32),
        scratch_shapes=[
            pltpu.VMEM(wa.shape, wa.dtype),
            pltpu.VMEM(wl.shape, wl.dtype),
            pltpu.VMEM(wr.shape, wr.dtype),
        ],
        cost_estimate=sweep_cost(wide),
        compiler_params=PARAMS,
        name="second_half",
    )(wa, wl, wr, panel)


def aligned_rows(ref, index, count):
    if count % PANEL == 0:
        return ref[pl.ds(pl.multiple_of(index * count, count), count), :]
    per_slab = PANEL // count
    slab = ref[pl.ds(pl.multiple_of(index // per_slab * PANEL, PANEL), PANEL), :]
    value = slab[:count]
    for i in range(1, per_slab):
        value = jnp.where(index % per_slab == i, slab[i * count : (i + 1) * count], value)
    return value


def product_kernel(place, total, winv_ref, ninv_ref, *refs):
    pieces, outs, flat = refs[:4], refs[4:12], refs[12]
    place_pieces(place, flat, pieces)
    ninv = ninv_ref[...]
    half = flat.shape[0] // 2
    inner = jnp.concatenate(
        [
            transposed_dot(flat[h * half : (h + 1) * half] / total, ninv, HIGHEST)
            for h in range(2)
        ],
        axis=0,
    )
    cols, _ = outs[0].shape
    wide = winv_ref.shape[1]
    far, second = lax.axis_index(place.far), lax.axis_index(place.second)
    far_stride = 2 ** (len(place.dp) - 1)
    base = place.index(place.dp) - far * far_stride - second * 2
    for j in range(4):
        index = base + (far ^ (j // 2)) * far_stride + (second ^ (j % 2)) * 2
        picked = aligned_rows(winv_ref, index, cols)
        update = lax.dot_general(
            picked,
            inner,
            (((1,), (0,)), ((), ())),
            precision=HIGHEST,
            preferred_element_type=jnp.float32,
        )
        for x in range(2):
            outs[2 * j + x][:, :wide] = picked
            outs[2 * j + x][:, wide:] = update


def products(place, winv, ninv, pieces, cols, total):
    wide, narrow = winv.shape[0], ninv.shape[0]
    shape = jax.ShapeDtypeStruct((cols, wide + narrow), jnp.float32)
    return pl.pallas_call(
        functools.partial(product_kernel, place, total),
        in_specs=[VMEM] * 6,
        out_specs=[VMEM] * 8,
        out_shape=[shape] * 8,
        scratch_shapes=[pltpu.VMEM((2 * narrow, LANES), jnp.float32)],
        compiler_params=PARAMS,
        name="products",
    )(winv, ninv, *pieces)


def placing_kernel(place, owner_map, *refs):
    got, (kept_ref, update_ref, slot_of) = refs[:8], refs[8:]
    slots, cols, wide = kept_ref.shape
    rows = update_ref.shape[2]
    own, dp = place.index(place.own), place.index(place.dp)
    row, col = iotas((cols, wide))
    empty = jnp.where(col == row + dp * cols, 1.0 / DAMP, 0.0)
    count = jnp.int32(0)
    for l in range(len(got)):
        mine = owner_map[l] == own
        slot_of[l] = jnp.where(mine, count, -1)
        count = count + mine.astype(jnp.int32)
    layer = place.layer()
    slot = [slot_of[jnp.bitwise_xor(layer, r)] for r in range(len(got))]
    for c in range(slots):
        value = empty
        for r, ref in enumerate(got):
            value = jnp.where(slot[r] == c, ref[:, :wide], value)
        kept_ref[c] = value
    parts = (got[0].shape[1] - wide) // rows
    for r, ref in enumerate(got):
        value = ref[:, wide : wide + rows]
        for p in range(1, parts):
            value = jnp.where(own == p, ref[:, wide + p * rows : wide + (p + 1) * rows], value)
        update_ref[jnp.bitwise_xor(layer, r)] = value


def placing(place, owner_map, got, wide, slots, rows):
    cols = got[0].shape[0]
    return pl.pallas_call(
        functools.partial(placing_kernel, place),
        in_specs=[SMEM] + [VMEM] * 8,
        out_specs=[VMEM, VMEM],
        out_shape=[
            jax.ShapeDtypeStruct((slots, cols, wide), jnp.float32),
            jax.ShapeDtypeStruct((len(got), cols, rows), jnp.float32),
        ],
        scratch_shapes=[pltpu.SMEM((len(got),), jnp.int32)],
        compiler_params=PARAMS,
        name="placing",
    )(owner_map, *got)


def swap(value, *axes):
    count = 2 ** len(axes)
    name = axes if len(axes) > 1 else axes[0]
    return lax.ppermute(value, name, [(i, count - 1 - i) for i in range(count)])


def swap_parts(parts, high, low):
    return [swap(parts[1], low), swap(parts[2], high), swap(parts[3], high, low)]


def add_parts(part, got):
    return (part + got[0]) + (got[1] + got[2])


def after(value, *others):
    return lax.optimization_barrier((value,) + others)[0]


def on_device(place, wide_rows, narrow_rows, owner_map):
    layers, rows, wide = wide_rows.shape
    narrow = narrow_rows.shape[2]
    n_dp, n_own = 2 ** len(place.dp), 2 ** len(place.own)
    total = float(rows * n_dp * n_own)

    s_keep, s_send = gram(squares_kernel, "squares", place, 88, wide_rows, narrow_rows)
    s_got = swap(s_send, place.core)
    m_keep, m_send = gram(mixed_kernel, "mixed", place, 64, after(wide_rows, s_send), narrow_rows)

    s = s_keep + s_got
    s_got = swap_parts(s, place.second, place.first)
    m_got = swap(after(m_send, s), place.core)

    s = add_parts(s[0], s_got).reshape((4,) + s.shape[3:])
    s_got = swap_parts(s, place.far, place.near)
    m = after(m_keep, s) + m_got
    m_got = swap_parts(m, place.second, place.first)

    s = add_parts(s[0], s_got)
    if place.extra:
        s = lax.psum(s, place.extra)
    pieces = [
        s,
        swap(s, place.near),
        swap(s, place.core),
        swap(s, place.near, place.core),
    ]
    m = add_parts(after(m[0], s), m_got).reshape((4,) + m.shape[3:])
    m_got = swap_parts(m, place.far, place.near)

    ninv, wa, wl, wr, panel = first_half(place, pieces, wide, narrow, total)
    m = add_parts(after(m[0], panel), m_got)
    if place.extra:
        m = lax.psum(m, place.extra)
    mixed = [
        m,
        swap(m, place.near),
        swap(m, place.core),
        swap(m, place.near, place.core),
    ]
    winv = second_half(wa, wl, wr, panel)
    cols = wide // n_dp
    sent = products(place, winv, ninv, mixed, cols, total)
    got = [sent[0]]
    axes = (place.far, place.second, place.first)
    for r in range(1, layers):
        used = tuple(a for b, a in enumerate(axes) if r >> (2 - b) & 1)
        got.append(swap(sent[r], *used))
    kept, update = placing(
        place, owner_map, got, wide, layers // n_own + 1, narrow // n_own
    )
    return (jnp.swapaxes(kept, 1, 2), jnp.swapaxes(update, 1, 2))


def solution(mesh):
    n_dp, n_own = mesh.shape["dp"], mesh.shape["own"]
    dp_names = tuple(f"dp{i}" for i in range(int(np.log2(n_dp))))
    own_names = tuple(f"own{i}" for i in range(int(np.log2(n_own))))
    names = dp_names + own_names
    bits = jax.sharding.Mesh(mesh.devices.reshape((2,) * len(names)), names)
    in_specs = (P(None, names, None), P(None, names, None), P())
    out_specs = (P(own_names, None, dp_names), P(None, own_names, dp_names))
    return jax.shard_map(
        functools.partial(on_device, Place(dp_names, own_names)),
        mesh=bits,
        in_specs=in_specs,
        out_specs=out_specs,
        check_vma=False,
    )
```

time: 84.7 us -> 76.6 us (0.904)
  blocking collectives: 12.9 us -> 0 us
  waiting for transfers between devices: 24.9 us -> 13.4 us
  starting transfers between devices: 21.9 us -> 32.9 us
  Pallas kernels: 20.1 us -> 25.5 us
    all_to_all x1 -> x0, blocking collectives: 12.9 us -> none  [on_device(): got = lax.all_to_all(sent, (far, second, first), 0, 0)]
    ppermute x22 -> x27, waiting for transfers between devices: 24.9 us -> 13.4 us  [swap(): return lax.ppermute(value, name, [(i, count - 1 - i) for i in range(count)])]
    ppermute x22 -> x27, starting transfers between devices: 21.9 us -> 32.9 us  [swap(): return lax.ppermute(value, name, [(i, count - 1 - i) for i in range(count)])]
    pallas_call x4 -> x6, Pallas kernels: 20.1 us -> 25.5 us  [the longest x2 12.9 us: gram(): pl.pallas_call(functools.partial(kernel, place), in_specs=[HBM, HBM], out...]
    unnamed x4 -> x6, local copies, waits for them, and re-layouts: 1.42 us -> 3.3 us
    pallas_call x6 -> x0, local copies, waits for them, and re-layouts: 1.71 us -> none  [the longest x2 1.59 us: placing(): pl.pallas_call(placing_kernel, in_specs=[smem, smem, vmem], out_specs=[vm...]
  transfers between devices with their start and end apart: 22 -> 27, of which waited for: 12 -> 10; matrix products, arithmetic and copies ran while one was open for 1% -> 0% of each run, Pallas kernels for 13% -> 22%
where the time goes in v2:
time: 76.6 us; the launch traced here: 76.4 us
  starting transfers between devices  32.9 us (43%)
  Pallas kernels  25.5 us (33%)
  waiting for transfers between devices  13.4 us (17%)
  local copies, waits for them, and re-layouts  3.4 us (4%)
  between operations  0.84 us (1%)
    ppermute x27, starting transfers between devices, swap(): return lax.ppermute(value, name, [(i, count - 1 - i) for i in range(count)])  32.9 us
    ppermute x27, waiting for transfers between devices, swap(): return lax.ppermute(value, name, [(i, count - 1 - i) for i in range(count)])  13.4 us
    pallas_call x2, Pallas kernels, gram(): pl.pallas_call(functools.partial(kernel, place), in_specs=[HBM, HBM], out...  12.9 us
    pallas_call x1, Pallas kernels, first_half(): pl.pallas_call(functools.partial(first_half_kernel, place, total), in_spe...  6.06 us
    pallas_call x1, Pallas kernels, second_half(): pl.pallas_call(second_half_kernel, in_specs=[VMEM] * 4, out_specs=VMEM, o...  4.55 us
    unnamed x6, local copies, waits for them, and re-layouts  3.3 us
  transfers between devices with their start and end apart: 27, of which 10 were waited for; matrix products, arithmetic and copies ran while one was open for 0% of the time, Pallas kernels for 22%

profile of v2, /device:TPU:0, one launch (start us, length us, event | category | flops | bytes accessed | tf_op | source)
XLA Modules:
  0.0 76.4 jit_solution(6156550562696498479)
XLA Ops:
  0.6 1.9 %copy-done = bf16[8,768,256]{2,1,0:T(8,128)(2,1)S(1)} copy-done((bf16[8,768,256]{2,1,0:T(8,128)(2,1)S(1)}, bf16[8,768,256]{2,1,0:T(8,128)(2,1)}, u32[]{:S(2)}) %copy-start) | copy-done | bytes 3145752
  2.5 1.4 %copy-done.1 = bf16[8,768,128]{2,1,0:T(8,128)(2,1)S(1)} copy-done((bf16[8,768,128]{2,1,0:T(8,128)(2,1)S(1)}, bf16[8,768,128]{2,1,0:T(8,128)(2,1)}, u32[]{:S(2)}) %copy-start.1) | copy-done | bytes 1572888
  3.9 7.0 %squares.1 = (f32[4,2,2,88,128]{4,3,2,1,0:T(8,128)S(1)}, f32[4,2,2,88,128]{4,3,2,1,0:T(8,128)S(1)}) custom-call(bf16[8,768,256]{2,1,0:T(8,128)(2,1)S(1)} %copy-done, bf16[8,768,128]{2,1,0:T(8,128)(2,1)S(1)} %copy-done.1), custom_call_target="tpu_custom_call" | custom-call | flops 805306368 | bytes 6291456 | tf_op jit(solution)/shard_map/squares/pallas_call | solution.py:168
  11.4 1.8 %collective-permute-done = f32[4,2,2,88,128]{4,3,2,1,0:T(8,128)S(1)} collective-permute-done((f32[4,2,2,88,128]{4,3,2,1,0:T(8,128)S(1)}, f32[4,2,2,88,128]{4,3,2,1,0:T(8,128)S(1)}, u32[]{:S(2)}, u32[]{:S(2)}) %collective-permute-start) | collective-permute-done | bytes 720928 | tf_op jit(solution)/shard_map/ppermute | solution.py:488
  13.4 3.9 %collective-permute-start.3 = (f32[2,2,88,128]{3,2,1,0:T(8,128)S(1)}, f32[2,2,88,128]{3,2,1,0:T(8,128)S(1)}, u32[]{:S(2)}, u32[]{:S(2)}) collective-permute-start(f32[2,2,88,128]{3,2,1,0:T(8,128)S(1)} %get-tuple-element.50), channel_id=1, source_target_pairs={{0,5},{1,4},{4,1},{5,0},{2,7},{3,6},{6,3},{7,2},{8,13},{9,12},{12,... | collective-permute-start | bytes 540680 | tf_op jit(solution)/shard_map/ppermute | solution.py:488
  17.9 6.0 %mixed.1 = (f32[4,2,2,64,128]{4,3,2,1,0:T(8,128)S(1)}, f32[4,2,2,64,128]{4,3,2,1,0:T(8,128)S(1)}) custom-call(bf16[8,768,256]{2,1,0:T(8,128)(2,1)S(1)} %copy-done, bf16[8,768,128]{2,1,0:T(8,128)(2,1)S(1)} %copy-done.1), custom_call_target="tpu_custom_call" | custom-call | flops 805306368 | bytes 6291456 | tf_op jit(solution)/shard_map/mixed/pallas_call | solution.py:168
  24.0 2.0 %collective-permute-done.2 = f32[2,2,88,128]{3,2,1,0:T(8,128)S(1)} collective-permute-done((f32[2,2,88,128]{3,2,1,0:T(8,128)S(1)}, f32[2,2,88,128]{3,2,1,0:T(8,128)S(1)}, u32[]{:S(2)}, u32[]{:S(2)}) %collective-permute-start.2) | collective-permute-done | bytes 180256 | tf_op jit(solution)/shard_map/ppermute | solution.py:488
  26.3 3.7 %collective-permute-start.6 = (f32[88,128]{1,0:T(8,128)S(1)}, f32[88,128]{1,0:T(8,128)S(1)}, u32[]{:S(2)}, u32[]{:S(2)}) collective-permute-start(f32[88,128]{1,0:T(8,128)S(1)} %get-tuple-element.57), channel_id=1, source_target_pairs={{0,24},{8,16},{16,8},{24,0},{1,25},{9,17},{17,9},{25,1},{2,26},{10... | collective-permute-start | bytes 135176 | tf_op jit(solution)/shard_map/ppermute | solution.py:488
  30.9 1.6 %collective-permute-start.11 = (f32[2,2,64,128]{3,2,1,0:T(8,128)S(1)}, f32[2,2,64,128]{3,2,1,0:T(8,128)S(1)}, u32[]{:S(2)}, u32[]{:S(2)}) collective-permute-start(f32[2,2,64,128]{3,2,1,0:T(8,128)S(1)} %get-tuple-element.53), channel_id=1, source_target_pairs={{0,1},{1,0},{2,3},{3,2},{4,5},{5,4},{6,7},{7,6},{8,9},{9,8},{10,11... | collective-permute-start | bytes 393224 | tf_op jit(solution)/shard_map/ppermute | solution.py:488
  32.5 1.4 %collective-permute-start.13 = (f32[2,2,64,128]{3,2,1,0:T(8,128)S(1)}, f32[2,2,64,128]{3,2,1,0:T(8,128)S(1)}, u32[]{:S(2)}, u32[]{:S(2)}) collective-permute-start(f32[2,2,64,128]{3,2,1,0:T(8,128)S(1)} %get-tuple-element.54), channel_id=1, source_target_pairs={{0,5},{1,4},{4,1},{5,0},{2,7},{3,6},{6,3},{7,2},{8,13},{9,12},{12,... | collective-permute-start | bytes 393224 | tf_op jit(solution)/shard_map/ppermute | solution.py:488
  37.0 1.4 %collective-permute-start.7 = (f32[88,128]{1,0:T(8,128)S(1)}, f32[88,128]{1,0:T(8,128)S(1)}, u32[]{:S(2)}, u32[]{:S(2)}) collective-permute-start(f32[88,128]{1,0:T(8,128)S(1)} %fusion.3.refs_0_), channel_id=1, source_target_pairs={{0,8},{8,0},{1,9},{9,1},{2,10},{10,2},{3,11},{11,3},{4,12},{12,4},... | collective-permute-start | bytes 135176 | tf_op jit(solution)/shard_map/ppermute | solution.py:488
  39.4 1.3 %collective-permute-done.12 = f32[2,2,64,128]{3,2,1,0:T(8,128)S(1)} collective-permute-done((f32[2,2,64,128]{3,2,1,0:T(8,128)S(1)}, f32[2,2,64,128]{3,2,1,0:T(8,128)S(1)}, u32[]{:S(2)}, u32[]{:S(2)}) %collective-permute-start.12) | collective-permute-done | bytes 131104 | tf_op jit(solution)/shard_map/ppermute | solution.py:488
  40.8 1.5 %collective-permute-start.14 = (f32[64,128]{1,0:T(8,128)S(1)}, f32[64,128]{1,0:T(8,128)S(1)}, u32[]{:S(2)}, u32[]{:S(2)}) collective-permute-start(f32[64,128]{1,0:T(8,128)S(1)} %get-tuple-element.60), channel_id=1, source_target_pairs={{0,8},{8,0},{1,9},{9,1},{2,10},{10,2},{3,11},{11,3},{4,12},{12,4},... | collective-permute-start | bytes 98312 | tf_op jit(solution)/shard_map/ppermute | solution.py:488
  42.3 2.4 %collective-permute-start.16 = (f32[64,128]{1,0:T(8,128)S(1)}, f32[64,128]{1,0:T(8,128)S(1)}, u32[]{:S(2)}, u32[]{:S(2)}) collective-permute-start(f32[64,128]{1,0:T(8,128)S(1)} %get-tuple-element.61), channel_id=1, source_target_pairs={{0,24},{8,16},{16,8},{24,0},{1,25},{9,17},{17,9},{25,1},{2,26},{10... | collective-permute-start | bytes 98312 | tf_op jit(solution)/shard_map/ppermute | solution.py:488
  44.9 6.1 %first_half.1 = (f32[128,128]{1,0:T(8,128)S(1)}, f32[272,256]{1,0:T(8,128)S(1)}, bf16[48,256]{1,0:T(8,128)(2,1)S(1)}, bf16[48,256]{1,0:T(8,128)(2,1)S(1)}, f32[8,256]{1,0:T(8,128)S(1)}) custom-call(f32[88,128]{1,0:T(8,128)S(1)} %fusion.3.refs_0_, f32[88,128]{1,0:T(8,128)S(1)} %collective-permute-done.7.refs_1_, ...), custom_call_target="tpu_custom_call" | custom-call | flops 1073741824 | bytes 1048576 | tf_op jit(solution)/shard_map/first_half/pallas_call | solution.py:344
  51.2 1.8 %collective-permute-start.18 = (f32[64,128]{1,0:T(8,128)S(1)}, f32[64,128]{1,0:T(8,128)S(1)}, u32[]{:S(2)}, u32[]{:S(2)}) collective-permute-start(f32[64,128]{1,0:T(8,128)S(1)} %add_add_fusion.1.refs_0_), channel_id=1, source_target_pairs={{0,2},{2,0},{1,3},{3,1},{4,6},{6,4},{5,7},{7,5},{8,10},{10,8},{9,1... | collective-permute-start | bytes 98312 | tf_op jit(solution)/shard_map/ppermute | solution.py:488
  53.3 4.5 %second_half.1.winv_ref = f32[256,256]{1,0:T(8,128)S(1)} custom-call(f32[272,256]{1,0:T(8,128)S(1)} %get-tuple-element.28.wa_in, bf16[48,256]{1,0:T(8,128)(2,1)S(1)} %get-tuple-element.29.wl_in, bf16[48,256]{1,0:T(8,128)(2,1)S(1)} %get-tuple-element.30.wr_in, f32[8,256]{1,0:T(8,128)S(1)} %get-tuple-element.31.panel_ref), custom_call_target="tpu_custom_call" | custom-call | flops 1073741824 | bytes 1048576 | tf_op jit(solution)/shard_map/second_half/pallas_call | solution.py:369
  58.9 1.7 %collective-permute-start.21 = (f32[16,384]{1,0:T(8,128)S(1)}, f32[16,384]{1,0:T(8,128)S(1)}, u32[]{:S(2)}, u32[]{:S(2)}) collective-permute-start(f32[16,384]{1,0:T(8,128)S(1)} %get-tuple-element.42), channel_id=1, source_target_pairs={{0,4},{4,0},{1,5},{5,1},{2,6},{6,2},{3,7},{7,3},{8,12},{12,8},{9,1... | collective-permute-start | bytes 73736 | tf_op jit(solution)/shard_map/ppermute | solution.py:488
  60.6 1.5 %collective-permute-start.22 = (f32[16,384]{1,0:T(8,128)S(1)}, f32[16,384]{1,0:T(8,128)S(1)}, u32[]{:S(2)}, u32[]{:S(2)}) collective-permute-start(f32[16,384]{1,0:T(8,128)S(1)} %get-tuple-element.43), channel_id=1, source_target_pairs={{0,5},{1,4},{4,1},{5,0},{2,7},{3,6},{6,3},{7,2},{8,13},{9,12},{12,... | collective-permute-start | bytes 73736 | tf_op jit(solution)/shard_map/ppermute | solution.py:488
  62.1 2.6 %collective-permute-start.23 = (f32[16,384]{1,0:T(8,128)S(1)}, f32[16,384]{1,0:T(8,128)S(1)}, u32[]{:S(2)}, u32[]{:S(2)}) collective-permute-start(f32[16,384]{1,0:T(8,128)S(1)} %get-tuple-element.44), channel_id=1, source_target_pairs={{0,16},{16,0},{1,17},{17,1},{2,18},{18,2},{3,19},{19,3},{4,20},{20... | collective-permute-start | bytes 73736 | tf_op jit(solution)/shard_map/ppermute | solution.py:488
  64.7 3.8 %collective-permute-start.25 = (f32[16,384]{1,0:T(8,128)S(1)}, f32[16,384]{1,0:T(8,128)S(1)}, u32[]{:S(2)}, u32[]{:S(2)}) collective-permute-start(f32[16,384]{1,0:T(8,128)S(1)} %get-tuple-element.46), channel_id=1, source_target_pairs={{0,20},{4,16},{16,4},{20,0},{1,21},{5,17},{17,5},{21,1},{2,22},{6,... | collective-permute-start | bytes 73736 | tf_op jit(solution)/shard_map/ppermute | solution.py:488
  68.5 1.2 %collective-permute-start.26 = (f32[16,384]{1,0:T(8,128)S(1)}, f32[16,384]{1,0:T(8,128)S(1)}, u32[]{:S(2)}, u32[]{:S(2)}) collective-permute-start(f32[16,384]{1,0:T(8,128)S(1)} %get-tuple-element.47), channel_id=1, source_target_pairs={{0,21},{1,20},{4,17},{5,16},{16,5},{17,4},{20,1},{21,0},{2,23},{3,... | collective-permute-start | bytes 73736 | tf_op jit(solution)/shard_map/ppermute | solution.py:488
  70.8 4.2 %collective-permute-done.26.refs_7_ = f32[16,384]{1,0:T(8,128)S(1)} collective-permute-done((f32[16,384]{1,0:T(8,128)S(1)}, f32[16,384]{1,0:T(8,128)S(1)}, u32[]{:S(2)}, u32[]{:S(2)}) %collective-permute-start.26) | collective-permute-done | bytes 24608 | tf_op jit(solution)/shard_map/ppermute | solution.py:488
  75.1 1.3 %placing.1 = (f32[5,16,256]{2,1,0:T(8,128)}, f32[8,16,64]{2,1,0:T(8,128)}) custom-call(s32[8]{0:T(128)S(1)} %copy-done.2, f32[16,384]{1,0:T(8,128)S(1)} %get-tuple-element.40.refs_0_, f32[16,384]{1,0:T(8,128)S(1)} %collective-permute-done.20.refs_1_, f32[16,384]{1,0:T(8,128)S(1)} %collective-permute-done.21.refs_2_, ...), custom_call_target="tpu_custom_call" | custom-call | tf_op jit(solution)/shard_map/placing/pallas_call | solution.py:471
  (52 shorter events, 9.6 us)
Async XLA Ops:
  13.4 10.6 %collective-permute-start.3 = (f32[2,2,88,128]{3,2,1,0:T(8,128)S(1)}, f32[2,2,88,128]{3,2,1,0:T(8,128)S(1)}, u32[]{:S(2)}, u32[]{:S(2)}) collective-permute-start(f32[2,2,88,128]{3,2,1,0:T(8,128)S(1)} %get-tuple-element.50), channel_id=1, source_target_pairs={{0,5},{1,4},{4,1},{5,0},{2,7},{3,6},{6,3},{7,2},{8,13},{9,12},{12,... | collective-permute-start | bytes 540680 | tf_op jit(solution)/shard_map/ppermute | solution.py:488
  17.3 8.7 %collective-permute-start.2 = (f32[2,2,88,128]{3,2,1,0:T(8,128)S(1)}, f32[2,2,88,128]{3,2,1,0:T(8,128)S(1)}, u32[]{:S(2)}, u32[]{:S(2)}) collective-permute-start(f32[2,2,88,128]{3,2,1,0:T(8,128)S(1)} %get-tuple-element.51), channel_id=1, source_target_pairs={{0,4},{4,0},{1,5},{5,1},{2,6},{6,2},{3,7},{7,3},{8,12},{12,8},{9,1... | collective-permute-start | bytes 540680 | tf_op jit(solution)/shard_map/ppermute | solution.py:488
  17.8 8.5 %collective-permute-start.1 = (f32[2,2,88,128]{3,2,1,0:T(8,128)S(1)}, f32[2,2,88,128]{3,2,1,0:T(8,128)S(1)}, u32[]{:S(2)}, u32[]{:S(2)}) collective-permute-start(f32[2,2,88,128]{3,2,1,0:T(8,128)S(1)} %get-tuple-element.52), channel_id=1, source_target_pairs={{0,1},{1,0},{2,3},{3,2},{4,5},{5,4},{6,7},{7,6},{8,9},{9,8},{10,11... | collective-permute-start | bytes 540680 | tf_op jit(solution)/shard_map/ppermute | solution.py:488
  23.9 6.9 %collective-permute-start.10 = (f32[4,2,2,64,128]{4,3,2,1,0:T(8,128)S(1)}, f32[4,2,2,64,128]{4,3,2,1,0:T(8,128)S(1)}, u32[]{:S(2)}, u32[]{:S(2)}) collective-permute-start(f32[4,2,2,64,128]{4,3,2,1,0:T(8,128)S(1)} %get-tuple-element.37), channel_id=1, source_target_pairs={{0,2},{2,0},{1,3},{3,1},{4,6},{6,4},{5,7},{7,5},{8,10},{10,8},{9,1... | collective-permute-start | bytes 1572872 | tf_op jit(solution)/shard_map/ppermute | solution.py:488
  26.3 7.5 %collective-permute-start.6 = (f32[88,128]{1,0:T(8,128)S(1)}, f32[88,128]{1,0:T(8,128)S(1)}, u32[]{:S(2)}, u32[]{:S(2)}) collective-permute-start(f32[88,128]{1,0:T(8,128)S(1)} %get-tuple-element.57), channel_id=1, source_target_pairs={{0,24},{8,16},{16,8},{24,0},{1,25},{9,17},{17,9},{25,1},{2,26},{10... | collective-permute-start | bytes 135176 | tf_op jit(solution)/shard_map/ppermute | solution.py:488
  30.0 4.9 %collective-permute-start.5 = (f32[88,128]{1,0:T(8,128)S(1)}, f32[88,128]{1,0:T(8,128)S(1)}, u32[]{:S(2)}, u32[]{:S(2)}) collective-permute-start(f32[88,128]{1,0:T(8,128)S(1)} %get-tuple-element.58), channel_id=1, source_target_pairs={{0,16},{16,0},{1,17},{17,1},{2,18},{18,2},{3,19},{19,3},{4,20},{20... | collective-permute-start | bytes 135176 | tf_op jit(solution)/shard_map/ppermute | solution.py:488
  30.9 6.1 %collective-permute-start.11 = (f32[2,2,64,128]{3,2,1,0:T(8,128)S(1)}, f32[2,2,64,128]{3,2,1,0:T(8,128)S(1)}, u32[]{:S(2)}, u32[]{:S(2)}) collective-permute-start(f32[2,2,64,128]{3,2,1,0:T(8,128)S(1)} %get-tuple-element.53), channel_id=1, source_target_pairs={{0,1},{1,0},{2,3},{3,2},{4,5},{5,4},{6,7},{7,6},{8,9},{9,8},{10,11... | collective-permute-start | bytes 393224 | tf_op jit(solution)/shard_map/ppermute | solution.py:488
  32.5 7.0 %collective-permute-start.13 = (f32[2,2,64,128]{3,2,1,0:T(8,128)S(1)}, f32[2,2,64,128]{3,2,1,0:T(8,128)S(1)}, u32[]{:S(2)}, u32[]{:S(2)}) collective-permute-start(f32[2,2,64,128]{3,2,1,0:T(8,128)S(1)} %get-tuple-element.54), channel_id=1, source_target_pairs={{0,5},{1,4},{4,1},{5,0},{2,7},{3,6},{6,3},{7,2},{8,13},{9,12},{12,... | collective-permute-start | bytes 393224 | tf_op jit(solution)/shard_map/ppermute | solution.py:488
  33.9 6.9 %collective-permute-start.12 = (f32[2,2,64,128]{3,2,1,0:T(8,128)S(1)}, f32[2,2,64,128]{3,2,1,0:T(8,128)S(1)}, u32[]{:S(2)}, u32[]{:S(2)}) collective-permute-start(f32[2,2,64,128]{3,2,1,0:T(8,128)S(1)} %get-tuple-element.55), channel_id=1, source_target_pairs={{0,4},{4,0},{1,5},{5,1},{2,6},{6,2},{3,7},{7,3},{8,12},{12,8},{9,1... | collective-permute-start | bytes 393224 | tf_op jit(solution)/shard_map/ppermute | solution.py:488
  35.0 9.7 %collective-permute-start.9 = (f32[88,128]{1,0:T(8,128)S(1)}, f32[88,128]{1,0:T(8,128)S(1)}, u32[]{:S(2)}, u32[]{:S(2)}) collective-permute-start(f32[88,128]{1,0:T(8,128)S(1)} %fusion.3.refs_0_), channel_id=1, source_target_pairs={{0,10},{2,8},{8,2},{10,0},{1,11},{3,9},{9,3},{11,1},{4,14},{6,12},... | collective-permute-start | bytes 135176 | tf_op jit(solution)/shard_map/ppermute | solution.py:488
  35.1 9.9 %collective-permute-start.8 = (f32[88,128]{1,0:T(8,128)S(1)}, f32[88,128]{1,0:T(8,128)S(1)}, u32[]{:S(2)}, u32[]{:S(2)}) collective-permute-start(f32[88,128]{1,0:T(8,128)S(1)} %fusion.3.refs_0_), channel_id=1, source_target_pairs={{0,2},{2,0},{1,3},{3,1},{4,6},{6,4},{5,7},{7,5},{8,10},{10,8},{9,1... | collective-permute-start | bytes 135176 | tf_op jit(solution)/shard_map/ppermute | solution.py:488
  37.0 7.9 %collective-permute-start.7 = (f32[88,128]{1,0:T(8,128)S(1)}, f32[88,128]{1,0:T(8,128)S(1)}, u32[]{:S(2)}, u32[]{:S(2)}) collective-permute-start(f32[88,128]{1,0:T(8,128)S(1)} %fusion.3.refs_0_), channel_id=1, source_target_pairs={{0,8},{8,0},{1,9},{9,1},{2,10},{10,2},{3,11},{11,3},{4,12},{12,4},... | collective-permute-start | bytes 135176 | tf_op jit(solution)/shard_map/ppermute | solution.py:488
  40.8 10.2 %collective-permute-start.14 = (f32[64,128]{1,0:T(8,128)S(1)}, f32[64,128]{1,0:T(8,128)S(1)}, u32[]{:S(2)}, u32[]{:S(2)}) collective-permute-start(f32[64,128]{1,0:T(8,128)S(1)} %get-tuple-element.60), channel_id=1, source_target_pairs={{0,8},{8,0},{1,9},{9,1},{2,10},{10,2},{3,11},{11,3},{4,12},{12,4},... | collective-permute-start | bytes 98312 | tf_op jit(solution)/shard_map/ppermute | solution.py:488
  42.3 8.8 %collective-permute-start.16 = (f32[64,128]{1,0:T(8,128)S(1)}, f32[64,128]{1,0:T(8,128)S(1)}, u32[]{:S(2)}, u32[]{:S(2)}) collective-permute-start(f32[64,128]{1,0:T(8,128)S(1)} %get-tuple-element.61), channel_id=1, source_target_pairs={{0,24},{8,16},{16,8},{24,0},{1,25},{9,17},{17,9},{25,1},{2,26},{10... | collective-permute-start | bytes 98312 | tf_op jit(solution)/shard_map/ppermute | solution.py:488
  44.6 6.4 %collective-permute-start.15 = (f32[64,128]{1,0:T(8,128)S(1)}, f32[64,128]{1,0:T(8,128)S(1)}, u32[]{:S(2)}, u32[]{:S(2)}) collective-permute-start(f32[64,128]{1,0:T(8,128)S(1)} %get-tuple-element.62), channel_id=1, source_target_pairs={{0,16},{16,0},{1,17},{17,1},{2,18},{18,2},{3,19},{19,3},{4,20},{20... | collective-permute-start | bytes 98312 | tf_op jit(solution)/shard_map/ppermute | solution.py:488
  51.1 6.8 %collective-permute-start.19 = (f32[64,128]{1,0:T(8,128)S(1)}, f32[64,128]{1,0:T(8,128)S(1)}, u32[]{:S(2)}, u32[]{:S(2)}) collective-permute-start(f32[64,128]{1,0:T(8,128)S(1)} %add_add_fusion.1.refs_0_), channel_id=1, source_target_pairs={{0,10},{2,8},{8,2},{10,0},{1,11},{3,9},{9,3},{11,1},{4,14},{6,12},... | collective-permute-start | bytes 98312 | tf_op jit(solution)/shard_map/ppermute | solution.py:488
  51.2 6.7 %collective-permute-start.18 = (f32[64,128]{1,0:T(8,128)S(1)}, f32[64,128]{1,0:T(8,128)S(1)}, u32[]{:S(2)}, u32[]{:S(2)}) collective-permute-start(f32[64,128]{1,0:T(8,128)S(1)} %add_add_fusion.1.refs_0_), channel_id=1, source_target_pairs={{0,2},{2,0},{1,3},{3,1},{4,6},{6,4},{5,7},{7,5},{8,10},{10,8},{9,1... | collective-permute-start | bytes 98312 | tf_op jit(solution)/shard_map/ppermute | solution.py:488
  58.5 6.2 %collective-permute-start.20 = (f32[16,384]{1,0:T(8,128)S(1)}, f32[16,384]{1,0:T(8,128)S(1)}, u32[]{:S(2)}, u32[]{:S(2)}) collective-permute-start(f32[16,384]{1,0:T(8,128)S(1)} %get-tuple-element.41), channel_id=1, source_target_pairs={{0,1},{1,0},{2,3},{3,2},{4,5},{5,4},{6,7},{7,6},{8,9},{9,8},{10,11... | collective-permute-start | bytes 73736 | tf_op jit(solution)/shard_map/ppermute | solution.py:488
  58.9 9.6 %collective-permute-start.21 = (f32[16,384]{1,0:T(8,128)S(1)}, f32[16,384]{1,0:T(8,128)S(1)}, u32[]{:S(2)}, u32[]{:S(2)}) collective-permute-start(f32[16,384]{1,0:T(8,128)S(1)} %get-tuple-element.42), channel_id=1, source_target_pairs={{0,4},{4,0},{1,5},{5,1},{2,6},{6,2},{3,7},{7,3},{8,12},{12,8},{9,1... | collective-permute-start | bytes 73736 | tf_op jit(solution)/shard_map/ppermute | solution.py:488
  60.6 9.1 %collective-permute-start.22 = (f32[16,384]{1,0:T(8,128)S(1)}, f32[16,384]{1,0:T(8,128)S(1)}, u32[]{:S(2)}, u32[]{:S(2)}) collective-permute-start(f32[16,384]{1,0:T(8,128)S(1)} %get-tuple-element.43), channel_id=1, source_target_pairs={{0,5},{1,4},{4,1},{5,0},{2,7},{3,6},{6,3},{7,2},{8,13},{9,12},{12,... | collective-permute-start | bytes 73736 | tf_op jit(solution)/shard_map/ppermute | solution.py:488
  62.1 7.7 %collective-permute-start.23 = (f32[16,384]{1,0:T(8,128)S(1)}, f32[16,384]{1,0:T(8,128)S(1)}, u32[]{:S(2)}, u32[]{:S(2)}) collective-permute-start(f32[16,384]{1,0:T(8,128)S(1)} %get-tuple-element.44), channel_id=1, source_target_pairs={{0,16},{16,0},{1,17},{17,1},{2,18},{18,2},{3,19},{19,3},{4,20},{20... | collective-permute-start | bytes 73736 | tf_op jit(solution)/shard_map/ppermute | solution.py:488
  64.7 5.6 %collective-permute-start.24 = (f32[16,384]{1,0:T(8,128)S(1)}, f32[16,384]{1,0:T(8,128)S(1)}, u32[]{:S(2)}, u32[]{:S(2)}) collective-permute-start(f32[16,384]{1,0:T(8,128)S(1)} %get-tuple-element.45), channel_id=1, source_target_pairs={{0,17},{1,16},{16,1},{17,0},{2,19},{3,18},{18,3},{19,2},{4,21},{5,... | collective-permute-start | bytes 73736 | tf_op jit(solution)/shard_map/ppermute | solution.py:488
  64.7 6.1 %collective-permute-start.25 = (f32[16,384]{1,0:T(8,128)S(1)}, f32[16,384]{1,0:T(8,128)S(1)}, u32[]{:S(2)}, u32[]{:S(2)}) collective-permute-start(f32[16,384]{1,0:T(8,128)S(1)} %get-tuple-element.46), channel_id=1, source_target_pairs={{0,20},{4,16},{16,4},{20,0},{1,21},{5,17},{17,5},{21,1},{2,22},{6,... | collective-permute-start | bytes 73736 | tf_op jit(solution)/shard_map/ppermute | solution.py:488
  68.5 6.5 %collective-permute-start.26 = (f32[16,384]{1,0:T(8,128)S(1)}, f32[16,384]{1,0:T(8,128)S(1)}, u32[]{:S(2)}, u32[]{:S(2)}) collective-permute-start(f32[16,384]{1,0:T(8,128)S(1)} %get-tuple-element.47), channel_id=1, source_target_pairs={{0,21},{1,20},{4,17},{5,16},{16,5},{17,4},{20,1},{21,0},{2,23},{3,... | collective-permute-start | bytes 73736 | tf_op jit(solution)/shard_map/ppermute | solution.py:488
  (6 other events, 39.5 us)

commit v3 on v2

--- a/solution.py
+++ b/solution.py
@@ -150,30 +150,33 @@
         write_quarters(place, i, flat, keep_ref, send_ref)
 
 
-def mixed_kernel(place, wide_hbm, narrow_hbm, keep_ref, send_ref, wides, narrows, flat, sems):
+def mixed_kernel(place, wide_hbm, narrow_hbm, out_ref, wides, narrows, sems):
     copies = read_layers(place, (wide_hbm, narrow_hbm), (wides, narrows), sems)
+    rows = out_ref.shape[5]
+    layer = place.layer()
     for i, group in enumerate(copies):
         for copy in group:
             copy.wait()
         mixed = transposed_dot(narrows[i], wides[i])
-        flat[i, :LANES] = mixed[:, :LANES]
-        flat[i, LANES:] = mixed[:, LANES:]
-        write_quarters(place, i, flat, keep_ref, send_ref)
-
-
-def gram(kernel, name, place, quarter_rows, wide_rows, narrow_rows):
+        here = jnp.bitwise_xor(layer, i)
+        for q in range(4):
+            core, near = q // 2, q % 2
+            part = mixed[near * rows : (near + 1) * rows, core * LANES : (core + 1) * LANES]
+            out_ref[here // 4, near, (here // 2) % 2, core, here % 2] = part
+
+
+def gram(kernel, name, place, out_shapes, extra_scratch, wide_rows, narrow_rows):
     layers = wide_rows.shape[0]
-    shape = jax.ShapeDtypeStruct((4, 2, 2, quarter_rows, LANES), jnp.float32)
     macs = wide_rows.shape[1] * wide_rows.shape[2] * 256
     return pl.pallas_call(
         functools.partial(kernel, place),
         in_specs=[HBM, HBM],
-        out_specs=[VMEM, VMEM],
-        out_shape=[shape, shape],
+        out_specs=[VMEM] * len(out_shapes),
+        out_shape=[jax.ShapeDtypeStruct(shape, jnp.float32) for shape in out_shapes],
         scratch_shapes=[
             pltpu.VMEM(wide_rows.shape, wide_rows.dtype),
             pltpu.VMEM(narrow_rows.shape, narrow_rows.dtype),
-            pltpu.VMEM((layers, 4 * quarter_rows, LANES), jnp.float32),
+            *extra_scratch,
             pltpu.SemaphoreType.DMA((layers, 2)),
         ],
         cost_estimate=pl.CostEstimate(
@@ -181,7 +184,10 @@
         ),
         compiler_params=PARAMS,
         name=name,
-    )(wide_rows, narrow_rows)
+    )(
+        pltpu.with_memory_space_constraint(wide_rows, pltpu.HBM),
+        pltpu.with_memory_space_constraint(narrow_rows, pltpu.HBM),
+    )
 
 
 def lane_gather(x, index):
@@ -393,25 +399,32 @@
     return value
 
 
-def product_kernel(place, total, winv_ref, ninv_ref, *refs):
-    pieces, outs, flat = refs[:4], refs[4:12], refs[12]
-    place_pieces(place, flat, pieces)
+def packs(cols, rows):
+    return cols == 2 * PANEL and 2 * rows == LANES
+
+
+def product_kernel(place, total, rows, winv_ref, ninv_ref, mixed_ref, out_ref):
     ninv = ninv_ref[...]
-    half = flat.shape[0] // 2
+    half = mixed_ref.shape[0]
     inner = jnp.concatenate(
         [
-            transposed_dot(flat[h * half : (h + 1) * half] / total, ninv, HIGHEST)
-            for h in range(2)
+            transposed_dot(
+                jnp.concatenate([mixed_ref[n, c] for n in range(half)], axis=0) / total,
+                ninv,
+                HIGHEST,
+            )
+            for c in range(2)
         ],
         axis=0,
     )
-    cols, _ = outs[0].shape
     wide = winv_ref.shape[1]
+    cols = wide // 2 ** len(place.dp)
     far, second = lax.axis_index(place.far), lax.axis_index(place.second)
     far_stride = 2 ** (len(place.dp) - 1)
     base = place.index(place.dp) - far * far_stride - second * 2
+    _, lane = iotas((PANEL, LANES))
     for j in range(4):
-        index = base + (far ^ (j // 2)) * far_stride + (second ^ (j % 2)) * 2
+        index = base + (j // 2) * far_stride + (j % 2) * 2
         picked = aligned_rows(winv_ref, index, cols)
         update = lax.dot_general(
             picked,
@@ -421,65 +434,77 @@
             preferred_element_type=jnp.float32,
         )
         for x in range(2):
-            outs[2 * j + x][:, :wide] = picked
-            outs[2 * j + x][:, wide:] = update
-
-
-def products(place, winv, ninv, pieces, cols, total):
-    wide, narrow = winv.shape[0], ninv.shape[0]
-    shape = jax.ShapeDtypeStruct((cols, wide + narrow), jnp.float32)
+            block = 2 * j + x
+            out_ref[block, :cols] = picked[:, :LANES]
+            out_ref[block, cols : 2 * cols] = picked[:, LANES:]
+            if packs(cols, rows):
+                upper, lower = update[:PANEL], update[PANEL:]
+                if x == 0:
+                    lower = pltpu.roll(lower, rows, 1)
+                else:
+                    upper = pltpu.roll(upper, rows, 1)
+                out_ref[block, 2 * cols :] = jnp.where(lane < rows, upper, lower)
+            else:
+                out_ref[block, 2 * cols :] = update
+
+
+def products(place, winv, ninv, mixed, cols, rows, total):
+    height = 2 * cols + (PANEL if packs(cols, rows) else cols)
     return pl.pallas_call(
-        functools.partial(product_kernel, place, total),
-        in_specs=[VMEM] * 6,
-        out_specs=[VMEM] * 8,
-        out_shape=[shape] * 8,
-        scratch_shapes=[pltpu.VMEM((2 * narrow, LANES), jnp.float32)],
+        functools.partial(product_kernel, place, total, rows),
+        in_specs=[VMEM] * 3,
+        out_specs=VMEM,
+        out_shape=jax.ShapeDtypeStruct((8, height, LANES), jnp.float32),
         compiler_params=PARAMS,
         name="products",
-    )(winv, ninv, *pieces)
-
-
-def placing_kernel(place, owner_map, *refs):
-    got, (kept_ref, update_ref, slot_of) = refs[:8], refs[8:]
+    )(winv, ninv, mixed)
+
+
+def placing_kernel(place, owner_map, got_ref, kept_ref, update_ref):
+    layers = got_ref.shape[0]
     slots, cols, wide = kept_ref.shape
     rows = update_ref.shape[2]
     own, dp = place.index(place.own), place.index(place.dp)
     row, col = iotas((cols, wide))
     empty = jnp.where(col == row + dp * cols, 1.0 / DAMP, 0.0)
     count = jnp.int32(0)
-    for l in range(len(got)):
+    slot = []
+    for l in range(layers):
         mine = owner_map[l] == own
-        slot_of[l] = jnp.where(mine, count, -1)
+        slot.append(jnp.where(mine, count, -1))
         count = count + mine.astype(jnp.int32)
-    layer = place.layer()
-    slot = [slot_of[jnp.bitwise_xor(layer, r)] for r in range(len(got))]
-    for c in range(slots):
-        value = empty
-        for r, ref in enumerate(got):
-            value = jnp.where(slot[r] == c, ref[:, :wide], value)
-        kept_ref[c] = value
-    parts = (got[0].shape[1] - wide) // rows
-    for r, ref in enumerate(got):
-        value = ref[:, wide : wide + rows]
-        for p in range(1, parts):
-            value = jnp.where(own == p, ref[:, wide + p * rows : wide + (p + 1) * rows], value)
-        update_ref[jnp.bitwise_xor(layer, r)] = value
-
-
-def placing(place, owner_map, got, wide, slots, rows):
-    cols = got[0].shape[0]
+    for h in range(2):
+        lanes = slice(h * LANES, (h + 1) * LANES)
+        for c in range(slots):
+            value = empty[:, lanes]
+            for l in range(layers):
+                value = jnp.where(slot[l] == c, got_ref[l, h * cols : (h + 1) * cols], value)
+            kept_ref[c, :, lanes] = value
+    for l in range(layers):
+        value = got_ref[l, 2 * cols :]
+        if packs(cols, rows):
+            update_ref[l, :PANEL] = value[:, :rows]
+            update_ref[l, PANEL:] = value[:, rows:]
+        else:
+            part = value[:, :rows]
+            for p in range(1, LANES // rows):
+                part = jnp.where(own == p, value[:, p * rows : (p + 1) * rows], part)
+            update_ref[l] = part
+
+
+def placing(place, owner_map, got, wide, cols, slots, rows):
+    layers = got.shape[0]
     return pl.pallas_call(
         functools.partial(placing_kernel, place),
-        in_specs=[SMEM] + [VMEM] * 8,
+        in_specs=[SMEM, VMEM],
         out_specs=[VMEM, VMEM],
         out_shape=[
             jax.ShapeDtypeStruct((slots, cols, wide), jnp.float32),
-            jax.ShapeDtypeStruct((len(got), cols, rows), jnp.float32),
+            jax.ShapeDtypeStruct((layers, cols, rows), jnp.float32),
         ],
-        scratch_shapes=[pltpu.SMEM((len(got),), jnp.int32)],
         compiler_params=PARAMS,
         name="placing",
-    )(owner_map, *got)
+    )(owner_map, got)
 
 
 def swap(value, *axes):
@@ -506,19 +531,40 @@
     n_dp, n_own = 2 ** len(place.dp), 2 ** len(place.own)
     total = float(rows * n_dp * n_own)
 
-    s_keep, s_send = gram(squares_kernel, "squares", place, 88, wide_rows, narrow_rows)
+    quarter = 88
+    split = (4, 2, 2, quarter, LANES)
+    s_keep, s_send = gram(
+        squares_kernel,
+        "squares",
+        place,
+        [split, split],
+        [pltpu.VMEM((layers, 4 * quarter, LANES), jnp.float32)],
+        wide_rows,
+        narrow_rows,
+    )
     s_got = swap(s_send, place.core)
-    m_keep, m_send = gram(mixed_kernel, "mixed", place, 64, after(wide_rows, s_send), narrow_rows)
+    group = (place.far, place.near, place.second, place.core, place.first)
+    (m,) = gram(
+        mixed_kernel,
+        "mixed",
+        place,
+        [(2, 2, 2, 2, 2, narrow // 2, LANES)],
+        [],
+        after(wide_rows, s_send),
+        narrow_rows,
+    )
+    s_keep, m = lax.optimization_barrier((s_keep, m))
+    m = m.reshape((-1,) + m.shape[5:])
+    m = lax.psum_scatter(m, group, scatter_dimension=0, tiled=True)
+    if place.extra:
+        m = lax.psum(m, place.extra)
+    m = lax.all_gather(m[0], (place.near, place.core))
+    m = m.reshape((2, 2) + m.shape[1:])
 
     s = s_keep + s_got
     s_got = swap_parts(s, place.second, place.first)
-    m_got = swap(after(m_send, s), place.core)
-
     s = add_parts(s[0], s_got).reshape((4,) + s.shape[3:])
     s_got = swap_parts(s, place.far, place.near)
-    m = after(m_keep, s) + m_got
-    m_got = swap_parts(m, place.second, place.first)
-
     s = add_parts(s[0], s_got)
     if place.extra:
         s = lax.psum(s, place.extra)
@@ -528,29 +574,13 @@
         swap(s, place.core),
         swap(s, place.near, place.core),
     ]
-    m = add_parts(after(m[0], s), m_got).reshape((4,) + m.shape[3:])
-    m_got = swap_parts(m, place.far, place.near)
-
     ninv, wa, wl, wr, panel = first_half(place, pieces, wide, narrow, total)
-    m = add_parts(after(m[0], panel), m_got)
-    if place.extra:
-        m = lax.psum(m, place.extra)
-    mixed = [
-        m,
-        swap(m, place.near),
-        swap(m, place.core),
-        swap(m, place.near, place.core),
-    ]
     winv = second_half(wa, wl, wr, panel)
-    cols = wide // n_dp
-    sent = products(place, winv, ninv, mixed, cols, total)
-    got = [sent[0]]
-    axes = (place.far, place.second, place.first)
-    for r in range(1, layers):
-        used = tuple(a for b, a in enumerate(axes) if r >> (2 - b) & 1)
-        got.append(swap(sent[r], *used))
+    cols, own_rows = wide // n_dp, narrow // n_own
+    sent = products(place, winv, ninv, m, cols, own_rows, total)
+    got = lax.all_to_all(sent, (place.far, place.second, place.first), 0, 0)
     kept, update = placing(
-        place, owner_map, got, wide, layers // n_own + 1, narrow // n_own
+        place, owner_map, got, wide, cols, layers // n_own + 1, own_rows
     )
     return (jnp.swapaxes(kept, 1, 2), jnp.swapaxes(update, 1, 2))
 

time: 76.6 us -> 180 us (2.35)
  waiting for transfers between devices: 13.4 us -> 116 us
  starting transfers between devices: 32.9 us -> 11.4 us
  blocking collectives: 0 us -> 16.6 us
  between operations: 0.84 us -> 14.1 us
  Pallas kernels: 25.5 us -> 21.4 us
  local copies, waits for them, and re-layouts: 3.4 us -> 0.06 us
    reduce_scatter x0 -> x1, waiting for transfers between devices: none -> 99.5 us  [on_device(): m = lax.psum_scatter(m, group, scatter_dimension=0, tiled=True)]
    ppermute x27 -> x10, starting transfers between devices: 32.9 us -> 11.3 us  [swap(): return lax.ppermute(value, name, [(i, count - 1 - i) for i in range(count)])]
    all_to_all x0 -> x1, blocking collectives: none -> 10.9 us  [on_device(): got = lax.all_to_all(sent, (place.far, place.second, place.first), 0, 0)]
    all_gather x0 -> x1, blocking collectives: none -> 5.62 us  [on_device(): m = lax.all_gather(m[0], (place.near, place.core))]
    pallas_call x2, Pallas kernels: 12.9 us -> 8.85 us  [gram(): pl.pallas_call(functools.partial(kernel, place), in_specs=[HBM, HBM], out...]
    unnamed x6 -> x2, local copies, waits for them, and re-layouts: 3.3 us -> 0.01 us
    ppermute x27 -> x10, waiting for transfers between devices: 13.4 us -> 16.7 us  [swap(): return lax.ppermute(value, name, [(i, count - 1 - i) for i in range(count)])]
  transfers between devices with their start and end apart: 27 -> 11, of which waited for: 10 -> 8; matrix products, arithmetic and copies ran while one was open for 0% -> 0% of each run, Pallas kernels for 22% -> 8%
where the time goes in v3:
time: 180 us
  waiting for transfers between devices  116 us (64%)
  Pallas kernels  21.4 us (12%)
  blocking collectives  16.6 us (9%)
  between operations  14.1 us (8%)
  starting transfers between devices  11.4 us (6%)
    reduce_scatter x1, waiting for transfers between devices, on_device(): m = lax.psum_scatter(m, group, scatter_dimension=0, tiled=True)  99.5 us
    ppermute x10, waiting for transfers between devices, swap(): return lax.ppermute(value, name, [(i, count - 1 - i) for i in range(count)])  16.7 us
    ppermute x10, starting transfers between devices, swap(): return lax.ppermute(value, name, [(i, count - 1 - i) for i in range(count)])  11.3 us
    all_to_all x1, blocking collectives, on_device(): got = lax.all_to_all(sent, (place.far, place.second, place.first), 0, 0)  10.9 us
    pallas_call x2, Pallas kernels, gram(): pl.pallas_call(functools.partial(kernel, place), in_specs=[HBM, HBM], out...  8.85 us
    pallas_call x1, Pallas kernels, first_half(): pl.pallas_call(functools.partial(first_half_kernel, place, total), in_spe...  6.08 us
    all_gather x1, blocking collectives, on_device(): m = lax.all_gather(m[0], (place.near, place.core))  5.62 us
    pallas_call x1, Pallas kernels, second_half(): pl.pallas_call(second_half_kernel, in_specs=[VMEM] * 4, out_specs=VMEM, o...  4.55 us
  transfers between devices with their start and end apart: 11, of which 8 were waited for; matrix products, arithmetic and copies ran while one was open for 0% of the time, Pallas kernels for 8%

profile of v3, /device:TPU:0, one launch (start us, length us, event | category | flops | bytes accessed | tf_op | source)
XLA Modules:
  0.0 179.9 jit_solution(8090933494432456060)
XLA Ops:
  7.2 4.5 %squares.1 = (f32[4,2,2,88,128]{4,3,2,1,0:T(8,128)S(1)}, f32[4,2,2,88,128]{4,3,2,1,0:T(8,128)S(1)}) custom-call(bf16[8,768,256]{2,1,0:T(8,128)(2,1)} %wide_hbm.2, bf16[8,768,128]{2,1,0:T(8,128)(2,1)} %narrow_hbm.3), custom_call_target="tpu_custom_call" | custom-call | flops 805306368 | bytes 6291456 | tf_op jit(solution)/shard_map/squares/pallas_call | solution.py:171
  11.7 0.5 collective-permute-start
  12.2 4.3 %mixed.1 = f32[2,2,2,2,2,64,128]{6,5,4,3,2,1,0:T(8,128)} custom-call(bf16[8,768,256]{2,1,0:T(8,128)(2,1)} %wide_hbm.2, bf16[8,768,128]{2,1,0:T(8,128)(2,1)} %narrow_hbm.3), custom_call_target="tpu_custom_call" | custom-call | flops 805306368 | bytes 6291456 | tf_op jit(solution)/shard_map/mixed/pallas_call | solution.py:171
  16.8 3.5 %collective-permute-start.3 = (f32[2,2,88,128]{3,2,1,0:T(8,128)S(1)}, f32[2,2,88,128]{3,2,1,0:T(8,128)S(1)}, u32[]{:S(2)}, u32[]{:S(2)}) collective-permute-start(f32[2,2,88,128]{3,2,1,0:T(8,128)S(1)} %get-tuple-element.26), channel_id=1, source_target_pairs={{0,5},{1,4},{4,1},{5,0},{2,7},{3,6},{6,3},{7,2},{8,13},{9,12},{12,... | collective-permute-start | bytes 540680 | tf_op jit(solution)/shard_map/ppermute | solution.py:513
  20.3 0.5 collective-permute-start.2
  20.8 0.1 collective-permute-start.1
  20.9 4.8 %collective-permute-done.3 = f32[2,2,88,128]{3,2,1,0:T(8,128)S(1)} collective-permute-done((f32[2,2,88,128]{3,2,1,0:T(8,128)S(1)}, f32[2,2,88,128]{3,2,1,0:T(8,128)S(1)}, u32[]{:S(2)}, u32[]{:S(2)}) %collective-permute-start.3) | collective-permute-done | bytes 180256 | tf_op jit(solution)/shard_map/ppermute | solution.py:513
  25.7 3.6 %collective-permute-done.2 = f32[2,2,88,128]{3,2,1,0:T(8,128)S(1)} collective-permute-done((f32[2,2,88,128]{3,2,1,0:T(8,128)S(1)}, f32[2,2,88,128]{3,2,1,0:T(8,128)S(1)}, u32[]{:S(2)}, u32[]{:S(2)}) %collective-permute-start.2) | collective-permute-done | bytes 180256 | tf_op jit(solution)/shard_map/ppermute | solution.py:513
  29.4 1.6 collective-permute-done.1
  31.0 3.8 %collective-permute-start.6 = (f32[88,128]{1,0:T(8,128)S(1)}, f32[88,128]{1,0:T(8,128)S(1)}, u32[]{:S(2)}, u32[]{:S(2)}) collective-permute-start(f32[88,128]{1,0:T(8,128)S(1)} %get-tuple-element.29), channel_id=1, source_target_pairs={{0,24},{8,16},{16,8},{24,0},{1,25},{9,17},{17,9},{25,1},{2,26},{10... | collective-permute-start | bytes 135176 | tf_op jit(solution)/shard_map/ppermute | solution.py:513
  34.8 0.7 collective-permute-start.4
  35.5 1.9 %collective-permute-done.6 = f32[88,128]{1,0:T(8,128)S(1)} collective-permute-done((f32[88,128]{1,0:T(8,128)S(1)}, f32[88,128]{1,0:T(8,128)S(1)}, u32[]{:S(2)}, u32[]{:S(2)}) %collective-permute-start.6) | collective-permute-done | bytes 45088 | tf_op jit(solution)/shard_map/ppermute | solution.py:513
  37.4 2.4 %collective-permute-done.5 = f32[88,128]{1,0:T(8,128)S(1)} collective-permute-done((f32[88,128]{1,0:T(8,128)S(1)}, f32[88,128]{1,0:T(8,128)S(1)}, u32[]{:S(2)}, u32[]{:S(2)}) %collective-permute-start.5) | collective-permute-done | bytes 45088 | tf_op jit(solution)/shard_map/ppermute | solution.py:513
  39.9 0.1 collective-permute-start.8
  40.0 2.0 %collective-permute-start.7 = (f32[88,128]{1,0:T(8,128)S(1)}, f32[88,128]{1,0:T(8,128)S(1)}, u32[]{:S(2)}, u32[]{:S(2)}) collective-permute-start(f32[88,128]{1,0:T(8,128)S(1)} %fusion.3.refs_0_), channel_id=1, source_target_pairs={{0,8},{8,0},{1,9},{9,1},{2,10},{10,2},{3,11},{11,3},{4,12},{12,4},... | collective-permute-start | bytes 135176 | tf_op jit(solution)/shard_map/ppermute | solution.py:513
  42.0 1.3 collective-permute-done.9.refs_3_
  43.4 1.0 collective-permute-done.7.refs_1_
  44.4 6.1 %first_half.1 = (f32[128,128]{1,0:T(8,128)S(1)}, f32[272,256]{1,0:T(8,128)S(1)}, bf16[48,256]{1,0:T(8,128)(2,1)S(1)}, bf16[48,256]{1,0:T(8,128)(2,1)S(1)}, f32[8,256]{1,0:T(8,128)S(1)}) custom-call(f32[88,128]{1,0:T(8,128)S(1)} %fusion.3.refs_0_, f32[88,128]{1,0:T(8,128)S(1)} %collective-permute-done.7.refs_1_, ...), custom_call_target="tpu_custom_call" | custom-call | flops 1073741824 | bytes 1048576 | tf_op jit(solution)/shard_map/first_half/pallas_call | solution.py:350
  50.5 4.5 %second_half.1.winv_ref = f32[256,256]{1,0:T(8,128)S(1)} custom-call(f32[272,256]{1,0:T(8,128)S(1)} %get-tuple-element.18.wa_in, bf16[48,256]{1,0:T(8,128)(2,1)S(1)} %get-tuple-element.19.wl_in, bf16[48,256]{1,0:T(8,128)(2,1)S(1)} %get-tuple-element.20.wr_in, f32[8,256]{1,0:T(8,128)S(1)} %get-tuple-element.21.panel_ref), custom_call_target="tpu_custom_call" | custom-call | flops 1073741824 | bytes 1048576 | tf_op jit(solution)/shard_map/second_half/pallas_call | solution.py:375
  55.0 99.5 %reduce-scatter.2.cloned.1.call-done = f32[1,64,128]{2,1,0:T(8,128)} async-done(((f32[32,64,128]{2,1,0:T(8,128)}), f32[1,64,128]{2,1,0:T(8,128)}) %reduce-scatter.2.cloned.1.call-update) | async-done | bytes 32784 | tf_op jit(solution)/shard_map/reduce_scatter | solution.py:558
  154.5 5.6 %all_gather.3 = f32[4,64,128]{2,1,0:T(8,128)S(1)} all-gather(f32[1,64,128]{2,1,0:T(8,128)} %reduce-scatter.2.cloned.1.call-done), channel_id=1, replica_groups=mesh['dp0'=2,'dp1'=2,'dp2'=2,'dp3'=2,'own0'=2] {'dp1','dp3'}, dimensions={0}, use_global_device_ids=true | all-gather | bytes 163840 | tf_op jit(solution)/shard_map/all_gather | solution.py:561
  160.2 0.7 products.1
  160.9 10.9 %all_to_all.5.got_ref = f32[8,40,128]{2,1,0:T(8,128)S(1)} all-to-all(f32[8,40,128]{2,1,0:T(8,128)S(1)} %products.1), channel_id=1, replica_groups=mesh['dp0'=2,'dp1'=2,'dp2'=2,'dp3'=2,'own0'=2] {'dp0','dp2','own0'}, dimensions={0} | all-to-all | bytes 327680 | tf_op jit(solution)/shard_map/all_to_all | solution.py:581
  171.8 1.3 placing.1
  (14 shorter events, 0.3 us)
Async XLA Ops:
  7.2 147.4 %reduce-scatter.2.cloned.1.call-start = ((), (), s32[]{:S(2)}) async-start(), calls=%async_computation.2 | async-start | bytes 1081344 | tf_op jit(solution)/shard_map/reduce_scatter | solution.py:558
  11.7 4.9 %collective-permute-start = (f32[4,2,2,88,128]{4,3,2,1,0:T(8,128)S(1)}, f32[4,2,2,88,128]{4,3,2,1,0:T(8,128)S(1)}, u32[]{:S(2)}, u32[]{:S(2)}) collective-permute-start(f32[4,2,2,88,128]{4,3,2,1,0:T(8,128)S(1)} %get-tuple-element.15), channel_id=1, source_target_pairs={{0,2},{2,0},{1,3},{3,1},{4,6},{6,4},{5,7},{7,5},{8,10},{10,8},{9,1... | collective-permute-start | bytes 2162696 | tf_op jit(solution)/shard_map/ppermute | solution.py:513
  16.8 9.0 %collective-permute-start.3 = (f32[2,2,88,128]{3,2,1,0:T(8,128)S(1)}, f32[2,2,88,128]{3,2,1,0:T(8,128)S(1)}, u32[]{:S(2)}, u32[]{:S(2)}) collective-permute-start(f32[2,2,88,128]{3,2,1,0:T(8,128)S(1)} %get-tuple-element.26), channel_id=1, source_target_pairs={{0,5},{1,4},{4,1},{5,0},{2,7},{3,6},{6,3},{7,2},{8,13},{9,12},{12,... | collective-permute-start | bytes 540680 | tf_op jit(solution)/shard_map/ppermute | solution.py:513
  20.3 9.1 %collective-permute-start.2 = (f32[2,2,88,128]{3,2,1,0:T(8,128)S(1)}, f32[2,2,88,128]{3,2,1,0:T(8,128)S(1)}, u32[]{:S(2)}, u32[]{:S(2)}) collective-permute-start(f32[2,2,88,128]{3,2,1,0:T(8,128)S(1)} %get-tuple-element.27), channel_id=1, source_target_pairs={{0,4},{4,0},{1,5},{5,1},{2,6},{6,2},{3,7},{7,3},{8,12},{12,8},{9,1... | collective-permute-start | bytes 540680 | tf_op jit(solution)/shard_map/ppermute | solution.py:513
  20.8 10.2 %collective-permute-start.1 = (f32[2,2,88,128]{3,2,1,0:T(8,128)S(1)}, f32[2,2,88,128]{3,2,1,0:T(8,128)S(1)}, u32[]{:S(2)}, u32[]{:S(2)}) collective-permute-start(f32[2,2,88,128]{3,2,1,0:T(8,128)S(1)} %get-tuple-element.28), channel_id=1, source_target_pairs={{0,1},{1,0},{2,3},{3,2},{4,5},{5,4},{6,7},{7,6},{8,9},{9,8},{10,11... | collective-permute-start | bytes 540680 | tf_op jit(solution)/shard_map/ppermute | solution.py:513
  31.0 6.4 %collective-permute-start.6 = (f32[88,128]{1,0:T(8,128)S(1)}, f32[88,128]{1,0:T(8,128)S(1)}, u32[]{:S(2)}, u32[]{:S(2)}) collective-permute-start(f32[88,128]{1,0:T(8,128)S(1)} %get-tuple-element.29), channel_id=1, source_target_pairs={{0,24},{8,16},{16,8},{24,0},{1,25},{9,17},{17,9},{25,1},{2,26},{10... | collective-permute-start | bytes 135176 | tf_op jit(solution)/shard_map/ppermute | solution.py:513
  34.8 5.0 %collective-permute-start.5 = (f32[88,128]{1,0:T(8,128)S(1)}, f32[88,128]{1,0:T(8,128)S(1)}, u32[]{:S(2)}, u32[]{:S(2)}) collective-permute-start(f32[88,128]{1,0:T(8,128)S(1)} %get-tuple-element.30), channel_id=1, source_target_pairs={{0,16},{16,0},{1,17},{17,1},{2,18},{18,2},{3,19},{19,3},{4,20},{20... | collective-permute-start | bytes 135176 | tf_op jit(solution)/shard_map/ppermute | solution.py:513
  34.8 5.0 %collective-permute-start.4 = (f32[88,128]{1,0:T(8,128)S(1)}, f32[88,128]{1,0:T(8,128)S(1)}, u32[]{:S(2)}, u32[]{:S(2)}) collective-permute-start(f32[88,128]{1,0:T(8,128)S(1)} %get-tuple-element.31), channel_id=1, source_target_pairs={{0,8},{8,0},{1,9},{9,1},{2,10},{10,2},{3,11},{11,3},{4,12},{12,4},... | collective-permute-start | bytes 135176 | tf_op jit(solution)/shard_map/ppermute | solution.py:513
  39.8 3.5 %collective-permute-start.9 = (f32[88,128]{1,0:T(8,128)S(1)}, f32[88,128]{1,0:T(8,128)S(1)}, u32[]{:S(2)}, u32[]{:S(2)}) collective-permute-start(f32[88,128]{1,0:T(8,128)S(1)} %fusion.3.refs_0_), channel_id=1, source_target_pairs={{0,10},{2,8},{8,2},{10,0},{1,11},{3,9},{9,3},{11,1},{4,14},{6,12},... | collective-permute-start | bytes 135176 | tf_op jit(solution)/shard_map/ppermute | solution.py:513
  39.9 3.5 %collective-permute-start.8 = (f32[88,128]{1,0:T(8,128)S(1)}, f32[88,128]{1,0:T(8,128)S(1)}, u32[]{:S(2)}, u32[]{:S(2)}) collective-permute-start(f32[88,128]{1,0:T(8,128)S(1)} %fusion.3.refs_0_), channel_id=1, source_target_pairs={{0,2},{2,0},{1,3},{3,1},{4,6},{6,4},{5,7},{7,5},{8,10},{10,8},{9,1... | collective-permute-start | bytes 135176 | tf_op jit(solution)/shard_map/ppermute | solution.py:513
  40.0 4.3 %collective-permute-start.7 = (f32[88,128]{1,0:T(8,128)S(1)}, f32[88,128]{1,0:T(8,128)S(1)}, u32[]{:S(2)}, u32[]{:S(2)}) collective-permute-start(f32[88,128]{1,0:T(8,128)S(1)} %fusion.3.refs_0_), channel_id=1, source_target_pairs={{0,8},{8,0},{1,9},{9,1},{2,10},{10,2},{3,11},{11,3},{4,12},{12,4},... | collective-permute-start | bytes 135176 | tf_op jit(solution)/shard_map/ppermute | solution.py:513
  50.5 121.4 %copy-start = (s32[8]{0:T(128)S(1)}, s32[8]{0:T(128)}, u32[]{:S(2)}) copy-start(s32[8]{0:T(128)} %owner_map.1) | copy-start | bytes 100
Sparse Core Ops, SparseCore 0:
  16.7 137.7 reduce-scatter.1

commit v4 on v3

--- a/solution.py
+++ b/solution.py
@@ -67,14 +67,16 @@
     return copies
 
 
-def write_quarters(place, i, flat, keep_ref, send_ref):
-    rows = keep_ref.shape[3]
-    quarter = place.quarter()
-    for q in range(2):
-        kept = pl.multiple_of(jnp.bitwise_xor(quarter, q) * rows, PANEL)
-        sent = pl.multiple_of(jnp.bitwise_xor(quarter, 2 + q) * rows, PANEL)
-        keep_ref[i % 4, i // 4, q] = flat[i, pl.ds(kept, rows), :]
-        send_ref[i % 4, i // 4, q] = flat[i, pl.ds(sent, rows), :]
+def write_halves(place, i, flat, keep_ref, send_ref):
+    rows = keep_ref.shape[2]
+    core = lax.axis_index(place.core)
+    z, y, x = i // 4, (i // 2) % 2, i % 2
+    mine = jnp.where(core == 0, x * 2 + y, y * 2 + x)
+    other = jnp.where(core == 0, y * 2 + x, x * 2 + y)
+    kept = pl.multiple_of(core * rows, PANEL)
+    sent = pl.multiple_of((1 - core) * rows, PANEL)
+    keep_ref[mine, z] = flat[i, pl.ds(kept, rows), :]
+    send_ref[other, z] = flat[i, pl.ds(sent, rows), :]
 
 
 def iotas(shape):
@@ -138,6 +140,7 @@
 
 def squares_kernel(place, wide_hbm, narrow_hbm, keep_ref, send_ref, wides, narrows, flat, sems):
     copies = read_layers(place, (wide_hbm, narrow_hbm), (wides, narrows), sems)
+    n = LANES
     for i, group in enumerate(copies):
         for copy in group:
             copy.wait()
@@ -145,49 +148,64 @@
         narrow = narrows[i]
         wcov = transposed_dot(wide, wide)
         ncov = transposed_dot(narrow, narrow)
-        n = LANES
         pack_squares(flat, i, wcov[:n, :n], wcov[:n, n:], wcov[n:, n:], ncov)
-        write_quarters(place, i, flat, keep_ref, send_ref)
-
-
-def mixed_kernel(place, wide_hbm, narrow_hbm, out_ref, wides, narrows, sems):
-    copies = read_layers(place, (wide_hbm, narrow_hbm), (wides, narrows), sems)
-    rows = out_ref.shape[5]
-    layer = place.layer()
-    for i, group in enumerate(copies):
-        for copy in group:
-            copy.wait()
+        write_halves(place, i, flat, keep_ref, send_ref)
+
+
+def mixed_kernel(place, wides, narrows, keep_ref, send_ref, flat):
+    for i in range(wides.shape[0]):
         mixed = transposed_dot(narrows[i], wides[i])
-        here = jnp.bitwise_xor(layer, i)
-        for q in range(4):
-            core, near = q // 2, q % 2
-            part = mixed[near * rows : (near + 1) * rows, core * LANES : (core + 1) * LANES]
-            out_ref[here // 4, near, (here // 2) % 2, core, here % 2] = part
-
-
-def gram(kernel, name, place, out_shapes, extra_scratch, wide_rows, narrow_rows):
+        flat[i, :LANES] = mixed[:, :LANES]
+        flat[i, LANES:] = mixed[:, LANES:]
+        write_halves(place, i, flat, keep_ref, send_ref)
+
+
+def gram_cost(wide_rows, columns):
+    return pl.CostEstimate(
+        flops=2 * wide_rows.size * columns, bytes_accessed=2 * wide_rows.size, transcendentals=0
+    )
+
+
+def squares(place, wide_rows, narrow_rows):
     layers = wide_rows.shape[0]
-    macs = wide_rows.shape[1] * wide_rows.shape[2] * 256
+    half = 176
+    shape = jax.ShapeDtypeStruct((4, 2, half, LANES), jnp.float32)
     return pl.pallas_call(
-        functools.partial(kernel, place),
+        functools.partial(squares_kernel, place),
         in_specs=[HBM, HBM],
-        out_specs=[VMEM] * len(out_shapes),
-        out_shape=[jax.ShapeDtypeStruct(shape, jnp.float32) for shape in out_shapes],
+        out_specs=[VMEM] * 4,
+        out_shape=[
+            shape,
+            shape,
+            jax.ShapeDtypeStruct(wide_rows.shape, wide_rows.dtype),
+            jax.ShapeDtypeStruct(narrow_rows.shape, narrow_rows.dtype),
+        ],
         scratch_shapes=[
-            pltpu.VMEM(wide_rows.shape, wide_rows.dtype),
-            pltpu.VMEM(narrow_rows.shape, narrow_rows.dtype),
-            *extra_scratch,
+            pltpu.VMEM((layers, 2 * half, LANES), jnp.float32),
             pltpu.SemaphoreType.DMA((layers, 2)),
         ],
-        cost_estimate=pl.CostEstimate(
-            flops=2 * layers * macs, bytes_accessed=2 * wide_rows.size * 2, transcendentals=0
-        ),
+        cost_estimate=gram_cost(wide_rows, 320),
         compiler_params=PARAMS,
-        name=name,
+        name="squares",
     )(
         pltpu.with_memory_space_constraint(wide_rows, pltpu.HBM),
         pltpu.with_memory_space_constraint(narrow_rows, pltpu.HBM),
     )
+
+
+def mixed_sums(place, wides, narrows):
+    layers, _, narrow = narrows.shape
+    shape = jax.ShapeDtypeStruct((4, 2, narrow, LANES), jnp.float32)
+    return pl.pallas_call(
+        functools.partial(mixed_kernel, place),
+        in_specs=[VMEM, VMEM],
+        out_specs=[VMEM, VMEM],
+        out_shape=[shape, shape],
+        scratch_shapes=[pltpu.VMEM((layers, 2 * narrow, LANES), jnp.float32)],
+        cost_estimate=gram_cost(wides, 128),
+        compiler_params=PARAMS,
+        name="mixed",
+    )(wides, narrows)
 
 
 def lane_gather(x, index):
@@ -281,15 +299,15 @@
 
 
 def place_pieces(place, flat, pieces):
-    quarter = place.quarter()
+    core = lax.axis_index(place.core)
     rows = pieces[0].shape[0]
     for r, piece in enumerate(pieces):
-        start = pl.multiple_of(jnp.bitwise_xor(quarter, r) * rows, PANEL)
+        start = pl.multiple_of(jnp.bitwise_xor(core, r) * rows, PANEL)
         flat[pl.ds(start, rows), :] = piece[...]
 
 
 def first_half_kernel(place, total, *refs):
-    pieces, refs = refs[:4], refs[4:]
+    pieces, refs = refs[:2], refs[2:]
     ninv_ref, wa, wl, wr, panel_ref, flat, na, nl, nr = refs
     place_pieces(place, flat, pieces)
     wide, narrow = wa.shape[1], na.shape[1]
@@ -323,8 +341,7 @@
     ninv_ref[...] = -na[PANEL : PANEL + narrow, :]
 
 
-def second_half_kernel(wa_in, wl_in, wr_in, panel_ref, winv_ref, wa, wl, wr):
-    wide = wa.shape[1]
+def later_panels_kernel(begin, end, wa_in, wl_in, wr_in, panel_in, wa, wl, wr, panel_out):
     wa[...] = wa_in[...]
     wl[...] = wl_in[...]
     wr[...] = wr_in[...]
@@ -332,7 +349,14 @@
     def only(step, panel):
         return sweep_panel(wa, wl, wr, 1, step, panel)
 
-    lax.fori_loop(0, LANES // PANEL, only, panel_ref[...])
+    panel_out[...] = lax.fori_loop(begin, end, only, panel_in[...])
+
+
+def last_panels_kernel(begin, wa_in, wl_in, wr_in, panel_in, winv_ref, wa, wl, wr, panel):
+    later_panels_kernel(
+        begin, LANES // PANEL, wa_in, wl_in, wr_in, panel_in, wa, wl, wr, panel
+    )
+    wide = wa.shape[1]
     trailing_update(wa, wl, wr, wide)
     winv_ref[...] = -wa[PANEL : PANEL + wide, :]
 
@@ -349,7 +373,7 @@
     matrix = (wide + 2 * PANEL, wide)
     return pl.pallas_call(
         functools.partial(first_half_kernel, place, total),
-        in_specs=[VMEM] * 4,
+        in_specs=[VMEM] * 2,
         out_specs=[VMEM] * 5,
         out_shape=[
             jax.ShapeDtypeStruct((narrow, narrow), jnp.float32),
@@ -359,7 +383,7 @@
             jax.ShapeDtypeStruct((PANEL, wide), jnp.float32),
         ],
         scratch_shapes=[
-            pltpu.VMEM((4 * rows, LANES), jnp.float32),
+            pltpu.VMEM((2 * rows, LANES), jnp.float32),
             pltpu.VMEM((narrow + 2 * PANEL, narrow), jnp.float32),
             pltpu.VMEM((splits, narrow), jnp.bfloat16),
             pltpu.VMEM((splits, narrow), jnp.bfloat16),
@@ -370,22 +394,30 @@
     )(*pieces)
 
 
-def second_half(wa, wl, wr, panel):
-    wide = wa.shape[1]
+def later_panels(state, begin, end):
     return pl.pallas_call(
-        second_half_kernel,
+        functools.partial(later_panels_kernel, begin, end),
+        in_specs=[VMEM] * 4,
+        out_specs=[VMEM] * 4,
+        out_shape=[jax.ShapeDtypeStruct(v.shape, v.dtype) for v in state],
+        cost_estimate=sweep_cost(state[0].shape[1]),
+        compiler_params=PARAMS,
+        name="later_panels",
+    )(*state)
+
+
+def last_panels(state, begin):
+    wide = state[0].shape[1]
+    return pl.pallas_call(
+        functools.partial(last_panels_kernel, begin),
         in_specs=[VMEM] * 4,
         out_specs=VMEM,
         out_shape=jax.ShapeDtypeStruct((wide, wide), jnp.float32),
-        scratch_shapes=[
-            pltpu.VMEM(wa.shape, wa.dtype),
-            pltpu.VMEM(wl.shape, wl.dtype),
-            pltpu.VMEM(wr.shape, wr.dtype),
-        ],
+        scratch_shapes=[pltpu.VMEM(v.shape, v.dtype) for v in state],
         cost_estimate=sweep_cost(wide),
         compiler_params=PARAMS,
-        name="second_half",
-    )(wa, wl, wr, panel)
+        name="last_panels",
+    )(*state)
 
 
 def aligned_rows(ref, index, count):
@@ -403,17 +435,14 @@
     return cols == 2 * PANEL and 2 * rows == LANES
 
 
-def product_kernel(place, total, rows, winv_ref, ninv_ref, mixed_ref, out_ref):
+def product_kernel(place, total, rows, winv_ref, ninv_ref, mine_ref, other_ref, out_ref, flat):
+    place_pieces(place, flat, (mine_ref, other_ref))
     ninv = ninv_ref[...]
-    half = mixed_ref.shape[0]
+    half = flat.shape[0] // 2
     inner = jnp.concatenate(
         [
-            transposed_dot(
-                jnp.concatenate([mixed_ref[n, c] for n in range(half)], axis=0) / total,
-                ninv,
-                HIGHEST,
-            )
-            for c in range(2)
+            transposed_dot(flat[h * half : (h + 1) * half] / total, ninv, HIGHEST)
+            for h in range(2)
         ],
         axis=0,
     )
@@ -448,16 +477,17 @@
                 out_ref[block, 2 * cols :] = update
 
 
-def products(place, winv, ninv, mixed, cols, rows, total):
+def products(place, winv, ninv, pieces, cols, rows, total):
     height = 2 * cols + (PANEL if packs(cols, rows) else cols)
     return pl.pallas_call(
         functools.partial(product_kernel, place, total, rows),
-        in_specs=[VMEM] * 3,
+        in_specs=[VMEM] * 4,
         out_specs=VMEM,
         out_shape=jax.ShapeDtypeStruct((8, height, LANES), jnp.float32),
+        scratch_shapes=[pltpu.VMEM((2 * ninv.shape[0], LANES), jnp.float32)],
         compiler_params=PARAMS,
         name="products",
-    )(winv, ninv, mixed)
+    )(winv, ninv, *pieces)
 
 
 def placing_kernel(place, owner_map, got_ref, kept_ref, update_ref):
@@ -507,18 +537,19 @@
     )(owner_map, got)
 
 
-def swap(value, *axes):
-    count = 2 ** len(axes)
-    name = axes if len(axes) > 1 else axes[0]
-    return lax.ppermute(value, name, [(i, count - 1 - i) for i in range(count)])
-
-
-def swap_parts(parts, high, low):
-    return [swap(parts[1], low), swap(parts[2], high), swap(parts[3], high, low)]
-
-
-def add_parts(part, got):
-    return (part + got[0]) + (got[1] + got[2])
+def swap(value, axis):
+    return lax.ppermute(value, axis, [(0, 1), (1, 0)])
+
+
+def swap_by_core(value, place, stage):
+    pairs = []
+    for y in range(2):
+        for core in range(2):
+            for x in range(2):
+                flip = 1 if core == stage else 4
+                here = y * 4 + core * 2 + x
+                pairs.append((here, here ^ flip))
+    return lax.ppermute(value, (place.second, place.core, place.first), pairs)
 
 
 def after(value, *others):
@@ -531,51 +562,44 @@
     n_dp, n_own = 2 ** len(place.dp), 2 ** len(place.own)
     total = float(rows * n_dp * n_own)
 
-    quarter = 88
-    split = (4, 2, 2, quarter, LANES)
-    s_keep, s_send = gram(
-        squares_kernel,
-        "squares",
-        place,
-        [split, split],
-        [pltpu.VMEM((layers, 4 * quarter, LANES), jnp.float32)],
-        wide_rows,
-        narrow_rows,
-    )
+    s_keep, s_send, wides, narrows = squares(place, wide_rows, narrow_rows)
     s_got = swap(s_send, place.core)
-    group = (place.far, place.near, place.second, place.core, place.first)
-    (m,) = gram(
-        mixed_kernel,
-        "mixed",
-        place,
-        [(2, 2, 2, 2, 2, narrow // 2, LANES)],
-        [],
-        after(wide_rows, s_send),
-        narrow_rows,
-    )
-    s_keep, m = lax.optimization_barrier((s_keep, m))
-    m = m.reshape((-1,) + m.shape[5:])
-    m = lax.psum_scatter(m, group, scatter_dimension=0, tiled=True)
+    m_keep, m_send = mixed_sums(place, after(wides, s_send), narrows)
+    s_keep, m_send = lax.optimization_barrier((s_keep, m_send))
+
+    s = s_keep + s_got
+    s_got = swap_by_core(s[2:], place, 0)
+    m_got = swap(after(m_send, s), place.core)
+
+    s = s[:2] + s_got
+    s_got = swap_by_core(s[1], place, 1)
+    m = after(m_keep, s) + m_got
+    m_got = swap_by_core(m[2:], place, 0)
+
+    s = s[0] + s_got
+    s_got = swap(s[1], place.far)
+    m = after(m[:2], s) + m_got
+    m_got = swap_by_core(m[1], place, 1)
+
+    s = s[0] + s_got
+    if place.extra:
+        s = lax.psum(s, place.extra)
+    s_got = swap(s, place.near)
+    m = after(m[0], s) + m_got
+    m_got = swap(m[1], place.far)
+
+    s = s + s_got
+    ninv, *state = first_half(place, [s, swap(s, place.core)], wide, narrow, total)
+    m = after(m[0], state[0]) + m_got
     if place.extra:
         m = lax.psum(m, place.extra)
-    m = lax.all_gather(m[0], (place.near, place.core))
-    m = m.reshape((2, 2) + m.shape[1:])
-
-    s = s_keep + s_got
-    s_got = swap_parts(s, place.second, place.first)
-    s = add_parts(s[0], s_got).reshape((4,) + s.shape[3:])
-    s_got = swap_parts(s, place.far, place.near)
-    s = add_parts(s[0], s_got)
-    if place.extra:
-        s = lax.psum(s, place.extra)
-    pieces = [
-        s,
-        swap(s, place.near),
-        swap(s, place.core),
-        swap(s, place.near, place.core),
-    ]
-    ninv, wa, wl, wr, panel = first_half(place, pieces, wide, narrow, total)
-    winv = second_half(wa, wl, wr, panel)
+    m_got = swap(m, place.near)
+    middle = LANES // PANEL // 2
+    state = later_panels(state, 0, middle)
+    m = after(m, state[0]) + m_got
+    m_got = swap(m, place.core)
+    winv = last_panels(state, middle)
+    m = [m, m_got]
     cols, own_rows = wide // n_dp, narrow // n_own
     sent = products(place, winv, ninv, m, cols, own_rows, total)
     got = lax.all_to_all(sent, (place.far, place.second, place.first), 0, 0)

time: 180 us -> 65.5 us (0.36)
  waiting for transfers between devices: 116 us -> 13.6 us
  between operations: 14.1 us -> 0.8 us
  starting transfers between devices: 11.4 us -> 19.7 us
  blocking collectives: 16.6 us -> 12.7 us
  Pallas kernels: 21.4 us -> 18.1 us
    reduce_scatter x1 -> x0, waiting for transfers between devices: 99.5 us -> none  [on_device(): m = lax.psum_scatter(m, group, scatter_dimension=0, tiled=True)]
    ppermute x10 -> x12, starting transfers between devices: 11.3 us -> 19.7 us  [the longest x8 11.5 us: swap(): return lax.ppermute(value, axis, [(0, 1), (1, 0)])]
    all_gather x1 -> x0, blocking collectives: 5.62 us -> none  [on_device(): m = lax.all_gather(m[0], (place.near, place.core))]
    pallas_call x3 -> x4, Pallas kernels: 13.4 us -> 10.1 us  [the longest x1 4.6 us: squares(): pl.pallas_call(functools.partial(squares_kernel, place), in_specs=[HBM, H...]
    ppermute x10 -> x12, waiting for transfers between devices: 16.7 us -> 13.6 us  [the longest x4 8.95 us: swap_by_core(): return lax.ppermute(value, (place.second, place.core, place.first), pairs)]
  transfers between devices with their start and end apart: 11 -> 12, of which waited for: 8 -> 6; matrix products, arithmetic and copies ran while one was open for 0% -> 0% of each run, Pallas kernels for 8% -> 18%
where the time goes in v4:
time: 65.5 us; the launch traced here: 65.4 us
  starting transfers between devices  19.7 us (30%)
  Pallas kernels  18.1 us (28%)
  waiting for transfers between devices  13.6 us (21%)
  blocking collectives  12.7 us (19%)
  between operations  0.8 us (1%)
    all_to_all x1, blocking collectives, on_device(): got = lax.all_to_all(sent, (place.far, place.second, place.first), 0, 0)  12.7 us
    ppermute x8, starting transfers between devices, swap(): return lax.ppermute(value, axis, [(0, 1), (1, 0)])  11.5 us
    ppermute x4, waiting for transfers between devices, swap_by_core(): return lax.ppermute(value, (place.second, place.core, place.first), pairs)  8.95 us
    ppermute x4, starting transfers between devices, swap_by_core(): return lax.ppermute(value, (place.second, place.core, place.first), pairs)  8.17 us
    pallas_call x1, Pallas kernels, first_half(): pl.pallas_call(functools.partial(first_half_kernel, place, total), in_spe...  6.06 us
    ppermute x8, waiting for transfers between devices, swap(): return lax.ppermute(value, axis, [(0, 1), (1, 0)])  4.65 us
    pallas_call x1, Pallas kernels, squares(): pl.pallas_call(functools.partial(squares_kernel, place), in_specs=[HBM, H...  4.6 us
    pallas_call x1, Pallas kernels, last_panels(): pl.pallas_call(functools.partial(last_panels_kernel, begin), in_specs=[VM...  2.38 us
  transfers between devices with their start and end apart: 12, of which 6 were waited for; matrix products, arithmetic and copies ran while one was open for 0% of the time, Pallas kernels for 18%

profile of v4, /device:TPU:0, one launch (start us, length us, event | category | flops | bytes accessed | tf_op | source)
XLA Modules:
  0.0 65.4 jit_solution(10940417062334878502)
XLA Ops:
  0.6 4.6 %squares.1 = (f32[4,2,176,128]{3,2,1,0:T(8,128)S(1)}, f32[4,2,176,128]{3,2,1,0:T(8,128)S(1)}, bf16[8,768,256]{2,1,0:T(8,128)(2,1)S(1)}, bf16[8,768,128]{2,1,0:T(8,128)(2,1)S(1)}) custom-call(bf16[8,768,256]{2,1,0:T(8,128)(2,1)} %wide_hbm.1, bf16[8,768,128]{2,1,0:T(8,128)(2,1)} %narrow_hbm.1), custom_call_target="tpu_custom_call" | custom-call | flops 1006632960 | bytes 3145728 | tf_op jit(solution)/shard_map/squares/pallas_call | solution.py:173
  5.2 0.5 collective-permute-start
  5.8 0.9 %mixed.1 = (f32[4,2,128,128]{3,2,1,0:T(8,128)S(1)}, f32[4,2,128,128]{3,2,1,0:T(8,128)S(1)}) custom-call(bf16[8,768,256]{2,1,0:T(8,128)(2,1)S(1)} %get-tuple-element.31.wides, bf16[8,768,128]{2,1,0:T(8,128)(2,1)S(1)} %get-tuple-element.32.narrows), custom_call_target="tpu_custom_call" | custom-call | flops 402653184 | bytes 3145728 | tf_op jit(solution)/shard_map/mixed/pallas_call | solution.py:199
  6.7 0.9 %collective-permute-done = f32[4,2,176,128]{3,2,1,0:T(8,128)S(1)} collective-permute-done((f32[4,2,176,128]{3,2,1,0:T(8,128)S(1)}, f32[4,2,176,128]{3,2,1,0:T(8,128)S(1)}, u32[]{:S(2)}, u32[]{:S(2)}) %collective-permute-start) | collective-permute-done | bytes 720928 | tf_op jit(solution)/shard_map/ppermute | solution.py:541
  7.6 0.1 add.30
  7.7 2.9 %collective-permute-start.1 = (f32[2,2,176,128]{3,2,1,0:T(8,128)S(1)}, f32[2,2,176,128]{3,2,1,0:T(8,128)S(1)}, u32[]{:S(2)}, u32[]{:S(2)}) collective-permute-start(f32[2,2,176,128]{3,2,1,0:T(8,128)S(1)} %slice.49), channel_id=1, source_target_pairs={{0,1},{1,0},{2,6},{3,7},{4,5},{5,4},{6,2},{7,3},{8,9},{9,8},{10,14... | collective-permute-start | bytes 1081352 | tf_op jit(solution)/shard_map/ppermute | solution.py:552
  10.6 5.4 %collective-permute-done.1 = f32[2,2,176,128]{3,2,1,0:T(8,128)S(1)} collective-permute-done((f32[2,2,176,128]{3,2,1,0:T(8,128)S(1)}, f32[2,2,176,128]{3,2,1,0:T(8,128)S(1)}, u32[]{:S(2)}, u32[]{:S(2)}) %collective-permute-start.1) | collective-permute-done | bytes 360480 | tf_op jit(solution)/shard_map/ppermute | solution.py:552
  16.1 2.1 %collective-permute-start.2 = (f32[2,176,128]{2,1,0:T(8,128)S(1)}, f32[2,176,128]{2,1,0:T(8,128)S(1)}, u32[]{:S(2)}, u32[]{:S(2)}) collective-permute-start(f32[2,176,128]{2,1,0:T(8,128)S(1)} %slice_bitcast_fusion), channel_id=1, source_target_pairs={{0,4},{1,5},{2,3},{3,2},{4,0},{5,1},{6,7},{7,6},{8,12},{9,13},{10,... | collective-permute-start | bytes 540680 | tf_op jit(solution)/shard_map/ppermute | solution.py:552
  18.3 1.6 %collective-permute-start.7 = (f32[2,2,128,128]{3,2,1,0:T(8,128)S(1)}, f32[2,2,128,128]{3,2,1,0:T(8,128)S(1)}, u32[]{:S(2)}, u32[]{:S(2)}) collective-permute-start(f32[2,2,128,128]{3,2,1,0:T(8,128)S(1)} %get-tuple-element.54), channel_id=1, source_target_pairs={{0,1},{1,0},{2,6},{3,7},{4,5},{5,4},{6,2},{7,3},{8,9},{9,8},{10,14... | collective-permute-start | bytes 786440 | tf_op jit(solution)/shard_map/ppermute | solution.py:552
  19.9 3.5 %collective-permute-done.2 = f32[2,176,128]{2,1,0:T(8,128)S(1)} collective-permute-done((f32[2,176,128]{2,1,0:T(8,128)S(1)}, f32[2,176,128]{2,1,0:T(8,128)S(1)}, u32[]{:S(2)}, u32[]{:S(2)}) %collective-permute-start.2) | collective-permute-done | bytes 180256 | tf_op jit(solution)/shard_map/ppermute | solution.py:552
  23.4 3.4 %collective-permute-start.3 = (f32[176,128]{1,0:T(8,128)S(1)}, f32[176,128]{1,0:T(8,128)S(1)}, u32[]{:S(2)}, u32[]{:S(2)}) collective-permute-start(f32[176,128]{1,0:T(8,128)S(1)} %slice_bitcast_fusion.4), channel_id=1, source_target_pairs={{0,16},{16,0},{1,17},{17,1},{2,18},{18,2},{3,19},{19,3},{4,20},{20... | collective-permute-start | bytes 270344 | tf_op jit(solution)/shard_map/ppermute | solution.py:541
  26.8 1.6 %collective-permute-start.8 = (f32[2,128,128]{2,1,0:T(8,128)S(1)}, f32[2,128,128]{2,1,0:T(8,128)S(1)}, u32[]{:S(2)}, u32[]{:S(2)}) collective-permute-start(f32[2,128,128]{2,1,0:T(8,128)S(1)} %get-tuple-element.56), channel_id=1, source_target_pairs={{0,4},{1,5},{2,3},{3,2},{4,0},{5,1},{6,7},{7,6},{8,12},{9,13},{10,... | collective-permute-start | bytes 393224 | tf_op jit(solution)/shard_map/ppermute | solution.py:552
  28.4 1.0 %collective-permute-done.3 = f32[176,128]{1,0:T(8,128)S(1)} collective-permute-done((f32[176,128]{1,0:T(8,128)S(1)}, f32[176,128]{1,0:T(8,128)S(1)}, u32[]{:S(2)}, u32[]{:S(2)}) %collective-permute-start.3) | collective-permute-done | bytes 90144 | tf_op jit(solution)/shard_map/ppermute | solution.py:541
  29.4 2.2 %collective-permute-start.4 = (f32[176,128]{1,0:T(8,128)S(1)}, f32[176,128]{1,0:T(8,128)S(1)}, u32[]{:S(2)}, u32[]{:S(2)}) collective-permute-start(f32[176,128]{1,0:T(8,128)S(1)} %fusion.1), channel_id=1, source_target_pairs={{0,8},{8,0},{1,9},{9,1},{2,10},{10,2},{3,11},{11,3},{4,12},{12,4},... | collective-permute-start | bytes 270344 | tf_op jit(solution)/shard_map/ppermute | solution.py:541
  31.6 2.5 %collective-permute-done.4 = f32[176,128]{1,0:T(8,128)S(1)} collective-permute-done((f32[176,128]{1,0:T(8,128)S(1)}, f32[176,128]{1,0:T(8,128)S(1)}, u32[]{:S(2)}, u32[]{:S(2)}) %collective-permute-start.4) | collective-permute-done | bytes 90144 | tf_op jit(solution)/shard_map/ppermute | solution.py:541
  34.3 3.2 %collective-permute-start.9 = (f32[128,128]{1,0:T(8,128)S(1)}, f32[128,128]{1,0:T(8,128)S(1)}, u32[]{:S(2)}, u32[]{:S(2)}) collective-permute-start(f32[128,128]{1,0:T(8,128)S(1)} %get-tuple-element.58), channel_id=1, source_target_pairs={{0,16},{16,0},{1,17},{17,1},{2,18},{18,2},{3,19},{19,3},{4,20},{20... | collective-permute-start | bytes 196616 | tf_op jit(solution)/shard_map/ppermute | solution.py:541
  37.5 6.1 %first_half.1 = (f32[128,128]{1,0:T(8,128)S(1)}, f32[272,256]{1,0:T(8,128)S(1)}, bf16[48,256]{1,0:T(8,128)(2,1)S(1)}, bf16[48,256]{1,0:T(8,128)(2,1)S(1)}, f32[8,256]{1,0:T(8,128)S(1)}) custom-call(f32[176,128]{1,0:T(8,128)S(1)} %add.34.refs_0_, f32[176,128]{1,0:T(8,128)S(1)} %collective-permute-done.5.refs_1_), custom_call_target="tpu_custom_call" | custom-call | flops 1073741824 | bytes 1048576 | tf_op jit(solution)/shard_map/first_half/pallas_call | solution.py:374
  43.6 2.1 %collective-permute-start.10 = (f32[128,128]{1,0:T(8,128)S(1)}, f32[128,128]{1,0:T(8,128)S(1)}, u32[]{:S(2)}, u32[]{:S(2)}) collective-permute-start(f32[128,128]{1,0:T(8,128)S(1)} %add.38), channel_id=1, source_target_pairs={{0,8},{8,0},{1,9},{9,1},{2,10},{10,2},{3,11},{11,3},{4,12},{12,4},... | collective-permute-start | bytes 196616 | tf_op jit(solution)/shard_map/ppermute | solution.py:541
  45.7 2.2 %later_panels.1 = (f32[272,256]{1,0:T(8,128)S(1)}, bf16[48,256]{1,0:T(8,128)(2,1)S(1)}, bf16[48,256]{1,0:T(8,128)(2,1)S(1)}, f32[8,256]{1,0:T(8,128)S(1)}) custom-call(f32[272,256]{1,0:T(8,128)S(1)} %get-tuple-element.35.wa_in, bf16[48,256]{1,0:T(8,128)(2,1)S(1)} %get-tuple-element.36.wl_in, bf16[48,256]{1,0:T(8,128)(2,1)S(1)} %get-tuple-element.37.wr_in, ...), custom_call_target="tpu_custom_call" | custom-call | flops 1073741824 | bytes 1048576 | tf_op jit(solution)/shard_map/later_panels/pallas_call | solution.py:398
  47.9 0.3 collective-permute-done.10
  48.2 2.4 %last_panels.1.winv_ref = f32[256,256]{1,0:T(8,128)S(1)} custom-call(f32[272,256]{1,0:T(8,128)S(1)} %get-tuple-element.39.wa_in, bf16[48,256]{1,0:T(8,128)(2,1)S(1)} %get-tuple-element.40.wl_in, bf16[48,256]{1,0:T(8,128)(2,1)S(1)} %get-tuple-element.41.wr_in, f32[8,256]{1,0:T(8,128)S(1)} %get-tuple-element.42.panel_in), custom_call_target="tpu_custom_call" | custom-call | flops 1073741824 | bytes 1048576 | tf_op jit(solution)/shard_map/last_panels/pallas_call | solution.py:411
  50.6 0.7 %products.1 = f32[8,40,128]{2,1,0:T(8,128)S(1)} custom-call(f32[256,256]{1,0:T(8,128)S(1)} %last_panels.1.winv_ref, f32[128,128]{1,0:T(8,128)S(1)} %get-tuple-element.43.ninv_ref, f32[128,128]{1,0:T(8,128)S(1)} %add.39.mine_ref, f32[128,128]{1,0:T(8,128)S(1)} %collective-permute-done.11.other_ref), custom_call_target="tpu_custom_call" | custom-call | tf_op jit(solution)/shard_map/products/pallas_call | solution.py:482
  51.3 12.7 %all_to_all.5.got_ref = f32[8,40,128]{2,1,0:T(8,128)S(1)} all-to-all(f32[8,40,128]{2,1,0:T(8,128)S(1)} %products.1), channel_id=1, replica_groups=mesh['dp0'=2,'dp1'=2,'dp2'=2,'dp3'=2,'own0'=2] {'dp0','dp2','own0'}, dimensions={0} | all-to-all | bytes 327680 | tf_op jit(solution)/shard_map/all_to_all | solution.py:605
  64.1 1.3 %placing.1 = (f32[5,16,256]{2,1,0:T(8,128)}, f32[8,16,64]{2,1,0:T(8,128)}) custom-call(s32[8]{0:T(128)S(1)} %copy-done, f32[8,40,128]{2,1,0:T(8,128)S(1)} %all_to_all.5.got_ref), custom_call_target="tpu_custom_call" | custom-call | tf_op jit(solution)/shard_map/placing/pallas_call | solution.py:527
  (26 shorter events, 0.5 us)
Async XLA Ops:
  5.2 2.4 %collective-permute-start = (f32[4,2,176,128]{3,2,1,0:T(8,128)S(1)}, f32[4,2,176,128]{3,2,1,0:T(8,128)S(1)}, u32[]{:S(2)}, u32[]{:S(2)}) collective-permute-start(f32[4,2,176,128]{3,2,1,0:T(8,128)S(1)} %get-tuple-element.30), channel_id=1, source_target_pairs={{0,2},{2,0},{1,3},{3,1},{4,6},{6,4},{5,7},{7,5},{8,10},{10,8},{9,1... | collective-permute-start | bytes 2162696 | tf_op jit(solution)/shard_map/ppermute | solution.py:541
  7.7 8.3 %collective-permute-start.1 = (f32[2,2,176,128]{3,2,1,0:T(8,128)S(1)}, f32[2,2,176,128]{3,2,1,0:T(8,128)S(1)}, u32[]{:S(2)}, u32[]{:S(2)}) collective-permute-start(f32[2,2,176,128]{3,2,1,0:T(8,128)S(1)} %slice.49), channel_id=1, source_target_pairs={{0,1},{1,0},{2,6},{3,7},{4,5},{5,4},{6,2},{7,3},{8,9},{9,8},{10,14... | collective-permute-start | bytes 1081352 | tf_op jit(solution)/shard_map/ppermute | solution.py:552
  10.6 7.6 %collective-permute-start.6 = (f32[4,2,128,128]{3,2,1,0:T(8,128)S(1)}, f32[4,2,128,128]{3,2,1,0:T(8,128)S(1)}, u32[]{:S(2)}, u32[]{:S(2)}) collective-permute-start(f32[4,2,128,128]{3,2,1,0:T(8,128)S(1)} %get-tuple-element.47), channel_id=1, source_target_pairs={{0,2},{2,0},{1,3},{3,1},{4,6},{6,4},{5,7},{7,5},{8,10},{10,8},{9,1... | collective-permute-start | bytes 1572872 | tf_op jit(solution)/shard_map/ppermute | solution.py:541
  16.1 7.3 %collective-permute-start.2 = (f32[2,176,128]{2,1,0:T(8,128)S(1)}, f32[2,176,128]{2,1,0:T(8,128)S(1)}, u32[]{:S(2)}, u32[]{:S(2)}) collective-permute-start(f32[2,176,128]{2,1,0:T(8,128)S(1)} %slice_bitcast_fusion), channel_id=1, source_target_pairs={{0,4},{1,5},{2,3},{3,2},{4,0},{5,1},{6,7},{7,6},{8,12},{9,13},{10,... | collective-permute-start | bytes 540680 | tf_op jit(solution)/shard_map/ppermute | solution.py:552
  18.3 8.5 %collective-permute-start.7 = (f32[2,2,128,128]{3,2,1,0:T(8,128)S(1)}, f32[2,2,128,128]{3,2,1,0:T(8,128)S(1)}, u32[]{:S(2)}, u32[]{:S(2)}) collective-permute-start(f32[2,2,128,128]{3,2,1,0:T(8,128)S(1)} %get-tuple-element.54), channel_id=1, source_target_pairs={{0,1},{1,0},{2,6},{3,7},{4,5},{5,4},{6,2},{7,3},{8,9},{9,8},{10,14... | collective-permute-start | bytes 786440 | tf_op jit(solution)/shard_map/ppermute | solution.py:552
  23.4 6.0 %collective-permute-start.3 = (f32[176,128]{1,0:T(8,128)S(1)}, f32[176,128]{1,0:T(8,128)S(1)}, u32[]{:S(2)}, u32[]{:S(2)}) collective-permute-start(f32[176,128]{1,0:T(8,128)S(1)} %slice_bitcast_fusion.4), channel_id=1, source_target_pairs={{0,16},{16,0},{1,17},{17,1},{2,18},{18,2},{3,19},{19,3},{4,20},{20... | collective-permute-start | bytes 270344 | tf_op jit(solution)/shard_map/ppermute | solution.py:541
  26.8 7.4 %collective-permute-start.8 = (f32[2,128,128]{2,1,0:T(8,128)S(1)}, f32[2,128,128]{2,1,0:T(8,128)S(1)}, u32[]{:S(2)}, u32[]{:S(2)}) collective-permute-start(f32[2,128,128]{2,1,0:T(8,128)S(1)} %get-tuple-element.56), channel_id=1, source_target_pairs={{0,4},{1,5},{2,3},{3,2},{4,0},{5,1},{6,7},{7,6},{8,12},{9,13},{10,... | collective-permute-start | bytes 393224 | tf_op jit(solution)/shard_map/ppermute | solution.py:552
  29.4 4.7 %collective-permute-start.4 = (f32[176,128]{1,0:T(8,128)S(1)}, f32[176,128]{1,0:T(8,128)S(1)}, u32[]{:S(2)}, u32[]{:S(2)}) collective-permute-start(f32[176,128]{1,0:T(8,128)S(1)} %fusion.1), channel_id=1, source_target_pairs={{0,8},{8,0},{1,9},{9,1},{2,10},{10,2},{3,11},{11,3},{4,12},{12,4},... | collective-permute-start | bytes 270344 | tf_op jit(solution)/shard_map/ppermute | solution.py:541
  34.1 3.4 %collective-permute-start.5 = (f32[176,128]{1,0:T(8,128)S(1)}, f32[176,128]{1,0:T(8,128)S(1)}, u32[]{:S(2)}, u32[]{:S(2)}) collective-permute-start(f32[176,128]{1,0:T(8,128)S(1)} %add.34.refs_0_), channel_id=1, source_target_pairs={{0,2},{2,0},{1,3},{3,1},{4,6},{6,4},{5,7},{7,5},{8,10},{10,8},{9,1... | collective-permute-start | bytes 270344 | tf_op jit(solution)/shard_map/ppermute | solution.py:541
  34.3 9.3 %collective-permute-start.9 = (f32[128,128]{1,0:T(8,128)S(1)}, f32[128,128]{1,0:T(8,128)S(1)}, u32[]{:S(2)}, u32[]{:S(2)}) collective-permute-start(f32[128,128]{1,0:T(8,128)S(1)} %get-tuple-element.58), channel_id=1, source_target_pairs={{0,16},{16,0},{1,17},{17,1},{2,18},{18,2},{3,19},{19,3},{4,20},{20... | collective-permute-start | bytes 196616 | tf_op jit(solution)/shard_map/ppermute | solution.py:541
  43.6 4.6 %collective-permute-start.10 = (f32[128,128]{1,0:T(8,128)S(1)}, f32[128,128]{1,0:T(8,128)S(1)}, u32[]{:S(2)}, u32[]{:S(2)}) collective-permute-start(f32[128,128]{1,0:T(8,128)S(1)} %add.38), channel_id=1, source_target_pairs={{0,8},{8,0},{1,9},{9,1},{2,10},{10,2},{3,11},{11,3},{4,12},{12,4},... | collective-permute-start | bytes 196616 | tf_op jit(solution)/shard_map/ppermute | solution.py:541
  47.9 16.2 %copy-start = (s32[8]{0:T(128)S(1)}, s32[8]{0:T(128)}, u32[]{:S(2)}) copy-start(s32[8]{0:T(128)} %owner_map.1) | copy-start | bytes 100
  48.1 2.5 %collective-permute-start.11 = (f32[128,128]{1,0:T(8,128)S(1)}, f32[128,128]{1,0:T(8,128)S(1)}, u32[]{:S(2)}, u32[]{:S(2)}) collective-permute-start(f32[128,128]{1,0:T(8,128)S(1)} %add.39.mine_ref), channel_id=1, source_target_pairs={{0,2},{2,0},{1,3},{3,1},{4,6},{6,4},{5,7},{7,5},{8,10},{10,8},{9,1... | collective-permute-start | bytes 196616 | tf_op jit(solution)/shard_map/ppermute | solution.py:541

commit v5 on v4

--- a/solution.py
+++ b/solution.py
@@ -86,59 +86,56 @@
     )
 
 
-def pack_squares(flat, i, first, corner, second, narrow):
-    n = LANES
-    row, col = iotas((n, n))
-    flat[i, :n] = jnp.where(row >= col, first, second)
-    flat[i, n : 2 * n] = corner
-    h = n // 2
-    row_h, col_h = iotas((h, n))
-    lower = pltpu.roll(narrow[h:], h, 1)
-    flat[i, 2 * n : 2 * n + h] = jnp.where(
-        (col_h >= h) | (row_h >= col_h), narrow[:h], lower
-    )
-    diagonal = row == col
-    pair = [
-        jnp.sum(jnp.where(diagonal, block, 0.0), axis=0, keepdims=True)
-        for block in (second, narrow)
-    ]
-    row_p, _ = iotas((PANEL, n))
-    shape = (PANEL, n)
-    base = 2 * n + h
-    flat[i, base : base + PANEL] = jnp.where(
-        row_p == 0,
-        jnp.broadcast_to(pair[0], shape),
-        jnp.where(row_p == 1, jnp.broadcast_to(pair[1], shape), 0.0),
-    )
-    pad = flat.shape[1] - base - PANEL
-    flat[i, base + PANEL :] = jnp.zeros((pad, n), jnp.float32)
-
-
-def unpack_squares(flat):
-    n = LANES
-    h = n // 2
-    row, col = iotas((n, n))
-    packed = flat[:n]
+def pack_pair(first, second):
+    row, col = iotas(first.shape)
+    return jnp.where(row >= col, first, second)
+
+
+def unpack_pair(packed, second_diagonal):
+    row, col = iotas(packed.shape)
     turned = packed.T
-    corner = flat[n : 2 * n]
-    folded = jnp.concatenate([flat[2 * n : 2 * n + h], jnp.zeros((h, n), jnp.float32)], axis=0)
-    slab = flat[2 * n + h : 2 * n + h + PANEL]
-    second_diagonal = jnp.broadcast_to(slab[0:1], (n, n))
-    narrow_diagonal = jnp.broadcast_to(slab[1:2], (n, n))
     first = jnp.where(row >= col, packed, turned)
     second = jnp.where(col > row, packed, turned)
-    second = jnp.where(row == col, second_diagonal, second)
-    folded_t = folded.T
-    top = jnp.where((col >= h) | (col <= row), folded, folded_t)
-    moved = pltpu.roll(pltpu.roll(folded, h, 0), h, 1)
-    moved_t = pltpu.roll(pltpu.roll(folded_t, h, 0), h, 1)
-    corner_n = jnp.where(col > row, moved, moved_t)
-    corner_n = jnp.where(row == col, narrow_diagonal, corner_n)
-    bottom = jnp.where(col < h, folded_t, corner_n)
-    return (first, corner, second, jnp.where(row < h, top, bottom))
-
-
-def squares_kernel(place, wide_hbm, narrow_hbm, keep_ref, send_ref, wides, narrows, flat, sems):
+    return first, jnp.where(row == col, second_diagonal, second)
+
+
+def fold(block):
+    h = block.shape[0] // 2
+    row, col = iotas((h, 2 * h))
+    last = pltpu.roll(block[h:], h, 1)
+    return jnp.where((col >= h) | (row >= col), block[:h], last)
+
+
+def unfold(folded, diagonal):
+    h, n = folded.shape
+    row, col = iotas((n, n))
+    block = jnp.concatenate([folded, jnp.zeros((h, n), jnp.float32)], axis=0)
+    turned = block.T
+    top = jnp.where((col >= h) | (col <= row), block, turned)
+    moved = pltpu.roll(pltpu.roll(block, h, 0), h, 1)
+    moved_turned = pltpu.roll(pltpu.roll(turned, h, 0), h, 1)
+    last = jnp.where(col > row, moved, moved_turned)
+    last = jnp.where(row == col, diagonal, last)
+    return jnp.where(row < h, top, jnp.where(col < h, turned, last))
+
+
+def diagonals(blocks, rows):
+    n = blocks[0].shape[0]
+    row, col = iotas((n, n))
+    slab_row, _ = iotas((rows, n))
+    slab = jnp.zeros((rows, n), jnp.float32)
+    for i, block in enumerate(blocks):
+        line = jnp.sum(jnp.where(row == col, block, 0.0), axis=0, keepdims=True)
+        slab = jnp.where(slab_row == i, jnp.broadcast_to(line, (rows, n)), slab)
+    return slab
+
+
+EARLY_ROWS = 144
+LATE_ROWS = 448
+
+
+def gram_kernel(place, wide_hbm, narrow_hbm, *refs):
+    a_keep, a_send, b_keep, b_send, wides, narrows, a_flat, b_flat, sems = refs
     copies = read_layers(place, (wide_hbm, narrow_hbm), (wides, narrows), sems)
     n = LANES
     for i, group in enumerate(copies):
@@ -148,64 +145,45 @@
         narrow = narrows[i]
         wcov = transposed_dot(wide, wide)
         ncov = transposed_dot(narrow, narrow)
-        pack_squares(flat, i, wcov[:n, :n], wcov[:n, n:], wcov[n:, n:], ncov)
-        write_halves(place, i, flat, keep_ref, send_ref)
-
-
-def mixed_kernel(place, wides, narrows, keep_ref, send_ref, flat):
-    for i in range(wides.shape[0]):
-        mixed = transposed_dot(narrows[i], wides[i])
-        flat[i, :LANES] = mixed[:, :LANES]
-        flat[i, LANES:] = mixed[:, LANES:]
-        write_halves(place, i, flat, keep_ref, send_ref)
-
-
-def gram_cost(wide_rows, columns):
-    return pl.CostEstimate(
-        flops=2 * wide_rows.size * columns, bytes_accessed=2 * wide_rows.size, transcendentals=0
-    )
-
-
-def squares(place, wide_rows, narrow_rows):
+        mixed = transposed_dot(narrow, wide)
+        last = wcov[n:, n:]
+        a_flat[i, :n] = pack_pair(wcov[:n, :n], ncov)
+        a_flat[i, n:] = diagonals((ncov, last), EARLY_ROWS - n)
+        write_halves(place, i, a_flat, a_keep, a_send)
+        b_flat[i, :n] = wcov[:n, n:]
+        b_flat[i, n : n + n // 2] = fold(last)
+        b_flat[i, n + n // 2 : 2 * n + n // 2] = mixed[:, :n]
+        b_flat[i, 2 * n + n // 2 :] = mixed[:, n:]
+        write_halves(place, i, b_flat, b_keep, b_send)
+
+
+def gram(place, wide_rows, narrow_rows):
     layers = wide_rows.shape[0]
-    half = 176
-    shape = jax.ShapeDtypeStruct((4, 2, half, LANES), jnp.float32)
+    early = jax.ShapeDtypeStruct((4, 2, EARLY_ROWS // 2, LANES), jnp.float32)
+    late = jax.ShapeDtypeStruct((4, 2, LATE_ROWS // 2, LANES), jnp.float32)
     return pl.pallas_call(
-        functools.partial(squares_kernel, place),
+        functools.partial(gram_kernel, place),
         in_specs=[HBM, HBM],
         out_specs=[VMEM] * 4,
-        out_shape=[
-            shape,
-            shape,
-            jax.ShapeDtypeStruct(wide_rows.shape, wide_rows.dtype),
-            jax.ShapeDtypeStruct(narrow_rows.shape, narrow_rows.dtype),
-        ],
+        out_shape=[early, early, late, late],
         scratch_shapes=[
-            pltpu.VMEM((layers, 2 * half, LANES), jnp.float32),
+            pltpu.VMEM(wide_rows.shape, wide_rows.dtype),
+            pltpu.VMEM(narrow_rows.shape, narrow_rows.dtype),
+            pltpu.VMEM((layers, EARLY_ROWS, LANES), jnp.float32),
+            pltpu.VMEM((layers, LATE_ROWS, LANES), jnp.float32),
             pltpu.SemaphoreType.DMA((layers, 2)),
         ],
-        cost_estimate=gram_cost(wide_rows, 320),
+        cost_estimate=pl.CostEstimate(
+            flops=2 * wide_rows.size * 448,
+            bytes_accessed=3 * wide_rows.size,
+            transcendentals=0,
+        ),
         compiler_params=PARAMS,
-        name="squares",
+        name="gram",
     )(
         pltpu.with_memory_space_constraint(wide_rows, pltpu.HBM),
         pltpu.with_memory_space_constraint(narrow_rows, pltpu.HBM),
     )
-
-
-def mixed_sums(place, wides, narrows):
-    layers, _, narrow = narrows.shape
-    shape = jax.ShapeDtypeStruct((4, 2, narrow, LANES), jnp.float32)
-    return pl.pallas_call(
-        functools.partial(mixed_kernel, place),
-        in_specs=[VMEM, VMEM],
-        out_specs=[VMEM, VMEM],
-        out_shape=[shape, shape],
-        scratch_shapes=[pltpu.VMEM((layers, 2 * narrow, LANES), jnp.float32)],
-        cost_estimate=gram_cost(wides, 128),
-        compiler_params=PARAMS,
-        name="mixed",
-    )(wides, narrows)
 
 
 def lane_gather(x, index):
@@ -306,118 +284,70 @@
         flat[pl.ds(start, rows), :] = piece[...]
 
 
-def first_half_kernel(place, total, *refs):
-    pieces, refs = refs[:2], refs[2:]
-    ninv_ref, wa, wl, wr, panel_ref, flat, na, nl, nr = refs
-    place_pieces(place, flat, pieces)
-    wide, narrow = wa.shape[1], na.shape[1]
-    half = LANES
-    first, corner, second, square = unpack_squares(flat)
-    row, col = iotas((half, half))
-    damp = jnp.where(row == col, DAMP, 0.0)
-    wa[:PANEL] = jnp.zeros((PANEL, wide), jnp.float32)
-    wa[PANEL + wide :] = jnp.zeros((PANEL, wide), jnp.float32)
-    na[:PANEL] = jnp.zeros((PANEL, narrow), jnp.float32)
-    na[PANEL + narrow :] = jnp.zeros((PANEL, narrow), jnp.float32)
-    corner = corner / total
-    wa[PANEL : PANEL + half, :half] = first / total + damp
-    wa[PANEL : PANEL + half, half:] = corner
-    wa[PANEL + half : PANEL + wide, :half] = corner.T
-    wa[PANEL + half : PANEL + wide, half:] = second / total + damp
-    na[PANEL : PANEL + narrow, :] = square / total + damp
-    for ref in (wl, wr, nl, nr):
-        ref[...] = jnp.zeros(ref.shape, ref.dtype)
-
-    def both(step, carry):
-        wide_panel, narrow_panel = carry
-        wide_panel = sweep_panel(wa, wl, wr, 0, step, wide_panel)
-        narrow_panel = sweep_panel(na, nl, nr, 0, step, narrow_panel)
-        return (wide_panel, narrow_panel)
-
-    start = (wa[PANEL : 2 * PANEL, :], na[PANEL : 2 * PANEL, :])
-    panel, _ = lax.fori_loop(0, LANES // PANEL, both, start)
-    panel_ref[...] = panel
-    trailing_update(na, nl, nr, narrow)
-    ninv_ref[...] = -na[PANEL : PANEL + narrow, :]
-
-
-def later_panels_kernel(begin, end, wa_in, wl_in, wr_in, panel_in, wa, wl, wr, panel_out):
-    wa[...] = wa_in[...]
-    wl[...] = wl_in[...]
-    wr[...] = wr_in[...]
-
-    def only(step, panel):
-        return sweep_panel(wa, wl, wr, 1, step, panel)
-
-    panel_out[...] = lax.fori_loop(begin, end, only, panel_in[...])
-
-
-def last_panels_kernel(begin, wa_in, wl_in, wr_in, panel_in, winv_ref, wa, wl, wr, panel):
-    later_panels_kernel(
-        begin, LANES // PANEL, wa_in, wl_in, wr_in, panel_in, wa, wl, wr, panel
-    )
-    wide = wa.shape[1]
-    trailing_update(wa, wl, wr, wide)
-    winv_ref[...] = -wa[PANEL : PANEL + wide, :]
-
-
-def sweep_cost(wide):
-    return pl.CostEstimate(
-        flops=64 * wide * wide * wide, bytes_accessed=16 * wide * wide, transcendentals=0
-    )
-
-
-def first_half(place, pieces, wide, narrow, total):
+def sweep_cost():
+    return pl.CostEstimate(flops=1 << 30, bytes_accessed=1 << 20, transcendentals=0)
+
+
+def load_damped(a_ref, block):
+    n = block.shape[0]
+    row, col = iotas(block.shape)
+    a_ref[:PANEL] = jnp.zeros((PANEL, n), jnp.float32)
+    a_ref[PANEL + n :] = jnp.zeros((PANEL, n), jnp.float32)
+    a_ref[PANEL : PANEL + n] = block + jnp.where(row == col, DAMP, 0.0)
+
+
+def sweep_all(works):
+    for _, left, right in works:
+        left[...] = jnp.zeros(left.shape, left.dtype)
+        right[...] = jnp.zeros(right.shape, right.dtype)
+
+    def step(i, panels):
+        return tuple(sweep_panel(*work, 0, i, panel) for work, panel in zip(works, panels))
+
+    size = works[0][0].shape[1]
+    lax.fori_loop(0, size // PANEL, step, tuple(a[PANEL : 2 * PANEL] for a, _, _ in works))
+    for work in works:
+        trailing_update(*work, size)
+    return [-a[PANEL : PANEL + size] for a, _, _ in works]
+
+
+def work_shapes(size):
     splits = 6 * PANEL
-    rows = pieces[0].shape[0]
-    matrix = (wide + 2 * PANEL, wide)
+    return [
+        pltpu.VMEM((size + 2 * PANEL, size), jnp.float32),
+        pltpu.VMEM((splits, size), jnp.bfloat16),
+        pltpu.VMEM((splits, size), jnp.bfloat16),
+    ]
+
+
+def early_kernel(place, total, mine, other, winv_ref, ninv_ref, slab_ref, flat, *works):
+    place_pieces(place, flat, (mine, other))
+    n = LANES
+    slab = flat[n : n + PANEL]
+    slab_ref[...] = slab
+    first, square = unpack_pair(flat[:n], jnp.broadcast_to(slab[:1], (n, n)))
+    load_damped(works[0], first / total)
+    load_damped(works[3], square / total)
+    winv_ref[...], ninv_ref[...] = sweep_all((works[:3], works[3:]))
+
+
+def early(place, pieces, total):
+    n = LANES
+    square = jax.ShapeDtypeStruct((n, n), jnp.float32)
     return pl.pallas_call(
-        functools.partial(first_half_kernel, place, total),
+        functools.partial(early_kernel, place, total),
         in_specs=[VMEM] * 2,
-        out_specs=[VMEM] * 5,
-        out_shape=[
-            jax.ShapeDtypeStruct((narrow, narrow), jnp.float32),
-            jax.ShapeDtypeStruct(matrix, jnp.float32),
-            jax.ShapeDtypeStruct((splits, wide), jnp.bfloat16),
-            jax.ShapeDtypeStruct((splits, wide), jnp.bfloat16),
-            jax.ShapeDtypeStruct((PANEL, wide), jnp.float32),
+        out_specs=[VMEM] * 3,
+        out_shape=[square, square, jax.ShapeDtypeStruct((PANEL, n), jnp.float32)],
+        scratch_shapes=[
+            pltpu.VMEM((EARLY_ROWS, n), jnp.float32),
+            *work_shapes(n),
+            *work_shapes(n),
         ],
-        scratch_shapes=[
-            pltpu.VMEM((2 * rows, LANES), jnp.float32),
-            pltpu.VMEM((narrow + 2 * PANEL, narrow), jnp.float32),
-            pltpu.VMEM((splits, narrow), jnp.bfloat16),
-            pltpu.VMEM((splits, narrow), jnp.bfloat16),
-        ],
-        cost_estimate=sweep_cost(wide),
+        cost_estimate=sweep_cost(),
         compiler_params=PARAMS,
-        name="first_half",
+        name="early",
     )(*pieces)
-
-
-def later_panels(state, begin, end):
-    return pl.pallas_call(
-        functools.partial(later_panels_kernel, begin, end),
-        in_specs=[VMEM] * 4,
-        out_specs=[VMEM] * 4,
-        out_shape=[jax.ShapeDtypeStruct(v.shape, v.dtype) for v in state],
-        cost_estimate=sweep_cost(state[0].shape[1]),
-        compiler_params=PARAMS,
-        name="later_panels",
-    )(*state)
-
-
-def last_panels(state, begin):
-    wide = state[0].shape[1]
-    return pl.pallas_call(
-        functools.partial(last_panels_kernel, begin),
-        in_specs=[VMEM] * 4,
-        out_specs=VMEM,
-        out_shape=jax.ShapeDtypeStruct((wide, wide), jnp.float32),
-        scratch_shapes=[pltpu.VMEM(v.shape, v.dtype) for v in state],
-        cost_estimate=sweep_cost(wide),
-        compiler_params=PARAMS,
-        name="last_panels",
-    )(*state)
 
 
 def aligned_rows(ref, index, count):
@@ -435,18 +365,42 @@
     return cols == 2 * PANEL and 2 * rows == LANES
 
 
-def product_kernel(place, total, rows, winv_ref, ninv_ref, mine_ref, other_ref, out_ref, flat):
-    place_pieces(place, flat, (mine_ref, other_ref))
+def dot(a, b, last=False):
+    return lax.dot_general(
+        a,
+        b,
+        (((1,), (1 if last else 0,)), ((), ())),
+        precision=HIGHEST,
+        preferred_element_type=jnp.float32,
+    )
+
+
+def late_kernel(place, total, rows, w11_ref, ninv_ref, slab_ref, mine, other, out_ref, *refs):
+    flat, winv, inner_ref = refs[:3]
+    work = refs[3:]
+    place_pieces(place, flat, (mine, other))
+    n = LANES
+    h = n // 2
+    w11 = w11_ref[...]
+    corner = flat[:n] / total
+    solved = dot(w11, corner)
+    schur = transposed_dot(corner, solved, HIGHEST)
+    last = unfold(flat[n : n + h], jnp.broadcast_to(slab_ref[1:2], (n, n)))
+    load_damped(work[0], last / total - schur)
     ninv = ninv_ref[...]
-    half = flat.shape[0] // 2
-    inner = jnp.concatenate(
-        [
-            transposed_dot(flat[h * half : (h + 1) * half] / total, ninv, HIGHEST)
-            for h in range(2)
-        ],
-        axis=0,
-    )
-    wide = winv_ref.shape[1]
+    for c in range(2):
+        start = n + h + c * n
+        inner_ref[c * n : (c + 1) * n] = transposed_dot(
+            flat[start : start + n] / total, ninv, HIGHEST
+        )
+    (sinv,) = sweep_all((work,))
+    cross = dot(solved, sinv)
+    winv[:n, :n] = w11 + dot(cross, solved, last=True)
+    winv[:n, n:] = -cross
+    winv[n:, :n] = -cross.T
+    winv[n:, n:] = sinv
+    inner = inner_ref[...]
+    wide = winv.shape[1]
     cols = wide // 2 ** len(place.dp)
     far, second = lax.axis_index(place.far), lax.axis_index(place.second)
     far_stride = 2 ** (len(place.dp) - 1)
@@ -454,7 +408,7 @@
     _, lane = iotas((PANEL, LANES))
     for j in range(4):
         index = base + (j // 2) * far_stride + (j % 2) * 2
-        picked = aligned_rows(winv_ref, index, cols)
+        picked = aligned_rows(winv, index, cols)
         update = lax.dot_general(
             picked,
             inner,
@@ -477,17 +431,25 @@
                 out_ref[block, 2 * cols :] = update
 
 
-def products(place, winv, ninv, pieces, cols, rows, total):
+def late(place, early_out, pieces, wide, rows, total):
+    cols = wide // 2 ** len(place.dp)
     height = 2 * cols + (PANEL if packs(cols, rows) else cols)
+    n = LANES
     return pl.pallas_call(
-        functools.partial(product_kernel, place, total, rows),
-        in_specs=[VMEM] * 4,
+        functools.partial(late_kernel, place, total, rows),
+        in_specs=[VMEM] * 5,
         out_specs=VMEM,
         out_shape=jax.ShapeDtypeStruct((8, height, LANES), jnp.float32),
-        scratch_shapes=[pltpu.VMEM((2 * ninv.shape[0], LANES), jnp.float32)],
+        scratch_shapes=[
+            pltpu.VMEM((LATE_ROWS, n), jnp.float32),
+            pltpu.VMEM((wide, wide), jnp.float32),
+            pltpu.VMEM((wide, n), jnp.float32),
+            *work_shapes(n),
+        ],
+        cost_estimate=sweep_cost(),
         compiler_params=PARAMS,
-        name="products",
-    )(winv, ninv, *pieces)
+        name="late",
+    )(*early_out, *pieces)
 
 
 def placing_kernel(place, owner_map, got_ref, kept_ref, update_ref):
@@ -562,46 +524,39 @@
     n_dp, n_own = 2 ** len(place.dp), 2 ** len(place.own)
     total = float(rows * n_dp * n_own)
 
-    s_keep, s_send, wides, narrows = squares(place, wide_rows, narrow_rows)
-    s_got = swap(s_send, place.core)
-    m_keep, m_send = mixed_sums(place, after(wides, s_send), narrows)
-    s_keep, m_send = lax.optimization_barrier((s_keep, m_send))
-
-    s = s_keep + s_got
-    s_got = swap_by_core(s[2:], place, 0)
-    m_got = swap(after(m_send, s), place.core)
-
-    s = s[:2] + s_got
-    s_got = swap_by_core(s[1], place, 1)
-    m = after(m_keep, s) + m_got
-    m_got = swap_by_core(m[2:], place, 0)
-
-    s = s[0] + s_got
-    s_got = swap(s[1], place.far)
-    m = after(m[:2], s) + m_got
-    m_got = swap_by_core(m[1], place, 1)
-
-    s = s[0] + s_got
+    a_keep, a_send, b_keep, b_send = gram(place, wide_rows, narrow_rows)
+    a_got = swap(a_send, place.core)
+    b_got = swap(b_send, place.core)
+
+    a = a_keep + a_got
+    a_got = swap_by_core(a[2:], place, 0)
+    b = after(b_keep, a) + b_got
+    b_got = swap_by_core(b[2:], place, 0)
+
+    a = after(a[:2], b) + a_got
+    a_got = swap_by_core(a[1], place, 1)
+    a = a[0] + a_got
+    a_keep, a_send = a[0], a[1]
+    a_got = swap(a_send, place.far)
+    b = after(b[:2], a_send) + b_got
+    b_got = swap_by_core(b[1], place, 1)
+
+    a = after(a_keep, b) + a_got
     if place.extra:
-        s = lax.psum(s, place.extra)
-    s_got = swap(s, place.near)
-    m = after(m[0], s) + m_got
-    m_got = swap(m[1], place.far)
-
-    s = s + s_got
-    ninv, *state = first_half(place, [s, swap(s, place.core)], wide, narrow, total)
-    m = after(m[0], state[0]) + m_got
+        a = lax.psum(a, place.extra)
+    b = after(b[0], a) + b_got
+    b_keep, b_send = b[0], b[1]
+    b_got = swap(b_send, place.far)
+
+    a = after(a, b_send)
+    a = a + swap(a, place.near)
+    early_out = early(place, [a, swap(a, place.core)], total)
+    b = after(b_keep, early_out[0]) + b_got
     if place.extra:
-        m = lax.psum(m, place.extra)
-    m_got = swap(m, place.near)
-    middle = LANES // PANEL // 2
-    state = later_panels(state, 0, middle)
-    m = after(m, state[0]) + m_got
-    m_got = swap(m, place.core)
-    winv = last_panels(state, middle)
-    m = [m, m_got]
+        b = lax.psum(b, place.extra)
+    b = b + swap(b, place.near)
     cols, own_rows = wide // n_dp, narrow // n_own
-    sent = products(place, winv, ninv, m, cols, own_rows, total)
+    sent = late(place, early_out, [b, swap(b, place.core)], wide, own_rows, total)
     got = lax.all_to_all(sent, (place.far, place.second, place.first), 0, 0)
     kept, update = placing(
         place, owner_map, got, wide, cols, layers // n_own + 1, own_rows

time: 65.5 us -> 72.3 us (1.10)
  waiting for transfers between devices: 13.6 us -> 23.1 us
  starting transfers between devices: 19.7 us -> 16 us
  blocking collectives: 12.7 us -> 13.9 us
    ppermute x8, waiting for transfers between devices: 4.65 us -> 12.2 us  [swap(): return lax.ppermute(value, axis, [(0, 1), (1, 0)])]
    ppermute x8, starting transfers between devices: 11.5 us -> 9.27 us  [swap(): return lax.ppermute(value, axis, [(0, 1), (1, 0)])]
    ppermute x4, waiting for transfers between devices: 8.95 us -> 11 us  [swap_by_core(): return lax.ppermute(value, (place.second, place.core, place.first), pairs)]
    ppermute x4, starting transfers between devices: 8.17 us -> 6.68 us  [swap_by_core(): return lax.ppermute(value, (place.second, place.core, place.first), pairs)]
    all_to_all x1, blocking collectives: 12.7 us -> 13.9 us  [on_device(): got = lax.all_to_all(sent, (place.far, place.second, place.first), 0, 0)]
    pallas_call x6 -> x3, Pallas kernels: 16.9 us -> 16.8 us  [the longest x1 5.87 us: late(): pl.pallas_call(functools.partial(late_kernel, place, total, rows), in_spe...]
  transfers between devices with their start and end apart: 12 -> 12, of which waited for: 6 -> 10; matrix products, arithmetic and copies ran while one was open for 0% -> 0% of each run, Pallas kernels for 18% -> 8%
where the time goes in v5:
time: 72.3 us; the launch traced here: 72.2 us
  waiting for transfers between devices  23.1 us (32%)
  Pallas kernels  18 us (25%)
  starting transfers between devices  16 us (22%)
  blocking collectives  13.9 us (19%)
  between operations  0.74 us (1%)
    all_to_all x1, blocking collectives, on_device(): got = lax.all_to_all(sent, (place.far, place.second, place.first), 0, 0)  13.9 us
    ppermute x8, waiting for transfers between devices, swap(): return lax.ppermute(value, axis, [(0, 1), (1, 0)])  12.2 us
    ppermute x4, waiting for transfers between devices, swap_by_core(): return lax.ppermute(value, (place.second, place.core, place.first), pairs)  11 us
    ppermute x8, starting transfers between devices, swap(): return lax.ppermute(value, axis, [(0, 1), (1, 0)])  9.27 us
    ppermute x4, starting transfers between devices, swap_by_core(): return lax.ppermute(value, (place.second, place.core, place.first), pairs)  6.68 us
    pallas_call x1, Pallas kernels, late(): pl.pallas_call(functools.partial(late_kernel, place, total, rows), in_spe...  5.87 us
    pallas_call x1, Pallas kernels, early(): pl.pallas_call(functools.partial(early_kernel, place, total), in_specs=[V...  5.8 us
    pallas_call x1, Pallas kernels, gram(): pl.pallas_call(functools.partial(gram_kernel, place), in_specs=[HBM, HBM]...  5.11 us
  transfers between devices with their start and end apart: 12, of which 10 were waited for; matrix products, arithmetic and copies ran while one was open for 0% of the time, Pallas kernels for 8%

profile of v5, /device:TPU:0, one launch (start us, length us, event | category | flops | bytes accessed | tf_op | source)
XLA Modules:
  0.0 72.2 jit_solution(4622957934994340739)
XLA Ops:
  0.6 5.1 %gram.1 = (f32[4,2,72,128]{3,2,1,0:T(8,128)S(1)}, f32[4,2,72,128]{3,2,1,0:T(8,128)S(1)}, f32[4,2,224,128]{3,2,1,0:T(8,128)S(1)}, f32[4,2,224,128]{3,2,1,0:T(8,128)S(1)}) custom-call(bf16[8,768,256]{2,1,0:T(8,128)(2,1)} %wide_hbm.1, bf16[8,768,128]{2,1,0:T(8,128)(2,1)} %narrow_hbm.1), custom_call_target="tpu_custom_call" | custom-call | flops 1409286144 | bytes 4718592 | tf_op jit(solution)/shard_map/gram/pallas_call | solution.py:164
  5.7 0.5 collective-permute-start.1
  6.4 2.4 %collective-permute-done = f32[4,2,72,128]{3,2,1,0:T(8,128)S(1)} collective-permute-done((f32[4,2,72,128]{3,2,1,0:T(8,128)S(1)}, f32[4,2,72,128]{3,2,1,0:T(8,128)S(1)}, u32[]{:S(2)}, u32[]{:S(2)}) %collective-permute-start) | collective-permute-done | bytes 294944 | tf_op jit(solution)/shard_map/ppermute | solution.py:503
  8.9 2.9 %collective-permute-start.2 = (f32[2,2,72,128]{3,2,1,0:T(8,128)S(1)}, f32[2,2,72,128]{3,2,1,0:T(8,128)S(1)}, u32[]{:S(2)}, u32[]{:S(2)}) collective-permute-start(f32[2,2,72,128]{3,2,1,0:T(8,128)S(1)} %get-tuple-element.38), channel_id=1, source_target_pairs={{0,1},{1,0},{2,6},{3,7},{4,5},{5,4},{6,2},{7,3},{8,9},{9,8},{10,14... | collective-permute-start | bytes 442376 | tf_op jit(solution)/shard_map/ppermute | solution.py:514
  11.8 0.1 add.31
  11.9 3.0 %collective-permute-done.2 = f32[2,2,72,128]{3,2,1,0:T(8,128)S(1)} collective-permute-done((f32[2,2,72,128]{3,2,1,0:T(8,128)S(1)}, f32[2,2,72,128]{3,2,1,0:T(8,128)S(1)}, u32[]{:S(2)}, u32[]{:S(2)}) %collective-permute-start.2) | collective-permute-done | bytes 147488 | tf_op jit(solution)/shard_map/ppermute | solution.py:514
  15.0 2.1 %collective-permute-start.3 = (f32[2,72,128]{2,1,0:T(8,128)S(1)}, f32[2,72,128]{2,1,0:T(8,128)S(1)}, u32[]{:S(2)}, u32[]{:S(2)}) collective-permute-start(f32[2,72,128]{2,1,0:T(8,128)S(1)} %slice_bitcast_fusion.4), channel_id=1, source_target_pairs={{0,4},{1,5},{2,3},{3,2},{4,0},{5,1},{6,7},{7,6},{8,12},{9,13},{10,... | collective-permute-start | bytes 221192 | tf_op jit(solution)/shard_map/ppermute | solution.py:514
  17.1 1.6 %collective-permute-start.4 = (f32[2,2,224,128]{3,2,1,0:T(8,128)S(1)}, f32[2,2,224,128]{3,2,1,0:T(8,128)S(1)}, u32[]{:S(2)}, u32[]{:S(2)}) collective-permute-start(f32[2,2,224,128]{3,2,1,0:T(8,128)S(1)} %get-tuple-element.34), channel_id=1, source_target_pairs={{0,1},{1,0},{2,6},{3,7},{4,5},{5,4},{6,2},{7,3},{8,9},{9,8},{10,14... | collective-permute-start | bytes 1376264 | tf_op jit(solution)/shard_map/ppermute | solution.py:514
  18.7 1.3 %collective-permute-done.3 = f32[2,72,128]{2,1,0:T(8,128)S(1)} collective-permute-done((f32[2,72,128]{2,1,0:T(8,128)S(1)}, f32[2,72,128]{2,1,0:T(8,128)S(1)}, u32[]{:S(2)}, u32[]{:S(2)}) %collective-permute-start.3) | collective-permute-done | bytes 73760 | tf_op jit(solution)/shard_map/ppermute | solution.py:514
  20.0 5.6 %collective-permute-done.4 = f32[2,2,224,128]{3,2,1,0:T(8,128)S(1)} collective-permute-done((f32[2,2,224,128]{3,2,1,0:T(8,128)S(1)}, f32[2,2,224,128]{3,2,1,0:T(8,128)S(1)}, u32[]{:S(2)}, u32[]{:S(2)}) %collective-permute-start.4) | collective-permute-done | bytes 458784 | tf_op jit(solution)/shard_map/ppermute | solution.py:514
  25.9 3.1 %collective-permute-start.5 = (f32[72,128]{1,0:T(8,128)S(1)}, f32[72,128]{1,0:T(8,128)S(1)}, u32[]{:S(2)}, u32[]{:S(2)}) collective-permute-start(f32[72,128]{1,0:T(8,128)S(1)} %get-tuple-element.42), channel_id=1, source_target_pairs={{0,16},{16,0},{1,17},{17,1},{2,18},{18,2},{3,19},{19,3},{4,20},{20... | collective-permute-start | bytes 110600 | tf_op jit(solution)/shard_map/ppermute | solution.py:503
  28.9 1.9 %collective-permute-done.5 = f32[72,128]{1,0:T(8,128)S(1)} collective-permute-done((f32[72,128]{1,0:T(8,128)S(1)}, f32[72,128]{1,0:T(8,128)S(1)}, u32[]{:S(2)}, u32[]{:S(2)}) %collective-permute-start.5) | collective-permute-done | bytes 36896 | tf_op jit(solution)/shard_map/ppermute | solution.py:503
  30.9 1.0 %collective-permute-done.6 = f32[2,224,128]{2,1,0:T(8,128)S(1)} collective-permute-done((f32[2,224,128]{2,1,0:T(8,128)S(1)}, f32[2,224,128]{2,1,0:T(8,128)S(1)}, u32[]{:S(2)}, u32[]{:S(2)}) %collective-permute-start.6) | collective-permute-done | bytes 229408 | tf_op jit(solution)/shard_map/ppermute | solution.py:514
  31.9 1.6 %collective-permute-start.7 = (f32[72,128]{1,0:T(8,128)S(1)}, f32[72,128]{1,0:T(8,128)S(1)}, u32[]{:S(2)}, u32[]{:S(2)}) collective-permute-start(f32[72,128]{1,0:T(8,128)S(1)} %add.35), channel_id=1, source_target_pairs={{0,8},{8,0},{1,9},{9,1},{2,10},{10,2},{3,11},{11,3},{4,12},{12,4},... | collective-permute-start | bytes 110600 | tf_op jit(solution)/shard_map/ppermute | solution.py:503
  33.6 2.4 %collective-permute-done.7 = f32[72,128]{1,0:T(8,128)S(1)} collective-permute-done((f32[72,128]{1,0:T(8,128)S(1)}, f32[72,128]{1,0:T(8,128)S(1)}, u32[]{:S(2)}, u32[]{:S(2)}) %collective-permute-start.7) | collective-permute-done | bytes 36896 | tf_op jit(solution)/shard_map/ppermute | solution.py:503
  36.0 2.7 %collective-permute-start.9 = (f32[224,128]{1,0:T(8,128)S(1)}, f32[224,128]{1,0:T(8,128)S(1)}, u32[]{:S(2)}, u32[]{:S(2)}) collective-permute-start(f32[224,128]{1,0:T(8,128)S(1)} %get-tuple-element.41), channel_id=1, source_target_pairs={{0,16},{16,0},{1,17},{17,1},{2,18},{18,2},{3,19},{19,3},{4,20},{20... | collective-permute-start | bytes 344072 | tf_op jit(solution)/shard_map/ppermute | solution.py:503
  38.6 5.8 %early.1 = (f32[128,128]{1,0:T(8,128)S(1)}, f32[128,128]{1,0:T(8,128)S(1)}, f32[8,128]{1,0:T(8,128)S(1)}) custom-call(f32[72,128]{1,0:T(8,128)S(1)} %add.37.mine, f32[72,128]{1,0:T(8,128)S(1)} %collective-permute-done.8.other), custom_call_target="tpu_custom_call" | custom-call | flops 1073741824 | bytes 1048576 | tf_op jit(solution)/shard_map/early/pallas_call | solution.py:337
  44.4 0.4 collective-permute-done.9
  44.9 1.2 %collective-permute-start.10 = (f32[224,128]{1,0:T(8,128)S(1)}, f32[224,128]{1,0:T(8,128)S(1)}, u32[]{:S(2)}, u32[]{:S(2)}) collective-permute-start(f32[224,128]{1,0:T(8,128)S(1)} %add.38), channel_id=1, source_target_pairs={{0,8},{8,0},{1,9},{9,1},{2,10},{10,2},{3,11},{11,3},{4,12},{12,4},... | collective-permute-start | bytes 344072 | tf_op jit(solution)/shard_map/ppermute | solution.py:503
  46.1 3.6 %collective-permute-done.10 = f32[224,128]{1,0:T(8,128)S(1)} collective-permute-done((f32[224,128]{1,0:T(8,128)S(1)}, f32[224,128]{1,0:T(8,128)S(1)}, u32[]{:S(2)}, u32[]{:S(2)}) %collective-permute-start.10) | collective-permute-done | bytes 114720 | tf_op jit(solution)/shard_map/ppermute | solution.py:503
  49.8 1.3 %collective-permute-done.11.other = f32[224,128]{1,0:T(8,128)S(1)} collective-permute-done((f32[224,128]{1,0:T(8,128)S(1)}, f32[224,128]{1,0:T(8,128)S(1)}, u32[]{:S(2)}, u32[]{:S(2)}) %collective-permute-start.11) | collective-permute-done | bytes 114720 | tf_op jit(solution)/shard_map/ppermute | solution.py:503
  51.2 5.9 %late.1 = f32[8,40,128]{2,1,0:T(8,128)S(1)} custom-call(f32[128,128]{1,0:T(8,128)S(1)} %get-tuple-element.28.w11_ref, f32[128,128]{1,0:T(8,128)S(1)} %get-tuple-element.29.ninv_ref, f32[8,128]{1,0:T(8,128)S(1)} %get-tuple-element.30.slab_ref, f32[224,128]{1,0:T(8,128)S(1)} %add.39.mine, f32[224,128]{1,0:T(8,128)S(1)} %collective-permute-done.11.other), custom_call_target="tpu_custom_call" | custom-call | flops 1073741824 | bytes 1048576 | tf_op jit(solution)/shard_map/late/pallas_call | solution.py:438
  57.0 13.9 %all_to_all.5.got_ref = f32[8,40,128]{2,1,0:T(8,128)S(1)} all-to-all(f32[8,40,128]{2,1,0:T(8,128)S(1)} %late.1), channel_id=1, replica_groups=mesh['dp0'=2,'dp1'=2,'dp2'=2,'dp3'=2,'own0'=2] {'dp0','dp2','own0'}, dimensions={0} | all-to-all | bytes 327680 | tf_op jit(solution)/shard_map/all_to_all | solution.py:560
  70.9 1.3 %placing.1 = (f32[5,16,256]{2,1,0:T(8,128)}, f32[8,16,64]{2,1,0:T(8,128)}) custom-call(s32[8]{0:T(128)S(1)} %copy-done, f32[8,40,128]{2,1,0:T(8,128)S(1)} %all_to_all.5.got_ref), custom_call_target="tpu_custom_call" | custom-call | tf_op jit(solution)/shard_map/placing/pallas_call | solution.py:489
  (23 shorter events, 0.6 us)
Async XLA Ops:
  5.7 6.0 %collective-permute-start.1 = (f32[4,2,224,128]{3,2,1,0:T(8,128)S(1)}, f32[4,2,224,128]{3,2,1,0:T(8,128)S(1)}, u32[]{:S(2)}, u32[]{:S(2)}) collective-permute-start(f32[4,2,224,128]{3,2,1,0:T(8,128)S(1)} %get-tuple-element.22), channel_id=1, source_target_pairs={{0,2},{2,0},{1,3},{3,1},{4,6},{6,4},{5,7},{7,5},{8,10},{10,8},{9,1... | collective-permute-start | bytes 2752520 | tf_op jit(solution)/shard_map/ppermute | solution.py:503
  6.3 2.5 %collective-permute-start = (f32[4,2,72,128]{3,2,1,0:T(8,128)S(1)}, f32[4,2,72,128]{3,2,1,0:T(8,128)S(1)}, u32[]{:S(2)}, u32[]{:S(2)}) collective-permute-start(f32[4,2,72,128]{3,2,1,0:T(8,128)S(1)} %get-tuple-element.19), channel_id=1, source_target_pairs={{0,2},{2,0},{1,3},{3,1},{4,6},{6,4},{5,7},{7,5},{8,10},{10,8},{9,1... | collective-permute-start | bytes 884744 | tf_op jit(solution)/shard_map/ppermute | solution.py:503
  8.9 6.0 %collective-permute-start.2 = (f32[2,2,72,128]{3,2,1,0:T(8,128)S(1)}, f32[2,2,72,128]{3,2,1,0:T(8,128)S(1)}, u32[]{:S(2)}, u32[]{:S(2)}) collective-permute-start(f32[2,2,72,128]{3,2,1,0:T(8,128)S(1)} %get-tuple-element.38), channel_id=1, source_target_pairs={{0,1},{1,0},{2,6},{3,7},{4,5},{5,4},{6,2},{7,3},{8,9},{9,8},{10,14... | collective-permute-start | bytes 442376 | tf_op jit(solution)/shard_map/ppermute | solution.py:514
  15.0 5.1 %collective-permute-start.3 = (f32[2,72,128]{2,1,0:T(8,128)S(1)}, f32[2,72,128]{2,1,0:T(8,128)S(1)}, u32[]{:S(2)}, u32[]{:S(2)}) collective-permute-start(f32[2,72,128]{2,1,0:T(8,128)S(1)} %slice_bitcast_fusion.4), channel_id=1, source_target_pairs={{0,4},{1,5},{2,3},{3,2},{4,0},{5,1},{6,7},{7,6},{8,12},{9,13},{10,... | collective-permute-start | bytes 221192 | tf_op jit(solution)/shard_map/ppermute | solution.py:514
  17.1 8.5 %collective-permute-start.4 = (f32[2,2,224,128]{3,2,1,0:T(8,128)S(1)}, f32[2,2,224,128]{3,2,1,0:T(8,128)S(1)}, u32[]{:S(2)}, u32[]{:S(2)}) collective-permute-start(f32[2,2,224,128]{3,2,1,0:T(8,128)S(1)} %get-tuple-element.34), channel_id=1, source_target_pairs={{0,1},{1,0},{2,6},{3,7},{4,5},{5,4},{6,2},{7,3},{8,9},{9,8},{10,14... | collective-permute-start | bytes 1376264 | tf_op jit(solution)/shard_map/ppermute | solution.py:514
  25.8 6.1 %collective-permute-start.6 = (f32[2,224,128]{2,1,0:T(8,128)S(1)}, f32[2,224,128]{2,1,0:T(8,128)S(1)}, u32[]{:S(2)}, u32[]{:S(2)}) collective-permute-start(f32[2,224,128]{2,1,0:T(8,128)S(1)} %get-tuple-element.36), channel_id=1, source_target_pairs={{0,4},{1,5},{2,3},{3,2},{4,0},{5,1},{6,7},{7,6},{8,12},{9,13},{10,... | collective-permute-start | bytes 688136 | tf_op jit(solution)/shard_map/ppermute | solution.py:514
  25.9 5.0 %collective-permute-start.5 = (f32[72,128]{1,0:T(8,128)S(1)}, f32[72,128]{1,0:T(8,128)S(1)}, u32[]{:S(2)}, u32[]{:S(2)}) collective-permute-start(f32[72,128]{1,0:T(8,128)S(1)} %get-tuple-element.42), channel_id=1, source_target_pairs={{0,16},{16,0},{1,17},{17,1},{2,18},{18,2},{3,19},{19,3},{4,20},{20... | collective-permute-start | bytes 110600 | tf_op jit(solution)/shard_map/ppermute | solution.py:503
  31.9 4.0 %collective-permute-start.7 = (f32[72,128]{1,0:T(8,128)S(1)}, f32[72,128]{1,0:T(8,128)S(1)}, u32[]{:S(2)}, u32[]{:S(2)}) collective-permute-start(f32[72,128]{1,0:T(8,128)S(1)} %add.35), channel_id=1, source_target_pairs={{0,8},{8,0},{1,9},{9,1},{2,10},{10,2},{3,11},{11,3},{4,12},{12,4},... | collective-permute-start | bytes 110600 | tf_op jit(solution)/shard_map/ppermute | solution.py:503
  36.0 2.7 %collective-permute-start.8 = (f32[72,128]{1,0:T(8,128)S(1)}, f32[72,128]{1,0:T(8,128)S(1)}, u32[]{:S(2)}, u32[]{:S(2)}) collective-permute-start(f32[72,128]{1,0:T(8,128)S(1)} %add.37.mine), channel_id=1, source_target_pairs={{0,2},{2,0},{1,3},{3,1},{4,6},{6,4},{5,7},{7,5},{8,10},{10,8},{9,1... | collective-permute-start | bytes 110600 | tf_op jit(solution)/shard_map/ppermute | solution.py:503
  36.0 8.9 %collective-permute-start.9 = (f32[224,128]{1,0:T(8,128)S(1)}, f32[224,128]{1,0:T(8,128)S(1)}, u32[]{:S(2)}, u32[]{:S(2)}) collective-permute-start(f32[224,128]{1,0:T(8,128)S(1)} %get-tuple-element.41), channel_id=1, source_target_pairs={{0,16},{16,0},{1,17},{17,1},{2,18},{18,2},{3,19},{19,3},{4,20},{20... | collective-permute-start | bytes 344072 | tf_op jit(solution)/shard_map/ppermute | solution.py:503
  44.4 26.5 %copy-start = (s32[8]{0:T(128)S(1)}, s32[8]{0:T(128)}, u32[]{:S(2)}) copy-start(s32[8]{0:T(128)} %owner_map.1) | copy-start | bytes 100
  44.9 4.9 %collective-permute-start.10 = (f32[224,128]{1,0:T(8,128)S(1)}, f32[224,128]{1,0:T(8,128)S(1)}, u32[]{:S(2)}, u32[]{:S(2)}) collective-permute-start(f32[224,128]{1,0:T(8,128)S(1)} %add.38), channel_id=1, source_target_pairs={{0,8},{8,0},{1,9},{9,1},{2,10},{10,2},{3,11},{11,3},{4,12},{12,4},... | collective-permute-start | bytes 344072 | tf_op jit(solution)/shard_map/ppermute | solution.py:503
  49.8 1.4 %collective-permute-start.11 = (f32[224,128]{1,0:T(8,128)S(1)}, f32[224,128]{1,0:T(8,128)S(1)}, u32[]{:S(2)}, u32[]{:S(2)}) collective-permute-start(f32[224,128]{1,0:T(8,128)S(1)} %add.39.mine), channel_id=1, source_target_pairs={{0,2},{2,0},{1,3},{3,1},{4,6},{6,4},{5,7},{7,5},{8,10},{10,8},{9,1... | collective-permute-start | bytes 344072 | tf_op jit(solution)/shard_map/ppermute | solution.py:503

commit v6 on v5

--- a/solution.py
+++ b/solution.py
@@ -67,16 +67,17 @@
     return copies
 
 
-def write_halves(place, i, flat, keep_ref, send_ref):
-    rows = keep_ref.shape[2]
+def write_halves(place, i, first_row, flat, keep_ref, send_ref):
+    rows = flat.shape[1] // 2
     core = lax.axis_index(place.core)
     z, y, x = i // 4, (i // 2) % 2, i % 2
     mine = jnp.where(core == 0, x * 2 + y, y * 2 + x)
     other = jnp.where(core == 0, y * 2 + x, x * 2 + y)
     kept = pl.multiple_of(core * rows, PANEL)
     sent = pl.multiple_of((1 - core) * rows, PANEL)
-    keep_ref[mine, z] = flat[i, pl.ds(kept, rows), :]
-    send_ref[other, z] = flat[i, pl.ds(sent, rows), :]
+    there = slice(first_row, first_row + rows)
+    keep_ref[mine, z, there] = flat[i, pl.ds(kept, rows), :]
+    send_ref[other, z, there] = flat[i, pl.ds(sent, rows), :]
 
 
 def iotas(shape):
@@ -135,7 +136,7 @@
 
 
 def gram_kernel(place, wide_hbm, narrow_hbm, *refs):
-    a_keep, a_send, b_keep, b_send, wides, narrows, a_flat, b_flat, sems = refs
+    keep, send, wides, narrows, a_flat, b_flat, sems = refs
     copies = read_layers(place, (wide_hbm, narrow_hbm), (wides, narrows), sems)
     n = LANES
     for i, group in enumerate(copies):
@@ -149,23 +150,22 @@
         last = wcov[n:, n:]
         a_flat[i, :n] = pack_pair(wcov[:n, :n], ncov)
         a_flat[i, n:] = diagonals((ncov, last), EARLY_ROWS - n)
-        write_halves(place, i, a_flat, a_keep, a_send)
+        write_halves(place, i, 0, a_flat, keep, send)
         b_flat[i, :n] = wcov[:n, n:]
         b_flat[i, n : n + n // 2] = fold(last)
         b_flat[i, n + n // 2 : 2 * n + n // 2] = mixed[:, :n]
         b_flat[i, 2 * n + n // 2 :] = mixed[:, n:]
-        write_halves(place, i, b_flat, b_keep, b_send)
+        write_halves(place, i, EARLY_ROWS // 2, b_flat, keep, send)
 
 
 def gram(place, wide_rows, narrow_rows):
     layers = wide_rows.shape[0]
-    early = jax.ShapeDtypeStruct((4, 2, EARLY_ROWS // 2, LANES), jnp.float32)
-    late = jax.ShapeDtypeStruct((4, 2, LATE_ROWS // 2, LANES), jnp.float32)
+    half = jax.ShapeDtypeStruct((4, 2, (EARLY_ROWS + LATE_ROWS) // 2, LANES), jnp.float32)
     return pl.pallas_call(
         functools.partial(gram_kernel, place),
         in_specs=[HBM, HBM],
-        out_specs=[VMEM] * 4,
-        out_shape=[early, early, late, late],
+        out_specs=[VMEM] * 2,
+        out_shape=[half, half],
         scratch_shapes=[
             pltpu.VMEM(wide_rows.shape, wide_rows.dtype),
             pltpu.VMEM(narrow_rows.shape, narrow_rows.dtype),
@@ -221,7 +221,10 @@
         for i in range(j, PANEL):
             d[i][j] = lane_gather(rows[j][tile], index[i])
     own = (lane >= first) & (lane < first + PANEL)
+    last = first == LANES - PANEL
+    next_lane = jnp.where(last, 0, first + PANEL) + sub
     q = [[None] * tiles for _ in range(PANEL)]
+    weights = [None] * PANEL
     factor = [[None] * PANEL for _ in range(PANEL)]
     for k in range(PANEL):
         scale = lax.rsqrt(d[k][k])
@@ -237,6 +240,13 @@
             for j in range(k):
                 value = value - factor[k][j] * q[j][t]
             q[k][t] = value * scale
+        source = rows[k][tile]
+        if tile + 1 < tiles:
+            source = jnp.where(last, rows[k][tile + 1], source)
+        value = lane_gather(source, next_lane)
+        for j in range(k):
+            value = value - factor[k][j] * weights[j]
+        weights[k] = value * scale
 
     packed = []
     for t in range(tiles):
@@ -256,14 +266,6 @@
 
     after = pl.multiple_of(base + 2 * PANEL, PANEL)
     following = a_ref[pl.ds(after, PANEL), :]
-    last = first == LANES - PANEL
-    next_lane = jnp.where(last, 0, first + PANEL) + sub
-    weights = []
-    for k in range(PANEL):
-        source = q[k][tile]
-        if tile + 1 < tiles:
-            source = jnp.where(last, q[k][tile + 1], source)
-        weights.append(lane_gather(source, next_lane))
     result = []
     for t in range(tiles):
         value = following[:, LANES * t : LANES * (t + 1)]
@@ -276,12 +278,13 @@
     return jnp.concatenate(result, axis=1) if tiles > 1 else result[0]
 
 
-def place_pieces(place, flat, pieces):
+def place_pieces(place, pieces, a_flat, b_flat):
     core = lax.axis_index(place.core)
-    rows = pieces[0].shape[0]
+    a_rows, b_rows = a_flat.shape[0] // 2, b_flat.shape[0] // 2
     for r, piece in enumerate(pieces):
-        start = pl.multiple_of(jnp.bitwise_xor(core, r) * rows, PANEL)
-        flat[pl.ds(start, rows), :] = piece[...]
+        half = jnp.bitwise_xor(core, r)
+        a_flat[pl.ds(pl.multiple_of(half * a_rows, PANEL), a_rows), :] = piece[:a_rows]
+        b_flat[pl.ds(pl.multiple_of(half * b_rows, PANEL), b_rows), :] = piece[a_rows:]
 
 
 def sweep_cost():
@@ -318,36 +321,6 @@
         pltpu.VMEM((splits, size), jnp.bfloat16),
         pltpu.VMEM((splits, size), jnp.bfloat16),
     ]
-
-
-def early_kernel(place, total, mine, other, winv_ref, ninv_ref, slab_ref, flat, *works):
-    place_pieces(place, flat, (mine, other))
-    n = LANES
-    slab = flat[n : n + PANEL]
-    slab_ref[...] = slab
-    first, square = unpack_pair(flat[:n], jnp.broadcast_to(slab[:1], (n, n)))
-    load_damped(works[0], first / total)
-    load_damped(works[3], square / total)
-    winv_ref[...], ninv_ref[...] = sweep_all((works[:3], works[3:]))
-
-
-def early(place, pieces, total):
-    n = LANES
-    square = jax.ShapeDtypeStruct((n, n), jnp.float32)
-    return pl.pallas_call(
-        functools.partial(early_kernel, place, total),
-        in_specs=[VMEM] * 2,
-        out_specs=[VMEM] * 3,
-        out_shape=[square, square, jax.ShapeDtypeStruct((PANEL, n), jnp.float32)],
-        scratch_shapes=[
-            pltpu.VMEM((EARLY_ROWS, n), jnp.float32),
-            *work_shapes(n),
-            *work_shapes(n),
-        ],
-        cost_estimate=sweep_cost(),
-        compiler_params=PARAMS,
-        name="early",
-    )(*pieces)
 
 
 def aligned_rows(ref, index, count):
@@ -375,27 +348,31 @@
     )
 
 
-def late_kernel(place, total, rows, w11_ref, ninv_ref, slab_ref, mine, other, out_ref, *refs):
-    flat, winv, inner_ref = refs[:3]
-    work = refs[3:]
-    place_pieces(place, flat, (mine, other))
+def inverse_kernel(place, total, rows, mine, other, out_ref, *refs):
+    a_flat, b_flat, winv, inner_ref = refs[:4]
+    first_work, narrow_work, last_work = refs[4:7], refs[7:10], refs[10:]
+    place_pieces(place, (mine, other), a_flat, b_flat)
     n = LANES
     h = n // 2
-    w11 = w11_ref[...]
-    corner = flat[:n] / total
+    slab = a_flat[n : n + PANEL]
+    first, square = unpack_pair(a_flat[:n], jnp.broadcast_to(slab[:1], (n, n)))
+    load_damped(first_work[0], first / total)
+    load_damped(narrow_work[0], square / total)
+    w11, ninv = sweep_all((first_work, narrow_work))
+    corner = b_flat[:n] / total
     solved = dot(w11, corner)
     schur = transposed_dot(corner, solved, HIGHEST)
-    last = unfold(flat[n : n + h], jnp.broadcast_to(slab_ref[1:2], (n, n)))
-    load_damped(work[0], last / total - schur)
-    ninv = ninv_ref[...]
+    last = unfold(b_flat[n : n + h], jnp.broadcast_to(slab[1:2], (n, n)))
+    load_damped(last_work[0], last / total - schur)
     for c in range(2):
         start = n + h + c * n
         inner_ref[c * n : (c + 1) * n] = transposed_dot(
-            flat[start : start + n] / total, ninv, HIGHEST
+            b_flat[start : start + n] / total, ninv, HIGHEST
         )
-    (sinv,) = sweep_all((work,))
+    winv[:n, :n] = w11
+    (sinv,) = sweep_all((last_work,))
     cross = dot(solved, sinv)
-    winv[:n, :n] = w11 + dot(cross, solved, last=True)
+    winv[:n, :n] += dot(cross, solved, last=True)
     winv[:n, n:] = -cross
     winv[n:, :n] = -cross.T
     winv[n:, n:] = sinv
@@ -431,25 +408,28 @@
                 out_ref[block, 2 * cols :] = update
 
 
-def late(place, early_out, pieces, wide, rows, total):
+def inverses(place, pieces, wide, rows, total):
     cols = wide // 2 ** len(place.dp)
     height = 2 * cols + (PANEL if packs(cols, rows) else cols)
     n = LANES
     return pl.pallas_call(
-        functools.partial(late_kernel, place, total, rows),
-        in_specs=[VMEM] * 5,
+        functools.partial(inverse_kernel, place, total, rows),
+        in_specs=[VMEM] * 2,
         out_specs=VMEM,
         out_shape=jax.ShapeDtypeStruct((8, height, LANES), jnp.float32),
         scratch_shapes=[
+            pltpu.VMEM((EARLY_ROWS, n), jnp.float32),
             pltpu.VMEM((LATE_ROWS, n), jnp.float32),
             pltpu.VMEM((wide, wide), jnp.float32),
             pltpu.VMEM((wide, n), jnp.float32),
             *work_shapes(n),
+            *work_shapes(n),
+            *work_shapes(n),
         ],
         cost_estimate=sweep_cost(),
         compiler_params=PARAMS,
-        name="late",
-    )(*early_out, *pieces)
+        name="inverses",
+    )(*pieces)
 
 
 def placing_kernel(place, owner_map, got_ref, kept_ref, update_ref):
@@ -514,8 +494,8 @@
     return lax.ppermute(value, (place.second, place.core, place.first), pairs)
 
 
-def after(value, *others):
-    return lax.optimization_barrier((value,) + others)[0]
+def in_two(value, exchange):
+    return jnp.stack([exchange(value[0]), exchange(value[1])])
 
 
 def on_device(place, wide_rows, narrow_rows, owner_map):
@@ -524,39 +504,16 @@
     n_dp, n_own = 2 ** len(place.dp), 2 ** len(place.own)
     total = float(rows * n_dp * n_own)
 
-    a_keep, a_send, b_keep, b_send = gram(place, wide_rows, narrow_rows)
-    a_got = swap(a_send, place.core)
-    b_got = swap(b_send, place.core)
-
-    a = a_keep + a_got
-    a_got = swap_by_core(a[2:], place, 0)
-    b = after(b_keep, a) + b_got
-    b_got = swap_by_core(b[2:], place, 0)
-
-    a = after(a[:2], b) + a_got
-    a_got = swap_by_core(a[1], place, 1)
-    a = a[0] + a_got
-    a_keep, a_send = a[0], a[1]
-    a_got = swap(a_send, place.far)
-    b = after(b[:2], a_send) + b_got
-    b_got = swap_by_core(b[1], place, 1)
-
-    a = after(a_keep, b) + a_got
+    s_keep, s_send = gram(place, wide_rows, narrow_rows)
+    s = s_keep + swap(s_send, place.core)
+    s = s[:2] + in_two(s[2:], lambda v: swap_by_core(v, place, 0))
+    s = s[0] + in_two(s[1], lambda v: swap_by_core(v, place, 1))
+    s = s[0] + swap(s[1], place.far)
+    s = s + swap(s, place.near)
     if place.extra:
-        a = lax.psum(a, place.extra)
-    b = after(b[0], a) + b_got
-    b_keep, b_send = b[0], b[1]
-    b_got = swap(b_send, place.far)
-
-    a = after(a, b_send)
-    a = a + swap(a, place.near)
-    early_out = early(place, [a, swap(a, place.core)], total)
-    b = after(b_keep, early_out[0]) + b_got
-    if place.extra:
-        b = lax.psum(b, place.extra)
-    b = b + swap(b, place.near)
+        s = lax.psum(s, place.extra)
     cols, own_rows = wide // n_dp, narrow // n_own
-    sent = late(place, early_out, [b, swap(b, place.core)], wide, own_rows, total)
+    sent = inverses(place, [s, swap(s, place.core)], wide, own_rows, total)
     got = lax.all_to_all(sent, (place.far, place.second, place.first), 0, 0)
     kept, update = placing(
         place, owner_map, got, wide, cols, layers // n_own + 1, own_rows

time: 72.3 us -> 68.2 us (0.943)
  starting transfers between devices: 16 us -> 9.33 us
  waiting for transfers between devices: 23.1 us -> 27.2 us
  Pallas kernels: 18 us -> 16.5 us
    ppermute x8 -> x4, starting transfers between devices: 9.27 us -> 4.14 us  [swap(): return lax.ppermute(value, axis, [(0, 1), (1, 0)])]
    ppermute x4, waiting for transfers between devices: 11 us -> 13.1 us  [swap_by_core(): return lax.ppermute(value, (place.second, place.core, place.first), pairs)]
    ppermute x8 -> x4, waiting for transfers between devices: 12.2 us -> 14.1 us  [swap(): return lax.ppermute(value, axis, [(0, 1), (1, 0)])]
    pallas_call x2 -> x1, Pallas kernels: 11.7 us -> 10.1 us  [inverses(): pl.pallas_call(functools.partial(inverse_kernel, place, total, rows), in_...]
    ppermute x4, starting transfers between devices: 6.68 us -> 5.19 us  [swap_by_core(): return lax.ppermute(value, (place.second, place.core, place.first), pairs)]
  transfers between devices with their start and end apart: 12 -> 8, of which waited for: 10 -> 8; matrix products, arithmetic and copies ran while one was open for 0% -> 0% of each run, Pallas kernels for 8% -> 0%
where the time goes in v6:
time: 68.2 us; the launch traced here: 68 us
  waiting for transfers between devices  27.2 us (40%)
  Pallas kernels  16.5 us (24%)
  blocking collectives  13.9 us (20%)
  starting transfers between devices  9.33 us (14%)
  between operations  0.69 us (1%)
    ppermute x4, waiting for transfers between devices, swap(): return lax.ppermute(value, axis, [(0, 1), (1, 0)])  14.1 us
    all_to_all x1, blocking collectives, on_device(): got = lax.all_to_all(sent, (place.far, place.second, place.first), 0, 0)  13.9 us
    ppermute x4, waiting for transfers between devices, swap_by_core(): return lax.ppermute(value, (place.second, place.core, place.first), pairs)  13.1 us
    pallas_call x1, Pallas kernels, inverses(): pl.pallas_call(functools.partial(inverse_kernel, place, total, rows), in_...  10.1 us
    ppermute x4, starting transfers between devices, swap_by_core(): return lax.ppermute(value, (place.second, place.core, place.first), pairs)  5.19 us
    pallas_call x1, Pallas kernels, gram(): pl.pallas_call(functools.partial(gram_kernel, place), in_specs=[HBM, HBM]...  5.12 us
    ppermute x4, starting transfers between devices, swap(): return lax.ppermute(value, axis, [(0, 1), (1, 0)])  4.14 us
  transfers between devices with their start and end apart: 8, of which 8 were waited for; matrix products, arithmetic and copies ran while one was open for 0% of the time, Pallas kernels for 0%

profile of v6, /device:TPU:0, one launch (start us, length us, event | category | flops | bytes accessed | tf_op | source)
XLA Modules:
  0.0 68.0 jit_solution(16106862805043535920)
XLA Ops:
  0.6 5.1 %gram.1 = (f32[4,2,296,128]{3,2,1,0:T(8,128)S(1)}, f32[4,2,296,128]{3,2,1,0:T(8,128)S(1)}) custom-call(bf16[8,768,256]{2,1,0:T(8,128)(2,1)} %wide_hbm.1, bf16[8,768,128]{2,1,0:T(8,128)(2,1)} %narrow_hbm.1), custom_call_target="tpu_custom_call" | custom-call | flops 1409286144 | bytes 4718592 | tf_op jit(solution)/shard_map/gram/pallas_call | solution.py:164
  5.8 0.5 collective-permute-start
  6.3 2.5 %collective-permute-done = f32[4,2,296,128]{3,2,1,0:T(8,128)S(1)} collective-permute-done((f32[4,2,296,128]{3,2,1,0:T(8,128)S(1)}, f32[4,2,296,128]{3,2,1,0:T(8,128)S(1)}, u32[]{:S(2)}, u32[]{:S(2)}) %collective-permute-start) | collective-permute-done | bytes 1212448 | tf_op jit(solution)/shard_map/ppermute | solution.py:483
  8.8 0.2 add.15
  9.0 2.9 %collective-permute-start.1 = (f32[2,296,128]{2,1,0:T(8,128)S(1)}, f32[2,296,128]{2,1,0:T(8,128)S(1)}, u32[]{:S(2)}, u32[]{:S(2)}) collective-permute-start(f32[2,296,128]{2,1,0:T(8,128)S(1)} %get-tuple-element.10), channel_id=1, source_target_pairs={{0,1},{1,0},{2,6},{3,7},{4,5},{5,4},{6,2},{7,3},{8,9},{9,8},{10,14... | collective-permute-start | bytes 909320 | tf_op jit(solution)/shard_map/ppermute | solution.py:494
  11.9 0.1 collective-permute-start.2
  12.0 4.7 %collective-permute-done.1 = f32[2,296,128]{2,1,0:T(8,128)S(1)} collective-permute-done((f32[2,296,128]{2,1,0:T(8,128)S(1)}, f32[2,296,128]{2,1,0:T(8,128)S(1)}, u32[]{:S(2)}, u32[]{:S(2)}) %collective-permute-start.1) | collective-permute-done | bytes 303136 | tf_op jit(solution)/shard_map/ppermute | solution.py:494
  16.7 3.2 %collective-permute-done.2 = f32[2,296,128]{2,1,0:T(8,128)S(1)} collective-permute-done((f32[2,296,128]{2,1,0:T(8,128)S(1)}, f32[2,296,128]{2,1,0:T(8,128)S(1)}, u32[]{:S(2)}, u32[]{:S(2)}) %collective-permute-start.2) | collective-permute-done | bytes 303136 | tf_op jit(solution)/shard_map/ppermute | solution.py:494
  20.0 0.1 slice_add_fusion
  20.1 2.1 %collective-permute-start.3 = (f32[296,128]{1,0:T(8,128)S(1)}, f32[296,128]{1,0:T(8,128)S(1)}, u32[]{:S(2)}, u32[]{:S(2)}) collective-permute-start(f32[296,128]{1,0:T(8,128)S(1)} %get-tuple-element.12), channel_id=1, source_target_pairs={{0,4},{1,5},{2,3},{3,2},{4,0},{5,1},{6,7},{7,6},{8,12},{9,13},{10,... | collective-permute-start | bytes 454664 | tf_op jit(solution)/shard_map/ppermute | solution.py:494
  22.2 0.1 collective-permute-start.4
  22.3 3.1 %collective-permute-done.3 = f32[296,128]{1,0:T(8,128)S(1)} collective-permute-done((f32[296,128]{1,0:T(8,128)S(1)}, f32[296,128]{1,0:T(8,128)S(1)}, u32[]{:S(2)}, u32[]{:S(2)}) %collective-permute-start.3) | collective-permute-done | bytes 151584 | tf_op jit(solution)/shard_map/ppermute | solution.py:494
  25.4 2.0 %collective-permute-done.4 = f32[296,128]{1,0:T(8,128)S(1)} collective-permute-done((f32[296,128]{1,0:T(8,128)S(1)}, f32[296,128]{1,0:T(8,128)S(1)}, u32[]{:S(2)}, u32[]{:S(2)}) %collective-permute-start.4) | collective-permute-done | bytes 151584 | tf_op jit(solution)/shard_map/ppermute | solution.py:494
  27.4 2.8 %collective-permute-start.5 = (f32[296,128]{1,0:T(8,128)S(1)}, f32[296,128]{1,0:T(8,128)S(1)}, u32[]{:S(2)}, u32[]{:S(2)}) collective-permute-start(f32[296,128]{1,0:T(8,128)S(1)} %slice_bitcast_fusion.3), channel_id=1, source_target_pairs={{0,16},{16,0},{1,17},{17,1},{2,18},{18,2},{3,19},{19,3},{4,20},{20... | collective-permute-start | bytes 454664 | tf_op jit(solution)/shard_map/ppermute | solution.py:483
  30.2 5.8 %collective-permute-done.5 = f32[296,128]{1,0:T(8,128)S(1)} collective-permute-done((f32[296,128]{1,0:T(8,128)S(1)}, f32[296,128]{1,0:T(8,128)S(1)}, u32[]{:S(2)}, u32[]{:S(2)}) %collective-permute-start.5) | collective-permute-done | bytes 151584 | tf_op jit(solution)/shard_map/ppermute | solution.py:483
  36.0 0.8 %collective-permute-start.6 = (f32[296,128]{1,0:T(8,128)S(1)}, f32[296,128]{1,0:T(8,128)S(1)}, u32[]{:S(2)}, u32[]{:S(2)}) collective-permute-start(f32[296,128]{1,0:T(8,128)S(1)} %fusion.1), channel_id=1, source_target_pairs={{0,8},{8,0},{1,9},{9,1},{2,10},{10,2},{3,11},{11,3},{4,12},{12,4},... | collective-permute-start | bytes 454664 | tf_op jit(solution)/shard_map/ppermute | solution.py:483
  36.8 4.5 %collective-permute-done.6 = f32[296,128]{1,0:T(8,128)S(1)} collective-permute-done((f32[296,128]{1,0:T(8,128)S(1)}, f32[296,128]{1,0:T(8,128)S(1)}, u32[]{:S(2)}, u32[]{:S(2)}) %collective-permute-start.6) | collective-permute-done | bytes 151584 | tf_op jit(solution)/shard_map/ppermute | solution.py:483
  41.3 0.0 copy-start
  41.3 0.1 collective-permute-start.7
  41.4 1.4 %collective-permute-done.7.other = f32[296,128]{1,0:T(8,128)S(1)} collective-permute-done((f32[296,128]{1,0:T(8,128)S(1)}, f32[296,128]{1,0:T(8,128)S(1)}, u32[]{:S(2)}, u32[]{:S(2)}) %collective-permute-start.7) | collective-permute-done | bytes 151584 | tf_op jit(solution)/shard_map/ppermute | solution.py:483
  42.7 10.1 %inverses.1 = f32[8,40,128]{2,1,0:T(8,128)S(1)} custom-call(f32[296,128]{1,0:T(8,128)S(1)} %add.19.mine, f32[296,128]{1,0:T(8,128)S(1)} %collective-permute-done.7.other), custom_call_target="tpu_custom_call" | custom-call | flops 1073741824 | bytes 1048576 | tf_op jit(solution)/shard_map/inverses/pallas_call | solution.py:415
  52.9 13.9 %all_to_all.5.got_ref = f32[8,40,128]{2,1,0:T(8,128)S(1)} all-to-all(f32[8,40,128]{2,1,0:T(8,128)S(1)} %inverses.1), channel_id=1, replica_groups=mesh['dp0'=2,'dp1'=2,'dp2'=2,'dp3'=2,'own0'=2] {'dp0','dp2','own0'}, dimensions={0} | all-to-all | bytes 327680 | tf_op jit(solution)/shard_map/all_to_all | solution.py:517
  66.8 0.0 copy-done
  66.8 1.3 %placing.1 = (f32[5,16,256]{2,1,0:T(8,128)}, f32[8,16,64]{2,1,0:T(8,128)}) custom-call(s32[8]{0:T(128)S(1)} %copy-done, f32[8,40,128]{2,1,0:T(8,128)S(1)} %all_to_all.5.got_ref), custom_call_target="tpu_custom_call" | custom-call | tf_op jit(solution)/shard_map/placing/pallas_call | solution.py:469
  (6 shorter events, 0.2 us)
Async XLA Ops:
  5.8 3.0 %collective-permute-start = (f32[4,2,296,128]{3,2,1,0:T(8,128)S(1)}, f32[4,2,296,128]{3,2,1,0:T(8,128)S(1)}, u32[]{:S(2)}, u32[]{:S(2)}) collective-permute-start(f32[4,2,296,128]{3,2,1,0:T(8,128)S(1)} %get-tuple-element.7), channel_id=1, source_target_pairs={{0,2},{2,0},{1,3},{3,1},{4,6},{6,4},{5,7},{7,5},{8,10},{10,8},{9,1... | collective-permute-start | bytes 3637256 | tf_op jit(solution)/shard_map/ppermute | solution.py:483
  9.0 7.7 %collective-permute-start.1 = (f32[2,296,128]{2,1,0:T(8,128)S(1)}, f32[2,296,128]{2,1,0:T(8,128)S(1)}, u32[]{:S(2)}, u32[]{:S(2)}) collective-permute-start(f32[2,296,128]{2,1,0:T(8,128)S(1)} %get-tuple-element.10), channel_id=1, source_target_pairs={{0,1},{1,0},{2,6},{3,7},{4,5},{5,4},{6,2},{7,3},{8,9},{9,8},{10,14... | collective-permute-start | bytes 909320 | tf_op jit(solution)/shard_map/ppermute | solution.py:494
  11.9 8.0 %collective-permute-start.2 = (f32[2,296,128]{2,1,0:T(8,128)S(1)}, f32[2,296,128]{2,1,0:T(8,128)S(1)}, u32[]{:S(2)}, u32[]{:S(2)}) collective-permute-start(f32[2,296,128]{2,1,0:T(8,128)S(1)} %get-tuple-element.11), channel_id=1, source_target_pairs={{0,1},{1,0},{2,6},{3,7},{4,5},{5,4},{6,2},{7,3},{8,9},{9,8},{10,14... | collective-permute-start | bytes 909320 | tf_op jit(solution)/shard_map/ppermute | solution.py:494
  20.1 5.3 %collective-permute-start.3 = (f32[296,128]{1,0:T(8,128)S(1)}, f32[296,128]{1,0:T(8,128)S(1)}, u32[]{:S(2)}, u32[]{:S(2)}) collective-permute-start(f32[296,128]{1,0:T(8,128)S(1)} %get-tuple-element.12), channel_id=1, source_target_pairs={{0,4},{1,5},{2,3},{3,2},{4,0},{5,1},{6,7},{7,6},{8,12},{9,13},{10,... | collective-permute-start | bytes 454664 | tf_op jit(solution)/shard_map/ppermute | solution.py:494
  22.2 5.2 %collective-permute-start.4 = (f32[296,128]{1,0:T(8,128)S(1)}, f32[296,128]{1,0:T(8,128)S(1)}, u32[]{:S(2)}, u32[]{:S(2)}) collective-permute-start(f32[296,128]{1,0:T(8,128)S(1)} %get-tuple-element.13), channel_id=1, source_target_pairs={{0,4},{1,5},{2,3},{3,2},{4,0},{5,1},{6,7},{7,6},{8,12},{9,13},{10,... | collective-permute-start | bytes 454664 | tf_op jit(solution)/shard_map/ppermute | solution.py:494
  27.4 8.5 %collective-permute-start.5 = (f32[296,128]{1,0:T(8,128)S(1)}, f32[296,128]{1,0:T(8,128)S(1)}, u32[]{:S(2)}, u32[]{:S(2)}) collective-permute-start(f32[296,128]{1,0:T(8,128)S(1)} %slice_bitcast_fusion.3), channel_id=1, source_target_pairs={{0,16},{16,0},{1,17},{17,1},{2,18},{18,2},{3,19},{19,3},{4,20},{20... | collective-permute-start | bytes 454664 | tf_op jit(solution)/shard_map/ppermute | solution.py:483
  36.0 5.3 %collective-permute-start.6 = (f32[296,128]{1,0:T(8,128)S(1)}, f32[296,128]{1,0:T(8,128)S(1)}, u32[]{:S(2)}, u32[]{:S(2)}) collective-permute-start(f32[296,128]{1,0:T(8,128)S(1)} %fusion.1), channel_id=1, source_target_pairs={{0,8},{8,0},{1,9},{9,1},{2,10},{10,2},{3,11},{11,3},{4,12},{12,4},... | collective-permute-start | bytes 454664 | tf_op jit(solution)/shard_map/ppermute | solution.py:483
  41.3 25.5 %copy-start = (s32[8]{0:T(128)S(1)}, s32[8]{0:T(128)}, u32[]{:S(2)}) copy-start(s32[8]{0:T(128)} %owner_map.1) | copy-start | bytes 100
  41.3 1.4 %collective-permute-start.7 = (f32[296,128]{1,0:T(8,128)S(1)}, f32[296,128]{1,0:T(8,128)S(1)}, u32[]{:S(2)}, u32[]{:S(2)}) collective-permute-start(f32[296,128]{1,0:T(8,128)S(1)} %add.19.mine), channel_id=1, source_target_pairs={{0,2},{2,0},{1,3},{3,1},{4,6},{6,4},{5,7},{7,5},{8,10},{10,8},{9,1... | collective-permute-start | bytes 454664 | tf_op jit(solution)/shard_map/ppermute | solution.py:483

commit v7 on v6

--- a/solution.py
+++ b/solution.py
@@ -39,10 +39,7 @@
         return value
 
     def layer(self):
-        return self.index((self.far, self.second, self.first))
-
-    def quarter(self):
-        return self.index((self.core, self.near))
+        return self.index((self.near, self.second, self.first))
 
 
 def transposed_dot(a, b, precision=None):
@@ -51,20 +48,20 @@
     )
 
 
-def read_layers(place, sources, buffers, sems):
+AHEAD = 3
+
+
+def layer_copies(place, sources, buffers, sems):
     layer = place.layer()
-    copies = []
-    for i in range(buffers[0].shape[0]):
-        group = [
+    return [
+        [
             pltpu.make_async_copy(
                 source.at[jnp.bitwise_xor(layer, i)], buffer.at[i], sems.at[i, s]
             )
             for s, (source, buffer) in enumerate(zip(sources, buffers))
         ]
-        for copy in group:
-            copy.start()
-        copies.append(group)
-    return copies
+        for i in range(buffers[0].shape[0])
+    ]
 
 
 def write_halves(place, i, first_row, flat, keep_ref, send_ref):
@@ -132,58 +129,89 @@
 
 
 EARLY_ROWS = 144
-LATE_ROWS = 448
-
-
-def gram_kernel(place, wide_hbm, narrow_hbm, *refs):
-    keep, send, wides, narrows, a_flat, b_flat, sems = refs
-    copies = read_layers(place, (wide_hbm, narrow_hbm), (wides, narrows), sems)
+LATE_ROWS = 192
+
+
+def squares_kernel(place, wide_hbm, narrow_hbm, keep, send, wides, narrows, a_flat, b_flat, sems):
+    copies = layer_copies(place, (wide_hbm, narrow_hbm), (wides, narrows), sems)
+    for group in copies[:AHEAD]:
+        for copy in group:
+            copy.start()
     n = LANES
     for i, group in enumerate(copies):
         for copy in group:
             copy.wait()
+        if i + AHEAD < len(copies):
+            for copy in copies[i + AHEAD]:
+                copy.start()
         wide = wides[i]
         narrow = narrows[i]
         wcov = transposed_dot(wide, wide)
         ncov = transposed_dot(narrow, narrow)
-        mixed = transposed_dot(narrow, wide)
         last = wcov[n:, n:]
         a_flat[i, :n] = pack_pair(wcov[:n, :n], ncov)
         a_flat[i, n:] = diagonals((ncov, last), EARLY_ROWS - n)
         write_halves(place, i, 0, a_flat, keep, send)
         b_flat[i, :n] = wcov[:n, n:]
-        b_flat[i, n : n + n // 2] = fold(last)
-        b_flat[i, n + n // 2 : 2 * n + n // 2] = mixed[:, :n]
-        b_flat[i, 2 * n + n // 2 :] = mixed[:, n:]
+        b_flat[i, n:] = fold(last)
         write_halves(place, i, EARLY_ROWS // 2, b_flat, keep, send)
 
 
-def gram(place, wide_rows, narrow_rows):
+def mixed_kernel(place, wides, narrows, keep, send, flat):
+    n = LANES
+    for i in range(wides.shape[0]):
+        mixed = transposed_dot(narrows[i], wides[i])
+        flat[i, :n] = mixed[:, :n]
+        flat[i, n:] = mixed[:, n:]
+        write_halves(place, i, 0, flat, keep, send)
+
+
+def gram_cost(wide_rows, columns):
+    return pl.CostEstimate(
+        flops=2 * wide_rows.size * columns, bytes_accessed=2 * wide_rows.size, transcendentals=0
+    )
+
+
+def squares(place, wide_rows, narrow_rows):
     layers = wide_rows.shape[0]
     half = jax.ShapeDtypeStruct((4, 2, (EARLY_ROWS + LATE_ROWS) // 2, LANES), jnp.float32)
     return pl.pallas_call(
-        functools.partial(gram_kernel, place),
+        functools.partial(squares_kernel, place),
         in_specs=[HBM, HBM],
-        out_specs=[VMEM] * 2,
-        out_shape=[half, half],
+        out_specs=[VMEM] * 4,
+        out_shape=[
+            half,
+            half,
+            jax.ShapeDtypeStruct(wide_rows.shape, wide_rows.dtype),
+            jax.ShapeDtypeStruct(narrow_rows.shape, narrow_rows.dtype),
+        ],
         scratch_shapes=[
-            pltpu.VMEM(wide_rows.shape, wide_rows.dtype),
-            pltpu.VMEM(narrow_rows.shape, narrow_rows.dtype),
             pltpu.VMEM((layers, EARLY_ROWS, LANES), jnp.float32),
             pltpu.VMEM((layers, LATE_ROWS, LANES), jnp.float32),
             pltpu.SemaphoreType.DMA((layers, 2)),
         ],
-        cost_estimate=pl.CostEstimate(
-            flops=2 * wide_rows.size * 448,
-            bytes_accessed=3 * wide_rows.size,
-            transcendentals=0,
-        ),
+        cost_estimate=gram_cost(wide_rows, 320),
         compiler_params=PARAMS,
-        name="gram",
+        name="squares",
     )(
         pltpu.with_memory_space_constraint(wide_rows, pltpu.HBM),
         pltpu.with_memory_space_constraint(narrow_rows, pltpu.HBM),
     )
+
+
+def mixed_sums(place, wides, narrows):
+    layers, _, narrow = narrows.shape
+    half = jax.ShapeDtypeStruct((4, 2, narrow, LANES), jnp.float32)
+    return pl.pallas_call(
+        functools.partial(mixed_kernel, place),
+        in_specs=[VMEM, VMEM],
+        out_specs=[VMEM, VMEM],
+        out_shape=[half, half],
+        scratch_shapes=[pltpu.VMEM((layers, 2 * narrow, LANES), jnp.float32)],
+        cost_estimate=gram_cost(wides, 128),
+        compiler_params=PARAMS,
+        name="mixed",
+    )(wides, narrows)
 
 
 def lane_gather(x, index):
@@ -278,13 +306,12 @@
     return jnp.concatenate(result, axis=1) if tiles > 1 else result[0]
 
 
-def place_pieces(place, pieces, a_flat, b_flat):
+def place_halves(place, pieces, first_row, flat):
     core = lax.axis_index(place.core)
-    a_rows, b_rows = a_flat.shape[0] // 2, b_flat.shape[0] // 2
+    rows = flat.shape[0] // 2
     for r, piece in enumerate(pieces):
-        half = jnp.bitwise_xor(core, r)
-        a_flat[pl.ds(pl.multiple_of(half * a_rows, PANEL), a_rows), :] = piece[:a_rows]
-        b_flat[pl.ds(pl.multiple_of(half * b_rows, PANEL), b_rows), :] = piece[a_rows:]
+        start = pl.multiple_of(jnp.bitwise_xor(core, r) * rows, PANEL)
+        flat[pl.ds(start, rows), :] = piece[first_row : first_row + rows]
 
 
 def sweep_cost():
@@ -348,43 +375,87 @@
     )
 
 
-def inverse_kernel(place, total, rows, mine, other, out_ref, *refs):
-    a_flat, b_flat, winv, inner_ref = refs[:4]
-    first_work, narrow_work, last_work = refs[4:7], refs[7:10], refs[10:]
-    place_pieces(place, (mine, other), a_flat, b_flat)
+def early_kernel(
+    place, total, mine, other, w11_ref, ninv_ref, corner_ref, last_ref, a_flat, b_flat, *works
+):
+    place_halves(place, (mine, other), 0, a_flat)
+    place_halves(place, (mine, other), a_flat.shape[0] // 2, b_flat)
     n = LANES
-    h = n // 2
     slab = a_flat[n : n + PANEL]
     first, square = unpack_pair(a_flat[:n], jnp.broadcast_to(slab[:1], (n, n)))
-    load_damped(first_work[0], first / total)
-    load_damped(narrow_work[0], square / total)
-    w11, ninv = sweep_all((first_work, narrow_work))
-    corner = b_flat[:n] / total
+    load_damped(works[0], first / total)
+    load_damped(works[3], square / total)
+    corner_ref[...] = b_flat[:n] / total
+    last_ref[...] = unfold(b_flat[n:], jnp.broadcast_to(slab[1:2], (n, n))) / total
+    w11_ref[...], ninv_ref[...] = sweep_all((works[:3], works[3:]))
+
+
+def early(place, pieces, total):
+    n = LANES
+    return pl.pallas_call(
+        functools.partial(early_kernel, place, total),
+        in_specs=[VMEM] * 2,
+        out_specs=[VMEM] * 4,
+        out_shape=[jax.ShapeDtypeStruct((n, n), jnp.float32)] * 4,
+        scratch_shapes=[
+            pltpu.VMEM((EARLY_ROWS, n), jnp.float32),
+            pltpu.VMEM((LATE_ROWS, n), jnp.float32),
+            *work_shapes(n),
+            *work_shapes(n),
+        ],
+        cost_estimate=sweep_cost(),
+        compiler_params=PARAMS,
+        name="early",
+    )(*pieces)
+
+
+def late_kernel(w11_ref, corner_ref, last_ref, winv, *work):
+    n = LANES
+    w11 = w11_ref[...]
+    corner = corner_ref[...]
     solved = dot(w11, corner)
-    schur = transposed_dot(corner, solved, HIGHEST)
-    last = unfold(b_flat[n : n + h], jnp.broadcast_to(slab[1:2], (n, n)))
-    load_damped(last_work[0], last / total - schur)
-    for c in range(2):
-        start = n + h + c * n
-        inner_ref[c * n : (c + 1) * n] = transposed_dot(
-            b_flat[start : start + n] / total, ninv, HIGHEST
-        )
-    winv[:n, :n] = w11
-    (sinv,) = sweep_all((last_work,))
+    load_damped(work[0], last_ref[...] - transposed_dot(corner, solved, HIGHEST))
+    (sinv,) = sweep_all((work,))
     cross = dot(solved, sinv)
-    winv[:n, :n] += dot(cross, solved, last=True)
+    winv[:n, :n] = w11 + dot(cross, solved, last=True)
     winv[:n, n:] = -cross
     winv[n:, :n] = -cross.T
     winv[n:, n:] = sinv
-    inner = inner_ref[...]
+
+
+def late(w11, corner, last):
+    n = LANES
+    return pl.pallas_call(
+        late_kernel,
+        in_specs=[VMEM] * 3,
+        out_specs=VMEM,
+        out_shape=jax.ShapeDtypeStruct((2 * n, 2 * n), jnp.float32),
+        scratch_shapes=work_shapes(n),
+        cost_estimate=sweep_cost(),
+        compiler_params=PARAMS,
+        name="late",
+    )(w11, corner, last)
+
+
+def product_kernel(place, total, rows, winv, ninv_ref, mine, other, out_ref, flat):
+    place_halves(place, (mine, other), 0, flat)
+    ninv = ninv_ref[...]
+    n = LANES
+    inner = jnp.concatenate(
+        [
+            transposed_dot(flat[c * n : (c + 1) * n] / total, ninv, HIGHEST)
+            for c in range(2)
+        ],
+        axis=0,
+    )
     wide = winv.shape[1]
     cols = wide // 2 ** len(place.dp)
-    far, second = lax.axis_index(place.far), lax.axis_index(place.second)
-    far_stride = 2 ** (len(place.dp) - 1)
-    base = place.index(place.dp) - far * far_stride - second * 2
+    near, second = lax.axis_index(place.near), lax.axis_index(place.second)
+    near_stride = 2 ** (len(place.dp) - 2)
+    base = place.index(place.dp) - near * near_stride - second * 2
     _, lane = iotas((PANEL, LANES))
     for j in range(4):
-        index = base + (j // 2) * far_stride + (j % 2) * 2
+        index = base + (j // 2) * near_stride + (j % 2) * 2
         picked = aligned_rows(winv, index, cols)
         update = lax.dot_general(
             picked,
@@ -408,28 +479,19 @@
                 out_ref[block, 2 * cols :] = update
 
 
-def inverses(place, pieces, wide, rows, total):
+def products(place, winv, ninv, pieces, rows, total):
+    wide, narrow = winv.shape[0], ninv.shape[0]
     cols = wide // 2 ** len(place.dp)
     height = 2 * cols + (PANEL if packs(cols, rows) else cols)
-    n = LANES
     return pl.pallas_call(
-        functools.partial(inverse_kernel, place, total, rows),
-        in_specs=[VMEM] * 2,
+        functools.partial(product_kernel, place, total, rows),
+        in_specs=[VMEM] * 4,
         out_specs=VMEM,
         out_shape=jax.ShapeDtypeStruct((8, height, LANES), jnp.float32),
-        scratch_shapes=[
-            pltpu.VMEM((EARLY_ROWS, n), jnp.float32),
-            pltpu.VMEM((LATE_ROWS, n), jnp.float32),
-            pltpu.VMEM((wide, wide), jnp.float32),
-            pltpu.VMEM((wide, n), jnp.float32),
-            *work_shapes(n),
-            *work_shapes(n),
-            *work_shapes(n),
-        ],
-        cost_estimate=sweep_cost(),
+        scratch_shapes=[pltpu.VMEM((2 * narrow, LANES), jnp.float32)],
         compiler_params=PARAMS,
-        name="inverses",
-    )(*pieces)
+        name="products",
+    )(winv, ninv, *pieces)
 
 
 def placing_kernel(place, owner_map, got_ref, kept_ref, update_ref):
@@ -494,8 +556,8 @@
     return lax.ppermute(value, (place.second, place.core, place.first), pairs)
 
 
-def in_two(value, exchange):
-    return jnp.stack([exchange(value[0]), exchange(value[1])])
+def after(value, *others):
+    return lax.optimization_barrier((value,) + others)[0]
 
 
 def on_device(place, wide_rows, narrow_rows, owner_map):
@@ -504,17 +566,46 @@
     n_dp, n_own = 2 ** len(place.dp), 2 ** len(place.own)
     total = float(rows * n_dp * n_own)
 
-    s_keep, s_send = gram(place, wide_rows, narrow_rows)
-    s = s_keep + swap(s_send, place.core)
-    s = s[:2] + in_two(s[2:], lambda v: swap_by_core(v, place, 0))
-    s = s[0] + in_two(s[1], lambda v: swap_by_core(v, place, 1))
-    s = s[0] + swap(s[1], place.far)
-    s = s + swap(s, place.near)
+    s_keep, s_send, wides, narrows = squares(place, wide_rows, narrow_rows)
+    s_got = swap(s_send, place.core)
+    m_keep, m_send = mixed_sums(place, after(wides, s_send), narrows)
+    s_keep, m_send = lax.optimization_barrier((s_keep, m_send))
+
+    s = s_keep + s_got
+    s_got = swap_by_core(s[2:], place, 0)
+    m_got = swap(after(m_send, s), place.core)
+
+    s = s[:2] + s_got
+    s_got = swap_by_core(s[1], place, 1)
+    m = after(m_keep, s) + m_got
+    m_got = swap_by_core(m[2:], place, 0)
+
+    s = s[0] + s_got
+    s_got = swap(s[1], place.near)
+    m = after(m[:2], s) + m_got
+    m_got = swap_by_core(m[1], place, 1)
+
+    s = s[0] + s_got
     if place.extra:
         s = lax.psum(s, place.extra)
+    s_got = swap(s, place.far)
+    m = after(m[0], s) + m_got
+    m_got = swap(m[1], place.near)
+
+    s = s + s_got
+    m = after(m[0], s) + m_got
+    if place.extra:
+        m = lax.psum(m, place.extra)
+    s_got = swap(after(s, m), place.core)
+    m_got = swap(m, place.far)
+
+    w11, ninv, corner, last = early(place, [s, s_got], total)
+    m = after(m, w11) + m_got
+    m_got = swap(m, place.core)
+    winv = late(w11, corner, last)
     cols, own_rows = wide // n_dp, narrow // n_own
-    sent = inverses(place, [s, swap(s, place.core)], wide, own_rows, total)
-    got = lax.all_to_all(sent, (place.far, place.second, place.first), 0, 0)
+    sent = products(place, winv, ninv, [m, m_got], own_rows, total)
+    got = lax.all_to_all(sent, (place.near, place.second, place.first), 0, 0)
     kept, update = placing(
         place, owner_map, got, wide, cols, layers // n_own + 1, own_rows
     )

time: 68.2 us -> 60.3 us (0.88)
  waiting for transfers between devices: 27.2 us -> 13.9 us
  starting transfers between devices: 9.33 us -> 17.3 us
  blocking collectives: 13.9 us -> 10.3 us
  Pallas kernels: 16.5 us -> 17.4 us
    ppermute x4 -> x8, waiting for transfers between devices: 14.1 us -> 5.32 us  [swap(): return lax.ppermute(value, axis, [(0, 1), (1, 0)])]
    ppermute x4 -> x8, starting transfers between devices: 4.14 us -> 9.19 us  [swap(): return lax.ppermute(value, axis, [(0, 1), (1, 0)])]
    ppermute x4, waiting for transfers between devices: 13.1 us -> 8.6 us  [swap_by_core(): return lax.ppermute(value, (place.second, place.core, place.first), pairs)]
    all_to_all x1, blocking collectives: 13.9 us -> 10.3 us  [on_device(): got = lax.all_to_all(sent, (place.near, place.second, place.first), 0, 0)]
    ppermute x4, starting transfers between devices: 5.19 us -> 8.16 us  [swap_by_core(): return lax.ppermute(value, (place.second, place.core, place.first), pairs)]
    pallas_call x2 -> x5, Pallas kernels: 15.2 us -> 16.1 us  [the longest x1 5.14 us: early(): pl.pallas_call(functools.partial(early_kernel, place, total), in_specs=[V...]
  transfers between devices with their start and end apart: 8 -> 12, of which waited for: 8 -> 7; matrix products, arithmetic and copies ran while one was open for 0% -> 0% of each run, Pallas kernels for 0% -> 18%
where the time goes in v7:
time: 60.3 us; the launch traced here: 60.1 us
  Pallas kernels  17.4 us (29%)
  starting transfers between devices  17.3 us (29%)
  waiting for transfers between devices  13.9 us (23%)
  blocking collectives  10.3 us (17%)
  between operations  0.76 us (1%)
    all_to_all x1, blocking collectives, on_device(): got = lax.all_to_all(sent, (place.near, place.second, place.first), 0, 0)  10.3 us
    ppermute x8, starting transfers between devices, swap(): return lax.ppermute(value, axis, [(0, 1), (1, 0)])  9.19 us
    ppermute x4, waiting for transfers between devices, swap_by_core(): return lax.ppermute(value, (place.second, place.core, place.first), pairs)  8.6 us
    ppermute x4, starting transfers between devices, swap_by_core(): return lax.ppermute(value, (place.second, place.core, place.first), pairs)  8.16 us
    ppermute x8, waiting for transfers between devices, swap(): return lax.ppermute(value, axis, [(0, 1), (1, 0)])  5.32 us
    pallas_call x1, Pallas kernels, early(): pl.pallas_call(functools.partial(early_kernel, place, total), in_specs=[V...  5.14 us
    pallas_call x1, Pallas kernels, squares(): pl.pallas_call(functools.partial(squares_kernel, place), in_specs=[HBM, H...  4.91 us
    pallas_call x1, Pallas kernels, late(): pl.pallas_call(late_kernel, in_specs=[VMEM] * 3, out_specs=VMEM, out_shap...  4.46 us
  transfers between devices with their start and end apart: 12, of which 7 were waited for; matrix products, arithmetic and copies ran while one was open for 0% of the time, Pallas kernels for 18%

profile of v7, /device:TPU:0, one launch (start us, length us, event | category | flops | bytes accessed | tf_op | source)
XLA Modules:
  0.0 60.1 jit_solution(2077890166035617165)
XLA Ops:
  0.6 4.9 %squares.1 = (f32[4,2,168,128]{3,2,1,0:T(8,128)S(1)}, f32[4,2,168,128]{3,2,1,0:T(8,128)S(1)}, bf16[8,768,256]{2,1,0:T(8,128)(2,1)S(1)}, bf16[8,768,128]{2,1,0:T(8,128)(2,1)S(1)}) custom-call(bf16[8,768,256]{2,1,0:T(8,128)(2,1)} %wide_hbm.1, bf16[8,768,128]{2,1,0:T(8,128)(2,1)} %narrow_hbm.1), custom_call_target="tpu_custom_call" | custom-call | flops 1006632960 | bytes 3145728 | tf_op jit(solution)/shard_map/squares/pallas_call | solution.py:178
  5.5 0.5 collective-permute-start
  6.1 0.9 %mixed.1 = (f32[4,2,128,128]{3,2,1,0:T(8,128)S(1)}, f32[4,2,128,128]{3,2,1,0:T(8,128)S(1)}) custom-call(bf16[8,768,256]{2,1,0:T(8,128)(2,1)S(1)} %get-tuple-element.27.wides, bf16[8,768,128]{2,1,0:T(8,128)(2,1)S(1)} %get-tuple-element.28.narrows), custom_call_target="tpu_custom_call" | custom-call | flops 402653184 | bytes 3145728 | tf_op jit(solution)/shard_map/mixed/pallas_call | solution.py:205
  7.0 0.8 %collective-permute-done = f32[4,2,168,128]{3,2,1,0:T(8,128)S(1)} collective-permute-done((f32[4,2,168,128]{3,2,1,0:T(8,128)S(1)}, f32[4,2,168,128]{3,2,1,0:T(8,128)S(1)}, u32[]{:S(2)}, u32[]{:S(2)}) %collective-permute-start) | collective-permute-done | bytes 688160 | tf_op jit(solution)/shard_map/ppermute | solution.py:545
  8.0 2.9 %collective-permute-start.1 = (f32[2,2,168,128]{3,2,1,0:T(8,128)S(1)}, f32[2,2,168,128]{3,2,1,0:T(8,128)S(1)}, u32[]{:S(2)}, u32[]{:S(2)}) collective-permute-start(f32[2,2,168,128]{3,2,1,0:T(8,128)S(1)} %slice.49), channel_id=1, source_target_pairs={{0,1},{1,0},{2,6},{3,7},{4,5},{5,4},{6,2},{7,3},{8,9},{9,8},{10,14... | collective-permute-start | bytes 1032200 | tf_op jit(solution)/shard_map/ppermute | solution.py:556
  10.9 5.2 %collective-permute-done.1 = f32[2,2,168,128]{3,2,1,0:T(8,128)S(1)} collective-permute-done((f32[2,2,168,128]{3,2,1,0:T(8,128)S(1)}, f32[2,2,168,128]{3,2,1,0:T(8,128)S(1)}, u32[]{:S(2)}, u32[]{:S(2)}) %collective-permute-start.1) | collective-permute-done | bytes 344096 | tf_op jit(solution)/shard_map/ppermute | solution.py:556
  16.2 2.1 %collective-permute-start.2 = (f32[2,168,128]{2,1,0:T(8,128)S(1)}, f32[2,168,128]{2,1,0:T(8,128)S(1)}, u32[]{:S(2)}, u32[]{:S(2)}) collective-permute-start(f32[2,168,128]{2,1,0:T(8,128)S(1)} %slice_bitcast_fusion), channel_id=1, source_target_pairs={{0,4},{1,5},{2,3},{3,2},{4,0},{5,1},{6,7},{7,6},{8,12},{9,13},{10,... | collective-permute-start | bytes 516104 | tf_op jit(solution)/shard_map/ppermute | solution.py:556
  18.4 1.6 %collective-permute-start.6 = (f32[2,2,128,128]{3,2,1,0:T(8,128)S(1)}, f32[2,2,128,128]{3,2,1,0:T(8,128)S(1)}, u32[]{:S(2)}, u32[]{:S(2)}) collective-permute-start(f32[2,2,128,128]{3,2,1,0:T(8,128)S(1)} %get-tuple-element.46), channel_id=1, source_target_pairs={{0,1},{1,0},{2,6},{3,7},{4,5},{5,4},{6,2},{7,3},{8,9},{9,8},{10,14... | collective-permute-start | bytes 786440 | tf_op jit(solution)/shard_map/ppermute | solution.py:556
  19.9 3.4 %collective-permute-done.2 = f32[2,168,128]{2,1,0:T(8,128)S(1)} collective-permute-done((f32[2,168,128]{2,1,0:T(8,128)S(1)}, f32[2,168,128]{2,1,0:T(8,128)S(1)}, u32[]{:S(2)}, u32[]{:S(2)}) %collective-permute-start.2) | collective-permute-done | bytes 172064 | tf_op jit(solution)/shard_map/ppermute | solution.py:556
  23.3 2.3 %collective-permute-start.3 = (f32[168,128]{1,0:T(8,128)S(1)}, f32[168,128]{1,0:T(8,128)S(1)}, u32[]{:S(2)}, u32[]{:S(2)}) collective-permute-start(f32[168,128]{1,0:T(8,128)S(1)} %slice_bitcast_fusion.4), channel_id=1, source_target_pairs={{0,8},{8,0},{1,9},{9,1},{2,10},{10,2},{3,11},{11,3},{4,12},{12,4},... | collective-permute-start | bytes 258056 | tf_op jit(solution)/shard_map/ppermute | solution.py:545
  25.8 1.6 %collective-permute-start.7 = (f32[2,128,128]{2,1,0:T(8,128)S(1)}, f32[2,128,128]{2,1,0:T(8,128)S(1)}, u32[]{:S(2)}, u32[]{:S(2)}) collective-permute-start(f32[2,128,128]{2,1,0:T(8,128)S(1)} %get-tuple-element.48), channel_id=1, source_target_pairs={{0,4},{1,5},{2,3},{3,2},{4,0},{5,1},{6,7},{7,6},{8,12},{9,13},{10,... | collective-permute-start | bytes 393224 | tf_op jit(solution)/shard_map/ppermute | solution.py:556
  27.3 0.8 %collective-permute-done.3 = f32[168,128]{1,0:T(8,128)S(1)} collective-permute-done((f32[168,128]{1,0:T(8,128)S(1)}, f32[168,128]{1,0:T(8,128)S(1)}, u32[]{:S(2)}, u32[]{:S(2)}) %collective-permute-start.3) | collective-permute-done | bytes 86048 | tf_op jit(solution)/shard_map/ppermute | solution.py:545
  28.2 3.9 %collective-permute-start.4 = (f32[168,128]{1,0:T(8,128)S(1)}, f32[168,128]{1,0:T(8,128)S(1)}, u32[]{:S(2)}, u32[]{:S(2)}) collective-permute-start(f32[168,128]{1,0:T(8,128)S(1)} %fusion.1), channel_id=1, source_target_pairs={{0,16},{16,0},{1,17},{17,1},{2,18},{18,2},{3,19},{19,3},{4,20},{20... | collective-permute-start | bytes 258056 | tf_op jit(solution)/shard_map/ppermute | solution.py:545
  32.1 0.9 %collective-permute-start.8 = (f32[128,128]{1,0:T(8,128)S(1)}, f32[128,128]{1,0:T(8,128)S(1)}, u32[]{:S(2)}, u32[]{:S(2)}) collective-permute-start(f32[128,128]{1,0:T(8,128)S(1)} %get-tuple-element.50), channel_id=1, source_target_pairs={{0,8},{8,0},{1,9},{9,1},{2,10},{10,2},{3,11},{11,3},{4,12},{12,4},... | collective-permute-start | bytes 196616 | tf_op jit(solution)/shard_map/ppermute | solution.py:545
  33.0 2.5 %collective-permute-done.4 = f32[168,128]{1,0:T(8,128)S(1)} collective-permute-done((f32[168,128]{1,0:T(8,128)S(1)}, f32[168,128]{1,0:T(8,128)S(1)}, u32[]{:S(2)}, u32[]{:S(2)}) %collective-permute-start.4) | collective-permute-done | bytes 86048 | tf_op jit(solution)/shard_map/ppermute | solution.py:545
  35.4 1.0 %collective-permute-done.8 = f32[128,128]{1,0:T(8,128)S(1)} collective-permute-done((f32[128,128]{1,0:T(8,128)S(1)}, f32[128,128]{1,0:T(8,128)S(1)}, u32[]{:S(2)}, u32[]{:S(2)}) %collective-permute-start.8) | collective-permute-done | bytes 65568 | tf_op jit(solution)/shard_map/ppermute | solution.py:545
  36.5 1.4 %collective-permute-start.10 = (f32[128,128]{1,0:T(8,128)S(1)}, f32[128,128]{1,0:T(8,128)S(1)}, u32[]{:S(2)}, u32[]{:S(2)}) collective-permute-start(f32[128,128]{1,0:T(8,128)S(1)} %add.38), channel_id=1, source_target_pairs={{0,16},{16,0},{1,17},{17,1},{2,18},{18,2},{3,19},{19,3},{4,20},{20... | collective-permute-start | bytes 196616 | tf_op jit(solution)/shard_map/ppermute | solution.py:545
  37.9 5.1 %early.1 = (f32[128,128]{1,0:T(8,128)S(1)}, f32[128,128]{1,0:T(8,128)S(1)}, f32[128,128]{1,0:T(8,128)S(1)}, f32[128,128]{1,0:T(8,128)S(1)}) custom-call(f32[168,128]{1,0:T(8,128)S(1)} %add.34.mine, f32[168,128]{1,0:T(8,128)S(1)} %collective-permute-done.9.other), custom_call_target="tpu_custom_call" | custom-call | flops 1073741824 | bytes 1048576 | tf_op jit(solution)/shard_map/early/pallas_call | solution.py:395
  43.1 0.2 collective-permute-done.10
  43.3 0.1 collective-permute-start.11
  43.4 4.5 %late.1.winv = f32[256,256]{1,0:T(8,128)S(1)} custom-call(f32[128,128]{1,0:T(8,128)S(1)} %get-tuple-element.39.w11_ref, f32[128,128]{1,0:T(8,128)S(1)} %get-tuple-element.40.corner_ref, f32[128,128]{1,0:T(8,128)S(1)} %get-tuple-element.41.last_ref), custom_call_target="tpu_custom_call" | custom-call | flops 1073741824 | bytes 1048576 | tf_op jit(solution)/shard_map/late/pallas_call | solution.py:428
  47.9 0.7 %products.1 = f32[8,40,128]{2,1,0:T(8,128)S(1)} custom-call(f32[256,256]{1,0:T(8,128)S(1)} %late.1.winv, f32[128,128]{1,0:T(8,128)S(1)} %get-tuple-element.42.ninv_ref, f32[128,128]{1,0:T(8,128)S(1)} %add.39.mine, f32[128,128]{1,0:T(8,128)S(1)} %collective-permute-done.11.other), custom_call_target="tpu_custom_call" | custom-call | tf_op jit(solution)/shard_map/products/pallas_call | solution.py:486
  48.6 10.3 %all_to_all.5.got_ref = f32[8,40,128]{2,1,0:T(8,128)S(1)} all-to-all(f32[8,40,128]{2,1,0:T(8,128)S(1)} %products.1), channel_id=1, replica_groups=mesh['dp0'=2,'dp1'=2,'dp2'=2,'dp3'=2,'own0'=2] {'dp1','dp2','own0'}, dimensions={0} | all-to-all | bytes 327680 | tf_op jit(solution)/shard_map/all_to_all | solution.py:608
  58.8 1.3 %placing.1 = (f32[5,16,256]{2,1,0:T(8,128)}, f32[8,16,64]{2,1,0:T(8,128)}) custom-call(s32[8]{0:T(128)S(1)} %copy-done, f32[8,40,128]{2,1,0:T(8,128)S(1)} %all_to_all.5.got_ref), custom_call_target="tpu_custom_call" | custom-call | tf_op jit(solution)/shard_map/placing/pallas_call | solution.py:531
  (25 shorter events, 0.5 us)
Async XLA Ops:
  5.5 2.3 %collective-permute-start = (f32[4,2,168,128]{3,2,1,0:T(8,128)S(1)}, f32[4,2,168,128]{3,2,1,0:T(8,128)S(1)}, u32[]{:S(2)}, u32[]{:S(2)}) collective-permute-start(f32[4,2,168,128]{3,2,1,0:T(8,128)S(1)} %get-tuple-element.26), channel_id=1, source_target_pairs={{0,2},{2,0},{1,3},{3,1},{4,6},{6,4},{5,7},{7,5},{8,10},{10,8},{9,1... | collective-permute-start | bytes 2064392 | tf_op jit(solution)/shard_map/ppermute | solution.py:545
  8.0 8.1 %collective-permute-start.1 = (f32[2,2,168,128]{3,2,1,0:T(8,128)S(1)}, f32[2,2,168,128]{3,2,1,0:T(8,128)S(1)}, u32[]{:S(2)}, u32[]{:S(2)}) collective-permute-start(f32[2,2,168,128]{3,2,1,0:T(8,128)S(1)} %slice.49), channel_id=1, source_target_pairs={{0,1},{1,0},{2,6},{3,7},{4,5},{5,4},{6,2},{7,3},{8,9},{9,8},{10,14... | collective-permute-start | bytes 1032200 | tf_op jit(solution)/shard_map/ppermute | solution.py:556
  10.9 7.4 %collective-permute-start.5 = (f32[4,2,128,128]{3,2,1,0:T(8,128)S(1)}, f32[4,2,128,128]{3,2,1,0:T(8,128)S(1)}, u32[]{:S(2)}, u32[]{:S(2)}) collective-permute-start(f32[4,2,128,128]{3,2,1,0:T(8,128)S(1)} %get-tuple-element.34), channel_id=1, source_target_pairs={{0,2},{2,0},{1,3},{3,1},{4,6},{6,4},{5,7},{7,5},{8,10},{10,8},{9,1... | collective-permute-start | bytes 1572872 | tf_op jit(solution)/shard_map/ppermute | solution.py:545
  16.2 7.1 %collective-permute-start.2 = (f32[2,168,128]{2,1,0:T(8,128)S(1)}, f32[2,168,128]{2,1,0:T(8,128)S(1)}, u32[]{:S(2)}, u32[]{:S(2)}) collective-permute-start(f32[2,168,128]{2,1,0:T(8,128)S(1)} %slice_bitcast_fusion), channel_id=1, source_target_pairs={{0,4},{1,5},{2,3},{3,2},{4,0},{5,1},{6,7},{7,6},{8,12},{9,13},{10,... | collective-permute-start | bytes 516104 | tf_op jit(solution)/shard_map/ppermute | solution.py:556
  18.4 7.3 %collective-permute-start.6 = (f32[2,2,128,128]{3,2,1,0:T(8,128)S(1)}, f32[2,2,128,128]{3,2,1,0:T(8,128)S(1)}, u32[]{:S(2)}, u32[]{:S(2)}) collective-permute-start(f32[2,2,128,128]{3,2,1,0:T(8,128)S(1)} %get-tuple-element.46), channel_id=1, source_target_pairs={{0,1},{1,0},{2,6},{3,7},{4,5},{5,4},{6,2},{7,3},{8,9},{9,8},{10,14... | collective-permute-start | bytes 786440 | tf_op jit(solution)/shard_map/ppermute | solution.py:556
  23.3 4.8 %collective-permute-start.3 = (f32[168,128]{1,0:T(8,128)S(1)}, f32[168,128]{1,0:T(8,128)S(1)}, u32[]{:S(2)}, u32[]{:S(2)}) collective-permute-start(f32[168,128]{1,0:T(8,128)S(1)} %slice_bitcast_fusion.4), channel_id=1, source_target_pairs={{0,8},{8,0},{1,9},{9,1},{2,10},{10,2},{3,11},{11,3},{4,12},{12,4},... | collective-permute-start | bytes 258056 | tf_op jit(solution)/shard_map/ppermute | solution.py:545
  25.8 6.3 %collective-permute-start.7 = (f32[2,128,128]{2,1,0:T(8,128)S(1)}, f32[2,128,128]{2,1,0:T(8,128)S(1)}, u32[]{:S(2)}, u32[]{:S(2)}) collective-permute-start(f32[2,128,128]{2,1,0:T(8,128)S(1)} %get-tuple-element.48), channel_id=1, source_target_pairs={{0,4},{1,5},{2,3},{3,2},{4,0},{5,1},{6,7},{7,6},{8,12},{9,13},{10,... | collective-permute-start | bytes 393224 | tf_op jit(solution)/shard_map/ppermute | solution.py:556
  28.2 7.2 %collective-permute-start.4 = (f32[168,128]{1,0:T(8,128)S(1)}, f32[168,128]{1,0:T(8,128)S(1)}, u32[]{:S(2)}, u32[]{:S(2)}) collective-permute-start(f32[168,128]{1,0:T(8,128)S(1)} %fusion.1), channel_id=1, source_target_pairs={{0,16},{16,0},{1,17},{17,1},{2,18},{18,2},{3,19},{19,3},{4,20},{20... | collective-permute-start | bytes 258056 | tf_op jit(solution)/shard_map/ppermute | solution.py:545
  32.1 4.3 %collective-permute-start.8 = (f32[128,128]{1,0:T(8,128)S(1)}, f32[128,128]{1,0:T(8,128)S(1)}, u32[]{:S(2)}, u32[]{:S(2)}) collective-permute-start(f32[128,128]{1,0:T(8,128)S(1)} %get-tuple-element.50), channel_id=1, source_target_pairs={{0,8},{8,0},{1,9},{9,1},{2,10},{10,2},{3,11},{11,3},{4,12},{12,4},... | collective-permute-start | bytes 196616 | tf_op jit(solution)/shard_map/ppermute | solution.py:545
  36.4 1.5 %collective-permute-start.9 = (f32[168,128]{1,0:T(8,128)S(1)}, f32[168,128]{1,0:T(8,128)S(1)}, u32[]{:S(2)}, u32[]{:S(2)}) collective-permute-start(f32[168,128]{1,0:T(8,128)S(1)} %add.34.mine), channel_id=1, source_target_pairs={{0,2},{2,0},{1,3},{3,1},{4,6},{6,4},{5,7},{7,5},{8,10},{10,8},{9,1... | collective-permute-start | bytes 258056 | tf_op jit(solution)/shard_map/ppermute | solution.py:545
  36.5 6.8 %collective-permute-start.10 = (f32[128,128]{1,0:T(8,128)S(1)}, f32[128,128]{1,0:T(8,128)S(1)}, u32[]{:S(2)}, u32[]{:S(2)}) collective-permute-start(f32[128,128]{1,0:T(8,128)S(1)} %add.38), channel_id=1, source_target_pairs={{0,16},{16,0},{1,17},{17,1},{2,18},{18,2},{3,19},{19,3},{4,20},{20... | collective-permute-start | bytes 196616 | tf_op jit(solution)/shard_map/ppermute | solution.py:545
  43.0 15.8 %copy-start = (s32[8]{0:T(128)S(1)}, s32[8]{0:T(128)}, u32[]{:S(2)}) copy-start(s32[8]{0:T(128)} %owner_map.1) | copy-start | bytes 100
  43.3 4.5 %collective-permute-start.11 = (f32[128,128]{1,0:T(8,128)S(1)}, f32[128,128]{1,0:T(8,128)S(1)}, u32[]{:S(2)}, u32[]{:S(2)}) collective-permute-start(f32[128,128]{1,0:T(8,128)S(1)} %add.39.mine), channel_id=1, source_target_pairs={{0,2},{2,0},{1,3},{3,1},{4,6},{6,4},{5,7},{7,5},{8,10},{10,8},{9,1... | collective-permute-start | bytes 196616 | tf_op jit(solution)/shard_map/ppermute | solution.py:545

commit v8 on v7

--- a/solution.py
+++ b/solution.py
@@ -49,6 +49,7 @@
 
 
 AHEAD = 3
+STEPS = 2
 
 
 def layer_copies(place, sources, buffers, sems):
@@ -64,12 +65,15 @@
     ]
 
 
-def write_halves(place, i, first_row, flat, keep_ref, send_ref):
+def write_halves(place, i, first_row, flat, keep_ref, send_ref, swapped=False):
     rows = flat.shape[1] // 2
     core = lax.axis_index(place.core)
     z, y, x = i // 4, (i // 2) % 2, i % 2
-    mine = jnp.where(core == 0, x * 2 + y, y * 2 + x)
-    other = jnp.where(core == 0, y * 2 + x, x * 2 + y)
+    orders = (x * 2 + y, y * 2 + x)
+    if swapped:
+        orders = orders[::-1]
+    mine = jnp.where(core == 0, *orders)
+    other = jnp.where(core == 1, *orders)
     kept = pl.multiple_of(core * rows, PANEL)
     sent = pl.multiple_of((1 - core) * rows, PANEL)
     there = slice(first_row, first_row + rows)
@@ -138,6 +142,17 @@
         for copy in group:
             copy.start()
     n = LANES
+
+    def pack(i, wcov, ncov):
+        last = wcov[n:, n:]
+        a_flat[i, :n] = pack_pair(wcov[:n, :n], ncov)
+        a_flat[i, n:] = diagonals((ncov, last), EARLY_ROWS - n)
+        write_halves(place, i, 0, a_flat, keep, send)
+        b_flat[i, :n] = wcov[:n, n:]
+        b_flat[i, n:] = fold(last)
+        write_halves(place, i, EARLY_ROWS // 2, b_flat, keep, send)
+
+    before = None
     for i, group in enumerate(copies):
         for copy in group:
             copy.wait()
@@ -146,15 +161,11 @@
                 copy.start()
         wide = wides[i]
         narrow = narrows[i]
-        wcov = transposed_dot(wide, wide)
-        ncov = transposed_dot(narrow, narrow)
-        last = wcov[n:, n:]
-        a_flat[i, :n] = pack_pair(wcov[:n, :n], ncov)
-        a_flat[i, n:] = diagonals((ncov, last), EARLY_ROWS - n)
-        write_halves(place, i, 0, a_flat, keep, send)
-        b_flat[i, :n] = wcov[:n, n:]
-        b_flat[i, n:] = fold(last)
-        write_halves(place, i, EARLY_ROWS // 2, b_flat, keep, send)
+        sums = (transposed_dot(wide, wide), transposed_dot(narrow, narrow))
+        if before is not None:
+            pack(i - 1, *before)
+        before = sums
+    pack(len(copies) - 1, *before)
 
 
 def mixed_kernel(place, wides, narrows, keep, send, flat):
@@ -163,7 +174,7 @@
         mixed = transposed_dot(narrows[i], wides[i])
         flat[i, :n] = mixed[:, :n]
         flat[i, n:] = mixed[:, n:]
-        write_halves(place, i, 0, flat, keep, send)
+        write_halves(place, i, 0, flat, keep, send, swapped=True)
 
 
 def gram_cost(wide_rows, columns):
@@ -332,10 +343,15 @@
         right[...] = jnp.zeros(right.shape, right.dtype)
 
     def step(i, panels):
-        return tuple(sweep_panel(*work, 0, i, panel) for work, panel in zip(works, panels))
+        for j in range(STEPS):
+            panels = tuple(
+                sweep_panel(*work, 0, i * STEPS + j, panel) for work, panel in zip(works, panels)
+            )
+        return panels
 
     size = works[0][0].shape[1]
-    lax.fori_loop(0, size // PANEL, step, tuple(a[PANEL : 2 * PANEL] for a, _, _ in works))
+    trips = size // (PANEL * STEPS)
+    lax.fori_loop(0, trips, step, tuple(a[PANEL : 2 * PANEL] for a, _, _ in works))
     for work in works:
         trailing_update(*work, size)
     return [-a[PANEL : PANEL + size] for a, _, _ in works]
@@ -578,12 +594,12 @@
     s = s[:2] + s_got
     s_got = swap_by_core(s[1], place, 1)
     m = after(m_keep, s) + m_got
-    m_got = swap_by_core(m[2:], place, 0)
+    m_got = swap_by_core(m[2:], place, 1)
 
     s = s[0] + s_got
     s_got = swap(s[1], place.near)
     m = after(m[:2], s) + m_got
-    m_got = swap_by_core(m[1], place, 1)
+    m_got = swap_by_core(m[1], place, 0)
 
     s = s[0] + s_got
     if place.extra:

time: 60.3 us -> 59.8 us (level)
    ppermute x8, waiting for transfers between devices: 5.32 us -> 3.38 us  [swap(): return lax.ppermute(value, axis, [(0, 1), (1, 0)])]
    ppermute x4, starting transfers between devices: 8.16 us -> 6.83 us  [swap_by_core(): return lax.ppermute(value, (place.second, place.core, place.first), pairs)]
    ppermute x4, waiting for transfers between devices: 8.6 us -> 9.89 us  [swap_by_core(): return lax.ppermute(value, (place.second, place.core, place.first), pairs)]
    ppermute x8, starting transfers between devices: 9.19 us -> 10.4 us  [swap(): return lax.ppermute(value, axis, [(0, 1), (1, 0)])]
where the time goes in v8:
time: 59.8 us; the launch traced here: 59.6 us
  Pallas kernels  17.2 us (29%)
  starting transfers between devices  17.2 us (29%)
  waiting for transfers between devices  13.3 us (22%)
  blocking collectives  10.8 us (18%)
  between operations  0.77 us (1%)
    all_to_all x1, blocking collectives, on_device(): got = lax.all_to_all(sent, (place.near, place.second, place.first), 0, 0)  10.8 us
    ppermute x8, starting transfers between devices, swap(): return lax.ppermute(value, axis, [(0, 1), (1, 0)])  10.4 us
    ppermute x4, waiting for transfers between devices, swap_by_core(): return lax.ppermute(value, (place.second, place.core, place.first), pairs)  9.89 us
    ppermute x4, starting transfers between devices, swap_by_core(): return lax.ppermute(value, (place.second, place.core, place.first), pairs)  6.83 us
    pallas_call x1, Pallas kernels, early(): pl.pallas_call(functools.partial(early_kernel, place, total), in_specs=[V...  5.29 us
    pallas_call x1, Pallas kernels, late(): pl.pallas_call(late_kernel, in_specs=[VMEM] * 3, out_specs=VMEM, out_shap...  4.59 us
    pallas_call x1, Pallas kernels, squares(): pl.pallas_call(functools.partial(squares_kernel, place), in_specs=[HBM, H...  4.39 us
    ppermute x8, waiting for transfers between devices, swap(): return lax.ppermute(value, axis, [(0, 1), (1, 0)])  3.38 us
  transfers between devices with their start and end apart: 12, of which 7 were waited for; matrix products, arithmetic and copies ran while one was open for 0% of the time, Pallas kernels for 18%

profile of v8, /device:TPU:0, one launch (start us, length us, event | category | flops | bytes accessed | tf_op | source)
XLA Modules:
  0.0 59.6 jit_solution(8097554071593528165)
XLA Ops:
  0.6 4.4 %squares.1 = (f32[4,2,168,128]{3,2,1,0:T(8,128)S(1)}, f32[4,2,168,128]{3,2,1,0:T(8,128)S(1)}, bf16[8,768,256]{2,1,0:T(8,128)(2,1)S(1)}, bf16[8,768,128]{2,1,0:T(8,128)(2,1)S(1)}) custom-call(bf16[8,768,256]{2,1,0:T(8,128)(2,1)} %wide_hbm.1, bf16[8,768,128]{2,1,0:T(8,128)(2,1)} %narrow_hbm.1), custom_call_target="tpu_custom_call" | custom-call | flops 1006632960 | bytes 3145728 | tf_op jit(solution)/shard_map/squares/pallas_call | solution.py:189
  5.0 0.5 collective-permute-start
  5.5 0.9 %mixed.1 = (f32[4,2,128,128]{3,2,1,0:T(8,128)S(1)}, f32[4,2,128,128]{3,2,1,0:T(8,128)S(1)}) custom-call(bf16[8,768,256]{2,1,0:T(8,128)(2,1)S(1)} %get-tuple-element.27.wides, bf16[8,768,128]{2,1,0:T(8,128)(2,1)S(1)} %get-tuple-element.28.narrows), custom_call_target="tpu_custom_call" | custom-call | flops 402653184 | bytes 3145728 | tf_op jit(solution)/shard_map/mixed/pallas_call | solution.py:216
  6.5 0.8 %collective-permute-done = f32[4,2,168,128]{3,2,1,0:T(8,128)S(1)} collective-permute-done((f32[4,2,168,128]{3,2,1,0:T(8,128)S(1)}, f32[4,2,168,128]{3,2,1,0:T(8,128)S(1)}, u32[]{:S(2)}, u32[]{:S(2)}) %collective-permute-start) | collective-permute-done | bytes 688160 | tf_op jit(solution)/shard_map/ppermute | solution.py:561
  7.4 2.9 %collective-permute-start.1 = (f32[2,2,168,128]{3,2,1,0:T(8,128)S(1)}, f32[2,2,168,128]{3,2,1,0:T(8,128)S(1)}, u32[]{:S(2)}, u32[]{:S(2)}) collective-permute-start(f32[2,2,168,128]{3,2,1,0:T(8,128)S(1)} %slice.49), channel_id=1, source_target_pairs={{0,1},{1,0},{2,6},{3,7},{4,5},{5,4},{6,2},{7,3},{8,9},{9,8},{10,14... | collective-permute-start | bytes 1032200 | tf_op jit(solution)/shard_map/ppermute | solution.py:572
  10.4 5.2 %collective-permute-done.1 = f32[2,2,168,128]{3,2,1,0:T(8,128)S(1)} collective-permute-done((f32[2,2,168,128]{3,2,1,0:T(8,128)S(1)}, f32[2,2,168,128]{3,2,1,0:T(8,128)S(1)}, u32[]{:S(2)}, u32[]{:S(2)}) %collective-permute-start.1) | collective-permute-done | bytes 344096 | tf_op jit(solution)/shard_map/ppermute | solution.py:572
  15.6 2.1 %collective-permute-start.2 = (f32[2,168,128]{2,1,0:T(8,128)S(1)}, f32[2,168,128]{2,1,0:T(8,128)S(1)}, u32[]{:S(2)}, u32[]{:S(2)}) collective-permute-start(f32[2,168,128]{2,1,0:T(8,128)S(1)} %slice_bitcast_fusion), channel_id=1, source_target_pairs={{0,4},{1,5},{2,3},{3,2},{4,0},{5,1},{6,7},{7,6},{8,12},{9,13},{10,... | collective-permute-start | bytes 516104 | tf_op jit(solution)/shard_map/ppermute | solution.py:572
  17.9 0.1 collective-permute-start.6
  18.0 3.2 %collective-permute-done.2 = f32[2,168,128]{2,1,0:T(8,128)S(1)} collective-permute-done((f32[2,168,128]{2,1,0:T(8,128)S(1)}, f32[2,168,128]{2,1,0:T(8,128)S(1)}, u32[]{:S(2)}, u32[]{:S(2)}) %collective-permute-start.2) | collective-permute-done | bytes 172064 | tf_op jit(solution)/shard_map/ppermute | solution.py:572
  21.2 2.1 %collective-permute-start.3 = (f32[168,128]{1,0:T(8,128)S(1)}, f32[168,128]{1,0:T(8,128)S(1)}, u32[]{:S(2)}, u32[]{:S(2)}) collective-permute-start(f32[168,128]{1,0:T(8,128)S(1)} %slice_bitcast_fusion.4), channel_id=1, source_target_pairs={{0,8},{8,0},{1,9},{9,1},{2,10},{10,2},{3,11},{11,3},{4,12},{12,4},... | collective-permute-start | bytes 258056 | tf_op jit(solution)/shard_map/ppermute | solution.py:561
  23.3 1.0 %collective-permute-done.6 = f32[2,2,128,128]{3,2,1,0:T(8,128)S(1)} collective-permute-done((f32[2,2,128,128]{3,2,1,0:T(8,128)S(1)}, f32[2,2,128,128]{3,2,1,0:T(8,128)S(1)}, u32[]{:S(2)}, u32[]{:S(2)}) %collective-permute-start.6) | collective-permute-done | bytes 262176 | tf_op jit(solution)/shard_map/ppermute | solution.py:572
  24.4 1.7 %collective-permute-start.7 = (f32[2,128,128]{2,1,0:T(8,128)S(1)}, f32[2,128,128]{2,1,0:T(8,128)S(1)}, u32[]{:S(2)}, u32[]{:S(2)}) collective-permute-start(f32[2,128,128]{2,1,0:T(8,128)S(1)} %get-tuple-element.48), channel_id=1, source_target_pairs={{0,1},{1,0},{2,6},{3,7},{4,5},{5,4},{6,2},{7,3},{8,9},{9,8},{10,14... | collective-permute-start | bytes 393224 | tf_op jit(solution)/shard_map/ppermute | solution.py:572
  26.1 2.8 %collective-permute-start.4 = (f32[168,128]{1,0:T(8,128)S(1)}, f32[168,128]{1,0:T(8,128)S(1)}, u32[]{:S(2)}, u32[]{:S(2)}) collective-permute-start(f32[168,128]{1,0:T(8,128)S(1)} %fusion.1), channel_id=1, source_target_pairs={{0,16},{16,0},{1,17},{17,1},{2,18},{18,2},{3,19},{19,3},{4,20},{20... | collective-permute-start | bytes 258056 | tf_op jit(solution)/shard_map/ppermute | solution.py:561
  28.9 0.5 collective-permute-done.7
  29.4 1.8 %collective-permute-start.8 = (f32[128,128]{1,0:T(8,128)S(1)}, f32[128,128]{1,0:T(8,128)S(1)}, u32[]{:S(2)}, u32[]{:S(2)}) collective-permute-start(f32[128,128]{1,0:T(8,128)S(1)} %get-tuple-element.50), channel_id=1, source_target_pairs={{0,8},{8,0},{1,9},{9,1},{2,10},{10,2},{3,11},{11,3},{4,12},{12,4},... | collective-permute-start | bytes 196616 | tf_op jit(solution)/shard_map/ppermute | solution.py:561
  31.2 0.3 collective-permute-done.4
  31.6 2.2 %collective-permute-done.8 = f32[128,128]{1,0:T(8,128)S(1)} collective-permute-done((f32[128,128]{1,0:T(8,128)S(1)}, f32[128,128]{1,0:T(8,128)S(1)}, u32[]{:S(2)}, u32[]{:S(2)}) %collective-permute-start.8) | collective-permute-done | bytes 65568 | tf_op jit(solution)/shard_map/ppermute | solution.py:561
  33.9 2.8 %collective-permute-start.10 = (f32[128,128]{1,0:T(8,128)S(1)}, f32[128,128]{1,0:T(8,128)S(1)}, u32[]{:S(2)}, u32[]{:S(2)}) collective-permute-start(f32[128,128]{1,0:T(8,128)S(1)} %add.38), channel_id=1, source_target_pairs={{0,16},{16,0},{1,17},{17,1},{2,18},{18,2},{3,19},{19,3},{4,20},{20... | collective-permute-start | bytes 196616 | tf_op jit(solution)/shard_map/ppermute | solution.py:561
  36.7 5.3 %early.1 = (f32[128,128]{1,0:T(8,128)S(1)}, f32[128,128]{1,0:T(8,128)S(1)}, f32[128,128]{1,0:T(8,128)S(1)}, f32[128,128]{1,0:T(8,128)S(1)}) custom-call(f32[168,128]{1,0:T(8,128)S(1)} %add.34.mine, f32[168,128]{1,0:T(8,128)S(1)} %collective-permute-done.9.other), custom_call_target="tpu_custom_call" | custom-call | flops 1073741824 | bytes 1048576 | tf_op jit(solution)/shard_map/early/pallas_call | solution.py:411
  42.0 0.2 collective-permute-start.11
  42.2 4.6 %late.1.winv = f32[256,256]{1,0:T(8,128)S(1)} custom-call(f32[128,128]{1,0:T(8,128)S(1)} %get-tuple-element.39.w11_ref, f32[128,128]{1,0:T(8,128)S(1)} %get-tuple-element.40.corner_ref, f32[128,128]{1,0:T(8,128)S(1)} %get-tuple-element.41.last_ref), custom_call_target="tpu_custom_call" | custom-call | flops 1073741824 | bytes 1048576 | tf_op jit(solution)/shard_map/late/pallas_call | solution.py:444
  46.8 0.7 %products.1 = f32[8,40,128]{2,1,0:T(8,128)S(1)} custom-call(f32[256,256]{1,0:T(8,128)S(1)} %late.1.winv, f32[128,128]{1,0:T(8,128)S(1)} %get-tuple-element.42.ninv_ref, f32[128,128]{1,0:T(8,128)S(1)} %add.39.mine, f32[128,128]{1,0:T(8,128)S(1)} %collective-permute-done.11.other), custom_call_target="tpu_custom_call" | custom-call | tf_op jit(solution)/shard_map/products/pallas_call | solution.py:502
  47.5 10.8 %all_to_all.5.got_ref = f32[8,40,128]{2,1,0:T(8,128)S(1)} all-to-all(f32[8,40,128]{2,1,0:T(8,128)S(1)} %products.1), channel_id=1, replica_groups=mesh['dp0'=2,'dp1'=2,'dp2'=2,'dp3'=2,'own0'=2] {'dp1','dp2','own0'}, dimensions={0} | all-to-all | bytes 327680 | tf_op jit(solution)/shard_map/all_to_all | solution.py:624
  58.3 1.3 %placing.1 = (f32[5,16,256]{2,1,0:T(8,128)}, f32[8,16,64]{2,1,0:T(8,128)}) custom-call(s32[8]{0:T(128)S(1)} %copy-done, f32[8,40,128]{2,1,0:T(8,128)S(1)} %all_to_all.5.got_ref), custom_call_target="tpu_custom_call" | custom-call | tf_op jit(solution)/shard_map/placing/pallas_call | solution.py:547
  (25 shorter events, 0.5 us)
Async XLA Ops:
  5.0 2.3 %collective-permute-start = (f32[4,2,168,128]{3,2,1,0:T(8,128)S(1)}, f32[4,2,168,128]{3,2,1,0:T(8,128)S(1)}, u32[]{:S(2)}, u32[]{:S(2)}) collective-permute-start(f32[4,2,168,128]{3,2,1,0:T(8,128)S(1)} %get-tuple-element.26), channel_id=1, source_target_pairs={{0,2},{2,0},{1,3},{3,1},{4,6},{6,4},{5,7},{7,5},{8,10},{10,8},{9,1... | collective-permute-start | bytes 2064392 | tf_op jit(solution)/shard_map/ppermute | solution.py:561
  7.4 8.1 %collective-permute-start.1 = (f32[2,2,168,128]{3,2,1,0:T(8,128)S(1)}, f32[2,2,168,128]{3,2,1,0:T(8,128)S(1)}, u32[]{:S(2)}, u32[]{:S(2)}) collective-permute-start(f32[2,2,168,128]{3,2,1,0:T(8,128)S(1)} %slice.49), channel_id=1, source_target_pairs={{0,1},{1,0},{2,6},{3,7},{4,5},{5,4},{6,2},{7,3},{8,9},{9,8},{10,14... | collective-permute-start | bytes 1032200 | tf_op jit(solution)/shard_map/ppermute | solution.py:572
  10.3 7.4 %collective-permute-start.5 = (f32[4,2,128,128]{3,2,1,0:T(8,128)S(1)}, f32[4,2,128,128]{3,2,1,0:T(8,128)S(1)}, u32[]{:S(2)}, u32[]{:S(2)}) collective-permute-start(f32[4,2,128,128]{3,2,1,0:T(8,128)S(1)} %get-tuple-element.34), channel_id=1, source_target_pairs={{0,2},{2,0},{1,3},{3,1},{4,6},{6,4},{5,7},{7,5},{8,10},{10,8},{9,1... | collective-permute-start | bytes 1572872 | tf_op jit(solution)/shard_map/ppermute | solution.py:561
  15.6 5.5 %collective-permute-start.2 = (f32[2,168,128]{2,1,0:T(8,128)S(1)}, f32[2,168,128]{2,1,0:T(8,128)S(1)}, u32[]{:S(2)}, u32[]{:S(2)}) collective-permute-start(f32[2,168,128]{2,1,0:T(8,128)S(1)} %slice_bitcast_fusion), channel_id=1, source_target_pairs={{0,4},{1,5},{2,3},{3,2},{4,0},{5,1},{6,7},{7,6},{8,12},{9,13},{10,... | collective-permute-start | bytes 516104 | tf_op jit(solution)/shard_map/ppermute | solution.py:572
  17.9 6.4 %collective-permute-start.6 = (f32[2,2,128,128]{3,2,1,0:T(8,128)S(1)}, f32[2,2,128,128]{3,2,1,0:T(8,128)S(1)}, u32[]{:S(2)}, u32[]{:S(2)}) collective-permute-start(f32[2,2,128,128]{3,2,1,0:T(8,128)S(1)} %get-tuple-element.46), channel_id=1, source_target_pairs={{0,4},{1,5},{2,3},{3,2},{4,0},{5,1},{6,7},{7,6},{8,12},{9,13},{10,... | collective-permute-start | bytes 786440 | tf_op jit(solution)/shard_map/ppermute | solution.py:572
  21.2 4.9 %collective-permute-start.3 = (f32[168,128]{1,0:T(8,128)S(1)}, f32[168,128]{1,0:T(8,128)S(1)}, u32[]{:S(2)}, u32[]{:S(2)}) collective-permute-start(f32[168,128]{1,0:T(8,128)S(1)} %slice_bitcast_fusion.4), channel_id=1, source_target_pairs={{0,8},{8,0},{1,9},{9,1},{2,10},{10,2},{3,11},{11,3},{4,12},{12,4},... | collective-permute-start | bytes 258056 | tf_op jit(solution)/shard_map/ppermute | solution.py:561
  24.4 5.0 %collective-permute-start.7 = (f32[2,128,128]{2,1,0:T(8,128)S(1)}, f32[2,128,128]{2,1,0:T(8,128)S(1)}, u32[]{:S(2)}, u32[]{:S(2)}) collective-permute-start(f32[2,128,128]{2,1,0:T(8,128)S(1)} %get-tuple-element.48), channel_id=1, source_target_pairs={{0,1},{1,0},{2,6},{3,7},{4,5},{5,4},{6,2},{7,3},{8,9},{9,8},{10,14... | collective-permute-start | bytes 393224 | tf_op jit(solution)/shard_map/ppermute | solution.py:572
  26.1 5.4 %collective-permute-start.4 = (f32[168,128]{1,0:T(8,128)S(1)}, f32[168,128]{1,0:T(8,128)S(1)}, u32[]{:S(2)}, u32[]{:S(2)}) collective-permute-start(f32[168,128]{1,0:T(8,128)S(1)} %fusion.1), channel_id=1, source_target_pairs={{0,16},{16,0},{1,17},{17,1},{2,18},{18,2},{3,19},{19,3},{4,20},{20... | collective-permute-start | bytes 258056 | tf_op jit(solution)/shard_map/ppermute | solution.py:561
  29.4 4.3 %collective-permute-start.8 = (f32[128,128]{1,0:T(8,128)S(1)}, f32[128,128]{1,0:T(8,128)S(1)}, u32[]{:S(2)}, u32[]{:S(2)}) collective-permute-start(f32[128,128]{1,0:T(8,128)S(1)} %get-tuple-element.50), channel_id=1, source_target_pairs={{0,8},{8,0},{1,9},{9,1},{2,10},{10,2},{3,11},{11,3},{4,12},{12,4},... | collective-permute-start | bytes 196616 | tf_op jit(solution)/shard_map/ppermute | solution.py:561
  33.8 2.9 %collective-permute-start.9 = (f32[168,128]{1,0:T(8,128)S(1)}, f32[168,128]{1,0:T(8,128)S(1)}, u32[]{:S(2)}, u32[]{:S(2)}) collective-permute-start(f32[168,128]{1,0:T(8,128)S(1)} %add.34.mine), channel_id=1, source_target_pairs={{0,2},{2,0},{1,3},{3,1},{4,6},{6,4},{5,7},{7,5},{8,10},{10,8},{9,1... | collective-permute-start | bytes 258056 | tf_op jit(solution)/shard_map/ppermute | solution.py:561
  33.9 8.1 %collective-permute-start.10 = (f32[128,128]{1,0:T(8,128)S(1)}, f32[128,128]{1,0:T(8,128)S(1)}, u32[]{:S(2)}, u32[]{:S(2)}) collective-permute-start(f32[128,128]{1,0:T(8,128)S(1)} %add.38), channel_id=1, source_target_pairs={{0,16},{16,0},{1,17},{17,1},{2,18},{18,2},{3,19},{19,3},{4,20},{20... | collective-permute-start | bytes 196616 | tf_op jit(solution)/shard_map/ppermute | solution.py:561
  42.0 16.3 %copy-start = (s32[8]{0:T(128)S(1)}, s32[8]{0:T(128)}, u32[]{:S(2)}) copy-start(s32[8]{0:T(128)} %owner_map.1) | copy-start | bytes 100
  42.0 4.8 %collective-permute-start.11 = (f32[128,128]{1,0:T(8,128)S(1)}, f32[128,128]{1,0:T(8,128)S(1)}, u32[]{:S(2)}, u32[]{:S(2)}) collective-permute-start(f32[128,128]{1,0:T(8,128)S(1)} %add.39.mine), channel_id=1, source_target_pairs={{0,2},{2,0},{1,3},{3,1},{4,6},{6,4},{5,7},{7,5},{8,10},{10,8},{9,1... | collective-permute-start | bytes 196616 | tf_op jit(solution)/shard_map/ppermute | solution.py:561

commit v9 on v8

--- a/solution.py
+++ b/solution.py
@@ -49,7 +49,6 @@
 
 
 AHEAD = 3
-STEPS = 2
 
 
 def layer_copies(place, sources, buffers, sems):
@@ -175,6 +174,16 @@
         flat[i, :n] = mixed[:, :n]
         flat[i, n:] = mixed[:, n:]
         write_halves(place, i, 0, flat, keep, send, swapped=True)
+
+
+def dot(a, b, last=False):
+    return lax.dot_general(
+        a,
+        b,
+        (((1,), (1 if last else 0,)), ((), ())),
+        precision=HIGHEST,
+        preferred_element_type=jnp.float32,
+    )
 
 
 def gram_cost(wide_rows, columns):
@@ -229,6 +238,10 @@
     return jnp.take_along_axis(x, index, axis=1, mode="promise_in_bounds")
 
 
+def spread(x, k):
+    return jnp.broadcast_to(x[k : k + 1, :], x.shape)
+
+
 def trailing_update(a_ref, left_ref, right_ref, base):
     size = a_ref.shape[1]
     a_ref[pl.ds(pl.multiple_of(base, PANEL), PANEL), :] = jnp.zeros((PANEL, size), jnp.float32)
@@ -240,31 +253,46 @@
     )
 
 
-def sweep_panel(a_ref, left_ref, right_ref, tile, step, panel):
-    size = a_ref.shape[1]
-    tiles = size // LANES
-    first = step * PANEL
-    base = tile * LANES + first
-    trailing_update(a_ref, left_ref, right_ref, base)
-
-    shape = (PANEL, LANES)
-    sub = lax.broadcasted_iota(jnp.int32, shape, 0)
-    lane = lax.broadcasted_iota(jnp.int32, shape, 1)
-    parts = [panel[:, LANES * t : LANES * (t + 1)] for t in range(tiles)]
-    rows = [
-        [jnp.broadcast_to(part[k : k + 1, :], shape) for part in parts] for k in range(PANEL)
-    ]
-    index = [jnp.full(shape, 0, jnp.int32) + (first + i) for i in range(PANEL)]
+def store_corner(d_ref, panel, first, corrections):
+    shape = panel.shape
+    lanes = [jnp.full(shape, 0, jnp.int32) + (first + i) for i in range(PANEL)]
+    at = 0
+    for j in range(PANEL):
+        row = spread(panel, j)
+        for i in range(j, PANEL):
+            value = lane_gather(row, lanes[i])
+            for w in corrections:
+                value = value - w[i] * w[j]
+            d_ref[at] = value
+            at += 1
+
+
+def sweep_panel(a_ref, left_ref, right_ref, d_ref, step, panel, before):
+    first = pl.multiple_of(step * PANEL, PANEL)
+    shape = panel.shape
+    sub, lane = iotas(shape)
+    next_first = jnp.where(first == LANES - PANEL, 0, first + PANEL)
+    next_lane = next_first + sub
+    following = a_ref[pl.ds(pl.multiple_of(first + 2 * PANEL, PANEL), PANEL), :]
+    trailing_update(a_ref, left_ref, right_ref, first)
+
+    following = jnp.where((lane >= first - PANEL) & (lane < first), 0.0, following)
+    for k in range(PANEL):
+        row = spread(before, k)
+        following = following - lane_gather(row, next_lane) * row
+    own = (lane >= first) & (lane < first + PANEL)
+    following = jnp.where(own, 0.0, following)
+
     d = [[None] * PANEL for _ in range(PANEL)]
+    at = 0
     for j in range(PANEL):
         for i in range(j, PANEL):
-            d[i][j] = lane_gather(rows[j][tile], index[i])
-    own = (lane >= first) & (lane < first + PANEL)
-    last = first == LANES - PANEL
-    next_lane = jnp.where(last, 0, first + PANEL) + sub
-    q = [[None] * tiles for _ in range(PANEL)]
+            d[i][j] = d_ref[at]
+            at += 1
+    q = [None] * PANEL
     weights = [None] * PANEL
     factor = [[None] * PANEL for _ in range(PANEL)]
+    middle = None
     for k in range(PANEL):
         scale = lax.rsqrt(d[k][k])
         for i in range(k + 1, PANEL):
@@ -272,28 +300,23 @@
         for i in range(k + 1, PANEL):
             for j in range(k + 1, i + 1):
                 d[i][j] = d[i][j] - factor[i][k] * factor[j][k]
-        for t in range(tiles):
-            value = rows[k][t]
-            if t == tile:
-                value = jnp.where(own, jnp.where(lane == first + k, -1.0, 0.0), value)
-            for j in range(k):
-                value = value - factor[k][j] * q[j][t]
-            q[k][t] = value * scale
-        source = rows[k][tile]
-        if tile + 1 < tiles:
-            source = jnp.where(last, rows[k][tile + 1], source)
-        value = lane_gather(source, next_lane)
+        row = spread(panel, k)
+        value = jnp.where(own, jnp.where(lane == first + k, -1.0, 0.0), row)
+        weight = lane_gather(row, next_lane)
         for j in range(k):
-            value = value - factor[k][j] * weights[j]
-        weights[k] = value * scale
-
-    packed = []
-    for t in range(tiles):
-        value = q[0][t]
-        for k in range(1, PANEL):
-            value = jnp.where(sub == k, q[k][t], value)
-        packed.append(value)
-    whole = jnp.concatenate(packed, axis=1) if tiles > 1 else packed[0]
+            value = value - factor[k][j] * q[j]
+            weight = weight - factor[k][j] * weights[j]
+        q[k] = value * scale
+        weights[k] = weight * scale
+        following = following - weights[k] * q[k]
+        if k == PANEL // 2 - 1:
+            middle = following
+    corrections = [[spread(w, i) for i in range(PANEL)] for w in weights[PANEL // 2 :]]
+    store_corner(d_ref, middle, next_first, corrections)
+
+    whole = q[0]
+    for k in range(1, PANEL):
+        whole = jnp.where(sub == k, q[k], whole)
     high = whole.astype(jnp.bfloat16).astype(jnp.float32)
     rest = whole - high
     middle = rest.astype(jnp.bfloat16).astype(jnp.float32)
@@ -302,19 +325,7 @@
     right = jnp.concatenate([high, middle, high, middle, low, high], axis=0)
     left_ref[...] = left.astype(jnp.bfloat16)
     right_ref[...] = right.astype(jnp.bfloat16)
-
-    after = pl.multiple_of(base + 2 * PANEL, PANEL)
-    following = a_ref[pl.ds(after, PANEL), :]
-    result = []
-    for t in range(tiles):
-        value = following[:, LANES * t : LANES * (t + 1)]
-        if t == tile:
-            value = jnp.where(own, 0.0, value)
-        terms = [weights[k] * q[k][t] for k in range(PANEL)]
-        while len(terms) > 1:
-            terms = [terms[i] + terms[i + 1] for i in range(0, len(terms), 2)]
-        result.append(value - terms[0])
-    return jnp.concatenate(result, axis=1) if tiles > 1 else result[0]
+    return following, whole
 
 
 def place_halves(place, pieces, first_row, flat):
@@ -338,57 +349,31 @@
 
 
 def sweep_all(works):
-    for _, left, right in works:
+    carry = []
+    for a_ref, left, right, d_ref in works:
         left[...] = jnp.zeros(left.shape, left.dtype)
         right[...] = jnp.zeros(right.shape, right.dtype)
-
-    def step(i, panels):
-        for j in range(STEPS):
-            panels = tuple(
-                sweep_panel(*work, 0, i * STEPS + j, panel) for work, panel in zip(works, panels)
-            )
-        return panels
-
-    size = works[0][0].shape[1]
-    trips = size // (PANEL * STEPS)
-    lax.fori_loop(0, trips, step, tuple(a[PANEL : 2 * PANEL] for a, _, _ in works))
-    for work in works:
-        trailing_update(*work, size)
-    return [-a[PANEL : PANEL + size] for a, _, _ in works]
-
-
-def work_shapes(size):
+        panel = a_ref[PANEL : 2 * PANEL]
+        store_corner(d_ref, panel, 0, ())
+        carry.append((panel, jnp.zeros(panel.shape, jnp.float32)))
+
+    def step(i, carry):
+        return tuple(sweep_panel(*work, i, *state) for work, state in zip(works, carry))
+
+    lax.fori_loop(0, LANES // PANEL, step, tuple(carry))
+    for a_ref, left, right, _ in works:
+        trailing_update(a_ref, left, right, LANES)
+    return [-work[0][PANEL : PANEL + LANES] for work in works]
+
+
+def work_shapes():
     splits = 6 * PANEL
     return [
-        pltpu.VMEM((size + 2 * PANEL, size), jnp.float32),
-        pltpu.VMEM((splits, size), jnp.bfloat16),
-        pltpu.VMEM((splits, size), jnp.bfloat16),
+        pltpu.VMEM((LANES + 2 * PANEL, LANES), jnp.float32),
+        pltpu.VMEM((splits, LANES), jnp.bfloat16),
+        pltpu.VMEM((splits, LANES), jnp.bfloat16),
+        pltpu.VMEM((PANEL * (PANEL + 1) // 2, PANEL, LANES), jnp.float32),
     ]
-
-
-def aligned_rows(ref, index, count):
-    if count % PANEL == 0:
-        return ref[pl.ds(pl.multiple_of(index * count, count), count), :]
-    per_slab = PANEL // count
-    slab = ref[pl.ds(pl.multiple_of(index // per_slab * PANEL, PANEL), PANEL), :]
-    value = slab[:count]
-    for i in range(1, per_slab):
-        value = jnp.where(index % per_slab == i, slab[i * count : (i + 1) * count], value)
-    return value
-
-
-def packs(cols, rows):
-    return cols == 2 * PANEL and 2 * rows == LANES
-
-
-def dot(a, b, last=False):
-    return lax.dot_general(
-        a,
-        b,
-        (((1,), (1 if last else 0,)), ((), ())),
-        precision=HIGHEST,
-        preferred_element_type=jnp.float32,
-    )
 
 
 def early_kernel(
@@ -400,10 +385,10 @@
     slab = a_flat[n : n + PANEL]
     first, square = unpack_pair(a_flat[:n], jnp.broadcast_to(slab[:1], (n, n)))
     load_damped(works[0], first / total)
-    load_damped(works[3], square / total)
+    load_damped(works[4], square / total)
     corner_ref[...] = b_flat[:n] / total
     last_ref[...] = unfold(b_flat[n:], jnp.broadcast_to(slab[1:2], (n, n))) / total
-    w11_ref[...], ninv_ref[...] = sweep_all((works[:3], works[3:]))
+    w11_ref[...], ninv_ref[...] = sweep_all((works[:4], works[4:]))
 
 
 def early(place, pieces, total):
@@ -416,8 +401,8 @@
         scratch_shapes=[
             pltpu.VMEM((EARLY_ROWS, n), jnp.float32),
             pltpu.VMEM((LATE_ROWS, n), jnp.float32),
-            *work_shapes(n),
-            *work_shapes(n),
+            *work_shapes(),
+            *work_shapes(),
         ],
         cost_estimate=sweep_cost(),
         compiler_params=PARAMS,
@@ -446,11 +431,26 @@
         in_specs=[VMEM] * 3,
         out_specs=VMEM,
         out_shape=jax.ShapeDtypeStruct((2 * n, 2 * n), jnp.float32),
-        scratch_shapes=work_shapes(n),
+        scratch_shapes=work_shapes(),
         cost_estimate=sweep_cost(),
         compiler_params=PARAMS,
         name="late",
     )(w11, corner, last)
+
+
+def aligned_rows(ref, index, count):
+    if count % PANEL == 0:
+        return ref[pl.ds(pl.multiple_of(index * count, count), count), :]
+    per_slab = PANEL // count
+    slab = ref[pl.ds(pl.multiple_of(index // per_slab * PANEL, PANEL), PANEL), :]
+    value = slab[:count]
+    for i in range(1, per_slab):
+        value = jnp.where(index % per_slab == i, slab[i * count : (i + 1) * count], value)
+    return value
+
+
+def packs(cols, rows):
+    return cols == 2 * PANEL and 2 * rows == LANES
 
 
 def product_kernel(place, total, rows, winv, ninv_ref, mine, other, out_ref, flat):

time: 59.8 us -> 64.2 us (1.074)
  Pallas kernels: 17.2 us -> 21.6 us
    pallas_call x1, Pallas kernels: 5.29 us -> 8.43 us  [early(): pl.pallas_call(functools.partial(early_kernel, place, total), in_specs=[V...]
    pallas_call x1, Pallas kernels: 4.59 us -> 5.86 us  [late(): pl.pallas_call(late_kernel, in_specs=[VMEM] * 3, out_specs=VMEM, out_shap...]
  transfers between devices with their start and end apart: 12 -> 12, of which waited for: 7 -> 7; matrix products, arithmetic and copies ran while one was open for 0% -> 0% of each run, Pallas kernels for 18% -> 24%
where the time goes in v9:
time: 64.2 us; the launch traced here: 64 us
  Pallas kernels  21.6 us (34%)
  starting transfers between devices  17.2 us (27%)
  waiting for transfers between devices  13.3 us (21%)
  blocking collectives  10.8 us (17%)
  between operations  0.77 us (1%)
    all_to_all x1, blocking collectives, on_device(): got = lax.all_to_all(sent, (place.near, place.second, place.first), 0, 0)  10.8 us
    ppermute x8, starting transfers between devices, swap(): return lax.ppermute(value, axis, [(0, 1), (1, 0)])  10.4 us
    ppermute x4, waiting for transfers between devices, swap_by_core(): return lax.ppermute(value, (place.second, place.core, place.first), pairs)  9.89 us
    pallas_call x1, Pallas kernels, early(): pl.pallas_call(functools.partial(early_kernel, place, total), in_specs=[V...  8.43 us
    ppermute x4, starting transfers between devices, swap_by_core(): return lax.ppermute(value, (place.second, place.core, place.first), pairs)  6.83 us
    pallas_call x1, Pallas kernels, late(): pl.pallas_call(late_kernel, in_specs=[VMEM] * 3, out_specs=VMEM, out_shap...  5.86 us
    pallas_call x1, Pallas kernels, squares(): pl.pallas_call(functools.partial(squares_kernel, place), in_specs=[HBM, H...  4.39 us
    ppermute x8, waiting for transfers between devices, swap(): return lax.ppermute(value, axis, [(0, 1), (1, 0)])  3.38 us
  transfers between devices with their start and end apart: 12, of which 7 were waited for; matrix products, arithmetic and copies ran while one was open for 0% of the time, Pallas kernels for 24%

profile of v9, /device:TPU:0, one launch (start us, length us, event | category | flops | bytes accessed | tf_op | source)
XLA Modules:
  0.0 64.0 jit_solution(7069574026625803683)
XLA Ops:
  0.6 4.4 %squares.1 = (f32[4,2,168,128]{3,2,1,0:T(8,128)S(1)}, f32[4,2,168,128]{3,2,1,0:T(8,128)S(1)}, bf16[8,768,256]{2,1,0:T(8,128)(2,1)S(1)}, bf16[8,768,128]{2,1,0:T(8,128)(2,1)S(1)}) custom-call(bf16[8,768,256]{2,1,0:T(8,128)(2,1)} %wide_hbm.1, bf16[8,768,128]{2,1,0:T(8,128)(2,1)} %narrow_hbm.1), custom_call_target="tpu_custom_call" | custom-call | flops 1006632960 | bytes 3145728 | tf_op jit(solution)/shard_map/squares/pallas_call | solution.py:198
  5.0 0.5 collective-permute-start
  5.5 0.9 %mixed.1 = (f32[4,2,128,128]{3,2,1,0:T(8,128)S(1)}, f32[4,2,128,128]{3,2,1,0:T(8,128)S(1)}) custom-call(bf16[8,768,256]{2,1,0:T(8,128)(2,1)S(1)} %get-tuple-element.27.wides, bf16[8,768,128]{2,1,0:T(8,128)(2,1)S(1)} %get-tuple-element.28.narrows), custom_call_target="tpu_custom_call" | custom-call | flops 402653184 | bytes 3145728 | tf_op jit(solution)/shard_map/mixed/pallas_call | solution.py:225
  6.5 0.8 %collective-permute-done = f32[4,2,168,128]{3,2,1,0:T(8,128)S(1)} collective-permute-done((f32[4,2,168,128]{3,2,1,0:T(8,128)S(1)}, f32[4,2,168,128]{3,2,1,0:T(8,128)S(1)}, u32[]{:S(2)}, u32[]{:S(2)}) %collective-permute-start) | collective-permute-done | bytes 688160 | tf_op jit(solution)/shard_map/ppermute | solution.py:561
  7.4 2.9 %collective-permute-start.1 = (f32[2,2,168,128]{3,2,1,0:T(8,128)S(1)}, f32[2,2,168,128]{3,2,1,0:T(8,128)S(1)}, u32[]{:S(2)}, u32[]{:S(2)}) collective-permute-start(f32[2,2,168,128]{3,2,1,0:T(8,128)S(1)} %slice.49), channel_id=1, source_target_pairs={{0,1},{1,0},{2,6},{3,7},{4,5},{5,4},{6,2},{7,3},{8,9},{9,8},{10,14... | collective-permute-start | bytes 1032200 | tf_op jit(solution)/shard_map/ppermute | solution.py:572
  10.4 5.2 %collective-permute-done.1 = f32[2,2,168,128]{3,2,1,0:T(8,128)S(1)} collective-permute-done((f32[2,2,168,128]{3,2,1,0:T(8,128)S(1)}, f32[2,2,168,128]{3,2,1,0:T(8,128)S(1)}, u32[]{:S(2)}, u32[]{:S(2)}) %collective-permute-start.1) | collective-permute-done | bytes 344096 | tf_op jit(solution)/shard_map/ppermute | solution.py:572
  15.6 2.1 %collective-permute-start.2 = (f32[2,168,128]{2,1,0:T(8,128)S(1)}, f32[2,168,128]{2,1,0:T(8,128)S(1)}, u32[]{:S(2)}, u32[]{:S(2)}) collective-permute-start(f32[2,168,128]{2,1,0:T(8,128)S(1)} %slice_bitcast_fusion), channel_id=1, source_target_pairs={{0,4},{1,5},{2,3},{3,2},{4,0},{5,1},{6,7},{7,6},{8,12},{9,13},{10,... | collective-permute-start | bytes 516104 | tf_op jit(solution)/shard_map/ppermute | solution.py:572
  17.9 0.1 collective-permute-start.6
  18.0 3.2 %collective-permute-done.2 = f32[2,168,128]{2,1,0:T(8,128)S(1)} collective-permute-done((f32[2,168,128]{2,1,0:T(8,128)S(1)}, f32[2,168,128]{2,1,0:T(8,128)S(1)}, u32[]{:S(2)}, u32[]{:S(2)}) %collective-permute-start.2) | collective-permute-done | bytes 172064 | tf_op jit(solution)/shard_map/ppermute | solution.py:572
  21.2 2.1 %collective-permute-start.3 = (f32[168,128]{1,0:T(8,128)S(1)}, f32[168,128]{1,0:T(8,128)S(1)}, u32[]{:S(2)}, u32[]{:S(2)}) collective-permute-start(f32[168,128]{1,0:T(8,128)S(1)} %slice_bitcast_fusion.4), channel_id=1, source_target_pairs={{0,8},{8,0},{1,9},{9,1},{2,10},{10,2},{3,11},{11,3},{4,12},{12,4},... | collective-permute-start | bytes 258056 | tf_op jit(solution)/shard_map/ppermute | solution.py:561
  23.3 1.0 %collective-permute-done.6 = f32[2,2,128,128]{3,2,1,0:T(8,128)S(1)} collective-permute-done((f32[2,2,128,128]{3,2,1,0:T(8,128)S(1)}, f32[2,2,128,128]{3,2,1,0:T(8,128)S(1)}, u32[]{:S(2)}, u32[]{:S(2)}) %collective-permute-start.6) | collective-permute-done | bytes 262176 | tf_op jit(solution)/shard_map/ppermute | solution.py:572
  24.4 1.7 %collective-permute-start.7 = (f32[2,128,128]{2,1,0:T(8,128)S(1)}, f32[2,128,128]{2,1,0:T(8,128)S(1)}, u32[]{:S(2)}, u32[]{:S(2)}) collective-permute-start(f32[2,128,128]{2,1,0:T(8,128)S(1)} %get-tuple-element.48), channel_id=1, source_target_pairs={{0,1},{1,0},{2,6},{3,7},{4,5},{5,4},{6,2},{7,3},{8,9},{9,8},{10,14... | collective-permute-start | bytes 393224 | tf_op jit(solution)/shard_map/ppermute | solution.py:572
  26.1 2.8 %collective-permute-start.4 = (f32[168,128]{1,0:T(8,128)S(1)}, f32[168,128]{1,0:T(8,128)S(1)}, u32[]{:S(2)}, u32[]{:S(2)}) collective-permute-start(f32[168,128]{1,0:T(8,128)S(1)} %fusion.1), channel_id=1, source_target_pairs={{0,16},{16,0},{1,17},{17,1},{2,18},{18,2},{3,19},{19,3},{4,20},{20... | collective-permute-start | bytes 258056 | tf_op jit(solution)/shard_map/ppermute | solution.py:561
  28.9 0.5 collective-permute-done.7
  29.4 1.8 %collective-permute-start.8 = (f32[128,128]{1,0:T(8,128)S(1)}, f32[128,128]{1,0:T(8,128)S(1)}, u32[]{:S(2)}, u32[]{:S(2)}) collective-permute-start(f32[128,128]{1,0:T(8,128)S(1)} %get-tuple-element.50), channel_id=1, source_target_pairs={{0,8},{8,0},{1,9},{9,1},{2,10},{10,2},{3,11},{11,3},{4,12},{12,4},... | collective-permute-start | bytes 196616 | tf_op jit(solution)/shard_map/ppermute | solution.py:561
  31.2 0.3 collective-permute-done.4
  31.6 2.2 %collective-permute-done.8 = f32[128,128]{1,0:T(8,128)S(1)} collective-permute-done((f32[128,128]{1,0:T(8,128)S(1)}, f32[128,128]{1,0:T(8,128)S(1)}, u32[]{:S(2)}, u32[]{:S(2)}) %collective-permute-start.8) | collective-permute-done | bytes 65568 | tf_op jit(solution)/shard_map/ppermute | solution.py:561
  33.9 2.8 %collective-permute-start.10 = (f32[128,128]{1,0:T(8,128)S(1)}, f32[128,128]{1,0:T(8,128)S(1)}, u32[]{:S(2)}, u32[]{:S(2)}) collective-permute-start(f32[128,128]{1,0:T(8,128)S(1)} %add.38), channel_id=1, source_target_pairs={{0,16},{16,0},{1,17},{17,1},{2,18},{18,2},{3,19},{19,3},{4,20},{20... | collective-permute-start | bytes 196616 | tf_op jit(solution)/shard_map/ppermute | solution.py:561
  36.7 8.4 %early.1 = (f32[128,128]{1,0:T(8,128)S(1)}, f32[128,128]{1,0:T(8,128)S(1)}, f32[128,128]{1,0:T(8,128)S(1)}, f32[128,128]{1,0:T(8,128)S(1)}) custom-call(f32[168,128]{1,0:T(8,128)S(1)} %add.34.mine, f32[168,128]{1,0:T(8,128)S(1)} %collective-permute-done.9.other), custom_call_target="tpu_custom_call" | custom-call | flops 1073741824 | bytes 1048576 | tf_op jit(solution)/shard_map/early/pallas_call | solution.py:396
  45.1 0.2 collective-permute-start.11
  45.4 5.9 %late.1.winv = f32[256,256]{1,0:T(8,128)S(1)} custom-call(f32[128,128]{1,0:T(8,128)S(1)} %get-tuple-element.39.w11_ref, f32[128,128]{1,0:T(8,128)S(1)} %get-tuple-element.40.corner_ref, f32[128,128]{1,0:T(8,128)S(1)} %get-tuple-element.41.last_ref), custom_call_target="tpu_custom_call" | custom-call | flops 1073741824 | bytes 1048576 | tf_op jit(solution)/shard_map/late/pallas_call | solution.py:429
  51.2 0.7 %products.1 = f32[8,40,128]{2,1,0:T(8,128)S(1)} custom-call(f32[256,256]{1,0:T(8,128)S(1)} %late.1.winv, f32[128,128]{1,0:T(8,128)S(1)} %get-tuple-element.42.ninv_ref, f32[128,128]{1,0:T(8,128)S(1)} %add.39.mine, f32[128,128]{1,0:T(8,128)S(1)} %collective-permute-done.11.other), custom_call_target="tpu_custom_call" | custom-call | tf_op jit(solution)/shard_map/products/pallas_call | solution.py:502
  52.0 10.8 %all_to_all.5.got_ref = f32[8,40,128]{2,1,0:T(8,128)S(1)} all-to-all(f32[8,40,128]{2,1,0:T(8,128)S(1)} %products.1), channel_id=1, replica_groups=mesh['dp0'=2,'dp1'=2,'dp2'=2,'dp3'=2,'own0'=2] {'dp1','dp2','own0'}, dimensions={0} | all-to-all | bytes 327680 | tf_op jit(solution)/shard_map/all_to_all | solution.py:624
  62.7 1.3 %placing.1 = (f32[5,16,256]{2,1,0:T(8,128)}, f32[8,16,64]{2,1,0:T(8,128)}) custom-call(s32[8]{0:T(128)S(1)} %copy-done, f32[8,40,128]{2,1,0:T(8,128)S(1)} %all_to_all.5.got_ref), custom_call_target="tpu_custom_call" | custom-call | tf_op jit(solution)/shard_map/placing/pallas_call | solution.py:547
  (25 shorter events, 0.5 us)
Async XLA Ops:
  5.0 2.3 %collective-permute-start = (f32[4,2,168,128]{3,2,1,0:T(8,128)S(1)}, f32[4,2,168,128]{3,2,1,0:T(8,128)S(1)}, u32[]{:S(2)}, u32[]{:S(2)}) collective-permute-start(f32[4,2,168,128]{3,2,1,0:T(8,128)S(1)} %get-tuple-element.26), channel_id=1, source_target_pairs={{0,2},{2,0},{1,3},{3,1},{4,6},{6,4},{5,7},{7,5},{8,10},{10,8},{9,1... | collective-permute-start | bytes 2064392 | tf_op jit(solution)/shard_map/ppermute | solution.py:561
  7.4 8.1 %collective-permute-start.1 = (f32[2,2,168,128]{3,2,1,0:T(8,128)S(1)}, f32[2,2,168,128]{3,2,1,0:T(8,128)S(1)}, u32[]{:S(2)}, u32[]{:S(2)}) collective-permute-start(f32[2,2,168,128]{3,2,1,0:T(8,128)S(1)} %slice.49), channel_id=1, source_target_pairs={{0,1},{1,0},{2,6},{3,7},{4,5},{5,4},{6,2},{7,3},{8,9},{9,8},{10,14... | collective-permute-start | bytes 1032200 | tf_op jit(solution)/shard_map/ppermute | solution.py:572
  10.3 7.4 %collective-permute-start.5 = (f32[4,2,128,128]{3,2,1,0:T(8,128)S(1)}, f32[4,2,128,128]{3,2,1,0:T(8,128)S(1)}, u32[]{:S(2)}, u32[]{:S(2)}) collective-permute-start(f32[4,2,128,128]{3,2,1,0:T(8,128)S(1)} %get-tuple-element.34), channel_id=1, source_target_pairs={{0,2},{2,0},{1,3},{3,1},{4,6},{6,4},{5,7},{7,5},{8,10},{10,8},{9,1... | collective-permute-start | bytes 1572872 | tf_op jit(solution)/shard_map/ppermute | solution.py:561
  15.6 5.5 %collective-permute-start.2 = (f32[2,168,128]{2,1,0:T(8,128)S(1)}, f32[2,168,128]{2,1,0:T(8,128)S(1)}, u32[]{:S(2)}, u32[]{:S(2)}) collective-permute-start(f32[2,168,128]{2,1,0:T(8,128)S(1)} %slice_bitcast_fusion), channel_id=1, source_target_pairs={{0,4},{1,5},{2,3},{3,2},{4,0},{5,1},{6,7},{7,6},{8,12},{9,13},{10,... | collective-permute-start | bytes 516104 | tf_op jit(solution)/shard_map/ppermute | solution.py:572
  17.9 6.4 %collective-permute-start.6 = (f32[2,2,128,128]{3,2,1,0:T(8,128)S(1)}, f32[2,2,128,128]{3,2,1,0:T(8,128)S(1)}, u32[]{:S(2)}, u32[]{:S(2)}) collective-permute-start(f32[2,2,128,128]{3,2,1,0:T(8,128)S(1)} %get-tuple-element.46), channel_id=1, source_target_pairs={{0,4},{1,5},{2,3},{3,2},{4,0},{5,1},{6,7},{7,6},{8,12},{9,13},{10,... | collective-permute-start | bytes 786440 | tf_op jit(solution)/shard_map/ppermute | solution.py:572
  21.2 4.9 %collective-permute-start.3 = (f32[168,128]{1,0:T(8,128)S(1)}, f32[168,128]{1,0:T(8,128)S(1)}, u32[]{:S(2)}, u32[]{:S(2)}) collective-permute-start(f32[168,128]{1,0:T(8,128)S(1)} %slice_bitcast_fusion.4), channel_id=1, source_target_pairs={{0,8},{8,0},{1,9},{9,1},{2,10},{10,2},{3,11},{11,3},{4,12},{12,4},... | collective-permute-start | bytes 258056 | tf_op jit(solution)/shard_map/ppermute | solution.py:561
  24.4 5.0 %collective-permute-start.7 = (f32[2,128,128]{2,1,0:T(8,128)S(1)}, f32[2,128,128]{2,1,0:T(8,128)S(1)}, u32[]{:S(2)}, u32[]{:S(2)}) collective-permute-start(f32[2,128,128]{2,1,0:T(8,128)S(1)} %get-tuple-element.48), channel_id=1, source_target_pairs={{0,1},{1,0},{2,6},{3,7},{4,5},{5,4},{6,2},{7,3},{8,9},{9,8},{10,14... | collective-permute-start | bytes 393224 | tf_op jit(solution)/shard_map/ppermute | solution.py:572
  26.1 5.4 %collective-permute-start.4 = (f32[168,128]{1,0:T(8,128)S(1)}, f32[168,128]{1,0:T(8,128)S(1)}, u32[]{:S(2)}, u32[]{:S(2)}) collective-permute-start(f32[168,128]{1,0:T(8,128)S(1)} %fusion.1), channel_id=1, source_target_pairs={{0,16},{16,0},{1,17},{17,1},{2,18},{18,2},{3,19},{19,3},{4,20},{20... | collective-permute-start | bytes 258056 | tf_op jit(solution)/shard_map/ppermute | solution.py:561
  29.4 4.3 %collective-permute-start.8 = (f32[128,128]{1,0:T(8,128)S(1)}, f32[128,128]{1,0:T(8,128)S(1)}, u32[]{:S(2)}, u32[]{:S(2)}) collective-permute-start(f32[128,128]{1,0:T(8,128)S(1)} %get-tuple-element.50), channel_id=1, source_target_pairs={{0,8},{8,0},{1,9},{9,1},{2,10},{10,2},{3,11},{11,3},{4,12},{12,4},... | collective-permute-start | bytes 196616 | tf_op jit(solution)/shard_map/ppermute | solution.py:561
  33.8 2.9 %collective-permute-start.9 = (f32[168,128]{1,0:T(8,128)S(1)}, f32[168,128]{1,0:T(8,128)S(1)}, u32[]{:S(2)}, u32[]{:S(2)}) collective-permute-start(f32[168,128]{1,0:T(8,128)S(1)} %add.34.mine), channel_id=1, source_target_pairs={{0,2},{2,0},{1,3},{3,1},{4,6},{6,4},{5,7},{7,5},{8,10},{10,8},{9,1... | collective-permute-start | bytes 258056 | tf_op jit(solution)/shard_map/ppermute | solution.py:561
  33.9 11.3 %collective-permute-start.10 = (f32[128,128]{1,0:T(8,128)S(1)}, f32[128,128]{1,0:T(8,128)S(1)}, u32[]{:S(2)}, u32[]{:S(2)}) collective-permute-start(f32[128,128]{1,0:T(8,128)S(1)} %add.38), channel_id=1, source_target_pairs={{0,16},{16,0},{1,17},{17,1},{2,18},{18,2},{3,19},{19,3},{4,20},{20... | collective-permute-start | bytes 196616 | tf_op jit(solution)/shard_map/ppermute | solution.py:561
  45.1 17.6 %copy-start = (s32[8]{0:T(128)S(1)}, s32[8]{0:T(128)}, u32[]{:S(2)}) copy-start(s32[8]{0:T(128)} %owner_map.1) | copy-start | bytes 100
  45.1 6.1 %collective-permute-start.11 = (f32[128,128]{1,0:T(8,128)S(1)}, f32[128,128]{1,0:T(8,128)S(1)}, u32[]{:S(2)}, u32[]{:S(2)}) collective-permute-start(f32[128,128]{1,0:T(8,128)S(1)} %add.39.mine), channel_id=1, source_target_pairs={{0,2},{2,0},{1,3},{3,1},{4,6},{6,4},{5,7},{7,5},{8,10},{10,8},{9,1... | collective-permute-start | bytes 196616 | tf_op jit(solution)/shard_map/ppermute | solution.py:561

commit v10 on v7

--- a/solution.py
+++ b/solution.py
@@ -64,17 +64,17 @@
     ]
 
 
-def write_halves(place, i, first_row, flat, keep_ref, send_ref):
+def both_halves(place, flat, i):
     rows = flat.shape[1] // 2
     core = lax.axis_index(place.core)
-    z, y, x = i // 4, (i // 2) % 2, i % 2
-    mine = jnp.where(core == 0, x * 2 + y, y * 2 + x)
-    other = jnp.where(core == 0, y * 2 + x, x * 2 + y)
     kept = pl.multiple_of(core * rows, PANEL)
     sent = pl.multiple_of((1 - core) * rows, PANEL)
-    there = slice(first_row, first_row + rows)
-    keep_ref[mine, z, there] = flat[i, pl.ds(kept, rows), :]
-    send_ref[other, z, there] = flat[i, pl.ds(sent, rows), :]
+    return flat[i, pl.ds(kept, rows), :], flat[i, pl.ds(sent, rows), :]
+
+
+def by_core(place, first, second):
+    core = lax.axis_index(place.core)
+    return jnp.where(core == 0, first, second), jnp.where(core == 0, second, first)
 
 
 def iotas(shape):
@@ -132,29 +132,69 @@
 LATE_ROWS = 192
 
 
-def squares_kernel(place, wide_hbm, narrow_hbm, keep, send, wides, narrows, a_flat, b_flat, sems):
+HOT = (1, 2, 3, 5, 6, 7)
+COLD = (0, 4)
+
+
+def square_sums(wide, narrow):
+    return transposed_dot(wide, wide), transposed_dot(narrow, narrow)
+
+
+def pack_layer(place, i, wcov, ncov, a_flat, b_flat):
+    n = LANES
+    last = wcov[n:, n:]
+    a_flat[i, :n] = pack_pair(wcov[:n, :n], ncov)
+    a_flat[i, n:] = diagonals((ncov, last), EARLY_ROWS - n)
+    b_flat[i, :n] = wcov[:n, n:]
+    b_flat[i, n:] = fold(last)
+    a_kept, a_sent = both_halves(place, a_flat, i)
+    b_kept, b_sent = both_halves(place, b_flat, i)
+    return (a_kept, b_kept), (a_sent, b_sent)
+
+
+def put(ref, index, parts):
+    rows = EARLY_ROWS // 2
+    ref[*index, :rows] = parts[0]
+    ref[*index, rows:] = parts[1]
+
+
+def hot_kernel(place, wide_hbm, narrow_hbm, keep, send, wides, narrows, a_flat, b_flat, sems):
     copies = layer_copies(place, (wide_hbm, narrow_hbm), (wides, narrows), sems)
-    for group in copies[:AHEAD]:
-        for copy in group:
+    order = HOT + COLD
+    for i in order[:AHEAD]:
+        for copy in copies[i]:
             copy.start()
-    n = LANES
-    for i, group in enumerate(copies):
-        for copy in group:
+
+    def pack(i, sums):
+        kept, sent = pack_layer(place, i, *sums, a_flat, b_flat)
+        z, y, x = i // 4, (i // 2) % 2, i % 2
+        if x and y:
+            mine = other = 1
+        else:
+            mine, other = by_core(place, 0 if x else 2, 2 if x else 0)
+        put(keep, (mine, z), kept)
+        put(send, (other, z), sent)
+
+    before = None
+    for at, i in enumerate(order):
+        for copy in copies[i]:
             copy.wait()
-        if i + AHEAD < len(copies):
-            for copy in copies[i + AHEAD]:
+        if at + AHEAD < len(order):
+            for copy in copies[order[at + AHEAD]]:
                 copy.start()
-        wide = wides[i]
-        narrow = narrows[i]
-        wcov = transposed_dot(wide, wide)
-        ncov = transposed_dot(narrow, narrow)
-        last = wcov[n:, n:]
-        a_flat[i, :n] = pack_pair(wcov[:n, :n], ncov)
-        a_flat[i, n:] = diagonals((ncov, last), EARLY_ROWS - n)
-        write_halves(place, i, 0, a_flat, keep, send)
-        b_flat[i, :n] = wcov[:n, n:]
-        b_flat[i, n:] = fold(last)
-        write_halves(place, i, EARLY_ROWS // 2, b_flat, keep, send)
+        if before is not None:
+            pack(*before)
+            before = None
+        if i in HOT:
+            before = (i, square_sums(wides[i], narrows[i]))
+
+
+def cold_kernel(place, wides, narrows, keep, send, a_flat, b_flat):
+    for i in COLD:
+        sums = square_sums(wides[i], narrows[i])
+        kept, sent = pack_layer(place, i, *sums, a_flat, b_flat)
+        put(keep, (i // 4,), kept)
+        put(send, (i // 4,), sent)
 
 
 def mixed_kernel(place, wides, narrows, keep, send, flat):
@@ -163,7 +203,11 @@
         mixed = transposed_dot(narrows[i], wides[i])
         flat[i, :n] = mixed[:, :n]
         flat[i, n:] = mixed[:, n:]
-        write_halves(place, i, 0, flat, keep, send)
+        kept, sent = both_halves(place, flat, i)
+        z, y, x = i // 4, (i // 2) % 2, i % 2
+        mine, other = by_core(place, y * 2 + x, x * 2 + y)
+        keep[mine, z] = kept
+        send[other, z] = sent
 
 
 def gram_cost(wide_rows, columns):
@@ -172,11 +216,21 @@
     )
 
 
-def squares(place, wide_rows, narrow_rows):
+HALF_ROWS = (EARLY_ROWS + LATE_ROWS) // 2
+
+
+def pack_shapes(layers):
+    return [
+        pltpu.VMEM((layers, EARLY_ROWS, LANES), jnp.float32),
+        pltpu.VMEM((layers, LATE_ROWS, LANES), jnp.float32),
+    ]
+
+
+def hot_squares(place, wide_rows, narrow_rows):
     layers = wide_rows.shape[0]
-    half = jax.ShapeDtypeStruct((4, 2, (EARLY_ROWS + LATE_ROWS) // 2, LANES), jnp.float32)
+    half = jax.ShapeDtypeStruct((3, 2, HALF_ROWS, LANES), jnp.float32)
     return pl.pallas_call(
-        functools.partial(squares_kernel, place),
+        functools.partial(hot_kernel, place),
         in_specs=[HBM, HBM],
         out_specs=[VMEM] * 4,
         out_shape=[
@@ -185,18 +239,28 @@
             jax.ShapeDtypeStruct(wide_rows.shape, wide_rows.dtype),
             jax.ShapeDtypeStruct(narrow_rows.shape, narrow_rows.dtype),
         ],
-        scratch_shapes=[
-            pltpu.VMEM((layers, EARLY_ROWS, LANES), jnp.float32),
-            pltpu.VMEM((layers, LATE_ROWS, LANES), jnp.float32),
-            pltpu.SemaphoreType.DMA((layers, 2)),
-        ],
-        cost_estimate=gram_cost(wide_rows, 320),
+        scratch_shapes=[*pack_shapes(layers), pltpu.SemaphoreType.DMA((layers, 2))],
+        cost_estimate=gram_cost(wide_rows, 240),
         compiler_params=PARAMS,
-        name="squares",
+        name="hot_squares",
     )(
         pltpu.with_memory_space_constraint(wide_rows, pltpu.HBM),
         pltpu.with_memory_space_constraint(narrow_rows, pltpu.HBM),
     )
+
+
+def cold_squares(place, wides, narrows):
+    half = jax.ShapeDtypeStruct((2, HALF_ROWS, LANES), jnp.float32)
+    return pl.pallas_call(
+        functools.partial(cold_kernel, place),
+        in_specs=[VMEM, VMEM],
+        out_specs=[VMEM, VMEM],
+        out_shape=[half, half],
+        scratch_shapes=pack_shapes(wides.shape[0]),
+        cost_estimate=gram_cost(wides, 80),
+        compiler_params=PARAMS,
+        name="cold_squares",
+    )(wides, narrows)
 
 
 def mixed_sums(place, wides, narrows):
@@ -299,10 +363,9 @@
         value = following[:, LANES * t : LANES * (t + 1)]
         if t == tile:
             value = jnp.where(own, 0.0, value)
-        terms = [weights[k] * q[k][t] for k in range(PANEL)]
-        while len(terms) > 1:
-            terms = [terms[i] + terms[i + 1] for i in range(0, len(terms), 2)]
-        result.append(value - terms[0])
+        for k in range(PANEL):
+            value = value - weights[k] * q[k][t]
+        result.append(value)
     return jnp.concatenate(result, axis=1) if tiles > 1 else result[0]
 
 
@@ -318,27 +381,13 @@
     return pl.CostEstimate(flops=1 << 30, bytes_accessed=1 << 20, transcendentals=0)
 
 
-def load_damped(a_ref, block):
-    n = block.shape[0]
-    row, col = iotas(block.shape)
-    a_ref[:PANEL] = jnp.zeros((PANEL, n), jnp.float32)
-    a_ref[PANEL + n :] = jnp.zeros((PANEL, n), jnp.float32)
-    a_ref[PANEL : PANEL + n] = block + jnp.where(row == col, DAMP, 0.0)
-
-
-def sweep_all(works):
-    for _, left, right in works:
-        left[...] = jnp.zeros(left.shape, left.dtype)
-        right[...] = jnp.zeros(right.shape, right.dtype)
-
-    def step(i, panels):
-        return tuple(sweep_panel(*work, 0, i, panel) for work, panel in zip(works, panels))
-
-    size = works[0][0].shape[1]
-    lax.fori_loop(0, size // PANEL, step, tuple(a[PANEL : 2 * PANEL] for a, _, _ in works))
-    for work in works:
-        trailing_update(*work, size)
-    return [-a[PANEL : PANEL + size] for a, _, _ in works]
+def clear(work):
+    a_ref, left, right = work
+    size = a_ref.shape[1]
+    a_ref[:PANEL] = jnp.zeros((PANEL, size), jnp.float32)
+    a_ref[PANEL + size :] = jnp.zeros((PANEL, size), jnp.float32)
+    left[...] = jnp.zeros(left.shape, left.dtype)
+    right[...] = jnp.zeros(right.shape, right.dtype)
 
 
 def work_shapes(size):
@@ -375,66 +424,88 @@
     )
 
 
-def early_kernel(
-    place, total, mine, other, w11_ref, ninv_ref, corner_ref, last_ref, a_flat, b_flat, *works
-):
+STEPS = LANES // PANEL
+
+
+def first_half_kernel(place, total, mine, other, ninv_ref, wa, wl, wr, panel_ref, *refs):
+    a_flat, b_flat, na, nl, nr = refs
+    wide_work, narrow_work = (wa, wl, wr), (na, nl, nr)
     place_halves(place, (mine, other), 0, a_flat)
     place_halves(place, (mine, other), a_flat.shape[0] // 2, b_flat)
     n = LANES
     slab = a_flat[n : n + PANEL]
     first, square = unpack_pair(a_flat[:n], jnp.broadcast_to(slab[:1], (n, n)))
-    load_damped(works[0], first / total)
-    load_damped(works[3], square / total)
-    corner_ref[...] = b_flat[:n] / total
-    last_ref[...] = unfold(b_flat[n:], jnp.broadcast_to(slab[1:2], (n, n))) / total
-    w11_ref[...], ninv_ref[...] = sweep_all((works[:3], works[3:]))
-
-
-def early(place, pieces, total):
-    n = LANES
+    corner = b_flat[:n] / total
+    last = unfold(b_flat[n:], jnp.broadcast_to(slab[1:2], (n, n)))
+    row, col = iotas((n, n))
+    damp = jnp.where(row == col, DAMP, 0.0)
+    clear(wide_work)
+    clear(narrow_work)
+    wa[PANEL : PANEL + n, :n] = first / total + damp
+    wa[PANEL : PANEL + n, n:] = corner
+    wa[PANEL + n : PANEL + 2 * n, :n] = corner.T
+    wa[PANEL + n : PANEL + 2 * n, n:] = last / total + damp
+    na[PANEL : PANEL + n, :] = square / total + damp
+
+    def step(i, panels):
+        return (
+            sweep_panel(*wide_work, 0, i, panels[0]),
+            sweep_panel(*narrow_work, 0, i, panels[1]),
+        )
+
+    start = (wa[PANEL : 2 * PANEL, :], na[PANEL : 2 * PANEL, :])
+    panel_ref[...], _ = lax.fori_loop(0, STEPS, step, start)
+    trailing_update(*narrow_work, n)
+    ninv_ref[...] = -na[PANEL : PANEL + n, :]
+
+
+def first_half(place, pieces, wide, narrow, total):
+    matrix, left, right = work_shapes(wide)
+    shapes = [jax.ShapeDtypeStruct((narrow, narrow), jnp.float32)]
+    shapes += [jax.ShapeDtypeStruct(v.shape, v.dtype) for v in (matrix, left, right)]
+    shapes += [jax.ShapeDtypeStruct((PANEL, wide), jnp.float32)]
     return pl.pallas_call(
-        functools.partial(early_kernel, place, total),
+        functools.partial(first_half_kernel, place, total),
         in_specs=[VMEM] * 2,
-        out_specs=[VMEM] * 4,
-        out_shape=[jax.ShapeDtypeStruct((n, n), jnp.float32)] * 4,
+        out_specs=[VMEM] * 5,
+        out_shape=shapes,
         scratch_shapes=[
-            pltpu.VMEM((EARLY_ROWS, n), jnp.float32),
-            pltpu.VMEM((LATE_ROWS, n), jnp.float32),
-            *work_shapes(n),
-            *work_shapes(n),
+            pltpu.VMEM((EARLY_ROWS, LANES), jnp.float32),
+            pltpu.VMEM((LATE_ROWS, LANES), jnp.float32),
+            *work_shapes(narrow),
         ],
         cost_estimate=sweep_cost(),
         compiler_params=PARAMS,
-        name="early",
+        name="first_half",
     )(*pieces)
 
 
-def late_kernel(w11_ref, corner_ref, last_ref, winv, *work):
-    n = LANES
-    w11 = w11_ref[...]
-    corner = corner_ref[...]
-    solved = dot(w11, corner)
-    load_damped(work[0], last_ref[...] - transposed_dot(corner, solved, HIGHEST))
-    (sinv,) = sweep_all((work,))
-    cross = dot(solved, sinv)
-    winv[:n, :n] = w11 + dot(cross, solved, last=True)
-    winv[:n, n:] = -cross
-    winv[n:, :n] = -cross.T
-    winv[n:, n:] = sinv
-
-
-def late(w11, corner, last):
-    n = LANES
+def second_half_kernel(wa_in, wl_in, wr_in, panel_in, winv, wa, wl, wr):
+    wa[...] = wa_in[...]
+    wl[...] = wl_in[...]
+    wr[...] = wr_in[...]
+    wide = wa.shape[1]
+
+    def step(i, panel):
+        return sweep_panel(wa, wl, wr, 1, i, panel)
+
+    lax.fori_loop(0, STEPS, step, panel_in[...])
+    trailing_update(wa, wl, wr, wide)
+    winv[...] = -wa[PANEL : PANEL + wide, :]
+
+
+def second_half(state):
+    wide = state[0].shape[1]
     return pl.pallas_call(
-        late_kernel,
-        in_specs=[VMEM] * 3,
+        second_half_kernel,
+        in_specs=[VMEM] * 4,
         out_specs=VMEM,
-        out_shape=jax.ShapeDtypeStruct((2 * n, 2 * n), jnp.float32),
-        scratch_shapes=work_shapes(n),
+        out_shape=jax.ShapeDtypeStruct((wide, wide), jnp.float32),
+        scratch_shapes=work_shapes(wide),
         cost_estimate=sweep_cost(),
         compiler_params=PARAMS,
-        name="late",
-    )(w11, corner, last)
+        name="second_half",
+    )(*state)
 
 
 def product_kernel(place, total, rows, winv, ninv_ref, mine, other, out_ref, flat):
@@ -566,24 +637,27 @@
     n_dp, n_own = 2 ** len(place.dp), 2 ** len(place.own)
     total = float(rows * n_dp * n_own)
 
-    s_keep, s_send, wides, narrows = squares(place, wide_rows, narrow_rows)
-    s_got = swap(s_send, place.core)
-    m_keep, m_send = mixed_sums(place, after(wides, s_send), narrows)
-    s_keep, m_send = lax.optimization_barrier((s_keep, m_send))
-
-    s = s_keep + s_got
-    s_got = swap_by_core(s[2:], place, 0)
-    m_got = swap(after(m_send, s), place.core)
-
-    s = s[:2] + s_got
+    h_keep, h_send, wides, narrows = hot_squares(place, wide_rows, narrow_rows)
+    h_got = swap(h_send[:2], place.core)
+    c_keep, c_send = cold_squares(place, after(wides, h_send), narrows)
+    h_keep, c_send = lax.optimization_barrier((h_keep, c_send))
+
+    hot = h_keep[:2] + h_got
+    s_got = swap_by_core(hot, place, 0)
+    c_got = swap(after(jnp.stack([c_send, h_send[2]]), hot), place.core)
+    m_keep, m_send = mixed_sums(place, after(wides, hot), narrows)
+    m_got = swap(m_send, place.core)
+    s = jnp.stack([c_keep, h_keep[2]]) + after(c_got, m_send)
+
+    s = s + s_got
     s_got = swap_by_core(s[1], place, 1)
     m = after(m_keep, s) + m_got
-    m_got = swap_by_core(m[2:], place, 0)
+    m_got = swap_by_core(m[2:], place, 1)
 
     s = s[0] + s_got
     s_got = swap(s[1], place.near)
     m = after(m[:2], s) + m_got
-    m_got = swap_by_core(m[1], place, 1)
+    m_got = swap_by_core(m[1], place, 0)
 
     s = s[0] + s_got
     if place.extra:
@@ -599,10 +673,10 @@
     s_got = swap(after(s, m), place.core)
     m_got = swap(m, place.far)
 
-    w11, ninv, corner, last = early(place, [s, s_got], total)
-    m = after(m, w11) + m_got
+    ninv, *state = first_half(place, [s, s_got], wide, narrow, total)
+    m = after(m, ninv) + m_got
     m_got = swap(m, place.core)
-    winv = late(w11, corner, last)
+    winv = second_half(state)
     cols, own_rows = wide // n_dp, narrow // n_own
     sent = products(place, winv, ninv, [m, m_got], own_rows, total)
     got = lax.all_to_all(sent, (place.near, place.second, place.first), 0, 0)

time: 60.3 us -> 58.6 us (0.972)
  waiting for transfers between devices: 13.9 us -> 12 us
    ppermute x8 -> x9, waiting for transfers between devices: 5.32 us -> 3.2 us  [swap(): return lax.ppermute(value, axis, [(0, 1), (1, 0)])]
    ppermute x8 -> x9, starting transfers between devices: 9.19 us -> 11 us  [swap(): return lax.ppermute(value, axis, [(0, 1), (1, 0)])]
    ppermute x4, starting transfers between devices: 8.16 us -> 6.52 us  [swap_by_core(): return lax.ppermute(value, (place.second, place.core, place.first), pairs)]
    pallas_call x3 -> x4, Pallas kernels: 14.5 us -> 14 us  [the longest x1 5.59 us: first_half(): pl.pallas_call(functools.partial(first_half_kernel, place, total), in_spe...]
  transfers between devices with their start and end apart: 12 -> 13, of which waited for: 7 -> 7; matrix products, arithmetic and copies ran while one was open for 0% -> 1% of each run, Pallas kernels for 18% -> 19%
where the time goes in v10:
time: 58.6 us; the launch traced here: 58.4 us
  starting transfers between devices  17.5 us (30%)
  Pallas kernels  16.9 us (29%)
  waiting for transfers between devices  12 us (20%)
  blocking collectives  10.8 us (18%)
  between operations  0.8 us (1%)
    ppermute x9, starting transfers between devices, swap(): return lax.ppermute(value, axis, [(0, 1), (1, 0)])  11 us
    all_to_all x1, blocking collectives, on_device(): got = lax.all_to_all(sent, (place.near, place.second, place.first), 0, 0)  10.8 us
    ppermute x4, waiting for transfers between devices, swap_by_core(): return lax.ppermute(value, (place.second, place.core, place.first), pairs)  8.76 us
    ppermute x4, starting transfers between devices, swap_by_core(): return lax.ppermute(value, (place.second, place.core, place.first), pairs)  6.52 us
    pallas_call x1, Pallas kernels, first_half(): pl.pallas_call(functools.partial(first_half_kernel, place, total), in_spe...  5.59 us
    pallas_call x1, Pallas kernels, second_half(): pl.pallas_call(second_half_kernel, in_specs=[VMEM] * 4, out_specs=VMEM, o...  3.97 us
    pallas_call x1, Pallas kernels, hot_squares(): pl.pallas_call(functools.partial(hot_kernel, place), in_specs=[HBM, HBM],...  3.88 us
    ppermute x9, waiting for transfers between devices, swap(): return lax.ppermute(value, axis, [(0, 1), (1, 0)])  3.2 us
  transfers between devices with their start and end apart: 13, of which 7 were waited for; matrix products, arithmetic and copies ran while one was open for 1% of the time, Pallas kernels for 19%

profile of v10, /device:TPU:0, one launch (start us, length us, event | category | flops | bytes accessed | tf_op | source)
XLA Modules:
  0.0 58.4 jit_solution(2240903015144123640)
XLA Ops:
  0.6 3.9 %hot_squares.1 = (f32[3,2,168,128]{3,2,1,0:T(8,128)S(1)}, f32[3,2,168,128]{3,2,1,0:T(8,128)S(1)}, bf16[8,768,256]{2,1,0:T(8,128)(2,1)S(1)}, bf16[8,768,128]{2,1,0:T(8,128)(2,1)S(1)}) custom-call(bf16[8,768,256]{2,1,0:T(8,128)(2,1)} %wide_hbm.1, bf16[8,768,128]{2,1,0:T(8,128)(2,1)} %narrow_hbm.1), custom_call_target="tpu_custom_call" | custom-call | flops 754974720 | bytes 3145728 | tf_op jit(solution)/shard_map/hot_squares/pallas_call | solution.py:232
  4.6 0.5 collective-permute-start
  5.1 0.6 %cold_squares.1 = (f32[2,168,128]{2,1,0:T(8,128)S(1)}, f32[2,168,128]{2,1,0:T(8,128)S(1)}) custom-call(bf16[8,768,256]{2,1,0:T(8,128)(2,1)S(1)} %get-tuple-element.39.wides, bf16[8,768,128]{2,1,0:T(8,128)(2,1)S(1)} %get-tuple-element.32.narrows), custom_call_target="tpu_custom_call" | custom-call | flops 251658240 | bytes 3145728 | tf_op jit(solution)/shard_map/cold_squares/pallas_call | solution.py:254
  5.7 0.6 %collective-permute-done = f32[2,2,168,128]{3,2,1,0:T(8,128)S(1)} collective-permute-done((f32[2,2,168,128]{3,2,1,0:T(8,128)S(1)}, f32[2,2,168,128]{3,2,1,0:T(8,128)S(1)}, u32[]{:S(2)}, u32[]{:S(2)}) %collective-permute-start) | collective-permute-done | bytes 344096 | tf_op jit(solution)/shard_map/ppermute | solution.py:616
  6.4 0.4 collective-permute-start.1
  6.8 2.6 %collective-permute-start.2 = (f32[2,2,168,128]{3,2,1,0:T(8,128)S(1)}, f32[2,2,168,128]{3,2,1,0:T(8,128)S(1)}, u32[]{:S(2)}, u32[]{:S(2)}) collective-permute-start(f32[2,2,168,128]{3,2,1,0:T(8,128)S(1)} %slice_add_fusion), channel_id=1, source_target_pairs={{0,1},{1,0},{2,6},{3,7},{4,5},{5,4},{6,2},{7,3},{8,9},{9,8},{10,14... | collective-permute-start | bytes 1032200 | tf_op jit(solution)/shard_map/ppermute | solution.py:627
  9.5 0.9 %mixed.1 = (f32[4,2,128,128]{3,2,1,0:T(8,128)S(1)}, f32[4,2,128,128]{3,2,1,0:T(8,128)S(1)}) custom-call(bf16[8,768,256]{2,1,0:T(8,128)(2,1)S(1)} %get-tuple-element.39.wides, bf16[8,768,128]{2,1,0:T(8,128)(2,1)S(1)} %get-tuple-element.32.narrows), custom_call_target="tpu_custom_call" | custom-call | flops 402653184 | bytes 3145728 | tf_op jit(solution)/shard_map/mixed/pallas_call | solution.py:269
  10.6 4.1 %collective-permute-done.2 = f32[2,2,168,128]{3,2,1,0:T(8,128)S(1)} collective-permute-done((f32[2,2,168,128]{3,2,1,0:T(8,128)S(1)}, f32[2,2,168,128]{3,2,1,0:T(8,128)S(1)}, u32[]{:S(2)}, u32[]{:S(2)}) %collective-permute-start.2) | collective-permute-done | bytes 344096 | tf_op jit(solution)/shard_map/ppermute | solution.py:627
  14.8 2.1 %collective-permute-start.3 = (f32[2,168,128]{2,1,0:T(8,128)S(1)}, f32[2,168,128]{2,1,0:T(8,128)S(1)}, u32[]{:S(2)}, u32[]{:S(2)}) collective-permute-start(f32[2,168,128]{2,1,0:T(8,128)S(1)} %slice_bitcast_fusion), channel_id=1, source_target_pairs={{0,4},{1,5},{2,3},{3,2},{4,0},{5,1},{6,7},{7,6},{8,12},{9,13},{10,... | collective-permute-start | bytes 516104 | tf_op jit(solution)/shard_map/ppermute | solution.py:627
  17.1 3.2 %collective-permute-done.3 = f32[2,168,128]{2,1,0:T(8,128)S(1)} collective-permute-done((f32[2,168,128]{2,1,0:T(8,128)S(1)}, f32[2,168,128]{2,1,0:T(8,128)S(1)}, u32[]{:S(2)}, u32[]{:S(2)}) %collective-permute-start.3) | collective-permute-done | bytes 172064 | tf_op jit(solution)/shard_map/ppermute | solution.py:627
  20.3 2.1 %collective-permute-start.4 = (f32[168,128]{1,0:T(8,128)S(1)}, f32[168,128]{1,0:T(8,128)S(1)}, u32[]{:S(2)}, u32[]{:S(2)}) collective-permute-start(f32[168,128]{1,0:T(8,128)S(1)} %slice_bitcast_fusion.4), channel_id=1, source_target_pairs={{0,8},{8,0},{1,9},{9,1},{2,10},{10,2},{3,11},{11,3},{4,12},{12,4},... | collective-permute-start | bytes 258056 | tf_op jit(solution)/shard_map/ppermute | solution.py:616
  22.5 1.0 %collective-permute-done.7 = f32[2,2,128,128]{3,2,1,0:T(8,128)S(1)} collective-permute-done((f32[2,2,128,128]{3,2,1,0:T(8,128)S(1)}, f32[2,2,128,128]{3,2,1,0:T(8,128)S(1)}, u32[]{:S(2)}, u32[]{:S(2)}) %collective-permute-start.7) | collective-permute-done | bytes 262176 | tf_op jit(solution)/shard_map/ppermute | solution.py:627
  23.5 1.7 %collective-permute-start.8 = (f32[2,128,128]{2,1,0:T(8,128)S(1)}, f32[2,128,128]{2,1,0:T(8,128)S(1)}, u32[]{:S(2)}, u32[]{:S(2)}) collective-permute-start(f32[2,128,128]{2,1,0:T(8,128)S(1)} %get-tuple-element.58), channel_id=1, source_target_pairs={{0,1},{1,0},{2,6},{3,7},{4,5},{5,4},{6,2},{7,3},{8,9},{9,8},{10,14... | collective-permute-start | bytes 393224 | tf_op jit(solution)/shard_map/ppermute | solution.py:627
  25.2 2.8 %collective-permute-start.5 = (f32[168,128]{1,0:T(8,128)S(1)}, f32[168,128]{1,0:T(8,128)S(1)}, u32[]{:S(2)}, u32[]{:S(2)}) collective-permute-start(f32[168,128]{1,0:T(8,128)S(1)} %fusion.2), channel_id=1, source_target_pairs={{0,16},{16,0},{1,17},{17,1},{2,18},{18,2},{3,19},{19,3},{4,20},{20... | collective-permute-start | bytes 258056 | tf_op jit(solution)/shard_map/ppermute | solution.py:616
  28.0 0.5 collective-permute-done.8
  28.6 1.8 %collective-permute-start.9 = (f32[128,128]{1,0:T(8,128)S(1)}, f32[128,128]{1,0:T(8,128)S(1)}, u32[]{:S(2)}, u32[]{:S(2)}) collective-permute-start(f32[128,128]{1,0:T(8,128)S(1)} %get-tuple-element.60), channel_id=1, source_target_pairs={{0,8},{8,0},{1,9},{9,1},{2,10},{10,2},{3,11},{11,3},{4,12},{12,4},... | collective-permute-start | bytes 196616 | tf_op jit(solution)/shard_map/ppermute | solution.py:616
  30.4 0.3 collective-permute-done.5
  30.7 2.2 %collective-permute-done.9 = f32[128,128]{1,0:T(8,128)S(1)} collective-permute-done((f32[128,128]{1,0:T(8,128)S(1)}, f32[128,128]{1,0:T(8,128)S(1)}, u32[]{:S(2)}, u32[]{:S(2)}) %collective-permute-start.9) | collective-permute-done | bytes 65568 | tf_op jit(solution)/shard_map/ppermute | solution.py:616
  33.0 2.8 %collective-permute-start.11 = (f32[128,128]{1,0:T(8,128)S(1)}, f32[128,128]{1,0:T(8,128)S(1)}, u32[]{:S(2)}, u32[]{:S(2)}) collective-permute-start(f32[128,128]{1,0:T(8,128)S(1)} %add.42), channel_id=1, source_target_pairs={{0,16},{16,0},{1,17},{17,1},{2,18},{18,2},{3,19},{19,3},{4,20},{20... | collective-permute-start | bytes 196616 | tf_op jit(solution)/shard_map/ppermute | solution.py:616
  35.8 5.6 %first_half.1 = (f32[128,128]{1,0:T(8,128)S(1)}, f32[272,256]{1,0:T(8,128)S(1)}, bf16[48,256]{1,0:T(8,128)(2,1)S(1)}, bf16[48,256]{1,0:T(8,128)(2,1)S(1)}, f32[8,256]{1,0:T(8,128)S(1)}) custom-call(f32[168,128]{1,0:T(8,128)S(1)} %add.38.mine, f32[168,128]{1,0:T(8,128)S(1)} %collective-permute-done.10.other), custom_call_target="tpu_custom_call" | custom-call | flops 1073741824 | bytes 1048576 | tf_op jit(solution)/shard_map/first_half/pallas_call | solution.py:467
  41.7 4.0 %second_half.1.winv = f32[256,256]{1,0:T(8,128)S(1)} custom-call(f32[272,256]{1,0:T(8,128)S(1)} %get-tuple-element.48.wa_in, bf16[48,256]{1,0:T(8,128)(2,1)S(1)} %get-tuple-element.49.wl_in, bf16[48,256]{1,0:T(8,128)(2,1)S(1)} %get-tuple-element.50.wr_in, f32[8,256]{1,0:T(8,128)S(1)} %get-tuple-element.51.panel_in), custom_call_target="tpu_custom_call" | custom-call | flops 1073741824 | bytes 1048576 | tf_op jit(solution)/shard_map/second_half/pallas_call | solution.py:499
  45.7 0.7 %products.1 = f32[8,40,128]{2,1,0:T(8,128)S(1)} custom-call(f32[256,256]{1,0:T(8,128)S(1)} %second_half.1.winv, f32[128,128]{1,0:T(8,128)S(1)} %get-tuple-element.52.ninv_ref, f32[128,128]{1,0:T(8,128)S(1)} %add.43.mine, f32[128,128]{1,0:T(8,128)S(1)} %collective-permute-done.12.other), custom_call_target="tpu_custom_call" | custom-call | tf_op jit(solution)/shard_map/products/pallas_call | solution.py:557
  46.4 10.8 %all_to_all.5.got_ref = f32[8,40,128]{2,1,0:T(8,128)S(1)} all-to-all(f32[8,40,128]{2,1,0:T(8,128)S(1)} %products.1), channel_id=1, replica_groups=mesh['dp0'=2,'dp1'=2,'dp2'=2,'dp3'=2,'own0'=2] {'dp1','dp2','own0'}, dimensions={0} | all-to-all | bytes 327680 | tf_op jit(solution)/shard_map/all_to_all | solution.py:682
  57.2 1.3 %placing.1 = (f32[5,16,256]{2,1,0:T(8,128)}, f32[8,16,64]{2,1,0:T(8,128)}) custom-call(s32[8]{0:T(128)S(1)} %copy-done, f32[8,40,128]{2,1,0:T(8,128)S(1)} %all_to_all.5.got_ref), custom_call_target="tpu_custom_call" | custom-call | tf_op jit(solution)/shard_map/placing/pallas_call | solution.py:602
  (31 shorter events, 1.1 us)
Async XLA Ops:
  4.6 1.8 %collective-permute-start = (f32[2,2,168,128]{3,2,1,0:T(8,128)S(1)}, f32[2,2,168,128]{3,2,1,0:T(8,128)S(1)}, u32[]{:S(2)}, u32[]{:S(2)}) collective-permute-start(f32[2,2,168,128]{3,2,1,0:T(8,128)S(1)} %slice.45), channel_id=1, source_target_pairs={{0,2},{2,0},{1,3},{3,1},{4,6},{6,4},{5,7},{7,5},{8,10},{10,8},{9,1... | collective-permute-start | bytes 1032200 | tf_op jit(solution)/shard_map/ppermute | solution.py:616
  6.4 4.2 %collective-permute-start.1 = (f32[2,2,168,128]{3,2,1,0:T(8,128)S(1)}, f32[2,2,168,128]{3,2,1,0:T(8,128)S(1)}, u32[]{:S(2)}, u32[]{:S(2)}) collective-permute-start(f32[2,2,168,128]{3,2,1,0:T(8,128)S(1)} %pad_maximum_fusion), channel_id=1, source_target_pairs={{0,2},{2,0},{1,3},{3,1},{4,6},{6,4},{5,7},{7,5},{8,10},{10,8},{9,1... | collective-permute-start | bytes 1032200 | tf_op jit(solution)/shard_map/ppermute | solution.py:616
  6.8 7.8 %collective-permute-start.2 = (f32[2,2,168,128]{3,2,1,0:T(8,128)S(1)}, f32[2,2,168,128]{3,2,1,0:T(8,128)S(1)}, u32[]{:S(2)}, u32[]{:S(2)}) collective-permute-start(f32[2,2,168,128]{3,2,1,0:T(8,128)S(1)} %slice_add_fusion), channel_id=1, source_target_pairs={{0,1},{1,0},{2,6},{3,7},{4,5},{5,4},{6,2},{7,3},{8,9},{9,8},{10,14... | collective-permute-start | bytes 1032200 | tf_op jit(solution)/shard_map/ppermute | solution.py:627
  10.4 6.5 %collective-permute-start.6 = (f32[4,2,128,128]{3,2,1,0:T(8,128)S(1)}, f32[4,2,128,128]{3,2,1,0:T(8,128)S(1)}, u32[]{:S(2)}, u32[]{:S(2)}) collective-permute-start(f32[4,2,128,128]{3,2,1,0:T(8,128)S(1)} %get-tuple-element.40), channel_id=1, source_target_pairs={{0,2},{2,0},{1,3},{3,1},{4,6},{6,4},{5,7},{7,5},{8,10},{10,8},{9,1... | collective-permute-start | bytes 1572872 | tf_op jit(solution)/shard_map/ppermute | solution.py:616
  14.8 5.5 %collective-permute-start.3 = (f32[2,168,128]{2,1,0:T(8,128)S(1)}, f32[2,168,128]{2,1,0:T(8,128)S(1)}, u32[]{:S(2)}, u32[]{:S(2)}) collective-permute-start(f32[2,168,128]{2,1,0:T(8,128)S(1)} %slice_bitcast_fusion), channel_id=1, source_target_pairs={{0,4},{1,5},{2,3},{3,2},{4,0},{5,1},{6,7},{7,6},{8,12},{9,13},{10,... | collective-permute-start | bytes 516104 | tf_op jit(solution)/shard_map/ppermute | solution.py:627
  17.0 6.4 %collective-permute-start.7 = (f32[2,2,128,128]{3,2,1,0:T(8,128)S(1)}, f32[2,2,128,128]{3,2,1,0:T(8,128)S(1)}, u32[]{:S(2)}, u32[]{:S(2)}) collective-permute-start(f32[2,2,128,128]{3,2,1,0:T(8,128)S(1)} %get-tuple-element.56), channel_id=1, source_target_pairs={{0,4},{1,5},{2,3},{3,2},{4,0},{5,1},{6,7},{7,6},{8,12},{9,13},{10,... | collective-permute-start | bytes 786440 | tf_op jit(solution)/shard_map/ppermute | solution.py:627
  20.3 4.9 %collective-permute-start.4 = (f32[168,128]{1,0:T(8,128)S(1)}, f32[168,128]{1,0:T(8,128)S(1)}, u32[]{:S(2)}, u32[]{:S(2)}) collective-permute-start(f32[168,128]{1,0:T(8,128)S(1)} %slice_bitcast_fusion.4), channel_id=1, source_target_pairs={{0,8},{8,0},{1,9},{9,1},{2,10},{10,2},{3,11},{11,3},{4,12},{12,4},... | collective-permute-start | bytes 258056 | tf_op jit(solution)/shard_map/ppermute | solution.py:616
  23.5 5.0 %collective-permute-start.8 = (f32[2,128,128]{2,1,0:T(8,128)S(1)}, f32[2,128,128]{2,1,0:T(8,128)S(1)}, u32[]{:S(2)}, u32[]{:S(2)}) collective-permute-start(f32[2,128,128]{2,1,0:T(8,128)S(1)} %get-tuple-element.58), channel_id=1, source_target_pairs={{0,1},{1,0},{2,6},{3,7},{4,5},{5,4},{6,2},{7,3},{8,9},{9,8},{10,14... | collective-permute-start | bytes 393224 | tf_op jit(solution)/shard_map/ppermute | solution.py:627
  25.2 5.4 %collective-permute-start.5 = (f32[168,128]{1,0:T(8,128)S(1)}, f32[168,128]{1,0:T(8,128)S(1)}, u32[]{:S(2)}, u32[]{:S(2)}) collective-permute-start(f32[168,128]{1,0:T(8,128)S(1)} %fusion.2), channel_id=1, source_target_pairs={{0,16},{16,0},{1,17},{17,1},{2,18},{18,2},{3,19},{19,3},{4,20},{20... | collective-permute-start | bytes 258056 | tf_op jit(solution)/shard_map/ppermute | solution.py:616
  28.6 4.3 %collective-permute-start.9 = (f32[128,128]{1,0:T(8,128)S(1)}, f32[128,128]{1,0:T(8,128)S(1)}, u32[]{:S(2)}, u32[]{:S(2)}) collective-permute-start(f32[128,128]{1,0:T(8,128)S(1)} %get-tuple-element.60), channel_id=1, source_target_pairs={{0,8},{8,0},{1,9},{9,1},{2,10},{10,2},{3,11},{11,3},{4,12},{12,4},... | collective-permute-start | bytes 196616 | tf_op jit(solution)/shard_map/ppermute | solution.py:616
  32.9 2.9 %collective-permute-start.10 = (f32[168,128]{1,0:T(8,128)S(1)}, f32[168,128]{1,0:T(8,128)S(1)}, u32[]{:S(2)}, u32[]{:S(2)}) collective-permute-start(f32[168,128]{1,0:T(8,128)S(1)} %add.38.mine), channel_id=1, source_target_pairs={{0,2},{2,0},{1,3},{3,1},{4,6},{6,4},{5,7},{7,5},{8,10},{10,8},{9,1... | collective-permute-start | bytes 258056 | tf_op jit(solution)/shard_map/ppermute | solution.py:616
  33.0 8.4 %collective-permute-start.11 = (f32[128,128]{1,0:T(8,128)S(1)}, f32[128,128]{1,0:T(8,128)S(1)}, u32[]{:S(2)}, u32[]{:S(2)}) collective-permute-start(f32[128,128]{1,0:T(8,128)S(1)} %add.42), channel_id=1, source_target_pairs={{0,16},{16,0},{1,17},{17,1},{2,18},{18,2},{3,19},{19,3},{4,20},{20... | collective-permute-start | bytes 196616 | tf_op jit(solution)/shard_map/ppermute | solution.py:616
  41.4 15.7 %copy-start = (s32[8]{0:T(128)S(1)}, s32[8]{0:T(128)}, u32[]{:S(2)}) copy-start(s32[8]{0:T(128)} %owner_map.1) | copy-start | bytes 100
  41.5 4.2 %collective-permute-start.12 = (f32[128,128]{1,0:T(8,128)S(1)}, f32[128,128]{1,0:T(8,128)S(1)}, u32[]{:S(2)}, u32[]{:S(2)}) collective-permute-start(f32[128,128]{1,0:T(8,128)S(1)} %add.43.mine), channel_id=1, source_target_pairs={{0,2},{2,0},{1,3},{3,1},{4,6},{6,4},{5,7},{7,5},{8,10},{10,8},{9,1... | collective-permute-start | bytes 196616 | tf_op jit(solution)/shard_map/ppermute | solution.py:616

commit v11 on v10

--- a/solution.py
+++ b/solution.py
@@ -48,7 +48,7 @@
     )
 
 
-AHEAD = 3
+AHEAD = 8
 
 
 def layer_copies(place, sources, buffers, sems):
@@ -425,10 +425,25 @@
 
 
 STEPS = LANES // PANEL
-
-
-def first_half_kernel(place, total, mine, other, ninv_ref, wa, wl, wr, panel_ref, *refs):
-    a_flat, b_flat, na, nl, nr = refs
+FIRST_STEPS = 10
+SECOND_STEPS = 10
+
+
+def sweep_both(wide_work, narrow_work, begin, end, panels):
+    def step(i, panels):
+        return (
+            sweep_panel(*wide_work, 0, i, panels[0]),
+            sweep_panel(*narrow_work, 0, i, panels[1]),
+        )
+
+    return lax.fori_loop(begin, end, step, panels)
+
+
+def sweep_wide(work, begin, end, panel):
+    return lax.fori_loop(begin, end, lambda i, panel: sweep_panel(*work, 1, i, panel), panel)
+
+
+def first_kernel(place, total, mine, other, wa, wl, wr, wp, na, nl, nr, np_, a_flat, b_flat):
     wide_work, narrow_work = (wa, wl, wr), (na, nl, nr)
     place_halves(place, (mine, other), 0, a_flat)
     place_halves(place, (mine, other), a_flat.shape[0] // 2, b_flat)
@@ -446,66 +461,78 @@
     wa[PANEL + n : PANEL + 2 * n, :n] = corner.T
     wa[PANEL + n : PANEL + 2 * n, n:] = last / total + damp
     na[PANEL : PANEL + n, :] = square / total + damp
-
-    def step(i, panels):
-        return (
-            sweep_panel(*wide_work, 0, i, panels[0]),
-            sweep_panel(*narrow_work, 0, i, panels[1]),
-        )
-
     start = (wa[PANEL : 2 * PANEL, :], na[PANEL : 2 * PANEL, :])
-    panel_ref[...], _ = lax.fori_loop(0, STEPS, step, start)
-    trailing_update(*narrow_work, n)
-    ninv_ref[...] = -na[PANEL : PANEL + n, :]
-
-
-def first_half(place, pieces, wide, narrow, total):
-    matrix, left, right = work_shapes(wide)
-    shapes = [jax.ShapeDtypeStruct((narrow, narrow), jnp.float32)]
-    shapes += [jax.ShapeDtypeStruct(v.shape, v.dtype) for v in (matrix, left, right)]
-    shapes += [jax.ShapeDtypeStruct((PANEL, wide), jnp.float32)]
-    return pl.pallas_call(
-        functools.partial(first_half_kernel, place, total),
-        in_specs=[VMEM] * 2,
-        out_specs=[VMEM] * 5,
-        out_shape=shapes,
-        scratch_shapes=[
-            pltpu.VMEM((EARLY_ROWS, LANES), jnp.float32),
-            pltpu.VMEM((LATE_ROWS, LANES), jnp.float32),
-            *work_shapes(narrow),
-        ],
-        cost_estimate=sweep_cost(),
-        compiler_params=PARAMS,
-        name="first_half",
-    )(*pieces)
-
-
-def second_half_kernel(wa_in, wl_in, wr_in, panel_in, winv, wa, wl, wr):
+    wp[...], np_[...] = sweep_both(wide_work, narrow_work, 0, FIRST_STEPS, start)
+
+
+def second_kernel(*refs):
+    given, ninv_ref, state, narrow_work = refs[:8], refs[8], refs[9:13], refs[13:]
+    wide_work, wp = state[:3], state[3]
+    for source, target in zip(given, (*wide_work, None, *narrow_work)):
+        if target is not None:
+            target[...] = source[...]
+    panels = (given[3][...], given[7][...])
+    panel, _ = sweep_both(wide_work, narrow_work, FIRST_STEPS, STEPS, panels)
+    trailing_update(*narrow_work, LANES)
+    ninv_ref[...] = -narrow_work[0][PANEL : PANEL + LANES, :]
+    wp[...] = sweep_wide(wide_work, 0, SECOND_STEPS, panel)
+
+
+def third_kernel(wa_in, wl_in, wr_in, panel_in, winv, wa, wl, wr):
     wa[...] = wa_in[...]
     wl[...] = wl_in[...]
     wr[...] = wr_in[...]
+    sweep_wide((wa, wl, wr), SECOND_STEPS, STEPS, panel_in[...])
     wide = wa.shape[1]
-
-    def step(i, panel):
-        return sweep_panel(wa, wl, wr, 1, i, panel)
-
-    lax.fori_loop(0, STEPS, step, panel_in[...])
     trailing_update(wa, wl, wr, wide)
     winv[...] = -wa[PANEL : PANEL + wide, :]
 
 
-def second_half(state):
-    wide = state[0].shape[1]
+def state_shapes(size):
+    shapes = [jax.ShapeDtypeStruct(v.shape, v.dtype) for v in work_shapes(size)]
+    return shapes + [jax.ShapeDtypeStruct((PANEL, size), jnp.float32)]
+
+
+def sweep_call(kernel, name, args, out_shapes, scratch):
     return pl.pallas_call(
-        second_half_kernel,
-        in_specs=[VMEM] * 4,
-        out_specs=VMEM,
-        out_shape=jax.ShapeDtypeStruct((wide, wide), jnp.float32),
-        scratch_shapes=work_shapes(wide),
+        kernel,
+        in_specs=[VMEM] * len(args),
+        out_specs=[VMEM] * len(out_shapes),
+        out_shape=out_shapes,
+        scratch_shapes=scratch,
         cost_estimate=sweep_cost(),
         compiler_params=PARAMS,
-        name="second_half",
-    )(*state)
+        name=name,
+    )(*args)
+
+
+def first_panels(place, pieces, wide, narrow, total):
+    return sweep_call(
+        functools.partial(first_kernel, place, total),
+        "first_panels",
+        pieces,
+        state_shapes(wide) + state_shapes(narrow),
+        [
+            pltpu.VMEM((EARLY_ROWS, LANES), jnp.float32),
+            pltpu.VMEM((LATE_ROWS, LANES), jnp.float32),
+        ],
+    )
+
+
+def second_panels(state, wide, narrow):
+    ninv = jax.ShapeDtypeStruct((narrow, narrow), jnp.float32)
+    return sweep_call(
+        second_kernel,
+        "second_panels",
+        state,
+        [ninv] + state_shapes(wide),
+        work_shapes(narrow),
+    )
+
+
+def third_panels(state, wide):
+    winv = jax.ShapeDtypeStruct((wide, wide), jnp.float32)
+    return sweep_call(third_kernel, "third_panels", state, [winv], work_shapes(wide))[0]
 
 
 def product_kernel(place, total, rows, winv, ninv_ref, mine, other, out_ref, flat):
@@ -667,16 +694,15 @@
     m_got = swap(m[1], place.near)
 
     s = s + s_got
-    m = after(m[0], s) + m_got
+    state = first_panels(place, [s, swap(s, place.core)], wide, narrow, total)
+    m = after(m[0], state[0]) + m_got
     if place.extra:
         m = lax.psum(m, place.extra)
-    s_got = swap(after(s, m), place.core)
     m_got = swap(m, place.far)
-
-    ninv, *state = first_half(place, [s, s_got], wide, narrow, total)
+    ninv, *state = second_panels(state, wide, narrow)
     m = after(m, ninv) + m_got
     m_got = swap(m, place.core)
-    winv = second_half(state)
+    winv = third_panels(state, wide)
     cols, own_rows = wide // n_dp, narrow // n_own
     sent = products(place, winv, ninv, [m, m_got], own_rows, total)
     got = lax.all_to_all(sent, (place.near, place.second, place.first), 0, 0)

time: 58.6 us -> 58.2 us (level)
    pallas_call x2 -> x3, Pallas kernels: 9.56 us -> 9.6 us  [sweep_call(): pl.pallas_call(kernel, in_specs=[VMEM] * len(args), out_specs=[VMEM] * le...]
  transfers between devices with their start and end apart: 13 -> 13, of which waited for: 7 -> 5; matrix products, arithmetic and copies ran while one was open for 1% -> 1% of each run, Pallas kernels for 19% -> 19%
where the time goes in v11:
time: 58.2 us; the launch traced here: 58.1 us
  starting transfers between devices  18 us (31%)
  Pallas kernels  16.7 us (29%)
  waiting for transfers between devices  11.6 us (20%)
  blocking collectives  10.5 us (18%)
  between operations  0.84 us (1%)
    ppermute x9, starting transfers between devices, swap(): return lax.ppermute(value, axis, [(0, 1), (1, 0)])  11.5 us
    all_to_all x1, blocking collectives, on_device(): got = lax.all_to_all(sent, (place.near, place.second, place.first), 0, 0)  10.5 us
    pallas_call x3, Pallas kernels, sweep_call(): pl.pallas_call(kernel, in_specs=[VMEM] * len(args), out_specs=[VMEM] * le...  9.6 us
    ppermute x4, waiting for transfers between devices, swap_by_core(): return lax.ppermute(value, (place.second, place.core, place.first), pairs)  8.26 us
    ppermute x4, starting transfers between devices, swap_by_core(): return lax.ppermute(value, (place.second, place.core, place.first), pairs)  6.51 us
    pallas_call x1, Pallas kernels, hot_squares(): pl.pallas_call(functools.partial(hot_kernel, place), in_specs=[HBM, HBM],...  3.62 us
    ppermute x9, waiting for transfers between devices, swap(): return lax.ppermute(value, axis, [(0, 1), (1, 0)])  3.31 us
    pallas_call x1, Pallas kernels, placing(): pl.pallas_call(functools.partial(placing_kernel, place), in_specs=[SMEM,...  1.26 us
  transfers between devices with their start and end apart: 13, of which 5 were waited for; matrix products, arithmetic and copies ran while one was open for 1% of the time, Pallas kernels for 19%

profile of v11, /device:TPU:0, one launch (start us, length us, event | category | flops | bytes accessed | tf_op | source)
XLA Modules:
  0.0 58.1 jit_solution(15520708053659338171)
XLA Ops:
  0.6 3.6 %hot_squares.1 = (f32[3,2,168,128]{3,2,1,0:T(8,128)S(1)}, f32[3,2,168,128]{3,2,1,0:T(8,128)S(1)}, bf16[8,768,256]{2,1,0:T(8,128)(2,1)S(1)}, bf16[8,768,128]{2,1,0:T(8,128)(2,1)S(1)}) custom-call(bf16[8,768,256]{2,1,0:T(8,128)(2,1)} %wide_hbm.1, bf16[8,768,128]{2,1,0:T(8,128)(2,1)} %narrow_hbm.1), custom_call_target="tpu_custom_call" | custom-call | flops 754974720 | bytes 3145728 | tf_op jit(solution)/shard_map/hot_squares/pallas_call | solution.py:232
  4.3 0.5 collective-permute-start
  4.8 0.6 %cold_squares.1 = (f32[2,168,128]{2,1,0:T(8,128)S(1)}, f32[2,168,128]{2,1,0:T(8,128)S(1)}) custom-call(bf16[8,768,256]{2,1,0:T(8,128)(2,1)S(1)} %get-tuple-element.46.wides, bf16[8,768,128]{2,1,0:T(8,128)(2,1)S(1)} %get-tuple-element.39.narrows), custom_call_target="tpu_custom_call" | custom-call | flops 251658240 | bytes 3145728 | tf_op jit(solution)/shard_map/cold_squares/pallas_call | solution.py:254
  5.4 0.6 %collective-permute-done = f32[2,2,168,128]{3,2,1,0:T(8,128)S(1)} collective-permute-done((f32[2,2,168,128]{3,2,1,0:T(8,128)S(1)}, f32[2,2,168,128]{3,2,1,0:T(8,128)S(1)}, u32[]{:S(2)}, u32[]{:S(2)}) %collective-permute-start) | collective-permute-done | bytes 344096 | tf_op jit(solution)/shard_map/ppermute | solution.py:643
  6.2 0.4 collective-permute-start.1
  6.6 2.6 %collective-permute-start.2 = (f32[2,2,168,128]{3,2,1,0:T(8,128)S(1)}, f32[2,2,168,128]{3,2,1,0:T(8,128)S(1)}, u32[]{:S(2)}, u32[]{:S(2)}) collective-permute-start(f32[2,2,168,128]{3,2,1,0:T(8,128)S(1)} %slice_add_fusion), channel_id=1, source_target_pairs={{0,1},{1,0},{2,6},{3,7},{4,5},{5,4},{6,2},{7,3},{8,9},{9,8},{10,14... | collective-permute-start | bytes 1032200 | tf_op jit(solution)/shard_map/ppermute | solution.py:654
  9.2 0.9 %mixed.1 = (f32[4,2,128,128]{3,2,1,0:T(8,128)S(1)}, f32[4,2,128,128]{3,2,1,0:T(8,128)S(1)}) custom-call(bf16[8,768,256]{2,1,0:T(8,128)(2,1)S(1)} %get-tuple-element.46.wides, bf16[8,768,128]{2,1,0:T(8,128)(2,1)S(1)} %get-tuple-element.39.narrows), custom_call_target="tpu_custom_call" | custom-call | flops 402653184 | bytes 3145728 | tf_op jit(solution)/shard_map/mixed/pallas_call | solution.py:269
  10.1 0.2 collective-permute-start.7
  10.3 4.1 %collective-permute-done.2 = f32[2,2,168,128]{3,2,1,0:T(8,128)S(1)} collective-permute-done((f32[2,2,168,128]{3,2,1,0:T(8,128)S(1)}, f32[2,2,168,128]{3,2,1,0:T(8,128)S(1)}, u32[]{:S(2)}, u32[]{:S(2)}) %collective-permute-start.2) | collective-permute-done | bytes 344096 | tf_op jit(solution)/shard_map/ppermute | solution.py:654
  14.5 2.1 %collective-permute-start.3 = (f32[2,168,128]{2,1,0:T(8,128)S(1)}, f32[2,168,128]{2,1,0:T(8,128)S(1)}, u32[]{:S(2)}, u32[]{:S(2)}) collective-permute-start(f32[2,168,128]{2,1,0:T(8,128)S(1)} %slice_bitcast_fusion), channel_id=1, source_target_pairs={{0,4},{1,5},{2,3},{3,2},{4,0},{5,1},{6,7},{7,6},{8,12},{9,13},{10,... | collective-permute-start | bytes 516104 | tf_op jit(solution)/shard_map/ppermute | solution.py:654
  16.8 3.2 %collective-permute-done.3 = f32[2,168,128]{2,1,0:T(8,128)S(1)} collective-permute-done((f32[2,168,128]{2,1,0:T(8,128)S(1)}, f32[2,168,128]{2,1,0:T(8,128)S(1)}, u32[]{:S(2)}, u32[]{:S(2)}) %collective-permute-start.3) | collective-permute-done | bytes 172064 | tf_op jit(solution)/shard_map/ppermute | solution.py:654
  20.1 2.1 %collective-permute-start.4 = (f32[168,128]{1,0:T(8,128)S(1)}, f32[168,128]{1,0:T(8,128)S(1)}, u32[]{:S(2)}, u32[]{:S(2)}) collective-permute-start(f32[168,128]{1,0:T(8,128)S(1)} %slice_bitcast_fusion.4), channel_id=1, source_target_pairs={{0,8},{8,0},{1,9},{9,1},{2,10},{10,2},{3,11},{11,3},{4,12},{12,4},... | collective-permute-start | bytes 258056 | tf_op jit(solution)/shard_map/ppermute | solution.py:643
  22.2 1.0 %collective-permute-done.8 = f32[2,2,128,128]{3,2,1,0:T(8,128)S(1)} collective-permute-done((f32[2,2,128,128]{3,2,1,0:T(8,128)S(1)}, f32[2,2,128,128]{3,2,1,0:T(8,128)S(1)}, u32[]{:S(2)}, u32[]{:S(2)}) %collective-permute-start.8) | collective-permute-done | bytes 262176 | tf_op jit(solution)/shard_map/ppermute | solution.py:654
  23.3 1.7 %collective-permute-start.9 = (f32[2,128,128]{2,1,0:T(8,128)S(1)}, f32[2,128,128]{2,1,0:T(8,128)S(1)}, u32[]{:S(2)}, u32[]{:S(2)}) collective-permute-start(f32[2,128,128]{2,1,0:T(8,128)S(1)} %get-tuple-element.72), channel_id=1, source_target_pairs={{0,1},{1,0},{2,6},{3,7},{4,5},{5,4},{6,2},{7,3},{8,9},{9,8},{10,14... | collective-permute-start | bytes 393224 | tf_op jit(solution)/shard_map/ppermute | solution.py:654
  25.0 2.8 %collective-permute-start.5 = (f32[168,128]{1,0:T(8,128)S(1)}, f32[168,128]{1,0:T(8,128)S(1)}, u32[]{:S(2)}, u32[]{:S(2)}) collective-permute-start(f32[168,128]{1,0:T(8,128)S(1)} %fusion.2), channel_id=1, source_target_pairs={{0,16},{16,0},{1,17},{17,1},{2,18},{18,2},{3,19},{19,3},{4,20},{20... | collective-permute-start | bytes 258056 | tf_op jit(solution)/shard_map/ppermute | solution.py:643
  27.8 2.6 %collective-permute-done.5 = f32[168,128]{1,0:T(8,128)S(1)} collective-permute-done((f32[168,128]{1,0:T(8,128)S(1)}, f32[168,128]{1,0:T(8,128)S(1)}, u32[]{:S(2)}, u32[]{:S(2)}) %collective-permute-start.5) | collective-permute-done | bytes 86048 | tf_op jit(solution)/shard_map/ppermute | solution.py:643
  30.6 1.8 %collective-permute-start.10 = (f32[128,128]{1,0:T(8,128)S(1)}, f32[128,128]{1,0:T(8,128)S(1)}, u32[]{:S(2)}, u32[]{:S(2)}) collective-permute-start(f32[128,128]{1,0:T(8,128)S(1)} %get-tuple-element.74), channel_id=1, source_target_pairs={{0,8},{8,0},{1,9},{9,1},{2,10},{10,2},{3,11},{11,3},{4,12},{12,4},... | collective-permute-start | bytes 196616 | tf_op jit(solution)/shard_map/ppermute | solution.py:643
  32.4 3.5 %first_panels.1 = (f32[272,256]{1,0:T(8,128)S(1)}, bf16[48,256]{1,0:T(8,128)(2,1)S(1)}, bf16[48,256]{1,0:T(8,128)(2,1)S(1)}, f32[8,256]{1,0:T(8,128)S(1)}, f32[1...) custom-call(f32[168,128]{1,0:T(8,128)S(1)} %add.38.mine, ...), custom_call_target="tpu_custom_call" | custom-call | flops 1073741824 | bytes 1048576 | tf_op jit(solution)/shard_map/first_panels/pallas_call | solution.py:497
  35.9 3.4 %collective-permute-start.11 = (f32[128,128]{1,0:T(8,128)S(1)}, f32[128,128]{1,0:T(8,128)S(1)}, u32[]{:S(2)}, u32[]{:S(2)}) collective-permute-start(f32[128,128]{1,0:T(8,128)S(1)} %add.42), channel_id=1, source_target_pairs={{0,16},{16,0},{1,17},{17,1},{2,18},{18,2},{3,19},{19,3},{4,20},{20... | collective-permute-start | bytes 196616 | tf_op jit(solution)/shard_map/ppermute | solution.py:643
  39.4 4.5 %second_panels.1 = (f32[128,128]{1,0:T(8,128)S(1)}, f32[272,256]{1,0:T(8,128)S(1)}, bf16[48,256]{1,0:T(8,128)(2,1)S(1)}, bf16[48,256]{1,0:T(8,128)(2,1)S(1)}, f32[8,256]{1,0:T(8,128)S(1)}) custom-call(f32[272,256]{1,0:T(8,128)S(1)} %get-tuple-element.49.refs_0_, bf16[48,256]{1,0:T(8,128)(2,1)S(1)} %get-tuple-element.50.refs_1_, ...), custom_call_target="tpu_custom_call" | custom-call | flops 1073741824 | bytes 1048576 | tf_op jit(solution)/shard_map/second_panels/pallas_call | solution.py:497
  44.0 1.6 %third_panels.1.winv = f32[256,256]{1,0:T(8,128)S(1)} custom-call(f32[272,256]{1,0:T(8,128)S(1)} %get-tuple-element.57.wa_in, bf16[48,256]{1,0:T(8,128)(2,1)S(1)} %get-tuple-element.58.wl_in, bf16[48,256]{1,0:T(8,128)(2,1)S(1)} %get-tuple-element.59.wr_in, f32[8,256]{1,0:T(8,128)S(1)} %get-tuple-element.60.panel_in), custom_call_target="tpu_custom_call" | custom-call | flops 1073741824 | bytes 1048576 | tf_op jit(solution)/shard_map/third_panels/pallas_call | solution.py:497
  45.6 0.7 %products.1 = f32[8,40,128]{2,1,0:T(8,128)S(1)} custom-call(f32[256,256]{1,0:T(8,128)S(1)} %third_panels.1.winv, f32[128,128]{1,0:T(8,128)S(1)} %get-tuple-element.61.ninv_ref, f32[128,128]{1,0:T(8,128)S(1)} %add.43.mine, f32[128,128]{1,0:T(8,128)S(1)} %collective-permute-done.12.other), custom_call_target="tpu_custom_call" | custom-call | tf_op jit(solution)/shard_map/products/pallas_call | solution.py:584
  46.3 10.5 %all_to_all.5.got_ref = f32[8,40,128]{2,1,0:T(8,128)S(1)} all-to-all(f32[8,40,128]{2,1,0:T(8,128)S(1)} %products.1), channel_id=1, replica_groups=mesh['dp0'=2,'dp1'=2,'dp2'=2,'dp3'=2,'own0'=2] {'dp1','dp2','own0'}, dimensions={0} | all-to-all | bytes 327680 | tf_op jit(solution)/shard_map/all_to_all | solution.py:708
  56.8 1.3 %placing.1 = (f32[5,16,256]{2,1,0:T(8,128)}, f32[8,16,64]{2,1,0:T(8,128)}) custom-call(s32[8]{0:T(128)S(1)} %copy-done, f32[8,40,128]{2,1,0:T(8,128)S(1)} %all_to_all.5.got_ref), custom_call_target="tpu_custom_call" | custom-call | tf_op jit(solution)/shard_map/placing/pallas_call | solution.py:629
  (32 shorter events, 0.7 us)
Async XLA Ops:
  4.3 1.8 %collective-permute-start = (f32[2,2,168,128]{3,2,1,0:T(8,128)S(1)}, f32[2,2,168,128]{3,2,1,0:T(8,128)S(1)}, u32[]{:S(2)}, u32[]{:S(2)}) collective-permute-start(f32[2,2,168,128]{3,2,1,0:T(8,128)S(1)} %slice.45), channel_id=1, source_target_pairs={{0,2},{2,0},{1,3},{3,1},{4,6},{6,4},{5,7},{7,5},{8,10},{10,8},{9,1... | collective-permute-start | bytes 1032200 | tf_op jit(solution)/shard_map/ppermute | solution.py:643
  6.2 4.2 %collective-permute-start.1 = (f32[2,2,168,128]{3,2,1,0:T(8,128)S(1)}, f32[2,2,168,128]{3,2,1,0:T(8,128)S(1)}, u32[]{:S(2)}, u32[]{:S(2)}) collective-permute-start(f32[2,2,168,128]{3,2,1,0:T(8,128)S(1)} %pad_maximum_fusion), channel_id=1, source_target_pairs={{0,2},{2,0},{1,3},{3,1},{4,6},{6,4},{5,7},{7,5},{8,10},{10,8},{9,1... | collective-permute-start | bytes 1032200 | tf_op jit(solution)/shard_map/ppermute | solution.py:643
  6.6 7.8 %collective-permute-start.2 = (f32[2,2,168,128]{3,2,1,0:T(8,128)S(1)}, f32[2,2,168,128]{3,2,1,0:T(8,128)S(1)}, u32[]{:S(2)}, u32[]{:S(2)}) collective-permute-start(f32[2,2,168,128]{3,2,1,0:T(8,128)S(1)} %slice_add_fusion), channel_id=1, source_target_pairs={{0,1},{1,0},{2,6},{3,7},{4,5},{5,4},{6,2},{7,3},{8,9},{9,8},{10,14... | collective-permute-start | bytes 1032200 | tf_op jit(solution)/shard_map/ppermute | solution.py:654
  10.1 6.5 %collective-permute-start.7 = (f32[4,2,128,128]{3,2,1,0:T(8,128)S(1)}, f32[4,2,128,128]{3,2,1,0:T(8,128)S(1)}, u32[]{:S(2)}, u32[]{:S(2)}) collective-permute-start(f32[4,2,128,128]{3,2,1,0:T(8,128)S(1)} %get-tuple-element.47), channel_id=1, source_target_pairs={{0,2},{2,0},{1,3},{3,1},{4,6},{6,4},{5,7},{7,5},{8,10},{10,8},{9,1... | collective-permute-start | bytes 1572872 | tf_op jit(solution)/shard_map/ppermute | solution.py:643
  14.5 5.5 %collective-permute-start.3 = (f32[2,168,128]{2,1,0:T(8,128)S(1)}, f32[2,168,128]{2,1,0:T(8,128)S(1)}, u32[]{:S(2)}, u32[]{:S(2)}) collective-permute-start(f32[2,168,128]{2,1,0:T(8,128)S(1)} %slice_bitcast_fusion), channel_id=1, source_target_pairs={{0,4},{1,5},{2,3},{3,2},{4,0},{5,1},{6,7},{7,6},{8,12},{9,13},{10,... | collective-permute-start | bytes 516104 | tf_op jit(solution)/shard_map/ppermute | solution.py:654
  16.8 6.4 %collective-permute-start.8 = (f32[2,2,128,128]{3,2,1,0:T(8,128)S(1)}, f32[2,2,128,128]{3,2,1,0:T(8,128)S(1)}, u32[]{:S(2)}, u32[]{:S(2)}) collective-permute-start(f32[2,2,128,128]{3,2,1,0:T(8,128)S(1)} %get-tuple-element.70), channel_id=1, source_target_pairs={{0,4},{1,5},{2,3},{3,2},{4,0},{5,1},{6,7},{7,6},{8,12},{9,13},{10,... | collective-permute-start | bytes 786440 | tf_op jit(solution)/shard_map/ppermute | solution.py:654
  20.1 4.9 %collective-permute-start.4 = (f32[168,128]{1,0:T(8,128)S(1)}, f32[168,128]{1,0:T(8,128)S(1)}, u32[]{:S(2)}, u32[]{:S(2)}) collective-permute-start(f32[168,128]{1,0:T(8,128)S(1)} %slice_bitcast_fusion.4), channel_id=1, source_target_pairs={{0,8},{8,0},{1,9},{9,1},{2,10},{10,2},{3,11},{11,3},{4,12},{12,4},... | collective-permute-start | bytes 258056 | tf_op jit(solution)/shard_map/ppermute | solution.py:643
  23.3 7.3 %collective-permute-start.9 = (f32[2,128,128]{2,1,0:T(8,128)S(1)}, f32[2,128,128]{2,1,0:T(8,128)S(1)}, u32[]{:S(2)}, u32[]{:S(2)}) collective-permute-start(f32[2,128,128]{2,1,0:T(8,128)S(1)} %get-tuple-element.72), channel_id=1, source_target_pairs={{0,1},{1,0},{2,6},{3,7},{4,5},{5,4},{6,2},{7,3},{8,9},{9,8},{10,14... | collective-permute-start | bytes 393224 | tf_op jit(solution)/shard_map/ppermute | solution.py:654
  25.0 5.4 %collective-permute-start.5 = (f32[168,128]{1,0:T(8,128)S(1)}, f32[168,128]{1,0:T(8,128)S(1)}, u32[]{:S(2)}, u32[]{:S(2)}) collective-permute-start(f32[168,128]{1,0:T(8,128)S(1)} %fusion.2), channel_id=1, source_target_pairs={{0,16},{16,0},{1,17},{17,1},{2,18},{18,2},{3,19},{19,3},{4,20},{20... | collective-permute-start | bytes 258056 | tf_op jit(solution)/shard_map/ppermute | solution.py:643
  30.4 1.9 %collective-permute-start.6 = (f32[168,128]{1,0:T(8,128)S(1)}, f32[168,128]{1,0:T(8,128)S(1)}, u32[]{:S(2)}, u32[]{:S(2)}) collective-permute-start(f32[168,128]{1,0:T(8,128)S(1)} %add.38.mine), channel_id=1, source_target_pairs={{0,2},{2,0},{1,3},{3,1},{4,6},{6,4},{5,7},{7,5},{8,10},{10,8},{9,1... | collective-permute-start | bytes 258056 | tf_op jit(solution)/shard_map/ppermute | solution.py:643
  30.6 5.3 %collective-permute-start.10 = (f32[128,128]{1,0:T(8,128)S(1)}, f32[128,128]{1,0:T(8,128)S(1)}, u32[]{:S(2)}, u32[]{:S(2)}) collective-permute-start(f32[128,128]{1,0:T(8,128)S(1)} %get-tuple-element.74), channel_id=1, source_target_pairs={{0,8},{8,0},{1,9},{9,1},{2,10},{10,2},{3,11},{11,3},{4,12},{12,4},... | collective-permute-start | bytes 196616 | tf_op jit(solution)/shard_map/ppermute | solution.py:643
  35.9 8.0 %collective-permute-start.11 = (f32[128,128]{1,0:T(8,128)S(1)}, f32[128,128]{1,0:T(8,128)S(1)}, u32[]{:S(2)}, u32[]{:S(2)}) collective-permute-start(f32[128,128]{1,0:T(8,128)S(1)} %add.42), channel_id=1, source_target_pairs={{0,16},{16,0},{1,17},{17,1},{2,18},{18,2},{3,19},{19,3},{4,20},{20... | collective-permute-start | bytes 196616 | tf_op jit(solution)/shard_map/ppermute | solution.py:643
  43.8 13.0 %copy-start = (s32[8]{0:T(128)S(1)}, s32[8]{0:T(128)}, u32[]{:S(2)}) copy-start(s32[8]{0:T(128)} %owner_map.1) | copy-start | bytes 100
  43.9 1.7 %collective-permute-start.12 = (f32[128,128]{1,0:T(8,128)S(1)}, f32[128,128]{1,0:T(8,128)S(1)}, u32[]{:S(2)}, u32[]{:S(2)}) collective-permute-start(f32[128,128]{1,0:T(8,128)S(1)} %add.43.mine), channel_id=1, source_target_pairs={{0,2},{2,0},{1,3},{3,1},{4,6},{6,4},{5,7},{7,5},{8,10},{10,8},{9,1... | collective-permute-start | bytes 196616 | tf_op jit(solution)/shard_map/ppermute | solution.py:643

commit v12 on v11

--- a/solution.py
+++ b/solution.py
@@ -48,9 +48,6 @@
     )
 
 
-AHEAD = 8
-
-
 def layer_copies(place, sources, buffers, sems):
     layer = place.layer()
     return [
@@ -161,9 +158,9 @@
 def hot_kernel(place, wide_hbm, narrow_hbm, keep, send, wides, narrows, a_flat, b_flat, sems):
     copies = layer_copies(place, (wide_hbm, narrow_hbm), (wides, narrows), sems)
     order = HOT + COLD
-    for i in order[:AHEAD]:
+    for at, i in enumerate(order):
         for copy in copies[i]:
-            copy.start()
+            copy.start(priority=at % 2)
 
     def pack(i, sums):
         kept, sent = pack_layer(place, i, *sums, a_flat, b_flat)
@@ -176,12 +173,9 @@
         put(send, (other, z), sent)
 
     before = None
-    for at, i in enumerate(order):
+    for i in order:
         for copy in copies[i]:
             copy.wait()
-        if at + AHEAD < len(order):
-            for copy in copies[order[at + AHEAD]]:
-                copy.start()
         if before is not None:
             pack(*before)
             before = None
@@ -293,7 +287,7 @@
     )
 
 
-def sweep_panel(a_ref, left_ref, right_ref, tile, step, panel):
+def sweep_panel(a_ref, left_ref, right_ref, rows_ref, cols_ref, tile, step, panel):
     size = a_ref.shape[1]
     tiles = size // LANES
     first = step * PANEL
@@ -303,15 +297,19 @@
     shape = (PANEL, LANES)
     sub = lax.broadcasted_iota(jnp.int32, shape, 0)
     lane = lax.broadcasted_iota(jnp.int32, shape, 1)
-    parts = [panel[:, LANES * t : LANES * (t + 1)] for t in range(tiles)]
-    rows = [
-        [jnp.broadcast_to(part[k : k + 1, :], shape) for part in parts] for k in range(PANEL)
-    ]
-    index = [jnp.full(shape, 0, jnp.int32) + (first + i) for i in range(PANEL)]
+
+    def on_all(ref, k, lanes):
+        return jnp.broadcast_to(ref[k : k + 1, lanes], shape)
+
+    rows_ref[...] = panel
+    lanes = [slice(LANES * t, LANES * (t + 1)) for t in range(tiles)]
+    rows = [[on_all(rows_ref, k, part) for part in lanes] for k in range(PANEL)]
+    for j in range(PANEL):
+        cols_ref[PANEL * j : PANEL * (j + 1)] = lane_gather(rows[j][tile], first + sub)
     d = [[None] * PANEL for _ in range(PANEL)]
     for j in range(PANEL):
         for i in range(j, PANEL):
-            d[i][j] = lane_gather(rows[j][tile], index[i])
+            d[i][j] = on_all(cols_ref, PANEL * j + i, slice(None))
     own = (lane >= first) & (lane < first + PANEL)
     last = first == LANES - PANEL
     next_lane = jnp.where(last, 0, first + PANEL) + sub
@@ -382,7 +380,7 @@
 
 
 def clear(work):
-    a_ref, left, right = work
+    a_ref, left, right = work[:3]
     size = a_ref.shape[1]
     a_ref[:PANEL] = jnp.zeros((PANEL, size), jnp.float32)
     a_ref[PANEL + size :] = jnp.zeros((PANEL, size), jnp.float32)
@@ -396,6 +394,13 @@
         pltpu.VMEM((size + 2 * PANEL, size), jnp.float32),
         pltpu.VMEM((splits, size), jnp.bfloat16),
         pltpu.VMEM((splits, size), jnp.bfloat16),
+    ]
+
+
+def row_shapes(size):
+    return [
+        pltpu.VMEM((PANEL, size), jnp.float32),
+        pltpu.VMEM((PANEL * PANEL, LANES), jnp.float32),
     ]
 
 
@@ -443,8 +448,9 @@
     return lax.fori_loop(begin, end, lambda i, panel: sweep_panel(*work, 1, i, panel), panel)
 
 
-def first_kernel(place, total, mine, other, wa, wl, wr, wp, na, nl, nr, np_, a_flat, b_flat):
-    wide_work, narrow_work = (wa, wl, wr), (na, nl, nr)
+def first_kernel(place, total, mine, other, wa, wl, wr, wp, na, nl, nr, np_, *refs):
+    a_flat, b_flat = refs[:2]
+    wide_work, narrow_work = (wa, wl, wr, *refs[2:4]), (na, nl, nr, *refs[4:])
     place_halves(place, (mine, other), 0, a_flat)
     place_halves(place, (mine, other), a_flat.shape[0] // 2, b_flat)
     n = LANES
@@ -466,23 +472,30 @@
 
 
 def second_kernel(*refs):
-    given, ninv_ref, state, narrow_work = refs[:8], refs[8], refs[9:13], refs[13:]
-    wide_work, wp = state[:3], state[3]
-    for source, target in zip(given, (*wide_work, None, *narrow_work)):
-        if target is not None:
-            target[...] = source[...]
+    given, ninv_ref, state, narrow_state, wide_rows, narrow_rows = (
+        refs[:8],
+        refs[8],
+        refs[9:13],
+        refs[13:16],
+        refs[16:18],
+        refs[18:],
+    )
+    for source, target in zip((*given[:3], *given[4:7]), (*state[:3], *narrow_state)):
+        target[...] = source[...]
+    wide_work, narrow_work = (*state[:3], *wide_rows), (*narrow_state, *narrow_rows)
+    wp = state[3]
     panels = (given[3][...], given[7][...])
     panel, _ = sweep_both(wide_work, narrow_work, FIRST_STEPS, STEPS, panels)
-    trailing_update(*narrow_work, LANES)
+    trailing_update(*narrow_work[:3], LANES)
     ninv_ref[...] = -narrow_work[0][PANEL : PANEL + LANES, :]
     wp[...] = sweep_wide(wide_work, 0, SECOND_STEPS, panel)
 
 
-def third_kernel(wa_in, wl_in, wr_in, panel_in, winv, wa, wl, wr):
+def third_kernel(wa_in, wl_in, wr_in, panel_in, winv, wa, wl, wr, *rows):
     wa[...] = wa_in[...]
     wl[...] = wl_in[...]
     wr[...] = wr_in[...]
-    sweep_wide((wa, wl, wr), SECOND_STEPS, STEPS, panel_in[...])
+    sweep_wide((wa, wl, wr, *rows), SECOND_STEPS, STEPS, panel_in[...])
     wide = wa.shape[1]
     trailing_update(wa, wl, wr, wide)
     winv[...] = -wa[PANEL : PANEL + wide, :]
@@ -515,6 +528,8 @@
         [
             pltpu.VMEM((EARLY_ROWS, LANES), jnp.float32),
             pltpu.VMEM((LATE_ROWS, LANES), jnp.float32),
+            *row_shapes(wide),
+            *row_shapes(narrow),
         ],
     )
 
@@ -526,13 +541,14 @@
         "second_panels",
         state,
         [ninv] + state_shapes(wide),
-        work_shapes(narrow),
+        [*work_shapes(narrow), *row_shapes(wide), *row_shapes(narrow)],
     )
 
 
 def third_panels(state, wide):
     winv = jax.ShapeDtypeStruct((wide, wide), jnp.float32)
-    return sweep_call(third_kernel, "third_panels", state, [winv], work_shapes(wide))[0]
+    scratch = [*work_shapes(wide), *row_shapes(wide)]
+    return sweep_call(third_kernel, "third_panels", state, [winv], scratch)[0]
 
 
 def product_kernel(place, total, rows, winv, ninv_ref, mine, other, out_ref, flat):

time: 58.2 us -> 58.1 us (level)
    pallas_call x3, Pallas kernels: 9.6 us -> 8.88 us  [sweep_call(): pl.pallas_call(kernel, in_specs=[VMEM] * len(args), out_specs=[VMEM] * le...]
  transfers between devices with their start and end apart: 13 -> 13, of which waited for: 5 -> 5; matrix products, arithmetic and copies ran while one was open for 1% -> 1% of each run, Pallas kernels for 19% -> 18%
where the time goes in v12:
time: 58.1 us; the launch traced here: 57.9 us
  starting transfers between devices  18 us (31%)
  Pallas kernels  16.4 us (28%)
  waiting for transfers between devices  11.6 us (20%)
  blocking collectives  10.7 us (18%)
  between operations  0.84 us (1%)
    ppermute x9, starting transfers between devices, swap(): return lax.ppermute(value, axis, [(0, 1), (1, 0)])  11.5 us
    all_to_all x1, blocking collectives, on_device(): got = lax.all_to_all(sent, (place.near, place.second, place.first), 0, 0)  10.7 us
    pallas_call x3, Pallas kernels, sweep_call(): pl.pallas_call(kernel, in_specs=[VMEM] * len(args), out_specs=[VMEM] * le...  8.88 us
    ppermute x4, waiting for transfers between devices, swap_by_core(): return lax.ppermute(value, (place.second, place.core, place.first), pairs)  8.26 us
    ppermute x4, starting transfers between devices, swap_by_core(): return lax.ppermute(value, (place.second, place.core, place.first), pairs)  6.51 us
    pallas_call x1, Pallas kernels, hot_squares(): pl.pallas_call(functools.partial(hot_kernel, place), in_specs=[HBM, HBM],...  3.99 us
    ppermute x9, waiting for transfers between devices, swap(): return lax.ppermute(value, axis, [(0, 1), (1, 0)])  3.3 us
    pallas_call x1, Pallas kernels, placing(): pl.pallas_call(functools.partial(placing_kernel, place), in_specs=[SMEM,...  1.26 us
  transfers between devices with their start and end apart: 13, of which 5 were waited for; matrix products, arithmetic and copies ran while one was open for 1% of the time, Pallas kernels for 18%

profile of v12, /device:TPU:0, one launch (start us, length us, event | category | flops | bytes accessed | tf_op | source)
XLA Modules:
  0.0 57.9 jit_solution(3776292811798075855)
XLA Ops:
  0.6 4.0 %hot_squares.1 = (f32[3,2,168,128]{3,2,1,0:T(8,128)S(1)}, f32[3,2,168,128]{3,2,1,0:T(8,128)S(1)}, bf16[8,768,256]{2,1,0:T(8,128)(2,1)S(1)}, bf16[8,768,128]{2,1,0:T(8,128)(2,1)S(1)}) custom-call(bf16[8,768,256]{2,1,0:T(8,128)(2,1)} %wide_hbm.1, bf16[8,768,128]{2,1,0:T(8,128)(2,1)} %narrow_hbm.1), custom_call_target="tpu_custom_call" | custom-call | flops 754974720 | bytes 3145728 | tf_op jit(solution)/shard_map/hot_squares/pallas_call | solution.py:226
  4.7 0.5 collective-permute-start
  5.2 0.6 %cold_squares.1 = (f32[2,168,128]{2,1,0:T(8,128)S(1)}, f32[2,168,128]{2,1,0:T(8,128)S(1)}) custom-call(bf16[8,768,256]{2,1,0:T(8,128)(2,1)S(1)} %get-tuple-element.46.wides, bf16[8,768,128]{2,1,0:T(8,128)(2,1)S(1)} %get-tuple-element.39.narrows), custom_call_target="tpu_custom_call" | custom-call | flops 251658240 | bytes 3145728 | tf_op jit(solution)/shard_map/cold_squares/pallas_call | solution.py:248
  5.8 0.6 %collective-permute-done = f32[2,2,168,128]{3,2,1,0:T(8,128)S(1)} collective-permute-done((f32[2,2,168,128]{3,2,1,0:T(8,128)S(1)}, f32[2,2,168,128]{3,2,1,0:T(8,128)S(1)}, u32[]{:S(2)}, u32[]{:S(2)}) %collective-permute-start) | collective-permute-done | bytes 344096 | tf_op jit(solution)/shard_map/ppermute | solution.py:659
  6.5 0.4 collective-permute-start.1
  7.0 2.6 %collective-permute-start.2 = (f32[2,2,168,128]{3,2,1,0:T(8,128)S(1)}, f32[2,2,168,128]{3,2,1,0:T(8,128)S(1)}, u32[]{:S(2)}, u32[]{:S(2)}) collective-permute-start(f32[2,2,168,128]{3,2,1,0:T(8,128)S(1)} %slice_add_fusion), channel_id=1, source_target_pairs={{0,1},{1,0},{2,6},{3,7},{4,5},{5,4},{6,2},{7,3},{8,9},{9,8},{10,14... | collective-permute-start | bytes 1032200 | tf_op jit(solution)/shard_map/ppermute | solution.py:670
  9.6 0.9 %mixed.1 = (f32[4,2,128,128]{3,2,1,0:T(8,128)S(1)}, f32[4,2,128,128]{3,2,1,0:T(8,128)S(1)}) custom-call(bf16[8,768,256]{2,1,0:T(8,128)(2,1)S(1)} %get-tuple-element.46.wides, bf16[8,768,128]{2,1,0:T(8,128)(2,1)S(1)} %get-tuple-element.39.narrows), custom_call_target="tpu_custom_call" | custom-call | flops 402653184 | bytes 3145728 | tf_op jit(solution)/shard_map/mixed/pallas_call | solution.py:263
  10.5 0.2 collective-permute-start.7
  10.7 4.1 %collective-permute-done.2 = f32[2,2,168,128]{3,2,1,0:T(8,128)S(1)} collective-permute-done((f32[2,2,168,128]{3,2,1,0:T(8,128)S(1)}, f32[2,2,168,128]{3,2,1,0:T(8,128)S(1)}, u32[]{:S(2)}, u32[]{:S(2)}) %collective-permute-start.2) | collective-permute-done | bytes 344096 | tf_op jit(solution)/shard_map/ppermute | solution.py:670
  14.9 2.1 %collective-permute-start.3 = (f32[2,168,128]{2,1,0:T(8,128)S(1)}, f32[2,168,128]{2,1,0:T(8,128)S(1)}, u32[]{:S(2)}, u32[]{:S(2)}) collective-permute-start(f32[2,168,128]{2,1,0:T(8,128)S(1)} %slice_bitcast_fusion), channel_id=1, source_target_pairs={{0,4},{1,5},{2,3},{3,2},{4,0},{5,1},{6,7},{7,6},{8,12},{9,13},{10,... | collective-permute-start | bytes 516104 | tf_op jit(solution)/shard_map/ppermute | solution.py:670
  17.2 3.2 %collective-permute-done.3 = f32[2,168,128]{2,1,0:T(8,128)S(1)} collective-permute-done((f32[2,168,128]{2,1,0:T(8,128)S(1)}, f32[2,168,128]{2,1,0:T(8,128)S(1)}, u32[]{:S(2)}, u32[]{:S(2)}) %collective-permute-start.3) | collective-permute-done | bytes 172064 | tf_op jit(solution)/shard_map/ppermute | solution.py:670
  20.4 2.1 %collective-permute-start.4 = (f32[168,128]{1,0:T(8,128)S(1)}, f32[168,128]{1,0:T(8,128)S(1)}, u32[]{:S(2)}, u32[]{:S(2)}) collective-permute-start(f32[168,128]{1,0:T(8,128)S(1)} %slice_bitcast_fusion.4), channel_id=1, source_target_pairs={{0,8},{8,0},{1,9},{9,1},{2,10},{10,2},{3,11},{11,3},{4,12},{12,4},... | collective-permute-start | bytes 258056 | tf_op jit(solution)/shard_map/ppermute | solution.py:659
  22.6 1.0 %collective-permute-done.8 = f32[2,2,128,128]{3,2,1,0:T(8,128)S(1)} collective-permute-done((f32[2,2,128,128]{3,2,1,0:T(8,128)S(1)}, f32[2,2,128,128]{3,2,1,0:T(8,128)S(1)}, u32[]{:S(2)}, u32[]{:S(2)}) %collective-permute-start.8) | collective-permute-done | bytes 262176 | tf_op jit(solution)/shard_map/ppermute | solution.py:670
  23.6 1.7 %collective-permute-start.9 = (f32[2,128,128]{2,1,0:T(8,128)S(1)}, f32[2,128,128]{2,1,0:T(8,128)S(1)}, u32[]{:S(2)}, u32[]{:S(2)}) collective-permute-start(f32[2,128,128]{2,1,0:T(8,128)S(1)} %get-tuple-element.72), channel_id=1, source_target_pairs={{0,1},{1,0},{2,6},{3,7},{4,5},{5,4},{6,2},{7,3},{8,9},{9,8},{10,14... | collective-permute-start | bytes 393224 | tf_op jit(solution)/shard_map/ppermute | solution.py:670
  25.3 2.8 %collective-permute-start.5 = (f32[168,128]{1,0:T(8,128)S(1)}, f32[168,128]{1,0:T(8,128)S(1)}, u32[]{:S(2)}, u32[]{:S(2)}) collective-permute-start(f32[168,128]{1,0:T(8,128)S(1)} %fusion.2), channel_id=1, source_target_pairs={{0,16},{16,0},{1,17},{17,1},{2,18},{18,2},{3,19},{19,3},{4,20},{20... | collective-permute-start | bytes 258056 | tf_op jit(solution)/shard_map/ppermute | solution.py:659
  28.2 2.6 %collective-permute-done.5 = f32[168,128]{1,0:T(8,128)S(1)} collective-permute-done((f32[168,128]{1,0:T(8,128)S(1)}, f32[168,128]{1,0:T(8,128)S(1)}, u32[]{:S(2)}, u32[]{:S(2)}) %collective-permute-start.5) | collective-permute-done | bytes 86048 | tf_op jit(solution)/shard_map/ppermute | solution.py:659
  30.9 1.8 %collective-permute-start.10 = (f32[128,128]{1,0:T(8,128)S(1)}, f32[128,128]{1,0:T(8,128)S(1)}, u32[]{:S(2)}, u32[]{:S(2)}) collective-permute-start(f32[128,128]{1,0:T(8,128)S(1)} %get-tuple-element.74), channel_id=1, source_target_pairs={{0,8},{8,0},{1,9},{9,1},{2,10},{10,2},{3,11},{11,3},{4,12},{12,4},... | collective-permute-start | bytes 196616 | tf_op jit(solution)/shard_map/ppermute | solution.py:659
  32.8 3.1 %first_panels.1 = (f32[272,256]{1,0:T(8,128)S(1)}, bf16[48,256]{1,0:T(8,128)(2,1)S(1)}, bf16[48,256]{1,0:T(8,128)(2,1)S(1)}, f32[8,256]{1,0:T(8,128)S(1)}, f32[1...) custom-call(f32[168,128]{1,0:T(8,128)S(1)} %add.38.mine, ...), custom_call_target="tpu_custom_call" | custom-call | flops 1073741824 | bytes 1048576 | tf_op jit(solution)/shard_map/first_panels/pallas_call | solution.py:510
  35.9 3.4 %collective-permute-start.11 = (f32[128,128]{1,0:T(8,128)S(1)}, f32[128,128]{1,0:T(8,128)S(1)}, u32[]{:S(2)}, u32[]{:S(2)}) collective-permute-start(f32[128,128]{1,0:T(8,128)S(1)} %add.42), channel_id=1, source_target_pairs={{0,16},{16,0},{1,17},{17,1},{2,18},{18,2},{3,19},{19,3},{4,20},{20... | collective-permute-start | bytes 196616 | tf_op jit(solution)/shard_map/ppermute | solution.py:659
  39.3 4.2 %second_panels.1 = (f32[128,128]{1,0:T(8,128)S(1)}, f32[272,256]{1,0:T(8,128)S(1)}, bf16[48,256]{1,0:T(8,128)(2,1)S(1)}, bf16[48,256]{1,0:T(8,128)(2,1)S(1)}, f32[8,256]{1,0:T(8,128)S(1)}) custom-call(f32[272,256]{1,0:T(8,128)S(1)} %get-tuple-element.49.refs_0_, bf16[48,256]{1,0:T(8,128)(2,1)S(1)} %get-tuple-element.50.refs_1_, ...), custom_call_target="tpu_custom_call" | custom-call | flops 1073741824 | bytes 1048576 | tf_op jit(solution)/shard_map/second_panels/pallas_call | solution.py:510
  43.7 1.6 %third_panels.1.winv = f32[256,256]{1,0:T(8,128)S(1)} custom-call(f32[272,256]{1,0:T(8,128)S(1)} %get-tuple-element.57.wa_in, bf16[48,256]{1,0:T(8,128)(2,1)S(1)} %get-tuple-element.58.wl_in, bf16[48,256]{1,0:T(8,128)(2,1)S(1)} %get-tuple-element.59.wr_in, f32[8,256]{1,0:T(8,128)S(1)} %get-tuple-element.60.panel_in), custom_call_target="tpu_custom_call" | custom-call | flops 1073741824 | bytes 1048576 | tf_op jit(solution)/shard_map/third_panels/pallas_call | solution.py:510
  45.3 0.7 %products.1 = f32[8,40,128]{2,1,0:T(8,128)S(1)} custom-call(f32[256,256]{1,0:T(8,128)S(1)} %third_panels.1.winv, f32[128,128]{1,0:T(8,128)S(1)} %get-tuple-element.61.ninv_ref, f32[128,128]{1,0:T(8,128)S(1)} %add.43.mine, f32[128,128]{1,0:T(8,128)S(1)} %collective-permute-done.12.other), custom_call_target="tpu_custom_call" | custom-call | tf_op jit(solution)/shard_map/products/pallas_call | solution.py:600
  46.0 10.7 %all_to_all.5.got_ref = f32[8,40,128]{2,1,0:T(8,128)S(1)} all-to-all(f32[8,40,128]{2,1,0:T(8,128)S(1)} %products.1), channel_id=1, replica_groups=mesh['dp0'=2,'dp1'=2,'dp2'=2,'dp3'=2,'own0'=2] {'dp1','dp2','own0'}, dimensions={0} | all-to-all | bytes 327680 | tf_op jit(solution)/shard_map/all_to_all | solution.py:724
  56.7 1.3 %placing.1 = (f32[5,16,256]{2,1,0:T(8,128)}, f32[8,16,64]{2,1,0:T(8,128)}) custom-call(s32[8]{0:T(128)S(1)} %copy-done, f32[8,40,128]{2,1,0:T(8,128)S(1)} %all_to_all.5.got_ref), custom_call_target="tpu_custom_call" | custom-call | tf_op jit(solution)/shard_map/placing/pallas_call | solution.py:645
  (32 shorter events, 0.7 us)
Async XLA Ops:
  4.7 1.8 %collective-permute-start = (f32[2,2,168,128]{3,2,1,0:T(8,128)S(1)}, f32[2,2,168,128]{3,2,1,0:T(8,128)S(1)}, u32[]{:S(2)}, u32[]{:S(2)}) collective-permute-start(f32[2,2,168,128]{3,2,1,0:T(8,128)S(1)} %slice.45), channel_id=1, source_target_pairs={{0,2},{2,0},{1,3},{3,1},{4,6},{6,4},{5,7},{7,5},{8,10},{10,8},{9,1... | collective-permute-start | bytes 1032200 | tf_op jit(solution)/shard_map/ppermute | solution.py:659
  6.5 4.2 %collective-permute-start.1 = (f32[2,2,168,128]{3,2,1,0:T(8,128)S(1)}, f32[2,2,168,128]{3,2,1,0:T(8,128)S(1)}, u32[]{:S(2)}, u32[]{:S(2)}) collective-permute-start(f32[2,2,168,128]{3,2,1,0:T(8,128)S(1)} %pad_maximum_fusion), channel_id=1, source_target_pairs={{0,2},{2,0},{1,3},{3,1},{4,6},{6,4},{5,7},{7,5},{8,10},{10,8},{9,1... | collective-permute-start | bytes 1032200 | tf_op jit(solution)/shard_map/ppermute | solution.py:659
  7.0 7.8 %collective-permute-start.2 = (f32[2,2,168,128]{3,2,1,0:T(8,128)S(1)}, f32[2,2,168,128]{3,2,1,0:T(8,128)S(1)}, u32[]{:S(2)}, u32[]{:S(2)}) collective-permute-start(f32[2,2,168,128]{3,2,1,0:T(8,128)S(1)} %slice_add_fusion), channel_id=1, source_target_pairs={{0,1},{1,0},{2,6},{3,7},{4,5},{5,4},{6,2},{7,3},{8,9},{9,8},{10,14... | collective-permute-start | bytes 1032200 | tf_op jit(solution)/shard_map/ppermute | solution.py:670
  10.5 6.5 %collective-permute-start.7 = (f32[4,2,128,128]{3,2,1,0:T(8,128)S(1)}, f32[4,2,128,128]{3,2,1,0:T(8,128)S(1)}, u32[]{:S(2)}, u32[]{:S(2)}) collective-permute-start(f32[4,2,128,128]{3,2,1,0:T(8,128)S(1)} %get-tuple-element.47), channel_id=1, source_target_pairs={{0,2},{2,0},{1,3},{3,1},{4,6},{6,4},{5,7},{7,5},{8,10},{10,8},{9,1... | collective-permute-start | bytes 1572872 | tf_op jit(solution)/shard_map/ppermute | solution.py:659
  14.9 5.5 %collective-permute-start.3 = (f32[2,168,128]{2,1,0:T(8,128)S(1)}, f32[2,168,128]{2,1,0:T(8,128)S(1)}, u32[]{:S(2)}, u32[]{:S(2)}) collective-permute-start(f32[2,168,128]{2,1,0:T(8,128)S(1)} %slice_bitcast_fusion), channel_id=1, source_target_pairs={{0,4},{1,5},{2,3},{3,2},{4,0},{5,1},{6,7},{7,6},{8,12},{9,13},{10,... | collective-permute-start | bytes 516104 | tf_op jit(solution)/shard_map/ppermute | solution.py:670
  17.1 6.4 %collective-permute-start.8 = (f32[2,2,128,128]{3,2,1,0:T(8,128)S(1)}, f32[2,2,128,128]{3,2,1,0:T(8,128)S(1)}, u32[]{:S(2)}, u32[]{:S(2)}) collective-permute-start(f32[2,2,128,128]{3,2,1,0:T(8,128)S(1)} %get-tuple-element.70), channel_id=1, source_target_pairs={{0,4},{1,5},{2,3},{3,2},{4,0},{5,1},{6,7},{7,6},{8,12},{9,13},{10,... | collective-permute-start | bytes 786440 | tf_op jit(solution)/shard_map/ppermute | solution.py:670
  20.4 4.9 %collective-permute-start.4 = (f32[168,128]{1,0:T(8,128)S(1)}, f32[168,128]{1,0:T(8,128)S(1)}, u32[]{:S(2)}, u32[]{:S(2)}) collective-permute-start(f32[168,128]{1,0:T(8,128)S(1)} %slice_bitcast_fusion.4), channel_id=1, source_target_pairs={{0,8},{8,0},{1,9},{9,1},{2,10},{10,2},{3,11},{11,3},{4,12},{12,4},... | collective-permute-start | bytes 258056 | tf_op jit(solution)/shard_map/ppermute | solution.py:659
  23.6 7.3 %collective-permute-start.9 = (f32[2,128,128]{2,1,0:T(8,128)S(1)}, f32[2,128,128]{2,1,0:T(8,128)S(1)}, u32[]{:S(2)}, u32[]{:S(2)}) collective-permute-start(f32[2,128,128]{2,1,0:T(8,128)S(1)} %get-tuple-element.72), channel_id=1, source_target_pairs={{0,1},{1,0},{2,6},{3,7},{4,5},{5,4},{6,2},{7,3},{8,9},{9,8},{10,14... | collective-permute-start | bytes 393224 | tf_op jit(solution)/shard_map/ppermute | solution.py:670
  25.3 5.4 %collective-permute-start.5 = (f32[168,128]{1,0:T(8,128)S(1)}, f32[168,128]{1,0:T(8,128)S(1)}, u32[]{:S(2)}, u32[]{:S(2)}) collective-permute-start(f32[168,128]{1,0:T(8,128)S(1)} %fusion.2), channel_id=1, source_target_pairs={{0,16},{16,0},{1,17},{17,1},{2,18},{18,2},{3,19},{19,3},{4,20},{20... | collective-permute-start | bytes 258056 | tf_op jit(solution)/shard_map/ppermute | solution.py:659
  30.8 1.9 %collective-permute-start.6 = (f32[168,128]{1,0:T(8,128)S(1)}, f32[168,128]{1,0:T(8,128)S(1)}, u32[]{:S(2)}, u32[]{:S(2)}) collective-permute-start(f32[168,128]{1,0:T(8,128)S(1)} %add.38.mine), channel_id=1, source_target_pairs={{0,2},{2,0},{1,3},{3,1},{4,6},{6,4},{5,7},{7,5},{8,10},{10,8},{9,1... | collective-permute-start | bytes 258056 | tf_op jit(solution)/shard_map/ppermute | solution.py:659
  30.9 4.9 %collective-permute-start.10 = (f32[128,128]{1,0:T(8,128)S(1)}, f32[128,128]{1,0:T(8,128)S(1)}, u32[]{:S(2)}, u32[]{:S(2)}) collective-permute-start(f32[128,128]{1,0:T(8,128)S(1)} %get-tuple-element.74), channel_id=1, source_target_pairs={{0,8},{8,0},{1,9},{9,1},{2,10},{10,2},{3,11},{11,3},{4,12},{12,4},... | collective-permute-start | bytes 196616 | tf_op jit(solution)/shard_map/ppermute | solution.py:659
  35.9 7.7 %collective-permute-start.11 = (f32[128,128]{1,0:T(8,128)S(1)}, f32[128,128]{1,0:T(8,128)S(1)}, u32[]{:S(2)}, u32[]{:S(2)}) collective-permute-start(f32[128,128]{1,0:T(8,128)S(1)} %add.42), channel_id=1, source_target_pairs={{0,16},{16,0},{1,17},{17,1},{2,18},{18,2},{3,19},{19,3},{4,20},{20... | collective-permute-start | bytes 196616 | tf_op jit(solution)/shard_map/ppermute | solution.py:659
  43.5 13.1 %copy-start = (s32[8]{0:T(128)S(1)}, s32[8]{0:T(128)}, u32[]{:S(2)}) copy-start(s32[8]{0:T(128)} %owner_map.1) | copy-start | bytes 100
  43.6 1.7 %collective-permute-start.12 = (f32[128,128]{1,0:T(8,128)S(1)}, f32[128,128]{1,0:T(8,128)S(1)}, u32[]{:S(2)}, u32[]{:S(2)}) collective-permute-start(f32[128,128]{1,0:T(8,128)S(1)} %add.43.mine), channel_id=1, source_target_pairs={{0,2},{2,0},{1,3},{3,1},{4,6},{6,4},{5,7},{7,5},{8,10},{10,8},{9,1... | collective-permute-start | bytes 196616 | tf_op jit(solution)/shard_map/ppermute | solution.py:659

commit v13 on v12

--- a/solution.py
+++ b/solution.py
@@ -158,9 +158,9 @@
 def hot_kernel(place, wide_hbm, narrow_hbm, keep, send, wides, narrows, a_flat, b_flat, sems):
     copies = layer_copies(place, (wide_hbm, narrow_hbm), (wides, narrows), sems)
     order = HOT + COLD
-    for at, i in enumerate(order):
+    for i in order:
         for copy in copies[i]:
-            copy.start(priority=at % 2)
+            copy.start()
 
     def pack(i, sums):
         kept, sent = pack_layer(place, i, *sums, a_flat, b_flat)
@@ -287,6 +287,13 @@
     )
 
 
+def in_three(x):
+    high = x.astype(jnp.bfloat16).astype(jnp.float32)
+    rest = x - high
+    middle = rest.astype(jnp.bfloat16).astype(jnp.float32)
+    return high, middle, rest - middle
+
+
 def sweep_panel(a_ref, left_ref, right_ref, rows_ref, cols_ref, tile, step, panel):
     size = a_ref.shape[1]
     tiles = size // LANES
@@ -304,8 +311,10 @@
     rows_ref[...] = panel
     lanes = [slice(LANES * t, LANES * (t + 1)) for t in range(tiles)]
     rows = [[on_all(rows_ref, k, part) for part in lanes] for k in range(PANEL)]
+    here = panel[:, lanes[tile]]
     for j in range(PANEL):
-        cols_ref[PANEL * j : PANEL * (j + 1)] = lane_gather(rows[j][tile], first + sub)
+        column = lane_gather(here, jnp.full(shape, 0, jnp.int32) + (first + j))
+        cols_ref[PANEL * j : PANEL * (j + 1)] = column
     d = [[None] * PANEL for _ in range(PANEL)]
     for j in range(PANEL):
         for i in range(j, PANEL):
@@ -314,45 +323,60 @@
     last = first == LANES - PANEL
     next_lane = jnp.where(last, 0, first + PANEL) + sub
     q = [[None] * tiles for _ in range(PANEL)]
+    p = [[None] * tiles for _ in range(PANEL)]
     weights = [None] * PANEL
     factor = [[None] * PANEL for _ in range(PANEL)]
-    for k in range(PANEL):
-        scale = lax.rsqrt(d[k][k])
-        for i in range(k + 1, PANEL):
-            factor[i][k] = d[i][k] * scale
-        for i in range(k + 1, PANEL):
-            for j in range(k + 1, i + 1):
-                d[i][j] = d[i][j] - factor[i][k] * factor[j][k]
+
+    def substitute(k, scale):
         for t in range(tiles):
             value = rows[k][t]
             if t == tile:
                 value = jnp.where(own, jnp.where(lane == first + k, -1.0, 0.0), value)
             for j in range(k):
                 value = value - factor[k][j] * q[j][t]
-            q[k][t] = value * scale
+            q[k][t] = value
+            p[k][t] = value * scale
         source = rows[k][tile]
         if tile + 1 < tiles:
             source = jnp.where(last, rows[k][tile + 1], source)
         value = lane_gather(source, next_lane)
         for j in range(k):
             value = value - factor[k][j] * weights[j]
-        weights[k] = value * scale
-
-    packed = []
-    for t in range(tiles):
-        value = q[0][t]
-        for k in range(1, PANEL):
-            value = jnp.where(sub == k, q[k][t], value)
-        packed.append(value)
-    whole = jnp.concatenate(packed, axis=1) if tiles > 1 else packed[0]
-    high = whole.astype(jnp.bfloat16).astype(jnp.float32)
-    rest = whole - high
-    middle = rest.astype(jnp.bfloat16).astype(jnp.float32)
-    low = rest - middle
-    left = jnp.concatenate([high, high, middle, middle, high, low], axis=0)
-    right = jnp.concatenate([high, middle, high, middle, low, high], axis=0)
-    left_ref[...] = left.astype(jnp.bfloat16)
-    right_ref[...] = right.astype(jnp.bfloat16)
+        weights[k] = value
+
+    for k in range(0, PANEL, 2):
+        m = k + 1
+        a, b, c = d[k][k], d[m][k], d[m][m]
+        first_scale = 1.0 / a
+        second_scale = a * (1.0 / (a * c - b * b))
+        factor[m][k] = b * first_scale
+        left_over = {i: d[i][m] - d[i][k] * factor[m][k] for i in range(k + 2, PANEL)}
+        for i in range(k + 2, PANEL):
+            factor[i][k] = d[i][k] * first_scale
+            factor[i][m] = left_over[i] * second_scale
+        for i in range(k + 2, PANEL):
+            for j in range(k + 2, i + 1):
+                value = d[i][j] - d[i][k] * factor[j][k]
+                d[i][j] = value - (left_over[i] * left_over[j]) * second_scale
+        substitute(k, first_scale)
+        substitute(m, second_scale)
+
+    def packed(values):
+        whole = []
+        for t in range(tiles):
+            value = values[0][t]
+            for k in range(1, PANEL):
+                value = jnp.where(sub == k, values[k][t], value)
+            whole.append(value)
+        return jnp.concatenate(whole, axis=1) if tiles > 1 else whole[0]
+
+    qs, ps = in_three(packed(q)), in_three(packed(p))
+    left_ref[...] = jnp.concatenate([qs[i] for i in (0, 0, 1, 1, 0, 2)], axis=0).astype(
+        jnp.bfloat16
+    )
+    right_ref[...] = jnp.concatenate([ps[i] for i in (0, 1, 0, 1, 2, 0)], axis=0).astype(
+        jnp.bfloat16
+    )
 
     after = pl.multiple_of(base + 2 * PANEL, PANEL)
     following = a_ref[pl.ds(after, PANEL), :]
@@ -362,7 +386,7 @@
         if t == tile:
             value = jnp.where(own, 0.0, value)
         for k in range(PANEL):
-            value = value - weights[k] * q[k][t]
+            value = value - weights[k] * p[k][t]
         result.append(value)
     return jnp.concatenate(result, axis=1) if tiles > 1 else result[0]
 
@@ -448,7 +472,20 @@
     return lax.fori_loop(begin, end, lambda i, panel: sweep_panel(*work, 1, i, panel), panel)
 
 
-def first_kernel(place, total, mine, other, wa, wl, wr, wp, na, nl, nr, np_, *refs):
+def unit_scale(block):
+    row, col = iotas(block.shape)
+    line = jnp.sum(jnp.where(row == col, block, 0.0), axis=0, keepdims=True)
+    return jnp.broadcast_to(lax.rsqrt(line), (PANEL, block.shape[1]))
+
+
+def scaled(block, down, across):
+    columns = jnp.broadcast_to(down[:1], block.shape).T
+    return (block * columns) * jnp.broadcast_to(across[:1], block.shape)
+
+
+def first_kernel(
+    place, total, mine, other, wa, wl, wr, wp, na, nl, nr, np_, ws_ref, ns_ref, *refs
+):
     a_flat, b_flat = refs[:2]
     wide_work, narrow_work = (wa, wl, wr, *refs[2:4]), (na, nl, nr, *refs[4:])
     place_halves(place, (mine, other), 0, a_flat)
@@ -462,23 +499,30 @@
     damp = jnp.where(row == col, DAMP, 0.0)
     clear(wide_work)
     clear(narrow_work)
-    wa[PANEL : PANEL + n, :n] = first / total + damp
+    first, last, square = first / total + damp, last / total + damp, square / total + damp
+    by_first, by_last, by_square = (unit_scale(block) for block in (first, last, square))
+    ws_ref[:, :n] = by_first
+    ws_ref[:, n:] = by_last
+    ns_ref[...] = by_square
+    corner = scaled(corner, by_first, by_last)
+    wa[PANEL : PANEL + n, :n] = scaled(first, by_first, by_first)
     wa[PANEL : PANEL + n, n:] = corner
     wa[PANEL + n : PANEL + 2 * n, :n] = corner.T
-    wa[PANEL + n : PANEL + 2 * n, n:] = last / total + damp
-    na[PANEL : PANEL + n, :] = square / total + damp
+    wa[PANEL + n : PANEL + 2 * n, n:] = scaled(last, by_last, by_last)
+    na[PANEL : PANEL + n, :] = scaled(square, by_square, by_square)
     start = (wa[PANEL : 2 * PANEL, :], na[PANEL : 2 * PANEL, :])
     wp[...], np_[...] = sweep_both(wide_work, narrow_work, 0, FIRST_STEPS, start)
 
 
 def second_kernel(*refs):
-    given, ninv_ref, state, narrow_state, wide_rows, narrow_rows = (
+    given, scale, ninv_ref, state, narrow_state, wide_rows, narrow_rows = (
         refs[:8],
         refs[8],
-        refs[9:13],
-        refs[13:16],
-        refs[16:18],
-        refs[18:],
+        refs[9],
+        refs[10:14],
+        refs[14:17],
+        refs[17:19],
+        refs[19:],
     )
     for source, target in zip((*given[:3], *given[4:7]), (*state[:3], *narrow_state)):
         target[...] = source[...]
@@ -487,18 +531,23 @@
     panels = (given[3][...], given[7][...])
     panel, _ = sweep_both(wide_work, narrow_work, FIRST_STEPS, STEPS, panels)
     trailing_update(*narrow_work[:3], LANES)
-    ninv_ref[...] = -narrow_work[0][PANEL : PANEL + LANES, :]
+    by_square = scale[...]
+    ninv_ref[...] = scaled(-narrow_work[0][PANEL : PANEL + LANES, :], by_square, by_square)
     wp[...] = sweep_wide(wide_work, 0, SECOND_STEPS, panel)
 
 
-def third_kernel(wa_in, wl_in, wr_in, panel_in, winv, wa, wl, wr, *rows):
+def third_kernel(wa_in, wl_in, wr_in, panel_in, scale, winv, wa, wl, wr, *rows):
     wa[...] = wa_in[...]
     wl[...] = wl_in[...]
     wr[...] = wr_in[...]
     sweep_wide((wa, wl, wr, *rows), SECOND_STEPS, STEPS, panel_in[...])
     wide = wa.shape[1]
     trailing_update(wa, wl, wr, wide)
-    winv[...] = -wa[PANEL : PANEL + wide, :]
+    parts = [slice(i, i + LANES) for i in range(0, wide, LANES)]
+    for i in parts:
+        for j in parts:
+            block = -wa[PANEL + i.start : PANEL + i.stop, j]
+            winv[i, j] = scaled(block, scale[:, i], scale[:, j])
 
 
 def state_shapes(size):
@@ -524,7 +573,9 @@
         functools.partial(first_kernel, place, total),
         "first_panels",
         pieces,
-        state_shapes(wide) + state_shapes(narrow),
+        state_shapes(wide)
+        + state_shapes(narrow)
+        + [jax.ShapeDtypeStruct((PANEL, n), jnp.float32) for n in (wide, narrow)],
         [
             pltpu.VMEM((EARLY_ROWS, LANES), jnp.float32),
             pltpu.VMEM((LATE_ROWS, LANES), jnp.float32),
@@ -715,10 +766,11 @@
     if place.extra:
         m = lax.psum(m, place.extra)
     m_got = swap(m, place.far)
-    ninv, *state = second_panels(state, wide, narrow)
+    *state, wide_scale, narrow_scale = state
+    ninv, *state = second_panels([*state, narrow_scale], wide, narrow)
     m = after(m, ninv) + m_got
     m_got = swap(m, place.core)
-    winv = third_panels(state, wide)
+    winv = third_panels([*state, wide_scale], wide)
     cols, own_rows = wide // n_dp, narrow // n_own
     sent = products(place, winv, ninv, [m, m_got], own_rows, total)
     got = lax.all_to_all(sent, (place.near, place.second, place.first), 0, 0)

time: 58.1 us -> 58.1 us (level)
  transfers between devices with their start and end apart: 13 -> 13, of which waited for: 5 -> 5; matrix products, arithmetic and copies ran while one was open for 1% -> 1% of each run, Pallas kernels for 18% -> 19%
where the time goes in v13:
time: 58.1 us; the launch traced here: 57.9 us
  starting transfers between devices  18 us (31%)
  Pallas kernels  16.5 us (28%)
  waiting for transfers between devices  11.6 us (20%)
  blocking collectives  10.4 us (18%)
  between operations  0.84 us (1%)
    ppermute x9, starting transfers between devices, swap(): return lax.ppermute(value, axis, [(0, 1), (1, 0)])  11.5 us
    all_to_all x1, blocking collectives, on_device(): got = lax.all_to_all(sent, (place.near, place.second, place.first), 0, 0)  10.4 us
    pallas_call x3, Pallas kernels, sweep_call(): pl.pallas_call(kernel, in_specs=[VMEM] * len(args), out_specs=[VMEM] * le...  9.42 us
    ppermute x4, waiting for transfers between devices, swap_by_core(): return lax.ppermute(value, (place.second, place.core, place.first), pairs)  8.26 us
    ppermute x4, starting transfers between devices, swap_by_core(): return lax.ppermute(value, (place.second, place.core, place.first), pairs)  6.51 us
    pallas_call x1, Pallas kernels, hot_squares(): pl.pallas_call(functools.partial(hot_kernel, place), in_specs=[HBM, HBM],...  3.62 us
    ppermute x9, waiting for transfers between devices, swap(): return lax.ppermute(value, axis, [(0, 1), (1, 0)])  3.31 us
    pallas_call x1, Pallas kernels, placing(): pl.pallas_call(functools.partial(placing_kernel, place), in_specs=[SMEM,...  1.26 us
  transfers between devices with their start and end apart: 13, of which 5 were waited for; matrix products, arithmetic and copies ran while one was open for 1% of the time, Pallas kernels for 19%

profile of v13, /device:TPU:0, one launch (start us, length us, event | category | flops | bytes accessed | tf_op | source)
XLA Modules:
  0.0 57.9 jit_solution(14459640757723532813)
XLA Ops:
  0.6 3.6 %hot_squares.1 = (f32[3,2,168,128]{3,2,1,0:T(8,128)S(1)}, f32[3,2,168,128]{3,2,1,0:T(8,128)S(1)}, bf16[8,768,256]{2,1,0:T(8,128)(2,1)S(1)}, bf16[8,768,128]{2,1,0:T(8,128)(2,1)S(1)}) custom-call(bf16[8,768,256]{2,1,0:T(8,128)(2,1)} %wide_hbm.1, bf16[8,768,128]{2,1,0:T(8,128)(2,1)} %narrow_hbm.1), custom_call_target="tpu_custom_call" | custom-call | flops 754974720 | bytes 3145728 | tf_op jit(solution)/shard_map/hot_squares/pallas_call | solution.py:226
  4.3 0.5 collective-permute-start
  4.8 0.6 %cold_squares.1 = (f32[2,168,128]{2,1,0:T(8,128)S(1)}, f32[2,168,128]{2,1,0:T(8,128)S(1)}) custom-call(bf16[8,768,256]{2,1,0:T(8,128)(2,1)S(1)} %get-tuple-element.48.wides, bf16[8,768,128]{2,1,0:T(8,128)(2,1)S(1)} %get-tuple-element.41.narrows), custom_call_target="tpu_custom_call" | custom-call | flops 251658240 | bytes 3145728 | tf_op jit(solution)/shard_map/cold_squares/pallas_call | solution.py:248
  5.4 0.6 %collective-permute-done = f32[2,2,168,128]{3,2,1,0:T(8,128)S(1)} collective-permute-done((f32[2,2,168,128]{3,2,1,0:T(8,128)S(1)}, f32[2,2,168,128]{3,2,1,0:T(8,128)S(1)}, u32[]{:S(2)}, u32[]{:S(2)}) %collective-permute-start) | collective-permute-done | bytes 344096 | tf_op jit(solution)/shard_map/ppermute | solution.py:710
  6.2 0.4 collective-permute-start.1
  6.6 2.6 %collective-permute-start.2 = (f32[2,2,168,128]{3,2,1,0:T(8,128)S(1)}, f32[2,2,168,128]{3,2,1,0:T(8,128)S(1)}, u32[]{:S(2)}, u32[]{:S(2)}) collective-permute-start(f32[2,2,168,128]{3,2,1,0:T(8,128)S(1)} %slice_add_fusion), channel_id=1, source_target_pairs={{0,1},{1,0},{2,6},{3,7},{4,5},{5,4},{6,2},{7,3},{8,9},{9,8},{10,14... | collective-permute-start | bytes 1032200 | tf_op jit(solution)/shard_map/ppermute | solution.py:721
  9.2 0.9 %mixed.1 = (f32[4,2,128,128]{3,2,1,0:T(8,128)S(1)}, f32[4,2,128,128]{3,2,1,0:T(8,128)S(1)}) custom-call(bf16[8,768,256]{2,1,0:T(8,128)(2,1)S(1)} %get-tuple-element.48.wides, bf16[8,768,128]{2,1,0:T(8,128)(2,1)S(1)} %get-tuple-element.41.narrows), custom_call_target="tpu_custom_call" | custom-call | flops 402653184 | bytes 3145728 | tf_op jit(solution)/shard_map/mixed/pallas_call | solution.py:263
  10.1 0.2 collective-permute-start.7
  10.3 4.1 %collective-permute-done.2 = f32[2,2,168,128]{3,2,1,0:T(8,128)S(1)} collective-permute-done((f32[2,2,168,128]{3,2,1,0:T(8,128)S(1)}, f32[2,2,168,128]{3,2,1,0:T(8,128)S(1)}, u32[]{:S(2)}, u32[]{:S(2)}) %collective-permute-start.2) | collective-permute-done | bytes 344096 | tf_op jit(solution)/shard_map/ppermute | solution.py:721
  14.5 2.1 %collective-permute-start.3 = (f32[2,168,128]{2,1,0:T(8,128)S(1)}, f32[2,168,128]{2,1,0:T(8,128)S(1)}, u32[]{:S(2)}, u32[]{:S(2)}) collective-permute-start(f32[2,168,128]{2,1,0:T(8,128)S(1)} %slice_bitcast_fusion), channel_id=1, source_target_pairs={{0,4},{1,5},{2,3},{3,2},{4,0},{5,1},{6,7},{7,6},{8,12},{9,13},{10,... | collective-permute-start | bytes 516104 | tf_op jit(solution)/shard_map/ppermute | solution.py:721
  16.8 3.2 %collective-permute-done.3 = f32[2,168,128]{2,1,0:T(8,128)S(1)} collective-permute-done((f32[2,168,128]{2,1,0:T(8,128)S(1)}, f32[2,168,128]{2,1,0:T(8,128)S(1)}, u32[]{:S(2)}, u32[]{:S(2)}) %collective-permute-start.3) | collective-permute-done | bytes 172064 | tf_op jit(solution)/shard_map/ppermute | solution.py:721
  20.1 2.1 %collective-permute-start.4 = (f32[168,128]{1,0:T(8,128)S(1)}, f32[168,128]{1,0:T(8,128)S(1)}, u32[]{:S(2)}, u32[]{:S(2)}) collective-permute-start(f32[168,128]{1,0:T(8,128)S(1)} %slice_bitcast_fusion.4), channel_id=1, source_target_pairs={{0,8},{8,0},{1,9},{9,1},{2,10},{10,2},{3,11},{11,3},{4,12},{12,4},... | collective-permute-start | bytes 258056 | tf_op jit(solution)/shard_map/ppermute | solution.py:710
  22.2 1.0 %collective-permute-done.8 = f32[2,2,128,128]{3,2,1,0:T(8,128)S(1)} collective-permute-done((f32[2,2,128,128]{3,2,1,0:T(8,128)S(1)}, f32[2,2,128,128]{3,2,1,0:T(8,128)S(1)}, u32[]{:S(2)}, u32[]{:S(2)}) %collective-permute-start.8) | collective-permute-done | bytes 262176 | tf_op jit(solution)/shard_map/ppermute | solution.py:721
  23.3 1.7 %collective-permute-start.9 = (f32[2,128,128]{2,1,0:T(8,128)S(1)}, f32[2,128,128]{2,1,0:T(8,128)S(1)}, u32[]{:S(2)}, u32[]{:S(2)}) collective-permute-start(f32[2,128,128]{2,1,0:T(8,128)S(1)} %get-tuple-element.76), channel_id=1, source_target_pairs={{0,1},{1,0},{2,6},{3,7},{4,5},{5,4},{6,2},{7,3},{8,9},{9,8},{10,14... | collective-permute-start | bytes 393224 | tf_op jit(solution)/shard_map/ppermute | solution.py:721
  25.0 2.8 %collective-permute-start.5 = (f32[168,128]{1,0:T(8,128)S(1)}, f32[168,128]{1,0:T(8,128)S(1)}, u32[]{:S(2)}, u32[]{:S(2)}) collective-permute-start(f32[168,128]{1,0:T(8,128)S(1)} %fusion.2), channel_id=1, source_target_pairs={{0,16},{16,0},{1,17},{17,1},{2,18},{18,2},{3,19},{19,3},{4,20},{20... | collective-permute-start | bytes 258056 | tf_op jit(solution)/shard_map/ppermute | solution.py:710
  27.8 2.6 %collective-permute-done.5 = f32[168,128]{1,0:T(8,128)S(1)} collective-permute-done((f32[168,128]{1,0:T(8,128)S(1)}, f32[168,128]{1,0:T(8,128)S(1)}, u32[]{:S(2)}, u32[]{:S(2)}) %collective-permute-start.5) | collective-permute-done | bytes 86048 | tf_op jit(solution)/shard_map/ppermute | solution.py:710
  30.6 1.8 %collective-permute-start.10 = (f32[128,128]{1,0:T(8,128)S(1)}, f32[128,128]{1,0:T(8,128)S(1)}, u32[]{:S(2)}, u32[]{:S(2)}) collective-permute-start(f32[128,128]{1,0:T(8,128)S(1)} %get-tuple-element.78), channel_id=1, source_target_pairs={{0,8},{8,0},{1,9},{9,1},{2,10},{10,2},{3,11},{11,3},{4,12},{12,4},... | collective-permute-start | bytes 196616 | tf_op jit(solution)/shard_map/ppermute | solution.py:710
  32.4 3.4 %first_panels.1 = (f32[272,256]{1,0:T(8,128)S(1)}, bf16[48,256]{1,0:T(8,128)(2,1)S(1)}, bf16[48,256]{1,0:T(8,128)(2,1)S(1)}, f32[8,256]{1,0:T(8,128)S(1)}, f32[1...) custom-call(f32[168,128]{1,0:T(8,128)S(1)} %add.38.mine, ...), custom_call_target="tpu_custom_call" | custom-call | flops 1073741824 | bytes 1048576 | tf_op jit(solution)/shard_map/first_panels/pallas_call | solution.py:559
  35.9 3.4 %collective-permute-start.11 = (f32[128,128]{1,0:T(8,128)S(1)}, f32[128,128]{1,0:T(8,128)S(1)}, u32[]{:S(2)}, u32[]{:S(2)}) collective-permute-start(f32[128,128]{1,0:T(8,128)S(1)} %add.42), channel_id=1, source_target_pairs={{0,16},{16,0},{1,17},{17,1},{2,18},{18,2},{3,19},{19,3},{4,20},{20... | collective-permute-start | bytes 196616 | tf_op jit(solution)/shard_map/ppermute | solution.py:710
  39.3 4.4 %second_panels.1 = (f32[128,128]{1,0:T(8,128)S(1)}, f32[272,256]{1,0:T(8,128)S(1)}, bf16[48,256]{1,0:T(8,128)(2,1)S(1)}, bf16[48,256]{1,0:T(8,128)(2,1)S(1)}, f32[8,256]{1,0:T(8,128)S(1)}) custom-call(f32[272,256]{1,0:T(8,128)S(1)} %get-tuple-element.51.refs_0_, bf16[48,256]{1,0:T(8,128)(2,1)S(1)} %get-tuple-element.52.refs_1_, ...), custom_call_target="tpu_custom_call" | custom-call | flops 1073741824 | bytes 1048576 | tf_op jit(solution)/shard_map/second_panels/pallas_call | solution.py:559
  43.8 1.6 %third_panels.1.winv = f32[256,256]{1,0:T(8,128)S(1)} custom-call(f32[272,256]{1,0:T(8,128)S(1)} %get-tuple-element.60.wa_in, bf16[48,256]{1,0:T(8,128)(2,1)S(1)} %get-tuple-element.61.wl_in, bf16[48,256]{1,0:T(8,128)(2,1)S(1)} %get-tuple-element.62.wr_in, f32[8,256]{1,0:T(8,128)S(1)} %get-tuple-element.63.panel_in, f32[8,256]{1,0:T(8,128)S(1)} %get-tuple-element.64.scale), custom_call_target="tpu_custom_call" | custom-call | flops 1073741824 | bytes 1048576 | tf_op jit(solution)/shard_map/third_panels/pallas_call | solution.py:559
  45.4 0.7 %products.1 = f32[8,40,128]{2,1,0:T(8,128)S(1)} custom-call(f32[256,256]{1,0:T(8,128)S(1)} %third_panels.1.winv, f32[128,128]{1,0:T(8,128)S(1)} %get-tuple-element.65.ninv_ref, f32[128,128]{1,0:T(8,128)S(1)} %add.43.mine, f32[128,128]{1,0:T(8,128)S(1)} %collective-permute-done.12.other), custom_call_target="tpu_custom_call" | custom-call | tf_op jit(solution)/shard_map/products/pallas_call | solution.py:651
  46.2 10.4 %all_to_all.5.got_ref = f32[8,40,128]{2,1,0:T(8,128)S(1)} all-to-all(f32[8,40,128]{2,1,0:T(8,128)S(1)} %products.1), channel_id=1, replica_groups=mesh['dp0'=2,'dp1'=2,'dp2'=2,'dp3'=2,'own0'=2] {'dp1','dp2','own0'}, dimensions={0} | all-to-all | bytes 327680 | tf_op jit(solution)/shard_map/all_to_all | solution.py:776
  56.6 1.3 %placing.1 = (f32[5,16,256]{2,1,0:T(8,128)}, f32[8,16,64]{2,1,0:T(8,128)}) custom-call(s32[8]{0:T(128)S(1)} %copy-done, f32[8,40,128]{2,1,0:T(8,128)S(1)} %all_to_all.5.got_ref), custom_call_target="tpu_custom_call" | custom-call | tf_op jit(solution)/shard_map/placing/pallas_call | solution.py:696
  (32 shorter events, 0.7 us)
Async XLA Ops:
  4.3 1.8 %collective-permute-start = (f32[2,2,168,128]{3,2,1,0:T(8,128)S(1)}, f32[2,2,168,128]{3,2,1,0:T(8,128)S(1)}, u32[]{:S(2)}, u32[]{:S(2)}) collective-permute-start(f32[2,2,168,128]{3,2,1,0:T(8,128)S(1)} %slice.45), channel_id=1, source_target_pairs={{0,2},{2,0},{1,3},{3,1},{4,6},{6,4},{5,7},{7,5},{8,10},{10,8},{9,1... | collective-permute-start | bytes 1032200 | tf_op jit(solution)/shard_map/ppermute | solution.py:710
  6.2 4.2 %collective-permute-start.1 = (f32[2,2,168,128]{3,2,1,0:T(8,128)S(1)}, f32[2,2,168,128]{3,2,1,0:T(8,128)S(1)}, u32[]{:S(2)}, u32[]{:S(2)}) collective-permute-start(f32[2,2,168,128]{3,2,1,0:T(8,128)S(1)} %pad_maximum_fusion), channel_id=1, source_target_pairs={{0,2},{2,0},{1,3},{3,1},{4,6},{6,4},{5,7},{7,5},{8,10},{10,8},{9,1... | collective-permute-start | bytes 1032200 | tf_op jit(solution)/shard_map/ppermute | solution.py:710
  6.6 7.8 %collective-permute-start.2 = (f32[2,2,168,128]{3,2,1,0:T(8,128)S(1)}, f32[2,2,168,128]{3,2,1,0:T(8,128)S(1)}, u32[]{:S(2)}, u32[]{:S(2)}) collective-permute-start(f32[2,2,168,128]{3,2,1,0:T(8,128)S(1)} %slice_add_fusion), channel_id=1, source_target_pairs={{0,1},{1,0},{2,6},{3,7},{4,5},{5,4},{6,2},{7,3},{8,9},{9,8},{10,14... | collective-permute-start | bytes 1032200 | tf_op jit(solution)/shard_map/ppermute | solution.py:721
  10.1 6.5 %collective-permute-start.7 = (f32[4,2,128,128]{3,2,1,0:T(8,128)S(1)}, f32[4,2,128,128]{3,2,1,0:T(8,128)S(1)}, u32[]{:S(2)}, u32[]{:S(2)}) collective-permute-start(f32[4,2,128,128]{3,2,1,0:T(8,128)S(1)} %get-tuple-element.49), channel_id=1, source_target_pairs={{0,2},{2,0},{1,3},{3,1},{4,6},{6,4},{5,7},{7,5},{8,10},{10,8},{9,1... | collective-permute-start | bytes 1572872 | tf_op jit(solution)/shard_map/ppermute | solution.py:710
  14.5 5.5 %collective-permute-start.3 = (f32[2,168,128]{2,1,0:T(8,128)S(1)}, f32[2,168,128]{2,1,0:T(8,128)S(1)}, u32[]{:S(2)}, u32[]{:S(2)}) collective-permute-start(f32[2,168,128]{2,1,0:T(8,128)S(1)} %slice_bitcast_fusion), channel_id=1, source_target_pairs={{0,4},{1,5},{2,3},{3,2},{4,0},{5,1},{6,7},{7,6},{8,12},{9,13},{10,... | collective-permute-start | bytes 516104 | tf_op jit(solution)/shard_map/ppermute | solution.py:721
  16.8 6.4 %collective-permute-start.8 = (f32[2,2,128,128]{3,2,1,0:T(8,128)S(1)}, f32[2,2,128,128]{3,2,1,0:T(8,128)S(1)}, u32[]{:S(2)}, u32[]{:S(2)}) collective-permute-start(f32[2,2,128,128]{3,2,1,0:T(8,128)S(1)} %get-tuple-element.74), channel_id=1, source_target_pairs={{0,4},{1,5},{2,3},{3,2},{4,0},{5,1},{6,7},{7,6},{8,12},{9,13},{10,... | collective-permute-start | bytes 786440 | tf_op jit(solution)/shard_map/ppermute | solution.py:721
  20.1 4.9 %collective-permute-start.4 = (f32[168,128]{1,0:T(8,128)S(1)}, f32[168,128]{1,0:T(8,128)S(1)}, u32[]{:S(2)}, u32[]{:S(2)}) collective-permute-start(f32[168,128]{1,0:T(8,128)S(1)} %slice_bitcast_fusion.4), channel_id=1, source_target_pairs={{0,8},{8,0},{1,9},{9,1},{2,10},{10,2},{3,11},{11,3},{4,12},{12,4},... | collective-permute-start | bytes 258056 | tf_op jit(solution)/shard_map/ppermute | solution.py:710
  23.3 7.3 %collective-permute-start.9 = (f32[2,128,128]{2,1,0:T(8,128)S(1)}, f32[2,128,128]{2,1,0:T(8,128)S(1)}, u32[]{:S(2)}, u32[]{:S(2)}) collective-permute-start(f32[2,128,128]{2,1,0:T(8,128)S(1)} %get-tuple-element.76), channel_id=1, source_target_pairs={{0,1},{1,0},{2,6},{3,7},{4,5},{5,4},{6,2},{7,3},{8,9},{9,8},{10,14... | collective-permute-start | bytes 393224 | tf_op jit(solution)/shard_map/ppermute | solution.py:721
  25.0 5.4 %collective-permute-start.5 = (f32[168,128]{1,0:T(8,128)S(1)}, f32[168,128]{1,0:T(8,128)S(1)}, u32[]{:S(2)}, u32[]{:S(2)}) collective-permute-start(f32[168,128]{1,0:T(8,128)S(1)} %fusion.2), channel_id=1, source_target_pairs={{0,16},{16,0},{1,17},{17,1},{2,18},{18,2},{3,19},{19,3},{4,20},{20... | collective-permute-start | bytes 258056 | tf_op jit(solution)/shard_map/ppermute | solution.py:710
  30.4 1.9 %collective-permute-start.6 = (f32[168,128]{1,0:T(8,128)S(1)}, f32[168,128]{1,0:T(8,128)S(1)}, u32[]{:S(2)}, u32[]{:S(2)}) collective-permute-start(f32[168,128]{1,0:T(8,128)S(1)} %add.38.mine), channel_id=1, source_target_pairs={{0,2},{2,0},{1,3},{3,1},{4,6},{6,4},{5,7},{7,5},{8,10},{10,8},{9,1... | collective-permute-start | bytes 258056 | tf_op jit(solution)/shard_map/ppermute | solution.py:710
  30.6 5.3 %collective-permute-start.10 = (f32[128,128]{1,0:T(8,128)S(1)}, f32[128,128]{1,0:T(8,128)S(1)}, u32[]{:S(2)}, u32[]{:S(2)}) collective-permute-start(f32[128,128]{1,0:T(8,128)S(1)} %get-tuple-element.78), channel_id=1, source_target_pairs={{0,8},{8,0},{1,9},{9,1},{2,10},{10,2},{3,11},{11,3},{4,12},{12,4},... | collective-permute-start | bytes 196616 | tf_op jit(solution)/shard_map/ppermute | solution.py:710
  35.9 7.8 %collective-permute-start.11 = (f32[128,128]{1,0:T(8,128)S(1)}, f32[128,128]{1,0:T(8,128)S(1)}, u32[]{:S(2)}, u32[]{:S(2)}) collective-permute-start(f32[128,128]{1,0:T(8,128)S(1)} %add.42), channel_id=1, source_target_pairs={{0,16},{16,0},{1,17},{17,1},{2,18},{18,2},{3,19},{19,3},{4,20},{20... | collective-permute-start | bytes 196616 | tf_op jit(solution)/shard_map/ppermute | solution.py:710
  43.7 12.9 %copy-start = (s32[8]{0:T(128)S(1)}, s32[8]{0:T(128)}, u32[]{:S(2)}) copy-start(s32[8]{0:T(128)} %owner_map.1) | copy-start | bytes 100
  43.7 1.7 %collective-permute-start.12 = (f32[128,128]{1,0:T(8,128)S(1)}, f32[128,128]{1,0:T(8,128)S(1)}, u32[]{:S(2)}, u32[]{:S(2)}) collective-permute-start(f32[128,128]{1,0:T(8,128)S(1)} %add.43.mine), channel_id=1, source_target_pairs={{0,2},{2,0},{1,3},{3,1},{4,6},{6,4},{5,7},{7,5},{8,10},{10,8},{9,1... | collective-permute-start | bytes 196616 | tf_op jit(solution)/shard_map/ppermute | solution.py:710

commit v14 on v13

--- a/solution.py
+++ b/solution.py
@@ -11,6 +11,7 @@
 DAMP = 0.5
 LANES = 128
 PANEL = 8
+BLOCK = 2 * PANEL
 VMEM_LIMIT = 48 * 1024 * 1024
 HIGHEST = lax.Precision.HIGHEST
 VMEM = pl.BlockSpec(memory_space=pltpu.VMEM)
@@ -278,12 +279,12 @@
 
 def trailing_update(a_ref, left_ref, right_ref, base):
     size = a_ref.shape[1]
-    a_ref[pl.ds(pl.multiple_of(base, PANEL), PANEL), :] = jnp.zeros((PANEL, size), jnp.float32)
+    a_ref[pl.ds(pl.multiple_of(base, BLOCK), BLOCK), :] = jnp.zeros((BLOCK, size), jnp.float32)
     lane = lax.broadcasted_iota(jnp.int32, (1, size), 1)
-    swept = (lane >= base - PANEL) & (lane < base)
+    swept = (lane >= base - BLOCK) & (lane < base)
     update = transposed_dot(left_ref[...], right_ref[...])
-    a_ref[PANEL : PANEL + size, :] = (
-        jnp.where(swept, 0.0, a_ref[PANEL : PANEL + size, :]) - update
+    a_ref[BLOCK : BLOCK + size, :] = (
+        jnp.where(swept, 0.0, a_ref[BLOCK : BLOCK + size, :]) - update
     )
 
 
@@ -294,16 +295,10 @@
     return high, middle, rest - middle
 
 
-def sweep_panel(a_ref, left_ref, right_ref, rows_ref, cols_ref, tile, step, panel):
-    size = a_ref.shape[1]
-    tiles = size // LANES
-    first = step * PANEL
-    base = tile * LANES + first
-    trailing_update(a_ref, left_ref, right_ref, base)
-
+def factor_panel(rows_ref, cols_ref, tile, first, panel, targets):
+    tiles = panel.shape[1] // LANES
     shape = (PANEL, LANES)
-    sub = lax.broadcasted_iota(jnp.int32, shape, 0)
-    lane = lax.broadcasted_iota(jnp.int32, shape, 1)
+    _, lane = iotas(shape)
 
     def on_all(ref, k, lanes):
         return jnp.broadcast_to(ref[k : k + 1, lanes], shape)
@@ -320,11 +315,9 @@
         for i in range(j, PANEL):
             d[i][j] = on_all(cols_ref, PANEL * j + i, slice(None))
     own = (lane >= first) & (lane < first + PANEL)
-    last = first == LANES - PANEL
-    next_lane = jnp.where(last, 0, first + PANEL) + sub
     q = [[None] * tiles for _ in range(PANEL)]
     p = [[None] * tiles for _ in range(PANEL)]
-    weights = [None] * PANEL
+    weights = [[None] * PANEL for _ in targets]
     factor = [[None] * PANEL for _ in range(PANEL)]
 
     def substitute(k, scale):
@@ -336,13 +329,12 @@
                 value = value - factor[k][j] * q[j][t]
             q[k][t] = value
             p[k][t] = value * scale
-        source = rows[k][tile]
-        if tile + 1 < tiles:
-            source = jnp.where(last, rows[k][tile + 1], source)
-        value = lane_gather(source, next_lane)
-        for j in range(k):
-            value = value - factor[k][j] * weights[j]
-        weights[k] = value
+        for target, weight in zip(targets, weights):
+            source, index = target(rows[k])
+            value = lane_gather(source, index)
+            for j in range(k):
+                value = value - factor[k][j] * weight[j]
+            weight[k] = value
 
     for k in range(0, PANEL, 2):
         m = k + 1
@@ -360,35 +352,91 @@
                 d[i][j] = value - (left_over[i] * left_over[j]) * second_scale
         substitute(k, first_scale)
         substitute(m, second_scale)
-
-    def packed(values):
-        whole = []
-        for t in range(tiles):
-            value = values[0][t]
-            for k in range(1, PANEL):
-                value = jnp.where(sub == k, values[k][t], value)
-            whole.append(value)
-        return jnp.concatenate(whole, axis=1) if tiles > 1 else whole[0]
-
-    qs, ps = in_three(packed(q)), in_three(packed(p))
-    left_ref[...] = jnp.concatenate([qs[i] for i in (0, 0, 1, 1, 0, 2)], axis=0).astype(
-        jnp.bfloat16
-    )
-    right_ref[...] = jnp.concatenate([ps[i] for i in (0, 1, 0, 1, 2, 0)], axis=0).astype(
-        jnp.bfloat16
-    )
-
-    after = pl.multiple_of(base + 2 * PANEL, PANEL)
-    following = a_ref[pl.ds(after, PANEL), :]
+    return q, p, weights
+
+
+def packed_rows(values):
+    sub, _ = iotas((PANEL, LANES))
+    whole = []
+    for t in range(len(values[0])):
+        value = values[0][t]
+        for k in range(1, PANEL):
+            value = jnp.where(sub == k, values[k][t], value)
+        whole.append(value)
+    return whole
+
+
+def side_by_side(tiles):
+    return jnp.concatenate(tiles, axis=1) if len(tiles) > 1 else tiles[0]
+
+
+def sweep_block(a_ref, left_ref, right_ref, a_rows, a_cols, b_rows, b_cols, tile, step, block):
+    size = a_ref.shape[1]
+    tiles = size // LANES
+    first = step * BLOCK
+    second = first + PANEL
+    base = tile * LANES + first
+    trailing_update(a_ref, left_ref, right_ref, base)
+
+    sub, lane = iotas((PANEL, LANES))
+    last = first == LANES - BLOCK
+    next_first = jnp.where(last, 0, first + BLOCK)
+
+    def in_block(row):
+        return row[tile], second + sub
+
+    def in_next(offset):
+        def target(row):
+            source = row[tile]
+            if tile + 1 < tiles:
+                source = jnp.where(last, row[tile + 1], source)
+            return source, next_first + offset + sub
+
+        return target
+
+    nexts = [in_next(0), in_next(PANEL)]
+    in_a = (lane >= first) & (lane < second)
+    in_b = (lane >= second) & (lane < second + PANEL)
+
+    def swept(tiles_of, mask):
+        return [jnp.where(mask, 0.0, v) if t == tile else v for t, v in enumerate(tiles_of)]
+
+    def minus(tiles_of, weight, p):
+        result = []
+        for t, value in enumerate(tiles_of):
+            for k in range(PANEL):
+                value = value - weight[k] * p[k][t]
+            result.append(value)
+        return result
+
+    def by_tile(rows):
+        return [rows[:, LANES * t : LANES * (t + 1)] for t in range(tiles)]
+
+    qa, pa, (to_b, *to_next_a) = factor_panel(
+        a_rows, a_cols, tile, first, block[:PANEL], [in_block, *nexts]
+    )
+    panel_b = side_by_side(minus(swept(by_tile(block[PANEL:]), in_a), to_b, pa))
+    qb, pb, to_next_b = factor_panel(b_rows, b_cols, tile, second, panel_b, nexts)
+
+    left, right = [], []
+    for q, p, mask in ((qa, pa, in_b), (qb, pb, None)):
+        q, p = packed_rows(q), packed_rows(p)
+        if mask is not None:
+            q, p = swept(q, mask), swept(p, mask)
+        qs, ps = in_three(side_by_side(q)), in_three(side_by_side(p))
+        left += [qs[i] for i in (0, 0, 1, 1, 0, 2)]
+        right += [ps[i] for i in (0, 1, 0, 1, 2, 0)]
+    left_ref[...] = jnp.concatenate(left, axis=0).astype(jnp.bfloat16)
+    right_ref[...] = jnp.concatenate(right, axis=0).astype(jnp.bfloat16)
+
+    following = a_ref[pl.ds(pl.multiple_of(base + 2 * BLOCK, BLOCK), BLOCK), :]
     result = []
-    for t in range(tiles):
-        value = following[:, LANES * t : LANES * (t + 1)]
-        if t == tile:
-            value = jnp.where(own, 0.0, value)
-        for k in range(PANEL):
-            value = value - weights[k] * p[k][t]
-        result.append(value)
-    return jnp.concatenate(result, axis=1) if tiles > 1 else result[0]
+    for g in range(2):
+        rows = by_tile(following[g * PANEL : (g + 1) * PANEL])
+        rows = minus(swept(rows, in_a), to_next_a[g], pa)
+        rows = minus(swept(rows, in_b), to_next_b[g], pb)
+        result.append(side_by_side(rows))
+    return jnp.concatenate(result, axis=0)
 
 
 def place_halves(place, pieces, first_row, flat):
@@ -406,16 +454,16 @@
 def clear(work):
     a_ref, left, right = work[:3]
     size = a_ref.shape[1]
-    a_ref[:PANEL] = jnp.zeros((PANEL, size), jnp.float32)
-    a_ref[PANEL + size :] = jnp.zeros((PANEL, size), jnp.float32)
+    a_ref[:BLOCK] = jnp.zeros((BLOCK, size), jnp.float32)
+    a_ref[BLOCK + size :] = jnp.zeros((BLOCK, size), jnp.float32)
     left[...] = jnp.zeros(left.shape, left.dtype)
     right[...] = jnp.zeros(right.shape, right.dtype)
 
 
 def work_shapes(size):
-    splits = 6 * PANEL
+    splits = 6 * BLOCK
     return [
-        pltpu.VMEM((size + 2 * PANEL, size), jnp.float32),
+        pltpu.VMEM((size + 2 * BLOCK, size), jnp.float32),
         pltpu.VMEM((splits, size), jnp.bfloat16),
         pltpu.VMEM((splits, size), jnp.bfloat16),
     ]
@@ -425,7 +473,7 @@
     return [
         pltpu.VMEM((PANEL, size), jnp.float32),
         pltpu.VMEM((PANEL * PANEL, LANES), jnp.float32),
-    ]
+    ] * 2
 
 
 def aligned_rows(ref, index, count):
@@ -453,23 +501,23 @@
     )
 
 
-STEPS = LANES // PANEL
-FIRST_STEPS = 10
-SECOND_STEPS = 10
-
-
-def sweep_both(wide_work, narrow_work, begin, end, panels):
-    def step(i, panels):
+STEPS = LANES // BLOCK
+FIRST_STEPS = 5
+SECOND_STEPS = 5
+
+
+def sweep_both(wide_work, narrow_work, begin, end, blocks):
+    def step(i, blocks):
         return (
-            sweep_panel(*wide_work, 0, i, panels[0]),
-            sweep_panel(*narrow_work, 0, i, panels[1]),
+            sweep_block(*wide_work, 0, i, blocks[0]),
+            sweep_block(*narrow_work, 0, i, blocks[1]),
         )
 
-    return lax.fori_loop(begin, end, step, panels)
-
-
-def sweep_wide(work, begin, end, panel):
-    return lax.fori_loop(begin, end, lambda i, panel: sweep_panel(*work, 1, i, panel), panel)
+    return lax.fori_loop(begin, end, step, blocks)
+
+
+def sweep_wide(work, begin, end, block):
+    return lax.fori_loop(begin, end, lambda i, block: sweep_block(*work, 1, i, block), block)
 
 
 def unit_scale(block):
@@ -487,7 +535,7 @@
     place, total, mine, other, wa, wl, wr, wp, na, nl, nr, np_, ws_ref, ns_ref, *refs
 ):
     a_flat, b_flat = refs[:2]
-    wide_work, narrow_work = (wa, wl, wr, *refs[2:4]), (na, nl, nr, *refs[4:])
+    wide_work, narrow_work = (wa, wl, wr, *refs[2:6]), (na, nl, nr, *refs[6:])
     place_halves(place, (mine, other), 0, a_flat)
     place_halves(place, (mine, other), a_flat.shape[0] // 2, b_flat)
     n = LANES
@@ -505,12 +553,12 @@
     ws_ref[:, n:] = by_last
     ns_ref[...] = by_square
     corner = scaled(corner, by_first, by_last)
-    wa[PANEL : PANEL + n, :n] = scaled(first, by_first, by_first)
-    wa[PANEL : PANEL + n, n:] = corner
-    wa[PANEL + n : PANEL + 2 * n, :n] = corner.T
-    wa[PANEL + n : PANEL + 2 * n, n:] = scaled(last, by_last, by_last)
-    na[PANEL : PANEL + n, :] = scaled(square, by_square, by_square)
-    start = (wa[PANEL : 2 * PANEL, :], na[PANEL : 2 * PANEL, :])
+    wa[BLOCK : BLOCK + n, :n] = scaled(first, by_first, by_first)
+    wa[BLOCK : BLOCK + n, n:] = corner
+    wa[BLOCK + n : BLOCK + 2 * n, :n] = corner.T
+    wa[BLOCK + n : BLOCK + 2 * n, n:] = scaled(last, by_last, by_last)
+    na[BLOCK : BLOCK + n, :] = scaled(square, by_square, by_square)
+    start = (wa[BLOCK : 2 * BLOCK, :], na[BLOCK : 2 * BLOCK, :])
     wp[...], np_[...] = sweep_both(wide_work, narrow_work, 0, FIRST_STEPS, start)
 
 
@@ -521,8 +569,8 @@
         refs[9],
         refs[10:14],
         refs[14:17],
-        refs[17:19],
-        refs[19:],
+        refs[17:21],
+        refs[21:],
     )
     for source, target in zip((*given[:3], *given[4:7]), (*state[:3], *narrow_state)):
         target[...] = source[...]
@@ -532,7 +580,7 @@
     panel, _ = sweep_both(wide_work, narrow_work, FIRST_STEPS, STEPS, panels)
     trailing_update(*narrow_work[:3], LANES)
     by_square = scale[...]
-    ninv_ref[...] = scaled(-narrow_work[0][PANEL : PANEL + LANES, :], by_square, by_square)
+    ninv_ref[...] = scaled(-narrow_work[0][BLOCK : BLOCK + LANES, :], by_square, by_square)
     wp[...] = sweep_wide(wide_work, 0, SECOND_STEPS, panel)
 
 
@@ -546,13 +594,13 @@
     parts = [slice(i, i + LANES) for i in range(0, wide, LANES)]
     for i in parts:
         for j in parts:
-            block = -wa[PANEL + i.start : PANEL + i.stop, j]
+            block = -wa[BLOCK + i.start : BLOCK + i.stop, j]
             winv[i, j] = scaled(block, scale[:, i], scale[:, j])
 
 
 def state_shapes(size):
     shapes = [jax.ShapeDtypeStruct(v.shape, v.dtype) for v in work_shapes(size)]
-    return shapes + [jax.ShapeDtypeStruct((PANEL, size), jnp.float32)]
+    return shapes + [jax.ShapeDtypeStruct((BLOCK, size), jnp.float32)]
 
 
 def sweep_call(kernel, name, args, out_shapes, scratch):

time: 58.1 us -> 57.2 us (0.985)
  Pallas kernels: 16.5 us -> 15.6 us
    pallas_call x3, Pallas kernels: 9.42 us -> 8.45 us  [sweep_call(): pl.pallas_call(kernel, in_specs=[VMEM] * len(args), out_specs=[VMEM] * le...]
  transfers between devices with their start and end apart: 13 -> 13, of which waited for: 5 -> 5; matrix products, arithmetic and copies ran while one was open for 1% -> 1% of each run, Pallas kernels for 19% -> 17%
where the time goes in v14:
time: 57.2 us; the launch traced here: 57 us
  starting transfers between devices  18 us (31%)
  Pallas kernels  15.6 us (27%)
  waiting for transfers between devices  11.6 us (20%)
  blocking collectives  10.6 us (19%)
  between operations  0.84 us (1%)
    ppermute x9, starting transfers between devices, swap(): return lax.ppermute(value, axis, [(0, 1), (1, 0)])  11.5 us
    all_to_all x1, blocking collectives, on_device(): got = lax.all_to_all(sent, (place.near, place.second, place.first), 0, 0)  10.6 us
    pallas_call x3, Pallas kernels, sweep_call(): pl.pallas_call(kernel, in_specs=[VMEM] * len(args), out_specs=[VMEM] * le...  8.45 us
    ppermute x4, waiting for transfers between devices, swap_by_core(): return lax.ppermute(value, (place.second, place.core, place.first), pairs)  8.26 us
    ppermute x4, starting transfers between devices, swap_by_core(): return lax.ppermute(value, (place.second, place.core, place.first), pairs)  6.51 us
    pallas_call x1, Pallas kernels, hot_squares(): pl.pallas_call(functools.partial(hot_kernel, place), in_specs=[HBM, HBM],...  3.62 us
    ppermute x9, waiting for transfers between devices, swap(): return lax.ppermute(value, axis, [(0, 1), (1, 0)])  3.31 us
    pallas_call x1, Pallas kernels, placing(): pl.pallas_call(functools.partial(placing_kernel, place), in_specs=[SMEM,...  1.26 us
  transfers between devices with their start and end apart: 13, of which 5 were waited for; matrix products, arithmetic and copies ran while one was open for 1% of the time, Pallas kernels for 17%

profile of v14, /device:TPU:0, one launch (start us, length us, event | category | flops | bytes accessed | tf_op | source)
XLA Modules:
  0.0 57.0 jit_solution(12920378580763441791)
XLA Ops:
  0.6 3.6 %hot_squares.1 = (f32[3,2,168,128]{3,2,1,0:T(8,128)S(1)}, f32[3,2,168,128]{3,2,1,0:T(8,128)S(1)}, bf16[8,768,256]{2,1,0:T(8,128)(2,1)S(1)}, bf16[8,768,128]{2,1,0:T(8,128)(2,1)S(1)}) custom-call(bf16[8,768,256]{2,1,0:T(8,128)(2,1)} %wide_hbm.1, bf16[8,768,128]{2,1,0:T(8,128)(2,1)} %narrow_hbm.1), custom_call_target="tpu_custom_call" | custom-call | flops 754974720 | bytes 3145728 | tf_op jit(solution)/shard_map/hot_squares/pallas_call | solution.py:227
  4.3 0.5 collective-permute-start
  4.8 0.6 %cold_squares.1 = (f32[2,168,128]{2,1,0:T(8,128)S(1)}, f32[2,168,128]{2,1,0:T(8,128)S(1)}) custom-call(bf16[8,768,256]{2,1,0:T(8,128)(2,1)S(1)} %get-tuple-element.48.wides, bf16[8,768,128]{2,1,0:T(8,128)(2,1)S(1)} %get-tuple-element.41.narrows), custom_call_target="tpu_custom_call" | custom-call | flops 251658240 | bytes 3145728 | tf_op jit(solution)/shard_map/cold_squares/pallas_call | solution.py:249
  5.4 0.6 %collective-permute-done = f32[2,2,168,128]{3,2,1,0:T(8,128)S(1)} collective-permute-done((f32[2,2,168,128]{3,2,1,0:T(8,128)S(1)}, f32[2,2,168,128]{3,2,1,0:T(8,128)S(1)}, u32[]{:S(2)}, u32[]{:S(2)}) %collective-permute-start) | collective-permute-done | bytes 344096 | tf_op jit(solution)/shard_map/ppermute | solution.py:758
  6.2 0.4 collective-permute-start.1
  6.6 2.6 %collective-permute-start.2 = (f32[2,2,168,128]{3,2,1,0:T(8,128)S(1)}, f32[2,2,168,128]{3,2,1,0:T(8,128)S(1)}, u32[]{:S(2)}, u32[]{:S(2)}) collective-permute-start(f32[2,2,168,128]{3,2,1,0:T(8,128)S(1)} %slice_add_fusion), channel_id=1, source_target_pairs={{0,1},{1,0},{2,6},{3,7},{4,5},{5,4},{6,2},{7,3},{8,9},{9,8},{10,14... | collective-permute-start | bytes 1032200 | tf_op jit(solution)/shard_map/ppermute | solution.py:769
  9.2 0.9 %mixed.1 = (f32[4,2,128,128]{3,2,1,0:T(8,128)S(1)}, f32[4,2,128,128]{3,2,1,0:T(8,128)S(1)}) custom-call(bf16[8,768,256]{2,1,0:T(8,128)(2,1)S(1)} %get-tuple-element.48.wides, bf16[8,768,128]{2,1,0:T(8,128)(2,1)S(1)} %get-tuple-element.41.narrows), custom_call_target="tpu_custom_call" | custom-call | flops 402653184 | bytes 3145728 | tf_op jit(solution)/shard_map/mixed/pallas_call | solution.py:264
  10.1 0.2 collective-permute-start.7
  10.3 4.1 %collective-permute-done.2 = f32[2,2,168,128]{3,2,1,0:T(8,128)S(1)} collective-permute-done((f32[2,2,168,128]{3,2,1,0:T(8,128)S(1)}, f32[2,2,168,128]{3,2,1,0:T(8,128)S(1)}, u32[]{:S(2)}, u32[]{:S(2)}) %collective-permute-start.2) | collective-permute-done | bytes 344096 | tf_op jit(solution)/shard_map/ppermute | solution.py:769
  14.5 2.1 %collective-permute-start.3 = (f32[2,168,128]{2,1,0:T(8,128)S(1)}, f32[2,168,128]{2,1,0:T(8,128)S(1)}, u32[]{:S(2)}, u32[]{:S(2)}) collective-permute-start(f32[2,168,128]{2,1,0:T(8,128)S(1)} %slice_bitcast_fusion), channel_id=1, source_target_pairs={{0,4},{1,5},{2,3},{3,2},{4,0},{5,1},{6,7},{7,6},{8,12},{9,13},{10,... | collective-permute-start | bytes 516104 | tf_op jit(solution)/shard_map/ppermute | solution.py:769
  16.8 3.2 %collective-permute-done.3 = f32[2,168,128]{2,1,0:T(8,128)S(1)} collective-permute-done((f32[2,168,128]{2,1,0:T(8,128)S(1)}, f32[2,168,128]{2,1,0:T(8,128)S(1)}, u32[]{:S(2)}, u32[]{:S(2)}) %collective-permute-start.3) | collective-permute-done | bytes 172064 | tf_op jit(solution)/shard_map/ppermute | solution.py:769
  20.1 2.1 %collective-permute-start.4 = (f32[168,128]{1,0:T(8,128)S(1)}, f32[168,128]{1,0:T(8,128)S(1)}, u32[]{:S(2)}, u32[]{:S(2)}) collective-permute-start(f32[168,128]{1,0:T(8,128)S(1)} %slice_bitcast_fusion.4), channel_id=1, source_target_pairs={{0,8},{8,0},{1,9},{9,1},{2,10},{10,2},{3,11},{11,3},{4,12},{12,4},... | collective-permute-start | bytes 258056 | tf_op jit(solution)/shard_map/ppermute | solution.py:758
  22.2 1.0 %collective-permute-done.8 = f32[2,2,128,128]{3,2,1,0:T(8,128)S(1)} collective-permute-done((f32[2,2,128,128]{3,2,1,0:T(8,128)S(1)}, f32[2,2,128,128]{3,2,1,0:T(8,128)S(1)}, u32[]{:S(2)}, u32[]{:S(2)}) %collective-permute-start.8) | collective-permute-done | bytes 262176 | tf_op jit(solution)/shard_map/ppermute | solution.py:769
  23.3 1.7 %collective-permute-start.9 = (f32[2,128,128]{2,1,0:T(8,128)S(1)}, f32[2,128,128]{2,1,0:T(8,128)S(1)}, u32[]{:S(2)}, u32[]{:S(2)}) collective-permute-start(f32[2,128,128]{2,1,0:T(8,128)S(1)} %get-tuple-element.76), channel_id=1, source_target_pairs={{0,1},{1,0},{2,6},{3,7},{4,5},{5,4},{6,2},{7,3},{8,9},{9,8},{10,14... | collective-permute-start | bytes 393224 | tf_op jit(solution)/shard_map/ppermute | solution.py:769
  25.0 2.8 %collective-permute-start.5 = (f32[168,128]{1,0:T(8,128)S(1)}, f32[168,128]{1,0:T(8,128)S(1)}, u32[]{:S(2)}, u32[]{:S(2)}) collective-permute-start(f32[168,128]{1,0:T(8,128)S(1)} %fusion.2), channel_id=1, source_target_pairs={{0,16},{16,0},{1,17},{17,1},{2,18},{18,2},{3,19},{19,3},{4,20},{20... | collective-permute-start | bytes 258056 | tf_op jit(solution)/shard_map/ppermute | solution.py:758
  27.8 2.6 %collective-permute-done.5 = f32[168,128]{1,0:T(8,128)S(1)} collective-permute-done((f32[168,128]{1,0:T(8,128)S(1)}, f32[168,128]{1,0:T(8,128)S(1)}, u32[]{:S(2)}, u32[]{:S(2)}) %collective-permute-start.5) | collective-permute-done | bytes 86048 | tf_op jit(solution)/shard_map/ppermute | solution.py:758
  30.6 1.8 %collective-permute-start.10 = (f32[128,128]{1,0:T(8,128)S(1)}, f32[128,128]{1,0:T(8,128)S(1)}, u32[]{:S(2)}, u32[]{:S(2)}) collective-permute-start(f32[128,128]{1,0:T(8,128)S(1)} %get-tuple-element.78), channel_id=1, source_target_pairs={{0,8},{8,0},{1,9},{9,1},{2,10},{10,2},{3,11},{11,3},{4,12},{12,4},... | collective-permute-start | bytes 196616 | tf_op jit(solution)/shard_map/ppermute | solution.py:758
  32.4 3.2 %first_panels.1 = (f32[288,256]{1,0:T(8,128)S(1)}, bf16[96,256]{1,0:T(8,128)(2,1)S(1)}, bf16[96,256]{1,0:T(8,128)(2,1)S(1)}, f32[16,256]{1,0:T(8,128)S(1)}, f32[...) custom-call(f32[168,128]{1,0:T(8,128)S(1)} %add.38.mine, ...), custom_call_target="tpu_custom_call" | custom-call | flops 1073741824 | bytes 1048576 | tf_op jit(solution)/shard_map/first_panels/pallas_call | solution.py:607
  35.6 3.4 %collective-permute-start.11 = (f32[128,128]{1,0:T(8,128)S(1)}, f32[128,128]{1,0:T(8,128)S(1)}, u32[]{:S(2)}, u32[]{:S(2)}) collective-permute-start(f32[128,128]{1,0:T(8,128)S(1)} %add.42), channel_id=1, source_target_pairs={{0,16},{16,0},{1,17},{17,1},{2,18},{18,2},{3,19},{19,3},{4,20},{20... | collective-permute-start | bytes 196616 | tf_op jit(solution)/shard_map/ppermute | solution.py:758
  39.1 3.9 %second_panels.1 = (f32[128,128]{1,0:T(8,128)S(1)}, f32[288,256]{1,0:T(8,128)S(1)}, bf16[96,256]{1,0:T(8,128)(2,1)S(1)}, bf16[96,256]{1,0:T(8,128)(2,1)S(1)}, f32[16,256]{1,0:T(8,128)S(1)}) custom-call(f32[288,256]{1,0:T(8,128)S(1)} %get-tuple-element.51.refs_0_, bf16[96,256]{1,0:T(8,128)(2,1)S(1)} %get-tuple-element.52.refs_1_, ...), custom_call_target="tpu_custom_call" | custom-call | flops 1073741824 | bytes 1048576 | tf_op jit(solution)/shard_map/second_panels/pallas_call | solution.py:607
  43.1 1.4 %third_panels.1.winv = f32[256,256]{1,0:T(8,128)S(1)} custom-call(f32[288,256]{1,0:T(8,128)S(1)} %get-tuple-element.60.wa_in, bf16[96,256]{1,0:T(8,128)(2,1)S(1)} %get-tuple-element.61.wl_in, bf16[96,256]{1,0:T(8,128)(2,1)S(1)} %get-tuple-element.62.wr_in, f32[16,256]{1,0:T(8,128)S(1)} %get-tuple-element.63.panel_in, f32[8,256]{1,0:T(8,128)S(1)} %get-tuple-element.64.scale), custom_call_target="tpu_custom_call" | custom-call | flops 1073741824 | bytes 1048576 | tf_op jit(solution)/shard_map/third_panels/pallas_call | solution.py:607
  44.5 0.7 %products.1 = f32[8,40,128]{2,1,0:T(8,128)S(1)} custom-call(f32[256,256]{1,0:T(8,128)S(1)} %third_panels.1.winv, f32[128,128]{1,0:T(8,128)S(1)} %get-tuple-element.65.ninv_ref, f32[128,128]{1,0:T(8,128)S(1)} %add.43.mine, f32[128,128]{1,0:T(8,128)S(1)} %collective-permute-done.12.other), custom_call_target="tpu_custom_call" | custom-call | tf_op jit(solution)/shard_map/products/pallas_call | solution.py:699
  45.2 10.6 %all_to_all.5.got_ref = f32[8,40,128]{2,1,0:T(8,128)S(1)} all-to-all(f32[8,40,128]{2,1,0:T(8,128)S(1)} %products.1), channel_id=1, replica_groups=mesh['dp0'=2,'dp1'=2,'dp2'=2,'dp3'=2,'own0'=2] {'dp1','dp2','own0'}, dimensions={0} | all-to-all | bytes 327680 | tf_op jit(solution)/shard_map/all_to_all | solution.py:824
  55.8 1.3 %placing.1 = (f32[5,16,256]{2,1,0:T(8,128)}, f32[8,16,64]{2,1,0:T(8,128)}) custom-call(s32[8]{0:T(128)S(1)} %copy-done, f32[8,40,128]{2,1,0:T(8,128)S(1)} %all_to_all.5.got_ref), custom_call_target="tpu_custom_call" | custom-call | tf_op jit(solution)/shard_map/placing/pallas_call | solution.py:744
  (32 shorter events, 0.7 us)
Async XLA Ops:
  4.3 1.8 %collective-permute-start = (f32[2,2,168,128]{3,2,1,0:T(8,128)S(1)}, f32[2,2,168,128]{3,2,1,0:T(8,128)S(1)}, u32[]{:S(2)}, u32[]{:S(2)}) collective-permute-start(f32[2,2,168,128]{3,2,1,0:T(8,128)S(1)} %slice.45), channel_id=1, source_target_pairs={{0,2},{2,0},{1,3},{3,1},{4,6},{6,4},{5,7},{7,5},{8,10},{10,8},{9,1... | collective-permute-start | bytes 1032200 | tf_op jit(solution)/shard_map/ppermute | solution.py:758
  6.2 4.2 %collective-permute-start.1 = (f32[2,2,168,128]{3,2,1,0:T(8,128)S(1)}, f32[2,2,168,128]{3,2,1,0:T(8,128)S(1)}, u32[]{:S(2)}, u32[]{:S(2)}) collective-permute-start(f32[2,2,168,128]{3,2,1,0:T(8,128)S(1)} %pad_maximum_fusion), channel_id=1, source_target_pairs={{0,2},{2,0},{1,3},{3,1},{4,6},{6,4},{5,7},{7,5},{8,10},{10,8},{9,1... | collective-permute-start | bytes 1032200 | tf_op jit(solution)/shard_map/ppermute | solution.py:758
  6.6 7.8 %collective-permute-start.2 = (f32[2,2,168,128]{3,2,1,0:T(8,128)S(1)}, f32[2,2,168,128]{3,2,1,0:T(8,128)S(1)}, u32[]{:S(2)}, u32[]{:S(2)}) collective-permute-start(f32[2,2,168,128]{3,2,1,0:T(8,128)S(1)} %slice_add_fusion), channel_id=1, source_target_pairs={{0,1},{1,0},{2,6},{3,7},{4,5},{5,4},{6,2},{7,3},{8,9},{9,8},{10,14... | collective-permute-start | bytes 1032200 | tf_op jit(solution)/shard_map/ppermute | solution.py:769
  10.1 6.5 %collective-permute-start.7 = (f32[4,2,128,128]{3,2,1,0:T(8,128)S(1)}, f32[4,2,128,128]{3,2,1,0:T(8,128)S(1)}, u32[]{:S(2)}, u32[]{:S(2)}) collective-permute-start(f32[4,2,128,128]{3,2,1,0:T(8,128)S(1)} %get-tuple-element.49), channel_id=1, source_target_pairs={{0,2},{2,0},{1,3},{3,1},{4,6},{6,4},{5,7},{7,5},{8,10},{10,8},{9,1... | collective-permute-start | bytes 1572872 | tf_op jit(solution)/shard_map/ppermute | solution.py:758
  14.5 5.5 %collective-permute-start.3 = (f32[2,168,128]{2,1,0:T(8,128)S(1)}, f32[2,168,128]{2,1,0:T(8,128)S(1)}, u32[]{:S(2)}, u32[]{:S(2)}) collective-permute-start(f32[2,168,128]{2,1,0:T(8,128)S(1)} %slice_bitcast_fusion), channel_id=1, source_target_pairs={{0,4},{1,5},{2,3},{3,2},{4,0},{5,1},{6,7},{7,6},{8,12},{9,13},{10,... | collective-permute-start | bytes 516104 | tf_op jit(solution)/shard_map/ppermute | solution.py:769
  16.8 6.4 %collective-permute-start.8 = (f32[2,2,128,128]{3,2,1,0:T(8,128)S(1)}, f32[2,2,128,128]{3,2,1,0:T(8,128)S(1)}, u32[]{:S(2)}, u32[]{:S(2)}) collective-permute-start(f32[2,2,128,128]{3,2,1,0:T(8,128)S(1)} %get-tuple-element.74), channel_id=1, source_target_pairs={{0,4},{1,5},{2,3},{3,2},{4,0},{5,1},{6,7},{7,6},{8,12},{9,13},{10,... | collective-permute-start | bytes 786440 | tf_op jit(solution)/shard_map/ppermute | solution.py:769
  20.1 4.9 %collective-permute-start.4 = (f32[168,128]{1,0:T(8,128)S(1)}, f32[168,128]{1,0:T(8,128)S(1)}, u32[]{:S(2)}, u32[]{:S(2)}) collective-permute-start(f32[168,128]{1,0:T(8,128)S(1)} %slice_bitcast_fusion.4), channel_id=1, source_target_pairs={{0,8},{8,0},{1,9},{9,1},{2,10},{10,2},{3,11},{11,3},{4,12},{12,4},... | collective-permute-start | bytes 258056 | tf_op jit(solution)/shard_map/ppermute | solution.py:758
  23.3 7.3 %collective-permute-start.9 = (f32[2,128,128]{2,1,0:T(8,128)S(1)}, f32[2,128,128]{2,1,0:T(8,128)S(1)}, u32[]{:S(2)}, u32[]{:S(2)}) collective-permute-start(f32[2,128,128]{2,1,0:T(8,128)S(1)} %get-tuple-element.76), channel_id=1, source_target_pairs={{0,1},{1,0},{2,6},{3,7},{4,5},{5,4},{6,2},{7,3},{8,9},{9,8},{10,14... | collective-permute-start | bytes 393224 | tf_op jit(solution)/shard_map/ppermute | solution.py:769
  25.0 5.4 %collective-permute-start.5 = (f32[168,128]{1,0:T(8,128)S(1)}, f32[168,128]{1,0:T(8,128)S(1)}, u32[]{:S(2)}, u32[]{:S(2)}) collective-permute-start(f32[168,128]{1,0:T(8,128)S(1)} %fusion.2), channel_id=1, source_target_pairs={{0,16},{16,0},{1,17},{17,1},{2,18},{18,2},{3,19},{19,3},{4,20},{20... | collective-permute-start | bytes 258056 | tf_op jit(solution)/shard_map/ppermute | solution.py:758
  30.4 1.9 %collective-permute-start.6 = (f32[168,128]{1,0:T(8,128)S(1)}, f32[168,128]{1,0:T(8,128)S(1)}, u32[]{:S(2)}, u32[]{:S(2)}) collective-permute-start(f32[168,128]{1,0:T(8,128)S(1)} %add.38.mine), channel_id=1, source_target_pairs={{0,2},{2,0},{1,3},{3,1},{4,6},{6,4},{5,7},{7,5},{8,10},{10,8},{9,1... | collective-permute-start | bytes 258056 | tf_op jit(solution)/shard_map/ppermute | solution.py:758
  30.6 5.0 %collective-permute-start.10 = (f32[128,128]{1,0:T(8,128)S(1)}, f32[128,128]{1,0:T(8,128)S(1)}, u32[]{:S(2)}, u32[]{:S(2)}) collective-permute-start(f32[128,128]{1,0:T(8,128)S(1)} %get-tuple-element.78), channel_id=1, source_target_pairs={{0,8},{8,0},{1,9},{9,1},{2,10},{10,2},{3,11},{11,3},{4,12},{12,4},... | collective-permute-start | bytes 196616 | tf_op jit(solution)/shard_map/ppermute | solution.py:758
  35.6 7.3 %collective-permute-start.11 = (f32[128,128]{1,0:T(8,128)S(1)}, f32[128,128]{1,0:T(8,128)S(1)}, u32[]{:S(2)}, u32[]{:S(2)}) collective-permute-start(f32[128,128]{1,0:T(8,128)S(1)} %add.42), channel_id=1, source_target_pairs={{0,16},{16,0},{1,17},{17,1},{2,18},{18,2},{3,19},{19,3},{4,20},{20... | collective-permute-start | bytes 196616 | tf_op jit(solution)/shard_map/ppermute | solution.py:758
  43.0 12.8 %copy-start = (s32[8]{0:T(128)S(1)}, s32[8]{0:T(128)}, u32[]{:S(2)}) copy-start(s32[8]{0:T(128)} %owner_map.1) | copy-start | bytes 100
  43.0 1.5 %collective-permute-start.12 = (f32[128,128]{1,0:T(8,128)S(1)}, f32[128,128]{1,0:T(8,128)S(1)}, u32[]{:S(2)}, u32[]{:S(2)}) collective-permute-start(f32[128,128]{1,0:T(8,128)S(1)} %add.43.mine), channel_id=1, source_target_pairs={{0,2},{2,0},{1,3},{3,1},{4,6},{6,4},{5,7},{7,5},{8,10},{10,8},{9,1... | collective-permute-start | bytes 196616 | tf_op jit(solution)/shard_map/ppermute | solution.py:758

commit v15 on v14

--- a/solution.py
+++ b/solution.py
@@ -192,8 +192,19 @@
         put(send, (i // 4,), sent)
 
 
-def mixed_kernel(place, wides, narrows, keep, send, flat):
+def write_slots(place, owner_map, slots_ref):
+    own = place.index(place.own)
+    count = jnp.int32(0)
+    for l in range(slots_ref.shape[0]):
+        mine = owner_map[l] == own
+        slot = jnp.where(mine, count, -1)
+        slots_ref[l] = jnp.full(slots_ref.shape[1:], 0, jnp.int32) + slot
+        count = count + mine.astype(jnp.int32)
+
+
+def mixed_kernel(place, owner_map, wides, narrows, keep, send, slots_ref, flat):
     n = LANES
+    write_slots(place, owner_map, slots_ref)
     for i in range(wides.shape[0]):
         mixed = transposed_dot(narrows[i], wides[i])
         flat[i, :n] = mixed[:, :n]
@@ -258,19 +269,19 @@
     )(wides, narrows)
 
 
-def mixed_sums(place, wides, narrows):
+def mixed_sums(place, owner_map, wides, narrows):
     layers, _, narrow = narrows.shape
     half = jax.ShapeDtypeStruct((4, 2, narrow, LANES), jnp.float32)
     return pl.pallas_call(
         functools.partial(mixed_kernel, place),
-        in_specs=[VMEM, VMEM],
-        out_specs=[VMEM, VMEM],
-        out_shape=[half, half],
+        in_specs=[SMEM, VMEM, VMEM],
+        out_specs=[VMEM] * 3,
+        out_shape=[half, half, jax.ShapeDtypeStruct((layers, PANEL, LANES), jnp.int32)],
         scratch_shapes=[pltpu.VMEM((layers, 2 * narrow, LANES), jnp.float32)],
         cost_estimate=gram_cost(wides, 128),
         compiler_params=PARAMS,
         name="mixed",
-    )(wides, narrows)
+    )(owner_map, wides, narrows)
 
 
 def lane_gather(x, index):
@@ -707,26 +718,24 @@
     )(winv, ninv, *pieces)
 
 
-def placing_kernel(place, owner_map, got_ref, kept_ref, update_ref):
+def placing_kernel(place, slots_ref, got_ref, kept_ref, update_ref):
     layers = got_ref.shape[0]
     slots, cols, wide = kept_ref.shape
     rows = update_ref.shape[2]
     own, dp = place.index(place.own), place.index(place.dp)
-    row, col = iotas((cols, wide))
-    empty = jnp.where(col == row + dp * cols, 1.0 / DAMP, 0.0)
-    count = jnp.int32(0)
-    slot = []
-    for l in range(layers):
-        mine = owner_map[l] == own
-        slot.append(jnp.where(mine, count, -1))
-        count = count + mine.astype(jnp.int32)
-    for h in range(2):
+    step = min(cols, PANEL)
+    row, col = iotas((step, LANES))
+    for h in range(wide // LANES):
         lanes = slice(h * LANES, (h + 1) * LANES)
-        for c in range(slots):
-            value = empty[:, lanes]
-            for l in range(layers):
-                value = jnp.where(slot[l] == c, got_ref[l, h * cols : (h + 1) * cols], value)
-            kept_ref[c, :, lanes] = value
+        for r in range(0, cols, step):
+            here = h * cols + r
+            empty = jnp.where(col + h * LANES == row + dp * cols + r, 1.0 / DAMP, 0.0)
+            for c in range(slots):
+                value = empty
+                for l in range(layers):
+                    taken = slots_ref[l, :step] == c
+                    value = jnp.where(taken, got_ref[l, here : here + step], value)
+                kept_ref[c, r : r + step, lanes] = value
     for l in range(layers):
         value = got_ref[l, 2 * cols :]
         if packs(cols, rows):
@@ -739,11 +748,11 @@
             update_ref[l] = part
 
 
-def placing(place, owner_map, got, wide, cols, slots, rows):
+def placing(place, slots_of, got, wide, cols, slots, rows):
     layers = got.shape[0]
     return pl.pallas_call(
         functools.partial(placing_kernel, place),
-        in_specs=[SMEM, VMEM],
+        in_specs=[VMEM, VMEM],
         out_specs=[VMEM, VMEM],
         out_shape=[
             jax.ShapeDtypeStruct((slots, cols, wide), jnp.float32),
@@ -751,7 +760,7 @@
         ],
         compiler_params=PARAMS,
         name="placing",
-    )(owner_map, got)
+    )(slots_of, got)
 
 
 def swap(value, axis):
@@ -786,12 +795,11 @@
 
     hot = h_keep[:2] + h_got
     s_got = swap_by_core(hot, place, 0)
-    c_got = swap(after(jnp.stack([c_send, h_send[2]]), hot), place.core)
-    m_keep, m_send = mixed_sums(place, after(wides, hot), narrows)
+    m_keep, m_send, slots_of = mixed_sums(place, owner_map, after(wides, hot), narrows)
+    c_got = swap(after(jnp.stack([c_send, h_send[2]]), m_send), place.core)
     m_got = swap(m_send, place.core)
-    s = jnp.stack([c_keep, h_keep[2]]) + after(c_got, m_send)
-
-    s = s + s_got
+    s = jnp.stack([c_keep, h_keep[2]]) + s_got
+    s = s + after(c_got, s)
     s_got = swap_by_core(s[1], place, 1)
     m = after(m_keep, s) + m_got
     m_got = swap_by_core(m[2:], place, 1)
@@ -823,7 +831,7 @@
     sent = products(place, winv, ninv, [m, m_got], own_rows, total)
     got = lax.all_to_all(sent, (place.near, place.second, place.first), 0, 0)
     kept, update = placing(
-        place, owner_map, got, wide, cols, layers // n_own + 1, own_rows
+        place, slots_of, got, wide, cols, layers // n_own + 1, own_rows
     )
     return (jnp.swapaxes(kept, 1, 2), jnp.swapaxes(update, 1, 2))
 

time: 57.2 us -> 56.5 us (0.988)
  waiting for transfers between devices: 11.6 us -> 10.6 us
    ppermute x4, waiting for transfers between devices: 8.26 us -> 7.23 us  [swap_by_core(): return lax.ppermute(value, (place.second, place.core, place.first), pairs)]
  transfers between devices with their start and end apart: 13 -> 13, of which waited for: 5 -> 5; matrix products, arithmetic and copies ran while one was open for 1% -> 1% of each run, Pallas kernels for 17% -> 19%
where the time goes in v15:
time: 56.5 us; the launch traced here: 56.3 us
  starting transfers between devices  18.3 us (32%)
  Pallas kernels  15.6 us (28%)
  waiting for transfers between devices  10.6 us (19%)
  blocking collectives  10.6 us (19%)
  between operations  0.84 us (1%)
    ppermute x9, starting transfers between devices, swap(): return lax.ppermute(value, axis, [(0, 1), (1, 0)])  11.5 us
    all_to_all x1, blocking collectives, on_device(): got = lax.all_to_all(sent, (place.near, place.second, place.first), 0, 0)  10.6 us
    pallas_call x3, Pallas kernels, sweep_call(): pl.pallas_call(kernel, in_specs=[VMEM] * len(args), out_specs=[VMEM] * le...  8.46 us
    ppermute x4, waiting for transfers between devices, swap_by_core(): return lax.ppermute(value, (place.second, place.core, place.first), pairs)  7.23 us
    ppermute x4, starting transfers between devices, swap_by_core(): return lax.ppermute(value, (place.second, place.core, place.first), pairs)  6.81 us
    pallas_call x1, Pallas kernels, hot_squares(): pl.pallas_call(functools.partial(hot_kernel, place), in_specs=[HBM, HBM],...  3.64 us
    ppermute x9, waiting for transfers between devices, swap(): return lax.ppermute(value, axis, [(0, 1), (1, 0)])  3.35 us
    pallas_call x1, Pallas kernels, mixed_sums(): pl.pallas_call(functools.partial(mixed_kernel, place), in_specs=[SMEM, VM...  1.45 us
  transfers between devices with their start and end apart: 13, of which 5 were waited for; matrix products, arithmetic and copies ran while one was open for 1% of the time, Pallas kernels for 19%

profile of v15, /device:TPU:0, one launch (start us, length us, event | category | flops | bytes accessed | tf_op | source)
XLA Modules:
  0.0 56.3 jit_solution(9608591653409155066)
XLA Ops:
  0.6 3.6 %hot_squares.1 = (f32[3,2,168,128]{3,2,1,0:T(8,128)S(1)}, f32[3,2,168,128]{3,2,1,0:T(8,128)S(1)}, bf16[8,768,256]{2,1,0:T(8,128)(2,1)S(1)}, bf16[8,768,128]{2,1,0:T(8,128)(2,1)S(1)}) custom-call(bf16[8,768,256]{2,1,0:T(8,128)(2,1)} %wide_hbm.1, bf16[8,768,128]{2,1,0:T(8,128)(2,1)} %narrow_hbm.1), custom_call_target="tpu_custom_call" | custom-call | flops 754974720 | bytes 3145728 | tf_op jit(solution)/shard_map/hot_squares/pallas_call | solution.py:238
  4.3 0.5 collective-permute-start
  4.8 0.6 %cold_squares.1 = (f32[2,168,128]{2,1,0:T(8,128)S(1)}, f32[2,168,128]{2,1,0:T(8,128)S(1)}) custom-call(bf16[8,768,256]{2,1,0:T(8,128)(2,1)S(1)} %get-tuple-element.46.wides, bf16[8,768,128]{2,1,0:T(8,128)(2,1)S(1)} %get-tuple-element.43.narrows), custom_call_target="tpu_custom_call" | custom-call | flops 251658240 | bytes 3145728 | tf_op jit(solution)/shard_map/cold_squares/pallas_call | solution.py:260
  5.4 0.7 %collective-permute-done = f32[2,2,168,128]{3,2,1,0:T(8,128)S(1)} collective-permute-done((f32[2,2,168,128]{3,2,1,0:T(8,128)S(1)}, f32[2,2,168,128]{3,2,1,0:T(8,128)S(1)}, u32[]{:S(2)}, u32[]{:S(2)}) %collective-permute-start) | collective-permute-done | bytes 344096 | tf_op jit(solution)/shard_map/ppermute | solution.py:767
  6.1 2.9 %collective-permute-start.1 = (f32[2,2,168,128]{3,2,1,0:T(8,128)S(1)}, f32[2,2,168,128]{3,2,1,0:T(8,128)S(1)}, u32[]{:S(2)}, u32[]{:S(2)}) collective-permute-start(f32[2,2,168,128]{3,2,1,0:T(8,128)S(1)} %slice_add_fusion), channel_id=1, source_target_pairs={{0,1},{1,0},{2,6},{3,7},{4,5},{5,4},{6,2},{7,3},{8,9},{9,8},{10,14... | collective-permute-start | bytes 1032200 | tf_op jit(solution)/shard_map/ppermute | solution.py:778
  9.1 1.4 %mixed.1 = (f32[4,2,128,128]{3,2,1,0:T(8,128)S(1)}, f32[4,2,128,128]{3,2,1,0:T(8,128)S(1)}, s32[8,8,128]{2,1,0:T(8,128)S(1)}) custom-call(s32[8]{0:T(128)S(1)} %copy-done, bf16[8,768,256]{2,1,0:T(8,128)(2,1)S(1)} %get-tuple-element.46.wides, bf16[8,768,128]{2,1,0:T(8,128)(2,1)S(1)} %get-tuple-element.43.narrows), custom_call_target="tpu_custom_call" | custom-call | flops 402653184 | bytes 3145728 | tf_op jit(solution)/shard_map/mixed/pallas_call | solution.py:275
  10.7 0.6 collective-permute-start.7
  11.2 3.1 %collective-permute-done.1 = f32[2,2,168,128]{3,2,1,0:T(8,128)S(1)} collective-permute-done((f32[2,2,168,128]{3,2,1,0:T(8,128)S(1)}, f32[2,2,168,128]{3,2,1,0:T(8,128)S(1)}, u32[]{:S(2)}, u32[]{:S(2)}) %collective-permute-start.1) | collective-permute-done | bytes 344096 | tf_op jit(solution)/shard_map/ppermute | solution.py:778
  14.4 2.1 %collective-permute-start.3 = (f32[2,168,128]{2,1,0:T(8,128)S(1)}, f32[2,168,128]{2,1,0:T(8,128)S(1)}, u32[]{:S(2)}, u32[]{:S(2)}) collective-permute-start(f32[2,168,128]{2,1,0:T(8,128)S(1)} %slice_bitcast_fusion), channel_id=1, source_target_pairs={{0,4},{1,5},{2,3},{3,2},{4,0},{5,1},{6,7},{7,6},{8,12},{9,13},{10,... | collective-permute-start | bytes 516104 | tf_op jit(solution)/shard_map/ppermute | solution.py:778
  16.6 0.1 collective-permute-start.8
  16.7 3.2 %collective-permute-done.3 = f32[2,168,128]{2,1,0:T(8,128)S(1)} collective-permute-done((f32[2,168,128]{2,1,0:T(8,128)S(1)}, f32[2,168,128]{2,1,0:T(8,128)S(1)}, u32[]{:S(2)}, u32[]{:S(2)}) %collective-permute-start.3) | collective-permute-done | bytes 172064 | tf_op jit(solution)/shard_map/ppermute | solution.py:778
  19.9 2.1 %collective-permute-start.4 = (f32[168,128]{1,0:T(8,128)S(1)}, f32[168,128]{1,0:T(8,128)S(1)}, u32[]{:S(2)}, u32[]{:S(2)}) collective-permute-start(f32[168,128]{1,0:T(8,128)S(1)} %slice_bitcast_fusion.4), channel_id=1, source_target_pairs={{0,8},{8,0},{1,9},{9,1},{2,10},{10,2},{3,11},{11,3},{4,12},{12,4},... | collective-permute-start | bytes 258056 | tf_op jit(solution)/shard_map/ppermute | solution.py:767
  22.1 1.0 %collective-permute-done.8 = f32[2,2,128,128]{3,2,1,0:T(8,128)S(1)} collective-permute-done((f32[2,2,128,128]{3,2,1,0:T(8,128)S(1)}, f32[2,2,128,128]{3,2,1,0:T(8,128)S(1)}, u32[]{:S(2)}, u32[]{:S(2)}) %collective-permute-start.8) | collective-permute-done | bytes 262176 | tf_op jit(solution)/shard_map/ppermute | solution.py:778
  23.1 1.7 %collective-permute-start.9 = (f32[2,128,128]{2,1,0:T(8,128)S(1)}, f32[2,128,128]{2,1,0:T(8,128)S(1)}, u32[]{:S(2)}, u32[]{:S(2)}) collective-permute-start(f32[2,128,128]{2,1,0:T(8,128)S(1)} %get-tuple-element.78), channel_id=1, source_target_pairs={{0,1},{1,0},{2,6},{3,7},{4,5},{5,4},{6,2},{7,3},{8,9},{9,8},{10,14... | collective-permute-start | bytes 393224 | tf_op jit(solution)/shard_map/ppermute | solution.py:778
  24.9 2.8 %collective-permute-start.5 = (f32[168,128]{1,0:T(8,128)S(1)}, f32[168,128]{1,0:T(8,128)S(1)}, u32[]{:S(2)}, u32[]{:S(2)}) collective-permute-start(f32[168,128]{1,0:T(8,128)S(1)} %fusion.1), channel_id=1, source_target_pairs={{0,16},{16,0},{1,17},{17,1},{2,18},{18,2},{3,19},{19,3},{4,20},{20... | collective-permute-start | bytes 258056 | tf_op jit(solution)/shard_map/ppermute | solution.py:767
  27.7 2.6 %collective-permute-done.5 = f32[168,128]{1,0:T(8,128)S(1)} collective-permute-done((f32[168,128]{1,0:T(8,128)S(1)}, f32[168,128]{1,0:T(8,128)S(1)}, u32[]{:S(2)}, u32[]{:S(2)}) %collective-permute-start.5) | collective-permute-done | bytes 86048 | tf_op jit(solution)/shard_map/ppermute | solution.py:767
  30.5 1.8 %collective-permute-start.10 = (f32[128,128]{1,0:T(8,128)S(1)}, f32[128,128]{1,0:T(8,128)S(1)}, u32[]{:S(2)}, u32[]{:S(2)}) collective-permute-start(f32[128,128]{1,0:T(8,128)S(1)} %get-tuple-element.80), channel_id=1, source_target_pairs={{0,8},{8,0},{1,9},{9,1},{2,10},{10,2},{3,11},{11,3},{4,12},{12,4},... | collective-permute-start | bytes 196616 | tf_op jit(solution)/shard_map/ppermute | solution.py:767
  32.3 3.2 %first_panels.1 = (f32[288,256]{1,0:T(8,128)S(1)}, bf16[96,256]{1,0:T(8,128)(2,1)S(1)}, bf16[96,256]{1,0:T(8,128)(2,1)S(1)}, f32[16,256]{1,0:T(8,128)S(1)}, f32[...) custom-call(f32[168,128]{1,0:T(8,128)S(1)} %add.38.mine, ...), custom_call_target="tpu_custom_call" | custom-call | flops 1073741824 | bytes 1048576 | tf_op jit(solution)/shard_map/first_panels/pallas_call | solution.py:618
  35.5 3.4 %collective-permute-start.11 = (f32[128,128]{1,0:T(8,128)S(1)}, f32[128,128]{1,0:T(8,128)S(1)}, u32[]{:S(2)}, u32[]{:S(2)}) collective-permute-start(f32[128,128]{1,0:T(8,128)S(1)} %add.42), channel_id=1, source_target_pairs={{0,16},{16,0},{1,17},{17,1},{2,18},{18,2},{3,19},{19,3},{4,20},{20... | collective-permute-start | bytes 196616 | tf_op jit(solution)/shard_map/ppermute | solution.py:767
  39.0 3.9 %second_panels.1 = (f32[128,128]{1,0:T(8,128)S(1)}, f32[288,256]{1,0:T(8,128)S(1)}, bf16[96,256]{1,0:T(8,128)(2,1)S(1)}, bf16[96,256]{1,0:T(8,128)(2,1)S(1)}, f32[16,256]{1,0:T(8,128)S(1)}) custom-call(f32[288,256]{1,0:T(8,128)S(1)} %get-tuple-element.53.refs_0_, bf16[96,256]{1,0:T(8,128)(2,1)S(1)} %get-tuple-element.54.refs_1_, ...), custom_call_target="tpu_custom_call" | custom-call | flops 1073741824 | bytes 1048576 | tf_op jit(solution)/shard_map/second_panels/pallas_call | solution.py:618
  42.9 1.4 %third_panels.1.winv = f32[256,256]{1,0:T(8,128)S(1)} custom-call(f32[288,256]{1,0:T(8,128)S(1)} %get-tuple-element.62.wa_in, bf16[96,256]{1,0:T(8,128)(2,1)S(1)} %get-tuple-element.63.wl_in, bf16[96,256]{1,0:T(8,128)(2,1)S(1)} %get-tuple-element.64.wr_in, f32[16,256]{1,0:T(8,128)S(1)} %get-tuple-element.65.panel_in, f32[8,256]{1,0:T(8,128)S(1)} %get-tuple-element.66.scale), custom_call_target="tpu_custom_call" | custom-call | flops 1073741824 | bytes 1048576 | tf_op jit(solution)/shard_map/third_panels/pallas_call | solution.py:618
  44.3 0.7 %products.1 = f32[8,40,128]{2,1,0:T(8,128)S(1)} custom-call(f32[256,256]{1,0:T(8,128)S(1)} %third_panels.1.winv, f32[128,128]{1,0:T(8,128)S(1)} %get-tuple-element.67.ninv_ref, f32[128,128]{1,0:T(8,128)S(1)} %add.43.mine, f32[128,128]{1,0:T(8,128)S(1)} %collective-permute-done.12.other), custom_call_target="tpu_custom_call" | custom-call | tf_op jit(solution)/shard_map/products/pallas_call | solution.py:710
  45.1 10.6 %all_to_all.5.got_ref = f32[8,40,128]{2,1,0:T(8,128)S(1)} all-to-all(f32[8,40,128]{2,1,0:T(8,128)S(1)} %products.1), channel_id=1, replica_groups=mesh['dp0'=2,'dp1'=2,'dp2'=2,'dp3'=2,'own0'=2] {'dp1','dp2','own0'}, dimensions={0} | all-to-all | bytes 327680 | tf_op jit(solution)/shard_map/all_to_all | solution.py:832
  55.6 0.7 %placing.1 = (f32[5,16,256]{2,1,0:T(8,128)}, f32[8,16,64]{2,1,0:T(8,128)}) custom-call(s32[8,8,128]{2,1,0:T(8,128)S(1)} %get-tuple-element.47.slots_ref, f32[8,40,128]{2,1,0:T(8,128)S(1)} %all_to_all.5.got_ref), custom_call_target="tpu_custom_call" | custom-call | tf_op jit(solution)/shard_map/placing/pallas_call | solution.py:753
  (32 shorter events, 0.7 us)
Async XLA Ops:
  4.3 1.8 %collective-permute-start = (f32[2,2,168,128]{3,2,1,0:T(8,128)S(1)}, f32[2,2,168,128]{3,2,1,0:T(8,128)S(1)}, u32[]{:S(2)}, u32[]{:S(2)}) collective-permute-start(f32[2,2,168,128]{3,2,1,0:T(8,128)S(1)} %slice.43), channel_id=1, source_target_pairs={{0,2},{2,0},{1,3},{3,1},{4,6},{6,4},{5,7},{7,5},{8,10},{10,8},{9,1... | collective-permute-start | bytes 1032200 | tf_op jit(solution)/shard_map/ppermute | solution.py:767
  4.8 4.3 %copy-start = (s32[8]{0:T(128)S(1)}, s32[8]{0:T(128)}, u32[]{:S(2)}) copy-start(s32[8]{0:T(128)} %owner_map.1) | copy-start | bytes 100
  6.1 8.2 %collective-permute-start.1 = (f32[2,2,168,128]{3,2,1,0:T(8,128)S(1)}, f32[2,2,168,128]{3,2,1,0:T(8,128)S(1)}, u32[]{:S(2)}, u32[]{:S(2)}) collective-permute-start(f32[2,2,168,128]{3,2,1,0:T(8,128)S(1)} %slice_add_fusion), channel_id=1, source_target_pairs={{0,1},{1,0},{2,6},{3,7},{4,5},{5,4},{6,2},{7,3},{8,9},{9,8},{10,14... | collective-permute-start | bytes 1032200 | tf_op jit(solution)/shard_map/ppermute | solution.py:778
  10.6 3.7 %collective-permute-start.2 = (f32[2,2,168,128]{3,2,1,0:T(8,128)S(1)}, f32[2,2,168,128]{3,2,1,0:T(8,128)S(1)}, u32[]{:S(2)}, u32[]{:S(2)}) collective-permute-start(f32[2,2,168,128]{3,2,1,0:T(8,128)S(1)} %pad_maximum_fusion), channel_id=1, source_target_pairs={{0,2},{2,0},{1,3},{3,1},{4,6},{6,4},{5,7},{7,5},{8,10},{10,8},{9,1... | collective-permute-start | bytes 1032200 | tf_op jit(solution)/shard_map/ppermute | solution.py:767
  10.7 5.8 %collective-permute-start.7 = (f32[4,2,128,128]{3,2,1,0:T(8,128)S(1)}, f32[4,2,128,128]{3,2,1,0:T(8,128)S(1)}, u32[]{:S(2)}, u32[]{:S(2)}) collective-permute-start(f32[4,2,128,128]{3,2,1,0:T(8,128)S(1)} %get-tuple-element.50), channel_id=1, source_target_pairs={{0,2},{2,0},{1,3},{3,1},{4,6},{6,4},{5,7},{7,5},{8,10},{10,8},{9,1... | collective-permute-start | bytes 1572872 | tf_op jit(solution)/shard_map/ppermute | solution.py:767
  14.4 5.5 %collective-permute-start.3 = (f32[2,168,128]{2,1,0:T(8,128)S(1)}, f32[2,168,128]{2,1,0:T(8,128)S(1)}, u32[]{:S(2)}, u32[]{:S(2)}) collective-permute-start(f32[2,168,128]{2,1,0:T(8,128)S(1)} %slice_bitcast_fusion), channel_id=1, source_target_pairs={{0,4},{1,5},{2,3},{3,2},{4,0},{5,1},{6,7},{7,6},{8,12},{9,13},{10,... | collective-permute-start | bytes 516104 | tf_op jit(solution)/shard_map/ppermute | solution.py:778
  16.6 6.4 %collective-permute-start.8 = (f32[2,2,128,128]{3,2,1,0:T(8,128)S(1)}, f32[2,2,128,128]{3,2,1,0:T(8,128)S(1)}, u32[]{:S(2)}, u32[]{:S(2)}) collective-permute-start(f32[2,2,128,128]{3,2,1,0:T(8,128)S(1)} %get-tuple-element.76), channel_id=1, source_target_pairs={{0,4},{1,5},{2,3},{3,2},{4,0},{5,1},{6,7},{7,6},{8,12},{9,13},{10,... | collective-permute-start | bytes 786440 | tf_op jit(solution)/shard_map/ppermute | solution.py:778
  19.9 4.9 %collective-permute-start.4 = (f32[168,128]{1,0:T(8,128)S(1)}, f32[168,128]{1,0:T(8,128)S(1)}, u32[]{:S(2)}, u32[]{:S(2)}) collective-permute-start(f32[168,128]{1,0:T(8,128)S(1)} %slice_bitcast_fusion.4), channel_id=1, source_target_pairs={{0,8},{8,0},{1,9},{9,1},{2,10},{10,2},{3,11},{11,3},{4,12},{12,4},... | collective-permute-start | bytes 258056 | tf_op jit(solution)/shard_map/ppermute | solution.py:767
  23.1 7.3 %collective-permute-start.9 = (f32[2,128,128]{2,1,0:T(8,128)S(1)}, f32[2,128,128]{2,1,0:T(8,128)S(1)}, u32[]{:S(2)}, u32[]{:S(2)}) collective-permute-start(f32[2,128,128]{2,1,0:T(8,128)S(1)} %get-tuple-element.78), channel_id=1, source_target_pairs={{0,1},{1,0},{2,6},{3,7},{4,5},{5,4},{6,2},{7,3},{8,9},{9,8},{10,14... | collective-permute-start | bytes 393224 | tf_op jit(solution)/shard_map/ppermute | solution.py:778
  24.9 5.4 %collective-permute-start.5 = (f32[168,128]{1,0:T(8,128)S(1)}, f32[168,128]{1,0:T(8,128)S(1)}, u32[]{:S(2)}, u32[]{:S(2)}) collective-permute-start(f32[168,128]{1,0:T(8,128)S(1)} %fusion.1), channel_id=1, source_target_pairs={{0,16},{16,0},{1,17},{17,1},{2,18},{18,2},{3,19},{19,3},{4,20},{20... | collective-permute-start | bytes 258056 | tf_op jit(solution)/shard_map/ppermute | solution.py:767
  30.3 2.0 %collective-permute-start.6 = (f32[168,128]{1,0:T(8,128)S(1)}, f32[168,128]{1,0:T(8,128)S(1)}, u32[]{:S(2)}, u32[]{:S(2)}) collective-permute-start(f32[168,128]{1,0:T(8,128)S(1)} %add.38.mine), channel_id=1, source_target_pairs={{0,2},{2,0},{1,3},{3,1},{4,6},{6,4},{5,7},{7,5},{8,10},{10,8},{9,1... | collective-permute-start | bytes 258056 | tf_op jit(solution)/shard_map/ppermute | solution.py:767
  30.5 5.0 %collective-permute-start.10 = (f32[128,128]{1,0:T(8,128)S(1)}, f32[128,128]{1,0:T(8,128)S(1)}, u32[]{:S(2)}, u32[]{:S(2)}) collective-permute-start(f32[128,128]{1,0:T(8,128)S(1)} %get-tuple-element.80), channel_id=1, source_target_pairs={{0,8},{8,0},{1,9},{9,1},{2,10},{10,2},{3,11},{11,3},{4,12},{12,4},... | collective-permute-start | bytes 196616 | tf_op jit(solution)/shard_map/ppermute | solution.py:767
  35.5 7.3 %collective-permute-start.11 = (f32[128,128]{1,0:T(8,128)S(1)}, f32[128,128]{1,0:T(8,128)S(1)}, u32[]{:S(2)}, u32[]{:S(2)}) collective-permute-start(f32[128,128]{1,0:T(8,128)S(1)} %add.42), channel_id=1, source_target_pairs={{0,16},{16,0},{1,17},{17,1},{2,18},{18,2},{3,19},{19,3},{4,20},{20... | collective-permute-start | bytes 196616 | tf_op jit(solution)/shard_map/ppermute | solution.py:767
  42.9 1.5 %collective-permute-start.12 = (f32[128,128]{1,0:T(8,128)S(1)}, f32[128,128]{1,0:T(8,128)S(1)}, u32[]{:S(2)}, u32[]{:S(2)}) collective-permute-start(f32[128,128]{1,0:T(8,128)S(1)} %add.43.mine), channel_id=1, source_target_pairs={{0,2},{2,0},{1,3},{3,1},{4,6},{6,4},{5,7},{7,5},{8,10},{10,8},{9,1... | collective-permute-start | bytes 196616 | tf_op jit(solution)/shard_map/ppermute | solution.py:767

commit v16 on v15

--- a/solution.py
+++ b/solution.py
@@ -49,6 +49,9 @@
     )
 
 
+AHEAD = 5
+
+
 def layer_copies(place, sources, buffers, sems):
     layer = place.layer()
     return [
@@ -159,7 +162,7 @@
 def hot_kernel(place, wide_hbm, narrow_hbm, keep, send, wides, narrows, a_flat, b_flat, sems):
     copies = layer_copies(place, (wide_hbm, narrow_hbm), (wides, narrows), sems)
     order = HOT + COLD
-    for i in order:
+    for i in order[:AHEAD]:
         for copy in copies[i]:
             copy.start()
 
@@ -174,9 +177,12 @@
         put(send, (other, z), sent)
 
     before = None
-    for i in order:
+    for at, i in enumerate(order):
         for copy in copies[i]:
             copy.wait()
+        if at + AHEAD < len(order):
+            for copy in copies[order[at + AHEAD]]:
+                copy.start()
         if before is not None:
             pack(*before)
             before = None
@@ -514,7 +520,7 @@
 
 STEPS = LANES // BLOCK
 FIRST_STEPS = 5
-SECOND_STEPS = 5
+SECOND_STEPS = 6
 
 
 def sweep_both(wide_work, narrow_work, begin, end, blocks):
@@ -537,9 +543,13 @@
     return jnp.broadcast_to(lax.rsqrt(line), (PANEL, block.shape[1]))
 
 
+def on_rows(scale):
+    n = scale.shape[1]
+    return jnp.broadcast_to(scale[:1], (n, n))
+
+
 def scaled(block, down, across):
-    columns = jnp.broadcast_to(down[:1], block.shape).T
-    return (block * columns) * jnp.broadcast_to(across[:1], block.shape)
+    return (block * on_rows(down).T) * on_rows(across)
 
 
 def first_kernel(
@@ -563,11 +573,13 @@
     ws_ref[:, :n] = by_first
     ws_ref[:, n:] = by_last
     ns_ref[...] = by_square
-    corner = scaled(corner, by_first, by_last)
-    wa[BLOCK : BLOCK + n, :n] = scaled(first, by_first, by_first)
+    first_across, last_across = on_rows(by_first), on_rows(by_last)
+    first_down, last_down = first_across.T, last_across.T
+    corner = (corner * first_down) * last_across
+    wa[BLOCK : BLOCK + n, :n] = (first * first_down) * first_across
     wa[BLOCK : BLOCK + n, n:] = corner
     wa[BLOCK + n : BLOCK + 2 * n, :n] = corner.T
-    wa[BLOCK + n : BLOCK + 2 * n, n:] = scaled(last, by_last, by_last)
+    wa[BLOCK + n : BLOCK + 2 * n, n:] = (last * last_down) * last_across
     na[BLOCK : BLOCK + n, :] = scaled(square, by_square, by_square)
     start = (wa[BLOCK : 2 * BLOCK, :], na[BLOCK : 2 * BLOCK, :])
     wp[...], np_[...] = sweep_both(wide_work, narrow_work, 0, FIRST_STEPS, start)
@@ -603,10 +615,12 @@
     wide = wa.shape[1]
     trailing_update(wa, wl, wr, wide)
     parts = [slice(i, i + LANES) for i in range(0, wide, LANES)]
-    for i in parts:
-        for j in parts:
+    across = [on_rows(scale[:, i]) for i in parts]
+    down = [block.T for block in across]
+    for i, rows_scale in zip(parts, down):
+        for j, columns_scale in zip(parts, across):
             block = -wa[BLOCK + i.start : BLOCK + i.stop, j]
-            winv[i, j] = scaled(block, scale[:, i], scale[:, j])
+            winv[i, j] = (block * rows_scale) * columns_scale
 
 
 def state_shapes(size):
@@ -678,16 +692,15 @@
     near_stride = 2 ** (len(place.dp) - 2)
     base = place.index(place.dp) - near * near_stride - second * 2
     _, lane = iotas((PANEL, LANES))
-    for j in range(4):
-        index = base + (j // 2) * near_stride + (j % 2) * 2
-        picked = aligned_rows(winv, index, cols)
-        update = lax.dot_general(
-            picked,
-            inner,
-            (((1,), (0,)), ((), ())),
-            precision=HIGHEST,
-            preferred_element_type=jnp.float32,
-        )
+    picks = [
+        aligned_rows(winv, base + (j // 2) * near_stride + (j % 2) * 2, cols) for j in range(4)
+    ]
+    if cols % PANEL == 0:
+        whole = dot(jnp.concatenate(picks, axis=0), inner)
+        updates = [whole[j * cols : (j + 1) * cols] for j in range(4)]
+    else:
+        updates = [dot(picked, inner) for picked in picks]
+    for j, (picked, update) in enumerate(zip(picks, updates)):
         for x in range(2):
             block = 2 * j + x
             out_ref[block, :cols] = picked[:, :LANES]

time: 56.5 us -> 56.5 us (level)
  transfers between devices with their start and end apart: 13 -> 13, of which waited for: 5 -> 6; matrix products, arithmetic and copies ran while one was open for 1% -> 1% of each run, Pallas kernels for 19% -> 19%
where the time goes in v16:
time: 56.5 us; the launch traced here: 56.3 us
  starting transfers between devices  18.3 us (32%)
  Pallas kernels  15.4 us (27%)
  waiting for transfers between devices  10.8 us (19%)
  blocking collectives  10.5 us (19%)
  between operations  0.83 us (1%)
    ppermute x9, starting transfers between devices, swap(): return lax.ppermute(value, axis, [(0, 1), (1, 0)])  11.5 us
    all_to_all x1, blocking collectives, on_device(): got = lax.all_to_all(sent, (place.near, place.second, place.first), 0, 0)  10.5 us
    pallas_call x3, Pallas kernels, sweep_call(): pl.pallas_call(kernel, in_specs=[VMEM] * len(args), out_specs=[VMEM] * le...  8.43 us
    ppermute x4, waiting for transfers between devices, swap_by_core(): return lax.ppermute(value, (place.second, place.core, place.first), pairs)  7.23 us
    ppermute x4, starting transfers between devices, swap_by_core(): return lax.ppermute(value, (place.second, place.core, place.first), pairs)  6.81 us
    pallas_call x1, Pallas kernels, hot_squares(): pl.pallas_call(functools.partial(hot_kernel, place), in_specs=[HBM, HBM],...  3.64 us
    ppermute x9, waiting for transfers between devices, swap(): return lax.ppermute(value, axis, [(0, 1), (1, 0)])  3.58 us
    pallas_call x1, Pallas kernels, mixed_sums(): pl.pallas_call(functools.partial(mixed_kernel, place), in_specs=[SMEM, VM...  1.45 us
  transfers between devices with their start and end apart: 13, of which 6 were waited for; matrix products, arithmetic and copies ran while one was open for 1% of the time, Pallas kernels for 19%

profile of v16, /device:TPU:0, one launch (start us, length us, event | category | flops | bytes accessed | tf_op | source)
XLA Modules:
  0.0 56.3 jit_solution(16318727606630984961)
XLA Ops:
  0.6 3.6 %hot_squares.1 = (f32[3,2,168,128]{3,2,1,0:T(8,128)S(1)}, f32[3,2,168,128]{3,2,1,0:T(8,128)S(1)}, bf16[8,768,256]{2,1,0:T(8,128)(2,1)S(1)}, bf16[8,768,128]{2,1,0:T(8,128)(2,1)S(1)}) custom-call(bf16[8,768,256]{2,1,0:T(8,128)(2,1)} %wide_hbm.1, bf16[8,768,128]{2,1,0:T(8,128)(2,1)} %narrow_hbm.1), custom_call_target="tpu_custom_call" | custom-call | flops 754974720 | bytes 3145728 | tf_op jit(solution)/shard_map/hot_squares/pallas_call | solution.py:244
  4.3 0.5 collective-permute-start
  4.8 0.6 %cold_squares.1 = (f32[2,168,128]{2,1,0:T(8,128)S(1)}, f32[2,168,128]{2,1,0:T(8,128)S(1)}) custom-call(bf16[8,768,256]{2,1,0:T(8,128)(2,1)S(1)} %get-tuple-element.46.wides, bf16[8,768,128]{2,1,0:T(8,128)(2,1)S(1)} %get-tuple-element.43.narrows), custom_call_target="tpu_custom_call" | custom-call | flops 251658240 | bytes 3145728 | tf_op jit(solution)/shard_map/cold_squares/pallas_call | solution.py:266
  5.4 0.7 %collective-permute-done = f32[2,2,168,128]{3,2,1,0:T(8,128)S(1)} collective-permute-done((f32[2,2,168,128]{3,2,1,0:T(8,128)S(1)}, f32[2,2,168,128]{3,2,1,0:T(8,128)S(1)}, u32[]{:S(2)}, u32[]{:S(2)}) %collective-permute-start) | collective-permute-done | bytes 344096 | tf_op jit(solution)/shard_map/ppermute | solution.py:780
  6.2 2.9 %collective-permute-start.1 = (f32[2,2,168,128]{3,2,1,0:T(8,128)S(1)}, f32[2,2,168,128]{3,2,1,0:T(8,128)S(1)}, u32[]{:S(2)}, u32[]{:S(2)}) collective-permute-start(f32[2,2,168,128]{3,2,1,0:T(8,128)S(1)} %slice_add_fusion), channel_id=1, source_target_pairs={{0,1},{1,0},{2,6},{3,7},{4,5},{5,4},{6,2},{7,3},{8,9},{9,8},{10,14... | collective-permute-start | bytes 1032200 | tf_op jit(solution)/shard_map/ppermute | solution.py:791
  9.1 1.4 %mixed.1 = (f32[4,2,128,128]{3,2,1,0:T(8,128)S(1)}, f32[4,2,128,128]{3,2,1,0:T(8,128)S(1)}, s32[8,8,128]{2,1,0:T(8,128)S(1)}) custom-call(s32[8]{0:T(128)S(1)} %copy-done, bf16[8,768,256]{2,1,0:T(8,128)(2,1)S(1)} %get-tuple-element.46.wides, bf16[8,768,128]{2,1,0:T(8,128)(2,1)S(1)} %get-tuple-element.43.narrows), custom_call_target="tpu_custom_call" | custom-call | flops 402653184 | bytes 3145728 | tf_op jit(solution)/shard_map/mixed/pallas_call | solution.py:281
  10.7 0.6 collective-permute-start.7
  11.2 3.1 %collective-permute-done.1 = f32[2,2,168,128]{3,2,1,0:T(8,128)S(1)} collective-permute-done((f32[2,2,168,128]{3,2,1,0:T(8,128)S(1)}, f32[2,2,168,128]{3,2,1,0:T(8,128)S(1)}, u32[]{:S(2)}, u32[]{:S(2)}) %collective-permute-start.1) | collective-permute-done | bytes 344096 | tf_op jit(solution)/shard_map/ppermute | solution.py:791
  14.4 2.1 %collective-permute-start.3 = (f32[2,168,128]{2,1,0:T(8,128)S(1)}, f32[2,168,128]{2,1,0:T(8,128)S(1)}, u32[]{:S(2)}, u32[]{:S(2)}) collective-permute-start(f32[2,168,128]{2,1,0:T(8,128)S(1)} %slice_bitcast_fusion), channel_id=1, source_target_pairs={{0,4},{1,5},{2,3},{3,2},{4,0},{5,1},{6,7},{7,6},{8,12},{9,13},{10,... | collective-permute-start | bytes 516104 | tf_op jit(solution)/shard_map/ppermute | solution.py:791
  16.7 3.2 %collective-permute-done.3 = f32[2,168,128]{2,1,0:T(8,128)S(1)} collective-permute-done((f32[2,168,128]{2,1,0:T(8,128)S(1)}, f32[2,168,128]{2,1,0:T(8,128)S(1)}, u32[]{:S(2)}, u32[]{:S(2)}) %collective-permute-start.3) | collective-permute-done | bytes 172064 | tf_op jit(solution)/shard_map/ppermute | solution.py:791
  19.9 2.1 %collective-permute-start.4 = (f32[168,128]{1,0:T(8,128)S(1)}, f32[168,128]{1,0:T(8,128)S(1)}, u32[]{:S(2)}, u32[]{:S(2)}) collective-permute-start(f32[168,128]{1,0:T(8,128)S(1)} %slice_bitcast_fusion.4), channel_id=1, source_target_pairs={{0,8},{8,0},{1,9},{9,1},{2,10},{10,2},{3,11},{11,3},{4,12},{12,4},... | collective-permute-start | bytes 258056 | tf_op jit(solution)/shard_map/ppermute | solution.py:780
  22.1 1.0 %collective-permute-done.8 = f32[2,2,128,128]{3,2,1,0:T(8,128)S(1)} collective-permute-done((f32[2,2,128,128]{3,2,1,0:T(8,128)S(1)}, f32[2,2,128,128]{3,2,1,0:T(8,128)S(1)}, u32[]{:S(2)}, u32[]{:S(2)}) %collective-permute-start.8) | collective-permute-done | bytes 262176 | tf_op jit(solution)/shard_map/ppermute | solution.py:791
  23.1 1.7 %collective-permute-start.9 = (f32[2,128,128]{2,1,0:T(8,128)S(1)}, f32[2,128,128]{2,1,0:T(8,128)S(1)}, u32[]{:S(2)}, u32[]{:S(2)}) collective-permute-start(f32[2,128,128]{2,1,0:T(8,128)S(1)} %get-tuple-element.78), channel_id=1, source_target_pairs={{0,1},{1,0},{2,6},{3,7},{4,5},{5,4},{6,2},{7,3},{8,9},{9,8},{10,14... | collective-permute-start | bytes 393224 | tf_op jit(solution)/shard_map/ppermute | solution.py:791
  24.9 2.8 %collective-permute-start.5 = (f32[168,128]{1,0:T(8,128)S(1)}, f32[168,128]{1,0:T(8,128)S(1)}, u32[]{:S(2)}, u32[]{:S(2)}) collective-permute-start(f32[168,128]{1,0:T(8,128)S(1)} %fusion.1), channel_id=1, source_target_pairs={{0,16},{16,0},{1,17},{17,1},{2,18},{18,2},{3,19},{19,3},{4,20},{20... | collective-permute-start | bytes 258056 | tf_op jit(solution)/shard_map/ppermute | solution.py:780
  27.7 2.6 %collective-permute-done.5 = f32[168,128]{1,0:T(8,128)S(1)} collective-permute-done((f32[168,128]{1,0:T(8,128)S(1)}, f32[168,128]{1,0:T(8,128)S(1)}, u32[]{:S(2)}, u32[]{:S(2)}) %collective-permute-start.5) | collective-permute-done | bytes 86048 | tf_op jit(solution)/shard_map/ppermute | solution.py:780
  30.5 1.8 %collective-permute-start.10 = (f32[128,128]{1,0:T(8,128)S(1)}, f32[128,128]{1,0:T(8,128)S(1)}, u32[]{:S(2)}, u32[]{:S(2)}) collective-permute-start(f32[128,128]{1,0:T(8,128)S(1)} %get-tuple-element.80), channel_id=1, source_target_pairs={{0,8},{8,0},{1,9},{9,1},{2,10},{10,2},{3,11},{11,3},{4,12},{12,4},... | collective-permute-start | bytes 196616 | tf_op jit(solution)/shard_map/ppermute | solution.py:780
  32.3 3.2 %first_panels.1 = (f32[288,256]{1,0:T(8,128)S(1)}, bf16[96,256]{1,0:T(8,128)(2,1)S(1)}, bf16[96,256]{1,0:T(8,128)(2,1)S(1)}, f32[16,256]{1,0:T(8,128)S(1)}, f32[...) custom-call(f32[168,128]{1,0:T(8,128)S(1)} %add.38.mine, ...), custom_call_target="tpu_custom_call" | custom-call | flops 1073741824 | bytes 1048576 | tf_op jit(solution)/shard_map/first_panels/pallas_call | solution.py:632
  35.5 3.4 %collective-permute-start.11 = (f32[128,128]{1,0:T(8,128)S(1)}, f32[128,128]{1,0:T(8,128)S(1)}, u32[]{:S(2)}, u32[]{:S(2)}) collective-permute-start(f32[128,128]{1,0:T(8,128)S(1)} %add.42), channel_id=1, source_target_pairs={{0,16},{16,0},{1,17},{17,1},{2,18},{18,2},{3,19},{19,3},{4,20},{20... | collective-permute-start | bytes 196616 | tf_op jit(solution)/shard_map/ppermute | solution.py:780
  38.9 4.2 %second_panels.1 = (f32[128,128]{1,0:T(8,128)S(1)}, f32[288,256]{1,0:T(8,128)S(1)}, bf16[96,256]{1,0:T(8,128)(2,1)S(1)}, bf16[96,256]{1,0:T(8,128)(2,1)S(1)}, f32[16,256]{1,0:T(8,128)S(1)}) custom-call(f32[288,256]{1,0:T(8,128)S(1)} %get-tuple-element.53.refs_0_, bf16[96,256]{1,0:T(8,128)(2,1)S(1)} %get-tuple-element.54.refs_1_, ...), custom_call_target="tpu_custom_call" | custom-call | flops 1073741824 | bytes 1048576 | tf_op jit(solution)/shard_map/second_panels/pallas_call | solution.py:632
  43.3 1.0 %third_panels.1.winv = f32[256,256]{1,0:T(8,128)S(1)} custom-call(f32[288,256]{1,0:T(8,128)S(1)} %get-tuple-element.62.wa_in, bf16[96,256]{1,0:T(8,128)(2,1)S(1)} %get-tuple-element.63.wl_in, bf16[96,256]{1,0:T(8,128)(2,1)S(1)} %get-tuple-element.64.wr_in, f32[16,256]{1,0:T(8,128)S(1)} %get-tuple-element.65.panel_in, f32[8,256]{1,0:T(8,128)S(1)} %get-tuple-element.66.scale), custom_call_target="tpu_custom_call" | custom-call | flops 1073741824 | bytes 1048576 | tf_op jit(solution)/shard_map/third_panels/pallas_call | solution.py:632
  44.3 0.2 collective-permute-done.12.other
  44.5 0.6 %products.1 = f32[8,40,128]{2,1,0:T(8,128)S(1)} custom-call(f32[256,256]{1,0:T(8,128)S(1)} %third_panels.1.winv, f32[128,128]{1,0:T(8,128)S(1)} %get-tuple-element.67.ninv_ref, f32[128,128]{1,0:T(8,128)S(1)} %add.43.mine, f32[128,128]{1,0:T(8,128)S(1)} %collective-permute-done.12.other), custom_call_target="tpu_custom_call" | custom-call | tf_op jit(solution)/shard_map/products/pallas_call | solution.py:723
  45.2 10.5 %all_to_all.5.got_ref = f32[8,40,128]{2,1,0:T(8,128)S(1)} all-to-all(f32[8,40,128]{2,1,0:T(8,128)S(1)} %products.1), channel_id=1, replica_groups=mesh['dp0'=2,'dp1'=2,'dp2'=2,'dp3'=2,'own0'=2] {'dp1','dp2','own0'}, dimensions={0} | all-to-all | bytes 327680 | tf_op jit(solution)/shard_map/all_to_all | solution.py:845
  55.6 0.7 %placing.1 = (f32[5,16,256]{2,1,0:T(8,128)}, f32[8,16,64]{2,1,0:T(8,128)}) custom-call(s32[8,8,128]{2,1,0:T(8,128)S(1)} %get-tuple-element.47.slots_ref, f32[8,40,128]{2,1,0:T(8,128)S(1)} %all_to_all.5.got_ref), custom_call_target="tpu_custom_call" | custom-call | tf_op jit(solution)/shard_map/placing/pallas_call | solution.py:766
  (32 shorter events, 0.8 us)
Async XLA Ops:
  4.3 1.8 %collective-permute-start = (f32[2,2,168,128]{3,2,1,0:T(8,128)S(1)}, f32[2,2,168,128]{3,2,1,0:T(8,128)S(1)}, u32[]{:S(2)}, u32[]{:S(2)}) collective-permute-start(f32[2,2,168,128]{3,2,1,0:T(8,128)S(1)} %slice.43), channel_id=1, source_target_pairs={{0,2},{2,0},{1,3},{3,1},{4,6},{6,4},{5,7},{7,5},{8,10},{10,8},{9,1... | collective-permute-start | bytes 1032200 | tf_op jit(solution)/shard_map/ppermute | solution.py:780
  4.8 4.3 %copy-start = (s32[8]{0:T(128)S(1)}, s32[8]{0:T(128)}, u32[]{:S(2)}) copy-start(s32[8]{0:T(128)} %owner_map.1) | copy-start | bytes 100
  6.2 8.1 %collective-permute-start.1 = (f32[2,2,168,128]{3,2,1,0:T(8,128)S(1)}, f32[2,2,168,128]{3,2,1,0:T(8,128)S(1)}, u32[]{:S(2)}, u32[]{:S(2)}) collective-permute-start(f32[2,2,168,128]{3,2,1,0:T(8,128)S(1)} %slice_add_fusion), channel_id=1, source_target_pairs={{0,1},{1,0},{2,6},{3,7},{4,5},{5,4},{6,2},{7,3},{8,9},{9,8},{10,14... | collective-permute-start | bytes 1032200 | tf_op jit(solution)/shard_map/ppermute | solution.py:791
  10.6 3.7 %collective-permute-start.2 = (f32[2,2,168,128]{3,2,1,0:T(8,128)S(1)}, f32[2,2,168,128]{3,2,1,0:T(8,128)S(1)}, u32[]{:S(2)}, u32[]{:S(2)}) collective-permute-start(f32[2,2,168,128]{3,2,1,0:T(8,128)S(1)} %pad_maximum_fusion), channel_id=1, source_target_pairs={{0,2},{2,0},{1,3},{3,1},{4,6},{6,4},{5,7},{7,5},{8,10},{10,8},{9,1... | collective-permute-start | bytes 1032200 | tf_op jit(solution)/shard_map/ppermute | solution.py:780
  10.7 5.8 %collective-permute-start.7 = (f32[4,2,128,128]{3,2,1,0:T(8,128)S(1)}, f32[4,2,128,128]{3,2,1,0:T(8,128)S(1)}, u32[]{:S(2)}, u32[]{:S(2)}) collective-permute-start(f32[4,2,128,128]{3,2,1,0:T(8,128)S(1)} %get-tuple-element.50), channel_id=1, source_target_pairs={{0,2},{2,0},{1,3},{3,1},{4,6},{6,4},{5,7},{7,5},{8,10},{10,8},{9,1... | collective-permute-start | bytes 1572872 | tf_op jit(solution)/shard_map/ppermute | solution.py:780
  14.4 5.5 %collective-permute-start.3 = (f32[2,168,128]{2,1,0:T(8,128)S(1)}, f32[2,168,128]{2,1,0:T(8,128)S(1)}, u32[]{:S(2)}, u32[]{:S(2)}) collective-permute-start(f32[2,168,128]{2,1,0:T(8,128)S(1)} %slice_bitcast_fusion), channel_id=1, source_target_pairs={{0,4},{1,5},{2,3},{3,2},{4,0},{5,1},{6,7},{7,6},{8,12},{9,13},{10,... | collective-permute-start | bytes 516104 | tf_op jit(solution)/shard_map/ppermute | solution.py:791
  16.6 6.4 %collective-permute-start.8 = (f32[2,2,128,128]{3,2,1,0:T(8,128)S(1)}, f32[2,2,128,128]{3,2,1,0:T(8,128)S(1)}, u32[]{:S(2)}, u32[]{:S(2)}) collective-permute-start(f32[2,2,128,128]{3,2,1,0:T(8,128)S(1)} %get-tuple-element.76), channel_id=1, source_target_pairs={{0,4},{1,5},{2,3},{3,2},{4,0},{5,1},{6,7},{7,6},{8,12},{9,13},{10,... | collective-permute-start | bytes 786440 | tf_op jit(solution)/shard_map/ppermute | solution.py:791
  19.9 4.9 %collective-permute-start.4 = (f32[168,128]{1,0:T(8,128)S(1)}, f32[168,128]{1,0:T(8,128)S(1)}, u32[]{:S(2)}, u32[]{:S(2)}) collective-permute-start(f32[168,128]{1,0:T(8,128)S(1)} %slice_bitcast_fusion.4), channel_id=1, source_target_pairs={{0,8},{8,0},{1,9},{9,1},{2,10},{10,2},{3,11},{11,3},{4,12},{12,4},... | collective-permute-start | bytes 258056 | tf_op jit(solution)/shard_map/ppermute | solution.py:780
  23.1 7.3 %collective-permute-start.9 = (f32[2,128,128]{2,1,0:T(8,128)S(1)}, f32[2,128,128]{2,1,0:T(8,128)S(1)}, u32[]{:S(2)}, u32[]{:S(2)}) collective-permute-start(f32[2,128,128]{2,1,0:T(8,128)S(1)} %get-tuple-element.78), channel_id=1, source_target_pairs={{0,1},{1,0},{2,6},{3,7},{4,5},{5,4},{6,2},{7,3},{8,9},{9,8},{10,14... | collective-permute-start | bytes 393224 | tf_op jit(solution)/shard_map/ppermute | solution.py:791
  24.9 5.4 %collective-permute-start.5 = (f32[168,128]{1,0:T(8,128)S(1)}, f32[168,128]{1,0:T(8,128)S(1)}, u32[]{:S(2)}, u32[]{:S(2)}) collective-permute-start(f32[168,128]{1,0:T(8,128)S(1)} %fusion.1), channel_id=1, source_target_pairs={{0,16},{16,0},{1,17},{17,1},{2,18},{18,2},{3,19},{19,3},{4,20},{20... | collective-permute-start | bytes 258056 | tf_op jit(solution)/shard_map/ppermute | solution.py:780
  30.3 2.0 %collective-permute-start.6 = (f32[168,128]{1,0:T(8,128)S(1)}, f32[168,128]{1,0:T(8,128)S(1)}, u32[]{:S(2)}, u32[]{:S(2)}) collective-permute-start(f32[168,128]{1,0:T(8,128)S(1)} %add.38.mine), channel_id=1, source_target_pairs={{0,2},{2,0},{1,3},{3,1},{4,6},{6,4},{5,7},{7,5},{8,10},{10,8},{9,1... | collective-permute-start | bytes 258056 | tf_op jit(solution)/shard_map/ppermute | solution.py:780
  30.5 5.0 %collective-permute-start.10 = (f32[128,128]{1,0:T(8,128)S(1)}, f32[128,128]{1,0:T(8,128)S(1)}, u32[]{:S(2)}, u32[]{:S(2)}) collective-permute-start(f32[128,128]{1,0:T(8,128)S(1)} %get-tuple-element.80), channel_id=1, source_target_pairs={{0,8},{8,0},{1,9},{9,1},{2,10},{10,2},{3,11},{11,3},{4,12},{12,4},... | collective-permute-start | bytes 196616 | tf_op jit(solution)/shard_map/ppermute | solution.py:780
  35.5 7.7 %collective-permute-start.11 = (f32[128,128]{1,0:T(8,128)S(1)}, f32[128,128]{1,0:T(8,128)S(1)}, u32[]{:S(2)}, u32[]{:S(2)}) collective-permute-start(f32[128,128]{1,0:T(8,128)S(1)} %add.42), channel_id=1, source_target_pairs={{0,16},{16,0},{1,17},{17,1},{2,18},{18,2},{3,19},{19,3},{4,20},{20... | collective-permute-start | bytes 196616 | tf_op jit(solution)/shard_map/ppermute | solution.py:780
  43.2 1.3 %collective-permute-start.12 = (f32[128,128]{1,0:T(8,128)S(1)}, f32[128,128]{1,0:T(8,128)S(1)}, u32[]{:S(2)}, u32[]{:S(2)}) collective-permute-start(f32[128,128]{1,0:T(8,128)S(1)} %add.43.mine), channel_id=1, source_target_pairs={{0,2},{2,0},{1,3},{3,1},{4,6},{6,4},{5,7},{7,5},{8,10},{10,8},{9,1... | collective-permute-start | bytes 196616 | tf_op jit(solution)/shard_map/ppermute | solution.py:780

commit v17 on v16

--- a/solution.py
+++ b/solution.py
@@ -73,8 +73,17 @@
     return flat[i, pl.ds(kept, rows), :], flat[i, pl.ds(sent, rows), :]
 
 
-def by_core(place, first, second):
+ORDERS = (("first", "second", "near"), ("second", "near", "first"))
+
+
+def position(axes, i):
+    bits = {"near": i // 4, "second": (i // 2) % 2, "first": i % 2}
+    return bits[axes[0]] * 4 + bits[axes[1]] * 2 + bits[axes[2]]
+
+
+def positions(place, i, orders):
     core = lax.axis_index(place.core)
+    first, second = (position(axes, i) for axes in orders)
     return jnp.where(core == 0, first, second), jnp.where(core == 0, second, first)
 
 
@@ -155,8 +164,22 @@
 
 def put(ref, index, parts):
     rows = EARLY_ROWS // 2
-    ref[*index, :rows] = parts[0]
-    ref[*index, rows:] = parts[1]
+    ref[index, :rows] = parts[0]
+    ref[index, rows:] = parts[1]
+
+
+def put_layer(place, i, sums, a_flat, b_flat, keep, send):
+    kept, sent = pack_layer(place, i, *sums, a_flat, b_flat)
+    mine, other = positions(place, i, ORDERS)
+    put(keep, mine, kept)
+    put(send, other, sent)
+
+
+def clear_others(place, layers, keep, send):
+    for i in layers:
+        mine, other = positions(place, i, ORDERS)
+        keep[mine] = jnp.zeros(keep.shape[1:], jnp.float32)
+        send[other] = jnp.zeros(send.shape[1:], jnp.float32)
 
 
 def hot_kernel(place, wide_hbm, narrow_hbm, keep, send, wides, narrows, a_flat, b_flat, sems):
@@ -165,16 +188,10 @@
     for i in order[:AHEAD]:
         for copy in copies[i]:
             copy.start()
+    clear_others(place, COLD, keep, send)
 
     def pack(i, sums):
-        kept, sent = pack_layer(place, i, *sums, a_flat, b_flat)
-        z, y, x = i // 4, (i // 2) % 2, i % 2
-        if x and y:
-            mine = other = 1
-        else:
-            mine, other = by_core(place, 0 if x else 2, 2 if x else 0)
-        put(keep, (mine, z), kept)
-        put(send, (other, z), sent)
+        put_layer(place, i, sums, a_flat, b_flat, keep, send)
 
     before = None
     for at, i in enumerate(order):
@@ -192,10 +209,17 @@
 
 def cold_kernel(place, wides, narrows, keep, send, a_flat, b_flat):
     for i in COLD:
-        sums = square_sums(wides[i], narrows[i])
-        kept, sent = pack_layer(place, i, *sums, a_flat, b_flat)
-        put(keep, (i // 4,), kept)
-        put(send, (i // 4,), sent)
+        put_layer(
+            place, i, square_sums(wides[i], narrows[i]), a_flat, b_flat, keep, send
+        )
+    core = lax.axis_index(place.core)
+    stay = [[i for i in HOT if position(axes, i) < 4] for axes in ORDERS]
+    for first, second in zip(*stay):
+        here = [position(axes, i) for axes, i in zip(ORDERS, (first, second))]
+        mine = jnp.where(core == 0, here[0], here[1])
+        other = jnp.where(core == 0, here[1], here[0])
+        keep[mine] = jnp.zeros(keep.shape[1:], jnp.float32)
+        send[other] = jnp.zeros(send.shape[1:], jnp.float32)
 
 
 def write_slots(place, owner_map, slots_ref):
@@ -216,10 +240,9 @@
         flat[i, :n] = mixed[:, :n]
         flat[i, n:] = mixed[:, n:]
         kept, sent = both_halves(place, flat, i)
-        z, y, x = i // 4, (i // 2) % 2, i % 2
-        mine, other = by_core(place, y * 2 + x, x * 2 + y)
-        keep[mine, z] = kept
-        send[other, z] = sent
+        mine, other = positions(place, i, ORDERS[::-1])
+        keep[mine] = kept
+        send[other] = sent
 
 
 def gram_cost(wide_rows, columns):
@@ -240,7 +263,7 @@
 
 def hot_squares(place, wide_rows, narrow_rows):
     layers = wide_rows.shape[0]
-    half = jax.ShapeDtypeStruct((3, 2, HALF_ROWS, LANES), jnp.float32)
+    half = jax.ShapeDtypeStruct((layers, HALF_ROWS, LANES), jnp.float32)
     return pl.pallas_call(
         functools.partial(hot_kernel, place),
         in_specs=[HBM, HBM],
@@ -262,7 +285,7 @@
 
 
 def cold_squares(place, wides, narrows):
-    half = jax.ShapeDtypeStruct((2, HALF_ROWS, LANES), jnp.float32)
+    half = jax.ShapeDtypeStruct((wides.shape[0] // 2, HALF_ROWS, LANES), jnp.float32)
     return pl.pallas_call(
         functools.partial(cold_kernel, place),
         in_specs=[VMEM, VMEM],
@@ -277,7 +300,7 @@
 
 def mixed_sums(place, owner_map, wides, narrows):
     layers, _, narrow = narrows.shape
-    half = jax.ShapeDtypeStruct((4, 2, narrow, LANES), jnp.float32)
+    half = jax.ShapeDtypeStruct((layers, narrow, LANES), jnp.float32)
     return pl.pallas_call(
         functools.partial(mixed_kernel, place),
         in_specs=[SMEM, VMEM, VMEM],
@@ -780,15 +803,11 @@
     return lax.ppermute(value, axis, [(0, 1), (1, 0)])
 
 
-def swap_by_core(value, place, stage):
-    pairs = []
-    for y in range(2):
-        for core in range(2):
-            for x in range(2):
-                flip = 1 if core == stage else 4
-                here = y * 4 + core * 2 + x
-                pairs.append((here, here ^ flip))
-    return lax.ppermute(value, (place.second, place.core, place.first), pairs)
+def swap_by_core(value, place, stage, orders):
+    names = (place.near, place.second, place.core, place.first)
+    flips = {"near": 8, "second": 4, "first": 1}
+    pairs = [(i, i ^ flips[orders[(i >> 1) & 1][stage]]) for i in range(16)]
+    return lax.ppermute(value, names, pairs)
 
 
 def after(value, *others):
@@ -802,32 +821,35 @@
     total = float(rows * n_dp * n_own)
 
     h_keep, h_send, wides, narrows = hot_squares(place, wide_rows, narrow_rows)
-    h_got = swap(h_send[:2], place.core)
-    c_keep, c_send = cold_squares(place, after(wides, h_send), narrows)
+    first_send = h_send[4:]
+    h_got = swap(first_send, place.core)
+    c_keep, c_send = cold_squares(place, after(wides, first_send), narrows)
     h_keep, c_send = lax.optimization_barrier((h_keep, c_send))
-
-    hot = h_keep[:2] + h_got
-    s_got = swap_by_core(hot, place, 0)
+    others = ORDERS[::-1]
+
+    hot = h_keep[4:] + h_got
+    s_got = swap_by_core(hot, place, 0, ORDERS)
     m_keep, m_send, slots_of = mixed_sums(place, owner_map, after(wides, hot), narrows)
-    c_got = swap(after(jnp.stack([c_send, h_send[2]]), m_send), place.core)
+    c_got = swap(after(c_send + h_send[:4], m_send), place.core)
     m_got = swap(m_send, place.core)
-    s = jnp.stack([c_keep, h_keep[2]]) + s_got
+
+    s = (c_keep + h_keep[:4]) + s_got
     s = s + after(c_got, s)
-    s_got = swap_by_core(s[1], place, 1)
+    s_got = swap_by_core(s[2:], place, 1, ORDERS)
     m = after(m_keep, s) + m_got
-    m_got = swap_by_core(m[2:], place, 1)
-
-    s = s[0] + s_got
-    s_got = swap(s[1], place.near)
-    m = after(m[:2], s) + m_got
-    m_got = swap_by_core(m[1], place, 0)
+    m_got = swap_by_core(m[4:], place, 0, others)
+
+    s = s[:2] + s_got
+    s_got = swap_by_core(s[1], place, 2, ORDERS)
+    m = after(m[:4], s) + m_got
+    m_got = swap_by_core(m[2:], place, 1, others)
 
     s = s[0] + s_got
     if place.extra:
         s = lax.psum(s, place.extra)
     s_got = swap(s, place.far)
-    m = after(m[0], s) + m_got
-    m_got = swap(m[1], place.near)
+    m = after(m[:2], s) + m_got
+    m_got = swap_by_core(m[1], place, 2, others)
 
     s = s + s_got
     state = first_panels(place, [s, swap(s, place.core)], wide, narrow, total)

time: 56.5 us -> 56.5 us (level)
  starting transfers between devices: 18.3 us -> 16.4 us
  waiting for transfers between devices: 10.8 us -> 12.6 us
    ppermute x9 -> x7, starting transfers between devices: 11.5 us -> 6.44 us  [swap(): return lax.ppermute(value, axis, [(0, 1), (1, 0)])]
    ppermute x4 -> x6, starting transfers between devices: 6.81 us -> 9.95 us  [swap_by_core(): return lax.ppermute(value, names, pairs)]
    ppermute x9 -> x7, waiting for transfers between devices: 3.58 us -> 5.32 us  [swap(): return lax.ppermute(value, axis, [(0, 1), (1, 0)])]
    ppermute x4 -> x6, waiting for transfers between devices: 7.23 us -> 7.27 us  [swap_by_core(): return lax.ppermute(value, names, pairs)]
  transfers between devices with their start and end apart: 13 -> 13, of which waited for: 6 -> 7; matrix products, arithmetic and copies ran while one was open for 1% -> 1% of each run, Pallas kernels for 19% -> 19%
where the time goes in v17:
time: 56.5 us; the launch traced here: 56.3 us
  starting transfers between devices  16.4 us (29%)
  Pallas kernels  15.4 us (27%)
  waiting for transfers between devices  12.6 us (22%)
  blocking collectives  10.6 us (19%)
  between operations  0.84 us (1%)
    all_to_all x1, blocking collectives, on_device(): got = lax.all_to_all(sent, (place.near, place.second, place.first), 0, 0)  10.6 us
    ppermute x6, starting transfers between devices, swap_by_core(): return lax.ppermute(value, names, pairs)  9.95 us
    pallas_call x3, Pallas kernels, sweep_call(): pl.pallas_call(kernel, in_specs=[VMEM] * len(args), out_specs=[VMEM] * le...  8.43 us
    ppermute x6, waiting for transfers between devices, swap_by_core(): return lax.ppermute(value, names, pairs)  7.27 us
    ppermute x7, starting transfers between devices, swap(): return lax.ppermute(value, axis, [(0, 1), (1, 0)])  6.44 us
    ppermute x7, waiting for transfers between devices, swap(): return lax.ppermute(value, axis, [(0, 1), (1, 0)])  5.32 us
    pallas_call x1, Pallas kernels, hot_squares(): pl.pallas_call(functools.partial(hot_kernel, place), in_specs=[HBM, HBM],...  3.58 us
    pallas_call x1, Pallas kernels, mixed_sums(): pl.pallas_call(functools.partial(mixed_kernel, place), in_specs=[SMEM, VM...  1.45 us
  transfers between devices with their start and end apart: 13, of which 7 were waited for; matrix products, arithmetic and copies ran while one was open for 1% of the time, Pallas kernels for 19%

profile of v17, /device:TPU:0, one launch (start us, length us, event | category | flops | bytes accessed | tf_op | source)
XLA Modules:
  0.0 56.3 jit_solution(18388278389855838141)
XLA Ops:
  0.6 3.6 %hot_squares.1 = (f32[8,168,128]{2,1,0:T(8,128)S(1)}, f32[8,168,128]{2,1,0:T(8,128)S(1)}, bf16[8,768,256]{2,1,0:T(8,128)(2,1)S(1)}, bf16[8,768,128]{2,1,0:T(8,128)(2,1)S(1)}) custom-call(bf16[8,768,256]{2,1,0:T(8,128)(2,1)} %wide_hbm.1, bf16[8,768,128]{2,1,0:T(8,128)(2,1)} %narrow_hbm.1), custom_call_target="tpu_custom_call" | custom-call | flops 754974720 | bytes 3145728 | tf_op jit(solution)/shard_map/hot_squares/pallas_call | solution.py:267
  4.3 0.5 collective-permute-start
  4.8 0.6 %cold_squares.1 = (f32[4,168,128]{2,1,0:T(8,128)S(1)}, f32[4,168,128]{2,1,0:T(8,128)S(1)}) custom-call(bf16[8,768,256]{2,1,0:T(8,128)(2,1)S(1)} %get-tuple-element.46.wides, bf16[8,768,128]{2,1,0:T(8,128)(2,1)S(1)} %get-tuple-element.43.narrows), custom_call_target="tpu_custom_call" | custom-call | flops 251658240 | bytes 3145728 | tf_op jit(solution)/shard_map/cold_squares/pallas_call | solution.py:289
  5.4 0.7 %collective-permute-done = f32[4,168,128]{2,1,0:T(8,128)S(1)} collective-permute-done((f32[4,168,128]{2,1,0:T(8,128)S(1)}, f32[4,168,128]{2,1,0:T(8,128)S(1)}, u32[]{:S(2)}, u32[]{:S(2)}) %collective-permute-start) | collective-permute-done | bytes 344096 | tf_op jit(solution)/shard_map/ppermute | solution.py:803
  6.1 2.9 %collective-permute-start.1 = (f32[4,168,128]{2,1,0:T(8,128)S(1)}, f32[4,168,128]{2,1,0:T(8,128)S(1)}, u32[]{:S(2)}, u32[]{:S(2)}) collective-permute-start(f32[4,168,128]{2,1,0:T(8,128)S(1)} %slice_add_fusion.1), channel_id=1, source_target_pairs={{0,1},{1,0},{2,6},{3,7},{4,5},{5,4},{6,2},{7,3},{8,9},{9,8},{10,14... | collective-permute-start | bytes 1032200 | tf_op jit(solution)/shard_map/ppermute | solution.py:810
  9.0 1.4 %mixed.1 = (f32[8,128,128]{2,1,0:T(8,128)S(1)}, f32[8,128,128]{2,1,0:T(8,128)S(1)}, s32[8,8,128]{2,1,0:T(8,128)S(1)}) custom-call(s32[8]{0:T(128)S(1)} %copy-done, bf16[8,768,256]{2,1,0:T(8,128)(2,1)S(1)} %get-tuple-element.46.wides, bf16[8,768,128]{2,1,0:T(8,128)(2,1)S(1)} %get-tuple-element.43.narrows), custom_call_target="tpu_custom_call" | custom-call | flops 402653184 | bytes 3145728 | tf_op jit(solution)/shard_map/mixed/pallas_call | solution.py:304
  10.6 0.6 collective-permute-start.2
  11.2 3.1 %collective-permute-done.1 = f32[4,168,128]{2,1,0:T(8,128)S(1)} collective-permute-done((f32[4,168,128]{2,1,0:T(8,128)S(1)}, f32[4,168,128]{2,1,0:T(8,128)S(1)}, u32[]{:S(2)}, u32[]{:S(2)}) %collective-permute-start.1) | collective-permute-done | bytes 344096 | tf_op jit(solution)/shard_map/ppermute | solution.py:810
  14.4 2.1 %collective-permute-start.3 = (f32[2,168,128]{2,1,0:T(8,128)S(1)}, f32[2,168,128]{2,1,0:T(8,128)S(1)}, u32[]{:S(2)}, u32[]{:S(2)}) collective-permute-start(f32[2,168,128]{2,1,0:T(8,128)S(1)} %slice.57), channel_id=1, source_target_pairs={{0,4},{1,5},{2,10},{3,11},{4,0},{5,1},{6,14},{7,15},{8,12},{9,13},... | collective-permute-start | bytes 516104 | tf_op jit(solution)/shard_map/ppermute | solution.py:810
  16.7 3.2 %collective-permute-done.3 = f32[2,168,128]{2,1,0:T(8,128)S(1)} collective-permute-done((f32[2,168,128]{2,1,0:T(8,128)S(1)}, f32[2,168,128]{2,1,0:T(8,128)S(1)}, u32[]{:S(2)}, u32[]{:S(2)}) %collective-permute-start.3) | collective-permute-done | bytes 172064 | tf_op jit(solution)/shard_map/ppermute | solution.py:810
  19.9 2.1 %collective-permute-start.4 = (f32[168,128]{1,0:T(8,128)S(1)}, f32[168,128]{1,0:T(8,128)S(1)}, u32[]{:S(2)}, u32[]{:S(2)}) collective-permute-start(f32[168,128]{1,0:T(8,128)S(1)} %slice_bitcast_fusion), channel_id=1, source_target_pairs={{0,8},{1,9},{2,3},{3,2},{4,12},{5,13},{6,7},{7,6},{8,0},{9,1},{10,... | collective-permute-start | bytes 258056 | tf_op jit(solution)/shard_map/ppermute | solution.py:810
  22.1 1.0 %collective-permute-done.8 = f32[4,128,128]{2,1,0:T(8,128)S(1)} collective-permute-done((f32[4,128,128]{2,1,0:T(8,128)S(1)}, f32[4,128,128]{2,1,0:T(8,128)S(1)}, u32[]{:S(2)}, u32[]{:S(2)}) %collective-permute-start.8) | collective-permute-done | bytes 262176 | tf_op jit(solution)/shard_map/ppermute | solution.py:810
  23.1 2.0 %collective-permute-start.9 = (f32[2,128,128]{2,1,0:T(8,128)S(1)}, f32[2,128,128]{2,1,0:T(8,128)S(1)}, u32[]{:S(2)}, u32[]{:S(2)}) collective-permute-start(f32[2,128,128]{2,1,0:T(8,128)S(1)} %get-tuple-element.78), channel_id=1, source_target_pairs={{0,8},{1,9},{2,6},{3,7},{4,12},{5,13},{6,2},{7,3},{8,0},{9,1},{10,... | collective-permute-start | bytes 393224 | tf_op jit(solution)/shard_map/ppermute | solution.py:810
  25.2 2.6 %collective-permute-start.5 = (f32[168,128]{1,0:T(8,128)S(1)}, f32[168,128]{1,0:T(8,128)S(1)}, u32[]{:S(2)}, u32[]{:S(2)}) collective-permute-start(f32[168,128]{1,0:T(8,128)S(1)} %fusion), channel_id=1, source_target_pairs={{0,16},{16,0},{1,17},{17,1},{2,18},{18,2},{3,19},{19,3},{4,20},{20... | collective-permute-start | bytes 258056 | tf_op jit(solution)/shard_map/ppermute | solution.py:803
  27.8 3.7 %collective-permute-done.5 = f32[168,128]{1,0:T(8,128)S(1)} collective-permute-done((f32[168,128]{1,0:T(8,128)S(1)}, f32[168,128]{1,0:T(8,128)S(1)}, u32[]{:S(2)}, u32[]{:S(2)}) %collective-permute-start.5) | collective-permute-done | bytes 86048 | tf_op jit(solution)/shard_map/ppermute | solution.py:803
  31.7 0.6 %collective-permute-start.10 = (f32[128,128]{1,0:T(8,128)S(1)}, f32[128,128]{1,0:T(8,128)S(1)}, u32[]{:S(2)}, u32[]{:S(2)}) collective-permute-start(f32[128,128]{1,0:T(8,128)S(1)} %get-tuple-element.80), channel_id=1, source_target_pairs={{0,1},{1,0},{2,10},{3,11},{4,5},{5,4},{6,14},{7,15},{8,9},{9,8},{1... | collective-permute-start | bytes 196616 | tf_op jit(solution)/shard_map/ppermute | solution.py:810
  32.4 0.6 %collective-permute-done.6.other = f32[168,128]{1,0:T(8,128)S(1)} collective-permute-done((f32[168,128]{1,0:T(8,128)S(1)}, f32[168,128]{1,0:T(8,128)S(1)}, u32[]{:S(2)}, u32[]{:S(2)}) %collective-permute-start.6) | collective-permute-done | bytes 86048 | tf_op jit(solution)/shard_map/ppermute | solution.py:803
  32.9 3.2 %first_panels.1 = (f32[288,256]{1,0:T(8,128)S(1)}, bf16[96,256]{1,0:T(8,128)(2,1)S(1)}, bf16[96,256]{1,0:T(8,128)(2,1)S(1)}, f32[16,256]{1,0:T(8,128)S(1)}, f32[...) custom-call(f32[168,128]{1,0:T(8,128)S(1)} %add.46.mine, ...), custom_call_target="tpu_custom_call" | custom-call | flops 1073741824 | bytes 1048576 | tf_op jit(solution)/shard_map/first_panels/pallas_call | solution.py:655
  36.1 2.2 %collective-permute-start.11 = (f32[128,128]{1,0:T(8,128)S(1)}, f32[128,128]{1,0:T(8,128)S(1)}, u32[]{:S(2)}, u32[]{:S(2)}) collective-permute-start(f32[128,128]{1,0:T(8,128)S(1)} %add.50), channel_id=1, source_target_pairs={{0,16},{16,0},{1,17},{17,1},{2,18},{18,2},{3,19},{19,3},{4,20},{20... | collective-permute-start | bytes 196616 | tf_op jit(solution)/shard_map/ppermute | solution.py:803
  38.3 4.2 %second_panels.1 = (f32[128,128]{1,0:T(8,128)S(1)}, f32[288,256]{1,0:T(8,128)S(1)}, bf16[96,256]{1,0:T(8,128)(2,1)S(1)}, bf16[96,256]{1,0:T(8,128)(2,1)S(1)}, f32[16,256]{1,0:T(8,128)S(1)}) custom-call(f32[288,256]{1,0:T(8,128)S(1)} %get-tuple-element.53.refs_0_, bf16[96,256]{1,0:T(8,128)(2,1)S(1)} %get-tuple-element.54.refs_1_, ...), custom_call_target="tpu_custom_call" | custom-call | flops 1073741824 | bytes 1048576 | tf_op jit(solution)/shard_map/second_panels/pallas_call | solution.py:655
  43.3 1.0 %third_panels.1.winv = f32[256,256]{1,0:T(8,128)S(1)} custom-call(f32[288,256]{1,0:T(8,128)S(1)} %get-tuple-element.62.wa_in, bf16[96,256]{1,0:T(8,128)(2,1)S(1)} %get-tuple-element.63.wl_in, bf16[96,256]{1,0:T(8,128)(2,1)S(1)} %get-tuple-element.64.wr_in, f32[16,256]{1,0:T(8,128)S(1)} %get-tuple-element.65.panel_in, f32[8,256]{1,0:T(8,128)S(1)} %get-tuple-element.66.scale), custom_call_target="tpu_custom_call" | custom-call | flops 1073741824 | bytes 1048576 | tf_op jit(solution)/shard_map/third_panels/pallas_call | solution.py:655
  44.3 0.6 %products.1 = f32[8,40,128]{2,1,0:T(8,128)S(1)} custom-call(f32[256,256]{1,0:T(8,128)S(1)} %third_panels.1.winv, f32[128,128]{1,0:T(8,128)S(1)} %get-tuple-element.67.ninv_ref, f32[128,128]{1,0:T(8,128)S(1)} %add.51.mine, f32[128,128]{1,0:T(8,128)S(1)} %collective-permute-done.12.other), custom_call_target="tpu_custom_call" | custom-call | tf_op jit(solution)/shard_map/products/pallas_call | solution.py:746
  44.9 10.6 %all_to_all.5.got_ref = f32[8,40,128]{2,1,0:T(8,128)S(1)} all-to-all(f32[8,40,128]{2,1,0:T(8,128)S(1)} %products.1), channel_id=1, replica_groups=mesh['dp0'=2,'dp1'=2,'dp2'=2,'dp3'=2,'own0'=2] {'dp1','dp2','own0'}, dimensions={0} | all-to-all | bytes 327680 | tf_op jit(solution)/shard_map/all_to_all | solution.py:867
  55.6 0.7 %placing.1 = (f32[5,16,256]{2,1,0:T(8,128)}, f32[8,16,64]{2,1,0:T(8,128)}) custom-call(s32[8,8,128]{2,1,0:T(8,128)S(1)} %get-tuple-element.47.slots_ref, f32[8,40,128]{2,1,0:T(8,128)S(1)} %all_to_all.5.got_ref), custom_call_target="tpu_custom_call" | custom-call | tf_op jit(solution)/shard_map/placing/pallas_call | solution.py:789
  (31 shorter events, 1.4 us)
Async XLA Ops:
  4.2 4.8 %copy-start = (s32[8]{0:T(128)S(1)}, s32[8]{0:T(128)}, u32[]{:S(2)}) copy-start(s32[8]{0:T(128)} %owner_map.1) | copy-start | bytes 100
  4.3 1.8 %collective-permute-start = (f32[4,168,128]{2,1,0:T(8,128)S(1)}, f32[4,168,128]{2,1,0:T(8,128)S(1)}, u32[]{:S(2)}, u32[]{:S(2)}) collective-permute-start(f32[4,168,128]{2,1,0:T(8,128)S(1)} %slice.42), channel_id=1, source_target_pairs={{0,2},{2,0},{1,3},{3,1},{4,6},{6,4},{5,7},{7,5},{8,10},{10,8},{9,1... | collective-permute-start | bytes 1032200 | tf_op jit(solution)/shard_map/ppermute | solution.py:803
  6.1 8.2 %collective-permute-start.1 = (f32[4,168,128]{2,1,0:T(8,128)S(1)}, f32[4,168,128]{2,1,0:T(8,128)S(1)}, u32[]{:S(2)}, u32[]{:S(2)}) collective-permute-start(f32[4,168,128]{2,1,0:T(8,128)S(1)} %slice_add_fusion.1), channel_id=1, source_target_pairs={{0,1},{1,0},{2,6},{3,7},{4,5},{5,4},{6,2},{7,3},{8,9},{9,8},{10,14... | collective-permute-start | bytes 1032200 | tf_op jit(solution)/shard_map/ppermute | solution.py:810
  10.5 6.0 %collective-permute-start.7 = (f32[8,128,128]{2,1,0:T(8,128)S(1)}, f32[8,128,128]{2,1,0:T(8,128)S(1)}, u32[]{:S(2)}, u32[]{:S(2)}) collective-permute-start(f32[8,128,128]{2,1,0:T(8,128)S(1)} %get-tuple-element.50), channel_id=1, source_target_pairs={{0,2},{2,0},{1,3},{3,1},{4,6},{6,4},{5,7},{7,5},{8,10},{10,8},{9,1... | collective-permute-start | bytes 1572872 | tf_op jit(solution)/shard_map/ppermute | solution.py:803
  10.6 3.7 %collective-permute-start.2 = (f32[4,168,128]{2,1,0:T(8,128)S(1)}, f32[4,168,128]{2,1,0:T(8,128)S(1)}, u32[]{:S(2)}, u32[]{:S(2)}) collective-permute-start(f32[4,168,128]{2,1,0:T(8,128)S(1)} %slice_add_fusion), channel_id=1, source_target_pairs={{0,2},{2,0},{1,3},{3,1},{4,6},{6,4},{5,7},{7,5},{8,10},{10,8},{9,1... | collective-permute-start | bytes 1032200 | tf_op jit(solution)/shard_map/ppermute | solution.py:803
  14.4 5.5 %collective-permute-start.3 = (f32[2,168,128]{2,1,0:T(8,128)S(1)}, f32[2,168,128]{2,1,0:T(8,128)S(1)}, u32[]{:S(2)}, u32[]{:S(2)}) collective-permute-start(f32[2,168,128]{2,1,0:T(8,128)S(1)} %slice.57), channel_id=1, source_target_pairs={{0,4},{1,5},{2,10},{3,11},{4,0},{5,1},{6,14},{7,15},{8,12},{9,13},... | collective-permute-start | bytes 516104 | tf_op jit(solution)/shard_map/ppermute | solution.py:810
  16.6 6.4 %collective-permute-start.8 = (f32[4,128,128]{2,1,0:T(8,128)S(1)}, f32[4,128,128]{2,1,0:T(8,128)S(1)}, u32[]{:S(2)}, u32[]{:S(2)}) collective-permute-start(f32[4,128,128]{2,1,0:T(8,128)S(1)} %get-tuple-element.76), channel_id=1, source_target_pairs={{0,4},{1,5},{2,3},{3,2},{4,0},{5,1},{6,7},{7,6},{8,12},{9,13},{10,... | collective-permute-start | bytes 786440 | tf_op jit(solution)/shard_map/ppermute | solution.py:810
  19.9 5.2 %collective-permute-start.4 = (f32[168,128]{1,0:T(8,128)S(1)}, f32[168,128]{1,0:T(8,128)S(1)}, u32[]{:S(2)}, u32[]{:S(2)}) collective-permute-start(f32[168,128]{1,0:T(8,128)S(1)} %slice_bitcast_fusion), channel_id=1, source_target_pairs={{0,8},{1,9},{2,3},{3,2},{4,12},{5,13},{6,7},{7,6},{8,0},{9,1},{10,... | collective-permute-start | bytes 258056 | tf_op jit(solution)/shard_map/ppermute | solution.py:810
  23.1 8.5 %collective-permute-start.9 = (f32[2,128,128]{2,1,0:T(8,128)S(1)}, f32[2,128,128]{2,1,0:T(8,128)S(1)}, u32[]{:S(2)}, u32[]{:S(2)}) collective-permute-start(f32[2,128,128]{2,1,0:T(8,128)S(1)} %get-tuple-element.78), channel_id=1, source_target_pairs={{0,8},{1,9},{2,6},{3,7},{4,12},{5,13},{6,2},{7,3},{8,0},{9,1},{10,... | collective-permute-start | bytes 393224 | tf_op jit(solution)/shard_map/ppermute | solution.py:810
  25.2 6.4 %collective-permute-start.5 = (f32[168,128]{1,0:T(8,128)S(1)}, f32[168,128]{1,0:T(8,128)S(1)}, u32[]{:S(2)}, u32[]{:S(2)}) collective-permute-start(f32[168,128]{1,0:T(8,128)S(1)} %fusion), channel_id=1, source_target_pairs={{0,16},{16,0},{1,17},{17,1},{2,18},{18,2},{3,19},{19,3},{4,20},{20... | collective-permute-start | bytes 258056 | tf_op jit(solution)/shard_map/ppermute | solution.py:803
  31.6 1.3 %collective-permute-start.6 = (f32[168,128]{1,0:T(8,128)S(1)}, f32[168,128]{1,0:T(8,128)S(1)}, u32[]{:S(2)}, u32[]{:S(2)}) collective-permute-start(f32[168,128]{1,0:T(8,128)S(1)} %add.46.mine), channel_id=1, source_target_pairs={{0,2},{2,0},{1,3},{3,1},{4,6},{6,4},{5,7},{7,5},{8,10},{10,8},{9,1... | collective-permute-start | bytes 258056 | tf_op jit(solution)/shard_map/ppermute | solution.py:803
  31.7 4.4 %collective-permute-start.10 = (f32[128,128]{1,0:T(8,128)S(1)}, f32[128,128]{1,0:T(8,128)S(1)}, u32[]{:S(2)}, u32[]{:S(2)}) collective-permute-start(f32[128,128]{1,0:T(8,128)S(1)} %get-tuple-element.80), channel_id=1, source_target_pairs={{0,1},{1,0},{2,10},{3,11},{4,5},{5,4},{6,14},{7,15},{8,9},{9,8},{1... | collective-permute-start | bytes 196616 | tf_op jit(solution)/shard_map/ppermute | solution.py:810
  36.1 6.8 %collective-permute-start.11 = (f32[128,128]{1,0:T(8,128)S(1)}, f32[128,128]{1,0:T(8,128)S(1)}, u32[]{:S(2)}, u32[]{:S(2)}) collective-permute-start(f32[128,128]{1,0:T(8,128)S(1)} %add.50), channel_id=1, source_target_pairs={{0,16},{16,0},{1,17},{17,1},{2,18},{18,2},{3,19},{19,3},{4,20},{20... | collective-permute-start | bytes 196616 | tf_op jit(solution)/shard_map/ppermute | solution.py:803
  42.9 1.4 %collective-permute-start.12 = (f32[128,128]{1,0:T(8,128)S(1)}, f32[128,128]{1,0:T(8,128)S(1)}, u32[]{:S(2)}, u32[]{:S(2)}) collective-permute-start(f32[128,128]{1,0:T(8,128)S(1)} %add.51.mine), channel_id=1, source_target_pairs={{0,2},{2,0},{1,3},{3,1},{4,6},{6,4},{5,7},{7,5},{8,10},{10,8},{9,1... | collective-permute-start | bytes 196616 | tf_op jit(solution)/shard_map/ppermute | solution.py:803

commit v18 on v17

--- a/solution.py
+++ b/solution.py
@@ -852,12 +852,12 @@
     m_got = swap_by_core(m[1], place, 2, others)
 
     s = s + s_got
-    state = first_panels(place, [s, swap(s, place.core)], wide, narrow, total)
-    m = after(m[0], state[0]) + m_got
+    m = after(m[0], s) + m_got
     if place.extra:
         m = lax.psum(m, place.extra)
+    s_got = swap(after(s, m), place.core)
     m_got = swap(m, place.far)
-    *state, wide_scale, narrow_scale = state
+    *state, wide_scale, narrow_scale = first_panels(place, [s, s_got], wide, narrow, total)
     ninv, *state = second_panels([*state, narrow_scale], wide, narrow)
     m = after(m, ninv) + m_got
     m_got = swap(m, place.core)

time: 56.5 us -> 58.3 us (1.032)
  starting transfers between devices: 16.4 us -> 17.9 us
  blocking collectives: 10.6 us -> 11.5 us
    ppermute x7, waiting for transfers between devices: 5.32 us -> 0.79 us  [swap(): return lax.ppermute(value, axis, [(0, 1), (1, 0)])]
    ppermute x6, waiting for transfers between devices: 7.27 us -> 11.3 us  [swap_by_core(): return lax.ppermute(value, names, pairs)]
    ppermute x6, starting transfers between devices: 9.95 us -> 10.9 us  [swap_by_core(): return lax.ppermute(value, names, pairs)]
    all_to_all x1, blocking collectives: 10.6 us -> 11.5 us  [on_device(): got = lax.all_to_all(sent, (place.near, place.second, place.first), 0, 0)]
  transfers between devices with their start and end apart: 13 -> 13, of which waited for: 7 -> 7; matrix products, arithmetic and copies ran while one was open for 1% -> 1% of each run, Pallas kernels for 19% -> 18%
where the time goes in v18:
time: 58.3 us; the launch traced here: 58.1 us
  starting transfers between devices  17.9 us (31%)
  Pallas kernels  15.4 us (26%)
  waiting for transfers between devices  12.1 us (21%)
  blocking collectives  11.5 us (20%)
  between operations  0.82 us (1%)
    all_to_all x1, blocking collectives, on_device(): got = lax.all_to_all(sent, (place.near, place.second, place.first), 0, 0)  11.5 us
    ppermute x6, waiting for transfers between devices, swap_by_core(): return lax.ppermute(value, names, pairs)  11.3 us
    ppermute x6, starting transfers between devices, swap_by_core(): return lax.ppermute(value, names, pairs)  10.9 us
    pallas_call x3, Pallas kernels, sweep_call(): pl.pallas_call(kernel, in_specs=[VMEM] * len(args), out_specs=[VMEM] * le...  8.44 us
    ppermute x7, starting transfers between devices, swap(): return lax.ppermute(value, axis, [(0, 1), (1, 0)])  6.97 us
    pallas_call x1, Pallas kernels, hot_squares(): pl.pallas_call(functools.partial(hot_kernel, place), in_specs=[HBM, HBM],...  3.58 us
    pallas_call x1, Pallas kernels, mixed_sums(): pl.pallas_call(functools.partial(mixed_kernel, place), in_specs=[SMEM, VM...  1.45 us
  transfers between devices with their start and end apart: 13, of which 7 were waited for; matrix products, arithmetic and copies ran while one was open for 1% of the time, Pallas kernels for 18%

profile of v18, /device:TPU:0, one launch (start us, length us, event | category | flops | bytes accessed | tf_op | source)
XLA Modules:
  0.0 58.1 jit_solution(15626621168479272185)
XLA Ops:
  0.6 3.6 %hot_squares.1 = (f32[8,168,128]{2,1,0:T(8,128)S(1)}, f32[8,168,128]{2,1,0:T(8,128)S(1)}, bf16[8,768,256]{2,1,0:T(8,128)(2,1)S(1)}, bf16[8,768,128]{2,1,0:T(8,128)(2,1)S(1)}) custom-call(bf16[8,768,256]{2,1,0:T(8,128)(2,1)} %wide_hbm.1, bf16[8,768,128]{2,1,0:T(8,128)(2,1)} %narrow_hbm.1), custom_call_target="tpu_custom_call" | custom-call | flops 754974720 | bytes 3145728 | tf_op jit(solution)/shard_map/hot_squares/pallas_call | solution.py:267
  4.3 0.5 collective-permute-start
  4.8 0.6 cold_squares.1
  5.4 0.7 %collective-permute-done = f32[4,168,128]{2,1,0:T(8,128)S(1)} collective-permute-done((f32[4,168,128]{2,1,0:T(8,128)S(1)}, f32[4,168,128]{2,1,0:T(8,128)S(1)}, u32[]{:S(2)}, u32[]{:S(2)}) %collective-permute-start) | collective-permute-done | bytes 344096 | tf_op jit(solution)/shard_map/ppermute | solution.py:803
  6.1 2.9 %collective-permute-start.1 = (f32[4,168,128]{2,1,0:T(8,128)S(1)}, f32[4,168,128]{2,1,0:T(8,128)S(1)}, u32[]{:S(2)}, u32[]{:S(2)}) collective-permute-start(f32[4,168,128]{2,1,0:T(8,128)S(1)} %slice_add_fusion.1), channel_id=1, source_target_pairs={{0,1},{1,0},{2,6},{3,7},{4,5},{5,4},{6,2},{7,3},{8,9},{9,8},{10,14... | collective-permute-start | bytes 1032200 | tf_op jit(solution)/shard_map/ppermute | solution.py:810
  9.0 1.4 %mixed.1 = (f32[8,128,128]{2,1,0:T(8,128)S(1)}, f32[8,128,128]{2,1,0:T(8,128)S(1)}, s32[8,8,128]{2,1,0:T(8,128)S(1)}) custom-call(s32[8]{0:T(128)S(1)} %copy-done, bf16[8,768,256]{2,1,0:T(8,128)(2,1)S(1)} %get-tuple-element.47.wides, bf16[8,768,128]{2,1,0:T(8,128)(2,1)S(1)} %get-tuple-element.44.narrows), custom_call_target="tpu_custom_call" | custom-call | flops 402653184 | bytes 3145728 | tf_op jit(solution)/shard_map/mixed/pallas_call | solution.py:304
  10.6 0.6 collective-permute-start.2
  11.2 3.1 %collective-permute-done.1 = f32[4,168,128]{2,1,0:T(8,128)S(1)} collective-permute-done((f32[4,168,128]{2,1,0:T(8,128)S(1)}, f32[4,168,128]{2,1,0:T(8,128)S(1)}, u32[]{:S(2)}, u32[]{:S(2)}) %collective-permute-start.1) | collective-permute-done | bytes 344096 | tf_op jit(solution)/shard_map/ppermute | solution.py:810
  14.4 2.1 %collective-permute-start.3 = (f32[2,168,128]{2,1,0:T(8,128)S(1)}, f32[2,168,128]{2,1,0:T(8,128)S(1)}, u32[]{:S(2)}, u32[]{:S(2)}) collective-permute-start(f32[2,168,128]{2,1,0:T(8,128)S(1)} %slice.57), channel_id=1, source_target_pairs={{0,4},{1,5},{2,10},{3,11},{4,0},{5,1},{6,14},{7,15},{8,12},{9,13},... | collective-permute-start | bytes 516104 | tf_op jit(solution)/shard_map/ppermute | solution.py:810
  16.7 3.2 %collective-permute-done.3 = f32[2,168,128]{2,1,0:T(8,128)S(1)} collective-permute-done((f32[2,168,128]{2,1,0:T(8,128)S(1)}, f32[2,168,128]{2,1,0:T(8,128)S(1)}, u32[]{:S(2)}, u32[]{:S(2)}) %collective-permute-start.3) | collective-permute-done | bytes 172064 | tf_op jit(solution)/shard_map/ppermute | solution.py:810
  19.9 2.1 %collective-permute-start.4 = (f32[168,128]{1,0:T(8,128)S(1)}, f32[168,128]{1,0:T(8,128)S(1)}, u32[]{:S(2)}, u32[]{:S(2)}) collective-permute-start(f32[168,128]{1,0:T(8,128)S(1)} %slice_bitcast_fusion), channel_id=1, source_target_pairs={{0,8},{1,9},{2,3},{3,2},{4,12},{5,13},{6,7},{7,6},{8,0},{9,1},{10,... | collective-permute-start | bytes 258056 | tf_op jit(solution)/shard_map/ppermute | solution.py:810
  22.1 1.0 %collective-permute-done.7 = f32[4,128,128]{2,1,0:T(8,128)S(1)} collective-permute-done((f32[4,128,128]{2,1,0:T(8,128)S(1)}, f32[4,128,128]{2,1,0:T(8,128)S(1)}, u32[]{:S(2)}, u32[]{:S(2)}) %collective-permute-start.7) | collective-permute-done | bytes 262176 | tf_op jit(solution)/shard_map/ppermute | solution.py:810
  23.1 2.0 %collective-permute-start.8 = (f32[2,128,128]{2,1,0:T(8,128)S(1)}, f32[2,128,128]{2,1,0:T(8,128)S(1)}, u32[]{:S(2)}, u32[]{:S(2)}) collective-permute-start(f32[2,128,128]{2,1,0:T(8,128)S(1)} %get-tuple-element.80), channel_id=1, source_target_pairs={{0,8},{1,9},{2,6},{3,7},{4,12},{5,13},{6,2},{7,3},{8,0},{9,1},{10,... | collective-permute-start | bytes 393224 | tf_op jit(solution)/shard_map/ppermute | solution.py:810
  25.2 2.6 %collective-permute-start.5 = (f32[168,128]{1,0:T(8,128)S(1)}, f32[168,128]{1,0:T(8,128)S(1)}, u32[]{:S(2)}, u32[]{:S(2)}) collective-permute-start(f32[168,128]{1,0:T(8,128)S(1)} %fusion), channel_id=1, source_target_pairs={{0,16},{16,0},{1,17},{17,1},{2,18},{18,2},{3,19},{19,3},{4,20},{20... | collective-permute-start | bytes 258056 | tf_op jit(solution)/shard_map/ppermute | solution.py:803
  27.8 1.3 %collective-permute-done.8 = f32[2,128,128]{2,1,0:T(8,128)S(1)} collective-permute-done((f32[2,128,128]{2,1,0:T(8,128)S(1)}, f32[2,128,128]{2,1,0:T(8,128)S(1)}, u32[]{:S(2)}, u32[]{:S(2)}) %collective-permute-start.8) | collective-permute-done | bytes 131104 | tf_op jit(solution)/shard_map/ppermute | solution.py:810
  29.2 1.6 %collective-permute-start.9 = (f32[128,128]{1,0:T(8,128)S(1)}, f32[128,128]{1,0:T(8,128)S(1)}, u32[]{:S(2)}, u32[]{:S(2)}) collective-permute-start(f32[128,128]{1,0:T(8,128)S(1)} %get-tuple-element.82), channel_id=1, source_target_pairs={{0,1},{1,0},{2,10},{3,11},{4,5},{5,4},{6,14},{7,15},{8,9},{9,8},{1... | collective-permute-start | bytes 196616 | tf_op jit(solution)/shard_map/ppermute | solution.py:810
  30.8 2.7 %collective-permute-done.9 = f32[128,128]{1,0:T(8,128)S(1)} collective-permute-done((f32[128,128]{1,0:T(8,128)S(1)}, f32[128,128]{1,0:T(8,128)S(1)}, u32[]{:S(2)}, u32[]{:S(2)}) %collective-permute-start.9) | collective-permute-done | bytes 65568 | tf_op jit(solution)/shard_map/ppermute | solution.py:810
  33.6 2.9 %collective-permute-start.11 = (f32[128,128]{1,0:T(8,128)S(1)}, f32[128,128]{1,0:T(8,128)S(1)}, u32[]{:S(2)}, u32[]{:S(2)}) collective-permute-start(f32[128,128]{1,0:T(8,128)S(1)} %add.50), channel_id=1, source_target_pairs={{0,16},{16,0},{1,17},{17,1},{2,18},{18,2},{3,19},{19,3},{4,20},{20... | collective-permute-start | bytes 196616 | tf_op jit(solution)/shard_map/ppermute | solution.py:803
  36.5 3.2 %first_panels.1 = (f32[288,256]{1,0:T(8,128)S(1)}, bf16[96,256]{1,0:T(8,128)(2,1)S(1)}, bf16[96,256]{1,0:T(8,128)(2,1)S(1)}, f32[16,256]{1,0:T(8,128)S(1)}, f32[...) custom-call(f32[168,128]{1,0:T(8,128)S(1)} %add.46.mine, ...), custom_call_target="tpu_custom_call" | custom-call | flops 1073741824 | bytes 1048576 | tf_op jit(solution)/shard_map/first_panels/pallas_call | solution.py:655
  39.7 4.3 %second_panels.1 = (f32[128,128]{1,0:T(8,128)S(1)}, f32[288,256]{1,0:T(8,128)S(1)}, bf16[96,256]{1,0:T(8,128)(2,1)S(1)}, bf16[96,256]{1,0:T(8,128)(2,1)S(1)}, f32[16,256]{1,0:T(8,128)S(1)}) custom-call(f32[288,256]{1,0:T(8,128)S(1)} %get-tuple-element.60.refs_0_, bf16[96,256]{1,0:T(8,128)(2,1)S(1)} %get-tuple-element.61.refs_1_, ...), custom_call_target="tpu_custom_call" | custom-call | flops 1073741824 | bytes 1048576 | tf_op jit(solution)/shard_map/second_panels/pallas_call | solution.py:655
  44.2 1.0 %third_panels.1.winv = f32[256,256]{1,0:T(8,128)S(1)} custom-call(f32[288,256]{1,0:T(8,128)S(1)} %get-tuple-element.69.wa_in, bf16[96,256]{1,0:T(8,128)(2,1)S(1)} %get-tuple-element.70.wl_in, bf16[96,256]{1,0:T(8,128)(2,1)S(1)} %get-tuple-element.71.wr_in, f32[16,256]{1,0:T(8,128)S(1)} %get-tuple-element.72.panel_in, f32[8,256]{1,0:T(8,128)S(1)} %get-tuple-element.73.scale), custom_call_target="tpu_custom_call" | custom-call | flops 1073741824 | bytes 1048576 | tf_op jit(solution)/shard_map/third_panels/pallas_call | solution.py:655
  45.3 0.6 %products.1 = f32[8,40,128]{2,1,0:T(8,128)S(1)} custom-call(f32[256,256]{1,0:T(8,128)S(1)} %third_panels.1.winv, f32[128,128]{1,0:T(8,128)S(1)} %get-tuple-element.74.ninv_ref, f32[128,128]{1,0:T(8,128)S(1)} %add.51.mine, f32[128,128]{1,0:T(8,128)S(1)} %collective-permute-done.12.other), custom_call_target="tpu_custom_call" | custom-call | tf_op jit(solution)/shard_map/products/pallas_call | solution.py:746
  45.9 11.5 %all_to_all.5.got_ref = f32[8,40,128]{2,1,0:T(8,128)S(1)} all-to-all(f32[8,40,128]{2,1,0:T(8,128)S(1)} %products.1), channel_id=1, replica_groups=mesh['dp0'=2,'dp1'=2,'dp2'=2,'dp3'=2,'own0'=2] {'dp1','dp2','own0'}, dimensions={0} | all-to-all | bytes 327680 | tf_op jit(solution)/shard_map/all_to_all | solution.py:867
  57.4 0.7 %placing.1 = (f32[5,16,256]{2,1,0:T(8,128)}, f32[8,16,64]{2,1,0:T(8,128)}) custom-call(s32[8,8,128]{2,1,0:T(8,128)S(1)} %get-tuple-element.48.slots_ref, f32[8,40,128]{2,1,0:T(8,128)S(1)} %all_to_all.5.got_ref), custom_call_target="tpu_custom_call" | custom-call | tf_op jit(solution)/shard_map/placing/pallas_call | solution.py:789
  (31 shorter events, 1.0 us)
Async XLA Ops:
  4.2 4.8 %copy-start = (s32[8]{0:T(128)S(1)}, s32[8]{0:T(128)}, u32[]{:S(2)}) copy-start(s32[8]{0:T(128)} %owner_map.1) | copy-start | bytes 100
  4.3 1.8 %collective-permute-start = (f32[4,168,128]{2,1,0:T(8,128)S(1)}, f32[4,168,128]{2,1,0:T(8,128)S(1)}, u32[]{:S(2)}, u32[]{:S(2)}) collective-permute-start(f32[4,168,128]{2,1,0:T(8,128)S(1)} %slice.42), channel_id=1, source_target_pairs={{0,2},{2,0},{1,3},{3,1},{4,6},{6,4},{5,7},{7,5},{8,10},{10,8},{9,1... | collective-permute-start | bytes 1032200 | tf_op jit(solution)/shard_map/ppermute | solution.py:803
  6.1 8.2 %collective-permute-start.1 = (f32[4,168,128]{2,1,0:T(8,128)S(1)}, f32[4,168,128]{2,1,0:T(8,128)S(1)}, u32[]{:S(2)}, u32[]{:S(2)}) collective-permute-start(f32[4,168,128]{2,1,0:T(8,128)S(1)} %slice_add_fusion.1), channel_id=1, source_target_pairs={{0,1},{1,0},{2,6},{3,7},{4,5},{5,4},{6,2},{7,3},{8,9},{9,8},{10,14... | collective-permute-start | bytes 1032200 | tf_op jit(solution)/shard_map/ppermute | solution.py:810
  10.5 6.0 %collective-permute-start.6 = (f32[8,128,128]{2,1,0:T(8,128)S(1)}, f32[8,128,128]{2,1,0:T(8,128)S(1)}, u32[]{:S(2)}, u32[]{:S(2)}) collective-permute-start(f32[8,128,128]{2,1,0:T(8,128)S(1)} %get-tuple-element.51), channel_id=1, source_target_pairs={{0,2},{2,0},{1,3},{3,1},{4,6},{6,4},{5,7},{7,5},{8,10},{10,8},{9,1... | collective-permute-start | bytes 1572872 | tf_op jit(solution)/shard_map/ppermute | solution.py:803
  10.6 3.7 %collective-permute-start.2 = (f32[4,168,128]{2,1,0:T(8,128)S(1)}, f32[4,168,128]{2,1,0:T(8,128)S(1)}, u32[]{:S(2)}, u32[]{:S(2)}) collective-permute-start(f32[4,168,128]{2,1,0:T(8,128)S(1)} %slice_add_fusion), channel_id=1, source_target_pairs={{0,2},{2,0},{1,3},{3,1},{4,6},{6,4},{5,7},{7,5},{8,10},{10,8},{9,1... | collective-permute-start | bytes 1032200 | tf_op jit(solution)/shard_map/ppermute | solution.py:803
  14.4 5.5 %collective-permute-start.3 = (f32[2,168,128]{2,1,0:T(8,128)S(1)}, f32[2,168,128]{2,1,0:T(8,128)S(1)}, u32[]{:S(2)}, u32[]{:S(2)}) collective-permute-start(f32[2,168,128]{2,1,0:T(8,128)S(1)} %slice.57), channel_id=1, source_target_pairs={{0,4},{1,5},{2,10},{3,11},{4,0},{5,1},{6,14},{7,15},{8,12},{9,13},... | collective-permute-start | bytes 516104 | tf_op jit(solution)/shard_map/ppermute | solution.py:810
  16.6 6.4 %collective-permute-start.7 = (f32[4,128,128]{2,1,0:T(8,128)S(1)}, f32[4,128,128]{2,1,0:T(8,128)S(1)}, u32[]{:S(2)}, u32[]{:S(2)}) collective-permute-start(f32[4,128,128]{2,1,0:T(8,128)S(1)} %get-tuple-element.78), channel_id=1, source_target_pairs={{0,4},{1,5},{2,3},{3,2},{4,0},{5,1},{6,7},{7,6},{8,12},{9,13},{10,... | collective-permute-start | bytes 786440 | tf_op jit(solution)/shard_map/ppermute | solution.py:810
  19.9 5.2 %collective-permute-start.4 = (f32[168,128]{1,0:T(8,128)S(1)}, f32[168,128]{1,0:T(8,128)S(1)}, u32[]{:S(2)}, u32[]{:S(2)}) collective-permute-start(f32[168,128]{1,0:T(8,128)S(1)} %slice_bitcast_fusion), channel_id=1, source_target_pairs={{0,8},{1,9},{2,3},{3,2},{4,12},{5,13},{6,7},{7,6},{8,0},{9,1},{10,... | collective-permute-start | bytes 258056 | tf_op jit(solution)/shard_map/ppermute | solution.py:810
  23.1 6.0 %collective-permute-start.8 = (f32[2,128,128]{2,1,0:T(8,128)S(1)}, f32[2,128,128]{2,1,0:T(8,128)S(1)}, u32[]{:S(2)}, u32[]{:S(2)}) collective-permute-start(f32[2,128,128]{2,1,0:T(8,128)S(1)} %get-tuple-element.80), channel_id=1, source_target_pairs={{0,8},{1,9},{2,6},{3,7},{4,12},{5,13},{6,2},{7,3},{8,0},{9,1},{10,... | collective-permute-start | bytes 393224 | tf_op jit(solution)/shard_map/ppermute | solution.py:810
  25.2 5.6 %collective-permute-start.5 = (f32[168,128]{1,0:T(8,128)S(1)}, f32[168,128]{1,0:T(8,128)S(1)}, u32[]{:S(2)}, u32[]{:S(2)}) collective-permute-start(f32[168,128]{1,0:T(8,128)S(1)} %fusion), channel_id=1, source_target_pairs={{0,16},{16,0},{1,17},{17,1},{2,18},{18,2},{3,19},{19,3},{4,20},{20... | collective-permute-start | bytes 258056 | tf_op jit(solution)/shard_map/ppermute | solution.py:803
  29.2 4.3 %collective-permute-start.9 = (f32[128,128]{1,0:T(8,128)S(1)}, f32[128,128]{1,0:T(8,128)S(1)}, u32[]{:S(2)}, u32[]{:S(2)}) collective-permute-start(f32[128,128]{1,0:T(8,128)S(1)} %get-tuple-element.82), channel_id=1, source_target_pairs={{0,1},{1,0},{2,10},{3,11},{4,5},{5,4},{6,14},{7,15},{8,9},{9,8},{1... | collective-permute-start | bytes 196616 | tf_op jit(solution)/shard_map/ppermute | solution.py:810
  33.5 3.0 %collective-permute-start.10 = (f32[168,128]{1,0:T(8,128)S(1)}, f32[168,128]{1,0:T(8,128)S(1)}, u32[]{:S(2)}, u32[]{:S(2)}) collective-permute-start(f32[168,128]{1,0:T(8,128)S(1)} %add.46.mine), channel_id=1, source_target_pairs={{0,2},{2,0},{1,3},{3,1},{4,6},{6,4},{5,7},{7,5},{8,10},{10,8},{9,1... | collective-permute-start | bytes 258056 | tf_op jit(solution)/shard_map/ppermute | solution.py:803
  33.6 10.3 %collective-permute-start.11 = (f32[128,128]{1,0:T(8,128)S(1)}, f32[128,128]{1,0:T(8,128)S(1)}, u32[]{:S(2)}, u32[]{:S(2)}) collective-permute-start(f32[128,128]{1,0:T(8,128)S(1)} %add.50), channel_id=1, source_target_pairs={{0,16},{16,0},{1,17},{17,1},{2,18},{18,2},{3,19},{19,3},{4,20},{20... | collective-permute-start | bytes 196616 | tf_op jit(solution)/shard_map/ppermute | solution.py:803
  44.0 1.3 %collective-permute-start.12 = (f32[128,128]{1,0:T(8,128)S(1)}, f32[128,128]{1,0:T(8,128)S(1)}, u32[]{:S(2)}, u32[]{:S(2)}) collective-permute-start(f32[128,128]{1,0:T(8,128)S(1)} %add.51.mine), channel_id=1, source_target_pairs={{0,2},{2,0},{1,3},{3,1},{4,6},{6,4},{5,7},{7,5},{8,10},{10,8},{9,1... | collective-permute-start | bytes 196616 | tf_op jit(solution)/shard_map/ppermute | solution.py:803

commit v19 on v17

--- a/solution.py
+++ b/solution.py
@@ -714,9 +714,10 @@
     near, second = lax.axis_index(place.near), lax.axis_index(place.second)
     near_stride = 2 ** (len(place.dp) - 2)
     base = place.index(place.dp) - near * near_stride - second * 2
+    halves = (near * near_stride, (1 - near) * near_stride)
     _, lane = iotas((PANEL, LANES))
     picks = [
-        aligned_rows(winv, base + (j // 2) * near_stride + (j % 2) * 2, cols) for j in range(4)
+        aligned_rows(winv, base + halves[j // 2] + (j % 2) * 2, cols) for j in range(4)
     ]
     if cols % PANEL == 0:
         whole = dot(jnp.concatenate(picks, axis=0), inner)
@@ -725,18 +726,18 @@
         updates = [dot(picked, inner) for picked in picks]
     for j, (picked, update) in enumerate(zip(picks, updates)):
         for x in range(2):
-            block = 2 * j + x
-            out_ref[block, :cols] = picked[:, :LANES]
-            out_ref[block, cols : 2 * cols] = picked[:, LANES:]
+            block = (j // 2, 2 * (j % 2) + x)
+            out_ref[*block, :cols] = picked[:, :LANES]
+            out_ref[*block, cols : 2 * cols] = picked[:, LANES:]
             if packs(cols, rows):
                 upper, lower = update[:PANEL], update[PANEL:]
                 if x == 0:
                     lower = pltpu.roll(lower, rows, 1)
                 else:
                     upper = pltpu.roll(upper, rows, 1)
-                out_ref[block, 2 * cols :] = jnp.where(lane < rows, upper, lower)
+                out_ref[*block, 2 * cols :] = jnp.where(lane < rows, upper, lower)
             else:
-                out_ref[block, 2 * cols :] = update
+                out_ref[*block, 2 * cols :] = update
 
 
 def products(place, winv, ninv, pieces, rows, total):
@@ -747,7 +748,7 @@
         functools.partial(product_kernel, place, total, rows),
         in_specs=[VMEM] * 4,
         out_specs=VMEM,
-        out_shape=jax.ShapeDtypeStruct((8, height, LANES), jnp.float32),
+        out_shape=jax.ShapeDtypeStruct((2, 4, height, LANES), jnp.float32),
         scratch_shapes=[pltpu.VMEM((2 * narrow, LANES), jnp.float32)],
         compiler_params=PARAMS,
         name="products",
@@ -755,7 +756,10 @@
 
 
 def placing_kernel(place, slots_ref, got_ref, kept_ref, update_ref):
-    layers = got_ref.shape[0]
+    near = lax.axis_index(place.near)
+    layers = slots_ref.shape[0]
+    got = [(i // 2, i % 2) for i in range(layers)]
+    layer = [jnp.bitwise_xor(near, r) * 4 + at for at, r in got]
     slots, cols, wide = kept_ref.shape
     rows = update_ref.shape[2]
     own, dp = place.index(place.own), place.index(place.dp)
@@ -769,23 +773,23 @@
             for c in range(slots):
                 value = empty
                 for l in range(layers):
-                    taken = slots_ref[l, :step] == c
-                    value = jnp.where(taken, got_ref[l, here : here + step], value)
+                    taken = slots_ref[layer[l], :step] == c
+                    value = jnp.where(taken, got_ref[*got[l], here : here + step], value)
                 kept_ref[c, r : r + step, lanes] = value
     for l in range(layers):
-        value = got_ref[l, 2 * cols :]
+        value = got_ref[*got[l], 2 * cols :]
         if packs(cols, rows):
-            update_ref[l, :PANEL] = value[:, :rows]
-            update_ref[l, PANEL:] = value[:, rows:]
+            update_ref[layer[l], :PANEL] = value[:, :rows]
+            update_ref[layer[l], PANEL:] = value[:, rows:]
         else:
             part = value[:, :rows]
             for p in range(1, LANES // rows):
                 part = jnp.where(own == p, value[:, p * rows : (p + 1) * rows], part)
-            update_ref[l] = part
+            update_ref[layer[l]] = part
 
 
 def placing(place, slots_of, got, wide, cols, slots, rows):
-    layers = got.shape[0]
+    layers = slots_of.shape[0]
     return pl.pallas_call(
         functools.partial(placing_kernel, place),
         in_specs=[VMEM, VMEM],
@@ -864,7 +868,8 @@
     winv = third_panels([*state, wide_scale], wide)
     cols, own_rows = wide // n_dp, narrow // n_own
     sent = products(place, winv, ninv, [m, m_got], own_rows, total)
-    got = lax.all_to_all(sent, (place.near, place.second, place.first), 0, 0)
+    sent = jnp.stack([sent[0], swap(sent[1], place.near)], axis=1)
+    got = lax.all_to_all(sent, (place.second, place.first), 0, 0)
     kept, update = placing(
         place, slots_of, got, wide, cols, layers // n_own + 1, own_rows
     )

time: 56.5 us -> 59.5 us (1.053)
  waiting for transfers between devices: 12.6 us -> 15.5 us
  starting transfers between devices: 16.4 us -> 18.3 us
  blocking collectives: 10.6 us -> 8.88 us
    ppermute x7 -> x8, waiting for transfers between devices: 5.32 us -> 8.2 us  [swap(): return lax.ppermute(value, axis, [(0, 1), (1, 0)])]
    ppermute x7 -> x8, starting transfers between devices: 6.44 us -> 8.3 us  [swap(): return lax.ppermute(value, axis, [(0, 1), (1, 0)])]
    all_to_all x1, blocking collectives: 10.6 us -> 8.88 us  [on_device(): got = lax.all_to_all(sent, (place.second, place.first), 0, 0)]
  transfers between devices with their start and end apart: 13 -> 14, of which waited for: 7 -> 8; matrix products, arithmetic and copies ran while one was open for 1% -> 1% of each run, Pallas kernels for 19% -> 18%
where the time goes in v19:
time: 59.5 us; the launch traced here: 59.3 us
  starting transfers between devices  18.3 us (31%)
  waiting for transfers between devices  15.5 us (26%)
  Pallas kernels  15.4 us (26%)
  blocking collectives  8.88 us (15%)
  between operations  0.85 us (1%)
    ppermute x6, starting transfers between devices, swap_by_core(): return lax.ppermute(value, names, pairs)  9.95 us
    all_to_all x1, blocking collectives, on_device(): got = lax.all_to_all(sent, (place.second, place.first), 0, 0)  8.88 us
    pallas_call x3, Pallas kernels, sweep_call(): pl.pallas_call(kernel, in_specs=[VMEM] * len(args), out_specs=[VMEM] * le...  8.43 us
    ppermute x8, starting transfers between devices, swap(): return lax.ppermute(value, axis, [(0, 1), (1, 0)])  8.3 us
    ppermute x8, waiting for transfers between devices, swap(): return lax.ppermute(value, axis, [(0, 1), (1, 0)])  8.2 us
    ppermute x6, waiting for transfers between devices, swap_by_core(): return lax.ppermute(value, names, pairs)  7.27 us
    pallas_call x1, Pallas kernels, hot_squares(): pl.pallas_call(functools.partial(hot_kernel, place), in_specs=[HBM, HBM],...  3.58 us
    pallas_call x1, Pallas kernels, mixed_sums(): pl.pallas_call(functools.partial(mixed_kernel, place), in_specs=[SMEM, VM...  1.45 us
  transfers between devices with their start and end apart: 14, of which 8 were waited for; matrix products, arithmetic and copies ran while one was open for 1% of the time, Pallas kernels for 18%

profile of v19, /device:TPU:0, one launch (start us, length us, event | category | flops | bytes accessed | tf_op | source)
XLA Modules:
  0.0 59.3 jit_solution(3415363668254320489)
XLA Ops:
  0.6 3.6 %hot_squares.1 = (f32[8,168,128]{2,1,0:T(8,128)S(1)}, f32[8,168,128]{2,1,0:T(8,128)S(1)}, bf16[8,768,256]{2,1,0:T(8,128)(2,1)S(1)}, bf16[8,768,128]{2,1,0:T(8,128)(2,1)S(1)}) custom-call(bf16[8,768,256]{2,1,0:T(8,128)(2,1)} %wide_hbm.1, bf16[8,768,128]{2,1,0:T(8,128)(2,1)} %narrow_hbm.1), custom_call_target="tpu_custom_call" | custom-call | flops 754974720 | bytes 3145728 | tf_op jit(solution)/shard_map/hot_squares/pallas_call | solution.py:267
  4.8 0.6 cold_squares.1
  5.4 0.7 %collective-permute-done = f32[4,168,128]{2,1,0:T(8,128)S(1)} collective-permute-done((f32[4,168,128]{2,1,0:T(8,128)S(1)}, f32[4,168,128]{2,1,0:T(8,128)S(1)}, u32[]{:S(2)}, u32[]{:S(2)}) %collective-permute-start) | collective-permute-done | bytes 344096 | tf_op jit(solution)/shard_map/ppermute | solution.py:807
  6.1 2.9 %collective-permute-start.1 = (f32[4,168,128]{2,1,0:T(8,128)S(1)}, f32[4,168,128]{2,1,0:T(8,128)S(1)}, u32[]{:S(2)}, u32[]{:S(2)}) collective-permute-start(f32[4,168,128]{2,1,0:T(8,128)S(1)} %slice_add_fusion.1), channel_id=1, source_target_pairs={{0,1},{1,0},{2,6},{3,7},{4,5},{5,4},{6,2},{7,3},{8,9},{9,8},{10,14... | collective-permute-start | bytes 1032200 | tf_op jit(solution)/shard_map/ppermute | solution.py:814
  9.0 1.4 %mixed.1 = (f32[8,128,128]{2,1,0:T(8,128)S(1)}, f32[8,128,128]{2,1,0:T(8,128)S(1)}, s32[8,8,128]{2,1,0:T(8,128)S(1)}) custom-call(s32[8]{0:T(128)S(1)} %copy-done, bf16[8,768,256]{2,1,0:T(8,128)(2,1)S(1)} %get-tuple-element.46.wides, bf16[8,768,128]{2,1,0:T(8,128)(2,1)S(1)} %get-tuple-element.43.narrows), custom_call_target="tpu_custom_call" | custom-call | flops 402653184 | bytes 3145728 | tf_op jit(solution)/shard_map/mixed/pallas_call | solution.py:304
  11.2 3.1 %collective-permute-done.1 = f32[4,168,128]{2,1,0:T(8,128)S(1)} collective-permute-done((f32[4,168,128]{2,1,0:T(8,128)S(1)}, f32[4,168,128]{2,1,0:T(8,128)S(1)}, u32[]{:S(2)}, u32[]{:S(2)}) %collective-permute-start.1) | collective-permute-done | bytes 344096 | tf_op jit(solution)/shard_map/ppermute | solution.py:814
  14.4 2.1 %collective-permute-start.3 = (f32[2,168,128]{2,1,0:T(8,128)S(1)}, f32[2,168,128]{2,1,0:T(8,128)S(1)}, u32[]{:S(2)}, u32[]{:S(2)}) collective-permute-start(f32[2,168,128]{2,1,0:T(8,128)S(1)} %slice.65), channel_id=1, source_target_pairs={{0,4},{1,5},{2,10},{3,11},{4,0},{5,1},{6,14},{7,15},{8,12},{9,13},... | collective-permute-start | bytes 516104 | tf_op jit(solution)/shard_map/ppermute | solution.py:814
  16.7 3.2 %collective-permute-done.3 = f32[2,168,128]{2,1,0:T(8,128)S(1)} collective-permute-done((f32[2,168,128]{2,1,0:T(8,128)S(1)}, f32[2,168,128]{2,1,0:T(8,128)S(1)}, u32[]{:S(2)}, u32[]{:S(2)}) %collective-permute-start.3) | collective-permute-done | bytes 172064 | tf_op jit(solution)/shard_map/ppermute | solution.py:814
  19.9 2.1 %collective-permute-start.4 = (f32[168,128]{1,0:T(8,128)S(1)}, f32[168,128]{1,0:T(8,128)S(1)}, u32[]{:S(2)}, u32[]{:S(2)}) collective-permute-start(f32[168,128]{1,0:T(8,128)S(1)} %slice_bitcast_fusion), channel_id=1, source_target_pairs={{0,8},{1,9},{2,3},{3,2},{4,12},{5,13},{6,7},{7,6},{8,0},{9,1},{10,... | collective-permute-start | bytes 258056 | tf_op jit(solution)/shard_map/ppermute | solution.py:814
  22.1 1.0 %collective-permute-done.8 = f32[4,128,128]{2,1,0:T(8,128)S(1)} collective-permute-done((f32[4,128,128]{2,1,0:T(8,128)S(1)}, f32[4,128,128]{2,1,0:T(8,128)S(1)}, u32[]{:S(2)}, u32[]{:S(2)}) %collective-permute-start.8) | collective-permute-done | bytes 262176 | tf_op jit(solution)/shard_map/ppermute | solution.py:814
  23.1 2.0 %collective-permute-start.9 = (f32[2,128,128]{2,1,0:T(8,128)S(1)}, f32[2,128,128]{2,1,0:T(8,128)S(1)}, u32[]{:S(2)}, u32[]{:S(2)}) collective-permute-start(f32[2,128,128]{2,1,0:T(8,128)S(1)} %get-tuple-element.78), channel_id=1, source_target_pairs={{0,8},{1,9},{2,6},{3,7},{4,12},{5,13},{6,2},{7,3},{8,0},{9,1},{10,... | collective-permute-start | bytes 393224 | tf_op jit(solution)/shard_map/ppermute | solution.py:814
  25.2 2.6 %collective-permute-start.5 = (f32[168,128]{1,0:T(8,128)S(1)}, f32[168,128]{1,0:T(8,128)S(1)}, u32[]{:S(2)}, u32[]{:S(2)}) collective-permute-start(f32[168,128]{1,0:T(8,128)S(1)} %fusion), channel_id=1, source_target_pairs={{0,16},{16,0},{1,17},{17,1},{2,18},{18,2},{3,19},{19,3},{4,20},{20... | collective-permute-start | bytes 258056 | tf_op jit(solution)/shard_map/ppermute | solution.py:807
  27.8 3.7 %collective-permute-done.5 = f32[168,128]{1,0:T(8,128)S(1)} collective-permute-done((f32[168,128]{1,0:T(8,128)S(1)}, f32[168,128]{1,0:T(8,128)S(1)}, u32[]{:S(2)}, u32[]{:S(2)}) %collective-permute-start.5) | collective-permute-done | bytes 86048 | tf_op jit(solution)/shard_map/ppermute | solution.py:807
  31.7 0.6 %collective-permute-start.10 = (f32[128,128]{1,0:T(8,128)S(1)}, f32[128,128]{1,0:T(8,128)S(1)}, u32[]{:S(2)}, u32[]{:S(2)}) collective-permute-start(f32[128,128]{1,0:T(8,128)S(1)} %get-tuple-element.82), channel_id=1, source_target_pairs={{0,1},{1,0},{2,10},{3,11},{4,5},{5,4},{6,14},{7,15},{8,9},{9,8},{1... | collective-permute-start | bytes 196616 | tf_op jit(solution)/shard_map/ppermute | solution.py:814
  32.4 0.6 collective-permute-done.6.other
  32.9 3.2 %first_panels.1 = (f32[288,256]{1,0:T(8,128)S(1)}, bf16[96,256]{1,0:T(8,128)(2,1)S(1)}, bf16[96,256]{1,0:T(8,128)(2,1)S(1)}, f32[16,256]{1,0:T(8,128)S(1)}, f32[...) custom-call(f32[168,128]{1,0:T(8,128)S(1)} %add.46.mine, ...), custom_call_target="tpu_custom_call" | custom-call | flops 1073741824 | bytes 1048576 | tf_op jit(solution)/shard_map/first_panels/pallas_call | solution.py:655
  36.1 2.2 %collective-permute-start.11 = (f32[128,128]{1,0:T(8,128)S(1)}, f32[128,128]{1,0:T(8,128)S(1)}, u32[]{:S(2)}, u32[]{:S(2)}) collective-permute-start(f32[128,128]{1,0:T(8,128)S(1)} %add.50), channel_id=1, source_target_pairs={{0,16},{16,0},{1,17},{17,1},{2,18},{18,2},{3,19},{19,3},{4,20},{20... | collective-permute-start | bytes 196616 | tf_op jit(solution)/shard_map/ppermute | solution.py:807
  38.3 4.2 %second_panels.1 = (f32[128,128]{1,0:T(8,128)S(1)}, f32[288,256]{1,0:T(8,128)S(1)}, bf16[96,256]{1,0:T(8,128)(2,1)S(1)}, bf16[96,256]{1,0:T(8,128)(2,1)S(1)}, f32[16,256]{1,0:T(8,128)S(1)}) custom-call(f32[288,256]{1,0:T(8,128)S(1)} %get-tuple-element.53.refs_0_, bf16[96,256]{1,0:T(8,128)(2,1)S(1)} %get-tuple-element.54.refs_1_, ...), custom_call_target="tpu_custom_call" | custom-call | flops 1073741824 | bytes 1048576 | tf_op jit(solution)/shard_map/second_panels/pallas_call | solution.py:655
  43.3 1.0 %third_panels.1.winv = f32[256,256]{1,0:T(8,128)S(1)} custom-call(f32[288,256]{1,0:T(8,128)S(1)} %get-tuple-element.62.wa_in, bf16[96,256]{1,0:T(8,128)(2,1)S(1)} %get-tuple-element.63.wl_in, bf16[96,256]{1,0:T(8,128)(2,1)S(1)} %get-tuple-element.64.wr_in, f32[16,256]{1,0:T(8,128)S(1)} %get-tuple-element.65.panel_in, f32[8,256]{1,0:T(8,128)S(1)} %get-tuple-element.66.scale), custom_call_target="tpu_custom_call" | custom-call | flops 1073741824 | bytes 1048576 | tf_op jit(solution)/shard_map/third_panels/pallas_call | solution.py:655
  44.3 0.6 %products.1 = f32[2,4,40,128]{3,2,1,0:T(8,128)S(1)} custom-call(f32[256,256]{1,0:T(8,128)S(1)} %third_panels.1.winv, f32[128,128]{1,0:T(8,128)S(1)} %get-tuple-element.67.ninv_ref, f32[128,128]{1,0:T(8,128)S(1)} %add.51.mine, f32[128,128]{1,0:T(8,128)S(1)} %collective-permute-done.12.other), custom_call_target="tpu_custom_call" | custom-call | tf_op jit(solution)/shard_map/products/pallas_call | solution.py:747
  45.0 1.9 %collective-permute-start.13 = (f32[4,40,128]{2,1,0:T(8,128)S(1)}, f32[4,40,128]{2,1,0:T(8,128)S(1)}, u32[]{:S(2)}, u32[]{:S(2)}) collective-permute-start(f32[4,40,128]{2,1,0:T(8,128)S(1)} %get-tuple-element.81), channel_id=1, source_target_pairs={{0,8},{8,0},{1,9},{9,1},{2,10},{10,2},{3,11},{11,3},{4,12},{12,4},... | collective-permute-start | bytes 245768 | tf_op jit(solution)/shard_map/ppermute | solution.py:807
  46.8 2.9 %collective-permute-done.13 = f32[4,40,128]{2,1,0:T(8,128)S(1)} collective-permute-done((f32[4,40,128]{2,1,0:T(8,128)S(1)}, f32[4,40,128]{2,1,0:T(8,128)S(1)}, u32[]{:S(2)}, u32[]{:S(2)}) %collective-permute-start.13) | collective-permute-done | bytes 81952 | tf_op jit(solution)/shard_map/ppermute | solution.py:807
  49.7 8.9 %all_to_all.5.got_ref = f32[4,2,40,128]{3,2,1,0:T(8,128)S(1)} all-to-all(f32[4,2,40,128]{3,2,1,0:T(8,128)S(1)} %pad_maximum_fusion), channel_id=1, replica_groups=mesh['dp0'=2,'dp1'=2,'dp2'=2,'dp3'=2,'own0'=2] {'dp2','own0'}, dimensions={0} | all-to-all | bytes 327680 | tf_op jit(solution)/shard_map/all_to_all | solution.py:872
  58.6 0.7 %placing.1 = (f32[5,16,256]{2,1,0:T(8,128)}, f32[8,16,64]{2,1,0:T(8,128)}) custom-call(s32[8,8,128]{2,1,0:T(8,128)S(1)} %get-tuple-element.47.slots_ref, f32[4,2,40,128]{3,2,1,0:T(8,128)S(1)} %all_to_all.5.got_ref), custom_call_target="tpu_custom_call" | custom-call | tf_op jit(solution)/shard_map/placing/pallas_call | solution.py:793
  (35 shorter events, 2.5 us)
Async XLA Ops:
  4.2 4.8 %copy-start = (s32[8]{0:T(128)S(1)}, s32[8]{0:T(128)}, u32[]{:S(2)}) copy-start(s32[8]{0:T(128)} %owner_map.1) | copy-start | bytes 100
  4.3 1.8 %collective-permute-start = (f32[4,168,128]{2,1,0:T(8,128)S(1)}, f32[4,168,128]{2,1,0:T(8,128)S(1)}, u32[]{:S(2)}, u32[]{:S(2)}) collective-permute-start(f32[4,168,128]{2,1,0:T(8,128)S(1)} %slice.48), channel_id=1, source_target_pairs={{0,2},{2,0},{1,3},{3,1},{4,6},{6,4},{5,7},{7,5},{8,10},{10,8},{9,1... | collective-permute-start | bytes 1032200 | tf_op jit(solution)/shard_map/ppermute | solution.py:807
  6.1 8.2 %collective-permute-start.1 = (f32[4,168,128]{2,1,0:T(8,128)S(1)}, f32[4,168,128]{2,1,0:T(8,128)S(1)}, u32[]{:S(2)}, u32[]{:S(2)}) collective-permute-start(f32[4,168,128]{2,1,0:T(8,128)S(1)} %slice_add_fusion.1), channel_id=1, source_target_pairs={{0,1},{1,0},{2,6},{3,7},{4,5},{5,4},{6,2},{7,3},{8,9},{9,8},{10,14... | collective-permute-start | bytes 1032200 | tf_op jit(solution)/shard_map/ppermute | solution.py:814
  10.5 6.0 %collective-permute-start.7 = (f32[8,128,128]{2,1,0:T(8,128)S(1)}, f32[8,128,128]{2,1,0:T(8,128)S(1)}, u32[]{:S(2)}, u32[]{:S(2)}) collective-permute-start(f32[8,128,128]{2,1,0:T(8,128)S(1)} %get-tuple-element.50), channel_id=1, source_target_pairs={{0,2},{2,0},{1,3},{3,1},{4,6},{6,4},{5,7},{7,5},{8,10},{10,8},{9,1... | collective-permute-start | bytes 1572872 | tf_op jit(solution)/shard_map/ppermute | solution.py:807
  10.6 3.7 %collective-permute-start.2 = (f32[4,168,128]{2,1,0:T(8,128)S(1)}, f32[4,168,128]{2,1,0:T(8,128)S(1)}, u32[]{:S(2)}, u32[]{:S(2)}) collective-permute-start(f32[4,168,128]{2,1,0:T(8,128)S(1)} %slice_add_fusion), channel_id=1, source_target_pairs={{0,2},{2,0},{1,3},{3,1},{4,6},{6,4},{5,7},{7,5},{8,10},{10,8},{9,1... | collective-permute-start | bytes 1032200 | tf_op jit(solution)/shard_map/ppermute | solution.py:807
  14.4 5.5 %collective-permute-start.3 = (f32[2,168,128]{2,1,0:T(8,128)S(1)}, f32[2,168,128]{2,1,0:T(8,128)S(1)}, u32[]{:S(2)}, u32[]{:S(2)}) collective-permute-start(f32[2,168,128]{2,1,0:T(8,128)S(1)} %slice.65), channel_id=1, source_target_pairs={{0,4},{1,5},{2,10},{3,11},{4,0},{5,1},{6,14},{7,15},{8,12},{9,13},... | collective-permute-start | bytes 516104 | tf_op jit(solution)/shard_map/ppermute | solution.py:814
  16.6 6.4 %collective-permute-start.8 = (f32[4,128,128]{2,1,0:T(8,128)S(1)}, f32[4,128,128]{2,1,0:T(8,128)S(1)}, u32[]{:S(2)}, u32[]{:S(2)}) collective-permute-start(f32[4,128,128]{2,1,0:T(8,128)S(1)} %get-tuple-element.76), channel_id=1, source_target_pairs={{0,4},{1,5},{2,3},{3,2},{4,0},{5,1},{6,7},{7,6},{8,12},{9,13},{10,... | collective-permute-start | bytes 786440 | tf_op jit(solution)/shard_map/ppermute | solution.py:814
  19.9 5.2 %collective-permute-start.4 = (f32[168,128]{1,0:T(8,128)S(1)}, f32[168,128]{1,0:T(8,128)S(1)}, u32[]{:S(2)}, u32[]{:S(2)}) collective-permute-start(f32[168,128]{1,0:T(8,128)S(1)} %slice_bitcast_fusion), channel_id=1, source_target_pairs={{0,8},{1,9},{2,3},{3,2},{4,12},{5,13},{6,7},{7,6},{8,0},{9,1},{10,... | collective-permute-start | bytes 258056 | tf_op jit(solution)/shard_map/ppermute | solution.py:814
  23.1 8.5 %collective-permute-start.9 = (f32[2,128,128]{2,1,0:T(8,128)S(1)}, f32[2,128,128]{2,1,0:T(8,128)S(1)}, u32[]{:S(2)}, u32[]{:S(2)}) collective-permute-start(f32[2,128,128]{2,1,0:T(8,128)S(1)} %get-tuple-element.78), channel_id=1, source_target_pairs={{0,8},{1,9},{2,6},{3,7},{4,12},{5,13},{6,2},{7,3},{8,0},{9,1},{10,... | collective-permute-start | bytes 393224 | tf_op jit(solution)/shard_map/ppermute | solution.py:814
  25.2 6.4 %collective-permute-start.5 = (f32[168,128]{1,0:T(8,128)S(1)}, f32[168,128]{1,0:T(8,128)S(1)}, u32[]{:S(2)}, u32[]{:S(2)}) collective-permute-start(f32[168,128]{1,0:T(8,128)S(1)} %fusion), channel_id=1, source_target_pairs={{0,16},{16,0},{1,17},{17,1},{2,18},{18,2},{3,19},{19,3},{4,20},{20... | collective-permute-start | bytes 258056 | tf_op jit(solution)/shard_map/ppermute | solution.py:807
  31.6 1.3 %collective-permute-start.6 = (f32[168,128]{1,0:T(8,128)S(1)}, f32[168,128]{1,0:T(8,128)S(1)}, u32[]{:S(2)}, u32[]{:S(2)}) collective-permute-start(f32[168,128]{1,0:T(8,128)S(1)} %add.46.mine), channel_id=1, source_target_pairs={{0,2},{2,0},{1,3},{3,1},{4,6},{6,4},{5,7},{7,5},{8,10},{10,8},{9,1... | collective-permute-start | bytes 258056 | tf_op jit(solution)/shard_map/ppermute | solution.py:807
  31.7 4.4 %collective-permute-start.10 = (f32[128,128]{1,0:T(8,128)S(1)}, f32[128,128]{1,0:T(8,128)S(1)}, u32[]{:S(2)}, u32[]{:S(2)}) collective-permute-start(f32[128,128]{1,0:T(8,128)S(1)} %get-tuple-element.82), channel_id=1, source_target_pairs={{0,1},{1,0},{2,10},{3,11},{4,5},{5,4},{6,14},{7,15},{8,9},{9,8},{1... | collective-permute-start | bytes 196616 | tf_op jit(solution)/shard_map/ppermute | solution.py:814
  36.1 6.8 %collective-permute-start.11 = (f32[128,128]{1,0:T(8,128)S(1)}, f32[128,128]{1,0:T(8,128)S(1)}, u32[]{:S(2)}, u32[]{:S(2)}) collective-permute-start(f32[128,128]{1,0:T(8,128)S(1)} %add.50), channel_id=1, source_target_pairs={{0,16},{16,0},{1,17},{17,1},{2,18},{18,2},{3,19},{19,3},{4,20},{20... | collective-permute-start | bytes 196616 | tf_op jit(solution)/shard_map/ppermute | solution.py:807
  42.9 1.4 %collective-permute-start.12 = (f32[128,128]{1,0:T(8,128)S(1)}, f32[128,128]{1,0:T(8,128)S(1)}, u32[]{:S(2)}, u32[]{:S(2)}) collective-permute-start(f32[128,128]{1,0:T(8,128)S(1)} %add.51.mine), channel_id=1, source_target_pairs={{0,2},{2,0},{1,3},{3,1},{4,6},{6,4},{5,7},{7,5},{8,10},{10,8},{9,1... | collective-permute-start | bytes 196616 | tf_op jit(solution)/shard_map/ppermute | solution.py:807
  45.0 4.7 %collective-permute-start.13 = (f32[4,40,128]{2,1,0:T(8,128)S(1)}, f32[4,40,128]{2,1,0:T(8,128)S(1)}, u32[]{:S(2)}, u32[]{:S(2)}) collective-permute-start(f32[4,40,128]{2,1,0:T(8,128)S(1)} %get-tuple-element.81), channel_id=1, source_target_pairs={{0,8},{8,0},{1,9},{9,1},{2,10},{10,2},{3,11},{11,3},{4,12},{12,4},... | collective-permute-start | bytes 245768 | tf_op jit(solution)/shard_map/ppermute | solution.py:807

commit v20 on v17

--- a/solution.py
+++ b/solution.py
@@ -74,6 +74,7 @@
 
 
 ORDERS = (("first", "second", "near"), ("second", "near", "first"))
+LATE_ORDERS = (("first", "second", "near"), ("near", "first", "second"))
 
 
 def position(axes, i):
@@ -240,7 +241,7 @@
         flat[i, :n] = mixed[:, :n]
         flat[i, n:] = mixed[:, n:]
         kept, sent = both_halves(place, flat, i)
-        mine, other = positions(place, i, ORDERS[::-1])
+        mine, other = positions(place, i, LATE_ORDERS)
         keep[mine] = kept
         send[other] = sent
 
@@ -825,7 +826,6 @@
     h_got = swap(first_send, place.core)
     c_keep, c_send = cold_squares(place, after(wides, first_send), narrows)
     h_keep, c_send = lax.optimization_barrier((h_keep, c_send))
-    others = ORDERS[::-1]
 
     hot = h_keep[4:] + h_got
     s_got = swap_by_core(hot, place, 0, ORDERS)
@@ -837,19 +837,19 @@
     s = s + after(c_got, s)
     s_got = swap_by_core(s[2:], place, 1, ORDERS)
     m = after(m_keep, s) + m_got
-    m_got = swap_by_core(m[4:], place, 0, others)
+    m_got = swap_by_core(m[4:], place, 0, LATE_ORDERS)
 
     s = s[:2] + s_got
     s_got = swap_by_core(s[1], place, 2, ORDERS)
     m = after(m[:4], s) + m_got
-    m_got = swap_by_core(m[2:], place, 1, others)
+    m_got = swap_by_core(m[2:], place, 1, LATE_ORDERS)
 
     s = s[0] + s_got
     if place.extra:
         s = lax.psum(s, place.extra)
     s_got = swap(s, place.far)
     m = after(m[:2], s) + m_got
-    m_got = swap_by_core(m[1], place, 2, others)
+    m_got = swap_by_core(m[1], place, 2, LATE_ORDERS)
 
     s = s + s_got
     state = first_panels(place, [s, swap(s, place.core)], wide, narrow, total)

time: 56.5 us -> 56.4 us (level)
  starting transfers between devices: 16.4 us -> 18.6 us
  waiting for transfers between devices: 12.6 us -> 10.5 us
    ppermute x7, waiting for transfers between devices: 5.32 us -> 3.4 us  [swap(): return lax.ppermute(value, axis, [(0, 1), (1, 0)])]
    ppermute x7, starting transfers between devices: 6.44 us -> 7.83 us  [swap(): return lax.ppermute(value, axis, [(0, 1), (1, 0)])]
    ppermute x6, starting transfers between devices: 9.95 us -> 10.8 us  [swap_by_core(): return lax.ppermute(value, names, pairs)]
where the time goes in v20:
time: 56.4 us; the launch traced here: 56.2 us
  starting transfers between devices  18.6 us (33%)
  Pallas kernels  15.4 us (27%)
  waiting for transfers between devices  10.5 us (19%)
  blocking collectives  10.3 us (18%)
  between operations  0.86 us (2%)
    ppermute x6, starting transfers between devices, swap_by_core(): return lax.ppermute(value, names, pairs)  10.8 us
    all_to_all x1, blocking collectives, on_device(): got = lax.all_to_all(sent, (place.near, place.second, place.first), 0, 0)  10.3 us
    pallas_call x3, Pallas kernels, sweep_call(): pl.pallas_call(kernel, in_specs=[VMEM] * len(args), out_specs=[VMEM] * le...  8.43 us
    ppermute x7, starting transfers between devices, swap(): return lax.ppermute(value, axis, [(0, 1), (1, 0)])  7.83 us
    ppermute x6, waiting for transfers between devices, swap_by_core(): return lax.ppermute(value, names, pairs)  7.12 us
    pallas_call x1, Pallas kernels, hot_squares(): pl.pallas_call(functools.partial(hot_kernel, place), in_specs=[HBM, HBM],...  3.58 us
    ppermute x7, waiting for transfers between devices, swap(): return lax.ppermute(value, axis, [(0, 1), (1, 0)])  3.4 us
    pallas_call x1, Pallas kernels, mixed_sums(): pl.pallas_call(functools.partial(mixed_kernel, place), in_specs=[SMEM, VM...  1.45 us
  transfers between devices with their start and end apart: 13, of which 7 were waited for; matrix products, arithmetic and copies ran while one was open for 1% of the time, Pallas kernels for 19%

profile of v20, /device:TPU:0, one launch (start us, length us, event | category | flops | bytes accessed | tf_op | source)
XLA Modules:
  0.0 56.2 jit_solution(1333135883111485530)
XLA Ops:
  0.6 3.6 %hot_squares.1 = (f32[8,168,128]{2,1,0:T(8,128)S(1)}, f32[8,168,128]{2,1,0:T(8,128)S(1)}, bf16[8,768,256]{2,1,0:T(8,128)(2,1)S(1)}, bf16[8,768,128]{2,1,0:T(8,128)(2,1)S(1)}) custom-call(bf16[8,768,256]{2,1,0:T(8,128)(2,1)} %wide_hbm.1, bf16[8,768,128]{2,1,0:T(8,128)(2,1)} %narrow_hbm.1), custom_call_target="tpu_custom_call" | custom-call | flops 754974720 | bytes 3145728 | tf_op jit(solution)/shard_map/hot_squares/pallas_call | solution.py:268
  4.3 0.5 collective-permute-start
  4.8 0.6 %cold_squares.1 = (f32[4,168,128]{2,1,0:T(8,128)S(1)}, f32[4,168,128]{2,1,0:T(8,128)S(1)}) custom-call(bf16[8,768,256]{2,1,0:T(8,128)(2,1)S(1)} %get-tuple-element.46.wides, bf16[8,768,128]{2,1,0:T(8,128)(2,1)S(1)} %get-tuple-element.43.narrows), custom_call_target="tpu_custom_call" | custom-call | flops 251658240 | bytes 3145728 | tf_op jit(solution)/shard_map/cold_squares/pallas_call | solution.py:290
  5.4 0.7 %collective-permute-done = f32[4,168,128]{2,1,0:T(8,128)S(1)} collective-permute-done((f32[4,168,128]{2,1,0:T(8,128)S(1)}, f32[4,168,128]{2,1,0:T(8,128)S(1)}, u32[]{:S(2)}, u32[]{:S(2)}) %collective-permute-start) | collective-permute-done | bytes 344096 | tf_op jit(solution)/shard_map/ppermute | solution.py:804
  6.1 2.9 %collective-permute-start.1 = (f32[4,168,128]{2,1,0:T(8,128)S(1)}, f32[4,168,128]{2,1,0:T(8,128)S(1)}, u32[]{:S(2)}, u32[]{:S(2)}) collective-permute-start(f32[4,168,128]{2,1,0:T(8,128)S(1)} %slice_add_fusion.1), channel_id=1, source_target_pairs={{0,1},{1,0},{2,6},{3,7},{4,5},{5,4},{6,2},{7,3},{8,9},{9,8},{10,14... | collective-permute-start | bytes 1032200 | tf_op jit(solution)/shard_map/ppermute | solution.py:811
  9.0 1.4 %mixed.1 = (f32[8,128,128]{2,1,0:T(8,128)S(1)}, f32[8,128,128]{2,1,0:T(8,128)S(1)}, s32[8,8,128]{2,1,0:T(8,128)S(1)}) custom-call(s32[8]{0:T(128)S(1)} %copy-done, bf16[8,768,256]{2,1,0:T(8,128)(2,1)S(1)} %get-tuple-element.46.wides, bf16[8,768,128]{2,1,0:T(8,128)(2,1)S(1)} %get-tuple-element.43.narrows), custom_call_target="tpu_custom_call" | custom-call | flops 402653184 | bytes 3145728 | tf_op jit(solution)/shard_map/mixed/pallas_call | solution.py:305
  10.6 0.6 collective-permute-start.2
  11.2 3.1 %collective-permute-done.1 = f32[4,168,128]{2,1,0:T(8,128)S(1)} collective-permute-done((f32[4,168,128]{2,1,0:T(8,128)S(1)}, f32[4,168,128]{2,1,0:T(8,128)S(1)}, u32[]{:S(2)}, u32[]{:S(2)}) %collective-permute-start.1) | collective-permute-done | bytes 344096 | tf_op jit(solution)/shard_map/ppermute | solution.py:811
  14.4 2.1 %collective-permute-start.3 = (f32[2,168,128]{2,1,0:T(8,128)S(1)}, f32[2,168,128]{2,1,0:T(8,128)S(1)}, u32[]{:S(2)}, u32[]{:S(2)}) collective-permute-start(f32[2,168,128]{2,1,0:T(8,128)S(1)} %slice.57), channel_id=1, source_target_pairs={{0,4},{1,5},{2,10},{3,11},{4,0},{5,1},{6,14},{7,15},{8,12},{9,13},... | collective-permute-start | bytes 516104 | tf_op jit(solution)/shard_map/ppermute | solution.py:811
  16.6 1.6 %collective-permute-start.8 = (f32[4,128,128]{2,1,0:T(8,128)S(1)}, f32[4,128,128]{2,1,0:T(8,128)S(1)}, u32[]{:S(2)}, u32[]{:S(2)}) collective-permute-start(f32[4,128,128]{2,1,0:T(8,128)S(1)} %get-tuple-element.76), channel_id=1, source_target_pairs={{0,1},{1,0},{2,10},{3,11},{4,5},{5,4},{6,14},{7,15},{8,9},{9,8},{1... | collective-permute-start | bytes 786440 | tf_op jit(solution)/shard_map/ppermute | solution.py:811
  18.2 1.7 %collective-permute-done.3 = f32[2,168,128]{2,1,0:T(8,128)S(1)} collective-permute-done((f32[2,168,128]{2,1,0:T(8,128)S(1)}, f32[2,168,128]{2,1,0:T(8,128)S(1)}, u32[]{:S(2)}, u32[]{:S(2)}) %collective-permute-start.3) | collective-permute-done | bytes 172064 | tf_op jit(solution)/shard_map/ppermute | solution.py:811
  19.9 2.1 %collective-permute-start.4 = (f32[168,128]{1,0:T(8,128)S(1)}, f32[168,128]{1,0:T(8,128)S(1)}, u32[]{:S(2)}, u32[]{:S(2)}) collective-permute-start(f32[168,128]{1,0:T(8,128)S(1)} %slice_bitcast_fusion), channel_id=1, source_target_pairs={{0,8},{1,9},{2,3},{3,2},{4,12},{5,13},{6,7},{7,6},{8,0},{9,1},{10,... | collective-permute-start | bytes 258056 | tf_op jit(solution)/shard_map/ppermute | solution.py:811
  22.1 1.9 %collective-permute-done.8 = f32[4,128,128]{2,1,0:T(8,128)S(1)} collective-permute-done((f32[4,128,128]{2,1,0:T(8,128)S(1)}, f32[4,128,128]{2,1,0:T(8,128)S(1)}, u32[]{:S(2)}, u32[]{:S(2)}) %collective-permute-start.8) | collective-permute-done | bytes 262176 | tf_op jit(solution)/shard_map/ppermute | solution.py:811
  24.1 0.4 collective-permute-done.4
  24.6 3.1 %collective-permute-start.5 = (f32[168,128]{1,0:T(8,128)S(1)}, f32[168,128]{1,0:T(8,128)S(1)}, u32[]{:S(2)}, u32[]{:S(2)}) collective-permute-start(f32[168,128]{1,0:T(8,128)S(1)} %fusion), channel_id=1, source_target_pairs={{0,16},{16,0},{1,17},{17,1},{2,18},{18,2},{3,19},{19,3},{4,20},{20... | collective-permute-start | bytes 258056 | tf_op jit(solution)/shard_map/ppermute | solution.py:804
  27.6 2.5 %collective-permute-done.5 = f32[168,128]{1,0:T(8,128)S(1)} collective-permute-done((f32[168,128]{1,0:T(8,128)S(1)}, f32[168,128]{1,0:T(8,128)S(1)}, u32[]{:S(2)}, u32[]{:S(2)}) %collective-permute-start.5) | collective-permute-done | bytes 86048 | tf_op jit(solution)/shard_map/ppermute | solution.py:804
  30.3 2.0 %collective-permute-start.10 = (f32[128,128]{1,0:T(8,128)S(1)}, f32[128,128]{1,0:T(8,128)S(1)}, u32[]{:S(2)}, u32[]{:S(2)}) collective-permute-start(f32[128,128]{1,0:T(8,128)S(1)} %get-tuple-element.80), channel_id=1, source_target_pairs={{0,8},{1,9},{2,6},{3,7},{4,12},{5,13},{6,2},{7,3},{8,0},{9,1},{10,... | collective-permute-start | bytes 196616 | tf_op jit(solution)/shard_map/ppermute | solution.py:811
  32.3 3.2 %first_panels.1 = (f32[288,256]{1,0:T(8,128)S(1)}, bf16[96,256]{1,0:T(8,128)(2,1)S(1)}, bf16[96,256]{1,0:T(8,128)(2,1)S(1)}, f32[16,256]{1,0:T(8,128)S(1)}, f32[...) custom-call(f32[168,128]{1,0:T(8,128)S(1)} %add.46.mine, ...), custom_call_target="tpu_custom_call" | custom-call | flops 1073741824 | bytes 1048576 | tf_op jit(solution)/shard_map/first_panels/pallas_call | solution.py:656
  35.5 3.4 %collective-permute-start.11 = (f32[128,128]{1,0:T(8,128)S(1)}, f32[128,128]{1,0:T(8,128)S(1)}, u32[]{:S(2)}, u32[]{:S(2)}) collective-permute-start(f32[128,128]{1,0:T(8,128)S(1)} %add.50), channel_id=1, source_target_pairs={{0,16},{16,0},{1,17},{17,1},{2,18},{18,2},{3,19},{19,3},{4,20},{20... | collective-permute-start | bytes 196616 | tf_op jit(solution)/shard_map/ppermute | solution.py:804
  38.9 4.2 %second_panels.1 = (f32[128,128]{1,0:T(8,128)S(1)}, f32[288,256]{1,0:T(8,128)S(1)}, bf16[96,256]{1,0:T(8,128)(2,1)S(1)}, bf16[96,256]{1,0:T(8,128)(2,1)S(1)}, f32[16,256]{1,0:T(8,128)S(1)}) custom-call(f32[288,256]{1,0:T(8,128)S(1)} %get-tuple-element.53.refs_0_, bf16[96,256]{1,0:T(8,128)(2,1)S(1)} %get-tuple-element.54.refs_1_, ...), custom_call_target="tpu_custom_call" | custom-call | flops 1073741824 | bytes 1048576 | tf_op jit(solution)/shard_map/second_panels/pallas_call | solution.py:656
  43.3 1.0 %third_panels.1.winv = f32[256,256]{1,0:T(8,128)S(1)} custom-call(f32[288,256]{1,0:T(8,128)S(1)} %get-tuple-element.62.wa_in, bf16[96,256]{1,0:T(8,128)(2,1)S(1)} %get-tuple-element.63.wl_in, bf16[96,256]{1,0:T(8,128)(2,1)S(1)} %get-tuple-element.64.wr_in, f32[16,256]{1,0:T(8,128)S(1)} %get-tuple-element.65.panel_in, f32[8,256]{1,0:T(8,128)S(1)} %get-tuple-element.66.scale), custom_call_target="tpu_custom_call" | custom-call | flops 1073741824 | bytes 1048576 | tf_op jit(solution)/shard_map/third_panels/pallas_call | solution.py:656
  44.5 0.6 %products.1 = f32[8,40,128]{2,1,0:T(8,128)S(1)} custom-call(f32[256,256]{1,0:T(8,128)S(1)} %third_panels.1.winv, f32[128,128]{1,0:T(8,128)S(1)} %get-tuple-element.67.ninv_ref, f32[128,128]{1,0:T(8,128)S(1)} %add.51.mine, f32[128,128]{1,0:T(8,128)S(1)} %collective-permute-done.12.other), custom_call_target="tpu_custom_call" | custom-call | tf_op jit(solution)/shard_map/products/pallas_call | solution.py:747
  45.1 10.3 %all_to_all.5.got_ref = f32[8,40,128]{2,1,0:T(8,128)S(1)} all-to-all(f32[8,40,128]{2,1,0:T(8,128)S(1)} %products.1), channel_id=1, replica_groups=mesh['dp0'=2,'dp1'=2,'dp2'=2,'dp3'=2,'own0'=2] {'dp1','dp2','own0'}, dimensions={0} | all-to-all | bytes 327680 | tf_op jit(solution)/shard_map/all_to_all | solution.py:867
  55.5 0.7 %placing.1 = (f32[5,16,256]{2,1,0:T(8,128)}, f32[8,16,64]{2,1,0:T(8,128)}) custom-call(s32[8,8,128]{2,1,0:T(8,128)S(1)} %get-tuple-element.47.slots_ref, f32[8,40,128]{2,1,0:T(8,128)S(1)} %all_to_all.5.got_ref), custom_call_target="tpu_custom_call" | custom-call | tf_op jit(solution)/shard_map/placing/pallas_call | solution.py:790
  (31 shorter events, 1.0 us)
Async XLA Ops:
  4.2 4.8 %copy-start = (s32[8]{0:T(128)S(1)}, s32[8]{0:T(128)}, u32[]{:S(2)}) copy-start(s32[8]{0:T(128)} %owner_map.1) | copy-start | bytes 100
  4.3 1.8 %collective-permute-start = (f32[4,168,128]{2,1,0:T(8,128)S(1)}, f32[4,168,128]{2,1,0:T(8,128)S(1)}, u32[]{:S(2)}, u32[]{:S(2)}) collective-permute-start(f32[4,168,128]{2,1,0:T(8,128)S(1)} %slice.42), channel_id=1, source_target_pairs={{0,2},{2,0},{1,3},{3,1},{4,6},{6,4},{5,7},{7,5},{8,10},{10,8},{9,1... | collective-permute-start | bytes 1032200 | tf_op jit(solution)/shard_map/ppermute | solution.py:804
  6.1 8.2 %collective-permute-start.1 = (f32[4,168,128]{2,1,0:T(8,128)S(1)}, f32[4,168,128]{2,1,0:T(8,128)S(1)}, u32[]{:S(2)}, u32[]{:S(2)}) collective-permute-start(f32[4,168,128]{2,1,0:T(8,128)S(1)} %slice_add_fusion.1), channel_id=1, source_target_pairs={{0,1},{1,0},{2,6},{3,7},{4,5},{5,4},{6,2},{7,3},{8,9},{9,8},{10,14... | collective-permute-start | bytes 1032200 | tf_op jit(solution)/shard_map/ppermute | solution.py:811
  10.5 6.0 %collective-permute-start.7 = (f32[8,128,128]{2,1,0:T(8,128)S(1)}, f32[8,128,128]{2,1,0:T(8,128)S(1)}, u32[]{:S(2)}, u32[]{:S(2)}) collective-permute-start(f32[8,128,128]{2,1,0:T(8,128)S(1)} %get-tuple-element.50), channel_id=1, source_target_pairs={{0,2},{2,0},{1,3},{3,1},{4,6},{6,4},{5,7},{7,5},{8,10},{10,8},{9,1... | collective-permute-start | bytes 1572872 | tf_op jit(solution)/shard_map/ppermute | solution.py:804
  10.6 3.7 %collective-permute-start.2 = (f32[4,168,128]{2,1,0:T(8,128)S(1)}, f32[4,168,128]{2,1,0:T(8,128)S(1)}, u32[]{:S(2)}, u32[]{:S(2)}) collective-permute-start(f32[4,168,128]{2,1,0:T(8,128)S(1)} %slice_add_fusion), channel_id=1, source_target_pairs={{0,2},{2,0},{1,3},{3,1},{4,6},{6,4},{5,7},{7,5},{8,10},{10,8},{9,1... | collective-permute-start | bytes 1032200 | tf_op jit(solution)/shard_map/ppermute | solution.py:804
  14.4 5.5 %collective-permute-start.3 = (f32[2,168,128]{2,1,0:T(8,128)S(1)}, f32[2,168,128]{2,1,0:T(8,128)S(1)}, u32[]{:S(2)}, u32[]{:S(2)}) collective-permute-start(f32[2,168,128]{2,1,0:T(8,128)S(1)} %slice.57), channel_id=1, source_target_pairs={{0,4},{1,5},{2,10},{3,11},{4,0},{5,1},{6,14},{7,15},{8,12},{9,13},... | collective-permute-start | bytes 516104 | tf_op jit(solution)/shard_map/ppermute | solution.py:811
  16.6 7.4 %collective-permute-start.8 = (f32[4,128,128]{2,1,0:T(8,128)S(1)}, f32[4,128,128]{2,1,0:T(8,128)S(1)}, u32[]{:S(2)}, u32[]{:S(2)}) collective-permute-start(f32[4,128,128]{2,1,0:T(8,128)S(1)} %get-tuple-element.76), channel_id=1, source_target_pairs={{0,1},{1,0},{2,10},{3,11},{4,5},{5,4},{6,14},{7,15},{8,9},{9,8},{1... | collective-permute-start | bytes 786440 | tf_op jit(solution)/shard_map/ppermute | solution.py:811
  19.9 4.6 %collective-permute-start.4 = (f32[168,128]{1,0:T(8,128)S(1)}, f32[168,128]{1,0:T(8,128)S(1)}, u32[]{:S(2)}, u32[]{:S(2)}) collective-permute-start(f32[168,128]{1,0:T(8,128)S(1)} %slice_bitcast_fusion), channel_id=1, source_target_pairs={{0,8},{1,9},{2,3},{3,2},{4,12},{5,13},{6,7},{7,6},{8,0},{9,1},{10,... | collective-permute-start | bytes 258056 | tf_op jit(solution)/shard_map/ppermute | solution.py:811
  24.1 6.2 %collective-permute-start.9 = (f32[2,128,128]{2,1,0:T(8,128)S(1)}, f32[2,128,128]{2,1,0:T(8,128)S(1)}, u32[]{:S(2)}, u32[]{:S(2)}) collective-permute-start(f32[2,128,128]{2,1,0:T(8,128)S(1)} %get-tuple-element.78), channel_id=1, source_target_pairs={{0,4},{1,5},{2,3},{3,2},{4,0},{5,1},{6,7},{7,6},{8,12},{9,13},{10,... | collective-permute-start | bytes 393224 | tf_op jit(solution)/shard_map/ppermute | solution.py:811
  24.6 5.6 %collective-permute-start.5 = (f32[168,128]{1,0:T(8,128)S(1)}, f32[168,128]{1,0:T(8,128)S(1)}, u32[]{:S(2)}, u32[]{:S(2)}) collective-permute-start(f32[168,128]{1,0:T(8,128)S(1)} %fusion), channel_id=1, source_target_pairs={{0,16},{16,0},{1,17},{17,1},{2,18},{18,2},{3,19},{19,3},{4,20},{20... | collective-permute-start | bytes 258056 | tf_op jit(solution)/shard_map/ppermute | solution.py:804
  30.1 2.1 %collective-permute-start.6 = (f32[168,128]{1,0:T(8,128)S(1)}, f32[168,128]{1,0:T(8,128)S(1)}, u32[]{:S(2)}, u32[]{:S(2)}) collective-permute-start(f32[168,128]{1,0:T(8,128)S(1)} %add.46.mine), channel_id=1, source_target_pairs={{0,2},{2,0},{1,3},{3,1},{4,6},{6,4},{5,7},{7,5},{8,10},{10,8},{9,1... | collective-permute-start | bytes 258056 | tf_op jit(solution)/shard_map/ppermute | solution.py:804
  30.3 5.2 %collective-permute-start.10 = (f32[128,128]{1,0:T(8,128)S(1)}, f32[128,128]{1,0:T(8,128)S(1)}, u32[]{:S(2)}, u32[]{:S(2)}) collective-permute-start(f32[128,128]{1,0:T(8,128)S(1)} %get-tuple-element.80), channel_id=1, source_target_pairs={{0,8},{1,9},{2,6},{3,7},{4,12},{5,13},{6,2},{7,3},{8,0},{9,1},{10,... | collective-permute-start | bytes 196616 | tf_op jit(solution)/shard_map/ppermute | solution.py:811
  35.5 7.7 %collective-permute-start.11 = (f32[128,128]{1,0:T(8,128)S(1)}, f32[128,128]{1,0:T(8,128)S(1)}, u32[]{:S(2)}, u32[]{:S(2)}) collective-permute-start(f32[128,128]{1,0:T(8,128)S(1)} %add.50), channel_id=1, source_target_pairs={{0,16},{16,0},{1,17},{17,1},{2,18},{18,2},{3,19},{19,3},{4,20},{20... | collective-permute-start | bytes 196616 | tf_op jit(solution)/shard_map/ppermute | solution.py:804
  43.2 1.3 %collective-permute-start.12 = (f32[128,128]{1,0:T(8,128)S(1)}, f32[128,128]{1,0:T(8,128)S(1)}, u32[]{:S(2)}, u32[]{:S(2)}) collective-permute-start(f32[128,128]{1,0:T(8,128)S(1)} %add.51.mine), channel_id=1, source_target_pairs={{0,2},{2,0},{1,3},{3,1},{4,6},{6,4},{5,7},{7,5},{8,10},{10,8},{9,1... | collective-permute-start | bytes 196616 | tf_op jit(solution)/shard_map/ppermute | solution.py:804

commit v21 on v20

--- a/solution.py
+++ b/solution.py
@@ -543,7 +543,7 @@
 
 
 STEPS = LANES // BLOCK
-FIRST_STEPS = 5
+FIRST_STEPS = 3
 SECOND_STEPS = 6
 
 

time: 56.4 us -> 57.4 us (1.018)
  blocking collectives: 10.3 us -> 11.2 us
    all_to_all x1, blocking collectives: 10.3 us -> 11.2 us  [on_device(): got = lax.all_to_all(sent, (place.near, place.second, place.first), 0, 0)]
  transfers between devices with their start and end apart: 13 -> 13, of which waited for: 7 -> 8; matrix products, arithmetic and copies ran while one was open for 1% -> 1% of each run, Pallas kernels for 19% -> 18%
where the time goes in v21:
time: 57.4 us; the launch traced here: 57.2 us
  starting transfers between devices  18.5 us (32%)
  Pallas kernels  15.4 us (27%)
  blocking collectives  11.2 us (20%)
  waiting for transfers between devices  10.8 us (19%)
  between operations  0.84 us (1%)
    all_to_all x1, blocking collectives, on_device(): got = lax.all_to_all(sent, (place.near, place.second, place.first), 0, 0)  11.2 us
    ppermute x6, starting transfers between devices, swap_by_core(): return lax.ppermute(value, names, pairs)  10.8 us
    pallas_call x3, Pallas kernels, sweep_call(): pl.pallas_call(kernel, in_specs=[VMEM] * len(args), out_specs=[VMEM] * le...  8.43 us
    ppermute x7, starting transfers between devices, swap(): return lax.ppermute(value, axis, [(0, 1), (1, 0)])  7.73 us
    ppermute x6, waiting for transfers between devices, swap_by_core(): return lax.ppermute(value, names, pairs)  7.41 us
    pallas_call x1, Pallas kernels, hot_squares(): pl.pallas_call(functools.partial(hot_kernel, place), in_specs=[HBM, HBM],...  3.58 us
    ppermute x7, waiting for transfers between devices, swap(): return lax.ppermute(value, axis, [(0, 1), (1, 0)])  3.4 us
    pallas_call x1, Pallas kernels, mixed_sums(): pl.pallas_call(functools.partial(mixed_kernel, place), in_specs=[SMEM, VM...  1.45 us
  transfers between devices with their start and end apart: 13, of which 8 were waited for; matrix products, arithmetic and copies ran while one was open for 1% of the time, Pallas kernels for 18%

profile of v21, /device:TPU:0, one launch (start us, length us, event | category | flops | bytes accessed | tf_op | source)
XLA Modules:
  0.0 57.2 jit_solution(10981356430801662309)
XLA Ops:
  0.6 3.6 %hot_squares.1 = (f32[8,168,128]{2,1,0:T(8,128)S(1)}, f32[8,168,128]{2,1,0:T(8,128)S(1)}, bf16[8,768,256]{2,1,0:T(8,128)(2,1)S(1)}, bf16[8,768,128]{2,1,0:T(8,128)(2,1)S(1)}) custom-call(bf16[8,768,256]{2,1,0:T(8,128)(2,1)} %wide_hbm.1, bf16[8,768,128]{2,1,0:T(8,128)(2,1)} %narrow_hbm.1), custom_call_target="tpu_custom_call" | custom-call | flops 754974720 | bytes 3145728 | tf_op jit(solution)/shard_map/hot_squares/pallas_call | solution.py:268
  4.3 0.5 collective-permute-start
  4.8 0.6 %cold_squares.1 = (f32[4,168,128]{2,1,0:T(8,128)S(1)}, f32[4,168,128]{2,1,0:T(8,128)S(1)}) custom-call(bf16[8,768,256]{2,1,0:T(8,128)(2,1)S(1)} %get-tuple-element.46.wides, bf16[8,768,128]{2,1,0:T(8,128)(2,1)S(1)} %get-tuple-element.43.narrows), custom_call_target="tpu_custom_call" | custom-call | flops 251658240 | bytes 3145728 | tf_op jit(solution)/shard_map/cold_squares/pallas_call | solution.py:290
  5.4 0.7 %collective-permute-done = f32[4,168,128]{2,1,0:T(8,128)S(1)} collective-permute-done((f32[4,168,128]{2,1,0:T(8,128)S(1)}, f32[4,168,128]{2,1,0:T(8,128)S(1)}, u32[]{:S(2)}, u32[]{:S(2)}) %collective-permute-start) | collective-permute-done | bytes 344096 | tf_op jit(solution)/shard_map/ppermute | solution.py:804
  6.1 2.9 %collective-permute-start.1 = (f32[4,168,128]{2,1,0:T(8,128)S(1)}, f32[4,168,128]{2,1,0:T(8,128)S(1)}, u32[]{:S(2)}, u32[]{:S(2)}) collective-permute-start(f32[4,168,128]{2,1,0:T(8,128)S(1)} %slice_add_fusion.1), channel_id=1, source_target_pairs={{0,1},{1,0},{2,6},{3,7},{4,5},{5,4},{6,2},{7,3},{8,9},{9,8},{10,14... | collective-permute-start | bytes 1032200 | tf_op jit(solution)/shard_map/ppermute | solution.py:811
  9.0 1.4 %mixed.1 = (f32[8,128,128]{2,1,0:T(8,128)S(1)}, f32[8,128,128]{2,1,0:T(8,128)S(1)}, s32[8,8,128]{2,1,0:T(8,128)S(1)}) custom-call(s32[8]{0:T(128)S(1)} %copy-done, bf16[8,768,256]{2,1,0:T(8,128)(2,1)S(1)} %get-tuple-element.46.wides, bf16[8,768,128]{2,1,0:T(8,128)(2,1)S(1)} %get-tuple-element.43.narrows), custom_call_target="tpu_custom_call" | custom-call | flops 402653184 | bytes 3145728 | tf_op jit(solution)/shard_map/mixed/pallas_call | solution.py:305
  10.6 0.6 collective-permute-start.2
  11.2 3.1 %collective-permute-done.1 = f32[4,168,128]{2,1,0:T(8,128)S(1)} collective-permute-done((f32[4,168,128]{2,1,0:T(8,128)S(1)}, f32[4,168,128]{2,1,0:T(8,128)S(1)}, u32[]{:S(2)}, u32[]{:S(2)}) %collective-permute-start.1) | collective-permute-done | bytes 344096 | tf_op jit(solution)/shard_map/ppermute | solution.py:811
  14.4 2.1 %collective-permute-start.3 = (f32[2,168,128]{2,1,0:T(8,128)S(1)}, f32[2,168,128]{2,1,0:T(8,128)S(1)}, u32[]{:S(2)}, u32[]{:S(2)}) collective-permute-start(f32[2,168,128]{2,1,0:T(8,128)S(1)} %slice.57), channel_id=1, source_target_pairs={{0,4},{1,5},{2,10},{3,11},{4,0},{5,1},{6,14},{7,15},{8,12},{9,13},... | collective-permute-start | bytes 516104 | tf_op jit(solution)/shard_map/ppermute | solution.py:811
  16.6 1.6 %collective-permute-start.8 = (f32[4,128,128]{2,1,0:T(8,128)S(1)}, f32[4,128,128]{2,1,0:T(8,128)S(1)}, u32[]{:S(2)}, u32[]{:S(2)}) collective-permute-start(f32[4,128,128]{2,1,0:T(8,128)S(1)} %get-tuple-element.76), channel_id=1, source_target_pairs={{0,1},{1,0},{2,10},{3,11},{4,5},{5,4},{6,14},{7,15},{8,9},{9,8},{1... | collective-permute-start | bytes 786440 | tf_op jit(solution)/shard_map/ppermute | solution.py:811
  18.2 1.7 %collective-permute-done.3 = f32[2,168,128]{2,1,0:T(8,128)S(1)} collective-permute-done((f32[2,168,128]{2,1,0:T(8,128)S(1)}, f32[2,168,128]{2,1,0:T(8,128)S(1)}, u32[]{:S(2)}, u32[]{:S(2)}) %collective-permute-start.3) | collective-permute-done | bytes 172064 | tf_op jit(solution)/shard_map/ppermute | solution.py:811
  19.9 2.1 %collective-permute-start.4 = (f32[168,128]{1,0:T(8,128)S(1)}, f32[168,128]{1,0:T(8,128)S(1)}, u32[]{:S(2)}, u32[]{:S(2)}) collective-permute-start(f32[168,128]{1,0:T(8,128)S(1)} %slice_bitcast_fusion), channel_id=1, source_target_pairs={{0,8},{1,9},{2,3},{3,2},{4,12},{5,13},{6,7},{7,6},{8,0},{9,1},{10,... | collective-permute-start | bytes 258056 | tf_op jit(solution)/shard_map/ppermute | solution.py:811
  22.1 1.9 %collective-permute-done.8 = f32[4,128,128]{2,1,0:T(8,128)S(1)} collective-permute-done((f32[4,128,128]{2,1,0:T(8,128)S(1)}, f32[4,128,128]{2,1,0:T(8,128)S(1)}, u32[]{:S(2)}, u32[]{:S(2)}) %collective-permute-start.8) | collective-permute-done | bytes 262176 | tf_op jit(solution)/shard_map/ppermute | solution.py:811
  24.1 0.4 collective-permute-done.4
  24.6 3.1 %collective-permute-start.5 = (f32[168,128]{1,0:T(8,128)S(1)}, f32[168,128]{1,0:T(8,128)S(1)}, u32[]{:S(2)}, u32[]{:S(2)}) collective-permute-start(f32[168,128]{1,0:T(8,128)S(1)} %fusion), channel_id=1, source_target_pairs={{0,16},{16,0},{1,17},{17,1},{2,18},{18,2},{3,19},{19,3},{4,20},{20... | collective-permute-start | bytes 258056 | tf_op jit(solution)/shard_map/ppermute | solution.py:804
  27.6 2.5 %collective-permute-done.5 = f32[168,128]{1,0:T(8,128)S(1)} collective-permute-done((f32[168,128]{1,0:T(8,128)S(1)}, f32[168,128]{1,0:T(8,128)S(1)}, u32[]{:S(2)}, u32[]{:S(2)}) %collective-permute-start.5) | collective-permute-done | bytes 86048 | tf_op jit(solution)/shard_map/ppermute | solution.py:804
  30.3 2.0 %collective-permute-start.10 = (f32[128,128]{1,0:T(8,128)S(1)}, f32[128,128]{1,0:T(8,128)S(1)}, u32[]{:S(2)}, u32[]{:S(2)}) collective-permute-start(f32[128,128]{1,0:T(8,128)S(1)} %get-tuple-element.80), channel_id=1, source_target_pairs={{0,8},{1,9},{2,6},{3,7},{4,12},{5,13},{6,2},{7,3},{8,0},{9,1},{10,... | collective-permute-start | bytes 196616 | tf_op jit(solution)/shard_map/ppermute | solution.py:811
  32.3 2.0 %first_panels.1 = (f32[288,256]{1,0:T(8,128)S(1)}, bf16[96,256]{1,0:T(8,128)(2,1)S(1)}, bf16[96,256]{1,0:T(8,128)(2,1)S(1)}, f32[16,256]{1,0:T(8,128)S(1)}, f32[...) custom-call(f32[168,128]{1,0:T(8,128)S(1)} %add.46.mine, ...), custom_call_target="tpu_custom_call" | custom-call | flops 1073741824 | bytes 1048576 | tf_op jit(solution)/shard_map/first_panels/pallas_call | solution.py:656
  34.6 3.3 %collective-permute-start.11 = (f32[128,128]{1,0:T(8,128)S(1)}, f32[128,128]{1,0:T(8,128)S(1)}, u32[]{:S(2)}, u32[]{:S(2)}) collective-permute-start(f32[128,128]{1,0:T(8,128)S(1)} %add.50), channel_id=1, source_target_pairs={{0,16},{16,0},{1,17},{17,1},{2,18},{18,2},{3,19},{19,3},{4,20},{20... | collective-permute-start | bytes 196616 | tf_op jit(solution)/shard_map/ppermute | solution.py:804
  38.0 5.4 %second_panels.1 = (f32[128,128]{1,0:T(8,128)S(1)}, f32[288,256]{1,0:T(8,128)S(1)}, bf16[96,256]{1,0:T(8,128)(2,1)S(1)}, bf16[96,256]{1,0:T(8,128)(2,1)S(1)}, f32[16,256]{1,0:T(8,128)S(1)}) custom-call(f32[288,256]{1,0:T(8,128)S(1)} %get-tuple-element.53.refs_0_, bf16[96,256]{1,0:T(8,128)(2,1)S(1)} %get-tuple-element.54.refs_1_, ...), custom_call_target="tpu_custom_call" | custom-call | flops 1073741824 | bytes 1048576 | tf_op jit(solution)/shard_map/second_panels/pallas_call | solution.py:656
  43.5 1.0 %third_panels.1.winv = f32[256,256]{1,0:T(8,128)S(1)} custom-call(f32[288,256]{1,0:T(8,128)S(1)} %get-tuple-element.62.wa_in, bf16[96,256]{1,0:T(8,128)(2,1)S(1)} %get-tuple-element.63.wl_in, bf16[96,256]{1,0:T(8,128)(2,1)S(1)} %get-tuple-element.64.wr_in, f32[16,256]{1,0:T(8,128)S(1)} %get-tuple-element.65.panel_in, f32[8,256]{1,0:T(8,128)S(1)} %get-tuple-element.66.scale), custom_call_target="tpu_custom_call" | custom-call | flops 1073741824 | bytes 1048576 | tf_op jit(solution)/shard_map/third_panels/pallas_call | solution.py:656
  44.7 0.6 %products.1 = f32[8,40,128]{2,1,0:T(8,128)S(1)} custom-call(f32[256,256]{1,0:T(8,128)S(1)} %third_panels.1.winv, f32[128,128]{1,0:T(8,128)S(1)} %get-tuple-element.67.ninv_ref, f32[128,128]{1,0:T(8,128)S(1)} %add.51.mine, f32[128,128]{1,0:T(8,128)S(1)} %collective-permute-done.12.other), custom_call_target="tpu_custom_call" | custom-call | tf_op jit(solution)/shard_map/products/pallas_call | solution.py:747
  45.3 11.2 %all_to_all.5.got_ref = f32[8,40,128]{2,1,0:T(8,128)S(1)} all-to-all(f32[8,40,128]{2,1,0:T(8,128)S(1)} %products.1), channel_id=1, replica_groups=mesh['dp0'=2,'dp1'=2,'dp2'=2,'dp3'=2,'own0'=2] {'dp1','dp2','own0'}, dimensions={0} | all-to-all | bytes 327680 | tf_op jit(solution)/shard_map/all_to_all | solution.py:867
  56.5 0.7 %placing.1 = (f32[5,16,256]{2,1,0:T(8,128)}, f32[8,16,64]{2,1,0:T(8,128)}) custom-call(s32[8,8,128]{2,1,0:T(8,128)S(1)} %get-tuple-element.47.slots_ref, f32[8,40,128]{2,1,0:T(8,128)S(1)} %all_to_all.5.got_ref), custom_call_target="tpu_custom_call" | custom-call | tf_op jit(solution)/shard_map/placing/pallas_call | solution.py:790
  (31 shorter events, 1.3 us)
Async XLA Ops:
  4.2 4.8 %copy-start = (s32[8]{0:T(128)S(1)}, s32[8]{0:T(128)}, u32[]{:S(2)}) copy-start(s32[8]{0:T(128)} %owner_map.1) | copy-start | bytes 100
  4.3 1.8 %collective-permute-start = (f32[4,168,128]{2,1,0:T(8,128)S(1)}, f32[4,168,128]{2,1,0:T(8,128)S(1)}, u32[]{:S(2)}, u32[]{:S(2)}) collective-permute-start(f32[4,168,128]{2,1,0:T(8,128)S(1)} %slice.42), channel_id=1, source_target_pairs={{0,2},{2,0},{1,3},{3,1},{4,6},{6,4},{5,7},{7,5},{8,10},{10,8},{9,1... | collective-permute-start | bytes 1032200 | tf_op jit(solution)/shard_map/ppermute | solution.py:804
  6.1 8.2 %collective-permute-start.1 = (f32[4,168,128]{2,1,0:T(8,128)S(1)}, f32[4,168,128]{2,1,0:T(8,128)S(1)}, u32[]{:S(2)}, u32[]{:S(2)}) collective-permute-start(f32[4,168,128]{2,1,0:T(8,128)S(1)} %slice_add_fusion.1), channel_id=1, source_target_pairs={{0,1},{1,0},{2,6},{3,7},{4,5},{5,4},{6,2},{7,3},{8,9},{9,8},{10,14... | collective-permute-start | bytes 1032200 | tf_op jit(solution)/shard_map/ppermute | solution.py:811
  10.5 6.0 %collective-permute-start.7 = (f32[8,128,128]{2,1,0:T(8,128)S(1)}, f32[8,128,128]{2,1,0:T(8,128)S(1)}, u32[]{:S(2)}, u32[]{:S(2)}) collective-permute-start(f32[8,128,128]{2,1,0:T(8,128)S(1)} %get-tuple-element.50), channel_id=1, source_target_pairs={{0,2},{2,0},{1,3},{3,1},{4,6},{6,4},{5,7},{7,5},{8,10},{10,8},{9,1... | collective-permute-start | bytes 1572872 | tf_op jit(solution)/shard_map/ppermute | solution.py:804
  10.6 3.7 %collective-permute-start.2 = (f32[4,168,128]{2,1,0:T(8,128)S(1)}, f32[4,168,128]{2,1,0:T(8,128)S(1)}, u32[]{:S(2)}, u32[]{:S(2)}) collective-permute-start(f32[4,168,128]{2,1,0:T(8,128)S(1)} %slice_add_fusion), channel_id=1, source_target_pairs={{0,2},{2,0},{1,3},{3,1},{4,6},{6,4},{5,7},{7,5},{8,10},{10,8},{9,1... | collective-permute-start | bytes 1032200 | tf_op jit(solution)/shard_map/ppermute | solution.py:804
  14.4 5.5 %collective-permute-start.3 = (f32[2,168,128]{2,1,0:T(8,128)S(1)}, f32[2,168,128]{2,1,0:T(8,128)S(1)}, u32[]{:S(2)}, u32[]{:S(2)}) collective-permute-start(f32[2,168,128]{2,1,0:T(8,128)S(1)} %slice.57), channel_id=1, source_target_pairs={{0,4},{1,5},{2,10},{3,11},{4,0},{5,1},{6,14},{7,15},{8,12},{9,13},... | collective-permute-start | bytes 516104 | tf_op jit(solution)/shard_map/ppermute | solution.py:811
  16.6 7.4 %collective-permute-start.8 = (f32[4,128,128]{2,1,0:T(8,128)S(1)}, f32[4,128,128]{2,1,0:T(8,128)S(1)}, u32[]{:S(2)}, u32[]{:S(2)}) collective-permute-start(f32[4,128,128]{2,1,0:T(8,128)S(1)} %get-tuple-element.76), channel_id=1, source_target_pairs={{0,1},{1,0},{2,10},{3,11},{4,5},{5,4},{6,14},{7,15},{8,9},{9,8},{1... | collective-permute-start | bytes 786440 | tf_op jit(solution)/shard_map/ppermute | solution.py:811
  19.9 4.6 %collective-permute-start.4 = (f32[168,128]{1,0:T(8,128)S(1)}, f32[168,128]{1,0:T(8,128)S(1)}, u32[]{:S(2)}, u32[]{:S(2)}) collective-permute-start(f32[168,128]{1,0:T(8,128)S(1)} %slice_bitcast_fusion), channel_id=1, source_target_pairs={{0,8},{1,9},{2,3},{3,2},{4,12},{5,13},{6,7},{7,6},{8,0},{9,1},{10,... | collective-permute-start | bytes 258056 | tf_op jit(solution)/shard_map/ppermute | solution.py:811
  24.1 6.2 %collective-permute-start.9 = (f32[2,128,128]{2,1,0:T(8,128)S(1)}, f32[2,128,128]{2,1,0:T(8,128)S(1)}, u32[]{:S(2)}, u32[]{:S(2)}) collective-permute-start(f32[2,128,128]{2,1,0:T(8,128)S(1)} %get-tuple-element.78), channel_id=1, source_target_pairs={{0,4},{1,5},{2,3},{3,2},{4,0},{5,1},{6,7},{7,6},{8,12},{9,13},{10,... | collective-permute-start | bytes 393224 | tf_op jit(solution)/shard_map/ppermute | solution.py:811
  24.6 5.6 %collective-permute-start.5 = (f32[168,128]{1,0:T(8,128)S(1)}, f32[168,128]{1,0:T(8,128)S(1)}, u32[]{:S(2)}, u32[]{:S(2)}) collective-permute-start(f32[168,128]{1,0:T(8,128)S(1)} %fusion), channel_id=1, source_target_pairs={{0,16},{16,0},{1,17},{17,1},{2,18},{18,2},{3,19},{19,3},{4,20},{20... | collective-permute-start | bytes 258056 | tf_op jit(solution)/shard_map/ppermute | solution.py:804
  30.1 2.1 %collective-permute-start.6 = (f32[168,128]{1,0:T(8,128)S(1)}, f32[168,128]{1,0:T(8,128)S(1)}, u32[]{:S(2)}, u32[]{:S(2)}) collective-permute-start(f32[168,128]{1,0:T(8,128)S(1)} %add.46.mine), channel_id=1, source_target_pairs={{0,2},{2,0},{1,3},{3,1},{4,6},{6,4},{5,7},{7,5},{8,10},{10,8},{9,1... | collective-permute-start | bytes 258056 | tf_op jit(solution)/shard_map/ppermute | solution.py:804
  30.3 4.3 %collective-permute-start.10 = (f32[128,128]{1,0:T(8,128)S(1)}, f32[128,128]{1,0:T(8,128)S(1)}, u32[]{:S(2)}, u32[]{:S(2)}) collective-permute-start(f32[128,128]{1,0:T(8,128)S(1)} %get-tuple-element.80), channel_id=1, source_target_pairs={{0,8},{1,9},{2,6},{3,7},{4,12},{5,13},{6,2},{7,3},{8,0},{9,1},{10,... | collective-permute-start | bytes 196616 | tf_op jit(solution)/shard_map/ppermute | solution.py:811
  34.6 8.8 %collective-permute-start.11 = (f32[128,128]{1,0:T(8,128)S(1)}, f32[128,128]{1,0:T(8,128)S(1)}, u32[]{:S(2)}, u32[]{:S(2)}) collective-permute-start(f32[128,128]{1,0:T(8,128)S(1)} %add.50), channel_id=1, source_target_pairs={{0,16},{16,0},{1,17},{17,1},{2,18},{18,2},{3,19},{19,3},{4,20},{20... | collective-permute-start | bytes 196616 | tf_op jit(solution)/shard_map/ppermute | solution.py:804
  43.4 1.3 %collective-permute-start.12 = (f32[128,128]{1,0:T(8,128)S(1)}, f32[128,128]{1,0:T(8,128)S(1)}, u32[]{:S(2)}, u32[]{:S(2)}) collective-permute-start(f32[128,128]{1,0:T(8,128)S(1)} %add.51.mine), channel_id=1, source_target_pairs={{0,2},{2,0},{1,3},{3,1},{4,6},{6,4},{5,7},{7,5},{8,10},{10,8},{9,1... | collective-permute-start | bytes 196616 | tf_op jit(solution)/shard_map/ppermute | solution.py:804

commit v22 on v20

--- a/solution.py
+++ b/solution.py
@@ -73,8 +73,8 @@
     return flat[i, pl.ds(kept, rows), :], flat[i, pl.ds(sent, rows), :]
 
 
-ORDERS = (("first", "second", "near"), ("second", "near", "first"))
-LATE_ORDERS = (("first", "second", "near"), ("near", "first", "second"))
+ORDERS = (("second", "near", "first"), ("first", "second", "near"))
+LATE_ORDERS = (("first", "second", "near"), ("second", "near", "first"))
 
 
 def position(axes, i):

time: 56.4 us -> 56.4 us (level)
  starting transfers between devices: 18.6 us -> 19.7 us
  waiting for transfers between devices: 10.5 us -> 9.46 us
    ppermute x6, starting transfers between devices: 10.8 us -> 12.1 us  [swap_by_core(): return lax.ppermute(value, names, pairs)]
    ppermute x6, waiting for transfers between devices: 7.12 us -> 5.94 us  [swap_by_core(): return lax.ppermute(value, names, pairs)]
  transfers between devices with their start and end apart: 13 -> 13, of which waited for: 7 -> 6; matrix products, arithmetic and copies ran while one was open for 1% -> 1% of each run, Pallas kernels for 19% -> 19%
where the time goes in v22:
time: 56.4 us; the launch traced here: 56.2 us
  starting transfers between devices  19.7 us (35%)
  Pallas kernels  15.4 us (27%)
  blocking collectives  10.3 us (18%)
  waiting for transfers between devices  9.46 us (17%)
  between operations  0.85 us (2%)
    ppermute x6, starting transfers between devices, swap_by_core(): return lax.ppermute(value, names, pairs)  12.1 us
    all_to_all x1, blocking collectives, on_device(): got = lax.all_to_all(sent, (place.near, place.second, place.first), 0, 0)  10.3 us
    pallas_call x3, Pallas kernels, sweep_call(): pl.pallas_call(kernel, in_specs=[VMEM] * len(args), out_specs=[VMEM] * le...  8.43 us
    ppermute x7, starting transfers between devices, swap(): return lax.ppermute(value, axis, [(0, 1), (1, 0)])  7.59 us
    ppermute x6, waiting for transfers between devices, swap_by_core(): return lax.ppermute(value, names, pairs)  5.94 us
    pallas_call x1, Pallas kernels, hot_squares(): pl.pallas_call(functools.partial(hot_kernel, place), in_specs=[HBM, HBM],...  3.58 us
    ppermute x7, waiting for transfers between devices, swap(): return lax.ppermute(value, axis, [(0, 1), (1, 0)])  3.52 us
    pallas_call x1, Pallas kernels, mixed_sums(): pl.pallas_call(functools.partial(mixed_kernel, place), in_specs=[SMEM, VM...  1.45 us
  transfers between devices with their start and end apart: 13, of which 6 were waited for; matrix products, arithmetic and copies ran while one was open for 1% of the time, Pallas kernels for 19%

profile of v22, /device:TPU:0, one launch (start us, length us, event | category | flops | bytes accessed | tf_op | source)
XLA Modules:
  0.0 56.2 jit_solution(16103937573952614912)
XLA Ops:
  0.6 3.6 %hot_squares.1 = (f32[8,168,128]{2,1,0:T(8,128)S(1)}, f32[8,168,128]{2,1,0:T(8,128)S(1)}, bf16[8,768,256]{2,1,0:T(8,128)(2,1)S(1)}, bf16[8,768,128]{2,1,0:T(8,128)(2,1)S(1)}) custom-call(bf16[8,768,256]{2,1,0:T(8,128)(2,1)} %wide_hbm.1, bf16[8,768,128]{2,1,0:T(8,128)(2,1)} %narrow_hbm.1), custom_call_target="tpu_custom_call" | custom-call | flops 754974720 | bytes 3145728 | tf_op jit(solution)/shard_map/hot_squares/pallas_call | solution.py:268
  4.3 0.5 collective-permute-start
  4.8 0.6 %cold_squares.1 = (f32[4,168,128]{2,1,0:T(8,128)S(1)}, f32[4,168,128]{2,1,0:T(8,128)S(1)}) custom-call(bf16[8,768,256]{2,1,0:T(8,128)(2,1)S(1)} %get-tuple-element.46.wides, bf16[8,768,128]{2,1,0:T(8,128)(2,1)S(1)} %get-tuple-element.43.narrows), custom_call_target="tpu_custom_call" | custom-call | flops 251658240 | bytes 3145728 | tf_op jit(solution)/shard_map/cold_squares/pallas_call | solution.py:290
  5.4 0.7 %collective-permute-done = f32[4,168,128]{2,1,0:T(8,128)S(1)} collective-permute-done((f32[4,168,128]{2,1,0:T(8,128)S(1)}, f32[4,168,128]{2,1,0:T(8,128)S(1)}, u32[]{:S(2)}, u32[]{:S(2)}) %collective-permute-start) | collective-permute-done | bytes 344096 | tf_op jit(solution)/shard_map/ppermute | solution.py:804
  6.1 3.0 %collective-permute-start.1 = (f32[4,168,128]{2,1,0:T(8,128)S(1)}, f32[4,168,128]{2,1,0:T(8,128)S(1)}, u32[]{:S(2)}, u32[]{:S(2)}) collective-permute-start(f32[4,168,128]{2,1,0:T(8,128)S(1)} %slice_add_fusion.1), channel_id=1, source_target_pairs={{0,4},{1,5},{2,3},{3,2},{4,0},{5,1},{6,7},{7,6},{8,12},{9,13},{10,... | collective-permute-start | bytes 1032200 | tf_op jit(solution)/shard_map/ppermute | solution.py:811
  9.1 1.4 %mixed.1 = (f32[8,128,128]{2,1,0:T(8,128)S(1)}, f32[8,128,128]{2,1,0:T(8,128)S(1)}, s32[8,8,128]{2,1,0:T(8,128)S(1)}) custom-call(s32[8]{0:T(128)S(1)} %copy-done, bf16[8,768,256]{2,1,0:T(8,128)(2,1)S(1)} %get-tuple-element.46.wides, bf16[8,768,128]{2,1,0:T(8,128)(2,1)S(1)} %get-tuple-element.43.narrows), custom_call_target="tpu_custom_call" | custom-call | flops 402653184 | bytes 3145728 | tf_op jit(solution)/shard_map/mixed/pallas_call | solution.py:305
  10.6 0.6 collective-permute-start.2
  11.2 3.1 %collective-permute-done.1 = f32[4,168,128]{2,1,0:T(8,128)S(1)} collective-permute-done((f32[4,168,128]{2,1,0:T(8,128)S(1)}, f32[4,168,128]{2,1,0:T(8,128)S(1)}, u32[]{:S(2)}, u32[]{:S(2)}) %collective-permute-start.1) | collective-permute-done | bytes 344096 | tf_op jit(solution)/shard_map/ppermute | solution.py:811
  14.4 2.1 %collective-permute-start.3 = (f32[2,168,128]{2,1,0:T(8,128)S(1)}, f32[2,168,128]{2,1,0:T(8,128)S(1)}, u32[]{:S(2)}, u32[]{:S(2)}) collective-permute-start(f32[2,168,128]{2,1,0:T(8,128)S(1)} %slice.57), channel_id=1, source_target_pairs={{0,8},{1,9},{2,6},{3,7},{4,12},{5,13},{6,2},{7,3},{8,0},{9,1},{10,... | collective-permute-start | bytes 516104 | tf_op jit(solution)/shard_map/ppermute | solution.py:811
  16.7 1.6 %collective-permute-start.8 = (f32[4,128,128]{2,1,0:T(8,128)S(1)}, f32[4,128,128]{2,1,0:T(8,128)S(1)}, u32[]{:S(2)}, u32[]{:S(2)}) collective-permute-start(f32[4,128,128]{2,1,0:T(8,128)S(1)} %get-tuple-element.76), channel_id=1, source_target_pairs={{0,1},{1,0},{2,6},{3,7},{4,5},{5,4},{6,2},{7,3},{8,9},{9,8},{10,14... | collective-permute-start | bytes 786440 | tf_op jit(solution)/shard_map/ppermute | solution.py:811
  18.2 1.7 %collective-permute-done.3 = f32[2,168,128]{2,1,0:T(8,128)S(1)} collective-permute-done((f32[2,168,128]{2,1,0:T(8,128)S(1)}, f32[2,168,128]{2,1,0:T(8,128)S(1)}, u32[]{:S(2)}, u32[]{:S(2)}) %collective-permute-start.3) | collective-permute-done | bytes 172064 | tf_op jit(solution)/shard_map/ppermute | solution.py:811
  20.0 2.0 %collective-permute-start.4 = (f32[168,128]{1,0:T(8,128)S(1)}, f32[168,128]{1,0:T(8,128)S(1)}, u32[]{:S(2)}, u32[]{:S(2)}) collective-permute-start(f32[168,128]{1,0:T(8,128)S(1)} %slice_bitcast_fusion), channel_id=1, source_target_pairs={{0,1},{1,0},{2,10},{3,11},{4,5},{5,4},{6,14},{7,15},{8,9},{9,8},{1... | collective-permute-start | bytes 258056 | tf_op jit(solution)/shard_map/ppermute | solution.py:811
  22.0 1.1 %collective-permute-done.8 = f32[4,128,128]{2,1,0:T(8,128)S(1)} collective-permute-done((f32[4,128,128]{2,1,0:T(8,128)S(1)}, f32[4,128,128]{2,1,0:T(8,128)S(1)}, u32[]{:S(2)}, u32[]{:S(2)}) %collective-permute-start.8) | collective-permute-done | bytes 262176 | tf_op jit(solution)/shard_map/ppermute | solution.py:811
  23.2 1.6 %collective-permute-start.9 = (f32[2,128,128]{2,1,0:T(8,128)S(1)}, f32[2,128,128]{2,1,0:T(8,128)S(1)}, u32[]{:S(2)}, u32[]{:S(2)}) collective-permute-start(f32[2,128,128]{2,1,0:T(8,128)S(1)} %get-tuple-element.78), channel_id=1, source_target_pairs={{0,4},{1,5},{2,10},{3,11},{4,0},{5,1},{6,14},{7,15},{8,12},{9,13},... | collective-permute-start | bytes 393224 | tf_op jit(solution)/shard_map/ppermute | solution.py:811
  24.8 2.9 %collective-permute-start.5 = (f32[168,128]{1,0:T(8,128)S(1)}, f32[168,128]{1,0:T(8,128)S(1)}, u32[]{:S(2)}, u32[]{:S(2)}) collective-permute-start(f32[168,128]{1,0:T(8,128)S(1)} %fusion), channel_id=1, source_target_pairs={{0,16},{16,0},{1,17},{17,1},{2,18},{18,2},{3,19},{19,3},{4,20},{20... | collective-permute-start | bytes 258056 | tf_op jit(solution)/shard_map/ppermute | solution.py:804
  27.6 2.6 %collective-permute-done.5 = f32[168,128]{1,0:T(8,128)S(1)} collective-permute-done((f32[168,128]{1,0:T(8,128)S(1)}, f32[168,128]{1,0:T(8,128)S(1)}, u32[]{:S(2)}, u32[]{:S(2)}) %collective-permute-start.5) | collective-permute-done | bytes 86048 | tf_op jit(solution)/shard_map/ppermute | solution.py:804
  30.4 1.9 %collective-permute-start.10 = (f32[128,128]{1,0:T(8,128)S(1)}, f32[128,128]{1,0:T(8,128)S(1)}, u32[]{:S(2)}, u32[]{:S(2)}) collective-permute-start(f32[128,128]{1,0:T(8,128)S(1)} %get-tuple-element.80), channel_id=1, source_target_pairs={{0,8},{1,9},{2,3},{3,2},{4,12},{5,13},{6,7},{7,6},{8,0},{9,1},{10,... | collective-permute-start | bytes 196616 | tf_op jit(solution)/shard_map/ppermute | solution.py:811
  32.3 3.2 %first_panels.1 = (f32[288,256]{1,0:T(8,128)S(1)}, bf16[96,256]{1,0:T(8,128)(2,1)S(1)}, bf16[96,256]{1,0:T(8,128)(2,1)S(1)}, f32[16,256]{1,0:T(8,128)S(1)}, f32[...) custom-call(f32[168,128]{1,0:T(8,128)S(1)} %add.46.mine, ...), custom_call_target="tpu_custom_call" | custom-call | flops 1073741824 | bytes 1048576 | tf_op jit(solution)/shard_map/first_panels/pallas_call | solution.py:656
  35.5 3.4 %collective-permute-start.11 = (f32[128,128]{1,0:T(8,128)S(1)}, f32[128,128]{1,0:T(8,128)S(1)}, u32[]{:S(2)}, u32[]{:S(2)}) collective-permute-start(f32[128,128]{1,0:T(8,128)S(1)} %add.50), channel_id=1, source_target_pairs={{0,16},{16,0},{1,17},{17,1},{2,18},{18,2},{3,19},{19,3},{4,20},{20... | collective-permute-start | bytes 196616 | tf_op jit(solution)/shard_map/ppermute | solution.py:804
  38.9 4.2 %second_panels.1 = (f32[128,128]{1,0:T(8,128)S(1)}, f32[288,256]{1,0:T(8,128)S(1)}, bf16[96,256]{1,0:T(8,128)(2,1)S(1)}, bf16[96,256]{1,0:T(8,128)(2,1)S(1)}, f32[16,256]{1,0:T(8,128)S(1)}) custom-call(f32[288,256]{1,0:T(8,128)S(1)} %get-tuple-element.53.refs_0_, bf16[96,256]{1,0:T(8,128)(2,1)S(1)} %get-tuple-element.54.refs_1_, ...), custom_call_target="tpu_custom_call" | custom-call | flops 1073741824 | bytes 1048576 | tf_op jit(solution)/shard_map/second_panels/pallas_call | solution.py:656
  43.3 1.0 %third_panels.1.winv = f32[256,256]{1,0:T(8,128)S(1)} custom-call(f32[288,256]{1,0:T(8,128)S(1)} %get-tuple-element.62.wa_in, bf16[96,256]{1,0:T(8,128)(2,1)S(1)} %get-tuple-element.63.wl_in, bf16[96,256]{1,0:T(8,128)(2,1)S(1)} %get-tuple-element.64.wr_in, f32[16,256]{1,0:T(8,128)S(1)} %get-tuple-element.65.panel_in, f32[8,256]{1,0:T(8,128)S(1)} %get-tuple-element.66.scale), custom_call_target="tpu_custom_call" | custom-call | flops 1073741824 | bytes 1048576 | tf_op jit(solution)/shard_map/third_panels/pallas_call | solution.py:656
  44.5 0.6 %products.1 = f32[8,40,128]{2,1,0:T(8,128)S(1)} custom-call(f32[256,256]{1,0:T(8,128)S(1)} %third_panels.1.winv, f32[128,128]{1,0:T(8,128)S(1)} %get-tuple-element.67.ninv_ref, f32[128,128]{1,0:T(8,128)S(1)} %add.51.mine, f32[128,128]{1,0:T(8,128)S(1)} %collective-permute-done.12.other), custom_call_target="tpu_custom_call" | custom-call | tf_op jit(solution)/shard_map/products/pallas_call | solution.py:747
  45.1 10.3 %all_to_all.5.got_ref = f32[8,40,128]{2,1,0:T(8,128)S(1)} all-to-all(f32[8,40,128]{2,1,0:T(8,128)S(1)} %products.1), channel_id=1, replica_groups=mesh['dp0'=2,'dp1'=2,'dp2'=2,'dp3'=2,'own0'=2] {'dp1','dp2','own0'}, dimensions={0} | all-to-all | bytes 327680 | tf_op jit(solution)/shard_map/all_to_all | solution.py:867
  55.5 0.7 %placing.1 = (f32[5,16,256]{2,1,0:T(8,128)}, f32[8,16,64]{2,1,0:T(8,128)}) custom-call(s32[8,8,128]{2,1,0:T(8,128)S(1)} %get-tuple-element.47.slots_ref, f32[8,40,128]{2,1,0:T(8,128)S(1)} %all_to_all.5.got_ref), custom_call_target="tpu_custom_call" | custom-call | tf_op jit(solution)/shard_map/placing/pallas_call | solution.py:790
  (31 shorter events, 0.9 us)
Async XLA Ops:
  4.2 4.8 %copy-start = (s32[8]{0:T(128)S(1)}, s32[8]{0:T(128)}, u32[]{:S(2)}) copy-start(s32[8]{0:T(128)} %owner_map.1) | copy-start | bytes 100
  4.3 1.8 %collective-permute-start = (f32[4,168,128]{2,1,0:T(8,128)S(1)}, f32[4,168,128]{2,1,0:T(8,128)S(1)}, u32[]{:S(2)}, u32[]{:S(2)}) collective-permute-start(f32[4,168,128]{2,1,0:T(8,128)S(1)} %slice.42), channel_id=1, source_target_pairs={{0,2},{2,0},{1,3},{3,1},{4,6},{6,4},{5,7},{7,5},{8,10},{10,8},{9,1... | collective-permute-start | bytes 1032200 | tf_op jit(solution)/shard_map/ppermute | solution.py:804
  6.1 8.2 %collective-permute-start.1 = (f32[4,168,128]{2,1,0:T(8,128)S(1)}, f32[4,168,128]{2,1,0:T(8,128)S(1)}, u32[]{:S(2)}, u32[]{:S(2)}) collective-permute-start(f32[4,168,128]{2,1,0:T(8,128)S(1)} %slice_add_fusion.1), channel_id=1, source_target_pairs={{0,4},{1,5},{2,3},{3,2},{4,0},{5,1},{6,7},{7,6},{8,12},{9,13},{10,... | collective-permute-start | bytes 1032200 | tf_op jit(solution)/shard_map/ppermute | solution.py:811
  10.5 6.1 %collective-permute-start.7 = (f32[8,128,128]{2,1,0:T(8,128)S(1)}, f32[8,128,128]{2,1,0:T(8,128)S(1)}, u32[]{:S(2)}, u32[]{:S(2)}) collective-permute-start(f32[8,128,128]{2,1,0:T(8,128)S(1)} %get-tuple-element.50), channel_id=1, source_target_pairs={{0,2},{2,0},{1,3},{3,1},{4,6},{6,4},{5,7},{7,5},{8,10},{10,8},{9,1... | collective-permute-start | bytes 1572872 | tf_op jit(solution)/shard_map/ppermute | solution.py:804
  10.6 3.7 %collective-permute-start.2 = (f32[4,168,128]{2,1,0:T(8,128)S(1)}, f32[4,168,128]{2,1,0:T(8,128)S(1)}, u32[]{:S(2)}, u32[]{:S(2)}) collective-permute-start(f32[4,168,128]{2,1,0:T(8,128)S(1)} %slice_add_fusion), channel_id=1, source_target_pairs={{0,2},{2,0},{1,3},{3,1},{4,6},{6,4},{5,7},{7,5},{8,10},{10,8},{9,1... | collective-permute-start | bytes 1032200 | tf_op jit(solution)/shard_map/ppermute | solution.py:804
  14.4 5.5 %collective-permute-start.3 = (f32[2,168,128]{2,1,0:T(8,128)S(1)}, f32[2,168,128]{2,1,0:T(8,128)S(1)}, u32[]{:S(2)}, u32[]{:S(2)}) collective-permute-start(f32[2,168,128]{2,1,0:T(8,128)S(1)} %slice.57), channel_id=1, source_target_pairs={{0,8},{1,9},{2,6},{3,7},{4,12},{5,13},{6,2},{7,3},{8,0},{9,1},{10,... | collective-permute-start | bytes 516104 | tf_op jit(solution)/shard_map/ppermute | solution.py:811
  16.7 6.4 %collective-permute-start.8 = (f32[4,128,128]{2,1,0:T(8,128)S(1)}, f32[4,128,128]{2,1,0:T(8,128)S(1)}, u32[]{:S(2)}, u32[]{:S(2)}) collective-permute-start(f32[4,128,128]{2,1,0:T(8,128)S(1)} %get-tuple-element.76), channel_id=1, source_target_pairs={{0,1},{1,0},{2,6},{3,7},{4,5},{5,4},{6,2},{7,3},{8,9},{9,8},{10,14... | collective-permute-start | bytes 786440 | tf_op jit(solution)/shard_map/ppermute | solution.py:811
  20.0 4.8 %collective-permute-start.4 = (f32[168,128]{1,0:T(8,128)S(1)}, f32[168,128]{1,0:T(8,128)S(1)}, u32[]{:S(2)}, u32[]{:S(2)}) collective-permute-start(f32[168,128]{1,0:T(8,128)S(1)} %slice_bitcast_fusion), channel_id=1, source_target_pairs={{0,1},{1,0},{2,10},{3,11},{4,5},{5,4},{6,14},{7,15},{8,9},{9,8},{1... | collective-permute-start | bytes 258056 | tf_op jit(solution)/shard_map/ppermute | solution.py:811
  23.2 7.1 %collective-permute-start.9 = (f32[2,128,128]{2,1,0:T(8,128)S(1)}, f32[2,128,128]{2,1,0:T(8,128)S(1)}, u32[]{:S(2)}, u32[]{:S(2)}) collective-permute-start(f32[2,128,128]{2,1,0:T(8,128)S(1)} %get-tuple-element.78), channel_id=1, source_target_pairs={{0,4},{1,5},{2,10},{3,11},{4,0},{5,1},{6,14},{7,15},{8,12},{9,13},... | collective-permute-start | bytes 393224 | tf_op jit(solution)/shard_map/ppermute | solution.py:811
  24.8 5.4 %collective-permute-start.5 = (f32[168,128]{1,0:T(8,128)S(1)}, f32[168,128]{1,0:T(8,128)S(1)}, u32[]{:S(2)}, u32[]{:S(2)}) collective-permute-start(f32[168,128]{1,0:T(8,128)S(1)} %fusion), channel_id=1, source_target_pairs={{0,16},{16,0},{1,17},{17,1},{2,18},{18,2},{3,19},{19,3},{4,20},{20... | collective-permute-start | bytes 258056 | tf_op jit(solution)/shard_map/ppermute | solution.py:804
  30.3 2.0 %collective-permute-start.6 = (f32[168,128]{1,0:T(8,128)S(1)}, f32[168,128]{1,0:T(8,128)S(1)}, u32[]{:S(2)}, u32[]{:S(2)}) collective-permute-start(f32[168,128]{1,0:T(8,128)S(1)} %add.46.mine), channel_id=1, source_target_pairs={{0,2},{2,0},{1,3},{3,1},{4,6},{6,4},{5,7},{7,5},{8,10},{10,8},{9,1... | collective-permute-start | bytes 258056 | tf_op jit(solution)/shard_map/ppermute | solution.py:804
  30.4 5.1 %collective-permute-start.10 = (f32[128,128]{1,0:T(8,128)S(1)}, f32[128,128]{1,0:T(8,128)S(1)}, u32[]{:S(2)}, u32[]{:S(2)}) collective-permute-start(f32[128,128]{1,0:T(8,128)S(1)} %get-tuple-element.80), channel_id=1, source_target_pairs={{0,8},{1,9},{2,3},{3,2},{4,12},{5,13},{6,7},{7,6},{8,0},{9,1},{10,... | collective-permute-start | bytes 196616 | tf_op jit(solution)/shard_map/ppermute | solution.py:811
  35.5 7.7 %collective-permute-start.11 = (f32[128,128]{1,0:T(8,128)S(1)}, f32[128,128]{1,0:T(8,128)S(1)}, u32[]{:S(2)}, u32[]{:S(2)}) collective-permute-start(f32[128,128]{1,0:T(8,128)S(1)} %add.50), channel_id=1, source_target_pairs={{0,16},{16,0},{1,17},{17,1},{2,18},{18,2},{3,19},{19,3},{4,20},{20... | collective-permute-start | bytes 196616 | tf_op jit(solution)/shard_map/ppermute | solution.py:804
  43.2 1.3 %collective-permute-start.12 = (f32[128,128]{1,0:T(8,128)S(1)}, f32[128,128]{1,0:T(8,128)S(1)}, u32[]{:S(2)}, u32[]{:S(2)}) collective-permute-start(f32[128,128]{1,0:T(8,128)S(1)} %add.51.mine), channel_id=1, source_target_pairs={{0,2},{2,0},{1,3},{3,1},{4,6},{6,4},{5,7},{7,5},{8,10},{10,8},{9,1... | collective-permute-start | bytes 196616 | tf_op jit(solution)/shard_map/ppermute | solution.py:804

commit v23 on v21

--- a/solution.py
+++ b/solution.py
@@ -543,7 +543,7 @@
 
 
 STEPS = LANES // BLOCK
-FIRST_STEPS = 3
+FIRST_STEPS = 7
 SECOND_STEPS = 6
 
 

time: 57.4 us -> 56.3 us (0.981)
  blocking collectives: 11.2 us -> 9.74 us
    all_to_all x1, blocking collectives: 11.2 us -> 9.74 us  [on_device(): got = lax.all_to_all(sent, (place.near, place.second, place.first), 0, 0)]
    ppermute x7, waiting for transfers between devices: 3.4 us -> 4.11 us  [swap(): return lax.ppermute(value, axis, [(0, 1), (1, 0)])]
where the time goes in v23:
time: 56.3 us; the launch traced here: 56.1 us
  starting transfers between devices  18.6 us (33%)
  Pallas kernels  15.2 us (27%)
  waiting for transfers between devices  11.2 us (20%)
  blocking collectives  9.74 us (17%)
  between operations  0.84 us (1%)
    ppermute x6, starting transfers between devices, swap_by_core(): return lax.ppermute(value, names, pairs)  10.8 us
    all_to_all x1, blocking collectives, on_device(): got = lax.all_to_all(sent, (place.near, place.second, place.first), 0, 0)  9.74 us
    pallas_call x3, Pallas kernels, sweep_call(): pl.pallas_call(kernel, in_specs=[VMEM] * len(args), out_specs=[VMEM] * le...  8.25 us
    ppermute x7, starting transfers between devices, swap(): return lax.ppermute(value, axis, [(0, 1), (1, 0)])  7.83 us
    ppermute x6, waiting for transfers between devices, swap_by_core(): return lax.ppermute(value, names, pairs)  7.12 us
    ppermute x7, waiting for transfers between devices, swap(): return lax.ppermute(value, axis, [(0, 1), (1, 0)])  4.11 us
    pallas_call x1, Pallas kernels, hot_squares(): pl.pallas_call(functools.partial(hot_kernel, place), in_specs=[HBM, HBM],...  3.58 us
    pallas_call x1, Pallas kernels, mixed_sums(): pl.pallas_call(functools.partial(mixed_kernel, place), in_specs=[SMEM, VM...  1.45 us
  transfers between devices with their start and end apart: 13, of which 8 were waited for; matrix products, arithmetic and copies ran while one was open for 1% of the time, Pallas kernels for 18%

profile of v23, /device:TPU:0, one launch (start us, length us, event | category | flops | bytes accessed | tf_op | source)
XLA Modules:
  0.0 56.1 jit_solution(11196001571958551484)
XLA Ops:
  0.6 3.6 %hot_squares.1 = (f32[8,168,128]{2,1,0:T(8,128)S(1)}, f32[8,168,128]{2,1,0:T(8,128)S(1)}, bf16[8,768,256]{2,1,0:T(8,128)(2,1)S(1)}, bf16[8,768,128]{2,1,0:T(8,128)(2,1)S(1)}) custom-call(bf16[8,768,256]{2,1,0:T(8,128)(2,1)} %wide_hbm.1, bf16[8,768,128]{2,1,0:T(8,128)(2,1)} %narrow_hbm.1), custom_call_target="tpu_custom_call" | custom-call | flops 754974720 | bytes 3145728 | tf_op jit(solution)/shard_map/hot_squares/pallas_call | solution.py:268
  4.3 0.5 collective-permute-start
  4.8 0.6 %cold_squares.1 = (f32[4,168,128]{2,1,0:T(8,128)S(1)}, f32[4,168,128]{2,1,0:T(8,128)S(1)}) custom-call(bf16[8,768,256]{2,1,0:T(8,128)(2,1)S(1)} %get-tuple-element.46.wides, bf16[8,768,128]{2,1,0:T(8,128)(2,1)S(1)} %get-tuple-element.43.narrows), custom_call_target="tpu_custom_call" | custom-call | flops 251658240 | bytes 3145728 | tf_op jit(solution)/shard_map/cold_squares/pallas_call | solution.py:290
  5.4 0.7 %collective-permute-done = f32[4,168,128]{2,1,0:T(8,128)S(1)} collective-permute-done((f32[4,168,128]{2,1,0:T(8,128)S(1)}, f32[4,168,128]{2,1,0:T(8,128)S(1)}, u32[]{:S(2)}, u32[]{:S(2)}) %collective-permute-start) | collective-permute-done | bytes 344096 | tf_op jit(solution)/shard_map/ppermute | solution.py:804
  6.1 2.9 %collective-permute-start.1 = (f32[4,168,128]{2,1,0:T(8,128)S(1)}, f32[4,168,128]{2,1,0:T(8,128)S(1)}, u32[]{:S(2)}, u32[]{:S(2)}) collective-permute-start(f32[4,168,128]{2,1,0:T(8,128)S(1)} %slice_add_fusion.1), channel_id=1, source_target_pairs={{0,1},{1,0},{2,6},{3,7},{4,5},{5,4},{6,2},{7,3},{8,9},{9,8},{10,14... | collective-permute-start | bytes 1032200 | tf_op jit(solution)/shard_map/ppermute | solution.py:811
  9.0 1.4 %mixed.1 = (f32[8,128,128]{2,1,0:T(8,128)S(1)}, f32[8,128,128]{2,1,0:T(8,128)S(1)}, s32[8,8,128]{2,1,0:T(8,128)S(1)}) custom-call(s32[8]{0:T(128)S(1)} %copy-done, bf16[8,768,256]{2,1,0:T(8,128)(2,1)S(1)} %get-tuple-element.46.wides, bf16[8,768,128]{2,1,0:T(8,128)(2,1)S(1)} %get-tuple-element.43.narrows), custom_call_target="tpu_custom_call" | custom-call | flops 402653184 | bytes 3145728 | tf_op jit(solution)/shard_map/mixed/pallas_call | solution.py:305
  10.6 0.6 collective-permute-start.2
  11.2 3.1 %collective-permute-done.1 = f32[4,168,128]{2,1,0:T(8,128)S(1)} collective-permute-done((f32[4,168,128]{2,1,0:T(8,128)S(1)}, f32[4,168,128]{2,1,0:T(8,128)S(1)}, u32[]{:S(2)}, u32[]{:S(2)}) %collective-permute-start.1) | collective-permute-done | bytes 344096 | tf_op jit(solution)/shard_map/ppermute | solution.py:811
  14.4 2.1 %collective-permute-start.3 = (f32[2,168,128]{2,1,0:T(8,128)S(1)}, f32[2,168,128]{2,1,0:T(8,128)S(1)}, u32[]{:S(2)}, u32[]{:S(2)}) collective-permute-start(f32[2,168,128]{2,1,0:T(8,128)S(1)} %slice.57), channel_id=1, source_target_pairs={{0,4},{1,5},{2,10},{3,11},{4,0},{5,1},{6,14},{7,15},{8,12},{9,13},... | collective-permute-start | bytes 516104 | tf_op jit(solution)/shard_map/ppermute | solution.py:811
  16.6 1.6 %collective-permute-start.8 = (f32[4,128,128]{2,1,0:T(8,128)S(1)}, f32[4,128,128]{2,1,0:T(8,128)S(1)}, u32[]{:S(2)}, u32[]{:S(2)}) collective-permute-start(f32[4,128,128]{2,1,0:T(8,128)S(1)} %get-tuple-element.76), channel_id=1, source_target_pairs={{0,1},{1,0},{2,10},{3,11},{4,5},{5,4},{6,14},{7,15},{8,9},{9,8},{1... | collective-permute-start | bytes 786440 | tf_op jit(solution)/shard_map/ppermute | solution.py:811
  18.2 1.7 %collective-permute-done.3 = f32[2,168,128]{2,1,0:T(8,128)S(1)} collective-permute-done((f32[2,168,128]{2,1,0:T(8,128)S(1)}, f32[2,168,128]{2,1,0:T(8,128)S(1)}, u32[]{:S(2)}, u32[]{:S(2)}) %collective-permute-start.3) | collective-permute-done | bytes 172064 | tf_op jit(solution)/shard_map/ppermute | solution.py:811
  19.9 2.1 %collective-permute-start.4 = (f32[168,128]{1,0:T(8,128)S(1)}, f32[168,128]{1,0:T(8,128)S(1)}, u32[]{:S(2)}, u32[]{:S(2)}) collective-permute-start(f32[168,128]{1,0:T(8,128)S(1)} %slice_bitcast_fusion), channel_id=1, source_target_pairs={{0,8},{1,9},{2,3},{3,2},{4,12},{5,13},{6,7},{7,6},{8,0},{9,1},{10,... | collective-permute-start | bytes 258056 | tf_op jit(solution)/shard_map/ppermute | solution.py:811
  22.1 1.9 %collective-permute-done.8 = f32[4,128,128]{2,1,0:T(8,128)S(1)} collective-permute-done((f32[4,128,128]{2,1,0:T(8,128)S(1)}, f32[4,128,128]{2,1,0:T(8,128)S(1)}, u32[]{:S(2)}, u32[]{:S(2)}) %collective-permute-start.8) | collective-permute-done | bytes 262176 | tf_op jit(solution)/shard_map/ppermute | solution.py:811
  24.6 3.1 %collective-permute-start.5 = (f32[168,128]{1,0:T(8,128)S(1)}, f32[168,128]{1,0:T(8,128)S(1)}, u32[]{:S(2)}, u32[]{:S(2)}) collective-permute-start(f32[168,128]{1,0:T(8,128)S(1)} %fusion), channel_id=1, source_target_pairs={{0,16},{16,0},{1,17},{17,1},{2,18},{18,2},{3,19},{19,3},{4,20},{20... | collective-permute-start | bytes 258056 | tf_op jit(solution)/shard_map/ppermute | solution.py:804
  27.6 2.5 %collective-permute-done.5 = f32[168,128]{1,0:T(8,128)S(1)} collective-permute-done((f32[168,128]{1,0:T(8,128)S(1)}, f32[168,128]{1,0:T(8,128)S(1)}, u32[]{:S(2)}, u32[]{:S(2)}) %collective-permute-start.5) | collective-permute-done | bytes 86048 | tf_op jit(solution)/shard_map/ppermute | solution.py:804
  30.3 2.0 %collective-permute-start.10 = (f32[128,128]{1,0:T(8,128)S(1)}, f32[128,128]{1,0:T(8,128)S(1)}, u32[]{:S(2)}, u32[]{:S(2)}) collective-permute-start(f32[128,128]{1,0:T(8,128)S(1)} %get-tuple-element.80), channel_id=1, source_target_pairs={{0,8},{1,9},{2,6},{3,7},{4,12},{5,13},{6,2},{7,3},{8,0},{9,1},{10,... | collective-permute-start | bytes 196616 | tf_op jit(solution)/shard_map/ppermute | solution.py:811
  32.3 4.3 %first_panels.1 = (f32[288,256]{1,0:T(8,128)S(1)}, bf16[96,256]{1,0:T(8,128)(2,1)S(1)}, bf16[96,256]{1,0:T(8,128)(2,1)S(1)}, f32[16,256]{1,0:T(8,128)S(1)}, f32[...) custom-call(f32[168,128]{1,0:T(8,128)S(1)} %add.46.mine, ...), custom_call_target="tpu_custom_call" | custom-call | flops 1073741824 | bytes 1048576 | tf_op jit(solution)/shard_map/first_panels/pallas_call | solution.py:656
  36.6 3.4 %collective-permute-start.11 = (f32[128,128]{1,0:T(8,128)S(1)}, f32[128,128]{1,0:T(8,128)S(1)}, u32[]{:S(2)}, u32[]{:S(2)}) collective-permute-start(f32[128,128]{1,0:T(8,128)S(1)} %add.50), channel_id=1, source_target_pairs={{0,16},{16,0},{1,17},{17,1},{2,18},{18,2},{3,19},{19,3},{4,20},{20... | collective-permute-start | bytes 196616 | tf_op jit(solution)/shard_map/ppermute | solution.py:804
  40.1 2.9 %second_panels.1 = (f32[128,128]{1,0:T(8,128)S(1)}, f32[288,256]{1,0:T(8,128)S(1)}, bf16[96,256]{1,0:T(8,128)(2,1)S(1)}, bf16[96,256]{1,0:T(8,128)(2,1)S(1)}, f32[16,256]{1,0:T(8,128)S(1)}) custom-call(f32[288,256]{1,0:T(8,128)S(1)} %get-tuple-element.53.refs_0_, bf16[96,256]{1,0:T(8,128)(2,1)S(1)} %get-tuple-element.54.refs_1_, ...), custom_call_target="tpu_custom_call" | custom-call | flops 1073741824 | bytes 1048576 | tf_op jit(solution)/shard_map/second_panels/pallas_call | solution.py:656
  43.0 0.7 %collective-permute-done.11 = f32[128,128]{1,0:T(8,128)S(1)} collective-permute-done((f32[128,128]{1,0:T(8,128)S(1)}, f32[128,128]{1,0:T(8,128)S(1)}, u32[]{:S(2)}, u32[]{:S(2)}) %collective-permute-start.11) | collective-permute-done | bytes 65568 | tf_op jit(solution)/shard_map/ppermute | solution.py:804
  43.8 1.0 %third_panels.1.winv = f32[256,256]{1,0:T(8,128)S(1)} custom-call(f32[288,256]{1,0:T(8,128)S(1)} %get-tuple-element.62.wa_in, bf16[96,256]{1,0:T(8,128)(2,1)S(1)} %get-tuple-element.63.wl_in, bf16[96,256]{1,0:T(8,128)(2,1)S(1)} %get-tuple-element.64.wr_in, f32[16,256]{1,0:T(8,128)S(1)} %get-tuple-element.65.panel_in, f32[8,256]{1,0:T(8,128)S(1)} %get-tuple-element.66.scale), custom_call_target="tpu_custom_call" | custom-call | flops 1073741824 | bytes 1048576 | tf_op jit(solution)/shard_map/third_panels/pallas_call | solution.py:656
  45.0 0.6 %products.1 = f32[8,40,128]{2,1,0:T(8,128)S(1)} custom-call(f32[256,256]{1,0:T(8,128)S(1)} %third_panels.1.winv, f32[128,128]{1,0:T(8,128)S(1)} %get-tuple-element.67.ninv_ref, f32[128,128]{1,0:T(8,128)S(1)} %add.51.mine, f32[128,128]{1,0:T(8,128)S(1)} %collective-permute-done.12.other), custom_call_target="tpu_custom_call" | custom-call | tf_op jit(solution)/shard_map/products/pallas_call | solution.py:747
  45.7 9.7 %all_to_all.5.got_ref = f32[8,40,128]{2,1,0:T(8,128)S(1)} all-to-all(f32[8,40,128]{2,1,0:T(8,128)S(1)} %products.1), channel_id=1, replica_groups=mesh['dp0'=2,'dp1'=2,'dp2'=2,'dp3'=2,'own0'=2] {'dp1','dp2','own0'}, dimensions={0} | all-to-all | bytes 327680 | tf_op jit(solution)/shard_map/all_to_all | solution.py:867
  55.4 0.7 %placing.1 = (f32[5,16,256]{2,1,0:T(8,128)}, f32[8,16,64]{2,1,0:T(8,128)}) custom-call(s32[8,8,128]{2,1,0:T(8,128)S(1)} %get-tuple-element.47.slots_ref, f32[8,40,128]{2,1,0:T(8,128)S(1)} %all_to_all.5.got_ref), custom_call_target="tpu_custom_call" | custom-call | tf_op jit(solution)/shard_map/placing/pallas_call | solution.py:790
  (31 shorter events, 1.4 us)
Async XLA Ops:
  4.2 4.8 %copy-start = (s32[8]{0:T(128)S(1)}, s32[8]{0:T(128)}, u32[]{:S(2)}) copy-start(s32[8]{0:T(128)} %owner_map.1) | copy-start | bytes 100
  4.3 1.8 %collective-permute-start = (f32[4,168,128]{2,1,0:T(8,128)S(1)}, f32[4,168,128]{2,1,0:T(8,128)S(1)}, u32[]{:S(2)}, u32[]{:S(2)}) collective-permute-start(f32[4,168,128]{2,1,0:T(8,128)S(1)} %slice.42), channel_id=1, source_target_pairs={{0,2},{2,0},{1,3},{3,1},{4,6},{6,4},{5,7},{7,5},{8,10},{10,8},{9,1... | collective-permute-start | bytes 1032200 | tf_op jit(solution)/shard_map/ppermute | solution.py:804
  6.1 8.2 %collective-permute-start.1 = (f32[4,168,128]{2,1,0:T(8,128)S(1)}, f32[4,168,128]{2,1,0:T(8,128)S(1)}, u32[]{:S(2)}, u32[]{:S(2)}) collective-permute-start(f32[4,168,128]{2,1,0:T(8,128)S(1)} %slice_add_fusion.1), channel_id=1, source_target_pairs={{0,1},{1,0},{2,6},{3,7},{4,5},{5,4},{6,2},{7,3},{8,9},{9,8},{10,14... | collective-permute-start | bytes 1032200 | tf_op jit(solution)/shard_map/ppermute | solution.py:811
  10.5 6.0 %collective-permute-start.7 = (f32[8,128,128]{2,1,0:T(8,128)S(1)}, f32[8,128,128]{2,1,0:T(8,128)S(1)}, u32[]{:S(2)}, u32[]{:S(2)}) collective-permute-start(f32[8,128,128]{2,1,0:T(8,128)S(1)} %get-tuple-element.50), channel_id=1, source_target_pairs={{0,2},{2,0},{1,3},{3,1},{4,6},{6,4},{5,7},{7,5},{8,10},{10,8},{9,1... | collective-permute-start | bytes 1572872 | tf_op jit(solution)/shard_map/ppermute | solution.py:804
  10.6 3.7 %collective-permute-start.2 = (f32[4,168,128]{2,1,0:T(8,128)S(1)}, f32[4,168,128]{2,1,0:T(8,128)S(1)}, u32[]{:S(2)}, u32[]{:S(2)}) collective-permute-start(f32[4,168,128]{2,1,0:T(8,128)S(1)} %slice_add_fusion), channel_id=1, source_target_pairs={{0,2},{2,0},{1,3},{3,1},{4,6},{6,4},{5,7},{7,5},{8,10},{10,8},{9,1... | collective-permute-start | bytes 1032200 | tf_op jit(solution)/shard_map/ppermute | solution.py:804
  14.4 5.5 %collective-permute-start.3 = (f32[2,168,128]{2,1,0:T(8,128)S(1)}, f32[2,168,128]{2,1,0:T(8,128)S(1)}, u32[]{:S(2)}, u32[]{:S(2)}) collective-permute-start(f32[2,168,128]{2,1,0:T(8,128)S(1)} %slice.57), channel_id=1, source_target_pairs={{0,4},{1,5},{2,10},{3,11},{4,0},{5,1},{6,14},{7,15},{8,12},{9,13},... | collective-permute-start | bytes 516104 | tf_op jit(solution)/shard_map/ppermute | solution.py:811
  16.6 7.4 %collective-permute-start.8 = (f32[4,128,128]{2,1,0:T(8,128)S(1)}, f32[4,128,128]{2,1,0:T(8,128)S(1)}, u32[]{:S(2)}, u32[]{:S(2)}) collective-permute-start(f32[4,128,128]{2,1,0:T(8,128)S(1)} %get-tuple-element.76), channel_id=1, source_target_pairs={{0,1},{1,0},{2,10},{3,11},{4,5},{5,4},{6,14},{7,15},{8,9},{9,8},{1... | collective-permute-start | bytes 786440 | tf_op jit(solution)/shard_map/ppermute | solution.py:811
  19.9 4.6 %collective-permute-start.4 = (f32[168,128]{1,0:T(8,128)S(1)}, f32[168,128]{1,0:T(8,128)S(1)}, u32[]{:S(2)}, u32[]{:S(2)}) collective-permute-start(f32[168,128]{1,0:T(8,128)S(1)} %slice_bitcast_fusion), channel_id=1, source_target_pairs={{0,8},{1,9},{2,3},{3,2},{4,12},{5,13},{6,7},{7,6},{8,0},{9,1},{10,... | collective-permute-start | bytes 258056 | tf_op jit(solution)/shard_map/ppermute | solution.py:811
  24.1 6.2 %collective-permute-start.9 = (f32[2,128,128]{2,1,0:T(8,128)S(1)}, f32[2,128,128]{2,1,0:T(8,128)S(1)}, u32[]{:S(2)}, u32[]{:S(2)}) collective-permute-start(f32[2,128,128]{2,1,0:T(8,128)S(1)} %get-tuple-element.78), channel_id=1, source_target_pairs={{0,4},{1,5},{2,3},{3,2},{4,0},{5,1},{6,7},{7,6},{8,12},{9,13},{10,... | collective-permute-start | bytes 393224 | tf_op jit(solution)/shard_map/ppermute | solution.py:811
  24.6 5.6 %collective-permute-start.5 = (f32[168,128]{1,0:T(8,128)S(1)}, f32[168,128]{1,0:T(8,128)S(1)}, u32[]{:S(2)}, u32[]{:S(2)}) collective-permute-start(f32[168,128]{1,0:T(8,128)S(1)} %fusion), channel_id=1, source_target_pairs={{0,16},{16,0},{1,17},{17,1},{2,18},{18,2},{3,19},{19,3},{4,20},{20... | collective-permute-start | bytes 258056 | tf_op jit(solution)/shard_map/ppermute | solution.py:804
  30.1 2.1 %collective-permute-start.6 = (f32[168,128]{1,0:T(8,128)S(1)}, f32[168,128]{1,0:T(8,128)S(1)}, u32[]{:S(2)}, u32[]{:S(2)}) collective-permute-start(f32[168,128]{1,0:T(8,128)S(1)} %add.46.mine), channel_id=1, source_target_pairs={{0,2},{2,0},{1,3},{3,1},{4,6},{6,4},{5,7},{7,5},{8,10},{10,8},{9,1... | collective-permute-start | bytes 258056 | tf_op jit(solution)/shard_map/ppermute | solution.py:804
  30.3 6.3 %collective-permute-start.10 = (f32[128,128]{1,0:T(8,128)S(1)}, f32[128,128]{1,0:T(8,128)S(1)}, u32[]{:S(2)}, u32[]{:S(2)}) collective-permute-start(f32[128,128]{1,0:T(8,128)S(1)} %get-tuple-element.80), channel_id=1, source_target_pairs={{0,8},{1,9},{2,6},{3,7},{4,12},{5,13},{6,2},{7,3},{8,0},{9,1},{10,... | collective-permute-start | bytes 196616 | tf_op jit(solution)/shard_map/ppermute | solution.py:811
  36.6 7.1 %collective-permute-start.11 = (f32[128,128]{1,0:T(8,128)S(1)}, f32[128,128]{1,0:T(8,128)S(1)}, u32[]{:S(2)}, u32[]{:S(2)}) collective-permute-start(f32[128,128]{1,0:T(8,128)S(1)} %add.50), channel_id=1, source_target_pairs={{0,16},{16,0},{1,17},{17,1},{2,18},{18,2},{3,19},{19,3},{4,20},{20... | collective-permute-start | bytes 196616 | tf_op jit(solution)/shard_map/ppermute | solution.py:804
  43.7 1.3 %collective-permute-start.12 = (f32[128,128]{1,0:T(8,128)S(1)}, f32[128,128]{1,0:T(8,128)S(1)}, u32[]{:S(2)}, u32[]{:S(2)}) collective-permute-start(f32[128,128]{1,0:T(8,128)S(1)} %add.51.mine), channel_id=1, source_target_pairs={{0,2},{2,0},{1,3},{3,1},{4,6},{6,4},{5,7},{7,5},{8,10},{10,8},{9,1... | collective-permute-start | bytes 196616 | tf_op jit(solution)/shard_map/ppermute | solution.py:804

commit v24 on v20

--- a/solution.py
+++ b/solution.py
@@ -196,16 +196,19 @@
 
     before = None
     for at, i in enumerate(order):
-        for copy in copies[i]:
-            copy.wait()
+        wide_copy, narrow_copy = copies[i]
+        wide_copy.wait()
         if at + AHEAD < len(order):
             for copy in copies[order[at + AHEAD]]:
                 copy.start()
+        if i in HOT:
+            wcov = transposed_dot(wides[i], wides[i])
         if before is not None:
             pack(*before)
             before = None
+        narrow_copy.wait()
         if i in HOT:
-            before = (i, square_sums(wides[i], narrows[i]))
+            before = (i, (wcov, transposed_dot(narrows[i], narrows[i])))
 
 
 def cold_kernel(place, wides, narrows, keep, send, a_flat, b_flat):
@@ -586,17 +589,18 @@
     n = LANES
     slab = a_flat[n : n + PANEL]
     first, square = unpack_pair(a_flat[:n], jnp.broadcast_to(slab[:1], (n, n)))
-    corner = b_flat[:n] / total
+    corner = b_flat[:n]
     last = unfold(b_flat[n:], jnp.broadcast_to(slab[1:2], (n, n)))
     row, col = iotas((n, n))
-    damp = jnp.where(row == col, DAMP, 0.0)
+    damp = jnp.where(row == col, DAMP * total, 0.0)
     clear(wide_work)
     clear(narrow_work)
-    first, last, square = first / total + damp, last / total + damp, square / total + damp
+    first, last, square = first + damp, last + damp, square + damp
     by_first, by_last, by_square = (unit_scale(block) for block in (first, last, square))
-    ws_ref[:, :n] = by_first
-    ws_ref[:, n:] = by_last
-    ns_ref[...] = by_square
+    root = total**0.5
+    ws_ref[:, :n] = by_first * root
+    ws_ref[:, n:] = by_last * root
+    ns_ref[...] = by_square * root
     first_across, last_across = on_rows(by_first), on_rows(by_last)
     first_down, last_down = first_across.T, last_across.T
     corner = (corner * first_down) * last_across

time: 56.4 us -> 57.9 us (1.027)
  Pallas kernels: 15.4 us -> 16.9 us
    pallas_call x1, Pallas kernels: 3.58 us -> 5.13 us  [hot_squares(): pl.pallas_call(functools.partial(hot_kernel, place), in_specs=[HBM, HBM],...]
  transfers between devices with their start and end apart: 13 -> 13, of which waited for: 7 -> 7; matrix products, arithmetic and copies ran while one was open for 1% -> 1% of each run, Pallas kernels for 19% -> 18%
where the time goes in v24:
time: 57.9 us; the launch traced here: 57.7 us
  starting transfers between devices  18.6 us (32%)
  Pallas kernels  16.9 us (29%)
  waiting for transfers between devices  10.5 us (18%)
  blocking collectives  10.3 us (18%)
  between operations  0.86 us (1%)
    ppermute x6, starting transfers between devices, swap_by_core(): return lax.ppermute(value, names, pairs)  10.8 us
    all_to_all x1, blocking collectives, on_device(): got = lax.all_to_all(sent, (place.near, place.second, place.first), 0, 0)  10.3 us
    pallas_call x3, Pallas kernels, sweep_call(): pl.pallas_call(kernel, in_specs=[VMEM] * len(args), out_specs=[VMEM] * le...  8.43 us
    ppermute x7, starting transfers between devices, swap(): return lax.ppermute(value, axis, [(0, 1), (1, 0)])  7.83 us
    ppermute x6, waiting for transfers between devices, swap_by_core(): return lax.ppermute(value, names, pairs)  7.13 us
    pallas_call x1, Pallas kernels, hot_squares(): pl.pallas_call(functools.partial(hot_kernel, place), in_specs=[HBM, HBM],...  5.13 us
    ppermute x7, waiting for transfers between devices, swap(): return lax.ppermute(value, axis, [(0, 1), (1, 0)])  3.4 us
    pallas_call x1, Pallas kernels, mixed_sums(): pl.pallas_call(functools.partial(mixed_kernel, place), in_specs=[SMEM, VM...  1.44 us
  transfers between devices with their start and end apart: 13, of which 7 were waited for; matrix products, arithmetic and copies ran while one was open for 1% of the time, Pallas kernels for 18%

profile of v24, /device:TPU:0, one launch (start us, length us, event | category | flops | bytes accessed | tf_op | source)
XLA Modules:
  0.0 57.7 jit_solution(3386654006133572245)
XLA Ops:
  0.6 5.1 %hot_squares.1 = (f32[8,168,128]{2,1,0:T(8,128)S(1)}, f32[8,168,128]{2,1,0:T(8,128)S(1)}, bf16[8,768,256]{2,1,0:T(8,128)(2,1)S(1)}, bf16[8,768,128]{2,1,0:T(8,128)(2,1)S(1)}) custom-call(bf16[8,768,256]{2,1,0:T(8,128)(2,1)} %wide_hbm.1, bf16[8,768,128]{2,1,0:T(8,128)(2,1)} %narrow_hbm.1), custom_call_target="tpu_custom_call" | custom-call | flops 754974720 | bytes 3145728 | tf_op jit(solution)/shard_map/hot_squares/pallas_call | solution.py:271
  5.8 0.5 collective-permute-start
  6.3 0.6 %cold_squares.1 = (f32[4,168,128]{2,1,0:T(8,128)S(1)}, f32[4,168,128]{2,1,0:T(8,128)S(1)}) custom-call(bf16[8,768,256]{2,1,0:T(8,128)(2,1)S(1)} %get-tuple-element.46.wides, bf16[8,768,128]{2,1,0:T(8,128)(2,1)S(1)} %get-tuple-element.43.narrows), custom_call_target="tpu_custom_call" | custom-call | flops 251658240 | bytes 3145728 | tf_op jit(solution)/shard_map/cold_squares/pallas_call | solution.py:293
  6.9 0.7 %collective-permute-done = f32[4,168,128]{2,1,0:T(8,128)S(1)} collective-permute-done((f32[4,168,128]{2,1,0:T(8,128)S(1)}, f32[4,168,128]{2,1,0:T(8,128)S(1)}, u32[]{:S(2)}, u32[]{:S(2)}) %collective-permute-start) | collective-permute-done | bytes 344096 | tf_op jit(solution)/shard_map/ppermute | solution.py:808
  7.7 2.9 %collective-permute-start.1 = (f32[4,168,128]{2,1,0:T(8,128)S(1)}, f32[4,168,128]{2,1,0:T(8,128)S(1)}, u32[]{:S(2)}, u32[]{:S(2)}) collective-permute-start(f32[4,168,128]{2,1,0:T(8,128)S(1)} %slice_add_fusion.1), channel_id=1, source_target_pairs={{0,1},{1,0},{2,6},{3,7},{4,5},{5,4},{6,2},{7,3},{8,9},{9,8},{10,14... | collective-permute-start | bytes 1032200 | tf_op jit(solution)/shard_map/ppermute | solution.py:815
  10.6 1.4 %mixed.1 = (f32[8,128,128]{2,1,0:T(8,128)S(1)}, f32[8,128,128]{2,1,0:T(8,128)S(1)}, s32[8,8,128]{2,1,0:T(8,128)S(1)}) custom-call(s32[8]{0:T(128)S(1)} %copy-done, bf16[8,768,256]{2,1,0:T(8,128)(2,1)S(1)} %get-tuple-element.46.wides, bf16[8,768,128]{2,1,0:T(8,128)(2,1)S(1)} %get-tuple-element.43.narrows), custom_call_target="tpu_custom_call" | custom-call | flops 402653184 | bytes 3145728 | tf_op jit(solution)/shard_map/mixed/pallas_call | solution.py:308
  12.2 0.6 collective-permute-start.2
  12.7 3.1 %collective-permute-done.1 = f32[4,168,128]{2,1,0:T(8,128)S(1)} collective-permute-done((f32[4,168,128]{2,1,0:T(8,128)S(1)}, f32[4,168,128]{2,1,0:T(8,128)S(1)}, u32[]{:S(2)}, u32[]{:S(2)}) %collective-permute-start.1) | collective-permute-done | bytes 344096 | tf_op jit(solution)/shard_map/ppermute | solution.py:815
  15.9 2.1 %collective-permute-start.3 = (f32[2,168,128]{2,1,0:T(8,128)S(1)}, f32[2,168,128]{2,1,0:T(8,128)S(1)}, u32[]{:S(2)}, u32[]{:S(2)}) collective-permute-start(f32[2,168,128]{2,1,0:T(8,128)S(1)} %slice.57), channel_id=1, source_target_pairs={{0,4},{1,5},{2,10},{3,11},{4,0},{5,1},{6,14},{7,15},{8,12},{9,13},... | collective-permute-start | bytes 516104 | tf_op jit(solution)/shard_map/ppermute | solution.py:815
  18.2 1.6 %collective-permute-start.8 = (f32[4,128,128]{2,1,0:T(8,128)S(1)}, f32[4,128,128]{2,1,0:T(8,128)S(1)}, u32[]{:S(2)}, u32[]{:S(2)}) collective-permute-start(f32[4,128,128]{2,1,0:T(8,128)S(1)} %get-tuple-element.76), channel_id=1, source_target_pairs={{0,1},{1,0},{2,10},{3,11},{4,5},{5,4},{6,14},{7,15},{8,9},{9,8},{1... | collective-permute-start | bytes 786440 | tf_op jit(solution)/shard_map/ppermute | solution.py:815
  19.7 1.7 %collective-permute-done.3 = f32[2,168,128]{2,1,0:T(8,128)S(1)} collective-permute-done((f32[2,168,128]{2,1,0:T(8,128)S(1)}, f32[2,168,128]{2,1,0:T(8,128)S(1)}, u32[]{:S(2)}, u32[]{:S(2)}) %collective-permute-start.3) | collective-permute-done | bytes 172064 | tf_op jit(solution)/shard_map/ppermute | solution.py:815
  21.5 2.1 %collective-permute-start.4 = (f32[168,128]{1,0:T(8,128)S(1)}, f32[168,128]{1,0:T(8,128)S(1)}, u32[]{:S(2)}, u32[]{:S(2)}) collective-permute-start(f32[168,128]{1,0:T(8,128)S(1)} %slice_bitcast_fusion), channel_id=1, source_target_pairs={{0,8},{1,9},{2,3},{3,2},{4,12},{5,13},{6,7},{7,6},{8,0},{9,1},{10,... | collective-permute-start | bytes 258056 | tf_op jit(solution)/shard_map/ppermute | solution.py:815
  23.6 1.9 %collective-permute-done.8 = f32[4,128,128]{2,1,0:T(8,128)S(1)} collective-permute-done((f32[4,128,128]{2,1,0:T(8,128)S(1)}, f32[4,128,128]{2,1,0:T(8,128)S(1)}, u32[]{:S(2)}, u32[]{:S(2)}) %collective-permute-start.8) | collective-permute-done | bytes 262176 | tf_op jit(solution)/shard_map/ppermute | solution.py:815
  25.7 0.4 collective-permute-done.4
  26.1 3.1 %collective-permute-start.5 = (f32[168,128]{1,0:T(8,128)S(1)}, f32[168,128]{1,0:T(8,128)S(1)}, u32[]{:S(2)}, u32[]{:S(2)}) collective-permute-start(f32[168,128]{1,0:T(8,128)S(1)} %fusion), channel_id=1, source_target_pairs={{0,16},{16,0},{1,17},{17,1},{2,18},{18,2},{3,19},{19,3},{4,20},{20... | collective-permute-start | bytes 258056 | tf_op jit(solution)/shard_map/ppermute | solution.py:808
  29.2 2.5 %collective-permute-done.5 = f32[168,128]{1,0:T(8,128)S(1)} collective-permute-done((f32[168,128]{1,0:T(8,128)S(1)}, f32[168,128]{1,0:T(8,128)S(1)}, u32[]{:S(2)}, u32[]{:S(2)}) %collective-permute-start.5) | collective-permute-done | bytes 86048 | tf_op jit(solution)/shard_map/ppermute | solution.py:808
  31.8 2.0 %collective-permute-start.10 = (f32[128,128]{1,0:T(8,128)S(1)}, f32[128,128]{1,0:T(8,128)S(1)}, u32[]{:S(2)}, u32[]{:S(2)}) collective-permute-start(f32[128,128]{1,0:T(8,128)S(1)} %get-tuple-element.80), channel_id=1, source_target_pairs={{0,8},{1,9},{2,6},{3,7},{4,12},{5,13},{6,2},{7,3},{8,0},{9,1},{10,... | collective-permute-start | bytes 196616 | tf_op jit(solution)/shard_map/ppermute | solution.py:815
  33.8 3.2 %first_panels.1 = (f32[288,256]{1,0:T(8,128)S(1)}, bf16[96,256]{1,0:T(8,128)(2,1)S(1)}, bf16[96,256]{1,0:T(8,128)(2,1)S(1)}, f32[16,256]{1,0:T(8,128)S(1)}, f32[...) custom-call(f32[168,128]{1,0:T(8,128)S(1)} %add.46.mine, ...), custom_call_target="tpu_custom_call" | custom-call | flops 1073741824 | bytes 1048576 | tf_op jit(solution)/shard_map/first_panels/pallas_call | solution.py:660
  37.0 3.4 %collective-permute-start.11 = (f32[128,128]{1,0:T(8,128)S(1)}, f32[128,128]{1,0:T(8,128)S(1)}, u32[]{:S(2)}, u32[]{:S(2)}) collective-permute-start(f32[128,128]{1,0:T(8,128)S(1)} %add.50), channel_id=1, source_target_pairs={{0,16},{16,0},{1,17},{17,1},{2,18},{18,2},{3,19},{19,3},{4,20},{20... | collective-permute-start | bytes 196616 | tf_op jit(solution)/shard_map/ppermute | solution.py:808
  40.5 4.2 %second_panels.1 = (f32[128,128]{1,0:T(8,128)S(1)}, f32[288,256]{1,0:T(8,128)S(1)}, bf16[96,256]{1,0:T(8,128)(2,1)S(1)}, bf16[96,256]{1,0:T(8,128)(2,1)S(1)}, f32[16,256]{1,0:T(8,128)S(1)}) custom-call(f32[288,256]{1,0:T(8,128)S(1)} %get-tuple-element.53.refs_0_, bf16[96,256]{1,0:T(8,128)(2,1)S(1)} %get-tuple-element.54.refs_1_, ...), custom_call_target="tpu_custom_call" | custom-call | flops 1073741824 | bytes 1048576 | tf_op jit(solution)/shard_map/second_panels/pallas_call | solution.py:660
  44.8 1.0 %third_panels.1.winv = f32[256,256]{1,0:T(8,128)S(1)} custom-call(f32[288,256]{1,0:T(8,128)S(1)} %get-tuple-element.62.wa_in, bf16[96,256]{1,0:T(8,128)(2,1)S(1)} %get-tuple-element.63.wl_in, bf16[96,256]{1,0:T(8,128)(2,1)S(1)} %get-tuple-element.64.wr_in, f32[16,256]{1,0:T(8,128)S(1)} %get-tuple-element.65.panel_in, f32[8,256]{1,0:T(8,128)S(1)} %get-tuple-element.66.scale), custom_call_target="tpu_custom_call" | custom-call | flops 1073741824 | bytes 1048576 | tf_op jit(solution)/shard_map/third_panels/pallas_call | solution.py:660
  46.1 0.6 %products.1 = f32[8,40,128]{2,1,0:T(8,128)S(1)} custom-call(f32[256,256]{1,0:T(8,128)S(1)} %third_panels.1.winv, f32[128,128]{1,0:T(8,128)S(1)} %get-tuple-element.67.ninv_ref, f32[128,128]{1,0:T(8,128)S(1)} %add.51.mine, f32[128,128]{1,0:T(8,128)S(1)} %collective-permute-done.12.other), custom_call_target="tpu_custom_call" | custom-call | tf_op jit(solution)/shard_map/products/pallas_call | solution.py:751
  46.7 10.3 %all_to_all.5.got_ref = f32[8,40,128]{2,1,0:T(8,128)S(1)} all-to-all(f32[8,40,128]{2,1,0:T(8,128)S(1)} %products.1), channel_id=1, replica_groups=mesh['dp0'=2,'dp1'=2,'dp2'=2,'dp3'=2,'own0'=2] {'dp1','dp2','own0'}, dimensions={0} | all-to-all | bytes 327680 | tf_op jit(solution)/shard_map/all_to_all | solution.py:871
  57.0 0.7 %placing.1 = (f32[5,16,256]{2,1,0:T(8,128)}, f32[8,16,64]{2,1,0:T(8,128)}) custom-call(s32[8,8,128]{2,1,0:T(8,128)S(1)} %get-tuple-element.47.slots_ref, f32[8,40,128]{2,1,0:T(8,128)S(1)} %all_to_all.5.got_ref), custom_call_target="tpu_custom_call" | custom-call | tf_op jit(solution)/shard_map/placing/pallas_call | solution.py:794
  (31 shorter events, 1.0 us)
Async XLA Ops:
  5.8 4.8 %copy-start = (s32[8]{0:T(128)S(1)}, s32[8]{0:T(128)}, u32[]{:S(2)}) copy-start(s32[8]{0:T(128)} %owner_map.1) | copy-start | bytes 100
  5.8 1.8 %collective-permute-start = (f32[4,168,128]{2,1,0:T(8,128)S(1)}, f32[4,168,128]{2,1,0:T(8,128)S(1)}, u32[]{:S(2)}, u32[]{:S(2)}) collective-permute-start(f32[4,168,128]{2,1,0:T(8,128)S(1)} %slice.42), channel_id=1, source_target_pairs={{0,2},{2,0},{1,3},{3,1},{4,6},{6,4},{5,7},{7,5},{8,10},{10,8},{9,1... | collective-permute-start | bytes 1032200 | tf_op jit(solution)/shard_map/ppermute | solution.py:808
  7.7 8.2 %collective-permute-start.1 = (f32[4,168,128]{2,1,0:T(8,128)S(1)}, f32[4,168,128]{2,1,0:T(8,128)S(1)}, u32[]{:S(2)}, u32[]{:S(2)}) collective-permute-start(f32[4,168,128]{2,1,0:T(8,128)S(1)} %slice_add_fusion.1), channel_id=1, source_target_pairs={{0,1},{1,0},{2,6},{3,7},{4,5},{5,4},{6,2},{7,3},{8,9},{9,8},{10,14... | collective-permute-start | bytes 1032200 | tf_op jit(solution)/shard_map/ppermute | solution.py:815
  12.0 6.0 %collective-permute-start.7 = (f32[8,128,128]{2,1,0:T(8,128)S(1)}, f32[8,128,128]{2,1,0:T(8,128)S(1)}, u32[]{:S(2)}, u32[]{:S(2)}) collective-permute-start(f32[8,128,128]{2,1,0:T(8,128)S(1)} %get-tuple-element.50), channel_id=1, source_target_pairs={{0,2},{2,0},{1,3},{3,1},{4,6},{6,4},{5,7},{7,5},{8,10},{10,8},{9,1... | collective-permute-start | bytes 1572872 | tf_op jit(solution)/shard_map/ppermute | solution.py:808
  12.2 3.7 %collective-permute-start.2 = (f32[4,168,128]{2,1,0:T(8,128)S(1)}, f32[4,168,128]{2,1,0:T(8,128)S(1)}, u32[]{:S(2)}, u32[]{:S(2)}) collective-permute-start(f32[4,168,128]{2,1,0:T(8,128)S(1)} %slice_add_fusion), channel_id=1, source_target_pairs={{0,2},{2,0},{1,3},{3,1},{4,6},{6,4},{5,7},{7,5},{8,10},{10,8},{9,1... | collective-permute-start | bytes 1032200 | tf_op jit(solution)/shard_map/ppermute | solution.py:808
  15.9 5.5 %collective-permute-start.3 = (f32[2,168,128]{2,1,0:T(8,128)S(1)}, f32[2,168,128]{2,1,0:T(8,128)S(1)}, u32[]{:S(2)}, u32[]{:S(2)}) collective-permute-start(f32[2,168,128]{2,1,0:T(8,128)S(1)} %slice.57), channel_id=1, source_target_pairs={{0,4},{1,5},{2,10},{3,11},{4,0},{5,1},{6,14},{7,15},{8,12},{9,13},... | collective-permute-start | bytes 516104 | tf_op jit(solution)/shard_map/ppermute | solution.py:815
  18.2 7.4 %collective-permute-start.8 = (f32[4,128,128]{2,1,0:T(8,128)S(1)}, f32[4,128,128]{2,1,0:T(8,128)S(1)}, u32[]{:S(2)}, u32[]{:S(2)}) collective-permute-start(f32[4,128,128]{2,1,0:T(8,128)S(1)} %get-tuple-element.76), channel_id=1, source_target_pairs={{0,1},{1,0},{2,10},{3,11},{4,5},{5,4},{6,14},{7,15},{8,9},{9,8},{1... | collective-permute-start | bytes 786440 | tf_op jit(solution)/shard_map/ppermute | solution.py:815
  21.5 4.6 %collective-permute-start.4 = (f32[168,128]{1,0:T(8,128)S(1)}, f32[168,128]{1,0:T(8,128)S(1)}, u32[]{:S(2)}, u32[]{:S(2)}) collective-permute-start(f32[168,128]{1,0:T(8,128)S(1)} %slice_bitcast_fusion), channel_id=1, source_target_pairs={{0,8},{1,9},{2,3},{3,2},{4,12},{5,13},{6,7},{7,6},{8,0},{9,1},{10,... | collective-permute-start | bytes 258056 | tf_op jit(solution)/shard_map/ppermute | solution.py:815
  25.6 6.2 %collective-permute-start.9 = (f32[2,128,128]{2,1,0:T(8,128)S(1)}, f32[2,128,128]{2,1,0:T(8,128)S(1)}, u32[]{:S(2)}, u32[]{:S(2)}) collective-permute-start(f32[2,128,128]{2,1,0:T(8,128)S(1)} %get-tuple-element.78), channel_id=1, source_target_pairs={{0,4},{1,5},{2,3},{3,2},{4,0},{5,1},{6,7},{7,6},{8,12},{9,13},{10,... | collective-permute-start | bytes 393224 | tf_op jit(solution)/shard_map/ppermute | solution.py:815
  26.1 5.6 %collective-permute-start.5 = (f32[168,128]{1,0:T(8,128)S(1)}, f32[168,128]{1,0:T(8,128)S(1)}, u32[]{:S(2)}, u32[]{:S(2)}) collective-permute-start(f32[168,128]{1,0:T(8,128)S(1)} %fusion), channel_id=1, source_target_pairs={{0,16},{16,0},{1,17},{17,1},{2,18},{18,2},{3,19},{19,3},{4,20},{20... | collective-permute-start | bytes 258056 | tf_op jit(solution)/shard_map/ppermute | solution.py:808
  31.7 2.1 %collective-permute-start.6 = (f32[168,128]{1,0:T(8,128)S(1)}, f32[168,128]{1,0:T(8,128)S(1)}, u32[]{:S(2)}, u32[]{:S(2)}) collective-permute-start(f32[168,128]{1,0:T(8,128)S(1)} %add.46.mine), channel_id=1, source_target_pairs={{0,2},{2,0},{1,3},{3,1},{4,6},{6,4},{5,7},{7,5},{8,10},{10,8},{9,1... | collective-permute-start | bytes 258056 | tf_op jit(solution)/shard_map/ppermute | solution.py:808
  31.8 5.2 %collective-permute-start.10 = (f32[128,128]{1,0:T(8,128)S(1)}, f32[128,128]{1,0:T(8,128)S(1)}, u32[]{:S(2)}, u32[]{:S(2)}) collective-permute-start(f32[128,128]{1,0:T(8,128)S(1)} %get-tuple-element.80), channel_id=1, source_target_pairs={{0,8},{1,9},{2,6},{3,7},{4,12},{5,13},{6,2},{7,3},{8,0},{9,1},{10,... | collective-permute-start | bytes 196616 | tf_op jit(solution)/shard_map/ppermute | solution.py:815
  37.0 7.7 %collective-permute-start.11 = (f32[128,128]{1,0:T(8,128)S(1)}, f32[128,128]{1,0:T(8,128)S(1)}, u32[]{:S(2)}, u32[]{:S(2)}) collective-permute-start(f32[128,128]{1,0:T(8,128)S(1)} %add.50), channel_id=1, source_target_pairs={{0,16},{16,0},{1,17},{17,1},{2,18},{18,2},{3,19},{19,3},{4,20},{20... | collective-permute-start | bytes 196616 | tf_op jit(solution)/shard_map/ppermute | solution.py:808
  44.8 1.3 %collective-permute-start.12 = (f32[128,128]{1,0:T(8,128)S(1)}, f32[128,128]{1,0:T(8,128)S(1)}, u32[]{:S(2)}, u32[]{:S(2)}) collective-permute-start(f32[128,128]{1,0:T(8,128)S(1)} %add.51.mine), channel_id=1, source_target_pairs={{0,2},{2,0},{1,3},{3,1},{4,6},{6,4},{5,7},{7,5},{8,10},{10,8},{9,1... | collective-permute-start | bytes 196616 | tf_op jit(solution)/shard_map/ppermute | solution.py:808

commit v25 on v20

--- a/solution.py
+++ b/solution.py
@@ -49,9 +49,6 @@
     )
 
 
-AHEAD = 5
-
-
 def layer_copies(place, sources, buffers, sems):
     layer = place.layer()
     return [
@@ -185,27 +182,18 @@
 
 def hot_kernel(place, wide_hbm, narrow_hbm, keep, send, wides, narrows, a_flat, b_flat, sems):
     copies = layer_copies(place, (wide_hbm, narrow_hbm), (wides, narrows), sems)
-    order = HOT + COLD
-    for i in order[:AHEAD]:
+    for i in HOT + COLD:
         for copy in copies[i]:
             copy.start()
     clear_others(place, COLD, keep, send)
-
-    def pack(i, sums):
-        put_layer(place, i, sums, a_flat, b_flat, keep, send)
-
-    before = None
-    for at, i in enumerate(order):
-        for copy in copies[i]:
-            copy.wait()
-        if at + AHEAD < len(order):
-            for copy in copies[order[at + AHEAD]]:
-                copy.start()
-        if before is not None:
-            pack(*before)
-            before = None
-        if i in HOT:
-            before = (i, square_sums(wides[i], narrows[i]))
+    for group in (HOT[:3], HOT[3:], COLD):
+        for i in group:
+            for copy in copies[i]:
+                copy.wait()
+        if group is not COLD:
+            for i in group:
+                sums = square_sums(wides[i], narrows[i])
+                put_layer(place, i, sums, a_flat, b_flat, keep, send)
 
 
 def cold_kernel(place, wides, narrows, keep, send, a_flat, b_flat):

time: 56.4 us -> 56 us (level)
  no operation moved by 1% of the time
where the time goes in v25:
time: 56 us; the launch traced here: 55.8 us
  starting transfers between devices  18.6 us (33%)
  Pallas kernels  15 us (27%)
  waiting for transfers between devices  10.5 us (19%)
  blocking collectives  10.3 us (18%)
  between operations  0.86 us (2%)
    ppermute x6, starting transfers between devices, swap_by_core(): return lax.ppermute(value, names, pairs)  10.8 us
    all_to_all x1, blocking collectives, on_device(): got = lax.all_to_all(sent, (place.near, place.second, place.first), 0, 0)  10.3 us
    pallas_call x3, Pallas kernels, sweep_call(): pl.pallas_call(kernel, in_specs=[VMEM] * len(args), out_specs=[VMEM] * le...  8.43 us
    ppermute x7, starting transfers between devices, swap(): return lax.ppermute(value, axis, [(0, 1), (1, 0)])  7.84 us
    ppermute x6, waiting for transfers between devices, swap_by_core(): return lax.ppermute(value, names, pairs)  7.13 us
    ppermute x7, waiting for transfers between devices, swap(): return lax.ppermute(value, axis, [(0, 1), (1, 0)])  3.4 us
    pallas_call x1, Pallas kernels, hot_squares(): pl.pallas_call(functools.partial(hot_kernel, place), in_specs=[HBM, HBM],...  3.22 us
    pallas_call x1, Pallas kernels, mixed_sums(): pl.pallas_call(functools.partial(mixed_kernel, place), in_specs=[SMEM, VM...  1.44 us
  transfers between devices with their start and end apart: 13, of which 7 were waited for; matrix products, arithmetic and copies ran while one was open for 1% of the time, Pallas kernels for 19%

profile of v25, /device:TPU:0, one launch (start us, length us, event | category | flops | bytes accessed | tf_op | source)
XLA Modules:
  0.0 55.8 jit_solution(9614032066652713371)
XLA Ops:
  0.6 3.2 %hot_squares.1 = (f32[8,168,128]{2,1,0:T(8,128)S(1)}, f32[8,168,128]{2,1,0:T(8,128)S(1)}, bf16[8,768,256]{2,1,0:T(8,128)(2,1)S(1)}, bf16[8,768,128]{2,1,0:T(8,128)(2,1)S(1)}) custom-call(bf16[8,768,256]{2,1,0:T(8,128)(2,1)} %wide_hbm.1, bf16[8,768,128]{2,1,0:T(8,128)(2,1)} %narrow_hbm.1), custom_call_target="tpu_custom_call" | custom-call | flops 754974720 | bytes 3145728 | tf_op jit(solution)/shard_map/hot_squares/pallas_call | solution.py:256
  3.9 0.5 collective-permute-start
  4.4 0.6 %cold_squares.1 = (f32[4,168,128]{2,1,0:T(8,128)S(1)}, f32[4,168,128]{2,1,0:T(8,128)S(1)}) custom-call(bf16[8,768,256]{2,1,0:T(8,128)(2,1)S(1)} %get-tuple-element.46.wides, bf16[8,768,128]{2,1,0:T(8,128)(2,1)S(1)} %get-tuple-element.43.narrows), custom_call_target="tpu_custom_call" | custom-call | flops 251658240 | bytes 3145728 | tf_op jit(solution)/shard_map/cold_squares/pallas_call | solution.py:278
  5.0 0.7 %collective-permute-done = f32[4,168,128]{2,1,0:T(8,128)S(1)} collective-permute-done((f32[4,168,128]{2,1,0:T(8,128)S(1)}, f32[4,168,128]{2,1,0:T(8,128)S(1)}, u32[]{:S(2)}, u32[]{:S(2)}) %collective-permute-start) | collective-permute-done | bytes 344096 | tf_op jit(solution)/shard_map/ppermute | solution.py:792
  5.7 2.9 %collective-permute-start.1 = (f32[4,168,128]{2,1,0:T(8,128)S(1)}, f32[4,168,128]{2,1,0:T(8,128)S(1)}, u32[]{:S(2)}, u32[]{:S(2)}) collective-permute-start(f32[4,168,128]{2,1,0:T(8,128)S(1)} %slice_add_fusion.1), channel_id=1, source_target_pairs={{0,1},{1,0},{2,6},{3,7},{4,5},{5,4},{6,2},{7,3},{8,9},{9,8},{10,14... | collective-permute-start | bytes 1032200 | tf_op jit(solution)/shard_map/ppermute | solution.py:799
  8.7 1.4 %mixed.1 = (f32[8,128,128]{2,1,0:T(8,128)S(1)}, f32[8,128,128]{2,1,0:T(8,128)S(1)}, s32[8,8,128]{2,1,0:T(8,128)S(1)}) custom-call(s32[8]{0:T(128)S(1)} %copy-done, bf16[8,768,256]{2,1,0:T(8,128)(2,1)S(1)} %get-tuple-element.46.wides, bf16[8,768,128]{2,1,0:T(8,128)(2,1)S(1)} %get-tuple-element.43.narrows), custom_call_target="tpu_custom_call" | custom-call | flops 402653184 | bytes 3145728 | tf_op jit(solution)/shard_map/mixed/pallas_call | solution.py:293
  10.2 0.6 collective-permute-start.2
  10.8 3.1 %collective-permute-done.1 = f32[4,168,128]{2,1,0:T(8,128)S(1)} collective-permute-done((f32[4,168,128]{2,1,0:T(8,128)S(1)}, f32[4,168,128]{2,1,0:T(8,128)S(1)}, u32[]{:S(2)}, u32[]{:S(2)}) %collective-permute-start.1) | collective-permute-done | bytes 344096 | tf_op jit(solution)/shard_map/ppermute | solution.py:799
  14.0 2.1 %collective-permute-start.3 = (f32[2,168,128]{2,1,0:T(8,128)S(1)}, f32[2,168,128]{2,1,0:T(8,128)S(1)}, u32[]{:S(2)}, u32[]{:S(2)}) collective-permute-start(f32[2,168,128]{2,1,0:T(8,128)S(1)} %slice.57), channel_id=1, source_target_pairs={{0,4},{1,5},{2,10},{3,11},{4,0},{5,1},{6,14},{7,15},{8,12},{9,13},... | collective-permute-start | bytes 516104 | tf_op jit(solution)/shard_map/ppermute | solution.py:799
  16.3 1.6 %collective-permute-start.8 = (f32[4,128,128]{2,1,0:T(8,128)S(1)}, f32[4,128,128]{2,1,0:T(8,128)S(1)}, u32[]{:S(2)}, u32[]{:S(2)}) collective-permute-start(f32[4,128,128]{2,1,0:T(8,128)S(1)} %get-tuple-element.76), channel_id=1, source_target_pairs={{0,1},{1,0},{2,10},{3,11},{4,5},{5,4},{6,14},{7,15},{8,9},{9,8},{1... | collective-permute-start | bytes 786440 | tf_op jit(solution)/shard_map/ppermute | solution.py:799
  17.8 1.7 %collective-permute-done.3 = f32[2,168,128]{2,1,0:T(8,128)S(1)} collective-permute-done((f32[2,168,128]{2,1,0:T(8,128)S(1)}, f32[2,168,128]{2,1,0:T(8,128)S(1)}, u32[]{:S(2)}, u32[]{:S(2)}) %collective-permute-start.3) | collective-permute-done | bytes 172064 | tf_op jit(solution)/shard_map/ppermute | solution.py:799
  19.6 2.1 %collective-permute-start.4 = (f32[168,128]{1,0:T(8,128)S(1)}, f32[168,128]{1,0:T(8,128)S(1)}, u32[]{:S(2)}, u32[]{:S(2)}) collective-permute-start(f32[168,128]{1,0:T(8,128)S(1)} %slice_bitcast_fusion), channel_id=1, source_target_pairs={{0,8},{1,9},{2,3},{3,2},{4,12},{5,13},{6,7},{7,6},{8,0},{9,1},{10,... | collective-permute-start | bytes 258056 | tf_op jit(solution)/shard_map/ppermute | solution.py:799
  21.7 1.9 %collective-permute-done.8 = f32[4,128,128]{2,1,0:T(8,128)S(1)} collective-permute-done((f32[4,128,128]{2,1,0:T(8,128)S(1)}, f32[4,128,128]{2,1,0:T(8,128)S(1)}, u32[]{:S(2)}, u32[]{:S(2)}) %collective-permute-start.8) | collective-permute-done | bytes 262176 | tf_op jit(solution)/shard_map/ppermute | solution.py:799
  23.8 0.4 collective-permute-done.4
  24.2 3.1 %collective-permute-start.5 = (f32[168,128]{1,0:T(8,128)S(1)}, f32[168,128]{1,0:T(8,128)S(1)}, u32[]{:S(2)}, u32[]{:S(2)}) collective-permute-start(f32[168,128]{1,0:T(8,128)S(1)} %fusion), channel_id=1, source_target_pairs={{0,16},{16,0},{1,17},{17,1},{2,18},{18,2},{3,19},{19,3},{4,20},{20... | collective-permute-start | bytes 258056 | tf_op jit(solution)/shard_map/ppermute | solution.py:792
  27.3 2.5 %collective-permute-done.5 = f32[168,128]{1,0:T(8,128)S(1)} collective-permute-done((f32[168,128]{1,0:T(8,128)S(1)}, f32[168,128]{1,0:T(8,128)S(1)}, u32[]{:S(2)}, u32[]{:S(2)}) %collective-permute-start.5) | collective-permute-done | bytes 86048 | tf_op jit(solution)/shard_map/ppermute | solution.py:792
  29.9 2.0 %collective-permute-start.10 = (f32[128,128]{1,0:T(8,128)S(1)}, f32[128,128]{1,0:T(8,128)S(1)}, u32[]{:S(2)}, u32[]{:S(2)}) collective-permute-start(f32[128,128]{1,0:T(8,128)S(1)} %get-tuple-element.80), channel_id=1, source_target_pairs={{0,8},{1,9},{2,6},{3,7},{4,12},{5,13},{6,2},{7,3},{8,0},{9,1},{10,... | collective-permute-start | bytes 196616 | tf_op jit(solution)/shard_map/ppermute | solution.py:799
  31.9 3.2 %first_panels.1 = (f32[288,256]{1,0:T(8,128)S(1)}, bf16[96,256]{1,0:T(8,128)(2,1)S(1)}, bf16[96,256]{1,0:T(8,128)(2,1)S(1)}, f32[16,256]{1,0:T(8,128)S(1)}, f32[...) custom-call(f32[168,128]{1,0:T(8,128)S(1)} %add.46.mine, ...), custom_call_target="tpu_custom_call" | custom-call | flops 1073741824 | bytes 1048576 | tf_op jit(solution)/shard_map/first_panels/pallas_call | solution.py:644
  35.1 3.4 %collective-permute-start.11 = (f32[128,128]{1,0:T(8,128)S(1)}, f32[128,128]{1,0:T(8,128)S(1)}, u32[]{:S(2)}, u32[]{:S(2)}) collective-permute-start(f32[128,128]{1,0:T(8,128)S(1)} %add.50), channel_id=1, source_target_pairs={{0,16},{16,0},{1,17},{17,1},{2,18},{18,2},{3,19},{19,3},{4,20},{20... | collective-permute-start | bytes 196616 | tf_op jit(solution)/shard_map/ppermute | solution.py:792
  38.6 4.2 %second_panels.1 = (f32[128,128]{1,0:T(8,128)S(1)}, f32[288,256]{1,0:T(8,128)S(1)}, bf16[96,256]{1,0:T(8,128)(2,1)S(1)}, bf16[96,256]{1,0:T(8,128)(2,1)S(1)}, f32[16,256]{1,0:T(8,128)S(1)}) custom-call(f32[288,256]{1,0:T(8,128)S(1)} %get-tuple-element.53.refs_0_, bf16[96,256]{1,0:T(8,128)(2,1)S(1)} %get-tuple-element.54.refs_1_, ...), custom_call_target="tpu_custom_call" | custom-call | flops 1073741824 | bytes 1048576 | tf_op jit(solution)/shard_map/second_panels/pallas_call | solution.py:644
  42.9 1.0 %third_panels.1.winv = f32[256,256]{1,0:T(8,128)S(1)} custom-call(f32[288,256]{1,0:T(8,128)S(1)} %get-tuple-element.62.wa_in, bf16[96,256]{1,0:T(8,128)(2,1)S(1)} %get-tuple-element.63.wl_in, bf16[96,256]{1,0:T(8,128)(2,1)S(1)} %get-tuple-element.64.wr_in, f32[16,256]{1,0:T(8,128)S(1)} %get-tuple-element.65.panel_in, f32[8,256]{1,0:T(8,128)S(1)} %get-tuple-element.66.scale), custom_call_target="tpu_custom_call" | custom-call | flops 1073741824 | bytes 1048576 | tf_op jit(solution)/shard_map/third_panels/pallas_call | solution.py:644
  44.2 0.6 %products.1 = f32[8,40,128]{2,1,0:T(8,128)S(1)} custom-call(f32[256,256]{1,0:T(8,128)S(1)} %third_panels.1.winv, f32[128,128]{1,0:T(8,128)S(1)} %get-tuple-element.67.ninv_ref, f32[128,128]{1,0:T(8,128)S(1)} %add.51.mine, f32[128,128]{1,0:T(8,128)S(1)} %collective-permute-done.12.other), custom_call_target="tpu_custom_call" | custom-call | tf_op jit(solution)/shard_map/products/pallas_call | solution.py:735
  44.8 10.3 %all_to_all.5.got_ref = f32[8,40,128]{2,1,0:T(8,128)S(1)} all-to-all(f32[8,40,128]{2,1,0:T(8,128)S(1)} %products.1), channel_id=1, replica_groups=mesh['dp0'=2,'dp1'=2,'dp2'=2,'dp3'=2,'own0'=2] {'dp1','dp2','own0'}, dimensions={0} | all-to-all | bytes 327680 | tf_op jit(solution)/shard_map/all_to_all | solution.py:855
  55.1 0.7 %placing.1 = (f32[5,16,256]{2,1,0:T(8,128)}, f32[8,16,64]{2,1,0:T(8,128)}) custom-call(s32[8,8,128]{2,1,0:T(8,128)S(1)} %get-tuple-element.47.slots_ref, f32[8,40,128]{2,1,0:T(8,128)S(1)} %all_to_all.5.got_ref), custom_call_target="tpu_custom_call" | custom-call | tf_op jit(solution)/shard_map/placing/pallas_call | solution.py:778
  (31 shorter events, 1.0 us)
Async XLA Ops:
  3.9 4.8 %copy-start = (s32[8]{0:T(128)S(1)}, s32[8]{0:T(128)}, u32[]{:S(2)}) copy-start(s32[8]{0:T(128)} %owner_map.1) | copy-start | bytes 100
  3.9 1.8 %collective-permute-start = (f32[4,168,128]{2,1,0:T(8,128)S(1)}, f32[4,168,128]{2,1,0:T(8,128)S(1)}, u32[]{:S(2)}, u32[]{:S(2)}) collective-permute-start(f32[4,168,128]{2,1,0:T(8,128)S(1)} %slice.42), channel_id=1, source_target_pairs={{0,2},{2,0},{1,3},{3,1},{4,6},{6,4},{5,7},{7,5},{8,10},{10,8},{9,1... | collective-permute-start | bytes 1032200 | tf_op jit(solution)/shard_map/ppermute | solution.py:792
  5.7 8.1 %collective-permute-start.1 = (f32[4,168,128]{2,1,0:T(8,128)S(1)}, f32[4,168,128]{2,1,0:T(8,128)S(1)}, u32[]{:S(2)}, u32[]{:S(2)}) collective-permute-start(f32[4,168,128]{2,1,0:T(8,128)S(1)} %slice_add_fusion.1), channel_id=1, source_target_pairs={{0,1},{1,0},{2,6},{3,7},{4,5},{5,4},{6,2},{7,3},{8,9},{9,8},{10,14... | collective-permute-start | bytes 1032200 | tf_op jit(solution)/shard_map/ppermute | solution.py:799
  10.1 6.0 %collective-permute-start.7 = (f32[8,128,128]{2,1,0:T(8,128)S(1)}, f32[8,128,128]{2,1,0:T(8,128)S(1)}, u32[]{:S(2)}, u32[]{:S(2)}) collective-permute-start(f32[8,128,128]{2,1,0:T(8,128)S(1)} %get-tuple-element.50), channel_id=1, source_target_pairs={{0,2},{2,0},{1,3},{3,1},{4,6},{6,4},{5,7},{7,5},{8,10},{10,8},{9,1... | collective-permute-start | bytes 1572872 | tf_op jit(solution)/shard_map/ppermute | solution.py:792
  10.2 3.7 %collective-permute-start.2 = (f32[4,168,128]{2,1,0:T(8,128)S(1)}, f32[4,168,128]{2,1,0:T(8,128)S(1)}, u32[]{:S(2)}, u32[]{:S(2)}) collective-permute-start(f32[4,168,128]{2,1,0:T(8,128)S(1)} %slice_add_fusion), channel_id=1, source_target_pairs={{0,2},{2,0},{1,3},{3,1},{4,6},{6,4},{5,7},{7,5},{8,10},{10,8},{9,1... | collective-permute-start | bytes 1032200 | tf_op jit(solution)/shard_map/ppermute | solution.py:792
  14.0 5.5 %collective-permute-start.3 = (f32[2,168,128]{2,1,0:T(8,128)S(1)}, f32[2,168,128]{2,1,0:T(8,128)S(1)}, u32[]{:S(2)}, u32[]{:S(2)}) collective-permute-start(f32[2,168,128]{2,1,0:T(8,128)S(1)} %slice.57), channel_id=1, source_target_pairs={{0,4},{1,5},{2,10},{3,11},{4,0},{5,1},{6,14},{7,15},{8,12},{9,13},... | collective-permute-start | bytes 516104 | tf_op jit(solution)/shard_map/ppermute | solution.py:799
  16.3 7.4 %collective-permute-start.8 = (f32[4,128,128]{2,1,0:T(8,128)S(1)}, f32[4,128,128]{2,1,0:T(8,128)S(1)}, u32[]{:S(2)}, u32[]{:S(2)}) collective-permute-start(f32[4,128,128]{2,1,0:T(8,128)S(1)} %get-tuple-element.76), channel_id=1, source_target_pairs={{0,1},{1,0},{2,10},{3,11},{4,5},{5,4},{6,14},{7,15},{8,9},{9,8},{1... | collective-permute-start | bytes 786440 | tf_op jit(solution)/shard_map/ppermute | solution.py:799
  19.6 4.6 %collective-permute-start.4 = (f32[168,128]{1,0:T(8,128)S(1)}, f32[168,128]{1,0:T(8,128)S(1)}, u32[]{:S(2)}, u32[]{:S(2)}) collective-permute-start(f32[168,128]{1,0:T(8,128)S(1)} %slice_bitcast_fusion), channel_id=1, source_target_pairs={{0,8},{1,9},{2,3},{3,2},{4,12},{5,13},{6,7},{7,6},{8,0},{9,1},{10,... | collective-permute-start | bytes 258056 | tf_op jit(solution)/shard_map/ppermute | solution.py:799
  23.7 6.2 %collective-permute-start.9 = (f32[2,128,128]{2,1,0:T(8,128)S(1)}, f32[2,128,128]{2,1,0:T(8,128)S(1)}, u32[]{:S(2)}, u32[]{:S(2)}) collective-permute-start(f32[2,128,128]{2,1,0:T(8,128)S(1)} %get-tuple-element.78), channel_id=1, source_target_pairs={{0,4},{1,5},{2,3},{3,2},{4,0},{5,1},{6,7},{7,6},{8,12},{9,13},{10,... | collective-permute-start | bytes 393224 | tf_op jit(solution)/shard_map/ppermute | solution.py:799
  24.2 5.6 %collective-permute-start.5 = (f32[168,128]{1,0:T(8,128)S(1)}, f32[168,128]{1,0:T(8,128)S(1)}, u32[]{:S(2)}, u32[]{:S(2)}) collective-permute-start(f32[168,128]{1,0:T(8,128)S(1)} %fusion), channel_id=1, source_target_pairs={{0,16},{16,0},{1,17},{17,1},{2,18},{18,2},{3,19},{19,3},{4,20},{20... | collective-permute-start | bytes 258056 | tf_op jit(solution)/shard_map/ppermute | solution.py:792
  29.8 2.1 %collective-permute-start.6 = (f32[168,128]{1,0:T(8,128)S(1)}, f32[168,128]{1,0:T(8,128)S(1)}, u32[]{:S(2)}, u32[]{:S(2)}) collective-permute-start(f32[168,128]{1,0:T(8,128)S(1)} %add.46.mine), channel_id=1, source_target_pairs={{0,2},{2,0},{1,3},{3,1},{4,6},{6,4},{5,7},{7,5},{8,10},{10,8},{9,1... | collective-permute-start | bytes 258056 | tf_op jit(solution)/shard_map/ppermute | solution.py:792
  29.9 5.2 %collective-permute-start.10 = (f32[128,128]{1,0:T(8,128)S(1)}, f32[128,128]{1,0:T(8,128)S(1)}, u32[]{:S(2)}, u32[]{:S(2)}) collective-permute-start(f32[128,128]{1,0:T(8,128)S(1)} %get-tuple-element.80), channel_id=1, source_target_pairs={{0,8},{1,9},{2,6},{3,7},{4,12},{5,13},{6,2},{7,3},{8,0},{9,1},{10,... | collective-permute-start | bytes 196616 | tf_op jit(solution)/shard_map/ppermute | solution.py:799
  35.1 7.7 %collective-permute-start.11 = (f32[128,128]{1,0:T(8,128)S(1)}, f32[128,128]{1,0:T(8,128)S(1)}, u32[]{:S(2)}, u32[]{:S(2)}) collective-permute-start(f32[128,128]{1,0:T(8,128)S(1)} %add.50), channel_id=1, source_target_pairs={{0,16},{16,0},{1,17},{17,1},{2,18},{18,2},{3,19},{19,3},{4,20},{20... | collective-permute-start | bytes 196616 | tf_op jit(solution)/shard_map/ppermute | solution.py:792
  42.8 1.3 %collective-permute-start.12 = (f32[128,128]{1,0:T(8,128)S(1)}, f32[128,128]{1,0:T(8,128)S(1)}, u32[]{:S(2)}, u32[]{:S(2)}) collective-permute-start(f32[128,128]{1,0:T(8,128)S(1)} %add.51.mine), channel_id=1, source_target_pairs={{0,2},{2,0},{1,3},{3,1},{4,6},{6,4},{5,7},{7,5},{8,10},{10,8},{9,1... | collective-permute-start | bytes 196616 | tf_op jit(solution)/shard_map/ppermute | solution.py:792

commit v26 on v25

--- a/solution.py
+++ b/solution.py
@@ -531,7 +531,7 @@
 
 
 STEPS = LANES // BLOCK
-FIRST_STEPS = 5
+FIRST_STEPS = 6
 SECOND_STEPS = 6
 
 

time: 56 us -> 56 us (level)
  no operation moved by 1% of the time
where the time goes in v26:
time: 56 us; the launch traced here: 55.8 us
  starting transfers between devices  18.6 us (33%)
  Pallas kernels  15 us (27%)
  waiting for transfers between devices  10.5 us (19%)
  blocking collectives  10.3 us (18%)
  between operations  0.86 us (2%)
    ppermute x6, starting transfers between devices, swap_by_core(): return lax.ppermute(value, names, pairs)  10.8 us
    all_to_all x1, blocking collectives, on_device(): got = lax.all_to_all(sent, (place.near, place.second, place.first), 0, 0)  10.3 us
    pallas_call x3, Pallas kernels, sweep_call(): pl.pallas_call(kernel, in_specs=[VMEM] * len(args), out_specs=[VMEM] * le...  8.43 us
    ppermute x7, starting transfers between devices, swap(): return lax.ppermute(value, axis, [(0, 1), (1, 0)])  7.84 us
    ppermute x6, waiting for transfers between devices, swap_by_core(): return lax.ppermute(value, names, pairs)  7.13 us
    ppermute x7, waiting for transfers between devices, swap(): return lax.ppermute(value, axis, [(0, 1), (1, 0)])  3.4 us
    pallas_call x1, Pallas kernels, hot_squares(): pl.pallas_call(functools.partial(hot_kernel, place), in_specs=[HBM, HBM],...  3.22 us
    pallas_call x1, Pallas kernels, mixed_sums(): pl.pallas_call(functools.partial(mixed_kernel, place), in_specs=[SMEM, VM...  1.44 us
  transfers between devices with their start and end apart: 13, of which 7 were waited for; matrix products, arithmetic and copies ran while one was open for 1% of the time, Pallas kernels for 19%

profile of v26, /device:TPU:0, one launch (start us, length us, event | category | flops | bytes accessed | tf_op | source)
XLA Modules:
  0.0 55.8 jit_solution(5943375475214092422)
XLA Ops:
  0.6 3.2 %hot_squares.1 = (f32[8,168,128]{2,1,0:T(8,128)S(1)}, f32[8,168,128]{2,1,0:T(8,128)S(1)}, bf16[8,768,256]{2,1,0:T(8,128)(2,1)S(1)}, bf16[8,768,128]{2,1,0:T(8,128)(2,1)S(1)}) custom-call(bf16[8,768,256]{2,1,0:T(8,128)(2,1)} %wide_hbm.1, bf16[8,768,128]{2,1,0:T(8,128)(2,1)} %narrow_hbm.1), custom_call_target="tpu_custom_call" | custom-call | flops 754974720 | bytes 3145728 | tf_op jit(solution)/shard_map/hot_squares/pallas_call | solution.py:256
  3.9 0.5 collective-permute-start
  4.4 0.6 %cold_squares.1 = (f32[4,168,128]{2,1,0:T(8,128)S(1)}, f32[4,168,128]{2,1,0:T(8,128)S(1)}) custom-call(bf16[8,768,256]{2,1,0:T(8,128)(2,1)S(1)} %get-tuple-element.46.wides, bf16[8,768,128]{2,1,0:T(8,128)(2,1)S(1)} %get-tuple-element.43.narrows), custom_call_target="tpu_custom_call" | custom-call | flops 251658240 | bytes 3145728 | tf_op jit(solution)/shard_map/cold_squares/pallas_call | solution.py:278
  5.0 0.7 %collective-permute-done = f32[4,168,128]{2,1,0:T(8,128)S(1)} collective-permute-done((f32[4,168,128]{2,1,0:T(8,128)S(1)}, f32[4,168,128]{2,1,0:T(8,128)S(1)}, u32[]{:S(2)}, u32[]{:S(2)}) %collective-permute-start) | collective-permute-done | bytes 344096 | tf_op jit(solution)/shard_map/ppermute | solution.py:792
  5.7 2.9 %collective-permute-start.1 = (f32[4,168,128]{2,1,0:T(8,128)S(1)}, f32[4,168,128]{2,1,0:T(8,128)S(1)}, u32[]{:S(2)}, u32[]{:S(2)}) collective-permute-start(f32[4,168,128]{2,1,0:T(8,128)S(1)} %slice_add_fusion.1), channel_id=1, source_target_pairs={{0,1},{1,0},{2,6},{3,7},{4,5},{5,4},{6,2},{7,3},{8,9},{9,8},{10,14... | collective-permute-start | bytes 1032200 | tf_op jit(solution)/shard_map/ppermute | solution.py:799
  8.7 1.4 %mixed.1 = (f32[8,128,128]{2,1,0:T(8,128)S(1)}, f32[8,128,128]{2,1,0:T(8,128)S(1)}, s32[8,8,128]{2,1,0:T(8,128)S(1)}) custom-call(s32[8]{0:T(128)S(1)} %copy-done, bf16[8,768,256]{2,1,0:T(8,128)(2,1)S(1)} %get-tuple-element.46.wides, bf16[8,768,128]{2,1,0:T(8,128)(2,1)S(1)} %get-tuple-element.43.narrows), custom_call_target="tpu_custom_call" | custom-call | flops 402653184 | bytes 3145728 | tf_op jit(solution)/shard_map/mixed/pallas_call | solution.py:293
  10.2 0.6 collective-permute-start.2
  10.8 3.1 %collective-permute-done.1 = f32[4,168,128]{2,1,0:T(8,128)S(1)} collective-permute-done((f32[4,168,128]{2,1,0:T(8,128)S(1)}, f32[4,168,128]{2,1,0:T(8,128)S(1)}, u32[]{:S(2)}, u32[]{:S(2)}) %collective-permute-start.1) | collective-permute-done | bytes 344096 | tf_op jit(solution)/shard_map/ppermute | solution.py:799
  14.0 2.1 %collective-permute-start.3 = (f32[2,168,128]{2,1,0:T(8,128)S(1)}, f32[2,168,128]{2,1,0:T(8,128)S(1)}, u32[]{:S(2)}, u32[]{:S(2)}) collective-permute-start(f32[2,168,128]{2,1,0:T(8,128)S(1)} %slice.57), channel_id=1, source_target_pairs={{0,4},{1,5},{2,10},{3,11},{4,0},{5,1},{6,14},{7,15},{8,12},{9,13},... | collective-permute-start | bytes 516104 | tf_op jit(solution)/shard_map/ppermute | solution.py:799
  16.3 1.6 %collective-permute-start.8 = (f32[4,128,128]{2,1,0:T(8,128)S(1)}, f32[4,128,128]{2,1,0:T(8,128)S(1)}, u32[]{:S(2)}, u32[]{:S(2)}) collective-permute-start(f32[4,128,128]{2,1,0:T(8,128)S(1)} %get-tuple-element.76), channel_id=1, source_target_pairs={{0,1},{1,0},{2,10},{3,11},{4,5},{5,4},{6,14},{7,15},{8,9},{9,8},{1... | collective-permute-start | bytes 786440 | tf_op jit(solution)/shard_map/ppermute | solution.py:799
  17.8 1.7 %collective-permute-done.3 = f32[2,168,128]{2,1,0:T(8,128)S(1)} collective-permute-done((f32[2,168,128]{2,1,0:T(8,128)S(1)}, f32[2,168,128]{2,1,0:T(8,128)S(1)}, u32[]{:S(2)}, u32[]{:S(2)}) %collective-permute-start.3) | collective-permute-done | bytes 172064 | tf_op jit(solution)/shard_map/ppermute | solution.py:799
  19.6 2.1 %collective-permute-start.4 = (f32[168,128]{1,0:T(8,128)S(1)}, f32[168,128]{1,0:T(8,128)S(1)}, u32[]{:S(2)}, u32[]{:S(2)}) collective-permute-start(f32[168,128]{1,0:T(8,128)S(1)} %slice_bitcast_fusion), channel_id=1, source_target_pairs={{0,8},{1,9},{2,3},{3,2},{4,12},{5,13},{6,7},{7,6},{8,0},{9,1},{10,... | collective-permute-start | bytes 258056 | tf_op jit(solution)/shard_map/ppermute | solution.py:799
  21.7 1.9 %collective-permute-done.8 = f32[4,128,128]{2,1,0:T(8,128)S(1)} collective-permute-done((f32[4,128,128]{2,1,0:T(8,128)S(1)}, f32[4,128,128]{2,1,0:T(8,128)S(1)}, u32[]{:S(2)}, u32[]{:S(2)}) %collective-permute-start.8) | collective-permute-done | bytes 262176 | tf_op jit(solution)/shard_map/ppermute | solution.py:799
  23.8 0.4 collective-permute-done.4
  24.2 3.1 %collective-permute-start.5 = (f32[168,128]{1,0:T(8,128)S(1)}, f32[168,128]{1,0:T(8,128)S(1)}, u32[]{:S(2)}, u32[]{:S(2)}) collective-permute-start(f32[168,128]{1,0:T(8,128)S(1)} %fusion), channel_id=1, source_target_pairs={{0,16},{16,0},{1,17},{17,1},{2,18},{18,2},{3,19},{19,3},{4,20},{20... | collective-permute-start | bytes 258056 | tf_op jit(solution)/shard_map/ppermute | solution.py:792
  27.3 2.5 %collective-permute-done.5 = f32[168,128]{1,0:T(8,128)S(1)} collective-permute-done((f32[168,128]{1,0:T(8,128)S(1)}, f32[168,128]{1,0:T(8,128)S(1)}, u32[]{:S(2)}, u32[]{:S(2)}) %collective-permute-start.5) | collective-permute-done | bytes 86048 | tf_op jit(solution)/shard_map/ppermute | solution.py:792
  29.9 2.0 %collective-permute-start.10 = (f32[128,128]{1,0:T(8,128)S(1)}, f32[128,128]{1,0:T(8,128)S(1)}, u32[]{:S(2)}, u32[]{:S(2)}) collective-permute-start(f32[128,128]{1,0:T(8,128)S(1)} %get-tuple-element.80), channel_id=1, source_target_pairs={{0,8},{1,9},{2,6},{3,7},{4,12},{5,13},{6,2},{7,3},{8,0},{9,1},{10,... | collective-permute-start | bytes 196616 | tf_op jit(solution)/shard_map/ppermute | solution.py:799
  31.9 3.8 %first_panels.1 = (f32[288,256]{1,0:T(8,128)S(1)}, bf16[96,256]{1,0:T(8,128)(2,1)S(1)}, bf16[96,256]{1,0:T(8,128)(2,1)S(1)}, f32[16,256]{1,0:T(8,128)S(1)}, f32[...) custom-call(f32[168,128]{1,0:T(8,128)S(1)} %add.46.mine, ...), custom_call_target="tpu_custom_call" | custom-call | flops 1073741824 | bytes 1048576 | tf_op jit(solution)/shard_map/first_panels/pallas_call | solution.py:644
  35.7 3.4 %collective-permute-start.11 = (f32[128,128]{1,0:T(8,128)S(1)}, f32[128,128]{1,0:T(8,128)S(1)}, u32[]{:S(2)}, u32[]{:S(2)}) collective-permute-start(f32[128,128]{1,0:T(8,128)S(1)} %add.50), channel_id=1, source_target_pairs={{0,16},{16,0},{1,17},{17,1},{2,18},{18,2},{3,19},{19,3},{4,20},{20... | collective-permute-start | bytes 196616 | tf_op jit(solution)/shard_map/ppermute | solution.py:792
  39.1 3.7 %second_panels.1 = (f32[128,128]{1,0:T(8,128)S(1)}, f32[288,256]{1,0:T(8,128)S(1)}, bf16[96,256]{1,0:T(8,128)(2,1)S(1)}, bf16[96,256]{1,0:T(8,128)(2,1)S(1)}, f32[16,256]{1,0:T(8,128)S(1)}) custom-call(f32[288,256]{1,0:T(8,128)S(1)} %get-tuple-element.53.refs_0_, bf16[96,256]{1,0:T(8,128)(2,1)S(1)} %get-tuple-element.54.refs_1_, ...), custom_call_target="tpu_custom_call" | custom-call | flops 1073741824 | bytes 1048576 | tf_op jit(solution)/shard_map/second_panels/pallas_call | solution.py:644
  42.9 1.0 %third_panels.1.winv = f32[256,256]{1,0:T(8,128)S(1)} custom-call(f32[288,256]{1,0:T(8,128)S(1)} %get-tuple-element.62.wa_in, bf16[96,256]{1,0:T(8,128)(2,1)S(1)} %get-tuple-element.63.wl_in, bf16[96,256]{1,0:T(8,128)(2,1)S(1)} %get-tuple-element.64.wr_in, f32[16,256]{1,0:T(8,128)S(1)} %get-tuple-element.65.panel_in, f32[8,256]{1,0:T(8,128)S(1)} %get-tuple-element.66.scale), custom_call_target="tpu_custom_call" | custom-call | flops 1073741824 | bytes 1048576 | tf_op jit(solution)/shard_map/third_panels/pallas_call | solution.py:644
  44.2 0.6 %products.1 = f32[8,40,128]{2,1,0:T(8,128)S(1)} custom-call(f32[256,256]{1,0:T(8,128)S(1)} %third_panels.1.winv, f32[128,128]{1,0:T(8,128)S(1)} %get-tuple-element.67.ninv_ref, f32[128,128]{1,0:T(8,128)S(1)} %add.51.mine, f32[128,128]{1,0:T(8,128)S(1)} %collective-permute-done.12.other), custom_call_target="tpu_custom_call" | custom-call | tf_op jit(solution)/shard_map/products/pallas_call | solution.py:735
  44.8 10.3 %all_to_all.5.got_ref = f32[8,40,128]{2,1,0:T(8,128)S(1)} all-to-all(f32[8,40,128]{2,1,0:T(8,128)S(1)} %products.1), channel_id=1, replica_groups=mesh['dp0'=2,'dp1'=2,'dp2'=2,'dp3'=2,'own0'=2] {'dp1','dp2','own0'}, dimensions={0} | all-to-all | bytes 327680 | tf_op jit(solution)/shard_map/all_to_all | solution.py:855
  55.1 0.7 %placing.1 = (f32[5,16,256]{2,1,0:T(8,128)}, f32[8,16,64]{2,1,0:T(8,128)}) custom-call(s32[8,8,128]{2,1,0:T(8,128)S(1)} %get-tuple-element.47.slots_ref, f32[8,40,128]{2,1,0:T(8,128)S(1)} %all_to_all.5.got_ref), custom_call_target="tpu_custom_call" | custom-call | tf_op jit(solution)/shard_map/placing/pallas_call | solution.py:778
  (31 shorter events, 1.0 us)
Async XLA Ops:
  3.9 4.8 %copy-start = (s32[8]{0:T(128)S(1)}, s32[8]{0:T(128)}, u32[]{:S(2)}) copy-start(s32[8]{0:T(128)} %owner_map.1) | copy-start | bytes 100
  3.9 1.8 %collective-permute-start = (f32[4,168,128]{2,1,0:T(8,128)S(1)}, f32[4,168,128]{2,1,0:T(8,128)S(1)}, u32[]{:S(2)}, u32[]{:S(2)}) collective-permute-start(f32[4,168,128]{2,1,0:T(8,128)S(1)} %slice.42), channel_id=1, source_target_pairs={{0,2},{2,0},{1,3},{3,1},{4,6},{6,4},{5,7},{7,5},{8,10},{10,8},{9,1... | collective-permute-start | bytes 1032200 | tf_op jit(solution)/shard_map/ppermute | solution.py:792
  5.7 8.1 %collective-permute-start.1 = (f32[4,168,128]{2,1,0:T(8,128)S(1)}, f32[4,168,128]{2,1,0:T(8,128)S(1)}, u32[]{:S(2)}, u32[]{:S(2)}) collective-permute-start(f32[4,168,128]{2,1,0:T(8,128)S(1)} %slice_add_fusion.1), channel_id=1, source_target_pairs={{0,1},{1,0},{2,6},{3,7},{4,5},{5,4},{6,2},{7,3},{8,9},{9,8},{10,14... | collective-permute-start | bytes 1032200 | tf_op jit(solution)/shard_map/ppermute | solution.py:799
  10.1 6.0 %collective-permute-start.7 = (f32[8,128,128]{2,1,0:T(8,128)S(1)}, f32[8,128,128]{2,1,0:T(8,128)S(1)}, u32[]{:S(2)}, u32[]{:S(2)}) collective-permute-start(f32[8,128,128]{2,1,0:T(8,128)S(1)} %get-tuple-element.50), channel_id=1, source_target_pairs={{0,2},{2,0},{1,3},{3,1},{4,6},{6,4},{5,7},{7,5},{8,10},{10,8},{9,1... | collective-permute-start | bytes 1572872 | tf_op jit(solution)/shard_map/ppermute | solution.py:792
  10.2 3.7 %collective-permute-start.2 = (f32[4,168,128]{2,1,0:T(8,128)S(1)}, f32[4,168,128]{2,1,0:T(8,128)S(1)}, u32[]{:S(2)}, u32[]{:S(2)}) collective-permute-start(f32[4,168,128]{2,1,0:T(8,128)S(1)} %slice_add_fusion), channel_id=1, source_target_pairs={{0,2},{2,0},{1,3},{3,1},{4,6},{6,4},{5,7},{7,5},{8,10},{10,8},{9,1... | collective-permute-start | bytes 1032200 | tf_op jit(solution)/shard_map/ppermute | solution.py:792
  14.0 5.5 %collective-permute-start.3 = (f32[2,168,128]{2,1,0:T(8,128)S(1)}, f32[2,168,128]{2,1,0:T(8,128)S(1)}, u32[]{:S(2)}, u32[]{:S(2)}) collective-permute-start(f32[2,168,128]{2,1,0:T(8,128)S(1)} %slice.57), channel_id=1, source_target_pairs={{0,4},{1,5},{2,10},{3,11},{4,0},{5,1},{6,14},{7,15},{8,12},{9,13},... | collective-permute-start | bytes 516104 | tf_op jit(solution)/shard_map/ppermute | solution.py:799
  16.3 7.4 %collective-permute-start.8 = (f32[4,128,128]{2,1,0:T(8,128)S(1)}, f32[4,128,128]{2,1,0:T(8,128)S(1)}, u32[]{:S(2)}, u32[]{:S(2)}) collective-permute-start(f32[4,128,128]{2,1,0:T(8,128)S(1)} %get-tuple-element.76), channel_id=1, source_target_pairs={{0,1},{1,0},{2,10},{3,11},{4,5},{5,4},{6,14},{7,15},{8,9},{9,8},{1... | collective-permute-start | bytes 786440 | tf_op jit(solution)/shard_map/ppermute | solution.py:799
  19.6 4.6 %collective-permute-start.4 = (f32[168,128]{1,0:T(8,128)S(1)}, f32[168,128]{1,0:T(8,128)S(1)}, u32[]{:S(2)}, u32[]{:S(2)}) collective-permute-start(f32[168,128]{1,0:T(8,128)S(1)} %slice_bitcast_fusion), channel_id=1, source_target_pairs={{0,8},{1,9},{2,3},{3,2},{4,12},{5,13},{6,7},{7,6},{8,0},{9,1},{10,... | collective-permute-start | bytes 258056 | tf_op jit(solution)/shard_map/ppermute | solution.py:799
  23.7 6.2 %collective-permute-start.9 = (f32[2,128,128]{2,1,0:T(8,128)S(1)}, f32[2,128,128]{2,1,0:T(8,128)S(1)}, u32[]{:S(2)}, u32[]{:S(2)}) collective-permute-start(f32[2,128,128]{2,1,0:T(8,128)S(1)} %get-tuple-element.78), channel_id=1, source_target_pairs={{0,4},{1,5},{2,3},{3,2},{4,0},{5,1},{6,7},{7,6},{8,12},{9,13},{10,... | collective-permute-start | bytes 393224 | tf_op jit(solution)/shard_map/ppermute | solution.py:799
  24.2 5.6 %collective-permute-start.5 = (f32[168,128]{1,0:T(8,128)S(1)}, f32[168,128]{1,0:T(8,128)S(1)}, u32[]{:S(2)}, u32[]{:S(2)}) collective-permute-start(f32[168,128]{1,0:T(8,128)S(1)} %fusion), channel_id=1, source_target_pairs={{0,16},{16,0},{1,17},{17,1},{2,18},{18,2},{3,19},{19,3},{4,20},{20... | collective-permute-start | bytes 258056 | tf_op jit(solution)/shard_map/ppermute | solution.py:792
  29.8 2.1 %collective-permute-start.6 = (f32[168,128]{1,0:T(8,128)S(1)}, f32[168,128]{1,0:T(8,128)S(1)}, u32[]{:S(2)}, u32[]{:S(2)}) collective-permute-start(f32[168,128]{1,0:T(8,128)S(1)} %add.46.mine), channel_id=1, source_target_pairs={{0,2},{2,0},{1,3},{3,1},{4,6},{6,4},{5,7},{7,5},{8,10},{10,8},{9,1... | collective-permute-start | bytes 258056 | tf_op jit(solution)/shard_map/ppermute | solution.py:792
  29.9 5.8 %collective-permute-start.10 = (f32[128,128]{1,0:T(8,128)S(1)}, f32[128,128]{1,0:T(8,128)S(1)}, u32[]{:S(2)}, u32[]{:S(2)}) collective-permute-start(f32[128,128]{1,0:T(8,128)S(1)} %get-tuple-element.80), channel_id=1, source_target_pairs={{0,8},{1,9},{2,6},{3,7},{4,12},{5,13},{6,2},{7,3},{8,0},{9,1},{10,... | collective-permute-start | bytes 196616 | tf_op jit(solution)/shard_map/ppermute | solution.py:799
  35.7 7.1 %collective-permute-start.11 = (f32[128,128]{1,0:T(8,128)S(1)}, f32[128,128]{1,0:T(8,128)S(1)}, u32[]{:S(2)}, u32[]{:S(2)}) collective-permute-start(f32[128,128]{1,0:T(8,128)S(1)} %add.50), channel_id=1, source_target_pairs={{0,16},{16,0},{1,17},{17,1},{2,18},{18,2},{3,19},{19,3},{4,20},{20... | collective-permute-start | bytes 196616 | tf_op jit(solution)/shard_map/ppermute | solution.py:792
  42.8 1.3 %collective-permute-start.12 = (f32[128,128]{1,0:T(8,128)S(1)}, f32[128,128]{1,0:T(8,128)S(1)}, u32[]{:S(2)}, u32[]{:S(2)}) collective-permute-start(f32[128,128]{1,0:T(8,128)S(1)} %add.51.mine), channel_id=1, source_target_pairs={{0,2},{2,0},{1,3},{3,1},{4,6},{6,4},{5,7},{7,5},{8,10},{10,8},{9,1... | collective-permute-start | bytes 196616 | tf_op jit(solution)/shard_map/ppermute | solution.py:792

commit v27 on v26

--- a/solution.py
+++ b/solution.py
@@ -186,7 +186,7 @@
         for copy in copies[i]:
             copy.start()
     clear_others(place, COLD, keep, send)
-    for group in (HOT[:3], HOT[3:], COLD):
+    for group in (HOT[:2], HOT[2:], COLD):
         for i in group:
             for copy in copies[i]:
                 copy.wait()

time: 56 us -> 55.8 us (level)
  no operation moved by 1% of the time
where the time goes in v27:
time: 55.8 us; the launch traced here: 55.7 us
  starting transfers between devices  18.6 us (33%)
  Pallas kernels  14.9 us (27%)
  waiting for transfers between devices  10.5 us (19%)
  blocking collectives  10.3 us (18%)
  between operations  0.86 us (2%)
    ppermute x6, starting transfers between devices, swap_by_core(): return lax.ppermute(value, names, pairs)  10.8 us
    all_to_all x1, blocking collectives, on_device(): got = lax.all_to_all(sent, (place.near, place.second, place.first), 0, 0)  10.3 us
    pallas_call x3, Pallas kernels, sweep_call(): pl.pallas_call(kernel, in_specs=[VMEM] * len(args), out_specs=[VMEM] * le...  8.43 us
    ppermute x7, starting transfers between devices, swap(): return lax.ppermute(value, axis, [(0, 1), (1, 0)])  7.84 us
    ppermute x6, waiting for transfers between devices, swap_by_core(): return lax.ppermute(value, names, pairs)  7.13 us
    ppermute x7, waiting for transfers between devices, swap(): return lax.ppermute(value, axis, [(0, 1), (1, 0)])  3.4 us
    pallas_call x1, Pallas kernels, hot_squares(): pl.pallas_call(functools.partial(hot_kernel, place), in_specs=[HBM, HBM],...  3.08 us
    pallas_call x1, Pallas kernels, mixed_sums(): pl.pallas_call(functools.partial(mixed_kernel, place), in_specs=[SMEM, VM...  1.45 us
  transfers between devices with their start and end apart: 13, of which 7 were waited for; matrix products, arithmetic and copies ran while one was open for 1% of the time, Pallas kernels for 19%

profile of v27, /device:TPU:0, one launch (start us, length us, event | category | flops | bytes accessed | tf_op | source)
XLA Modules:
  0.0 55.7 jit_solution(4617984116477526412)
XLA Ops:
  0.6 3.1 %hot_squares.1 = (f32[8,168,128]{2,1,0:T(8,128)S(1)}, f32[8,168,128]{2,1,0:T(8,128)S(1)}, bf16[8,768,256]{2,1,0:T(8,128)(2,1)S(1)}, bf16[8,768,128]{2,1,0:T(8,128)(2,1)S(1)}) custom-call(bf16[8,768,256]{2,1,0:T(8,128)(2,1)} %wide_hbm.1, bf16[8,768,128]{2,1,0:T(8,128)(2,1)} %narrow_hbm.1), custom_call_target="tpu_custom_call" | custom-call | flops 754974720 | bytes 3145728 | tf_op jit(solution)/shard_map/hot_squares/pallas_call | solution.py:256
  3.8 0.5 collective-permute-start
  4.3 0.6 %cold_squares.1 = (f32[4,168,128]{2,1,0:T(8,128)S(1)}, f32[4,168,128]{2,1,0:T(8,128)S(1)}) custom-call(bf16[8,768,256]{2,1,0:T(8,128)(2,1)S(1)} %get-tuple-element.46.wides, bf16[8,768,128]{2,1,0:T(8,128)(2,1)S(1)} %get-tuple-element.43.narrows), custom_call_target="tpu_custom_call" | custom-call | flops 251658240 | bytes 3145728 | tf_op jit(solution)/shard_map/cold_squares/pallas_call | solution.py:278
  4.9 0.7 %collective-permute-done = f32[4,168,128]{2,1,0:T(8,128)S(1)} collective-permute-done((f32[4,168,128]{2,1,0:T(8,128)S(1)}, f32[4,168,128]{2,1,0:T(8,128)S(1)}, u32[]{:S(2)}, u32[]{:S(2)}) %collective-permute-start) | collective-permute-done | bytes 344096 | tf_op jit(solution)/shard_map/ppermute | solution.py:792
  5.6 2.9 %collective-permute-start.1 = (f32[4,168,128]{2,1,0:T(8,128)S(1)}, f32[4,168,128]{2,1,0:T(8,128)S(1)}, u32[]{:S(2)}, u32[]{:S(2)}) collective-permute-start(f32[4,168,128]{2,1,0:T(8,128)S(1)} %slice_add_fusion.1), channel_id=1, source_target_pairs={{0,1},{1,0},{2,6},{3,7},{4,5},{5,4},{6,2},{7,3},{8,9},{9,8},{10,14... | collective-permute-start | bytes 1032200 | tf_op jit(solution)/shard_map/ppermute | solution.py:799
  8.5 1.4 %mixed.1 = (f32[8,128,128]{2,1,0:T(8,128)S(1)}, f32[8,128,128]{2,1,0:T(8,128)S(1)}, s32[8,8,128]{2,1,0:T(8,128)S(1)}) custom-call(s32[8]{0:T(128)S(1)} %copy-done, bf16[8,768,256]{2,1,0:T(8,128)(2,1)S(1)} %get-tuple-element.46.wides, bf16[8,768,128]{2,1,0:T(8,128)(2,1)S(1)} %get-tuple-element.43.narrows), custom_call_target="tpu_custom_call" | custom-call | flops 402653184 | bytes 3145728 | tf_op jit(solution)/shard_map/mixed/pallas_call | solution.py:293
  10.1 0.6 collective-permute-start.2
  10.7 3.1 %collective-permute-done.1 = f32[4,168,128]{2,1,0:T(8,128)S(1)} collective-permute-done((f32[4,168,128]{2,1,0:T(8,128)S(1)}, f32[4,168,128]{2,1,0:T(8,128)S(1)}, u32[]{:S(2)}, u32[]{:S(2)}) %collective-permute-start.1) | collective-permute-done | bytes 344096 | tf_op jit(solution)/shard_map/ppermute | solution.py:799
  13.9 2.1 %collective-permute-start.3 = (f32[2,168,128]{2,1,0:T(8,128)S(1)}, f32[2,168,128]{2,1,0:T(8,128)S(1)}, u32[]{:S(2)}, u32[]{:S(2)}) collective-permute-start(f32[2,168,128]{2,1,0:T(8,128)S(1)} %slice.57), channel_id=1, source_target_pairs={{0,4},{1,5},{2,10},{3,11},{4,0},{5,1},{6,14},{7,15},{8,12},{9,13},... | collective-permute-start | bytes 516104 | tf_op jit(solution)/shard_map/ppermute | solution.py:799
  16.1 1.6 %collective-permute-start.8 = (f32[4,128,128]{2,1,0:T(8,128)S(1)}, f32[4,128,128]{2,1,0:T(8,128)S(1)}, u32[]{:S(2)}, u32[]{:S(2)}) collective-permute-start(f32[4,128,128]{2,1,0:T(8,128)S(1)} %get-tuple-element.76), channel_id=1, source_target_pairs={{0,1},{1,0},{2,10},{3,11},{4,5},{5,4},{6,14},{7,15},{8,9},{9,8},{1... | collective-permute-start | bytes 786440 | tf_op jit(solution)/shard_map/ppermute | solution.py:799
  17.7 1.7 %collective-permute-done.3 = f32[2,168,128]{2,1,0:T(8,128)S(1)} collective-permute-done((f32[2,168,128]{2,1,0:T(8,128)S(1)}, f32[2,168,128]{2,1,0:T(8,128)S(1)}, u32[]{:S(2)}, u32[]{:S(2)}) %collective-permute-start.3) | collective-permute-done | bytes 172064 | tf_op jit(solution)/shard_map/ppermute | solution.py:799
  19.4 2.1 %collective-permute-start.4 = (f32[168,128]{1,0:T(8,128)S(1)}, f32[168,128]{1,0:T(8,128)S(1)}, u32[]{:S(2)}, u32[]{:S(2)}) collective-permute-start(f32[168,128]{1,0:T(8,128)S(1)} %slice_bitcast_fusion), channel_id=1, source_target_pairs={{0,8},{1,9},{2,3},{3,2},{4,12},{5,13},{6,7},{7,6},{8,0},{9,1},{10,... | collective-permute-start | bytes 258056 | tf_op jit(solution)/shard_map/ppermute | solution.py:799
  21.6 1.9 %collective-permute-done.8 = f32[4,128,128]{2,1,0:T(8,128)S(1)} collective-permute-done((f32[4,128,128]{2,1,0:T(8,128)S(1)}, f32[4,128,128]{2,1,0:T(8,128)S(1)}, u32[]{:S(2)}, u32[]{:S(2)}) %collective-permute-start.8) | collective-permute-done | bytes 262176 | tf_op jit(solution)/shard_map/ppermute | solution.py:799
  23.6 0.4 collective-permute-done.4
  24.0 3.1 %collective-permute-start.5 = (f32[168,128]{1,0:T(8,128)S(1)}, f32[168,128]{1,0:T(8,128)S(1)}, u32[]{:S(2)}, u32[]{:S(2)}) collective-permute-start(f32[168,128]{1,0:T(8,128)S(1)} %fusion), channel_id=1, source_target_pairs={{0,16},{16,0},{1,17},{17,1},{2,18},{18,2},{3,19},{19,3},{4,20},{20... | collective-permute-start | bytes 258056 | tf_op jit(solution)/shard_map/ppermute | solution.py:792
  27.1 2.5 %collective-permute-done.5 = f32[168,128]{1,0:T(8,128)S(1)} collective-permute-done((f32[168,128]{1,0:T(8,128)S(1)}, f32[168,128]{1,0:T(8,128)S(1)}, u32[]{:S(2)}, u32[]{:S(2)}) %collective-permute-start.5) | collective-permute-done | bytes 86048 | tf_op jit(solution)/shard_map/ppermute | solution.py:792
  29.8 2.0 %collective-permute-start.10 = (f32[128,128]{1,0:T(8,128)S(1)}, f32[128,128]{1,0:T(8,128)S(1)}, u32[]{:S(2)}, u32[]{:S(2)}) collective-permute-start(f32[128,128]{1,0:T(8,128)S(1)} %get-tuple-element.80), channel_id=1, source_target_pairs={{0,8},{1,9},{2,6},{3,7},{4,12},{5,13},{6,2},{7,3},{8,0},{9,1},{10,... | collective-permute-start | bytes 196616 | tf_op jit(solution)/shard_map/ppermute | solution.py:799
  31.8 3.8 %first_panels.1 = (f32[288,256]{1,0:T(8,128)S(1)}, bf16[96,256]{1,0:T(8,128)(2,1)S(1)}, bf16[96,256]{1,0:T(8,128)(2,1)S(1)}, f32[16,256]{1,0:T(8,128)S(1)}, f32[...) custom-call(f32[168,128]{1,0:T(8,128)S(1)} %add.46.mine, ...), custom_call_target="tpu_custom_call" | custom-call | flops 1073741824 | bytes 1048576 | tf_op jit(solution)/shard_map/first_panels/pallas_call | solution.py:644
  35.5 3.4 %collective-permute-start.11 = (f32[128,128]{1,0:T(8,128)S(1)}, f32[128,128]{1,0:T(8,128)S(1)}, u32[]{:S(2)}, u32[]{:S(2)}) collective-permute-start(f32[128,128]{1,0:T(8,128)S(1)} %add.50), channel_id=1, source_target_pairs={{0,16},{16,0},{1,17},{17,1},{2,18},{18,2},{3,19},{19,3},{4,20},{20... | collective-permute-start | bytes 196616 | tf_op jit(solution)/shard_map/ppermute | solution.py:792
  39.0 3.7 %second_panels.1 = (f32[128,128]{1,0:T(8,128)S(1)}, f32[288,256]{1,0:T(8,128)S(1)}, bf16[96,256]{1,0:T(8,128)(2,1)S(1)}, bf16[96,256]{1,0:T(8,128)(2,1)S(1)}, f32[16,256]{1,0:T(8,128)S(1)}) custom-call(f32[288,256]{1,0:T(8,128)S(1)} %get-tuple-element.53.refs_0_, bf16[96,256]{1,0:T(8,128)(2,1)S(1)} %get-tuple-element.54.refs_1_, ...), custom_call_target="tpu_custom_call" | custom-call | flops 1073741824 | bytes 1048576 | tf_op jit(solution)/shard_map/second_panels/pallas_call | solution.py:644
  42.8 1.0 %third_panels.1.winv = f32[256,256]{1,0:T(8,128)S(1)} custom-call(f32[288,256]{1,0:T(8,128)S(1)} %get-tuple-element.62.wa_in, bf16[96,256]{1,0:T(8,128)(2,1)S(1)} %get-tuple-element.63.wl_in, bf16[96,256]{1,0:T(8,128)(2,1)S(1)} %get-tuple-element.64.wr_in, f32[16,256]{1,0:T(8,128)S(1)} %get-tuple-element.65.panel_in, f32[8,256]{1,0:T(8,128)S(1)} %get-tuple-element.66.scale), custom_call_target="tpu_custom_call" | custom-call | flops 1073741824 | bytes 1048576 | tf_op jit(solution)/shard_map/third_panels/pallas_call | solution.py:644
  44.0 0.6 %products.1 = f32[8,40,128]{2,1,0:T(8,128)S(1)} custom-call(f32[256,256]{1,0:T(8,128)S(1)} %third_panels.1.winv, f32[128,128]{1,0:T(8,128)S(1)} %get-tuple-element.67.ninv_ref, f32[128,128]{1,0:T(8,128)S(1)} %add.51.mine, f32[128,128]{1,0:T(8,128)S(1)} %collective-permute-done.12.other), custom_call_target="tpu_custom_call" | custom-call | tf_op jit(solution)/shard_map/products/pallas_call | solution.py:735
  44.6 10.3 %all_to_all.5.got_ref = f32[8,40,128]{2,1,0:T(8,128)S(1)} all-to-all(f32[8,40,128]{2,1,0:T(8,128)S(1)} %products.1), channel_id=1, replica_groups=mesh['dp0'=2,'dp1'=2,'dp2'=2,'dp3'=2,'own0'=2] {'dp1','dp2','own0'}, dimensions={0} | all-to-all | bytes 327680 | tf_op jit(solution)/shard_map/all_to_all | solution.py:855
  55.0 0.7 %placing.1 = (f32[5,16,256]{2,1,0:T(8,128)}, f32[8,16,64]{2,1,0:T(8,128)}) custom-call(s32[8,8,128]{2,1,0:T(8,128)S(1)} %get-tuple-element.47.slots_ref, f32[8,40,128]{2,1,0:T(8,128)S(1)} %all_to_all.5.got_ref), custom_call_target="tpu_custom_call" | custom-call | tf_op jit(solution)/shard_map/placing/pallas_call | solution.py:778
  (31 shorter events, 1.0 us)
Async XLA Ops:
  3.7 4.8 %copy-start = (s32[8]{0:T(128)S(1)}, s32[8]{0:T(128)}, u32[]{:S(2)}) copy-start(s32[8]{0:T(128)} %owner_map.1) | copy-start | bytes 100
  3.8 1.8 %collective-permute-start = (f32[4,168,128]{2,1,0:T(8,128)S(1)}, f32[4,168,128]{2,1,0:T(8,128)S(1)}, u32[]{:S(2)}, u32[]{:S(2)}) collective-permute-start(f32[4,168,128]{2,1,0:T(8,128)S(1)} %slice.42), channel_id=1, source_target_pairs={{0,2},{2,0},{1,3},{3,1},{4,6},{6,4},{5,7},{7,5},{8,10},{10,8},{9,1... | collective-permute-start | bytes 1032200 | tf_op jit(solution)/shard_map/ppermute | solution.py:792
  5.6 8.1 %collective-permute-start.1 = (f32[4,168,128]{2,1,0:T(8,128)S(1)}, f32[4,168,128]{2,1,0:T(8,128)S(1)}, u32[]{:S(2)}, u32[]{:S(2)}) collective-permute-start(f32[4,168,128]{2,1,0:T(8,128)S(1)} %slice_add_fusion.1), channel_id=1, source_target_pairs={{0,1},{1,0},{2,6},{3,7},{4,5},{5,4},{6,2},{7,3},{8,9},{9,8},{10,14... | collective-permute-start | bytes 1032200 | tf_op jit(solution)/shard_map/ppermute | solution.py:799
  10.0 6.0 %collective-permute-start.7 = (f32[8,128,128]{2,1,0:T(8,128)S(1)}, f32[8,128,128]{2,1,0:T(8,128)S(1)}, u32[]{:S(2)}, u32[]{:S(2)}) collective-permute-start(f32[8,128,128]{2,1,0:T(8,128)S(1)} %get-tuple-element.50), channel_id=1, source_target_pairs={{0,2},{2,0},{1,3},{3,1},{4,6},{6,4},{5,7},{7,5},{8,10},{10,8},{9,1... | collective-permute-start | bytes 1572872 | tf_op jit(solution)/shard_map/ppermute | solution.py:792
  10.1 3.7 %collective-permute-start.2 = (f32[4,168,128]{2,1,0:T(8,128)S(1)}, f32[4,168,128]{2,1,0:T(8,128)S(1)}, u32[]{:S(2)}, u32[]{:S(2)}) collective-permute-start(f32[4,168,128]{2,1,0:T(8,128)S(1)} %slice_add_fusion), channel_id=1, source_target_pairs={{0,2},{2,0},{1,3},{3,1},{4,6},{6,4},{5,7},{7,5},{8,10},{10,8},{9,1... | collective-permute-start | bytes 1032200 | tf_op jit(solution)/shard_map/ppermute | solution.py:792
  13.9 5.5 %collective-permute-start.3 = (f32[2,168,128]{2,1,0:T(8,128)S(1)}, f32[2,168,128]{2,1,0:T(8,128)S(1)}, u32[]{:S(2)}, u32[]{:S(2)}) collective-permute-start(f32[2,168,128]{2,1,0:T(8,128)S(1)} %slice.57), channel_id=1, source_target_pairs={{0,4},{1,5},{2,10},{3,11},{4,0},{5,1},{6,14},{7,15},{8,12},{9,13},... | collective-permute-start | bytes 516104 | tf_op jit(solution)/shard_map/ppermute | solution.py:799
  16.1 7.4 %collective-permute-start.8 = (f32[4,128,128]{2,1,0:T(8,128)S(1)}, f32[4,128,128]{2,1,0:T(8,128)S(1)}, u32[]{:S(2)}, u32[]{:S(2)}) collective-permute-start(f32[4,128,128]{2,1,0:T(8,128)S(1)} %get-tuple-element.76), channel_id=1, source_target_pairs={{0,1},{1,0},{2,10},{3,11},{4,5},{5,4},{6,14},{7,15},{8,9},{9,8},{1... | collective-permute-start | bytes 786440 | tf_op jit(solution)/shard_map/ppermute | solution.py:799
  19.4 4.6 %collective-permute-start.4 = (f32[168,128]{1,0:T(8,128)S(1)}, f32[168,128]{1,0:T(8,128)S(1)}, u32[]{:S(2)}, u32[]{:S(2)}) collective-permute-start(f32[168,128]{1,0:T(8,128)S(1)} %slice_bitcast_fusion), channel_id=1, source_target_pairs={{0,8},{1,9},{2,3},{3,2},{4,12},{5,13},{6,7},{7,6},{8,0},{9,1},{10,... | collective-permute-start | bytes 258056 | tf_op jit(solution)/shard_map/ppermute | solution.py:799
  23.5 6.2 %collective-permute-start.9 = (f32[2,128,128]{2,1,0:T(8,128)S(1)}, f32[2,128,128]{2,1,0:T(8,128)S(1)}, u32[]{:S(2)}, u32[]{:S(2)}) collective-permute-start(f32[2,128,128]{2,1,0:T(8,128)S(1)} %get-tuple-element.78), channel_id=1, source_target_pairs={{0,4},{1,5},{2,3},{3,2},{4,0},{5,1},{6,7},{7,6},{8,12},{9,13},{10,... | collective-permute-start | bytes 393224 | tf_op jit(solution)/shard_map/ppermute | solution.py:799
  24.0 5.6 %collective-permute-start.5 = (f32[168,128]{1,0:T(8,128)S(1)}, f32[168,128]{1,0:T(8,128)S(1)}, u32[]{:S(2)}, u32[]{:S(2)}) collective-permute-start(f32[168,128]{1,0:T(8,128)S(1)} %fusion), channel_id=1, source_target_pairs={{0,16},{16,0},{1,17},{17,1},{2,18},{18,2},{3,19},{19,3},{4,20},{20... | collective-permute-start | bytes 258056 | tf_op jit(solution)/shard_map/ppermute | solution.py:792
  29.6 2.1 %collective-permute-start.6 = (f32[168,128]{1,0:T(8,128)S(1)}, f32[168,128]{1,0:T(8,128)S(1)}, u32[]{:S(2)}, u32[]{:S(2)}) collective-permute-start(f32[168,128]{1,0:T(8,128)S(1)} %add.46.mine), channel_id=1, source_target_pairs={{0,2},{2,0},{1,3},{3,1},{4,6},{6,4},{5,7},{7,5},{8,10},{10,8},{9,1... | collective-permute-start | bytes 258056 | tf_op jit(solution)/shard_map/ppermute | solution.py:792
  29.8 5.8 %collective-permute-start.10 = (f32[128,128]{1,0:T(8,128)S(1)}, f32[128,128]{1,0:T(8,128)S(1)}, u32[]{:S(2)}, u32[]{:S(2)}) collective-permute-start(f32[128,128]{1,0:T(8,128)S(1)} %get-tuple-element.80), channel_id=1, source_target_pairs={{0,8},{1,9},{2,6},{3,7},{4,12},{5,13},{6,2},{7,3},{8,0},{9,1},{10,... | collective-permute-start | bytes 196616 | tf_op jit(solution)/shard_map/ppermute | solution.py:799
  35.5 7.1 %collective-permute-start.11 = (f32[128,128]{1,0:T(8,128)S(1)}, f32[128,128]{1,0:T(8,128)S(1)}, u32[]{:S(2)}, u32[]{:S(2)}) collective-permute-start(f32[128,128]{1,0:T(8,128)S(1)} %add.50), channel_id=1, source_target_pairs={{0,16},{16,0},{1,17},{17,1},{2,18},{18,2},{3,19},{19,3},{4,20},{20... | collective-permute-start | bytes 196616 | tf_op jit(solution)/shard_map/ppermute | solution.py:792
  42.7 1.3 %collective-permute-start.12 = (f32[128,128]{1,0:T(8,128)S(1)}, f32[128,128]{1,0:T(8,128)S(1)}, u32[]{:S(2)}, u32[]{:S(2)}) collective-permute-start(f32[128,128]{1,0:T(8,128)S(1)} %add.51.mine), channel_id=1, source_target_pairs={{0,2},{2,0},{1,3},{3,1},{4,6},{6,4},{5,7},{7,5},{8,10},{10,8},{9,1... | collective-permute-start | bytes 196616 | tf_op jit(solution)/shard_map/ppermute | solution.py:792
